TPU v7x, 32 devices: a whole 2x2x4 slice. The times are simulated.
32 devices in a mesh: groups: 2 (over y), wide: 4 (over z), narrow: 4 (over x, core).
Axes of the slice: x: 2, y: 2, z: 4, core: 2. Of those that a mesh axis runs over, the one named last changes fastest.
Arguments:
- zone_labels: int32 [512, 128, 128], P(('groups', 'wide'), 'narrow'), parts along dimension 0, may hold values from 0 to 2, as said below
- cell_scale: float32 [512, 128, 128], P(('groups', 'wide'), 'narrow'), parts along dimension 0, may hold values from 0.4 to 2.5
- diffusivity: float32 [3, 3], replicated, may hold values from 0.3 to 3
- decay_rates: float32 [3], replicated, may hold values from 0.0003 to 0.003
- load_field: float32 [512, 128, 128], P(('groups', 'wide'), 'narrow'), parts along dimension 0, may hold values from -4 to 4
Outputs:
- concentration: float32 [512, 128, 128], P(('groups', 'wide'), 'narrow'), parts along dimension 0
- residual: float32 [512, 128, 128], P(('groups', 'wide'), 'narrow'), parts along dimension 0
There are 2 independent parts, one for each index of `groups`. A program takes and returns all parts, laid end to end along the dimension named above; an argument that names none is the same for every part. Nothing has to cross between parts.
Inputs may be any that keep to these rules, and one draw needn't show every extreme that they name: `zone_labels`: zone of each cell: 0 resting, 1 proliferative, 2 hypertrophic.
All inputs are finite; a program needn't handle non-finite values.
Results may differ from a plain program's by a relative error of at most 0.0003.
Values sent between devices are 32-bit elements; how exact they have to be, the bound alone decides.
No kernel may reach another device: no remote copies, remote signals or barrier semaphores. Data moves between devices by JAX's collectives and lax.ppermute only.
A program may use at most 64 MiB of HBM per device.

v0:
```python
import jax
import jax.numpy as jnp
from jax import lax
from jax.sharding import PartitionSpec as P

MARGIN = 4


precise = lax.Precision.HIGHEST
cheb_center = 1.3
cheb_radius = 1.2
cheb_ratio = 1.3 / 1.2


def with_halo(array, sides, width):
    for axis, dim in sides:
        size, length = (lax.axis_size(axis), array.shape[dim])
        up = [(i, (i + 1) % size) for i in range(size - 1)]
        down = [(j, i) for i, j in up]
        last = lax.slice_in_dim(array, length - width, length, axis=dim)
        first = lax.slice_in_dim(array, 0, width, axis=dim)
        before = lax.ppermute(last, axis, up)
        after = lax.ppermute(first, axis, down)
        array = jnp.concatenate([before, array, after], axis=dim)
    return array


def zone_lookup(zone_labels, zone_table):
    summed = jnp.zeros(zone_labels.shape, zone_table.dtype)
    for zone_id in range(zone_table.shape[0]):
        summed = summed + jnp.where(
            zone_labels == zone_id, zone_table[zone_id], jnp.zeros((), zone_table.dtype)
        )
    return summed


def conductances(zone_labels, cell_scale, diffusivity):
    return jnp.stack(
        [zone_lookup(zone_labels, diffusivity[:, direction]) * cell_scale for direction in range(3)]
    )


def face_term(center, neighbour, own_cond, near_cond):
    return 0.5 * (own_cond + near_cond) * (center - neighbour)


def operate(window, cond_window, mass_term):
    center = window[1:-1, 1:-1]
    own_cond = cond_window[:, 1:-1, 1:-1]
    result = mass_term * center
    result = result + face_term(center, window[2:, 1:-1], own_cond[0], cond_window[0, 2:, 1:-1])
    result = result + face_term(center, window[:-2, 1:-1], own_cond[0], cond_window[0, :-2, 1:-1])
    result = result + face_term(center, window[1:-1, 2:], own_cond[1], cond_window[1, 1:-1, 2:])
    result = result + face_term(center, window[1:-1, :-2], own_cond[1], cond_window[1, 1:-1, :-2])
    deep_field = jnp.pad(center, ((0, 0), (0, 0), (1, 1)))
    deep_cond = jnp.pad(own_cond[2], ((0, 0), (0, 0), (1, 1)))
    result = result + face_term(center, deep_field[:, :, 2:], own_cond[2], deep_cond[:, :, 2:])
    result = result + face_term(center, deep_field[:, :, :-2], own_cond[2], deep_cond[:, :, :-2])
    return result


def sine_basis(length):
    indices = jnp.arange(1, length + 1, dtype=jnp.int32)
    phases = indices[:, None] * indices[None, :] % (2 * (length + 1))
    angles = jnp.pi * phases.astype(jnp.float32) / (length + 1)
    sine_table = jnp.sqrt(jnp.float32(2.0 / (length + 1))) * jnp.sin(angles)
    eigvals = 4.0 * jnp.sin(jnp.pi * indices.astype(jnp.float32) / (2.0 * (length + 1))) ** 2
    return (sine_table, eigvals)


def transform(source_field, tables):
    spectral = jnp.einsum("ai,ajk->ijk", tables[0][0], source_field, precision=precise)
    spectral = jnp.einsum("bj,ibk->ijk", tables[1][0], spectral, precision=precise)
    return jnp.einsum("ijc,ck->ijk", spectral, tables[2][0], precision=precise)


def box_solve(extended, box_means, tables):
    divisor = (
        box_means[3]
        + box_means[0] * tables[0][1][:, None, None]
        + box_means[1] * tables[1][1][None, :, None]
        + box_means[2] * tables[2][1][None, None, :]
    )
    return transform(transform(extended, tables) / divisor, tables)


def assemble(diagonal, couple_long, couple_across, across):
    box_count = diagonal.shape[0]
    row_ids = jnp.arange(box_count, dtype=jnp.int32)[:, None]
    col_ids = jnp.arange(box_count, dtype=jnp.int32)[None, :]
    nothing = jnp.zeros((), diagonal.dtype)
    matrix = jnp.where(row_ids == col_ids, diagonal[:, None], nothing)
    matrix = matrix - jnp.where(col_ids == row_ids + across, couple_long[:, None], nothing)
    matrix = matrix - jnp.where(row_ids == col_ids + across, couple_long[None, :], nothing)
    matrix = matrix - jnp.where(col_ids == row_ids + 1, couple_across[:, None], nothing)
    matrix = matrix - jnp.where(row_ids == col_ids + 1, couple_across[None, :], nothing)
    return matrix


def on_device(zone_labels, cell_scale, diffusivity, decay_rates, load_field):
    cells_long, cells_across, cells_deep = load_field.shape
    conduct = conductances(zone_labels, cell_scale, diffusivity)
    mass_term = zone_lookup(zone_labels, decay_rates)
    tables = (
        sine_basis(cells_long + 2 * MARGIN),
        sine_basis(cells_across + 2 * MARGIN),
        sine_basis(cells_deep),
    )
    box_means = jnp.stack(
        [jnp.mean(conduct[0]), jnp.mean(conduct[1]), jnp.mean(conduct[2]), jnp.mean(mass_term)]
    )
    long_count = lax.axis_size("wide")
    across_count = lax.axis_size("narrow")
    long_pos = lax.axis_index("wide")
    across_pos = lax.axis_index("narrow")
    own_box = long_pos * across_count + across_pos
    reach_width = 1
    cond_window = with_halo(conduct, (("wide", 1), ("narrow", 2)), 1)

    def margin_of(own_field):
        return with_halo(own_field, (("wide", 0), ("narrow", 1)), MARGIN)

    def final_residual(iterate):
        window = with_halo(iterate, (("wide", 0), ("narrow", 1)), 1)
        return load_field - operate(window, cond_window, mass_term)

    first_pair = (load_field, margin_of(load_field))
    face_high_long = jnp.sum(
        0.5
        * (
            conduct[0, -1]
            + cond_window[0, reach_width + cells_long, reach_width : reach_width + cells_across]
        )
    )
    face_low_long = jnp.sum(
        0.5
        * (
            conduct[0, 0]
            + cond_window[0, reach_width - 1, reach_width : reach_width + cells_across]
        )
    )
    face_high_across = jnp.sum(
        0.5
        * (
            conduct[1][:, -1]
            + cond_window[1, reach_width : reach_width + cells_long, reach_width + cells_across]
        )
    )
    face_low_across = jnp.sum(
        0.5
        * (
            conduct[1][:, 0]
            + cond_window[1, reach_width : reach_width + cells_long, reach_width - 1]
        )
    )
    face_deep = jnp.sum(0.5 * conduct[2][:, :, 0]) + jnp.sum(0.5 * conduct[2][:, :, -1])
    diagonal = (
        jnp.sum(mass_term)
        + face_high_long
        + face_low_long
        + face_high_across
        + face_low_across
        + face_deep
    )
    couple_long = jnp.where(
        long_pos < long_count - 1, face_high_long, jnp.zeros((), face_high_long.dtype)
    )
    couple_across = jnp.where(
        across_pos < across_count - 1, face_high_across, jnp.zeros((), face_high_across.dtype)
    )
    entries = lax.all_gather(
        jnp.stack([diagonal, couple_long, couple_across])[None, :],
        ("wide", "narrow"),
        axis=0,
        tiled=True,
    )
    factor = jnp.linalg.cholesky(
        assemble(entries[:, 0], entries[:, 1], entries[:, 2], across_count)
    )

    def coarse_value(own_part):
        all_sums = lax.all_gather(
            jnp.sum(own_part).reshape(1), ("wide", "narrow"), axis=0, tiled=True
        )
        solved = jax.scipy.linalg.cho_solve((factor, True), all_sums)
        return lax.dynamic_index_in_dim(solved, own_box, 0, keepdims=False)

    def precondition(own_part, extended):
        coarse = coarse_value(own_part)
        solved = box_solve(extended, box_means, tables)[
            MARGIN : MARGIN + cells_long, MARGIN : MARGIN + cells_across
        ]
        return solved + coarse

    iterate = precondition(first_pair[0], first_pair[1]) / cheb_center
    update = iterate
    rho_now = 1.0 / cheb_ratio
    rho_next = 1.0 / (2.0 * cheb_ratio - rho_now)
    own_res = final_residual(iterate)
    own_res, ext_res = (own_res, margin_of(own_res))
    update = rho_next * rho_now * update + 2.0 * rho_next / cheb_radius * precondition(
        own_res, ext_res
    )
    iterate = iterate + update
    return (iterate, final_residual(iterate))


def solution(mesh):
    return jax.shard_map(
        on_device,
        mesh=mesh,
        in_specs=(
            P(("groups", "wide"), "narrow", None),
            P(("groups", "wide"), "narrow", None),
            P(),
            P(),
            P(("groups", "wide"), "narrow", None),
        ),
        out_specs=(P(("groups", "wide"), "narrow", None), P(("groups", "wide"), "narrow", None)),
        check_vma=False,
    )
```

profile of v0, /device:TPU:0, one launch (start us, length us, event | category | flops | bytes accessed | tf_op | source)
XLA Modules:
  0.0 210.4 jit_solution(15769213087794981697)
XLA Ops:
  0.7 1.9 copy.15
  3.3 5.7 %collective-permute-start = (f32[4,32,128]{2,0,1:T(4,128)}, f32[4,32,128]{2,0,1:T(4,128)}, u32[]{:S(2)}, u32[]{:S(2)}) collective-permute-start(f32[4,32,128]{2,0,1:T(4,128)} %get-tuple-element.52), channel_id=1, source_target_pairs={{0,4},{4,8},{8,12},{1,5},{5,9},{9,13},{2,6},{6,10},{10,14},{3,7},{... | collective-permute-start | bytes 196616 | tf_op jit(solution)/shard_map/ppermute | solution.py:22
  11.6 3.1 %fusion.99 = (f32[]{:T(128)}, pred[64,32,128]{2,1,0:T(8,128)(4,1)S(1)}, pred[64,32,128]{2,1,0:T(8,128)(4,1)S(1)}, pred[64,32,128]{2,1,0:T(8,128)(4,1)S(1)}) fusion(f32[]{:T(128)} %bitcast.6, f32[]{:T(128)} %bitcast.5, f32[]{:T(128)} %bitcast.4, s32[64,32,128]{2,1,0:T(8,128)S(1)} %copy-done.17), kind=kLoop, calls=%fused_computation.144 | loop fusion | flops 2359295 | bytes 1835024 | tf_op jit(solution)/shard_map/reduce_sum | solution.py:110
  14.7 7.9 %fusion.279 = (f32[]{:T(128)}, f32[64,32,128]{2,1,0:T(8,128)S(1)}, f32[]{:T(128)}, f32[64,32,128]{2,1,0:T(8,128)S(1)}, f32[]{:T(128)}, /*index=5*/f32[64,32,128]{2,1,0:T(8,128)S(1)}) fusion(f32[64,32,128]{2,1,0:T(8,128)S(1)} %copy-done.18, pred[64,32,128]{2,1,0:T(8,128)(4,1)S(1)} %get-tuple-element.21, f32[]{:T(128)} %bitcast.9, ...), kind=kLoop, calls=%fused_computation.372 | loop fusion | flops 5505021 | bytes 4980784 | tf_op jit(solution)/shard_map/reduce_sum | solution.py:110
  24.5 5.2 %collective-permute-start.5 = (f32[3,1,32,128]{3,2,1,0:T(8,128)}, f32[3,1,32,128]{3,2,1,0:T(8,128)S(1)}, u32[]{:S(2)}, u32[]{:S(2)}) collective-permute-start(f32[3,1,32,128]{3,2,1,0:T(8,128)} %get-tuple-element.30), channel_id=1, source_target_pairs={{0,4},{4,8},{8,12},{1,5},{5,9},{9,13},{2,6},{6,10},{10,14},{3,7},{... | collective-permute-start | bytes 147464 | tf_op jit(solution)/shard_map/ppermute | solution.py:22
  36.4 2.1 reduce_sum.122
  44.4 1.9 collective-permute-start.7
  50.9 1.7 pad_maximum_fusion.38
  52.6 4.8 %collective-permute-start.2 = (f32[72,4,128]{2,0,1:T(8,128)}, f32[72,4,128]{2,0,1:T(8,128)}, u32[]{:S(2)}, u32[]{:S(2)}) collective-permute-start(f32[72,4,128]{2,0,1:T(8,128)} %get-tuple-element.38), channel_id=1, source_target_pairs={{0,1},{1,2},{2,3},{4,5},{5,6},{6,7},{8,9},{9,10},{10,11},{12,13},{... | collective-permute-start | bytes 442376 | tf_op jit(solution)/shard_map/ppermute | solution.py:22
  63.5 32.7 %all-reduce.6 = (f32[48]{0:T(128)S(1)}, f32[16]{0:T(128)S(1)}) all-reduce(f32[48]{0:T(128)S(1)} %maximum_dynamic-update-slice_fusion, f32[16]{0:T(128)S(1)} %dynamic-update-slice.4), channel_id=2, replica_groups=mesh['groups'=2,'wide'=4,'narrow'=4] {'wide','narrow'}, use_global_device_ids=true, to_apply=%add.3 | all-reduce | flops 64 | bytes 512
  97.4 1.4 cholesky.19
  102.3 2.9 %fusion = f32[72,40,128]{2,0,1:T(8,128)S(1)} fusion(f32[72,4,128]{2,0,1:T(8,128)} %collective-permute-done.3, f32[4,32,128]{2,0,1:T(4,128)} %collective-permute-done.1, f32[64,32,128]{2,0,1:T(8,128)} %copy-done.5, f32[4,32,128]{2,0,1:T(4,128)} %collective-permute-done, f32[72,4,128]{2,0,1:T(8,128)} %collective-permute-done.2, s32[72]{0:T(128)S(1)} %iota_add_fusion.4), kind=kOutput, calls=%fused_computation.8 | convolution fusion | flops 320031360 | bytes 2949408 | tf_op jit(solution)/shard_map/ai,ajk->ijk/dot_general | solution.py:72
  105.2 1.6 fusion.26
  106.9 1.6 add_divide_fusion.1
  108.6 1.7 fusion.24
  110.3 1.6 fusion.28
  111.9 2.9 %broadcast_multiply_fusion = (f32[64,32,128]{2,1,0:T(8,128)S(1)}, f32[64,32,128]{2,1,0:T(8,128)}) fusion(f32[]{:T(128)} %bitcast.36, s32[128]{0:T(128)S(1)} %copy-done.25, f32[72,40,128]{2,1,0:T(8,128)S(1)} %fusion.28), kind=kOutput, calls=%fused_computation.145 | convolution fusion | flops 403341312 | bytes 3277828 | tf_op jit(solution)/shard_map/ijc,ck->ijk/dot_general | solution.py:74
  116.3 4.5 %collective-permute-start.9 = (f32[1,32,128]{2,1,0:T(8,128)S(1)}, f32[1,32,128]{2,1,0:T(8,128)S(1)}, u32[]{:S(2)}, u32[]{:S(2)}) collective-permute-start(f32[1,32,128]{2,1,0:T(8,128)S(1)} %get-tuple-element.48), channel_id=1, source_target_pairs={{0,4},{4,8},{8,12},{1,5},{5,9},{9,13},{2,6},{6,10},{10,14},{3,7},{... | collective-permute-start | bytes 49160 | tf_op jit(solution)/shard_map/ppermute | solution.py:22
  123.6 3.0 %collective-permute-start.11 = (f32[66,1,128]{2,1,0:T(1,128)S(1)}, f32[66,1,128]{2,1,0:T(1,128)S(1)}, u32[]{:S(2)}, u32[]{:S(2)}) collective-permute-start(f32[66,1,128]{2,1,0:T(1,128)S(1)} %get-tuple-element.43), channel_id=1, source_target_pairs={{0,1},{1,2},{2,3},{4,5},{5,6},{6,7},{8,9},{9,10},{10,11},{12,13},{... | collective-permute-start | bytes 101384 | tf_op jit(solution)/shard_map/ppermute | solution.py:22
  127.7 8.4 %fusion.273 = (f32[]{:T(128)}, f32[64,32,128]{2,1,0:T(8,128)S(1)}, f32[64,32,128]{2,1,0:T(8,128)}, f32[64,32,128]{2,1,0:T(8,128)}, f32[64,32,128]{2,1,0:T(8,128)}, /*index=5*/f32[64,32,128]{2,1,0:T(8,128)}) fusion(f32[64,32,128]{2,1,0:T(8,128)S(1)} %copy-done, f32[64,32,128]{2,1,0:T(8,128)S(1)} %get-tuple-element.66, ...), kind=kLoop, calls=%fused_computation.371 | loop fusion | flops 16252927 | bytes 14819344 | tf_op jit(solution)/shard_map/reduce_sum | solution.py:183
  137.1 4.3 %collective-permute-start.12 = (f32[4,32,128]{2,1,0:T(8,128)S(1)}, f32[4,32,128]{2,1,0:T(8,128)S(1)}, u32[]{:S(2)}, u32[]{:S(2)}) collective-permute-start(f32[4,32,128]{2,1,0:T(8,128)S(1)} %get-tuple-element.46), channel_id=1, source_target_pairs={{0,4},{4,8},{8,12},{1,5},{5,9},{9,13},{2,6},{6,10},{10,14},{3,7},{... | collective-permute-start | bytes 196616 | tf_op jit(solution)/shard_map/ppermute | solution.py:22
  144.1 29.7 %all-reduce.5 = f32[16]{0:T(128)S(1)} all-reduce(f32[16]{0:T(128)S(1)} %dynamic-update-slice.5), channel_id=1, replica_groups=mesh['groups'=2,'wide'=4,'narrow'=4] {'wide','narrow'}, use_global_device_ids=true, to_apply=%add.5 | all-reduce | flops 16 | bytes 128
  174.9 1.8 collective-permute-start.14
  180.2 1.7 fusion.20
  181.9 1.6 fusion.18
  183.6 1.6 add_divide_fusion
  185.2 1.7 fusion.16
  186.9 1.6 fusion.31
  188.6 2.1 %fusion.40 = f32[64,32,128]{2,1,0:T(8,128)S(1)} fusion(f32[72,40,128]{2,1,0:T(8,128)S(1)} %fusion.31, f32[64,32,128]{2,1,0:T(8,128)S(1)} %copy-done.12, f32[]{:T(128)} %bitcast.50, s32[128]{0:T(128)S(1)} %copy-done.26), kind=kOutput, calls=%fused_computation.43 | convolution fusion | flops 404389888 | bytes 3277828 | tf_op jit(solution)/shard_map/ijc,ck->ijk/dot_general | solution.py:74
  192.1 4.5 %collective-permute-start.17 = (f32[1,32,128]{2,1,0:T(8,128)S(1)}, f32[1,32,128]{2,1,0:T(8,128)S(1)}, u32[]{:S(2)}, u32[]{:S(2)}) collective-permute-start(f32[1,32,128]{2,1,0:T(8,128)S(1)} %get-tuple-element.44), channel_id=1, source_target_pairs={{0,4},{4,8},{8,12},{1,5},{5,9},{9,13},{2,6},{6,10},{10,14},{3,7},{... | collective-permute-start | bytes 49160 | tf_op jit(solution)/shard_map/ppermute | solution.py:22
  199.4 4.6 %collective-permute-start.19 = (f32[66,1,128]{2,1,0:T(1,128)S(1)}, f32[66,1,128]{2,1,0:T(1,128)S(1)}, u32[]{:S(2)}, u32[]{:S(2)}) collective-permute-start(f32[66,1,128]{2,1,0:T(1,128)S(1)} %get-tuple-element.41), channel_id=1, source_target_pairs={{0,1},{1,2},{2,3},{4,5},{5,6},{6,7},{8,9},{9,10},{10,11},{12,13},{... | collective-permute-start | bytes 101384 | tf_op jit(solution)/shard_map/ppermute | solution.py:22
  204.9 5.5 %fusion.58 = f32[64,32,128]{2,1,0:T(8,128)} fusion(f32[64,32,128]{2,1,0:T(8,128)S(1)} %copy-done.1, f32[64,32,128]{2,1,0:T(8,128)S(1)} %fusion.40, f32[64,32,128]{2,1,0:T(8,128)S(1)} %copy-done.16, f32[66,1,128]{2,1,0:T(1,128)S(1)} %collective-permute-done.19, f32[1,32,128]{2,1,0:T(8,128)S(1)} %collective-permute-done.16, ...), kind=kLoop, calls=%fused_computation.65 | loop fusion | flops 9699328 | bytes 9275404 | tf_op jit(solution)/shard_map/sub | solution.py:125
  (138 shorter events, 42.7 us)
Async XLA Ops:
  3.3 47.6 %collective-permute-start = (f32[4,32,128]{2,0,1:T(4,128)}, f32[4,32,128]{2,0,1:T(4,128)}, u32[]{:S(2)}, u32[]{:S(2)}) collective-permute-start(f32[4,32,128]{2,0,1:T(4,128)} %get-tuple-element.52), channel_id=1, source_target_pairs={{0,4},{4,8},{8,12},{1,5},{5,9},{9,13},{2,6},{6,10},{10,14},{3,7},{... | collective-permute-start | bytes 196616 | tf_op jit(solution)/shard_map/ppermute | solution.py:22
  9.0 41.9 %collective-permute-start.1 = (f32[4,32,128]{2,0,1:T(4,128)}, f32[4,32,128]{2,0,1:T(4,128)}, u32[]{:S(2)}, u32[]{:S(2)}) collective-permute-start(f32[4,32,128]{2,0,1:T(4,128)} %get-tuple-element.53), channel_id=1, source_target_pairs={{4,0},{8,4},{12,8},{5,1},{9,5},{13,9},{6,2},{10,6},{14,10},{7,3},{... | collective-permute-start | bytes 196616 | tf_op jit(solution)/shard_map/ppermute | solution.py:23
  23.2 19.7 %collective-permute-start.4 = (f32[3,1,32,128]{3,2,1,0:T(8,128)}, f32[3,1,32,128]{3,2,1,0:T(8,128)S(1)}, u32[]{:S(2)}, u32[]{:S(2)}) collective-permute-start(f32[3,1,32,128]{3,2,1,0:T(8,128)} %get-tuple-element.31), channel_id=1, source_target_pairs={{4,0},{8,4},{12,8},{5,1},{9,5},{13,9},{6,2},{10,6},{14,10},{7,3},{... | collective-permute-start | bytes 147464 | tf_op jit(solution)/shard_map/ppermute | solution.py:23
  24.5 18.4 %collective-permute-start.5 = (f32[3,1,32,128]{3,2,1,0:T(8,128)}, f32[3,1,32,128]{3,2,1,0:T(8,128)S(1)}, u32[]{:S(2)}, u32[]{:S(2)}) collective-permute-start(f32[3,1,32,128]{3,2,1,0:T(8,128)} %get-tuple-element.30), channel_id=1, source_target_pairs={{0,4},{4,8},{8,12},{1,5},{5,9},{9,13},{2,6},{6,10},{10,14},{3,7},{... | collective-permute-start | bytes 147464 | tf_op jit(solution)/shard_map/ppermute | solution.py:22
  29.7 72.6 %copy-start.21 = (s32[72]{0:T(128)}, s32[72]{0:T(128)S(1)}, u32[]{:S(2)}) copy-start(s32[72]{0:T(128)S(1)} %iota_add_fusion.4) | copy-start | bytes 868
  44.4 16.3 %collective-permute-start.7 = (f32[3,66,1,128]{3,1,2,0:T(8,128)}, f32[3,66,1,128]{3,1,2,0:T(8,128)}, u32[]{:S(2)}, u32[]{:S(2)}) collective-permute-start(f32[3,66,1,128]{3,1,2,0:T(8,128)} %copy.31), channel_id=1, source_target_pairs={{0,1},{1,2},{2,3},{4,5},{5,6},{6,7},{8,9},{9,10},{10,11},{12,13},{... | collective-permute-start | bytes 304136 | tf_op jit(solution)/shard_map/ppermute | solution.py:22
  48.3 10.4 %collective-permute-start.6 = (f32[3,66,1,128]{3,2,1,0:T(1,128)}, f32[3,66,1,128]{3,2,1,0:T(1,128)}, u32[]{:S(2)}, u32[]{:S(2)}) collective-permute-start(f32[3,66,1,128]{3,2,1,0:T(1,128)} %get-tuple-element.29), channel_id=1, source_target_pairs={{1,0},{2,1},{3,2},{5,4},{6,5},{7,6},{9,8},{10,9},{11,10},{13,12},{... | collective-permute-start | bytes 304136 | tf_op jit(solution)/shard_map/ppermute | solution.py:23
  52.6 49.7 %collective-permute-start.2 = (f32[72,4,128]{2,0,1:T(8,128)}, f32[72,4,128]{2,0,1:T(8,128)}, u32[]{:S(2)}, u32[]{:S(2)}) collective-permute-start(f32[72,4,128]{2,0,1:T(8,128)} %get-tuple-element.38), channel_id=1, source_target_pairs={{0,1},{1,2},{2,3},{4,5},{5,6},{6,7},{8,9},{9,10},{10,11},{12,13},{... | collective-permute-start | bytes 442376 | tf_op jit(solution)/shard_map/ppermute | solution.py:22
  57.4 44.9 %collective-permute-start.3 = (f32[72,4,128]{2,0,1:T(8,128)}, f32[72,4,128]{2,0,1:T(8,128)}, u32[]{:S(2)}, u32[]{:S(2)}) collective-permute-start(f32[72,4,128]{2,0,1:T(8,128)} %get-tuple-element.39), channel_id=1, source_target_pairs={{1,0},{2,1},{3,2},{5,4},{6,5},{7,6},{9,8},{10,9},{11,10},{13,12},{... | collective-permute-start | bytes 442376 | tf_op jit(solution)/shard_map/ppermute | solution.py:23
  111.9 15.8 %copy-start.10 = (pred[64,32,128]{2,1,0:T(8,128)(4,1)S(1)}, pred[64,32,128]{2,1,0:T(8,128)(4,1)}, u32[]{:S(2)}) copy-start(pred[64,32,128]{2,1,0:T(8,128)(4,1)} %copy-done.9) | copy-start | bytes 786436
  114.9 12.9 %copy-start.7 = (pred[64,32,128]{2,1,0:T(8,128)(4,1)S(1)}, pred[64,32,128]{2,1,0:T(8,128)(4,1)}, u32[]{:S(2)}) copy-start(pred[64,32,128]{2,1,0:T(8,128)(4,1)} %copy-done.6) | copy-start | bytes 786436
  114.9 6.0 %collective-permute-start.8 = (f32[1,32,128]{2,1,0:T(8,128)S(1)}, f32[1,32,128]{2,1,0:T(8,128)S(1)}, u32[]{:S(2)}, u32[]{:S(2)}) collective-permute-start(f32[1,32,128]{2,1,0:T(8,128)S(1)} %get-tuple-element.49), channel_id=1, source_target_pairs={{4,0},{8,4},{12,8},{5,1},{9,5},{13,9},{6,2},{10,6},{14,10},{7,3},{... | collective-permute-start | bytes 49160 | tf_op jit(solution)/shard_map/ppermute | solution.py:23
  116.3 6.0 %collective-permute-start.9 = (f32[1,32,128]{2,1,0:T(8,128)S(1)}, f32[1,32,128]{2,1,0:T(8,128)S(1)}, u32[]{:S(2)}, u32[]{:S(2)}) collective-permute-start(f32[1,32,128]{2,1,0:T(8,128)S(1)} %get-tuple-element.48), channel_id=1, source_target_pairs={{0,4},{4,8},{8,12},{1,5},{5,9},{9,13},{2,6},{6,10},{10,14},{3,7},{... | collective-permute-start | bytes 49160 | tf_op jit(solution)/shard_map/ppermute | solution.py:22
  122.3 5.3 %collective-permute-start.10 = (f32[66,1,128]{2,1,0:T(1,128)S(1)}, f32[66,1,128]{2,1,0:T(1,128)S(1)}, u32[]{:S(2)}, u32[]{:S(2)}) collective-permute-start(f32[66,1,128]{2,1,0:T(1,128)S(1)} %get-tuple-element.42), channel_id=1, source_target_pairs={{1,0},{2,1},{3,2},{5,4},{6,5},{7,6},{9,8},{10,9},{11,10},{13,12},{... | collective-permute-start | bytes 101384 | tf_op jit(solution)/shard_map/ppermute | solution.py:23
  123.6 4.1 %collective-permute-start.11 = (f32[66,1,128]{2,1,0:T(1,128)S(1)}, f32[66,1,128]{2,1,0:T(1,128)S(1)}, u32[]{:S(2)}, u32[]{:S(2)}) collective-permute-start(f32[66,1,128]{2,1,0:T(1,128)S(1)} %get-tuple-element.43), channel_id=1, source_target_pairs={{0,1},{1,2},{2,3},{4,5},{5,6},{6,7},{8,9},{9,10},{10,11},{12,13},{... | collective-permute-start | bytes 101384 | tf_op jit(solution)/shard_map/ppermute | solution.py:22
  137.1 42.9 %copy-start.3 = (f32[64,32,128]{2,1,0:T(8,128)S(1)}, f32[64,32,128]{2,1,0:T(8,128)}, u32[]{:S(2)}) copy-start(f32[64,32,128]{2,1,0:T(8,128)} %copy-done.2) | copy-start | bytes 3145732
  137.1 36.7 %collective-permute-start.12 = (f32[4,32,128]{2,1,0:T(8,128)S(1)}, f32[4,32,128]{2,1,0:T(8,128)S(1)}, u32[]{:S(2)}, u32[]{:S(2)}) collective-permute-start(f32[4,32,128]{2,1,0:T(8,128)S(1)} %get-tuple-element.46), channel_id=1, source_target_pairs={{0,4},{4,8},{8,12},{1,5},{5,9},{9,13},{2,6},{6,10},{10,14},{3,7},{... | collective-permute-start | bytes 196616 | tf_op jit(solution)/shard_map/ppermute | solution.py:22
  141.5 32.4 %collective-permute-start.13 = (f32[4,32,128]{2,1,0:T(8,128)S(1)}, f32[4,32,128]{2,1,0:T(8,128)S(1)}, u32[]{:S(2)}, u32[]{:S(2)}) collective-permute-start(f32[4,32,128]{2,1,0:T(8,128)S(1)} %get-tuple-element.47), channel_id=1, source_target_pairs={{4,0},{8,4},{12,8},{5,1},{9,5},{13,9},{6,2},{10,6},{14,10},{7,3},{... | collective-permute-start | bytes 196616 | tf_op jit(solution)/shard_map/ppermute | solution.py:23
  174.9 4.0 %collective-permute-start.14 = (f32[72,4,128]{2,1,0:T(4,128)S(1)}, f32[72,4,128]{2,1,0:T(4,128)S(1)}, u32[]{:S(2)}, u32[]{:S(2)}) collective-permute-start(f32[72,4,128]{2,1,0:T(4,128)S(1)} %get-tuple-element.36), channel_id=1, source_target_pairs={{0,1},{1,2},{2,3},{4,5},{5,6},{6,7},{8,9},{9,10},{10,11},{12,13},{... | collective-permute-start | bytes 442376 | tf_op jit(solution)/shard_map/ppermute | solution.py:22
  176.7 3.3 %collective-permute-start.15 = (f32[72,4,128]{2,1,0:T(4,128)S(1)}, f32[72,4,128]{2,1,0:T(4,128)S(1)}, u32[]{:S(2)}, u32[]{:S(2)}) collective-permute-start(f32[72,4,128]{2,1,0:T(4,128)S(1)} %get-tuple-element.37), channel_id=1, source_target_pairs={{1,0},{2,1},{3,2},{5,4},{6,5},{7,6},{9,8},{10,9},{11,10},{13,12},{... | collective-permute-start | bytes 442376 | tf_op jit(solution)/shard_map/ppermute | solution.py:23
  186.9 18.0 %copy-start.15 = (f32[64,32,128]{2,1,0:T(8,128)S(1)}, f32[64,32,128]{2,1,0:T(8,128)}, u32[]{:S(2)}) copy-start(f32[64,32,128]{2,1,0:T(8,128)} %get-tuple-element.16) | copy-start | bytes 3145732
  186.9 17.9 %copy-start.16 = (f32[64,32,128]{2,1,0:T(8,128)S(1)}, f32[64,32,128]{2,1,0:T(8,128)}, u32[]{:S(2)}) copy-start(f32[64,32,128]{2,1,0:T(8,128)} %get-tuple-element.17) | copy-start | bytes 3145732
  188.6 16.3 %copy-start.1 = (f32[64,32,128]{2,1,0:T(8,128)S(1)}, f32[64,32,128]{2,1,0:T(8,128)}, u32[]{:S(2)}) copy-start(f32[64,32,128]{2,1,0:T(8,128)} %param.11) | copy-start | bytes 3145732
  188.6 16.3 %copy-start.8 = (pred[64,32,128]{2,1,0:T(8,128)(4,1)S(1)}, pred[64,32,128]{2,1,0:T(8,128)(4,1)}, u32[]{:S(2)}) copy-start(pred[64,32,128]{2,1,0:T(8,128)(4,1)} %copy-done.6) | copy-start | bytes 786436
  188.6 16.3 %copy-start.11 = (pred[64,32,128]{2,1,0:T(8,128)(4,1)S(1)}, pred[64,32,128]{2,1,0:T(8,128)(4,1)}, u32[]{:S(2)}) copy-start(pred[64,32,128]{2,1,0:T(8,128)(4,1)} %copy-done.9) | copy-start | bytes 786436
  188.6 16.3 %copy-start.13 = (f32[64,32,128]{2,1,0:T(8,128)S(1)}, f32[64,32,128]{2,1,0:T(8,128)}, u32[]{:S(2)}) copy-start(f32[64,32,128]{2,1,0:T(8,128)} %get-tuple-element.14) | copy-start | bytes 3145732
  188.6 16.3 %copy-start.14 = (f32[64,32,128]{2,1,0:T(8,128)S(1)}, f32[64,32,128]{2,1,0:T(8,128)}, u32[]{:S(2)}) copy-start(f32[64,32,128]{2,1,0:T(8,128)} %get-tuple-element.15) | copy-start | bytes 3145732
  190.8 19.6 %copy-start.4 = (f32[64,32,128]{2,1,0:T(8,128)}, f32[64,32,128]{2,1,0:T(8,128)S(1)}, u32[]{:S(2)}) copy-start(f32[64,32,128]{2,1,0:T(8,128)S(1)} %fusion.40) | copy-start | bytes 3145732
  190.8 5.9 %collective-permute-start.16 = (f32[1,32,128]{2,1,0:T(8,128)S(1)}, f32[1,32,128]{2,1,0:T(8,128)S(1)}, u32[]{:S(2)}, u32[]{:S(2)}) collective-permute-start(f32[1,32,128]{2,1,0:T(8,128)S(1)} %get-tuple-element.45), channel_id=1, source_target_pairs={{4,0},{8,4},{12,8},{5,1},{9,5},{13,9},{6,2},{10,6},{14,10},{7,3},{... | collective-permute-start | bytes 49160 | tf_op jit(solution)/shard_map/ppermute | solution.py:23
  192.1 6.0 %collective-permute-start.17 = (f32[1,32,128]{2,1,0:T(8,128)S(1)}, f32[1,32,128]{2,1,0:T(8,128)S(1)}, u32[]{:S(2)}, u32[]{:S(2)}) collective-permute-start(f32[1,32,128]{2,1,0:T(8,128)S(1)} %get-tuple-element.44), channel_id=1, source_target_pairs={{0,4},{4,8},{8,12},{1,5},{5,9},{9,13},{2,6},{6,10},{10,14},{3,7},{... | collective-permute-start | bytes 49160 | tf_op jit(solution)/shard_map/ppermute | solution.py:22
  198.1 5.9 %collective-permute-start.18 = (f32[66,1,128]{2,1,0:T(1,128)S(1)}, f32[66,1,128]{2,1,0:T(1,128)S(1)}, u32[]{:S(2)}, u32[]{:S(2)}) collective-permute-start(f32[66,1,128]{2,1,0:T(1,128)S(1)} %get-tuple-element.40), channel_id=1, source_target_pairs={{1,0},{2,1},{3,2},{5,4},{6,5},{7,6},{9,8},{10,9},{11,10},{13,12},{... | collective-permute-start | bytes 101384 | tf_op jit(solution)/shard_map/ppermute | solution.py:23
  199.4 5.5 %collective-permute-start.19 = (f32[66,1,128]{2,1,0:T(1,128)S(1)}, f32[66,1,128]{2,1,0:T(1,128)S(1)}, u32[]{:S(2)}, u32[]{:S(2)}) collective-permute-start(f32[66,1,128]{2,1,0:T(1,128)S(1)} %get-tuple-element.41), channel_id=1, source_target_pairs={{0,1},{1,2},{2,3},{4,5},{5,6},{6,7},{8,9},{9,10},{10,11},{12,13},{... | collective-permute-start | bytes 101384 | tf_op jit(solution)/shard_map/ppermute | solution.py:22
  (18 other events, 106.2 us)
where the time goes:
time: 213 us; the launch traced here: 210 us
  blocking collectives  62.4 us (29%)
  starting transfers between devices  53.4 us (25%)
  other arithmetic  42.7 us (20%)
  matrix products  23.3 us (11%)
  local copies, waits for them, and re-layouts  13.7 us (6%)
  between operations  10.1 us (5%)
  waiting for transfers between devices  4.79 us (2%)
    unnamed x2, blocking collectives  62.4 us
    ppermute x10, starting transfers between devices, with_halo(): before = lax.ppermute(last, axis, up)  40.4 us
    ppermute x10, starting transfers between devices, with_halo(): after = lax.ppermute(first, axis, down)  13 us
    reduce_sum x2, other arithmetic, coarse_value(): jnp.sum(own_part).reshape(1)  10.5 us
    dot_general x4, matrix products, transform(): return jnp.einsum('ijc,ck->ijk', spectral, tables[2][0], precision=precise)  8.29 us
    dot_general x4, matrix products, transform(): jnp.einsum('ai,ajk->ijk', tables[0][0], source_field, precision=precise)  7.96 us
    reduce_sum x1, other arithmetic, on_device(): jnp.mean(conduct[0])  7.85 us
    unnamed x68, local copies, waits for them, and re-layouts  7.68 us
  transfers between devices with their start and end apart: 20, of which 4 were waited for; matrix products, arithmetic and copies ran while one was open for 18% of the time, Pallas kernels for 0%

commit v1 on v0

--- a/solution.py
+++ b/solution.py
@@ -21,6 +21,24 @@
         first = lax.slice_in_dim(array, 0, width, axis=dim)
         before = lax.ppermute(last, axis, up)
         after = lax.ppermute(first, axis, down)
+        array = jnp.concatenate([before, array, after], axis=dim)
+    return array
+
+
+def with_faces(array, sides):
+    for axis, dim in sides:
+        size, length = (lax.axis_size(axis), array.shape[dim])
+        own = lax.axis_index(axis)
+        last = lax.slice_in_dim(array, length - 1, length, axis=dim)
+        first = lax.slice_in_dim(array, 0, 1, axis=dim)
+        place = jnp.arange(size, dtype=jnp.int32).reshape((size,) + (1,) * array.ndim)
+        sent = jnp.where(place > own, last[None], first[None])
+        got = lax.all_to_all(sent, axis, split_axis=0, concat_axis=0, tiled=True)
+        nothing = jnp.zeros((), array.dtype)
+        before = lax.dynamic_index_in_dim(got, jnp.maximum(own - 1, 0), 0, keepdims=False)
+        after = lax.dynamic_index_in_dim(got, jnp.minimum(own + 1, size - 1), 0, keepdims=False)
+        before = jnp.where(own > 0, before, nothing)
+        after = jnp.where(own < size - 1, after, nothing)
         array = jnp.concatenate([before, array, after], axis=dim)
     return array
 
@@ -121,7 +139,7 @@
         return with_halo(own_field, (("wide", 0), ("narrow", 1)), MARGIN)
 
     def final_residual(iterate):
-        window = with_halo(iterate, (("wide", 0), ("narrow", 1)), 1)
+        window = with_faces(iterate, (("wide", 0), ("narrow", 1)))
         return load_field - operate(window, cond_window, mass_term)
 
     first_pair = (load_field, margin_of(load_field))
@@ -168,20 +186,25 @@
     couple_across = jnp.where(
         across_pos < across_count - 1, face_high_across, jnp.zeros((), face_high_across.dtype)
     )
-    entries = lax.all_gather(
-        jnp.stack([diagonal, couple_long, couple_across])[None, :],
+    box_count = long_count * across_count
+    own_entries = jnp.pad(
+        jnp.stack([diagonal, couple_long, couple_across])[None, None, :], ((0, 0), (0, 0), (0, 125))
+    )
+    entries = lax.all_to_all(
+        jnp.broadcast_to(own_entries, (box_count, 1, 128)),
         ("wide", "narrow"),
-        axis=0,
+        split_axis=0,
+        concat_axis=0,
         tiled=True,
-    )
+    )[:, 0, :3]
     factor = jnp.linalg.cholesky(
         assemble(entries[:, 0], entries[:, 1], entries[:, 2], across_count)
     )
 
     def coarse_value(own_part):
         all_sums = lax.all_gather(
-            jnp.sum(own_part).reshape(1), ("wide", "narrow"), axis=0, tiled=True
-        )
+            jnp.broadcast_to(jnp.sum(own_part), (8, 128)), ("wide", "narrow"), axis=0, tiled=True
+        )[::8, 0]
         solved = jax.scipy.linalg.cho_solve((factor, True), all_sums)
         return lax.dynamic_index_in_dim(solved, own_box, 0, keepdims=False)
 

time: 213 us -> 245 us (1.15)
  other arithmetic: 42.7 us -> 58.8 us
  blocking collectives: 62.4 us -> 77.1 us
  starting transfers between devices: 53.4 us -> 39.4 us
  waiting for transfers between devices: 4.79 us -> 15.5 us
  local copies, waits for them, and re-layouts: 13.7 us -> 18 us
    ppermute x10 -> x6, starting transfers between devices: 40.4 us -> 18.9 us  [with_halo(): before = lax.ppermute(last, axis, up)]
    all_to_all x0 -> x2, blocking collectives: none -> 17.4 us  [with_faces(): got = lax.all_to_all(sent, axis, split_axis=0, concat_axis=0, tiled=True)]
    all_to_all x0 -> x3, starting transfers between devices: none -> 12.4 us  [the longest x2 8.32 us: with_faces(): got = lax.all_to_all(sent, axis, split_axis=0, concat_axis=0, tiled=True)]
    all_to_all x0 -> x3, waiting for transfers between devices: none -> 9.97 us  [the longest x2 9.97 us: with_faces(): got = lax.all_to_all(sent, axis, split_axis=0, concat_axis=0, tiled=True)]
    ppermute x10 -> x6, starting transfers between devices: 13 us -> 8.11 us  [with_halo(): after = lax.ppermute(first, axis, down)]
    reduce_sum x2, other arithmetic: 10.5 us -> 14.8 us  [coarse_value(): jnp.sum(own_part)]
    ppermute x10 -> x6, waiting for transfers between devices: 1.11 us -> 5.15 us  [with_halo(): after = lax.ppermute(first, axis, down)]
    ppermute x10 -> x6, waiting for transfers between devices: 3.68 us -> 0.38 us  [with_halo(): before = lax.ppermute(last, axis, up)]
  transfers between devices with their start and end apart: 20 -> 15, of which waited for: 4 -> 5; matrix products, arithmetic and copies ran while one was open for 18% -> 20% of each run, Pallas kernels for 0% -> 0%
where the time goes in v1:
time: 245 us; the launch traced here: 243 us
  blocking collectives  77.1 us (31%)
  other arithmetic  58.8 us (24%)
  starting transfers between devices  39.4 us (16%)
  matrix products  24.7 us (10%)
  local copies, waits for them, and re-layouts  18 us (7%)
  waiting for transfers between devices  15.5 us (6%)
  between operations  9.6 us (4%)
    unnamed x2, blocking collectives  59.7 us
    ppermute x6, starting transfers between devices, with_halo(): before = lax.ppermute(last, axis, up)  18.9 us
    all_to_all x2, blocking collectives, with_faces(): got = lax.all_to_all(sent, axis, split_axis=0, concat_axis=0, tiled=True)  17.4 us
    reduce_sum x2, other arithmetic, coarse_value(): jnp.sum(own_part)  14.8 us
    all_to_all x2, waiting for transfers between devices, with_faces(): got = lax.all_to_all(sent, axis, split_axis=0, concat_axis=0, tiled=True)  9.97 us
    all_to_all x2, starting transfers between devices, with_faces(): got = lax.all_to_all(sent, axis, split_axis=0, concat_axis=0, tiled=True)  8.32 us
    dot_general x4, matrix products, transform(): return jnp.einsum('ijc,ck->ijk', spectral, tables[2][0], precision=precise)  8.25 us
    ppermute x6, starting transfers between devices, with_halo(): after = lax.ppermute(first, axis, down)  8.11 us
  transfers between devices with their start and end apart: 15, of which 5 were waited for; matrix products, arithmetic and copies ran while one was open for 20% of the time, Pallas kernels for 0%

profile of v1, /device:TPU:0, one launch (start us, length us, event | category | flops | bytes accessed | tf_op | source)
XLA Modules:
  0.0 243.2 jit_solution(8575012355843732342)
XLA Ops:
  0.7 1.9 copy.29
  3.3 5.7 %collective-permute-start = (f32[4,32,128]{2,0,1:T(4,128)}, f32[4,32,128]{2,0,1:T(4,128)}, u32[]{:S(2)}, u32[]{:S(2)}) collective-permute-start(f32[4,32,128]{2,0,1:T(4,128)} %get-tuple-element.47), channel_id=1, source_target_pairs={{0,4},{4,8},{8,12},{1,5},{5,9},{9,13},{2,6},{6,10},{10,14},{3,7},{... | collective-permute-start | bytes 196616 | tf_op jit(solution)/shard_map/ppermute | solution.py:22
  11.5 3.0 %fusion.99 = (f32[]{:T(128)}, pred[64,32,128]{2,1,0:T(8,128)(4,1)S(1)}, pred[64,32,128]{2,1,0:T(8,128)(4,1)S(1)}, pred[64,32,128]{2,1,0:T(8,128)(4,1)S(1)}) fusion(f32[]{:T(128)} %bitcast.6, f32[]{:T(128)} %bitcast.5, f32[]{:T(128)} %bitcast.4, s32[64,32,128]{2,1,0:T(8,128)S(1)} %copy-done.14), kind=kLoop, calls=%fused_computation.144 | loop fusion | flops 2359295 | bytes 1835024 | tf_op jit(solution)/shard_map/reduce_sum | solution.py:128
  14.6 8.1 %fusion.283 = (f32[]{:T(128)}, f32[64,32,128]{2,1,0:T(8,128)S(1)}, f32[]{:T(128)}, f32[64,32,128]{2,1,0:T(8,128)S(1)}, f32[]{:T(128)}, /*index=5*/f32[64,32,128]{2,1,0:T(8,128)S(1)}) fusion(f32[64,32,128]{2,1,0:T(8,128)S(1)} %copy-done.15, pred[64,32,128]{2,1,0:T(8,128)(4,1)S(1)} %get-tuple-element.16, f32[]{:T(128)} %bitcast.9, ...), kind=kLoop, calls=%fused_computation.401 | loop fusion | flops 5505021 | bytes 4980784 | tf_op jit(solution)/shard_map/reduce_sum | solution.py:128
  24.6 5.2 %collective-permute-start.5 = (f32[3,1,32,128]{3,2,1,0:T(8,128)}, f32[3,1,32,128]{3,2,1,0:T(8,128)S(1)}, u32[]{:S(2)}, u32[]{:S(2)}) collective-permute-start(f32[3,1,32,128]{3,2,1,0:T(8,128)} %get-tuple-element.25), channel_id=1, source_target_pairs={{0,4},{4,8},{8,12},{1,5},{5,9},{9,13},{2,6},{6,10},{10,14},{3,7},{... | collective-permute-start | bytes 147464 | tf_op jit(solution)/shard_map/ppermute | solution.py:22
  36.3 2.1 reduce_sum.122
  40.4 30.2 %all-reduce.4 = f32[16]{0:T(128)S(1)} all-reduce(f32[16]{0:T(128)S(1)} %dynamic-update-slice.3), channel_id=2, replica_groups=mesh['groups'=2,'wide'=4,'narrow'=4] {'wide','narrow'}, use_global_device_ids=true, to_apply=%add.4 | all-reduce | flops 16 | bytes 128
  77.5 1.9 collective-permute-start.7
  90.1 4.1 %all-to-all-start = ((f32[16,1,128]{2,1,0:T(1,128)}), f32[16,1,128]{2,1,0:T(1,128)}, u32[]{:S(2)}, u32[]{:S(2)}) async-start(f32[16,1,128]{2,1,0:T(1,128)} %broadcast_in_dim.260), calls=%async_computation | async-start | bytes 16384 | tf_op jit(solution)/shard_map/all_to_all | solution.py:193
  94.2 1.7 pad_maximum_fusion.38
  95.9 3.6 %collective-permute-start.2 = (f32[72,4,128]{2,0,1:T(8,128)}, f32[72,4,128]{2,0,1:T(8,128)}, u32[]{:S(2)}, u32[]{:S(2)}) collective-permute-start(f32[72,4,128]{2,0,1:T(8,128)} %get-tuple-element.33), channel_id=1, source_target_pairs={{0,1},{1,2},{2,3},{4,5},{5,6},{6,7},{8,9},{9,10},{10,11},{12,13},{... | collective-permute-start | bytes 442376 | tf_op jit(solution)/shard_map/ppermute | solution.py:22
  104.4 2.8 %cholesky.19 = f32[16,16]{1,0:T(8,128)} custom-call(f32[16,16]{1,0:T(8,128)} %fusion.221), custom_call_target="Cholesky" | custom-call | tf_op jit(solution)/shard_map/jit(cholesky)/cholesky | solution.py:200
  108.6 1.9 fusion.219
  110.5 2.5 %custom-call.9 = f32[1,16,16]{1,2,0:T(8,128)} custom-call(f32[1,16,16]{2,1,0:T(8,128)} %fusion.219), custom_call_target="InvertDiagBlocksLowerTriangular" | custom-call | tf_op jit(solution)/shard_map/jit(_cho_solve)/triangular_solve | solution.py:208
  115.3 2.9 %fusion = f32[72,40,128]{2,0,1:T(8,128)S(1)} fusion(f32[72,4,128]{2,0,1:T(8,128)} %collective-permute-done.3, f32[4,32,128]{2,0,1:T(4,128)} %collective-permute-done.1, f32[64,32,128]{2,0,1:T(8,128)} %copy-done.4, f32[4,32,128]{2,0,1:T(4,128)} %collective-permute-done, f32[72,4,128]{2,0,1:T(8,128)} %collective-permute-done.2, s32[72]{0:T(128)} %iota_add_fusion.4), kind=kOutput, calls=%fused_computation.8 | convolution fusion | flops 320031360 | bytes 2949408 | tf_op jit(solution)/shard_map/ai,ajk->ijk/dot_general | solution.py:90
  121.6 1.7 fusion.24
  124.9 2.9 %broadcast_multiply_fusion = (f32[64,32,128]{2,1,0:T(8,128)S(1)}, f32[64,32,128]{2,1,0:T(8,128)}) fusion(f32[]{:T(128)} %bitcast.41, s32[128]{0:T(128)S(1)} %copy-done.25, f32[72,40,128]{2,1,0:T(8,128)S(1)} %fusion.28), kind=kOutput, calls=%fused_computation.145 | convolution fusion | flops 403341312 | bytes 3277828 | tf_op jit(solution)/shard_map/ijc,ck->ijk/dot_general | solution.py:92
  129.4 4.0 %all-to-all-start.1 = ((f32[4,1,32,128]{3,2,1,0:T(8,128)}), f32[4,1,32,128]{3,2,1,0:T(8,128)S(1)}, u32[]{:S(2)}, u32[]{:S(2)}) async-start(f32[4,1,32,128]{3,2,1,0:T(8,128)} %broadcast_select_fusion.7), calls=%async_computation.1 | async-start | bytes 131072 | tf_op jit(solution)/shard_map/all_to_all | solution.py:36
  133.5 5.7 %all-to-all-done.1 = f32[4,1,32,128]{3,2,1,0:T(8,128)S(1)} async-done(((f32[4,1,32,128]{3,2,1,0:T(8,128)}), f32[4,1,32,128]{3,2,1,0:T(8,128)S(1)}, u32[]{:S(2)}, u32[]{:S(2)}) %all-to-all-start.1) | async-done | bytes 65568 | tf_op jit(solution)/shard_map/all_to_all | solution.py:36
  141.1 4.3 %all-to-all-start.2 = ((f32[4,66,1,128]{3,2,1,0:T(1,128)}), f32[4,66,1,128]{3,2,1,0:T(1,128)}, u32[]{:S(2)}, u32[]{:S(2)}) async-start(f32[4,66,1,128]{3,2,1,0:T(1,128)} %broadcast_select_fusion.1), calls=%async_computation.2 | async-start | bytes 270336 | tf_op jit(solution)/shard_map/all_to_all | solution.py:36
  146.4 4.2 %all-to-all-done.2 = f32[4,66,1,128]{3,2,1,0:T(1,128)} async-done(((f32[4,66,1,128]{3,2,1,0:T(1,128)}), f32[4,66,1,128]{3,2,1,0:T(1,128)}, u32[]{:S(2)}, u32[]{:S(2)}) %all-to-all-start.2) | async-done | bytes 135200 | tf_op jit(solution)/shard_map/all_to_all | solution.py:36
  151.5 12.7 %fusion.277 = (f32[]{:T(128)}, f32[64,32,128]{2,1,0:T(8,128)}, f32[64,32,128]{2,1,0:T(8,128)}, f32[64,32,128]{2,1,0:T(8,128)}, f32[64,32,128]{2,1,0:T(8,128)}, /*index=5*/f32[64,32,128]{2,1,0:T(8,128)}) fusion(f32[64,32,128]{2,1,0:T(8,128)} %param.11, f32[64,32,128]{2,1,0:T(8,128)} %copy-done.2, f32[64,32,128]{2,1,0:T(8,128)S(1)} %get-tuple-element.28, ...), kind=kLoop, calls=%fused_computation.400 | loop fusion | flops 16252927 | bytes 14819344 | tf_op jit(solution)/shard_map/reduce_sum | solution.py:206
  165.6 29.5 %all-reduce.5 = f32[16]{0:T(128)S(1)} all-reduce(f32[16]{0:T(128)S(1)} %dynamic-update-slice.4), channel_id=3, replica_groups=mesh['groups'=2,'wide'=4,'narrow'=4] {'wide','narrow'}, use_global_device_ids=true, to_apply=%add.5 | all-reduce | flops 16 | bytes 128
  199.1 4.3 %collective-permute-done.9 = f32[4,32,128]{2,1,0:T(8,128)S(1)} collective-permute-done((f32[4,32,128]{2,1,0:T(8,128)S(1)}, f32[4,32,128]{2,1,0:T(8,128)S(1)}, u32[]{:S(2)}, u32[]{:S(2)}) %collective-permute-start.9) | collective-permute-done | bytes 65568 | tf_op jit(solution)/shard_map/ppermute | solution.py:23
  209.3 1.7 fusion.20
  211.0 1.6 fusion.18
  214.3 1.7 fusion.16
  216.0 1.6 fusion.31
  217.7 2.2 fusion.40
  220.0 8.2 %all_to_all.25 = f32[4,1,32,128]{3,2,1,0:T(8,128)S(1)} all-to-all(f32[4,1,32,128]{3,2,1,0:T(8,128)S(1)} %broadcast_select_fusion.6), channel_id=1, replica_groups=mesh['groups'=2,'wide'=4,'narrow'=4] {'wide'}, dimensions={0} | all-to-all | bytes 131072 | tf_op jit(solution)/shard_map/all_to_all | solution.py:36
  228.5 9.2 %all_to_all.26 = f32[4,66,1,128]{3,2,1,0:T(1,128)S(1)} all-to-all(f32[4,66,1,128]{3,2,1,0:T(1,128)S(1)} %broadcast_select_fusion), channel_id=1, replica_groups=mesh['groups'=2,'wide'=4,'narrow'=4] {'narrow'}, dimensions={0} | all-to-all | bytes 270336 | tf_op jit(solution)/shard_map/all_to_all | solution.py:36
  237.8 5.4 %fusion.58 = f32[64,32,128]{2,1,0:T(8,128)} fusion(f32[64,32,128]{2,1,0:T(8,128)S(1)} %copy-done, f32[64,32,128]{2,1,0:T(8,128)S(1)} %fusion.40, f32[64,32,128]{2,1,0:T(8,128)S(1)} %copy-done.13, f32[66,1,128]{2,1,0:T(1,128)S(1)} %get-tuple-element.50, f32[1,32,128]{2,1,0:T(8,128)S(1)} %get-tuple-element.54, f32[1,32,128]{2,1,0:T(8,128)S(1)} %get-tuple-element.53, ...), kind=kLoop, calls=%fused_computation.65 | loop fusion | flops 9699328 | bytes 9275404 | tf_op jit(solution)/shard_map/sub | solution.py:143
  (157 shorter events, 55.2 us)
Async XLA Ops:
  0.6 9.6 %copy-start.26 = (f32[3]{0:T(128)S(1)}, f32[3]{0:T(128)}, u32[]{:S(2)}) copy-start(f32[3]{0:T(128)} %param.10) | copy-start | bytes 40
  0.6 10.2 %copy-start.24 = (f32[3,3]{1,0:T(4,128)S(1)}, f32[3,3]{1,0:T(4,128)}, u32[]{:S(2)}) copy-start(f32[3,3]{1,0:T(4,128)} %param.9) | copy-start | bytes 112
  0.6 10.9 %copy-start.14 = (s32[64,32,128]{2,1,0:T(8,128)S(1)}, s32[64,32,128]{2,1,0:T(8,128)}, u32[]{:S(2)}) copy-start(s32[64,32,128]{2,1,0:T(8,128)} %param.7) | copy-start | bytes 3145732
  2.6 12.0 %copy-start.4 = (f32[64,32,128]{2,0,1:T(8,128)}, f32[64,32,128]{2,0,1:T(8,128)S(1)}, u32[]{:S(2)}) copy-start(f32[64,32,128]{2,0,1:T(8,128)S(1)} %copy.29) | copy-start | bytes 3145732
  2.6 11.9 %copy-start.15 = (f32[64,32,128]{2,1,0:T(8,128)S(1)}, f32[64,32,128]{2,1,0:T(8,128)}, u32[]{:S(2)}) copy-start(f32[64,32,128]{2,1,0:T(8,128)} %param.8) | copy-start | bytes 3145732
  3.3 90.9 %collective-permute-start = (f32[4,32,128]{2,0,1:T(4,128)}, f32[4,32,128]{2,0,1:T(4,128)}, u32[]{:S(2)}, u32[]{:S(2)}) collective-permute-start(f32[4,32,128]{2,0,1:T(4,128)} %get-tuple-element.47), channel_id=1, source_target_pairs={{0,4},{4,8},{8,12},{1,5},{5,9},{9,13},{2,6},{6,10},{10,14},{3,7},{... | collective-permute-start | bytes 196616 | tf_op jit(solution)/shard_map/ppermute | solution.py:22
  8.9 85.2 %collective-permute-start.1 = (f32[4,32,128]{2,0,1:T(4,128)}, f32[4,32,128]{2,0,1:T(4,128)}, u32[]{:S(2)}, u32[]{:S(2)}) collective-permute-start(f32[4,32,128]{2,0,1:T(4,128)} %get-tuple-element.48), channel_id=1, source_target_pairs={{4,0},{8,4},{12,8},{5,1},{9,5},{13,9},{6,2},{10,6},{14,10},{7,3},{... | collective-permute-start | bytes 196616 | tf_op jit(solution)/shard_map/ppermute | solution.py:23
  23.3 52.8 %collective-permute-start.4 = (f32[3,1,32,128]{3,2,1,0:T(8,128)}, f32[3,1,32,128]{3,2,1,0:T(8,128)S(1)}, u32[]{:S(2)}, u32[]{:S(2)}) collective-permute-start(f32[3,1,32,128]{3,2,1,0:T(8,128)} %get-tuple-element.26), channel_id=1, source_target_pairs={{4,0},{8,4},{12,8},{5,1},{9,5},{13,9},{6,2},{10,6},{14,10},{7,3},{... | collective-permute-start | bytes 147464 | tf_op jit(solution)/shard_map/ppermute | solution.py:23
  24.6 51.5 %collective-permute-start.5 = (f32[3,1,32,128]{3,2,1,0:T(8,128)}, f32[3,1,32,128]{3,2,1,0:T(8,128)S(1)}, u32[]{:S(2)}, u32[]{:S(2)}) collective-permute-start(f32[3,1,32,128]{3,2,1,0:T(8,128)} %get-tuple-element.25), channel_id=1, source_target_pairs={{0,4},{4,8},{8,12},{1,5},{5,9},{9,13},{2,6},{6,10},{10,14},{3,7},{... | collective-permute-start | bytes 147464 | tf_op jit(solution)/shard_map/ppermute | solution.py:22
  77.5 9.2 %collective-permute-start.7 = (f32[3,66,1,128]{3,1,2,0:T(8,128)}, f32[3,66,1,128]{3,1,2,0:T(8,128)}, u32[]{:S(2)}, u32[]{:S(2)}) collective-permute-start(f32[3,66,1,128]{3,1,2,0:T(8,128)} %copy.50), channel_id=1, source_target_pairs={{0,1},{1,2},{2,3},{4,5},{5,6},{6,7},{8,9},{9,10},{10,11},{12,13},{... | collective-permute-start | bytes 304136 | tf_op jit(solution)/shard_map/ppermute | solution.py:22
  79.4 4.5 %collective-permute-start.6 = (f32[3,66,1,128]{3,2,1,0:T(1,128)}, f32[3,66,1,128]{3,2,1,0:T(1,128)}, u32[]{:S(2)}, u32[]{:S(2)}) collective-permute-start(f32[3,66,1,128]{3,2,1,0:T(1,128)} %get-tuple-element.24), channel_id=1, source_target_pairs={{1,0},{2,1},{3,2},{5,4},{6,5},{7,6},{9,8},{10,9},{11,10},{13,12},{... | collective-permute-start | bytes 304136 | tf_op jit(solution)/shard_map/ppermute | solution.py:23
  90.1 10.9 %all-to-all-start = ((f32[16,1,128]{2,1,0:T(1,128)}), f32[16,1,128]{2,1,0:T(1,128)}, u32[]{:S(2)}, u32[]{:S(2)}) async-start(f32[16,1,128]{2,1,0:T(1,128)} %broadcast_in_dim.260), calls=%async_computation | async-start | bytes 16384 | tf_op jit(solution)/shard_map/all_to_all | solution.py:193
  95.9 19.4 %collective-permute-start.2 = (f32[72,4,128]{2,0,1:T(8,128)}, f32[72,4,128]{2,0,1:T(8,128)}, u32[]{:S(2)}, u32[]{:S(2)}) collective-permute-start(f32[72,4,128]{2,0,1:T(8,128)} %get-tuple-element.33), channel_id=1, source_target_pairs={{0,1},{1,2},{2,3},{4,5},{5,6},{6,7},{8,9},{9,10},{10,11},{12,13},{... | collective-permute-start | bytes 442376 | tf_op jit(solution)/shard_map/ppermute | solution.py:22
  99.4 15.8 %collective-permute-start.3 = (f32[72,4,128]{2,0,1:T(8,128)S(1)}, f32[72,4,128]{2,0,1:T(8,128)}, u32[]{:S(2)}, u32[]{:S(2)}) collective-permute-start(f32[72,4,128]{2,0,1:T(8,128)S(1)} %get-tuple-element.34), channel_id=1, source_target_pairs={{1,0},{2,1},{3,2},{5,4},{6,5},{7,6},{9,8},{10,9},{11,10},{13,12},{... | collective-permute-start | bytes 442376 | tf_op jit(solution)/shard_map/ppermute | solution.py:23
  129.4 9.8 %all-to-all-start.1 = ((f32[4,1,32,128]{3,2,1,0:T(8,128)}), f32[4,1,32,128]{3,2,1,0:T(8,128)S(1)}, u32[]{:S(2)}, u32[]{:S(2)}) async-start(f32[4,1,32,128]{3,2,1,0:T(8,128)} %broadcast_select_fusion.7), calls=%async_computation.1 | async-start | bytes 131072 | tf_op jit(solution)/shard_map/all_to_all | solution.py:36
  133.5 12.0 %copy-start.28 = (pred[4]{0:T(512)(128)(4,1)}, pred[4]{0:T(512)(128)(4,1)S(1)}, u32[]{:S(2)}) copy-start(pred[4]{0:T(512)(128)(4,1)S(1)} %iota_compare_fusion.7) | copy-start | bytes 16
  141.1 9.5 %all-to-all-start.2 = ((f32[4,66,1,128]{3,2,1,0:T(1,128)}), f32[4,66,1,128]{3,2,1,0:T(1,128)}, u32[]{:S(2)}, u32[]{:S(2)}) async-start(f32[4,66,1,128]{3,2,1,0:T(1,128)} %broadcast_select_fusion.1), calls=%async_computation.2 | async-start | bytes 270336 | tf_op jit(solution)/shard_map/all_to_all | solution.py:36
  164.2 43.1 %copy-start.18 = (f32[1,16,16]{1,2,0:T(8,128)S(1)}, f32[1,16,16]{1,2,0:T(8,128)}, u32[]{:S(2)}) copy-start(f32[1,16,16]{1,2,0:T(8,128)} %custom-call.9) | copy-start | bytes 3076
  164.2 44.9 %copy-start.1 = (f32[64,32,128]{2,1,0:T(8,128)S(1)}, f32[64,32,128]{2,1,0:T(8,128)}, u32[]{:S(2)}) copy-start(f32[64,32,128]{2,1,0:T(8,128)} %get-tuple-element.8) | copy-start | bytes 3145732
  195.9 3.2 %collective-permute-start.8 = (f32[4,32,128]{2,1,0:T(8,128)S(1)}, f32[4,32,128]{2,1,0:T(8,128)S(1)}, u32[]{:S(2)}, u32[]{:S(2)}) collective-permute-start(f32[4,32,128]{2,1,0:T(8,128)S(1)} %get-tuple-element.41), channel_id=1, source_target_pairs={{0,4},{4,8},{8,12},{1,5},{5,9},{9,13},{2,6},{6,10},{10,14},{3,7},{... | collective-permute-start | bytes 196616 | tf_op jit(solution)/shard_map/ppermute | solution.py:22
  197.2 6.2 %collective-permute-start.9 = (f32[4,32,128]{2,1,0:T(8,128)S(1)}, f32[4,32,128]{2,1,0:T(8,128)S(1)}, u32[]{:S(2)}, u32[]{:S(2)}) collective-permute-start(f32[4,32,128]{2,1,0:T(8,128)S(1)} %get-tuple-element.42), channel_id=1, source_target_pairs={{4,0},{8,4},{12,8},{5,1},{9,5},{13,9},{6,2},{10,6},{14,10},{7,3},{... | collective-permute-start | bytes 196616 | tf_op jit(solution)/shard_map/ppermute | solution.py:23
  204.5 3.7 %collective-permute-start.10 = (f32[72,4,128]{2,1,0:T(4,128)S(1)}, f32[72,4,128]{2,1,0:T(4,128)S(1)}, u32[]{:S(2)}, u32[]{:S(2)}) collective-permute-start(f32[72,4,128]{2,1,0:T(4,128)S(1)} %get-tuple-element.31), channel_id=1, source_target_pairs={{0,1},{1,2},{2,3},{4,5},{5,6},{6,7},{8,9},{9,10},{10,11},{12,13},{... | collective-permute-start | bytes 442376 | tf_op jit(solution)/shard_map/ppermute | solution.py:22
  205.8 3.3 %collective-permute-start.11 = (f32[72,4,128]{2,1,0:T(4,128)S(1)}, f32[72,4,128]{2,1,0:T(4,128)S(1)}, u32[]{:S(2)}, u32[]{:S(2)}) collective-permute-start(f32[72,4,128]{2,1,0:T(4,128)S(1)} %get-tuple-element.32), channel_id=1, source_target_pairs={{1,0},{2,1},{3,2},{5,4},{6,5},{7,6},{9,8},{10,9},{11,10},{13,12},{... | collective-permute-start | bytes 442376 | tf_op jit(solution)/shard_map/ppermute | solution.py:23
  216.0 21.7 %copy-start.13 = (f32[64,32,128]{2,1,0:T(8,128)S(1)}, f32[64,32,128]{2,1,0:T(8,128)}, u32[]{:S(2)}) copy-start(f32[64,32,128]{2,1,0:T(8,128)} %get-tuple-element.12) | copy-start | bytes 3145732
  217.7 20.1 %copy-start.10 = (f32[64,32,128]{2,1,0:T(8,128)S(1)}, f32[64,32,128]{2,1,0:T(8,128)}, u32[]{:S(2)}) copy-start(f32[64,32,128]{2,1,0:T(8,128)} %get-tuple-element.9) | copy-start | bytes 3145732
  217.7 20.1 %copy-start.11 = (f32[64,32,128]{2,1,0:T(8,128)S(1)}, f32[64,32,128]{2,1,0:T(8,128)}, u32[]{:S(2)}) copy-start(f32[64,32,128]{2,1,0:T(8,128)} %get-tuple-element.10) | copy-start | bytes 3145732
  217.7 20.1 %copy-start.12 = (f32[64,32,128]{2,1,0:T(8,128)S(1)}, f32[64,32,128]{2,1,0:T(8,128)}, u32[]{:S(2)}) copy-start(f32[64,32,128]{2,1,0:T(8,128)} %get-tuple-element.11) | copy-start | bytes 3145732
  219.9 23.3 %copy-start.3 = (f32[64,32,128]{2,1,0:T(8,128)}, f32[64,32,128]{2,1,0:T(8,128)S(1)}, u32[]{:S(2)}) copy-start(f32[64,32,128]{2,1,0:T(8,128)S(1)} %fusion.40) | copy-start | bytes 3145732
  219.9 8.5 %copy-start.29 = (pred[4]{0:T(512)(128)(4,1)S(1)}, pred[4]{0:T(512)(128)(4,1)}, u32[]{:S(2)}) copy-start(pred[4]{0:T(512)(128)(4,1)} %copy-done.28) | copy-start | bytes 16
  219.9 17.9 %copy-start = (f32[64,32,128]{2,1,0:T(8,128)S(1)}, f32[64,32,128]{2,1,0:T(8,128)}, u32[]{:S(2)}) copy-start(f32[64,32,128]{2,1,0:T(8,128)} %param.11) | copy-start | bytes 3145732
  219.9 17.9 %copy-start.6 = (pred[64,32,128]{2,1,0:T(8,128)(4,1)S(1)}, pred[64,32,128]{2,1,0:T(8,128)(4,1)}, u32[]{:S(2)}) copy-start(pred[64,32,128]{2,1,0:T(8,128)(4,1)} %copy-done.5) | copy-start | bytes 786436
  219.9 17.9 %copy-start.8 = (pred[64,32,128]{2,1,0:T(8,128)(4,1)S(1)}, pred[64,32,128]{2,1,0:T(8,128)(4,1)}, u32[]{:S(2)}) copy-start(pred[64,32,128]{2,1,0:T(8,128)(4,1)} %copy-done.7) | copy-start | bytes 786436
  (16 other events, 52.9 us)

commit v2 on v0

v2 whole, which is shorter than its diff:
```python
import functools

import jax
import jax.numpy as jnp
import numpy as np
from jax import lax
from jax.experimental import pallas as pl
from jax.experimental.pallas import tpu as pltpu
from jax.sharding import PartitionSpec as P

MARGIN = 4
REACH = MARGIN + 1
EDGE = 8

precise = lax.Precision.HIGHEST
cheb_center = 1.3
cheb_radius = 1.2
cheb_ratio = 1.3 / 1.2
rho_first = 1.0 / cheb_ratio
rho_second = 1.0 / (2.0 * cheb_ratio - rho_first)

DIAGONAL, LONG_HIGH, LONG_LOW, ACROSS_HIGH, ACROSS_LOW, LOAD_SUM, IMAGE_SUM = range(7)
FLOW_LONG_HIGH, FLOW_LONG_LOW, FLOW_ACROSS_HIGH, FLOW_ACROSS_LOW = range(7, 11)
MEANS = range(11, 15)

VMEM = pl.BlockSpec(memory_space=pltpu.VMEM)
SMEM = pl.BlockSpec(memory_space=pltpu.SMEM)


def sine_basis(length):
    indices = np.arange(1, length + 1)
    phases = indices[:, None] * indices[None, :] % (2 * (length + 1))
    table = np.sqrt(2.0 / (length + 1)) * np.sin(np.pi * phases / (length + 1))
    eigvals = 4.0 * np.sin(np.pi * indices / (2.0 * (length + 1))) ** 2
    return table.astype(np.float32), eigvals.astype(np.float32)


def call(body, out_shape, in_specs, scratch=(), flops=0, moved=0):
    return pl.pallas_call(
        body,
        out_shape=out_shape,
        in_specs=in_specs,
        out_specs=jax.tree.map(lambda _: VMEM, out_shape),
        scratch_shapes=list(scratch),
        compiler_params=pltpu.CompilerParams(vmem_limit_bytes=30 * 2**20),
        cost_estimate=pl.CostEstimate(flops=flops, bytes_accessed=moved, transcendentals=0),
    )


def f32(*shape):
    return jax.ShapeDtypeStruct(shape, jnp.float32)


def dot(left, right):
    return lax.dot_general(
        left, right, (((1,), (0,)), ((), ())), precision=precise, preferred_element_type=jnp.float32
    )


class Box:
    def __init__(self, shape):
        self.long, self.across, self.deep = shape
        self.ex = self.long + 2 * MARGIN
        self.ey = self.across + 2 * MARGIN
        self.rows = self.long + 2 * REACH
        self.cols = self.across + 2 * EDGE
        self.flat = self.rows * self.cols


def tables_of(box):
    sine_x, eig_x = sine_basis(box.ex)
    sine_y, eig_y = sine_basis(box.ey)
    sine_z, eig_z = sine_basis(box.deep)
    skip = EDGE - MARGIN
    into_y = np.zeros((box.ey, box.cols), np.float32)
    into_y[:, skip : skip + box.ey] = sine_y
    from_y = sine_y[MARGIN : MARGIN + box.across]
    from_x = sine_x[MARGIN : MARGIN + box.long]
    spread = np.broadcast_to(eig_x[:, None], (box.ex, box.deep))
    return [
        jnp.asarray(np.ascontiguousarray(t))
        for t in (into_y, sine_x, from_x, from_y, sine_z, spread, eig_z[None, :], eig_y[None, :])
    ]


def box_solve(box, source, means, tables, row_mask, col_mask, spectral, middle, emit):
    into_y, into_x, from_x, from_y, sine_z, spread, eig_z, eig_y = tables
    deep = box.deep
    into_y = into_y[...] * col_mask
    into_x = into_x[...] * row_mask
    from_x, from_y, sine_z = from_x[...], from_y[...], sine_z[...]
    spectral_flat = spectral.reshape(box.ey * box.ex, deep)
    middle_flat = middle.reshape(box.long * box.ey, deep)
    for start in range(0, box.ex, 8):
        block = source[start : start + 8].reshape(8 * box.cols, deep)
        block = dot(block, sine_z).reshape(8, box.cols, deep)
        for row in range(0, 8, 2):
            pair = jnp.concatenate([block[row], block[row + 1]], axis=1)
            pair = dot(into_y, pair)
            for part in range(2):
                spectral_flat[pl.ds(start + row + part, box.ey, stride=box.ex), :] = pair[
                    :, part * deep : (part + 1) * deep
                ]
    base = means[3] + means[0] * spread[...] + means[2] * eig_z[...]
    for col in range(0, box.ey, 2):
        pair = jnp.concatenate([spectral[col], spectral[col + 1]], axis=1)
        pair = dot(into_x, pair)
        pair = jnp.concatenate(
            [
                pair[:, part * deep : (part + 1) * deep]
                / (base + means[1] * eig_y[0, col + part])
                for part in range(2)
            ],
            axis=1,
        )
        pair = dot(from_x, pair)
        for part in range(2):
            middle_flat[pl.ds(col + part, box.long, stride=box.ey), :] = pair[
                :, part * deep : (part + 1) * deep
            ]
    for start in range(0, box.long, 8):
        parts = []
        for row in range(start, start + 8, 2):
            pair = jnp.concatenate([middle[row], middle[row + 1]], axis=1)
            pair = dot(from_y, pair)
            parts += [pair[:, :deep], pair[:, deep:]]
        emit(start, dot(jnp.concatenate(parts, axis=0), sine_z))


def position():
    long_pos, across_pos = lax.axis_index("wide"), lax.axis_index("narrow")
    return long_pos, across_pos, lax.axis_size("wide"), lax.axis_size("narrow")


def as_float(flag):
    return jnp.where(flag, jnp.float32(1.0), jnp.float32(0.0))


def row_of(stride, col, count, first=0):
    return pl.ds(first * stride + col, count, stride=stride)


def widths():
    return (MARGIN, REACH, REACH)


def pack_columns(box, fields, lows, highs, wides, up, down):
    total = sum(wides)
    corner = total * box.long
    place = 0
    for field, low, high, wide in zip(fields, lows, highs, wides):
        for step in range(wide):
            for target, col in ((up, box.across - wide + step), (down, step)):
                values = field[row_of(box.across, col, box.long), :]
                target[place * box.long : (place + 1) * box.long, :] = values.astype(jnp.float32)
                at = corner + 2 * REACH * place
                target[at : at + wide, :] = low[row_of(box.across, col, wide), :]
                target[at + REACH : at + REACH + wide, :] = high[row_of(box.across, col, wide), :]
            place += 1


def message_rows(box, wides):
    total = sum(wides)
    return -(-(total * (box.long + 2 * REACH)) // 8) * 8


def pack_inputs(box, zone, scale, load, low, high, up, down):
    edges = np.cumsum((0,) + widths())

    def part(ref, index):
        size = widths()[index] * box.across
        start = int(edges[index]) * box.across
        return ref.reshape(sum(widths()) * box.across, box.deep).at[start : start + size]

    flat = [ref.reshape(box.long * box.across, box.deep) for ref in (load, scale, zone)]
    lows = [part(low, index) for index in range(3)]
    highs = [part(high, index) for index in range(3)]
    pack_columns(box, flat, lows, highs, widths(), up, down)


def fill_window(box, window, own, low, high, left, right, wide, place, total, add=None):
    flat = window.reshape(box.flat, box.deep)
    nothing = jnp.zeros((box.rows, EDGE, box.deep), jnp.float32)
    window[:, :EDGE, :] = nothing
    window[:, EDGE + box.across :, :] = nothing
    if add is None:
        add = lambda values, row_side, col_side: values
    inner = slice(EDGE, EDGE + box.across)
    first, last = REACH, REACH + box.long
    if wide < REACH:
        blank = jnp.zeros((1, box.across, box.deep), jnp.float32)
        window[0:1, inner, :] = blank
        window[box.rows - 1 :, inner, :] = blank
    window[first:last, inner, :] = add(own[...].astype(jnp.float32), 0, 0)
    window[first - wide : first, inner, :] = add(low, -1, 0)
    window[last : last + wide, inner, :] = add(high, 1, 0)
    corner = total * box.long
    for step in range(wide):
        for source, col, side in (
            (left, EDGE - wide + step, -1),
            (right, EDGE + box.across + step, 1),
        ):
            at = (place + step) * box.long
            values = source[at : at + box.long, :]
            flat[row_of(box.cols, col, box.long, first), :] = add(values, 0, side)
            at = corner + 2 * REACH * (place + step)
            values = source[at : at + wide, :]
            flat[row_of(box.cols, col, wide, first - wide), :] = add(values, -1, side)
            values = source[at + REACH : at + REACH + wide, :]
            flat[row_of(box.cols, col, wide, last), :] = add(values, 1, side)


def negative_image(row, x, x_next, flow_before, weights):
    to_long, to_across, to_deep, mass = weights
    rows, lanes = x.shape
    flow_long = to_long[row] * (x_next - x)
    flow_across = to_across[row] * (pltpu.roll(x, rows - 1, 0) - x)
    flow_deep = to_deep[row] * (pltpu.roll(x, lanes - 1, 1) - x)
    total = flow_long - flow_before - mass[row] * x
    total = total + (flow_across - pltpu.roll(flow_across, 1, 0))
    total = total + (flow_deep - pltpu.roll(flow_deep, 1, 1))
    return total, flow_long


def first_solve(
    box,
    zone,
    scale,
    load,
    low,
    high,
    left,
    right,
    diffusivity,
    decay,
    *rest,
):
    tables = rest[:8]
    to_long, to_across, to_deep, mass, load_window, local, told = rest[8:15]
    zone_window, scale_window, spectral, middle = rest[15:]
    wides = widths()
    total = sum(wides)
    places = np.cumsum((0,) + wides)
    own = (load, scale, zone)
    for index, window in enumerate((load_window, scale_window, zone_window)):
        part = slice(int(places[index]), int(places[index + 1]))
        fill_window(
            box, window, own[index], low[part], high[part], left, right, wides[index], part.start, total
        )
    half = [[0.5 * diffusivity[z, d] for d in range(3)] for z in range(3)]
    rates = [decay[z] for z in range(3)]
    lane = lax.broadcasted_iota(jnp.int32, (box.cols, box.deep), 1)
    ends = jnp.where((lane == 0) | (lane == box.deep - 1), jnp.float32(1.0), jnp.float32(0.0))
    not_last = jnp.where(lane == box.deep - 1, jnp.float32(0.0), jnp.float32(1.0))

    def looked_up(labels, values):
        return jnp.where(labels == 0.0, values[0], jnp.where(labels == 1.0, values[1], values[2]))

    def halves(row):
        labels, factor = zone_window[row], scale_window[row]
        return [looked_up(labels, [half[z][d] for z in range(3)]) * factor for d in range(3)] + [
            looked_up(labels, rates)
        ]

    def set_row(row, own_halves, next_long):
        to_long[row] = own_halves[0] + next_long
        to_across[row] = own_halves[1] + pltpu.roll(own_halves[1], box.cols - 1, 0)
        to_deep[row] = (own_halves[2] + pltpu.roll(own_halves[2], box.deep - 1, 1)) * not_last
        mass[row] = own_halves[3] + own_halves[2] * ends

    def plain_row(row, now):
        later = halves(row + 1)
        set_row(row, now, later[0])
        return later

    def own_row(row, carry):
        now, sums = carry
        later = plain_row(row, now)
        inner = slice(EDGE, EDGE + box.across)
        sums = [s + v[inner] for s, v in zip(sums, now)]
        return later, sums

    first, last = REACH, REACH + box.long
    now = lax.fori_loop(0, first, plain_row, halves(0))
    nothing = jnp.zeros((box.across, box.deep), jnp.float32)
    now, sums = lax.fori_loop(first, last, own_row, (now, [nothing] * 4))
    now = lax.fori_loop(last, box.rows - 1, plain_row, now)
    set_row(box.rows - 1, now, jnp.zeros_like(now[0]))
    cells = box.long * box.across * box.deep
    totals = [jnp.sum(s, keepdims=True) for s in sums]
    means = [2.0 * t / cells for t in totals[:3]] + [totals[3] / cells]

    one = jnp.ones((1, 1), jnp.float32)
    collected = [jnp.zeros((8 * box.across, box.deep), jnp.float32)]

    def emit(start, values):
        values = values * (1.0 / cheb_center)
        rows = values.reshape(8, box.across, box.deep)
        local[start : start + 8] = rows
        own_mass = mass[first + start : first + start + 8, EDGE : EDGE + box.across, :]
        collected[0] = collected[0] + values * own_mass.reshape(values.shape)

    box_solve(
        box,
        load_window.at[1 : 1 + box.ex],
        means,
        tables,
        one,
        one,
        spectral,
        middle,
        emit,
    )
    long_pos, across_pos, long_count, across_count = position()
    has = [
        as_float(long_pos < long_count - 1),
        as_float(long_pos > 0),
        as_float(across_pos < across_count - 1),
        as_float(across_pos > 0),
    ]
    inner = slice(EDGE, EDGE + box.across)
    across_flat = to_across.reshape(box.flat, box.deep)
    local_flat = local.reshape(box.long * box.across, box.deep)
    faces = [
        (to_long[last - 1, inner], local[box.long - 1]),
        (to_long[first - 1, inner], local[0]),
        (
            across_flat[row_of(box.cols, EDGE + box.across - 1, box.long, first), :],
            local_flat[row_of(box.across, box.across - 1, box.long), :],
        ),
        (
            across_flat[row_of(box.cols, EDGE - 1, box.long, first), :],
            local_flat[row_of(box.across, 0, box.long), :],
        ),
    ]
    weights = [jnp.sum(w, keepdims=True) for w, _ in faces]
    flows = [jnp.sum(w * v, keepdims=True) for w, v in faces]
    own_mass = mass[first:last, inner, :]
    numbers = [jnp.sum(own_mass, keepdims=True).reshape(1, 1) + sum(weights)]
    numbers += [w * h for w, h in zip(weights, has)]
    numbers += [jnp.sum(load[...], keepdims=True).reshape(1, 1)]
    numbers += [jnp.sum(collected[0], keepdims=True) + sum(flows)]
    numbers += [f * h for f, h in zip(flows, has)]
    numbers += means
    lanes = lax.broadcasted_iota(jnp.int32, told.shape, 1)
    line = jnp.zeros(told.shape, jnp.float32)
    for index, number in enumerate(numbers):
        line = jnp.where(lanes == index, number, line)
    told[...] = line


def pack_iterate(box, own, low, high, up, down):
    flat = [own.reshape(box.long * box.across, box.deep)]
    low = low.reshape(REACH * box.across, box.deep)
    high = high.reshape(REACH * box.across, box.deep)
    pack_columns(box, flat, [low], [high], (REACH,), up, down)


def coarse_solve(told, answers, solved):
    count, width = solved.shape
    across = lax.axis_size("narrow")
    numbers = told[...]

    def column(index, values=numbers):
        return values[:, index : index + 1]

    image = column(IMAGE_SUM)
    image = image - column(FLOW_LONG_LOW, pltpu.roll(numbers, count - across, 0))
    image = image - column(FLOW_LONG_HIGH, pltpu.roll(numbers, across, 0))
    image = image - column(FLOW_ACROSS_LOW, pltpu.roll(numbers, count - 1, 0))
    image = image - column(FLOW_ACROSS_HIGH, pltpu.roll(numbers, 1, 0))
    rows = lax.broadcasted_iota(jnp.int32, (count, width), 0)
    cols = lax.broadcasted_iota(jnp.int32, (count, width), 1)
    nothing = jnp.zeros((count, width), jnp.float32)
    matrix = jnp.where(cols == rows, column(DIAGONAL), nothing)
    matrix = matrix - jnp.where(cols == rows + across, column(LONG_HIGH), nothing)
    matrix = matrix - jnp.where(cols == rows - across, column(LONG_LOW), nothing)
    matrix = matrix - jnp.where(cols == rows + 1, column(ACROSS_HIGH), nothing)
    matrix = matrix - jnp.where(cols == rows - 1, column(ACROSS_LOW), nothing)
    matrix = jnp.where(cols == count, column(LOAD_SUM), matrix)
    matrix = jnp.where(cols == count + 1, image, matrix)
    solved[...] = matrix

    def eliminate(step, _):
        values = solved[...]
        pivot_row = solved[pl.ds(step, 1), :]
        at_step = cols == step
        factors = jnp.sum(jnp.where(at_step, values, nothing), axis=1, keepdims=True)
        pivot = jnp.sum(jnp.where(at_step[:1], pivot_row, nothing[:1]), axis=1, keepdims=True)
        pivot_row = pivot_row / pivot
        solved[...] = jnp.where(rows == step, pivot_row, values - factors * pivot_row)
        return 0

    lax.fori_loop(0, count, eliminate, 0)
    values = solved[...]
    lanes = lax.broadcasted_iota(jnp.int32, answers.shape, 1)
    answers[...] = jnp.where(
        lanes == 0, values[:, count : count + 1], values[:, count + 1 : count + 2]
    )


def second_solve(box, local, low, high, left, right, solved, told, *rest):
    to_long, to_across, to_deep, mass, load_window = rest[:5]
    tables = rest[5:13]
    iterate, top, bottom, last_col, first_col = rest[13:18]
    window, residual, spectral, middle = rest[18:]
    long_pos, across_pos, long_count, across_count = position()
    count = long_count * across_count
    own_box = long_pos * across_count + across_pos

    def coarse(row_side, col_side, lane):
        there_long, there_across = long_pos + row_side, across_pos + col_side
        inside = (
            (there_long >= 0)
            & (there_long < long_count)
            & (there_across >= 0)
            & (there_across < across_count)
        )
        place = jnp.clip(there_long * across_count + there_across, 0, count - 1)
        return solved[pl.ds(place, 1), lane : lane + 1] * as_float(inside)

    shifts = {
        (row_side, col_side): coarse(row_side, col_side, 0) * (1.0 / cheb_center)
        for row_side in (-1, 0, 1)
        for col_side in (-1, 0, 1)
    }

    def add(values, row_side, col_side):
        shift = shifts[row_side, col_side]
        if values.ndim == 3:
            shift = shift.reshape(1, 1, 1)
        return values + shift

    fill_window(box, window, local, low[...], high[...], left, right, REACH, 0, REACH, add)
    weights = (to_long, to_across, to_deep, mass)

    def one_row(row, flow):
        image, flow = negative_image(row, window[row], window[row + 1], flow, weights)
        residual[row - 1] = load_window[row] + image
        return flow

    flow = to_long[0] * (window[1] - window[0])
    lax.fori_loop(1, 1 + box.ex, one_row, flow)
    inner = slice(EDGE, EDGE + box.across)
    first = REACH
    means = [told[0:1, index : index + 1] for index in MEANS]
    row_ids = lax.broadcasted_iota(jnp.int32, (1, box.ex), 1)
    col_ids = lax.broadcasted_iota(jnp.int32, (1, box.cols), 1)
    row_mask = jnp.where(row_ids < MARGIN, as_float(long_pos > 0), 1.0)
    row_mask = jnp.where(row_ids >= MARGIN + box.long, as_float(long_pos < long_count - 1), row_mask)
    col_mask = jnp.where(col_ids < EDGE, as_float(across_pos > 0), 1.0)
    col_mask = jnp.where(
        col_ids >= EDGE + box.across, as_float(across_pos < across_count - 1), col_mask
    )
    own_c = coarse(0, 0, 0) * (1.0 - 1.0 / cheb_center) - coarse(0, 0, 1)
    keep = 1.0 + rho_second * rho_first
    gain = 2.0 * rho_second / cheb_radius

    def emit(start, values):
        rows = (values + own_c).reshape(8, box.across, box.deep)
        before = window[first + start : first + start + 8, inner, :]
        iterate[start : start + 8] = keep * before + gain * rows

    box_solve(box, residual, means, tables, row_mask, col_mask, spectral, middle, emit)
    top[...] = iterate[box.long - 1]
    bottom[...] = iterate[0]
    flat = iterate.reshape(box.long * box.across, box.deep)
    last_col[...] = flat[row_of(box.across, box.across - 1, box.long), :]
    first_col[...] = flat[row_of(box.across, 0, box.long), :]


def last_residual(box, load, iterate, low, high, left, right, to_long, to_across, to_deep, mass, out):
    first = REACH
    left_col, right_col = left[...], right[...]
    rows = lax.broadcasted_iota(jnp.int32, (box.cols, box.deep), 0)
    inner = slice(EDGE, EDGE + box.across)
    blank = jnp.zeros((EDGE, box.deep), jnp.float32)
    weights = (to_long, to_across, to_deep, mass)

    def padded(values):
        return jnp.concatenate([blank, values, blank], axis=0)

    def own(row):
        values = padded(iterate[row])
        values = jnp.where(rows == EDGE - 1, left[pl.ds(row, 1), :], values)
        return jnp.where(rows == EDGE + box.across, right[pl.ds(row, 1), :], values)

    def one_row(row, carry):
        now, flow = carry
        later = own(row + 1)
        image, flow = negative_image(first + row, now, later, flow, weights)
        out[row] = load[row] + image[inner]
        return later, flow

    now = own(0)
    flow = to_long[first - 1] * (now - padded(low[...]))
    now, flow = lax.fori_loop(0, box.long - 1, one_row, (now, flow))
    row = box.long - 1
    image, _ = negative_image(first + row, now, padded(high[...]), flow, weights)
    out[row] = load[row] + image[inner]


def exchange(axis, last, first):
    size = lax.axis_size(axis)
    up = [(i, i + 1) for i in range(size - 1)]
    down = [(j, i) for i, j in up]
    return lax.ppermute(last, axis, up), lax.ppermute(first, axis, down)


def on_device(zone, scale, diffusivity, decay, load):
    box = Box(load.shape)
    long, across, deep = load.shape
    count = lax.axis_size("wide") * lax.axis_size("narrow")
    tables = tables_of(box)
    wides = widths()

    def edge(high):
        parts = []
        for field, wide in zip((load, scale, zone), wides):
            start = long - wide if high else 0
            parts.append(lax.slice_in_dim(field, start, start + wide, axis=0).astype(jnp.float32))
        return jnp.concatenate(parts, axis=0)

    low, high = exchange("wide", edge(True), edge(False))
    message = f32(message_rows(box, wides), deep)
    up, down = call(
        functools.partial(pack_inputs, box), (message, message), [VMEM] * 5
    )(zone, scale, load, low, high)
    left, right = exchange("narrow", up, down)
    window = f32(box.rows, box.cols, deep)
    window_scratch = pltpu.VMEM(window.shape, jnp.float32)
    spectral = pltpu.VMEM((box.ey, box.ex, deep), jnp.float32)
    middle = pltpu.VMEM((box.long, box.ey, deep), jnp.float32)
    to_long, to_across, to_deep, mass, load_window, local, told = call(
        functools.partial(first_solve, box),
        (window,) * 5 + (f32(long, across, deep), f32(count, 128)),
        [VMEM] * 7 + [SMEM] * 2 + [VMEM] * 8,
        [window_scratch] * 2 + [spectral, middle],
    )(zone, scale, load, low, high, left, right, diffusivity, decay, *tables)
    low, high = exchange("wide", local[long - REACH :], local[:REACH])
    all_told = lax.all_to_all(
        told.reshape(count, 1, 128), ("wide", "narrow"), split_axis=0, concat_axis=0, tiled=True
    ).reshape(count, 128)
    message = f32(message_rows(box, (REACH,)), deep)
    up, down = call(
        functools.partial(pack_iterate, box), (message, message), [VMEM] * 3
    )(local, low, high)
    left, right = exchange("narrow", up, down)
    solved_width = -(-(count + 2) // 128) * 128
    solved = call(
        coarse_solve,
        f32(count, 128),
        [VMEM],
        [pltpu.VMEM((count, solved_width), jnp.float32)],
    )(all_told)
    iterate, top, bottom, last_col, first_col = call(
        functools.partial(second_solve, box),
        (
            f32(long, across, deep),
            f32(across, deep),
            f32(across, deep),
            f32(long, deep),
            f32(long, deep),
        ),
        [VMEM] * 20,
        [window_scratch, pltpu.VMEM((box.ex, box.cols, deep), jnp.float32), spectral, middle],
    )(
        local,
        low,
        high,
        left,
        right,
        solved,
        told,
        to_long,
        to_across,
        to_deep,
        mass,
        load_window,
        *tables,
    )
    low, high = exchange("wide", top, bottom)
    left, right = exchange("narrow", last_col, first_col)
    residual = call(
        functools.partial(last_residual, box), f32(long, across, deep), [VMEM] * 10
    )(load, iterate, low, high, left, right, to_long, to_across, to_deep, mass)
    return iterate, residual


def solution(mesh):
    split = P(("groups", "wide"), "narrow", None)
    return jax.shard_map(
        on_device,
        mesh=mesh,
        in_specs=(split, split, P(), P(), split),
        out_specs=(split, split),
        check_vma=False,
    )
```

time: 213 us -> 133 us (0.62)
  Pallas kernels: 0 us -> 60.9 us
  blocking collectives: 62.4 us -> 14.6 us
  other arithmetic: 42.7 us -> 0.98 us
  matrix products: 23.3 us -> 0 us
  starting transfers between devices: 53.4 us -> 31.1 us
  waiting for transfers between devices: 4.79 us -> 18.2 us
  between operations: 10.1 us -> 0.97 us
  local copies, waits for them, and re-layouts: 13.7 us -> 5.67 us
    unnamed x2 -> x0, blocking collectives: 62.4 us -> none
    pallas_call x0 -> x6, Pallas kernels: none -> 60.9 us  [the longest x1 25.9 us: on_device(): call(functools.partial(second_solve, box), (f32(long, across, deep), f32(...]
    reduce_sum x8 -> x0, other arithmetic: 25.1 us -> none  [the longest x2 10.5 us: coarse_value(): jnp.sum(own_part).reshape(1)]
    dot_general x12 -> x0, matrix products: 22.8 us -> none  [the longest x4 8.29 us: transform(): return jnp.einsum('ijc,ck->ijk', spectral, tables[2][0], precision=precise)]
    ppermute x20 -> x12, starting transfers between devices: 53.4 us -> 31.1 us  [exchange(): return (lax.ppermute(last, axis, up), lax.ppermute(first, axis, down))]
    all_to_all x0 -> x1, blocking collectives: none -> 14.6 us  [on_device(): lax.all_to_all(told.reshape(count, 1, 128), ('wide', 'narrow'), split_axi...]
    ppermute x20 -> x12, waiting for transfers between devices: 4.79 us -> 18.2 us  [exchange(): return (lax.ppermute(last, axis, up), lax.ppermute(first, axis, down))]
    sub x1 -> x0, other arithmetic: 5.45 us -> none  [final_residual(): return load_field - operate(window, cond_window, mass_term)]
  transfers between devices with their start and end apart: 20 -> 12, of which waited for: 4 -> 8; matrix products, arithmetic and copies ran while one was open for 18% -> 0% of each run, Pallas kernels for 0% -> 1%
where the time goes in v2:
time: 133 us; the launch traced here: 132 us
  Pallas kernels  60.9 us (46%)
  starting transfers between devices  31.1 us (23%)
  waiting for transfers between devices  18.2 us (14%)
  blocking collectives  14.6 us (11%)
  local copies, waits for them, and re-layouts  5.67 us (4%)
    ppermute x12, starting transfers between devices, exchange(): return (lax.ppermute(last, axis, up), lax.ppermute(first, axis, down))  31.1 us
    pallas_call x1, Pallas kernels, on_device(): call(functools.partial(second_solve, box), (f32(long, across, deep), f32(...  25.9 us
    pallas_call x1, Pallas kernels, on_device(): call(functools.partial(first_solve, box), (window,) * 5 + (f32(long, acro...  22.2 us
    ppermute x12, waiting for transfers between devices, exchange(): return (lax.ppermute(last, axis, up), lax.ppermute(first, axis, down))  18.2 us
    all_to_all x1, blocking collectives, on_device(): lax.all_to_all(told.reshape(count, 1, 128), ('wide', 'narrow'), split_axi...  14.6 us
    pallas_call x1, Pallas kernels, on_device(): call(functools.partial(last_residual, box), f32(long, across, deep), [VME...  10.2 us
    unnamed x28, local copies, waits for them, and re-layouts  3.75 us
  transfers between devices with their start and end apart: 12, of which 8 were waited for; matrix products, arithmetic and copies ran while one was open for 0% of the time, Pallas kernels for 1%

profile of v2, /device:TPU:0, one launch (start us, length us, event | category | flops | bytes accessed | tf_op | source)
XLA Modules:
  0.0 132.5 jit_solution(9766679163583724214)
XLA Ops:
  0.6 1.0 fusion.1
  1.6 0.9 slice_convert_fusion
  2.6 0.9 fusion.2
  3.5 4.9 %collective-permute-start = (f32[14,32,128]{2,1,0:T(8,128)S(1)}, f32[14,32,128]{2,1,0:T(8,128)S(1)}, u32[]{:S(2)}, u32[]{:S(2)}) collective-permute-start(f32[14,32,128]{2,1,0:T(8,128)S(1)} %pad_maximum_fusion), channel_id=1, source_target_pairs={{0,4},{4,8},{8,12},{1,5},{5,9},{9,13},{2,6},{6,10},{10,14},{3,7},{... | collective-permute-start | bytes 688136 | tf_op jit(solution)/shard_map/ppermute | solution.py:507
  8.6 1.4 %collective-permute-start.1 = (f32[14,32,128]{2,1,0:T(8,128)S(1)}, f32[14,32,128]{2,1,0:T(8,128)S(1)}, u32[]{:S(2)}, u32[]{:S(2)}) collective-permute-start(f32[14,32,128]{2,1,0:T(8,128)S(1)} %pad_maximum_fusion.1), channel_id=1, source_target_pairs={{4,0},{8,4},{12,8},{5,1},{9,5},{13,9},{6,2},{10,6},{14,10},{7,3},{... | collective-permute-start | bytes 688136 | tf_op jit(solution)/shard_map/ppermute | solution.py:507
  10.1 3.2 %collective-permute-done.low = f32[14,32,128]{2,1,0:T(8,128)S(1)} collective-permute-done((f32[14,32,128]{2,1,0:T(8,128)S(1)}, f32[14,32,128]{2,1,0:T(8,128)S(1)}, u32[]{:S(2)}, u32[]{:S(2)}) %collective-permute-start) | collective-permute-done | bytes 229408 | tf_op jit(solution)/shard_map/ppermute | solution.py:507
  13.3 4.4 %collective-permute-done.1.high = f32[14,32,128]{2,1,0:T(8,128)S(1)} collective-permute-done((f32[14,32,128]{2,1,0:T(8,128)S(1)}, f32[14,32,128]{2,1,0:T(8,128)S(1)}, u32[]{:S(2)}, u32[]{:S(2)}) %collective-permute-start.1) | collective-permute-done | bytes 229408 | tf_op jit(solution)/shard_map/ppermute | solution.py:507
  17.7 1.2 copy-done.1
  18.9 1.2 copy-done.2
  20.2 0.7 shard_map.140
  20.9 1.3 collective-permute-start.2
  22.2 1.3 collective-permute-start.3
  23.5 0.2 collective-permute-done.2.left
  23.7 4.0 %collective-permute-done.3.right = f32[1040,128]{1,0:T(8,128)S(1)} collective-permute-done((f32[1040,128]{1,0:T(8,128)S(1)}, f32[1040,128]{1,0:T(8,128)S(1)}, u32[]{:S(2)}, u32[]{:S(2)}) %collective-permute-start.3) | collective-permute-done | bytes 532512 | tf_op jit(solution)/shard_map/ppermute | solution.py:507
  27.8 22.2 %shard_map.141 = (f32[74,48,128]{2,1,0:T(8,128)S(1)}, f32[74,48,128]{2,1,0:T(8,128)S(1)}, f32[74,48,128]{2,1,0:T(8,128)S(1)}, f32[74,48,128]{2,1,0:T(8,128)S(1)}...) custom-call(s32[64,32,128]{2,1,0:T(8,128)S(1)} %copy-done.1, ...), custom_call_target="tpu_custom_call" | custom-call | tf_op jit(solution)/shard_map/pallas_call | solution.py:534
  50.0 1.5 %collective-permute-start.5 = (f32[5,32,128]{2,1,0:T(8,128)S(1)}, f32[5,32,128]{2,1,0:T(8,128)S(1)}, u32[]{:S(2)}, u32[]{:S(2)}) collective-permute-start(f32[5,32,128]{2,1,0:T(8,128)S(1)} %get-tuple-element.34), channel_id=1, source_target_pairs={{4,0},{8,4},{12,8},{5,1},{9,5},{13,9},{6,2},{10,6},{14,10},{7,3},{... | collective-permute-start | bytes 245768 | tf_op jit(solution)/shard_map/ppermute | solution.py:507
  51.5 4.6 %collective-permute-start.4 = (f32[5,32,128]{2,1,0:T(8,128)S(1)}, f32[5,32,128]{2,1,0:T(8,128)S(1)}, u32[]{:S(2)}, u32[]{:S(2)}) collective-permute-start(f32[5,32,128]{2,1,0:T(8,128)S(1)} %get-tuple-element.35), channel_id=1, source_target_pairs={{0,4},{4,8},{8,12},{1,5},{5,9},{9,13},{2,6},{6,10},{10,14},{3,7},{... | collective-permute-start | bytes 245768 | tf_op jit(solution)/shard_map/ppermute | solution.py:507
  56.0 0.5 collective-permute-done.5.high
  56.5 1.6 %collective-permute-done.4.low = f32[5,32,128]{2,1,0:T(8,128)S(1)} collective-permute-done((f32[5,32,128]{2,1,0:T(8,128)S(1)}, f32[5,32,128]{2,1,0:T(8,128)S(1)}, u32[]{:S(2)}, u32[]{:S(2)}) %collective-permute-start.4) | collective-permute-done | bytes 81952 | tf_op jit(solution)/shard_map/ppermute | solution.py:507
  58.1 0.3 shard_map.142
  58.3 8.1 %collective-permute-start.6 = (f32[376,128]{1,0:T(8,128)S(1)}, f32[376,128]{1,0:T(8,128)S(1)}, u32[]{:S(2)}, u32[]{:S(2)}) collective-permute-start(f32[376,128]{1,0:T(8,128)S(1)} %get-tuple-element.21), channel_id=1, source_target_pairs={{0,1},{1,2},{2,3},{4,5},{5,6},{6,7},{8,9},{9,10},{10,11},{12,13},{... | collective-permute-start | bytes 577544 | tf_op jit(solution)/shard_map/ppermute | solution.py:507
  66.4 1.3 collective-permute-start.7
  67.7 14.6 %all_to_all.5 = f32[16,1,128]{2,1,0:T(1,128)S(1)} all-to-all(f32[16,1,128]{2,1,0:T(1,128)S(1)} %bitcast.5), channel_id=1, replica_groups=mesh['groups'=2,'wide'=4,'narrow'=4] {'wide','narrow'}, dimensions={0} | all-to-all | bytes 16384 | tf_op jit(solution)/shard_map/all_to_all | solution.py:541
  82.3 1.7 %shard_map.143.solved = f32[16,128]{1,0:T(8,128)S(1)} custom-call(f32[16,128]{1,0:T(8,128)S(1)} %bitcast.4), custom_call_target="tpu_custom_call" | custom-call | tf_op jit(solution)/shard_map/pallas_call | solution.py:550
  84.0 25.9 %shard_map.144 = (f32[64,32,128]{2,1,0:T(8,128)}, f32[32,128]{1,0:T(8,128)S(1)}, f32[32,128]{1,0:T(8,128)S(1)}, f32[64,128]{1,0:T(8,128)S(1)}, f32[64,128]{1,0:T(8,128)S(1)}) custom-call(f32[64,32,128]{2,1,0:T(8,128)S(1)} %get-tuple-element.20.own.local, f32[5,32,128]{2,1,0:T(8,128)S(1)} %collective-permute-done.4.low, ...), custom_call_target="tpu_custom_call" | custom-call | tf_op jit(solution)/shard_map/pallas_call | solution.py:556
  109.9 1.7 %collective-permute-start.10 = (f32[64,128]{1,0:T(8,128)S(1)}, f32[64,128]{1,0:T(8,128)S(1)}, u32[]{:S(2)}, u32[]{:S(2)}) collective-permute-start(f32[64,128]{1,0:T(8,128)S(1)} %get-tuple-element.32), channel_id=1, source_target_pairs={{0,1},{1,2},{2,3},{4,5},{5,6},{6,7},{8,9},{9,10},{10,11},{12,13},{... | collective-permute-start | bytes 98312 | tf_op jit(solution)/shard_map/ppermute | solution.py:507
  111.6 1.3 collective-permute-start.11
  112.9 2.5 %collective-permute-start.8 = (f32[32,128]{1,0:T(8,128)S(1)}, f32[32,128]{1,0:T(8,128)S(1)}, u32[]{:S(2)}, u32[]{:S(2)}) collective-permute-start(f32[32,128]{1,0:T(8,128)S(1)} %get-tuple-element.30), channel_id=1, source_target_pairs={{0,4},{4,8},{8,12},{1,5},{5,9},{9,13},{2,6},{6,10},{10,14},{3,7},{... | collective-permute-start | bytes 49160 | tf_op jit(solution)/shard_map/ppermute | solution.py:507
  115.4 1.3 collective-permute-start.9
  116.8 4.2 %collective-permute-done.9.high = f32[32,128]{1,0:T(8,128)S(1)} collective-permute-done((f32[32,128]{1,0:T(8,128)S(1)}, f32[32,128]{1,0:T(8,128)S(1)}, u32[]{:S(2)}, u32[]{:S(2)}) %collective-permute-start.9) | collective-permute-done | bytes 16416 | tf_op jit(solution)/shard_map/ppermute | solution.py:507
  121.0 1.2 copy-done.3
  122.3 10.2 %shard_map.145 = f32[64,32,128]{2,1,0:T(8,128)} custom-call(f32[64,32,128]{2,1,0:T(8,128)S(1)} %copy-done, f32[64,32,128]{2,1,0:T(8,128)S(1)} %copy-done.3, f32[32,128]{1,0:T(8,128)S(1)} %collective-permute-done.8.low, f32[32,128]{1,0:T(8,128)S(1)} %collective-permute-done.9.high, f32[64,128]{1,0:T(8,128)S(1)} %collective-permute-done.10.left, ...), custom_call_target="tpu_custom_call" | custom-call | tf_op jit(solution)/shard_map/pallas_call | solution.py:584
  (33 shorter events, 0.3 us)
Async XLA Ops:
  0.6 17.1 %copy-start = (f32[64,32,128]{2,1,0:T(8,128)S(1)}, f32[64,32,128]{2,1,0:T(8,128)}, u32[]{:S(2)}) copy-start(f32[64,32,128]{2,1,0:T(8,128)} %load.5) | copy-start | bytes 3145732
  3.5 9.8 %collective-permute-start = (f32[14,32,128]{2,1,0:T(8,128)S(1)}, f32[14,32,128]{2,1,0:T(8,128)S(1)}, u32[]{:S(2)}, u32[]{:S(2)}) collective-permute-start(f32[14,32,128]{2,1,0:T(8,128)S(1)} %pad_maximum_fusion), channel_id=1, source_target_pairs={{0,4},{4,8},{8,12},{1,5},{5,9},{9,13},{2,6},{6,10},{10,14},{3,7},{... | collective-permute-start | bytes 688136 | tf_op jit(solution)/shard_map/ppermute | solution.py:507
  8.5 19.2 %copy-start.4 = (f32[128,128]{1,0:T(8,128)S(1)}, f32[128,128]{1,0:T(8,128)}, u32[]{:S(2)}) copy-start(f32[128,128]{1,0:T(8,128)} %constant.20.clone.rest_4_.rest_9_) | copy-start | bytes 196612
  8.5 19.2 %copy-start.5 = (f32[72,128]{1,0:T(8,128)S(1)}, f32[72,128]{1,0:T(8,128)}, u32[]{:S(2)}) copy-start(f32[72,128]{1,0:T(8,128)} %constant.21.clone.rest_5_.rest_10_) | copy-start | bytes 110596
  8.5 19.2 %copy-start.6 = (f32[72,72]{1,0:T(8,128)S(1)}, f32[72,72]{1,0:T(8,128)}, u32[]{:S(2)}) copy-start(f32[72,72]{1,0:T(8,128)} %constant.17.clone.rest_1_.rest_6_) | copy-start | bytes 62212
  8.5 19.2 %copy-start.7 = (f32[64,72]{1,0:T(8,128)S(1)}, f32[64,72]{1,0:T(8,128)}, u32[]{:S(2)}) copy-start(f32[64,72]{1,0:T(8,128)} %constant.18.clone.rest_2_.rest_7_) | copy-start | bytes 55300
  8.5 19.2 %copy-start.8 = (f32[40,48]{1,0:T(8,128)S(1)}, f32[40,48]{1,0:T(8,128)}, u32[]{:S(2)}) copy-start(f32[40,48]{1,0:T(8,128)} %constant.16.clone.rest_0_.rest_5_) | copy-start | bytes 23044
  8.5 19.2 %copy-start.9 = (f32[32,40]{1,0:T(8,128)S(1)}, f32[32,40]{1,0:T(8,128)}, u32[]{:S(2)}) copy-start(f32[32,40]{1,0:T(8,128)} %constant.19.clone.rest_3_.rest_8_) | copy-start | bytes 15364
  8.6 19.2 %copy-start.10 = (f32[3,3]{1,0:T(4,128)S(1)}, f32[3,3]{1,0:T(4,128)}, u32[]{:S(2)}) copy-start(f32[3,3]{1,0:T(4,128)} %diffusivity.1) | copy-start | bytes 112
  8.6 19.2 %copy-start.11 = (f32[1,40]{1,0:T(1,128)S(1)}, f32[1,40]{1,0:T(1,128)}, u32[]{:S(2)}) copy-start(f32[1,40]{1,0:T(1,128)} %constant.23.clone.rest_7_.rest_12_) | copy-start | bytes 484
  8.6 19.2 %copy-start.12 = (f32[1,128]{1,0:T(1,128)S(1)}, f32[1,128]{1,0:T(1,128)}, u32[]{:S(2)}) copy-start(f32[1,128]{1,0:T(1,128)} %constant.22.clone.rest_6_.rest_11_) | copy-start | bytes 1540
  8.6 19.2 %copy-start.13 = (f32[3]{0:T(128)S(1)}, f32[3]{0:T(128)}, u32[]{:S(2)}) copy-start(f32[3]{0:T(128)} %decay.1) | copy-start | bytes 40
  8.6 9.1 %collective-permute-start.1 = (f32[14,32,128]{2,1,0:T(8,128)S(1)}, f32[14,32,128]{2,1,0:T(8,128)S(1)}, u32[]{:S(2)}, u32[]{:S(2)}) collective-permute-start(f32[14,32,128]{2,1,0:T(8,128)S(1)} %pad_maximum_fusion.1), channel_id=1, source_target_pairs={{4,0},{8,4},{12,8},{5,1},{9,5},{13,9},{6,2},{10,6},{14,10},{7,3},{... | collective-permute-start | bytes 688136 | tf_op jit(solution)/shard_map/ppermute | solution.py:507
  17.7 1.2 copy-start.1
  18.9 1.2 copy-start.2
  20.9 2.8 %collective-permute-start.2 = (f32[1040,128]{1,0:T(8,128)S(1)}, f32[1040,128]{1,0:T(8,128)S(1)}, u32[]{:S(2)}, u32[]{:S(2)}) collective-permute-start(f32[1040,128]{1,0:T(8,128)S(1)} %get-tuple-element.18), channel_id=1, source_target_pairs={{0,1},{1,2},{2,3},{4,5},{5,6},{6,7},{8,9},{9,10},{10,11},{12,13},{... | collective-permute-start | bytes 1597448 | tf_op jit(solution)/shard_map/ppermute | solution.py:507
  22.2 5.5 %collective-permute-start.3 = (f32[1040,128]{1,0:T(8,128)S(1)}, f32[1040,128]{1,0:T(8,128)S(1)}, u32[]{:S(2)}, u32[]{:S(2)}) collective-permute-start(f32[1040,128]{1,0:T(8,128)S(1)} %get-tuple-element.19), channel_id=1, source_target_pairs={{1,0},{2,1},{3,2},{5,4},{6,5},{7,6},{9,8},{10,9},{11,10},{13,12},{... | collective-permute-start | bytes 1597448 | tf_op jit(solution)/shard_map/ppermute | solution.py:507
  50.0 6.5 %collective-permute-start.5 = (f32[5,32,128]{2,1,0:T(8,128)S(1)}, f32[5,32,128]{2,1,0:T(8,128)S(1)}, u32[]{:S(2)}, u32[]{:S(2)}) collective-permute-start(f32[5,32,128]{2,1,0:T(8,128)S(1)} %get-tuple-element.34), channel_id=1, source_target_pairs={{4,0},{8,4},{12,8},{5,1},{9,5},{13,9},{6,2},{10,6},{14,10},{7,3},{... | collective-permute-start | bytes 245768 | tf_op jit(solution)/shard_map/ppermute | solution.py:507
  51.5 6.6 %collective-permute-start.4 = (f32[5,32,128]{2,1,0:T(8,128)S(1)}, f32[5,32,128]{2,1,0:T(8,128)S(1)}, u32[]{:S(2)}, u32[]{:S(2)}) collective-permute-start(f32[5,32,128]{2,1,0:T(8,128)S(1)} %get-tuple-element.35), channel_id=1, source_target_pairs={{0,4},{4,8},{8,12},{1,5},{5,9},{9,13},{2,6},{6,10},{10,14},{3,7},{... | collective-permute-start | bytes 245768 | tf_op jit(solution)/shard_map/ppermute | solution.py:507
  58.3 25.7 %collective-permute-start.6 = (f32[376,128]{1,0:T(8,128)S(1)}, f32[376,128]{1,0:T(8,128)S(1)}, u32[]{:S(2)}, u32[]{:S(2)}) collective-permute-start(f32[376,128]{1,0:T(8,128)S(1)} %get-tuple-element.21), channel_id=1, source_target_pairs={{0,1},{1,2},{2,3},{4,5},{5,6},{6,7},{8,9},{9,10},{10,11},{12,13},{... | collective-permute-start | bytes 577544 | tf_op jit(solution)/shard_map/ppermute | solution.py:507
  66.4 17.6 %collective-permute-start.7 = (f32[376,128]{1,0:T(8,128)S(1)}, f32[376,128]{1,0:T(8,128)S(1)}, u32[]{:S(2)}, u32[]{:S(2)}) collective-permute-start(f32[376,128]{1,0:T(8,128)S(1)} %get-tuple-element.22), channel_id=1, source_target_pairs={{1,0},{2,1},{3,2},{5,4},{6,5},{7,6},{9,8},{10,9},{11,10},{13,12},{... | collective-permute-start | bytes 577544 | tf_op jit(solution)/shard_map/ppermute | solution.py:507
  109.9 11.1 %collective-permute-start.10 = (f32[64,128]{1,0:T(8,128)S(1)}, f32[64,128]{1,0:T(8,128)S(1)}, u32[]{:S(2)}, u32[]{:S(2)}) collective-permute-start(f32[64,128]{1,0:T(8,128)S(1)} %get-tuple-element.32), channel_id=1, source_target_pairs={{0,1},{1,2},{2,3},{4,5},{5,6},{6,7},{8,9},{9,10},{10,11},{12,13},{... | collective-permute-start | bytes 98312 | tf_op jit(solution)/shard_map/ppermute | solution.py:507
  111.6 9.4 %collective-permute-start.11 = (f32[64,128]{1,0:T(8,128)S(1)}, f32[64,128]{1,0:T(8,128)S(1)}, u32[]{:S(2)}, u32[]{:S(2)}) collective-permute-start(f32[64,128]{1,0:T(8,128)S(1)} %get-tuple-element.33), channel_id=1, source_target_pairs={{1,0},{2,1},{3,2},{5,4},{6,5},{7,6},{9,8},{10,9},{11,10},{13,12},{... | collective-permute-start | bytes 98312 | tf_op jit(solution)/shard_map/ppermute | solution.py:507
  112.9 3.9 %collective-permute-start.8 = (f32[32,128]{1,0:T(8,128)S(1)}, f32[32,128]{1,0:T(8,128)S(1)}, u32[]{:S(2)}, u32[]{:S(2)}) collective-permute-start(f32[32,128]{1,0:T(8,128)S(1)} %get-tuple-element.30), channel_id=1, source_target_pairs={{0,4},{4,8},{8,12},{1,5},{5,9},{9,13},{2,6},{6,10},{10,14},{3,7},{... | collective-permute-start | bytes 49160 | tf_op jit(solution)/shard_map/ppermute | solution.py:507
  115.4 5.6 %collective-permute-start.9 = (f32[32,128]{1,0:T(8,128)S(1)}, f32[32,128]{1,0:T(8,128)S(1)}, u32[]{:S(2)}, u32[]{:S(2)}) collective-permute-start(f32[32,128]{1,0:T(8,128)S(1)} %get-tuple-element.31), channel_id=1, source_target_pairs={{4,0},{8,4},{12,8},{5,1},{9,5},{13,9},{6,2},{10,6},{14,10},{7,3},{... | collective-permute-start | bytes 49160 | tf_op jit(solution)/shard_map/ppermute | solution.py:507
  121.0 1.2 copy-start.3

commit v3 on v2

v3 whole, which is shorter than its diff:
```python
import functools

import jax
import jax.numpy as jnp
import ml_dtypes
import numpy as np
from jax import lax
from jax.experimental import pallas as pl
from jax.experimental.pallas import tpu as pltpu
from jax.sharding import PartitionSpec as P

MARGIN = 4
REACH = MARGIN + 1
EDGE = 8

cheb_center = 1.3
cheb_radius = 1.2
cheb_ratio = 1.3 / 1.2
rho_first = 1.0 / cheb_ratio
rho_second = 1.0 / (2.0 * cheb_ratio - rho_first)

DIAGONAL, LONG_HIGH, LONG_LOW, ACROSS_HIGH, ACROSS_LOW, LOAD_SUM, IMAGE_SUM = range(7)
FLOW_LONG_HIGH, FLOW_LONG_LOW, FLOW_ACROSS_HIGH, FLOW_ACROSS_LOW = range(7, 11)

VMEM = pl.BlockSpec(memory_space=pltpu.VMEM)
SMEM = pl.BlockSpec(memory_space=pltpu.SMEM)


def sine_basis(length):
    indices = np.arange(1, length + 1)
    phases = indices[:, None] * indices[None, :] % (2 * (length + 1))
    table = np.sqrt(2.0 / (length + 1)) * np.sin(np.pi * phases / (length + 1))
    eigvals = 4.0 * np.sin(np.pi * indices / (2.0 * (length + 1))) ** 2
    return table.astype(np.float32), eigvals.astype(np.float32)


def call(body, out_shape, in_specs, scratch=(), flops=0, moved=0):
    return pl.pallas_call(
        body,
        out_shape=out_shape,
        in_specs=in_specs,
        out_specs=jax.tree.map(lambda _: VMEM, out_shape),
        scratch_shapes=list(scratch),
        compiler_params=pltpu.CompilerParams(vmem_limit_bytes=30 * 2**20),
        cost_estimate=pl.CostEstimate(flops=flops, bytes_accessed=moved, transcendentals=0),
    )


def f32(*shape):
    return jax.ShapeDtypeStruct(shape, jnp.float32)


class Box:
    def __init__(self, shape):
        self.long, self.across, self.deep = shape
        self.ex = self.long + 2 * MARGIN
        self.ey = self.across + 2 * MARGIN
        self.rows = self.long + 2 * REACH
        self.cols = self.across + 2 * EDGE
        self.flat = self.rows * self.cols


def pieces(values, count):
    parts = []
    for _ in range(count):
        part = values.astype(jnp.bfloat16)
        parts.append(part)
        values = values - part.astype(jnp.float32)
    return parts


def left_table(table, depth, count):
    rows, cols = table.shape
    wide = np.zeros((rows, depth), np.float32)
    wide[:, :cols] = table
    parts = []
    rest = wide
    for _ in range(count):
        part = rest.astype(ml_dtypes.bfloat16)
        parts.append(part)
        rest = rest - part.astype(np.float32)
    blank = np.zeros_like(parts[0])
    lines = []
    for index in range(count):
        used = count - index if count > 2 else count
        lines.append(np.concatenate([parts[index]] * used + [blank] * (count - used), axis=1))
    return np.concatenate(lines, axis=0)


def right_tables(table):
    rest, parts = table, []
    for _ in range(3):
        part = rest.astype(ml_dtypes.bfloat16)
        parts.append(part)
        rest = rest - part.astype(np.float32)
    both = np.concatenate([parts[0], parts[1]], axis=1)
    return np.concatenate([both, both], axis=0), np.concatenate([parts[2], parts[0]], axis=0)


def padded(size):
    return -(-size // 16) * 16


FORWARD, BACKWARD = 2, 3


def tables_of(box):
    sine_x, eig_x = sine_basis(box.ex)
    sine_y, eig_y = sine_basis(box.ey)
    sine_z, eig_z = sine_basis(box.deep)
    skip = EDGE - MARGIN
    into_y = np.zeros((box.ey, box.cols), np.float32)
    into_y[:, skip : skip + box.ey] = sine_y
    from_y = sine_y[MARGIN : MARGIN + box.across]
    from_x = sine_x[MARGIN : MARGIN + box.long]
    spread = np.broadcast_to(eig_x[:, None], (box.ex, box.deep))
    main_z, rest_z = right_tables(sine_z)
    return [
        jnp.asarray(np.ascontiguousarray(t))
        for t in (
            left_table(into_y, box.cols, FORWARD),
            left_table(sine_x, padded(box.ex), FORWARD),
            left_table(from_x, padded(box.ex), BACKWARD),
            left_table(from_y, padded(box.ey), BACKWARD),
            main_z,
            rest_z,
            spread,
            eig_z[None, :],
            eig_y[None, :],
        )
    ]


N_TABLES = 9


def bf16_dot(left, right):
    return lax.dot_general(
        left, right, (((1,), (0,)), ((), ())), preferred_element_type=jnp.float32
    )


def dot_left(table, values, count, rows):
    total = bf16_dot(table, jnp.concatenate(pieces(values, count), axis=0))
    return sum(total[index * rows : (index + 1) * rows] for index in range(1, count)) + total[:rows]


def dot_right(values, main, rest, count):
    deep = values.shape[1]
    parts = pieces(values, count)
    total = bf16_dot(jnp.concatenate(parts[:2], axis=1), main)
    result = total[:, :deep] + total[:, deep:]
    if count == 3:
        result = result + bf16_dot(jnp.concatenate([parts[0], parts[2]], axis=1), rest)
    return result


def with_rows(values, rows):
    if values.shape[0] == rows:
        return values
    blank = jnp.zeros((rows - values.shape[0],) + values.shape[1:], values.dtype)
    return jnp.concatenate([values, blank], axis=0)


def box_solve(box, source, means, tables, row_mask, col_mask, spectral, middle, emit):
    into_y, into_x, from_x, from_y, main_z, rest_z, spread, eig_z, eig_y = tables
    deep = box.deep
    deep_x, deep_y = padded(box.ex), padded(box.ey)
    into_y, into_x = into_y[...], into_x[...]
    if col_mask is not None:
        mask = jnp.concatenate([col_mask] * FORWARD, axis=1)
        into_y = (into_y.astype(jnp.float32) * mask).astype(jnp.bfloat16)
        mask = jnp.concatenate([row_mask] * FORWARD, axis=1)
        into_x = (into_x.astype(jnp.float32) * mask).astype(jnp.bfloat16)
    from_x, from_y, main_z, rest_z = from_x[...], from_y[...], main_z[...], rest_z[...]
    spectral_flat = spectral.reshape(box.ey * deep_x, deep)
    middle_flat = middle.reshape(box.long * deep_y, deep)
    if deep_x > box.ex:
        spectral[:, box.ex :, :] = jnp.zeros((box.ey, deep_x - box.ex, deep), jnp.float32)
    if deep_y > box.ey:
        middle[:, box.ey :, :] = jnp.zeros((box.long, deep_y - box.ey, deep), jnp.float32)
    for start in range(0, box.ex, 8):
        block = source[start : start + 8].reshape(8 * box.cols, deep)
        block = dot_right(block, main_z, rest_z, FORWARD).reshape(8, box.cols, deep)
        for row in range(0, 8, 2):
            pair = jnp.concatenate([block[row], block[row + 1]], axis=1)
            pair = dot_left(into_y, pair, FORWARD, box.ey)
            for part in range(2):
                spectral_flat[pl.ds(start + row + part, box.ey, stride=deep_x), :] = pair[
                    :, part * deep : (part + 1) * deep
                ]
    base = means[3] + means[0] * spread[...] + means[2] * eig_z[...]
    for col in range(0, box.ey, 2):
        pair = jnp.concatenate([spectral[col], spectral[col + 1]], axis=1)
        pair = dot_left(into_x, pair, FORWARD, box.ex)
        pair = jnp.concatenate(
            [
                pair[:, part * deep : (part + 1) * deep]
                / (base + means[1] * eig_y[0, col + part])
                for part in range(2)
            ],
            axis=1,
        )
        pair = dot_left(from_x, with_rows(pair, deep_x), BACKWARD, box.long)
        for part in range(2):
            middle_flat[pl.ds(col + part, box.long, stride=deep_y), :] = pair[
                :, part * deep : (part + 1) * deep
            ]
    for start in range(0, box.long, 8):
        parts = []
        for row in range(start, start + 8, 2):
            pair = jnp.concatenate([middle[row], middle[row + 1]], axis=1)
            pair = dot_left(from_y, pair, BACKWARD, box.across)
            parts += [pair[:, :deep], pair[:, deep:]]
        emit(start, dot_right(jnp.concatenate(parts, axis=0), main_z, rest_z, BACKWARD))


def position():
    long_pos, across_pos = lax.axis_index("wide"), lax.axis_index("narrow")
    return long_pos, across_pos, lax.axis_size("wide"), lax.axis_size("narrow")


def as_float(flag):
    return jnp.where(flag, jnp.float32(1.0), jnp.float32(0.0))


def row_of(stride, col, count, first=0):
    return pl.ds(first * stride + col, count, stride=stride)


def pack_columns(box, fields, lows, highs, wide, up, down):
    corner = len(fields) * wide * box.long
    place = 0
    for field, low, high in zip(fields, lows, highs):
        for step in range(wide):
            for target, col in ((up, box.across - wide + step), (down, step)):
                values = field[row_of(box.across, col, box.long), :]
                target[place * box.long : (place + 1) * box.long, :] = values.astype(jnp.float32)
                at = corner + 2 * REACH * place
                target[at : at + wide, :] = low[row_of(box.across, col, wide), :]
                target[at + REACH : at + REACH + wide, :] = high[row_of(box.across, col, wide), :]
            place += 1


def message_rows(box, count):
    return -(-(count * (box.long + 2 * REACH)) // 8) * 8


def pack_fields(box, wide, *refs):
    *fields, low, high, up, down = refs
    size = wide * box.across
    flat = [field.reshape(box.long * box.across, box.deep) for field in fields]
    sides = [
        [
            ref.reshape(len(fields) * size, box.deep).at[index * size : (index + 1) * size]
            for index in range(len(fields))
        ]
        for ref in (low, high)
    ]
    pack_columns(box, flat, sides[0], sides[1], wide, up, down)


def pack_edges(box, zone, scale, load, load_up, load_down, up, down, staged, sems):
    last = box.long
    copies = [
        (load.at[last - MARGIN :], load_up),
        (load.at[:MARGIN], load_down),
        (scale.at[last - REACH :], up.at[:REACH]),
        (scale.at[:REACH], down.at[:REACH]),
        (zone.at[last - REACH :], staged.at[0]),
        (zone.at[:REACH], staged.at[1]),
    ]
    copies = [
        pltpu.make_async_copy(source, target, sems.at[index])
        for index, (source, target) in enumerate(copies)
    ]
    for copy in copies:
        copy.start()
    for copy in copies:
        copy.wait()
    up[REACH:] = staged[0].astype(jnp.float32)
    down[REACH:] = staged[1].astype(jnp.float32)


def fill_window(box, window, own, low, high, left, right, wide, place, total, add=None):
    flat = window.reshape(box.flat, box.deep)
    nothing = jnp.zeros((box.rows, EDGE, box.deep), jnp.float32)
    window[:, :EDGE, :] = nothing
    window[:, EDGE + box.across :, :] = nothing
    if add is None:
        add = lambda values, row_side, col_side: values
    inner = slice(EDGE, EDGE + box.across)
    first, last = REACH, REACH + box.long
    if wide < REACH:
        blank = jnp.zeros((1, box.across, box.deep), jnp.float32)
        window[0:1, inner, :] = blank
        window[box.rows - 1 :, inner, :] = blank
    window[first:last, inner, :] = add(own[...].astype(jnp.float32), 0, 0)
    window[first - wide : first, inner, :] = add(low, -1, 0)
    window[last : last + wide, inner, :] = add(high, 1, 0)
    corner = total * box.long
    for step in range(wide):
        for source, col, side in (
            (left, EDGE - wide + step, -1),
            (right, EDGE + box.across + step, 1),
        ):
            at = (place + step) * box.long
            values = source[at : at + box.long, :]
            flat[row_of(box.cols, col, box.long, first), :] = add(values, 0, side)
            at = corner + 2 * REACH * (place + step)
            values = source[at : at + wide, :]
            flat[row_of(box.cols, col, wide, first - wide), :] = add(values, -1, side)
            values = source[at + REACH : at + REACH + wide, :]
            flat[row_of(box.cols, col, wide, last), :] = add(values, 1, side)


def negative_image(row, x, x_next, flow_before, weights):
    to_long, to_across, to_deep, mass = weights
    rows, lanes = x.shape
    flow_long = to_long[row] * (x_next - x)
    flow_across = to_across[row] * (pltpu.roll(x, rows - 1, 0) - x)
    flow_deep = to_deep[row] * (pltpu.roll(x, lanes - 1, 1) - x)
    total = flow_long - flow_before - mass[row] * x
    total = total + (flow_across - pltpu.roll(flow_across, 1, 0))
    total = total + (flow_deep - pltpu.roll(flow_deep, 1, 1))
    return total, flow_long


def looked_up(labels, values):
    return jnp.where(labels == 0, values[0], jnp.where(labels == 1, values[1], values[2]))


def box_means(box, zone, scale, diffusivity, decay, out):
    step = 4
    nothing = jnp.zeros((box.across, box.deep), jnp.float32)

    def some_rows(index, sums):
        for row in range(step):
            labels, factor = zone[index * step + row], scale[index * step + row]
            sums = [
                sums[d] + looked_up(labels, [diffusivity[z, d] for z in range(3)]) * factor
                for d in range(3)
            ] + [sums[3] + looked_up(labels, [decay[z] for z in range(3)])]
        return sums

    sums = lax.fori_loop(0, box.long // step, some_rows, [nothing] * 4)
    cells = box.long * box.across * box.deep
    lanes = lax.broadcasted_iota(jnp.int32, out.shape, 1)
    line = jnp.zeros(out.shape, jnp.float32)
    for index, values in enumerate(sums):
        line = jnp.where(lanes == index, jnp.sum(values, keepdims=True) / cells, line)
    out[...] = line


def means_of(ref):
    return [ref[0:1, index : index + 1] for index in range(4)]


def first_solve(box, load, low, high, left, right, means, *rest):
    tables = rest[:N_TABLES]
    window, local, spectral, middle = rest[N_TABLES:]
    fill_window(box, window, load, low[...], high[...], left, right, MARGIN, 0, MARGIN)

    def emit(start, values):
        values = values * (1.0 / cheb_center)
        local[start : start + 8] = values.reshape(8, box.across, box.deep)

    box_solve(
        box,
        window.at[1 : 1 + box.ex],
        means_of(means),
        tables,
        None,
        None,
        spectral,
        middle,
        emit,
    )


def weights_of(
    box,
    zone,
    scale,
    load,
    local,
    low,
    high,
    left,
    right,
    diffusivity,
    decay,
    to_long,
    to_across,
    to_deep,
    mass,
    told,
    zone_window,
    scale_window,
):
    for index, (window, own) in enumerate(((scale_window, scale), (zone_window, zone))):
        part = slice(index * REACH, (index + 1) * REACH)
        fill_window(
            box, window, own, low[part], high[part], left, right, REACH, part.start, 2 * REACH
        )
    half = [[0.5 * diffusivity[z, d] for d in range(3)] for z in range(3)]
    rates = [decay[z] for z in range(3)]
    lane = lax.broadcasted_iota(jnp.int32, (box.cols, box.deep), 1)
    ends = jnp.where((lane == 0) | (lane == box.deep - 1), jnp.float32(1.0), jnp.float32(0.0))
    not_last = jnp.where(lane == box.deep - 1, jnp.float32(0.0), jnp.float32(1.0))

    def one_row(row, before):
        labels, factor = zone_window[row], scale_window[row]
        now = [looked_up(labels, [half[z][d] for z in range(3)]) * factor for d in range(3)]
        to_across[row] = now[1] + pltpu.roll(now[1], box.cols - 1, 0)
        to_deep[row] = (now[2] + pltpu.roll(now[2], box.deep - 1, 1)) * not_last
        mass[row] = looked_up(labels, rates) + now[2] * ends
        to_long[jnp.maximum(row - 1, 0)] = before + now[0]
        return now[0]

    last_long = lax.fori_loop(0, box.rows - 2, one_row, jnp.zeros_like(ends), unroll=4)
    for row in range(box.rows - 2, box.rows):
        last_long = one_row(row, last_long)
    to_long[box.rows - 1] = last_long

    first, last = REACH, REACH + box.long
    inner = slice(EDGE, EDGE + box.across)
    step = 8
    nothing = jnp.zeros((box.across, box.deep), jnp.float32)

    def add_rows(index, sums):
        mass_sum, image_sum, load_sum = sums
        for row in range(step):
            row = index * step + row
            own_mass = mass[first + row, inner]
            mass_sum = mass_sum + own_mass
            image_sum = image_sum + own_mass * local[row]
            load_sum = load_sum + load[row]
        return mass_sum, image_sum, load_sum

    mass_sum, image_sum, load_sum = lax.fori_loop(0, box.long // step, add_rows, (nothing,) * 3)
    long_pos, across_pos, long_count, across_count = position()
    has = [
        as_float(long_pos < long_count - 1),
        as_float(long_pos > 0),
        as_float(across_pos < across_count - 1),
        as_float(across_pos > 0),
    ]
    across_flat = to_across.reshape(box.flat, box.deep)
    local_flat = local.reshape(box.long * box.across, box.deep)
    faces = [
        (to_long[last - 1, inner], local[box.long - 1]),
        (to_long[first - 1, inner], local[0]),
        (
            across_flat[row_of(box.cols, EDGE + box.across - 1, box.long, first), :],
            local_flat[row_of(box.across, box.across - 1, box.long), :],
        ),
        (
            across_flat[row_of(box.cols, EDGE - 1, box.long, first), :],
            local_flat[row_of(box.across, 0, box.long), :],
        ),
    ]
    weights = [jnp.sum(w, keepdims=True) for w, _ in faces]
    flows = [jnp.sum(w * v, keepdims=True) for w, v in faces]
    numbers = [jnp.sum(mass_sum, keepdims=True) + sum(weights)]
    numbers += [w * h for w, h in zip(weights, has)]
    numbers += [jnp.sum(load_sum, keepdims=True)]
    numbers += [jnp.sum(image_sum, keepdims=True) + sum(flows)]
    numbers += [f * h for f, h in zip(flows, has)]
    lanes = lax.broadcasted_iota(jnp.int32, told.shape, 1)
    line = jnp.zeros(told.shape, jnp.float32)
    for index, number in enumerate(numbers):
        line = jnp.where(lanes == index, number, line)
    told[...] = line


def coarse_solve(told, answers, solved):
    count, width = solved.shape
    across = lax.axis_size("narrow")
    numbers = told[...]

    def column(index, values=numbers):
        return values[:, index : index + 1]

    image = column(IMAGE_SUM)
    image = image - column(FLOW_LONG_LOW, pltpu.roll(numbers, count - across, 0))
    image = image - column(FLOW_LONG_HIGH, pltpu.roll(numbers, across, 0))
    image = image - column(FLOW_ACROSS_LOW, pltpu.roll(numbers, count - 1, 0))
    image = image - column(FLOW_ACROSS_HIGH, pltpu.roll(numbers, 1, 0))
    rows = lax.broadcasted_iota(jnp.int32, (count, width), 0)
    cols = lax.broadcasted_iota(jnp.int32, (count, width), 1)
    nothing = jnp.zeros((count, width), jnp.float32)
    matrix = jnp.where(cols == rows, column(DIAGONAL), nothing)
    matrix = matrix - jnp.where(cols == rows + across, column(LONG_HIGH), nothing)
    matrix = matrix - jnp.where(cols == rows - across, column(LONG_LOW), nothing)
    matrix = matrix - jnp.where(cols == rows + 1, column(ACROSS_HIGH), nothing)
    matrix = matrix - jnp.where(cols == rows - 1, column(ACROSS_LOW), nothing)
    matrix = jnp.where(cols == count, column(LOAD_SUM), matrix)
    matrix = jnp.where(cols == count + 1, image, matrix)
    solved[...] = matrix

    def eliminate(step, _):
        values = solved[...]
        pivot_row = solved[pl.ds(step, 1), :]
        at_step = cols == step
        factors = jnp.sum(jnp.where(at_step, values, nothing), axis=1, keepdims=True)
        pivot = jnp.sum(jnp.where(at_step[:1], pivot_row, nothing[:1]), axis=1, keepdims=True)
        pivot_row = pivot_row / pivot
        solved[...] = jnp.where(rows == step, pivot_row, values - factors * pivot_row)
        return 0

    lax.fori_loop(0, count, eliminate, 0)
    values = solved[...]
    lanes = lax.broadcasted_iota(jnp.int32, answers.shape, 1)
    answers[...] = jnp.where(
        lanes == 0, values[:, count : count + 1], values[:, count + 1 : count + 2]
    )


def second_solve(box, local, low, high, left, right, solved, means, *rest):
    to_long, to_across, to_deep, mass, load_window = rest[:5]
    tables = rest[5 : 5 + N_TABLES]
    iterate, top, bottom, last_col, first_col = rest[5 + N_TABLES : 10 + N_TABLES]
    window, residual, spectral, middle = rest[10 + N_TABLES :]
    long_pos, across_pos, long_count, across_count = position()
    count = long_count * across_count
    own_box = long_pos * across_count + across_pos

    def coarse(row_side, col_side, lane):
        there_long, there_across = long_pos + row_side, across_pos + col_side
        inside = (
            (there_long >= 0)
            & (there_long < long_count)
            & (there_across >= 0)
            & (there_across < across_count)
        )
        place = jnp.clip(there_long * across_count + there_across, 0, count - 1)
        return solved[pl.ds(place, 1), lane : lane + 1] * as_float(inside)

    shifts = {
        (row_side, col_side): coarse(row_side, col_side, 0) * (1.0 / cheb_center)
        for row_side in (-1, 0, 1)
        for col_side in (-1, 0, 1)
    }

    def add(values, row_side, col_side):
        shift = shifts[row_side, col_side]
        if values.ndim == 3:
            shift = shift.reshape(1, 1, 1)
        return values + shift

    fill_window(box, window, local, low[...], high[...], left, right, REACH, 0, REACH, add)
    weights = (to_long, to_across, to_deep, mass)

    def one_row(row, flow):
        image, flow = negative_image(row, window[row], window[row + 1], flow, weights)
        residual[row - 1] = load_window[row] + image
        return flow

    flow = to_long[0] * (window[1] - window[0])
    lax.fori_loop(1, 1 + box.ex, one_row, flow, unroll=4)
    inner = slice(EDGE, EDGE + box.across)
    first = REACH
    row_ids = lax.broadcasted_iota(jnp.int32, (1, padded(box.ex)), 1)
    col_ids = lax.broadcasted_iota(jnp.int32, (1, box.cols), 1)
    row_mask = jnp.where(row_ids < MARGIN, as_float(long_pos > 0), 1.0)
    row_mask = jnp.where(row_ids >= MARGIN + box.long, as_float(long_pos < long_count - 1), row_mask)
    col_mask = jnp.where(col_ids < EDGE, as_float(across_pos > 0), 1.0)
    col_mask = jnp.where(
        col_ids >= EDGE + box.across, as_float(across_pos < across_count - 1), col_mask
    )
    own_c = coarse(0, 0, 0) * (1.0 - 1.0 / cheb_center) - coarse(0, 0, 1)
    keep = 1.0 + rho_second * rho_first
    gain = 2.0 * rho_second / cheb_radius

    def emit(start, values):
        rows = (values + own_c).reshape(8, box.across, box.deep)
        before = window[first + start : first + start + 8, inner, :]
        iterate[start : start + 8] = keep * before + gain * rows

    box_solve(
        box, residual, means_of(means), tables, row_mask, col_mask, spectral, middle, emit
    )
    top[...] = iterate[box.long - 1]
    bottom[...] = iterate[0]
    flat = iterate.reshape(box.long * box.across, box.deep)
    last_col[...] = flat[row_of(box.across, box.across - 1, box.long), :]
    first_col[...] = flat[row_of(box.across, 0, box.long), :]


def last_residual(
    box, load, iterate, low, high, left, right, to_long, to_across, to_deep, mass, out, window
):
    inner = slice(EDGE, EDGE + box.across)
    flat = window.reshape((box.long + 2) * box.cols, box.deep)
    blank = jnp.zeros((box.long + 2, EDGE, box.deep), jnp.float32)
    window[:, :EDGE, :] = blank
    window[:, EDGE + box.across :, :] = blank
    window[1 : 1 + box.long, inner, :] = iterate[...]
    window[0, inner, :] = low[...]
    window[1 + box.long, inner, :] = high[...]
    flat[row_of(box.cols, EDGE - 1, box.long, 1), :] = left[...]
    flat[row_of(box.cols, EDGE + box.across, box.long, 1), :] = right[...]
    weights = (to_long, to_across, to_deep, mass)

    def one_row(row, flow):
        image, flow = negative_image(REACH + row, window[row + 1], window[row + 2], flow, weights)
        out[row] = load[row] + image[inner]
        return flow

    flow = to_long[REACH - 1] * (window[1] - window[0])
    lax.fori_loop(0, box.long, one_row, flow, unroll=4)


def exchange(axis, last, first):
    size = lax.axis_size(axis)
    up = [(i, i + 1) for i in range(size - 1)]
    down = [(j, i) for i, j in up]
    return lax.ppermute(last, axis, up), lax.ppermute(first, axis, down)


def on_device(zone, scale, diffusivity, decay, load):
    box = Box(load.shape)
    long, across, deep = load.shape
    count = lax.axis_size("wide") * lax.axis_size("narrow")
    tables = tables_of(box)
    cells = f32(long, across, deep)
    window = f32(box.rows, box.cols, deep)

    def scratch(shape):
        return pltpu.VMEM(shape, jnp.float32)

    spectral = scratch((box.ey, padded(box.ex), deep))
    middle = scratch((long, padded(box.ey), deep))

    def pack(wide, *fields):
        message = f32(message_rows(box, wide * (len(fields) - 2)), deep)
        body = functools.partial(pack_fields, box, wide)
        return call(body, (message, message), [VMEM] * len(fields))(*fields)

    near, far = f32(MARGIN, across, deep), f32(2 * REACH, across, deep)
    load_up, load_down, up, down = call(
        functools.partial(pack_edges, box),
        (near, near, far, far),
        [pl.BlockSpec(memory_space=pltpu.HBM)] * 3,
        [pltpu.VMEM((2, REACH, across, deep), jnp.int32), pltpu.SemaphoreType.DMA((6,))],
    )(zone, scale, load)
    load_low, load_high = exchange("wide", load_up, load_down)
    means = call(functools.partial(box_means, box), f32(8, 128), [VMEM] * 2 + [SMEM] * 2)(
        zone, scale, diffusivity, decay
    )
    low, high = exchange("wide", up, down)
    load_left, load_right = exchange("narrow", *pack(MARGIN, load, load_low, load_high))
    left, right = exchange("narrow", *pack(REACH, scale, zone, low, high))
    load_window, local = call(
        functools.partial(first_solve, box),
        (window, cells),
        [VMEM] * (6 + N_TABLES),
        [spectral, middle],
        flops=4 * 10**9,
    )(load, load_low, load_high, load_left, load_right, means, *tables)
    to_long, to_across, to_deep, mass, told = call(
        functools.partial(weights_of, box),
        (window,) * 4 + (f32(count, 128),),
        [VMEM] * 8 + [SMEM] * 2,
        [scratch(window.shape)] * 2,
        flops=10**9,
    )(zone, scale, load, local, low, high, left, right, diffusivity, decay)
    low, high = exchange("wide", local[long - REACH :], local[:REACH])
    all_told = lax.all_to_all(
        told.reshape(count, 1, 128), ("wide", "narrow"), split_axis=0, concat_axis=0, tiled=True
    ).reshape(count, 128)
    left, right = exchange("narrow", *pack(REACH, local, low, high))
    solved_width = -(-(count + 2) // 128) * 128
    solved = call(coarse_solve, f32(count, 128), [VMEM], [scratch((count, solved_width))])(all_told)
    row, col = f32(across, deep), f32(long, deep)
    iterate, top, bottom, last_col, first_col = call(
        functools.partial(second_solve, box),
        (cells, row, row, col, col),
        [VMEM] * (12 + N_TABLES),
        [scratch(window.shape), scratch((box.ex, box.cols, deep)), spectral, middle],
        flops=4 * 10**9,
    )(
        local,
        low,
        high,
        left,
        right,
        solved,
        means,
        to_long,
        to_across,
        to_deep,
        mass,
        load_window,
        *tables,
    )
    low, high = exchange("wide", top, bottom)
    left, right = exchange("narrow", last_col, first_col)
    residual = call(
        functools.partial(last_residual, box),
        cells,
        [VMEM] * 10,
        [scratch((long + 2, box.cols, deep))],
    )(load, iterate, low, high, left, right, to_long, to_across, to_deep, mass)
    return iterate, residual


def solution(mesh):
    split = P(("groups", "wide"), "narrow", None)
    return jax.shard_map(
        on_device,
        mesh=mesh,
        in_specs=(split, split, P(), P(), split),
        out_specs=(split, split),
        check_vma=False,
    )
```

time: 133 us -> 99.2 us (0.75)
  Pallas kernels: 60.9 us -> 30.3 us
  waiting for transfers between devices: 18.2 us -> 7.77 us
  starting transfers between devices: 31.1 us -> 37.4 us
  blocking collectives: 14.6 us -> 16.7 us
    pallas_call x6 -> x10, Pallas kernels: 60.9 us -> 30.3 us  [the longest x1 11.1 us: on_device(): call(functools.partial(second_solve, box), (cells, row, row, col, col), [...]
    ppermute x12 -> x16, waiting for transfers between devices: 18.2 us -> 7.77 us  [exchange(): return (lax.ppermute(last, axis, up), lax.ppermute(first, axis, down))]
    ppermute x12 -> x16, starting transfers between devices: 31.1 us -> 37.4 us  [exchange(): return (lax.ppermute(last, axis, up), lax.ppermute(first, axis, down))]
    all_to_all x1, blocking collectives: 14.6 us -> 16.7 us  [on_device(): lax.all_to_all(told.reshape(count, 1, 128), ('wide', 'narrow'), split_axi...]
    slice x2 -> x0, local copies, waits for them, and re-layouts: 1.91 us -> none  [edge(): lax.slice_in_dim(field, start, start + wide, axis=0).astype(jnp.float32)]
    unnamed x28 -> x36, local copies, waits for them, and re-layouts: 3.75 us -> 4.97 us
  transfers between devices with their start and end apart: 12 -> 16, of which waited for: 8 -> 5; matrix products, arithmetic and copies ran while one was open for 0% -> 0% of each run, Pallas kernels for 1% -> 15%
where the time goes in v3:
time: 99.2 us; the launch traced here: 98.3 us
  starting transfers between devices  37.4 us (38%)
  Pallas kernels  30.3 us (31%)
  blocking collectives  16.7 us (17%)
  waiting for transfers between devices  7.77 us (8%)
  local copies, waits for them, and re-layouts  4.99 us (5%)
  between operations  1.12 us (1%)
    ppermute x16, starting transfers between devices, exchange(): return (lax.ppermute(last, axis, up), lax.ppermute(first, axis, down))  37.4 us
    all_to_all x1, blocking collectives, on_device(): lax.all_to_all(told.reshape(count, 1, 128), ('wide', 'narrow'), split_axi...  16.7 us
    pallas_call x1, Pallas kernels, on_device(): call(functools.partial(second_solve, box), (cells, row, row, col, col), [...  11.1 us
    ppermute x16, waiting for transfers between devices, exchange(): return (lax.ppermute(last, axis, up), lax.ppermute(first, axis, down))  7.77 us
    pallas_call x1, Pallas kernels, on_device(): call(functools.partial(first_solve, box), (window, cells), [VMEM] * (6 +...  6.71 us
    unnamed x36, local copies, waits for them, and re-layouts  4.97 us
    pallas_call x1, Pallas kernels, on_device(): call(functools.partial(weights_of, box), (window,) * 4 + (f32(count, 128)...  4.13 us
    pallas_call x1, Pallas kernels, on_device(): call(functools.partial(last_residual, box), cells, [VMEM] * 10, [scratch(...  3.68 us
  transfers between devices with their start and end apart: 16, of which 5 were waited for; matrix products, arithmetic and copies ran while one was open for 0% of the time, Pallas kernels for 15%

profile of v3, /device:TPU:0, one launch (start us, length us, event | category | flops | bytes accessed | tf_op | source)
XLA Modules:
  0.0 98.3 jit_solution(5830614190009800357)
XLA Ops:
  0.6 1.2 %copy-done = s32[64,32,128]{2,1,0:T(8,128)S(1)} copy-done((s32[64,32,128]{2,1,0:T(8,128)S(1)}, s32[64,32,128]{2,1,0:T(8,128)}, u32[]{:S(2)}) %copy-start) | copy-done | bytes 1048600
  1.9 1.2 %copy-done.2 = f32[64,32,128]{2,1,0:T(8,128)S(1)} copy-done((f32[64,32,128]{2,1,0:T(8,128)S(1)}, f32[64,32,128]{2,1,0:T(8,128)}, u32[]{:S(2)}) %copy-start.2) | copy-done | bytes 1048600
  3.1 1.2 %copy-done.4 = f32[64,32,128]{2,1,0:T(8,128)S(1)} copy-done((f32[64,32,128]{2,1,0:T(8,128)S(1)}, f32[64,32,128]{2,1,0:T(8,128)}, u32[]{:S(2)}) %copy-start.4) | copy-done | bytes 1048600
  4.3 0.7 shard_map.149
  5.0 4.9 %collective-permute-start = (f32[4,32,128]{2,1,0:T(8,128)S(1)}, f32[4,32,128]{2,1,0:T(8,128)S(1)}, u32[]{:S(2)}, u32[]{:S(2)}) collective-permute-start(f32[4,32,128]{2,1,0:T(8,128)S(1)} %get-tuple-element.24), channel_id=1, source_target_pairs={{0,4},{4,8},{8,12},{1,5},{5,9},{9,13},{2,6},{6,10},{10,14},{3,7},{... | collective-permute-start | bytes 196616 | tf_op jit(solution)/shard_map/ppermute | solution.py:619
  9.9 1.3 %collective-permute-start.1 = (f32[4,32,128]{2,1,0:T(8,128)S(1)}, f32[4,32,128]{2,1,0:T(8,128)S(1)}, u32[]{:S(2)}, u32[]{:S(2)}) collective-permute-start(f32[4,32,128]{2,1,0:T(8,128)S(1)} %get-tuple-element.25), channel_id=1, source_target_pairs={{4,0},{8,4},{12,8},{5,1},{9,5},{13,9},{6,2},{10,6},{14,10},{7,3},{... | collective-permute-start | bytes 196616 | tf_op jit(solution)/shard_map/ppermute | solution.py:619
  11.2 4.6 %collective-permute-start.8 = (f32[10,32,128]{2,1,0:T(8,128)S(1)}, f32[10,32,128]{2,1,0:T(8,128)S(1)}, u32[]{:S(2)}, u32[]{:S(2)}) collective-permute-start(f32[10,32,128]{2,1,0:T(8,128)S(1)} %get-tuple-element.31), channel_id=1, source_target_pairs={{0,4},{4,8},{8,12},{1,5},{5,9},{9,13},{2,6},{6,10},{10,14},{3,7},{... | collective-permute-start | bytes 491528 | tf_op jit(solution)/shard_map/ppermute | solution.py:619
  15.8 1.3 %collective-permute-start.9 = (f32[10,32,128]{2,1,0:T(8,128)S(1)}, f32[10,32,128]{2,1,0:T(8,128)S(1)}, u32[]{:S(2)}, u32[]{:S(2)}) collective-permute-start(f32[10,32,128]{2,1,0:T(8,128)S(1)} %get-tuple-element.32), channel_id=1, source_target_pairs={{4,0},{8,4},{12,8},{5,1},{9,5},{13,9},{6,2},{10,6},{14,10},{7,3},{... | collective-permute-start | bytes 491528 | tf_op jit(solution)/shard_map/ppermute | solution.py:619
  17.3 1.3 %collective-permute-start.2 = (f32[296,128]{1,0:T(8,128)S(1)}, f32[296,128]{1,0:T(8,128)S(1)}, u32[]{:S(2)}, u32[]{:S(2)}) collective-permute-start(f32[296,128]{1,0:T(8,128)S(1)} %get-tuple-element.26), channel_id=1, source_target_pairs={{0,1},{1,2},{2,3},{4,5},{5,6},{6,7},{8,9},{9,10},{10,11},{12,13},{... | collective-permute-start | bytes 454664 | tf_op jit(solution)/shard_map/ppermute | solution.py:619
  18.8 1.4 %collective-permute-start.3 = (f32[296,128]{1,0:T(8,128)S(1)}, f32[296,128]{1,0:T(8,128)S(1)}, u32[]{:S(2)}, u32[]{:S(2)}) collective-permute-start(f32[296,128]{1,0:T(8,128)S(1)} %get-tuple-element.27), channel_id=1, source_target_pairs={{1,0},{2,1},{3,2},{5,4},{6,5},{7,6},{9,8},{10,9},{11,10},{13,12},{... | collective-permute-start | bytes 454664 | tf_op jit(solution)/shard_map/ppermute | solution.py:619
  20.2 1.4 %shard_map.151.means = f32[8,128]{1,0:T(8,128)S(1)} custom-call(s32[64,32,128]{2,1,0:T(8,128)S(1)} %copy-done.1, f32[64,32,128]{2,1,0:T(8,128)S(1)} %copy-done.3, f32[3,3]{1,0:T(4,128)S(1)} %copy-done.7, f32[3]{0:T(128)S(1)} %copy-done.8), custom_call_target="tpu_custom_call" | custom-call | tf_op jit(solution)/shard_map/pallas_call | solution.py:649
  21.6 1.4 %collective-permute-done.9.refs_3_.high = f32[10,32,128]{2,1,0:T(8,128)S(1)} collective-permute-done((f32[10,32,128]{2,1,0:T(8,128)S(1)}, f32[10,32,128]{2,1,0:T(8,128)S(1)}, u32[]{:S(2)}, u32[]{:S(2)}) %collective-permute-start.9) | collective-permute-done | bytes 163872 | tf_op jit(solution)/shard_map/ppermute | solution.py:619
  23.0 0.5 shard_map.154
  23.5 3.4 %collective-permute-start.10 = (f32[744,128]{1,0:T(8,128)S(1)}, f32[744,128]{1,0:T(8,128)S(1)}, u32[]{:S(2)}, u32[]{:S(2)}) collective-permute-start(f32[744,128]{1,0:T(8,128)S(1)} %get-tuple-element.33), channel_id=1, source_target_pairs={{0,1},{1,2},{2,3},{4,5},{5,6},{6,7},{8,9},{9,10},{10,11},{12,13},{... | collective-permute-start | bytes 1142792 | tf_op jit(solution)/shard_map/ppermute | solution.py:619
  26.9 1.3 %collective-permute-start.11 = (f32[744,128]{1,0:T(8,128)S(1)}, f32[744,128]{1,0:T(8,128)S(1)}, u32[]{:S(2)}, u32[]{:S(2)}) collective-permute-start(f32[744,128]{1,0:T(8,128)S(1)} %get-tuple-element.34), channel_id=1, source_target_pairs={{1,0},{2,1},{3,2},{5,4},{6,5},{7,6},{9,8},{10,9},{11,10},{13,12},{... | collective-permute-start | bytes 1142792 | tf_op jit(solution)/shard_map/ppermute | solution.py:619
  28.4 6.7 %shard_map.152 = (f32[74,48,128]{2,1,0:T(8,128)S(1)}, f32[64,32,128]{2,1,0:T(8,128)S(1)}) custom-call(f32[64,32,128]{2,1,0:T(8,128)S(1)} %copy-done.5, f32[4,32,128]{2,1,0:T(8,128)S(1)} %collective-permute-done.refs_1_.low, f32[4,32,128]{2,1,0:T(8,128)S(1)} %collective-permute-done.1.refs_2_.high, f32[296,128]{1,0:T(8,128)S(1)} %collective-permute-done.2.left, ...), custom_call_target="tpu_custom_call" | custom-call | flops 4000000000 | tf_op jit(solution)/shard_map/pallas_call | solution.py:655
  35.1 1.3 %collective-permute-start.5 = (f32[5,32,128]{2,1,0:T(8,128)S(1)}, f32[5,32,128]{2,1,0:T(8,128)S(1)}, u32[]{:S(2)}, u32[]{:S(2)}) collective-permute-start(f32[5,32,128]{2,1,0:T(8,128)S(1)} %get-tuple-element.46), channel_id=1, source_target_pairs={{4,0},{8,4},{12,8},{5,1},{9,5},{13,9},{6,2},{10,6},{14,10},{7,3},{... | collective-permute-start | bytes 245768 | tf_op jit(solution)/shard_map/ppermute | solution.py:619
  36.4 5.2 %collective-permute-start.4 = (f32[5,32,128]{2,1,0:T(8,128)S(1)}, f32[5,32,128]{2,1,0:T(8,128)S(1)}, u32[]{:S(2)}, u32[]{:S(2)}) collective-permute-start(f32[5,32,128]{2,1,0:T(8,128)S(1)} %get-tuple-element.47), channel_id=1, source_target_pairs={{0,4},{4,8},{8,12},{1,5},{5,9},{9,13},{2,6},{6,10},{10,14},{3,7},{... | collective-permute-start | bytes 245768 | tf_op jit(solution)/shard_map/ppermute | solution.py:619
  42.0 1.6 %collective-permute-done.4.refs_1_.low = f32[5,32,128]{2,1,0:T(8,128)S(1)} collective-permute-done((f32[5,32,128]{2,1,0:T(8,128)S(1)}, f32[5,32,128]{2,1,0:T(8,128)S(1)}, u32[]{:S(2)}, u32[]{:S(2)}) %collective-permute-start.4) | collective-permute-done | bytes 81952 | tf_op jit(solution)/shard_map/ppermute | solution.py:619
  43.9 3.4 %collective-permute-start.6 = (f32[376,128]{1,0:T(8,128)S(1)}, f32[376,128]{1,0:T(8,128)S(1)}, u32[]{:S(2)}, u32[]{:S(2)}) collective-permute-start(f32[376,128]{1,0:T(8,128)S(1)} %get-tuple-element.29), channel_id=1, source_target_pairs={{0,1},{1,2},{2,3},{4,5},{5,6},{6,7},{8,9},{9,10},{10,11},{12,13},{... | collective-permute-start | bytes 577544 | tf_op jit(solution)/shard_map/ppermute | solution.py:619
  47.3 1.3 %collective-permute-start.7 = (f32[376,128]{1,0:T(8,128)S(1)}, f32[376,128]{1,0:T(8,128)S(1)}, u32[]{:S(2)}, u32[]{:S(2)}) collective-permute-start(f32[376,128]{1,0:T(8,128)S(1)} %get-tuple-element.30), channel_id=1, source_target_pairs={{1,0},{2,1},{3,2},{5,4},{6,5},{7,6},{9,8},{10,9},{11,10},{13,12},{... | collective-permute-start | bytes 577544 | tf_op jit(solution)/shard_map/ppermute | solution.py:619
  48.6 4.1 %shard_map.155 = (f32[74,48,128]{2,1,0:T(8,128)S(1)}, f32[74,48,128]{2,1,0:T(8,128)S(1)}, f32[74,48,128]{2,1,0:T(8,128)S(1)}, f32[74,48,128]{2,1,0:T(8,128)S(1)}, f32[16,128]{1,0:T(8,128)S(1)}) custom-call(s32[64,32,128]{2,1,0:T(8,128)S(1)} %copy-done.1, f32[64,32,128]{2,1,0:T(8,128)S(1)} %copy-done.3, f32[64,32,128]{2,1,0:T(8,128)S(1)} %copy-done.5, ...), custom_call_target="tpu_custom_call" | custom-call | flops 1000000000 | tf_op jit(solution)/shard_map/pallas_call | solution.py:662
  52.7 16.7 %all_to_all.5 = f32[16,1,128]{2,1,0:T(1,128)S(1)} all-to-all(f32[16,1,128]{2,1,0:T(1,128)S(1)} %bitcast.5), channel_id=1, replica_groups=mesh['groups'=2,'wide'=4,'narrow'=4] {'wide','narrow'}, dimensions={0} | all-to-all | bytes 16384 | tf_op jit(solution)/shard_map/all_to_all | solution.py:670
  69.4 1.7 %shard_map.156.solved = f32[16,128]{1,0:T(8,128)S(1)} custom-call(f32[16,128]{1,0:T(8,128)S(1)} %bitcast.4), custom_call_target="tpu_custom_call" | custom-call | tf_op jit(solution)/shard_map/pallas_call | solution.py:675
  71.1 11.1 %shard_map.157 = (f32[64,32,128]{2,1,0:T(8,128)}, f32[32,128]{1,0:T(8,128)S(1)}, f32[32,128]{1,0:T(8,128)S(1)}, f32[64,128]{1,0:T(8,128)S(1)}, f32[64,128]{1,0:T(8,128)S(1)}) custom-call(f32[64,32,128]{2,1,0:T(8,128)S(1)} %get-tuple-element.28.refs_0_.local, f32[5,32,128]{2,1,0:T(8,128)S(1)} %collective-permute-done.4.refs_1_.low, ...), custom_call_target="tpu_custom_call" | custom-call | flops 4000000000 | tf_op jit(solution)/shard_map/pallas_call | solution.py:677
  82.3 1.7 %collective-permute-start.14 = (f32[64,128]{1,0:T(8,128)S(1)}, f32[64,128]{1,0:T(8,128)S(1)}, u32[]{:S(2)}, u32[]{:S(2)}) collective-permute-start(f32[64,128]{1,0:T(8,128)S(1)} %get-tuple-element.44), channel_id=1, source_target_pairs={{0,1},{1,2},{2,3},{4,5},{5,6},{6,7},{8,9},{9,10},{10,11},{12,13},{... | collective-permute-start | bytes 98312 | tf_op jit(solution)/shard_map/ppermute | solution.py:619
  84.0 1.3 %collective-permute-start.15 = (f32[64,128]{1,0:T(8,128)S(1)}, f32[64,128]{1,0:T(8,128)S(1)}, u32[]{:S(2)}, u32[]{:S(2)}) collective-permute-start(f32[64,128]{1,0:T(8,128)S(1)} %get-tuple-element.45), channel_id=1, source_target_pairs={{1,0},{2,1},{3,2},{5,4},{6,5},{7,6},{9,8},{10,9},{11,10},{13,12},{... | collective-permute-start | bytes 98312 | tf_op jit(solution)/shard_map/ppermute | solution.py:619
  85.3 2.5 %collective-permute-start.12 = (f32[32,128]{1,0:T(8,128)S(1)}, f32[32,128]{1,0:T(8,128)S(1)}, u32[]{:S(2)}, u32[]{:S(2)}) collective-permute-start(f32[32,128]{1,0:T(8,128)S(1)} %get-tuple-element.42), channel_id=1, source_target_pairs={{0,4},{4,8},{8,12},{1,5},{5,9},{9,13},{2,6},{6,10},{10,14},{3,7},{... | collective-permute-start | bytes 49160 | tf_op jit(solution)/shard_map/ppermute | solution.py:619
  87.8 1.3 %collective-permute-start.13 = (f32[32,128]{1,0:T(8,128)S(1)}, f32[32,128]{1,0:T(8,128)S(1)}, u32[]{:S(2)}, u32[]{:S(2)}) collective-permute-start(f32[32,128]{1,0:T(8,128)S(1)} %get-tuple-element.43), channel_id=1, source_target_pairs={{4,0},{8,4},{12,8},{5,1},{9,5},{13,9},{6,2},{10,6},{14,10},{7,3},{... | collective-permute-start | bytes 49160 | tf_op jit(solution)/shard_map/ppermute | solution.py:619
  89.2 4.2 %collective-permute-done.13.high = f32[32,128]{1,0:T(8,128)S(1)} collective-permute-done((f32[32,128]{1,0:T(8,128)S(1)}, f32[32,128]{1,0:T(8,128)S(1)}, u32[]{:S(2)}, u32[]{:S(2)}) %collective-permute-start.13) | collective-permute-done | bytes 16416 | tf_op jit(solution)/shard_map/ppermute | solution.py:619
  93.4 1.2 %copy-done.6 = f32[64,32,128]{2,1,0:T(8,128)S(1)} copy-done((f32[64,32,128]{2,1,0:T(8,128)S(1)}, f32[64,32,128]{2,1,0:T(8,128)}, u32[]{:S(2)}) %copy-start.6) | copy-done | bytes 1048600
  94.6 3.7 %shard_map.158 = f32[64,32,128]{2,1,0:T(8,128)} custom-call(f32[64,32,128]{2,1,0:T(8,128)S(1)} %copy-done.5, f32[64,32,128]{2,1,0:T(8,128)S(1)} %copy-done.6, f32[32,128]{1,0:T(8,128)S(1)} %collective-permute-done.12.low, f32[32,128]{1,0:T(8,128)S(1)} %collective-permute-done.13.high, f32[64,128]{1,0:T(8,128)S(1)} %collective-permute-done.14.left, ...), custom_call_target="tpu_custom_call" | custom-call | tf_op jit(solution)/shard_map/pallas_call | solution.py:700
  (48 shorter events, 1.2 us)
Async XLA Ops:
  0.6 1.2 %copy-start = (s32[64,32,128]{2,1,0:T(8,128)S(1)}, s32[64,32,128]{2,1,0:T(8,128)}, u32[]{:S(2)}) copy-start(s32[64,32,128]{2,1,0:T(8,128)} %zone.5) | copy-start | bytes 3145732
  4.3 15.9 %copy-start.1 = (s32[64,32,128]{2,1,0:T(8,128)S(1)}, s32[64,32,128]{2,1,0:T(8,128)}, u32[]{:S(2)}) copy-start(s32[64,32,128]{2,1,0:T(8,128)} %zone.5) | copy-start | bytes 3145732
  4.3 15.9 %copy-start.3 = (f32[64,32,128]{2,1,0:T(8,128)S(1)}, f32[64,32,128]{2,1,0:T(8,128)}, u32[]{:S(2)}) copy-start(f32[64,32,128]{2,1,0:T(8,128)} %scale.5) | copy-start | bytes 3145732
  4.3 15.9 %copy-start.7 = (f32[3,3]{1,0:T(4,128)S(1)}, f32[3,3]{1,0:T(4,128)}, u32[]{:S(2)}) copy-start(f32[3,3]{1,0:T(4,128)} %diffusivity.3) | copy-start | bytes 112
  4.3 15.9 %copy-start.8 = (f32[3]{0:T(128)S(1)}, f32[3]{0:T(128)}, u32[]{:S(2)}) copy-start(f32[3]{0:T(128)} %decay.3) | copy-start | bytes 40
  5.0 12.1 %collective-permute-start = (f32[4,32,128]{2,1,0:T(8,128)S(1)}, f32[4,32,128]{2,1,0:T(8,128)S(1)}, u32[]{:S(2)}, u32[]{:S(2)}) collective-permute-start(f32[4,32,128]{2,1,0:T(8,128)S(1)} %get-tuple-element.24), channel_id=1, source_target_pairs={{0,4},{4,8},{8,12},{1,5},{5,9},{9,13},{2,6},{6,10},{10,14},{3,7},{... | collective-permute-start | bytes 196616 | tf_op jit(solution)/shard_map/ppermute | solution.py:619
  9.9 7.2 %collective-permute-start.1 = (f32[4,32,128]{2,1,0:T(8,128)S(1)}, f32[4,32,128]{2,1,0:T(8,128)S(1)}, u32[]{:S(2)}, u32[]{:S(2)}) collective-permute-start(f32[4,32,128]{2,1,0:T(8,128)S(1)} %get-tuple-element.25), channel_id=1, source_target_pairs={{4,0},{8,4},{12,8},{5,1},{9,5},{13,9},{6,2},{10,6},{14,10},{7,3},{... | collective-permute-start | bytes 196616 | tf_op jit(solution)/shard_map/ppermute | solution.py:619
  11.2 10.4 %collective-permute-start.8 = (f32[10,32,128]{2,1,0:T(8,128)S(1)}, f32[10,32,128]{2,1,0:T(8,128)S(1)}, u32[]{:S(2)}, u32[]{:S(2)}) collective-permute-start(f32[10,32,128]{2,1,0:T(8,128)S(1)} %get-tuple-element.31), channel_id=1, source_target_pairs={{0,4},{4,8},{8,12},{1,5},{5,9},{9,13},{2,6},{6,10},{10,14},{3,7},{... | collective-permute-start | bytes 491528 | tf_op jit(solution)/shard_map/ppermute | solution.py:619
  15.8 7.2 %collective-permute-start.9 = (f32[10,32,128]{2,1,0:T(8,128)S(1)}, f32[10,32,128]{2,1,0:T(8,128)S(1)}, u32[]{:S(2)}, u32[]{:S(2)}) collective-permute-start(f32[10,32,128]{2,1,0:T(8,128)S(1)} %get-tuple-element.32), channel_id=1, source_target_pairs={{4,0},{8,4},{12,8},{5,1},{9,5},{13,9},{6,2},{10,6},{14,10},{7,3},{... | collective-permute-start | bytes 491528 | tf_op jit(solution)/shard_map/ppermute | solution.py:619
  17.3 10.9 %collective-permute-start.2 = (f32[296,128]{1,0:T(8,128)S(1)}, f32[296,128]{1,0:T(8,128)S(1)}, u32[]{:S(2)}, u32[]{:S(2)}) collective-permute-start(f32[296,128]{1,0:T(8,128)S(1)} %get-tuple-element.26), channel_id=1, source_target_pairs={{0,1},{1,2},{2,3},{4,5},{5,6},{6,7},{8,9},{9,10},{10,11},{12,13},{... | collective-permute-start | bytes 454664 | tf_op jit(solution)/shard_map/ppermute | solution.py:619
  18.6 9.6 %copy-start.5 = (f32[64,32,128]{2,1,0:T(8,128)S(1)}, f32[64,32,128]{2,1,0:T(8,128)}, u32[]{:S(2)}) copy-start(f32[64,32,128]{2,1,0:T(8,128)} %load.7) | copy-start | bytes 3145732
  18.6 9.6 %copy-start.9 = (bf16[256,256]{1,0:T(8,128)(2,1)S(1)}, bf16[256,256]{1,0:T(8,128)(2,1)}, u32[]{:S(2)}) copy-start(bf16[256,256]{1,0:T(8,128)(2,1)} %constant.22.clone.rest_4_.rest_9_) | copy-start | bytes 393220
  18.7 9.6 %copy-start.10 = (bf16[192,240]{1,0:T(8,128)(2,1)S(1)}, bf16[192,240]{1,0:T(8,128)(2,1)}, u32[]{:S(2)}) copy-start(bf16[192,240]{1,0:T(8,128)(2,1)} %constant.20.clone.rest_2_.rest_7_) | copy-start | bytes 276484
  18.7 9.6 %copy-start.11 = (bf16[144,160]{1,0:T(8,128)(2,1)S(1)}, bf16[144,160]{1,0:T(8,128)(2,1)}, u32[]{:S(2)}) copy-start(bf16[144,160]{1,0:T(8,128)(2,1)} %constant.19.clone.rest_1_.rest_6_) | copy-start | bytes 138244
  18.7 9.6 %copy-start.12 = (bf16[256,128]{1,0:T(8,128)(2,1)S(1)}, bf16[256,128]{1,0:T(8,128)(2,1)}, u32[]{:S(2)}) copy-start(bf16[256,128]{1,0:T(8,128)(2,1)} %constant.23.clone.rest_5_.rest_10_) | copy-start | bytes 196612
  18.7 9.6 %copy-start.13 = (bf16[96,144]{1,0:T(8,128)(2,1)S(1)}, bf16[96,144]{1,0:T(8,128)(2,1)}, u32[]{:S(2)}) copy-start(bf16[96,144]{1,0:T(8,128)(2,1)} %constant.21.clone.rest_3_.rest_8_) | copy-start | bytes 82948
  18.7 9.6 %copy-start.14 = (f32[72,128]{1,0:T(8,128)S(1)}, f32[72,128]{1,0:T(8,128)}, u32[]{:S(2)}) copy-start(f32[72,128]{1,0:T(8,128)} %constant.24.clone.rest_6_.rest_11_) | copy-start | bytes 110596
  18.7 9.6 %copy-start.15 = (bf16[80,96]{1,0:T(8,128)(2,1)S(1)}, bf16[80,96]{1,0:T(8,128)(2,1)}, u32[]{:S(2)}) copy-start(bf16[80,96]{1,0:T(8,128)(2,1)} %constant.18.clone.rest_0_.rest_5_) | copy-start | bytes 46084
  18.7 9.6 %copy-start.16 = (f32[1,40]{1,0:T(1,128)S(1)}, f32[1,40]{1,0:T(1,128)}, u32[]{:S(2)}) copy-start(f32[1,40]{1,0:T(1,128)} %constant.26.clone.rest_8_.rest_13_) | copy-start | bytes 484
  18.7 9.6 %copy-start.17 = (f32[1,128]{1,0:T(1,128)S(1)}, f32[1,128]{1,0:T(1,128)}, u32[]{:S(2)}) copy-start(f32[1,128]{1,0:T(1,128)} %constant.25.clone.rest_7_.rest_12_) | copy-start | bytes 1540
  18.8 9.5 %collective-permute-start.3 = (f32[296,128]{1,0:T(8,128)S(1)}, f32[296,128]{1,0:T(8,128)S(1)}, u32[]{:S(2)}, u32[]{:S(2)}) collective-permute-start(f32[296,128]{1,0:T(8,128)S(1)} %get-tuple-element.27), channel_id=1, source_target_pairs={{1,0},{2,1},{3,2},{5,4},{6,5},{7,6},{9,8},{10,9},{11,10},{13,12},{... | collective-permute-start | bytes 454664 | tf_op jit(solution)/shard_map/ppermute | solution.py:619
  23.5 25.1 %collective-permute-start.10 = (f32[744,128]{1,0:T(8,128)S(1)}, f32[744,128]{1,0:T(8,128)S(1)}, u32[]{:S(2)}, u32[]{:S(2)}) collective-permute-start(f32[744,128]{1,0:T(8,128)S(1)} %get-tuple-element.33), channel_id=1, source_target_pairs={{0,1},{1,2},{2,3},{4,5},{5,6},{6,7},{8,9},{9,10},{10,11},{12,13},{... | collective-permute-start | bytes 1142792 | tf_op jit(solution)/shard_map/ppermute | solution.py:619
  26.9 21.7 %collective-permute-start.11 = (f32[744,128]{1,0:T(8,128)S(1)}, f32[744,128]{1,0:T(8,128)S(1)}, u32[]{:S(2)}, u32[]{:S(2)}) collective-permute-start(f32[744,128]{1,0:T(8,128)S(1)} %get-tuple-element.34), channel_id=1, source_target_pairs={{1,0},{2,1},{3,2},{5,4},{6,5},{7,6},{9,8},{10,9},{11,10},{13,12},{... | collective-permute-start | bytes 1142792 | tf_op jit(solution)/shard_map/ppermute | solution.py:619
  35.1 7.0 %collective-permute-start.5 = (f32[5,32,128]{2,1,0:T(8,128)S(1)}, f32[5,32,128]{2,1,0:T(8,128)S(1)}, u32[]{:S(2)}, u32[]{:S(2)}) collective-permute-start(f32[5,32,128]{2,1,0:T(8,128)S(1)} %get-tuple-element.46), channel_id=1, source_target_pairs={{4,0},{8,4},{12,8},{5,1},{9,5},{13,9},{6,2},{10,6},{14,10},{7,3},{... | collective-permute-start | bytes 245768 | tf_op jit(solution)/shard_map/ppermute | solution.py:619
  36.4 7.2 %collective-permute-start.4 = (f32[5,32,128]{2,1,0:T(8,128)S(1)}, f32[5,32,128]{2,1,0:T(8,128)S(1)}, u32[]{:S(2)}, u32[]{:S(2)}) collective-permute-start(f32[5,32,128]{2,1,0:T(8,128)S(1)} %get-tuple-element.47), channel_id=1, source_target_pairs={{0,4},{4,8},{8,12},{1,5},{5,9},{9,13},{2,6},{6,10},{10,14},{3,7},{... | collective-permute-start | bytes 245768 | tf_op jit(solution)/shard_map/ppermute | solution.py:619
  43.9 27.2 %collective-permute-start.6 = (f32[376,128]{1,0:T(8,128)S(1)}, f32[376,128]{1,0:T(8,128)S(1)}, u32[]{:S(2)}, u32[]{:S(2)}) collective-permute-start(f32[376,128]{1,0:T(8,128)S(1)} %get-tuple-element.29), channel_id=1, source_target_pairs={{0,1},{1,2},{2,3},{4,5},{5,6},{6,7},{8,9},{9,10},{10,11},{12,13},{... | collective-permute-start | bytes 577544 | tf_op jit(solution)/shard_map/ppermute | solution.py:619
  47.3 23.8 %collective-permute-start.7 = (f32[376,128]{1,0:T(8,128)S(1)}, f32[376,128]{1,0:T(8,128)S(1)}, u32[]{:S(2)}, u32[]{:S(2)}) collective-permute-start(f32[376,128]{1,0:T(8,128)S(1)} %get-tuple-element.30), channel_id=1, source_target_pairs={{1,0},{2,1},{3,2},{5,4},{6,5},{7,6},{9,8},{10,9},{11,10},{13,12},{... | collective-permute-start | bytes 577544 | tf_op jit(solution)/shard_map/ppermute | solution.py:619
  82.3 11.1 %collective-permute-start.14 = (f32[64,128]{1,0:T(8,128)S(1)}, f32[64,128]{1,0:T(8,128)S(1)}, u32[]{:S(2)}, u32[]{:S(2)}) collective-permute-start(f32[64,128]{1,0:T(8,128)S(1)} %get-tuple-element.44), channel_id=1, source_target_pairs={{0,1},{1,2},{2,3},{4,5},{5,6},{6,7},{8,9},{9,10},{10,11},{12,13},{... | collective-permute-start | bytes 98312 | tf_op jit(solution)/shard_map/ppermute | solution.py:619
  84.0 9.4 %collective-permute-start.15 = (f32[64,128]{1,0:T(8,128)S(1)}, f32[64,128]{1,0:T(8,128)S(1)}, u32[]{:S(2)}, u32[]{:S(2)}) collective-permute-start(f32[64,128]{1,0:T(8,128)S(1)} %get-tuple-element.45), channel_id=1, source_target_pairs={{1,0},{2,1},{3,2},{5,4},{6,5},{7,6},{9,8},{10,9},{11,10},{13,12},{... | collective-permute-start | bytes 98312 | tf_op jit(solution)/shard_map/ppermute | solution.py:619
  85.3 3.9 %collective-permute-start.12 = (f32[32,128]{1,0:T(8,128)S(1)}, f32[32,128]{1,0:T(8,128)S(1)}, u32[]{:S(2)}, u32[]{:S(2)}) collective-permute-start(f32[32,128]{1,0:T(8,128)S(1)} %get-tuple-element.42), channel_id=1, source_target_pairs={{0,4},{4,8},{8,12},{1,5},{5,9},{9,13},{2,6},{6,10},{10,14},{3,7},{... | collective-permute-start | bytes 49160 | tf_op jit(solution)/shard_map/ppermute | solution.py:619
  87.8 5.6 %collective-permute-start.13 = (f32[32,128]{1,0:T(8,128)S(1)}, f32[32,128]{1,0:T(8,128)S(1)}, u32[]{:S(2)}, u32[]{:S(2)}) collective-permute-start(f32[32,128]{1,0:T(8,128)S(1)} %get-tuple-element.43), channel_id=1, source_target_pairs={{4,0},{8,4},{12,8},{5,1},{9,5},{13,9},{6,2},{10,6},{14,10},{7,3},{... | collective-permute-start | bytes 49160 | tf_op jit(solution)/shard_map/ppermute | solution.py:619
  93.4 1.2 %copy-start.6 = (f32[64,32,128]{2,1,0:T(8,128)S(1)}, f32[64,32,128]{2,1,0:T(8,128)}, u32[]{:S(2)}) copy-start(f32[64,32,128]{2,1,0:T(8,128)} %get-tuple-element.22.iterate) | copy-start | bytes 3145732
  (2 other events, 2.4 us)

commit v4 on v3

--- a/solution.py
+++ b/solution.py
@@ -18,9 +18,11 @@
 cheb_ratio = 1.3 / 1.2
 rho_first = 1.0 / cheb_ratio
 rho_second = 1.0 / (2.0 * cheb_ratio - rho_first)
-
-DIAGONAL, LONG_HIGH, LONG_LOW, ACROSS_HIGH, ACROSS_LOW, LOAD_SUM, IMAGE_SUM = range(7)
-FLOW_LONG_HIGH, FLOW_LONG_LOW, FLOW_ACROSS_HIGH, FLOW_ACROSS_LOW = range(7, 11)
+gain = 2.0 * rho_second / cheb_radius
+
+MEANS = range(4)
+BOX_DIAGONAL, LONG_HIGH, LONG_LOW, ACROSS_HIGH, ACROSS_LOW, LOAD_SUM = range(4, 10)
+IMAGE_SUM, FLOW_LONG_HIGH, FLOW_LONG_LOW, FLOW_ACROSS_HIGH, FLOW_ACROSS_LOW = range(5)
 
 VMEM = pl.BlockSpec(memory_space=pltpu.VMEM)
 SMEM = pl.BlockSpec(memory_space=pltpu.SMEM)
@@ -34,12 +36,12 @@
     return table.astype(np.float32), eigvals.astype(np.float32)
 
 
-def call(body, out_shape, in_specs, scratch=(), flops=0, moved=0):
+def call(body, out_shape, in_specs, scratch=(), flops=0, moved=0, out_spec=VMEM):
     return pl.pallas_call(
         body,
         out_shape=out_shape,
         in_specs=in_specs,
-        out_specs=jax.tree.map(lambda _: VMEM, out_shape),
+        out_specs=jax.tree.map(lambda _: out_spec, out_shape),
         scratch_shapes=list(scratch),
         compiler_params=pltpu.CompilerParams(vmem_limit_bytes=30 * 2**20),
         cost_estimate=pl.CostEstimate(flops=flops, bytes_accessed=moved, transcendentals=0),
@@ -260,26 +262,12 @@
     pack_columns(box, flat, sides[0], sides[1], wide, up, down)
 
 
-def pack_edges(box, zone, scale, load, load_up, load_down, up, down, staged, sems):
+def pack_edges(box, zone, scale, up, down):
     last = box.long
-    copies = [
-        (load.at[last - MARGIN :], load_up),
-        (load.at[:MARGIN], load_down),
-        (scale.at[last - REACH :], up.at[:REACH]),
-        (scale.at[:REACH], down.at[:REACH]),
-        (zone.at[last - REACH :], staged.at[0]),
-        (zone.at[:REACH], staged.at[1]),
-    ]
-    copies = [
-        pltpu.make_async_copy(source, target, sems.at[index])
-        for index, (source, target) in enumerate(copies)
-    ]
-    for copy in copies:
-        copy.start()
-    for copy in copies:
-        copy.wait()
-    up[REACH:] = staged[0].astype(jnp.float32)
-    down[REACH:] = staged[1].astype(jnp.float32)
+    up[:REACH] = scale[last - REACH :]
+    down[:REACH] = scale[:REACH]
+    up[REACH:] = zone[last - REACH :].astype(jnp.float32)
+    down[REACH:] = zone[:REACH].astype(jnp.float32)
 
 
 def fill_window(box, window, own, low, high, left, right, wide, place, total, add=None):
@@ -330,26 +318,49 @@
     return jnp.where(labels == 0, values[0], jnp.where(labels == 1, values[1], values[2]))
 
 
-def box_means(box, zone, scale, diffusivity, decay, out):
+def line_of(numbers, shape):
+    lanes = lax.broadcasted_iota(jnp.int32, shape, 1)
+    line = jnp.zeros(shape, jnp.float32)
+    for index, number in numbers:
+        line = jnp.where(lanes == index, number, line)
+    return line
+
+
+def box_sums(box, zone, scale, load, diffusivity, decay, out):
     step = 4
     nothing = jnp.zeros((box.across, box.deep), jnp.float32)
+    half = [[0.5 * diffusivity[z, d] for z in range(3)] for d in range(3)]
+    rates = [decay[z] for z in range(3)]
+
+    def halves(row):
+        labels, factor = zone[row], scale[row]
+        return [looked_up(labels, half[d]) * factor for d in range(3)] + [looked_up(labels, rates)]
 
     def some_rows(index, sums):
         for row in range(step):
-            labels, factor = zone[index * step + row], scale[index * step + row]
-            sums = [
-                sums[d] + looked_up(labels, [diffusivity[z, d] for z in range(3)]) * factor
-                for d in range(3)
-            ] + [sums[3] + looked_up(labels, [decay[z] for z in range(3)])]
+            row = index * step + row
+            sums = [total + more for total, more in zip(sums, halves(row) + [load[row]])]
         return sums
 
-    sums = lax.fori_loop(0, box.long // step, some_rows, [nothing] * 4)
+    sums = lax.fori_loop(0, box.long // step, some_rows, [nothing] * 5)
+
+    def total(values):
+        return jnp.sum(values, keepdims=True).reshape(1, 1)
+
     cells = box.long * box.across * box.deep
-    lanes = lax.broadcasted_iota(jnp.int32, out.shape, 1)
-    line = jnp.zeros(out.shape, jnp.float32)
-    for index, values in enumerate(sums):
-        line = jnp.where(lanes == index, jnp.sum(values, keepdims=True) / cells, line)
-    out[...] = line
+    numbers = [(index, total(sums[index]) * (2.0 / cells)) for index in range(3)]
+    mass = total(sums[3])
+    numbers += [(3, mass / cells)]
+    ends = total(sums[2][:, :1]) + total(sums[2][:, box.deep - 1 :])
+    numbers += [
+        (BOX_DIAGONAL, mass + ends),
+        (LONG_HIGH, total(halves(box.long - 1)[0])),
+        (LONG_LOW, total(halves(0)[0])),
+        (ACROSS_HIGH, total(sums[1][box.across - 1 :])),
+        (ACROSS_LOW, total(sums[1][:1])),
+        (LOAD_SUM, total(sums[4])),
+    ]
+    out[...] = line_of(numbers, out.shape)
 
 
 def means_of(ref):
@@ -382,7 +393,6 @@
     box,
     zone,
     scale,
-    load,
     local,
     low,
     high,
@@ -426,119 +436,117 @@
     first, last = REACH, REACH + box.long
     inner = slice(EDGE, EDGE + box.across)
     step = 8
-    nothing = jnp.zeros((box.across, box.deep), jnp.float32)
-
-    def add_rows(index, sums):
-        mass_sum, image_sum, load_sum = sums
+
+    def add_rows(index, total):
         for row in range(step):
             row = index * step + row
-            own_mass = mass[first + row, inner]
-            mass_sum = mass_sum + own_mass
-            image_sum = image_sum + own_mass * local[row]
-            load_sum = load_sum + load[row]
-        return mass_sum, image_sum, load_sum
-
-    mass_sum, image_sum, load_sum = lax.fori_loop(0, box.long // step, add_rows, (nothing,) * 3)
+            total = total + mass[first + row, inner] * local[row]
+        return total
+
+    nothing = jnp.zeros((box.across, box.deep), jnp.float32)
+    image_sum = lax.fori_loop(0, box.long // step, add_rows, nothing)
     long_pos, across_pos, long_count, across_count = position()
-    has = [
-        as_float(long_pos < long_count - 1),
-        as_float(long_pos > 0),
-        as_float(across_pos < across_count - 1),
-        as_float(across_pos > 0),
-    ]
     across_flat = to_across.reshape(box.flat, box.deep)
     local_flat = local.reshape(box.long * box.across, box.deep)
-    faces = [
-        (to_long[last - 1, inner], local[box.long - 1]),
-        (to_long[first - 1, inner], local[0]),
-        (
-            across_flat[row_of(box.cols, EDGE + box.across - 1, box.long, first), :],
-            local_flat[row_of(box.across, box.across - 1, box.long), :],
-        ),
-        (
-            across_flat[row_of(box.cols, EDGE - 1, box.long, first), :],
-            local_flat[row_of(box.across, 0, box.long), :],
-        ),
+    flows = [
+        to_long[last - 1, inner] * local[box.long - 1],
+        to_long[first - 1, inner] * local[0],
+        across_flat[row_of(box.cols, EDGE + box.across - 1, box.long, first), :]
+        * local_flat[row_of(box.across, box.across - 1, box.long), :],
+        across_flat[row_of(box.cols, EDGE - 1, box.long, first), :]
+        * local_flat[row_of(box.across, 0, box.long), :],
     ]
-    weights = [jnp.sum(w, keepdims=True) for w, _ in faces]
-    flows = [jnp.sum(w * v, keepdims=True) for w, v in faces]
-    numbers = [jnp.sum(mass_sum, keepdims=True) + sum(weights)]
-    numbers += [w * h for w, h in zip(weights, has)]
-    numbers += [jnp.sum(load_sum, keepdims=True)]
-    numbers += [jnp.sum(image_sum, keepdims=True) + sum(flows)]
-    numbers += [f * h for f, h in zip(flows, has)]
-    lanes = lax.broadcasted_iota(jnp.int32, told.shape, 1)
-    line = jnp.zeros(told.shape, jnp.float32)
-    for index, number in enumerate(numbers):
-        line = jnp.where(lanes == index, number, line)
-    told[...] = line
-
-
-def coarse_solve(told, answers, solved):
-    count, width = solved.shape
+    flows = [jnp.sum(flow, keepdims=True) for flow in flows]
+    numbers = [
+        (IMAGE_SUM, jnp.sum(image_sum, keepdims=True) + sum(flows)),
+        (FLOW_LONG_HIGH, flows[0] * as_float(long_pos < long_count - 1)),
+        (FLOW_LONG_LOW, flows[1] * as_float(long_pos > 0)),
+        (FLOW_ACROSS_HIGH, flows[2] * as_float(across_pos < across_count - 1)),
+        (FLOW_ACROSS_LOW, flows[3] * as_float(across_pos > 0)),
+    ]
+    told[...] = line_of(numbers, told.shape)
+
+
+def column(values, index):
+    return values[:, index : index + 1]
+
+
+def coarse_inverse(told, inverse, work):
+    count, width = work.shape
     across = lax.axis_size("narrow")
     numbers = told[...]
-
-    def column(index, values=numbers):
-        return values[:, index : index + 1]
-
-    image = column(IMAGE_SUM)
-    image = image - column(FLOW_LONG_LOW, pltpu.roll(numbers, count - across, 0))
-    image = image - column(FLOW_LONG_HIGH, pltpu.roll(numbers, across, 0))
-    image = image - column(FLOW_ACROSS_LOW, pltpu.roll(numbers, count - 1, 0))
-    image = image - column(FLOW_ACROSS_HIGH, pltpu.roll(numbers, 1, 0))
+    beyond = pltpu.roll(numbers, count - across, 0)
+    beside = pltpu.roll(numbers, count - 1, 0)
+    before = pltpu.roll(numbers, across, 0)
+    ahead = pltpu.roll(numbers, 1, 0)
+    place = lax.broadcasted_iota(jnp.int32, (count, 1), 0)
+    across_pos = lax.rem(place, across)
+    nothing = jnp.zeros((count, 1), jnp.float32)
+    couplings = []
+    diagonal = column(numbers, BOX_DIAGONAL)
+    for own, other, there, inside in (
+        (LONG_HIGH, LONG_LOW, beyond, place < count - across),
+        (LONG_LOW, LONG_HIGH, before, place >= across),
+        (ACROSS_HIGH, ACROSS_LOW, beside, across_pos < across - 1),
+        (ACROSS_LOW, ACROSS_HIGH, ahead, across_pos > 0),
+    ):
+        shared = jnp.where(inside, column(there, other), nothing)
+        diagonal = diagonal + column(numbers, own) + shared
+        couplings.append(jnp.where(inside, column(numbers, own) + shared, nothing))
     rows = lax.broadcasted_iota(jnp.int32, (count, width), 0)
     cols = lax.broadcasted_iota(jnp.int32, (count, width), 1)
-    nothing = jnp.zeros((count, width), jnp.float32)
-    matrix = jnp.where(cols == rows, column(DIAGONAL), nothing)
-    matrix = matrix - jnp.where(cols == rows + across, column(LONG_HIGH), nothing)
-    matrix = matrix - jnp.where(cols == rows - across, column(LONG_LOW), nothing)
-    matrix = matrix - jnp.where(cols == rows + 1, column(ACROSS_HIGH), nothing)
-    matrix = matrix - jnp.where(cols == rows - 1, column(ACROSS_LOW), nothing)
-    matrix = jnp.where(cols == count, column(LOAD_SUM), matrix)
-    matrix = jnp.where(cols == count + 1, image, matrix)
-    solved[...] = matrix
+    blank = jnp.zeros((count, width), jnp.float32)
+    matrix = jnp.where(cols == rows, diagonal, blank)
+    for shift, coupling in zip((across, -across, 1, -1), couplings):
+        matrix = matrix - jnp.where((cols == rows + shift) & (cols < count), coupling, blank)
+    matrix = jnp.where(cols == rows + count, jnp.ones((count, 1), jnp.float32), matrix)
+    work[...] = matrix
 
     def eliminate(step, _):
-        values = solved[...]
-        pivot_row = solved[pl.ds(step, 1), :]
+        values = work[...]
+        pivot_row = work[pl.ds(step, 1), :]
         at_step = cols == step
-        factors = jnp.sum(jnp.where(at_step, values, nothing), axis=1, keepdims=True)
-        pivot = jnp.sum(jnp.where(at_step[:1], pivot_row, nothing[:1]), axis=1, keepdims=True)
+        factors = jnp.sum(jnp.where(at_step, values, blank), axis=1, keepdims=True)
+        pivot = jnp.sum(jnp.where(at_step[:1], pivot_row, blank[:1]), axis=1, keepdims=True)
         pivot_row = pivot_row / pivot
-        solved[...] = jnp.where(rows == step, pivot_row, values - factors * pivot_row)
+        work[...] = jnp.where(rows == step, pivot_row, values - factors * pivot_row)
         return 0
 
     lax.fori_loop(0, count, eliminate, 0)
-    values = solved[...]
-    lanes = lax.broadcasted_iota(jnp.int32, answers.shape, 1)
-    answers[...] = jnp.where(
-        lanes == 0, values[:, count : count + 1], values[:, count + 1 : count + 2]
-    )
-
-
-def second_solve(box, local, low, high, left, right, solved, means, *rest):
+    values = work[...]
+    if count % 128:
+        inverse[...] = pltpu.roll(values, width - count, 1)[:, : inverse.shape[1]]
+    else:
+        inverse[...] = values[:, count : 2 * count]
+
+
+def answer(inverse, sums):
+    return jnp.sum(inverse[...] * sums, axis=0, keepdims=True)
+
+
+def at_box(values, row_side, col_side):
+    long_pos, across_pos, long_count, across_count = position()
+    there_long, there_across = long_pos + row_side, across_pos + col_side
+    inside = (
+        (there_long >= 0)
+        & (there_long < long_count)
+        & (there_across >= 0)
+        & (there_across < across_count)
+    )
+    lanes = lax.broadcasted_iota(jnp.int32, values.shape, 1)
+    wanted = (lanes == there_long * across_count + there_across) & inside
+    return jnp.sum(jnp.where(wanted, values, jnp.zeros_like(values)), axis=1, keepdims=True)
+
+
+def second_solve(box, local, low, high, left, right, inverse, told, means, *rest):
     to_long, to_across, to_deep, mass, load_window = rest[:5]
     tables = rest[5 : 5 + N_TABLES]
     iterate, top, bottom, last_col, first_col = rest[5 + N_TABLES : 10 + N_TABLES]
     window, residual, spectral, middle = rest[10 + N_TABLES :]
     long_pos, across_pos, long_count, across_count = position()
-    count = long_count * across_count
-    own_box = long_pos * across_count + across_pos
-
-    def coarse(row_side, col_side, lane):
-        there_long, there_across = long_pos + row_side, across_pos + col_side
-        inside = (
-            (there_long >= 0)
-            & (there_long < long_count)
-            & (there_across >= 0)
-            & (there_across < across_count)
-        )
-        place = jnp.clip(there_long * across_count + there_across, 0, count - 1)
-        return solved[pl.ds(place, 1), lane : lane + 1] * as_float(inside)
-
+    coarse = answer(inverse, column(told, LOAD_SUM)) * (1.0 / cheb_center)
     shifts = {
-        (row_side, col_side): coarse(row_side, col_side, 0) * (1.0 / cheb_center)
+        (row_side, col_side): at_box(coarse, row_side, col_side)
         for row_side in (-1, 0, 1)
         for col_side in (-1, 0, 1)
     }
@@ -569,12 +577,10 @@
     col_mask = jnp.where(
         col_ids >= EDGE + box.across, as_float(across_pos < across_count - 1), col_mask
     )
-    own_c = coarse(0, 0, 0) * (1.0 - 1.0 / cheb_center) - coarse(0, 0, 1)
     keep = 1.0 + rho_second * rho_first
-    gain = 2.0 * rho_second / cheb_radius
 
     def emit(start, values):
-        rows = (values + own_c).reshape(8, box.across, box.deep)
+        rows = values.reshape(8, box.across, box.deep)
         before = window[first + start : first + start + 8, inner, :]
         iterate[start : start + 8] = keep * before + gain * rows
 
@@ -589,27 +595,66 @@
 
 
 def last_residual(
-    box, load, iterate, low, high, left, right, to_long, to_across, to_deep, mass, out, window
+    box,
+    load,
+    partial,
+    low,
+    high,
+    left,
+    right,
+    inverse,
+    load_told,
+    image_told,
+    to_long,
+    to_across,
+    to_deep,
+    mass,
+    iterate,
+    out,
+    window,
+    result,
+    sems,
 ):
+    count = load_told.shape[0]
+    across_count = lax.axis_size("narrow")
+    numbers = image_told[...]
+    sums = column(numbers, IMAGE_SUM)
+    sums = sums - column(pltpu.roll(numbers, count - across_count, 0), FLOW_LONG_LOW)
+    sums = sums - column(pltpu.roll(numbers, across_count, 0), FLOW_LONG_HIGH)
+    sums = sums - column(pltpu.roll(numbers, count - 1, 0), FLOW_ACROSS_LOW)
+    sums = sums - column(pltpu.roll(numbers, 1, 0), FLOW_ACROSS_HIGH)
+    sums = column(load_told, LOAD_SUM) * (1.0 - 1.0 / cheb_center) - sums
+    coarse = answer(inverse, sums) * gain
     inner = slice(EDGE, EDGE + box.across)
     flat = window.reshape((box.long + 2) * box.cols, box.deep)
     blank = jnp.zeros((box.long + 2, EDGE, box.deep), jnp.float32)
     window[:, :EDGE, :] = blank
     window[:, EDGE + box.across :, :] = blank
-    window[1 : 1 + box.long, inner, :] = iterate[...]
-    window[0, inner, :] = low[...]
-    window[1 + box.long, inner, :] = high[...]
-    flat[row_of(box.cols, EDGE - 1, box.long, 1), :] = left[...]
-    flat[row_of(box.cols, EDGE + box.across, box.long, 1), :] = right[...]
+    window[1 : 1 + box.long, inner, :] = partial[...] + at_box(coarse, 0, 0).reshape(1, 1, 1)
+    own = pltpu.make_async_copy(window.at[1 : 1 + box.long, inner, :], iterate, sems.at[0])
+    own.start()
+    window[0, inner, :] = low[...] + at_box(coarse, -1, 0)
+    window[1 + box.long, inner, :] = high[...] + at_box(coarse, 1, 0)
+    flat[row_of(box.cols, EDGE - 1, box.long, 1), :] = left[...] + at_box(coarse, 0, -1)
+    flat[row_of(box.cols, EDGE + box.across, box.long, 1), :] = right[...] + at_box(coarse, 0, 1)
     weights = (to_long, to_across, to_deep, mass)
 
     def one_row(row, flow):
         image, flow = negative_image(REACH + row, window[row + 1], window[row + 2], flow, weights)
-        out[row] = load[row] + image[inner]
+        result[row] = load[row] + image[inner]
         return flow
 
     flow = to_long[REACH - 1] * (window[1] - window[0])
-    lax.fori_loop(0, box.long, one_row, flow, unroll=4)
+    chunk = box.long // 4
+    copies = [own]
+    for index in range(4):
+        rows = slice(index * chunk, (index + 1) * chunk)
+        flow = lax.fori_loop(rows.start, rows.stop, one_row, flow, unroll=4)
+        copy = pltpu.make_async_copy(result.at[rows], out.at[rows], sems.at[1 + index])
+        copy.start()
+        copies.append(copy)
+    for copy in copies:
+        copy.wait()
 
 
 def exchange(axis, last, first):
@@ -638,17 +683,13 @@
         body = functools.partial(pack_fields, box, wide)
         return call(body, (message, message), [VMEM] * len(fields))(*fields)
 
-    near, far = f32(MARGIN, across, deep), f32(2 * REACH, across, deep)
-    load_up, load_down, up, down = call(
-        functools.partial(pack_edges, box),
-        (near, near, far, far),
-        [pl.BlockSpec(memory_space=pltpu.HBM)] * 3,
-        [pltpu.VMEM((2, REACH, across, deep), jnp.int32), pltpu.SemaphoreType.DMA((6,))],
-    )(zone, scale, load)
-    load_low, load_high = exchange("wide", load_up, load_down)
-    means = call(functools.partial(box_means, box), f32(8, 128), [VMEM] * 2 + [SMEM] * 2)(
-        zone, scale, diffusivity, decay
-    )
+    load_low, load_high = exchange("wide", load[long - MARGIN :], load[:MARGIN])
+    own_told = call(functools.partial(box_sums, box), f32(8, 128), [VMEM] * 3 + [SMEM] * 2)(
+        zone, scale, load, diffusivity, decay
+    )
+    load_told = lax.all_gather(own_told[:1], ("wide", "narrow"), axis=0, tiled=True)
+    far = f32(2 * REACH, across, deep)
+    up, down = call(functools.partial(pack_edges, box), (far, far), [VMEM] * 2)(zone, scale)
     low, high = exchange("wide", up, down)
     load_left, load_right = exchange("narrow", *pack(MARGIN, load, load_low, load_high))
     left, right = exchange("narrow", *pack(REACH, scale, zone, low, high))
@@ -658,26 +699,28 @@
         [VMEM] * (6 + N_TABLES),
         [spectral, middle],
         flops=4 * 10**9,
-    )(load, load_low, load_high, load_left, load_right, means, *tables)
-    to_long, to_across, to_deep, mass, told = call(
+    )(load, load_low, load_high, load_left, load_right, own_told, *tables)
+    to_long, to_across, to_deep, mass, image_told = call(
         functools.partial(weights_of, box),
-        (window,) * 4 + (f32(count, 128),),
-        [VMEM] * 8 + [SMEM] * 2,
+        (window,) * 4 + (f32(8, 128),),
+        [VMEM] * 7 + [SMEM] * 2,
         [scratch(window.shape)] * 2,
         flops=10**9,
-    )(zone, scale, load, local, low, high, left, right, diffusivity, decay)
+    )(zone, scale, local, low, high, left, right, diffusivity, decay)
     low, high = exchange("wide", local[long - REACH :], local[:REACH])
-    all_told = lax.all_to_all(
-        told.reshape(count, 1, 128), ("wide", "narrow"), split_axis=0, concat_axis=0, tiled=True
-    ).reshape(count, 128)
+    image_told = lax.all_gather(image_told[:1], ("wide", "narrow"), axis=0, tiled=True)
     left, right = exchange("narrow", *pack(REACH, local, low, high))
-    solved_width = -(-(count + 2) // 128) * 128
-    solved = call(coarse_solve, f32(count, 128), [VMEM], [scratch((count, solved_width))])(all_told)
+    inverse = call(
+        coarse_inverse,
+        f32(count, -(-count // 128) * 128),
+        [VMEM],
+        [scratch((count, -(-2 * count // 128) * 128))],
+    )(load_told)
     row, col = f32(across, deep), f32(long, deep)
-    iterate, top, bottom, last_col, first_col = call(
+    partial, top, bottom, last_col, first_col = call(
         functools.partial(second_solve, box),
         (cells, row, row, col, col),
-        [VMEM] * (12 + N_TABLES),
+        [VMEM] * (13 + N_TABLES),
         [scratch(window.shape), scratch((box.ex, box.cols, deep)), spectral, middle],
         flops=4 * 10**9,
     )(
@@ -686,8 +729,9 @@
         high,
         left,
         right,
-        solved,
-        means,
+        inverse,
+        load_told,
+        own_told,
         to_long,
         to_across,
         to_deep,
@@ -697,13 +741,27 @@
     )
     low, high = exchange("wide", top, bottom)
     left, right = exchange("narrow", last_col, first_col)
-    residual = call(
+    return call(
         functools.partial(last_residual, box),
-        cells,
-        [VMEM] * 10,
-        [scratch((long + 2, box.cols, deep))],
-    )(load, iterate, low, high, left, right, to_long, to_across, to_deep, mass)
-    return iterate, residual
+        (cells, cells),
+        [VMEM] * 13,
+        [scratch((long + 2, box.cols, deep)), scratch(cells.shape), pltpu.SemaphoreType.DMA((5,))],
+        out_spec=pl.BlockSpec(memory_space=pl.ANY),
+    )(
+        load,
+        partial,
+        low,
+        high,
+        left,
+        right,
+        inverse,
+        load_told,
+        image_told,
+        to_long,
+        to_across,
+        to_deep,
+        mass,
+    )
 
 
 def solution(mesh):

time: 99.2 us -> 124 us (1.25)
  blocking collectives: 16.7 us -> 48 us
  waiting for transfers between devices: 7.77 us -> 2.28 us
  Pallas kernels: 30.3 us -> 28.8 us
    all_gather x0 -> x2, blocking collectives: none -> 48 us  [the longest x1 26.3 us: on_device(): lax.all_gather(own_told[:1], ('wide', 'narrow'), axis=0, tiled=True)]
    all_to_all x1 -> x0, blocking collectives: 16.7 us -> none  [on_device(): lax.all_to_all(told.reshape(count, 1, 128), ('wide', 'narrow'), split_axi...]
    ppermute x16, waiting for transfers between devices: 7.77 us -> 2.28 us  [exchange(): return (lax.ppermute(last, axis, up), lax.ppermute(first, axis, down))]
  transfers between devices with their start and end apart: 16 -> 16, of which waited for: 5 -> 3; matrix products, arithmetic and copies ran while one was open for 0% -> 0% of each run, Pallas kernels for 15% -> 12%
where the time goes in v4:
time: 124 us; the launch traced here: 123 us
  blocking collectives  48 us (39%)
  starting transfers between devices  37.9 us (31%)
  Pallas kernels  28.8 us (23%)
  local copies, waits for them, and re-layouts  4.66 us (4%)
  waiting for transfers between devices  2.28 us (2%)
  between operations  1.27 us (1%)
    ppermute x16, starting transfers between devices, exchange(): return (lax.ppermute(last, axis, up), lax.ppermute(first, axis, down))  37.9 us
    all_gather x1, blocking collectives, on_device(): lax.all_gather(own_told[:1], ('wide', 'narrow'), axis=0, tiled=True)  26.3 us
    all_gather x1, blocking collectives, on_device(): lax.all_gather(image_told[:1], ('wide', 'narrow'), axis=0, tiled=True)  21.7 us
    pallas_call x1, Pallas kernels, on_device(): call(functools.partial(second_solve, box), (cells, row, row, col, col), [...  10.2 us
    pallas_call x1, Pallas kernels, on_device(): call(functools.partial(first_solve, box), (window, cells), [VMEM] * (6 +...  6.69 us
    pallas_call x1, Pallas kernels, on_device(): call(functools.partial(weights_of, box), (window,) * 4 + (f32(8, 128),),...  4.08 us
    unnamed x36, local copies, waits for them, and re-layouts  3.75 us
    pallas_call x1, Pallas kernels, on_device(): call(functools.partial(last_residual, box), (cells, cells), [VMEM] * 13,...  3.69 us
  transfers between devices with their start and end apart: 16, of which 3 were waited for; matrix products, arithmetic and copies ran while one was open for 0% of the time, Pallas kernels for 12%

profile of v4, /device:TPU:0, one launch (start us, length us, event | category | flops | bytes accessed | tf_op | source)
XLA Modules:
  0.0 122.9 jit_solution(16955302598869360624)
XLA Ops:
  0.6 0.9 fusion.1
  1.5 1.3 %collective-permute-start.1 = (f32[4,32,128]{2,1,0:T(8,128)S(1)}, f32[4,32,128]{2,1,0:T(8,128)S(1)}, u32[]{:S(2)}, u32[]{:S(2)}) collective-permute-start(f32[4,32,128]{2,1,0:T(8,128)S(1)} %get-tuple-element.44), channel_id=1, source_target_pairs={{4,0},{8,4},{12,8},{5,1},{9,5},{13,9},{6,2},{10,6},{14,10},{7,3},{... | collective-permute-start | bytes 196616 | tf_op jit(solution)/shard_map/ppermute | solution.py:664
  2.8 5.6 %collective-permute-start = (f32[4,32,128]{2,1,0:T(8,128)S(1)}, f32[4,32,128]{2,1,0:T(8,128)S(1)}, u32[]{:S(2)}, u32[]{:S(2)}) collective-permute-start(f32[4,32,128]{2,1,0:T(8,128)S(1)} %get-tuple-element.45), channel_id=1, source_target_pairs={{0,4},{4,8},{8,12},{1,5},{5,9},{9,13},{2,6},{6,10},{10,14},{3,7},{... | collective-permute-start | bytes 196616 | tf_op jit(solution)/shard_map/ppermute | solution.py:664
  8.4 1.2 copy-done
  9.6 1.2 copy-done.2
  10.9 4.1 %collective-permute-start.8 = (f32[10,32,128]{2,1,0:T(8,128)S(1)}, f32[10,32,128]{2,1,0:T(8,128)S(1)}, u32[]{:S(2)}, u32[]{:S(2)}) collective-permute-start(f32[10,32,128]{2,1,0:T(8,128)S(1)} %get-tuple-element.27), channel_id=1, source_target_pairs={{0,4},{4,8},{8,12},{1,5},{5,9},{9,13},{2,6},{6,10},{10,14},{3,7},{... | collective-permute-start | bytes 491528 | tf_op jit(solution)/shard_map/ppermute | solution.py:664
  15.0 1.3 %collective-permute-start.9 = (f32[10,32,128]{2,1,0:T(8,128)S(1)}, f32[10,32,128]{2,1,0:T(8,128)S(1)}, u32[]{:S(2)}, u32[]{:S(2)}) collective-permute-start(f32[10,32,128]{2,1,0:T(8,128)S(1)} %get-tuple-element.28), channel_id=1, source_target_pairs={{4,0},{8,4},{12,8},{5,1},{9,5},{13,9},{6,2},{10,6},{14,10},{7,3},{... | collective-permute-start | bytes 491528 | tf_op jit(solution)/shard_map/ppermute | solution.py:664
  16.3 1.2 copy-done.4
  17.7 1.3 %collective-permute-start.2 = (f32[296,128]{1,0:T(8,128)S(1)}, f32[296,128]{1,0:T(8,128)S(1)}, u32[]{:S(2)}, u32[]{:S(2)}) collective-permute-start(f32[296,128]{1,0:T(8,128)S(1)} %get-tuple-element.22), channel_id=1, source_target_pairs={{0,1},{1,2},{2,3},{4,5},{5,6},{6,7},{8,9},{9,10},{10,11},{12,13},{... | collective-permute-start | bytes 454664 | tf_op jit(solution)/shard_map/ppermute | solution.py:664
  19.0 1.3 %collective-permute-start.3 = (f32[296,128]{1,0:T(8,128)S(1)}, f32[296,128]{1,0:T(8,128)S(1)}, u32[]{:S(2)}, u32[]{:S(2)}) collective-permute-start(f32[296,128]{1,0:T(8,128)S(1)} %get-tuple-element.23), channel_id=1, source_target_pairs={{1,0},{2,1},{3,2},{5,4},{6,5},{7,6},{9,8},{10,9},{11,10},{13,12},{... | collective-permute-start | bytes 454664 | tf_op jit(solution)/shard_map/ppermute | solution.py:664
  20.4 1.5 %shard_map.150.means = f32[8,128]{1,0:T(8,128)S(1)} custom-call(s32[64,32,128]{2,1,0:T(8,128)S(1)} %copy-done.1, f32[64,32,128]{2,1,0:T(8,128)S(1)} %copy-done.3, f32[64,32,128]{2,1,0:T(8,128)S(1)} %copy-done.4, f32[3,3]{1,0:T(4,128)S(1)} %copy-done.6, f32[3]{0:T(128)S(1)} %copy-done.7), custom_call_target="tpu_custom_call" | custom-call | tf_op jit(solution)/shard_map/pallas_call | solution.py:687
  22.2 0.5 shard_map.155
  22.7 4.6 %collective-permute-start.10 = (f32[744,128]{1,0:T(8,128)S(1)}, f32[744,128]{1,0:T(8,128)S(1)}, u32[]{:S(2)}, u32[]{:S(2)}) collective-permute-start(f32[744,128]{1,0:T(8,128)S(1)} %get-tuple-element.29), channel_id=1, source_target_pairs={{0,1},{1,2},{2,3},{4,5},{5,6},{6,7},{8,9},{9,10},{10,11},{12,13},{... | collective-permute-start | bytes 1142792 | tf_op jit(solution)/shard_map/ppermute | solution.py:664
  27.3 1.3 %collective-permute-start.11 = (f32[744,128]{1,0:T(8,128)S(1)}, f32[744,128]{1,0:T(8,128)S(1)}, u32[]{:S(2)}, u32[]{:S(2)}) collective-permute-start(f32[744,128]{1,0:T(8,128)S(1)} %get-tuple-element.30), channel_id=1, source_target_pairs={{1,0},{2,1},{3,2},{5,4},{6,5},{7,6},{9,8},{10,9},{11,10},{13,12},{... | collective-permute-start | bytes 1142792 | tf_op jit(solution)/shard_map/ppermute | solution.py:664
  28.7 6.7 %shard_map.151 = (f32[74,48,128]{2,1,0:T(8,128)S(1)}, f32[64,32,128]{2,1,0:T(8,128)S(1)}) custom-call(f32[64,32,128]{2,1,0:T(8,128)S(1)} %copy-done.4, f32[4,32,128]{2,1,0:T(8,128)S(1)} %collective-permute-done.refs_1_.low, f32[4,32,128]{2,1,0:T(8,128)S(1)} %collective-permute-done.1.refs_2_.high, f32[296,128]{1,0:T(8,128)S(1)} %collective-permute-done.2.left, ...), custom_call_target="tpu_custom_call" | custom-call | flops 4000000000 | tf_op jit(solution)/shard_map/pallas_call | solution.py:696
  35.4 1.3 %collective-permute-start.5 = (f32[5,32,128]{2,1,0:T(8,128)S(1)}, f32[5,32,128]{2,1,0:T(8,128)S(1)}, u32[]{:S(2)}, u32[]{:S(2)}) collective-permute-start(f32[5,32,128]{2,1,0:T(8,128)S(1)} %get-tuple-element.42), channel_id=1, source_target_pairs={{4,0},{8,4},{12,8},{5,1},{9,5},{13,9},{6,2},{10,6},{14,10},{7,3},{... | collective-permute-start | bytes 245768 | tf_op jit(solution)/shard_map/ppermute | solution.py:664
  36.7 5.2 %collective-permute-start.4 = (f32[5,32,128]{2,1,0:T(8,128)S(1)}, f32[5,32,128]{2,1,0:T(8,128)S(1)}, u32[]{:S(2)}, u32[]{:S(2)}) collective-permute-start(f32[5,32,128]{2,1,0:T(8,128)S(1)} %get-tuple-element.43), channel_id=1, source_target_pairs={{0,4},{4,8},{8,12},{1,5},{5,9},{9,13},{2,6},{6,10},{10,14},{3,7},{... | collective-permute-start | bytes 245768 | tf_op jit(solution)/shard_map/ppermute | solution.py:664
  41.9 0.5 collective-permute-done.5.refs_2_.high
  42.4 1.6 %collective-permute-done.4.refs_1_.low = f32[5,32,128]{2,1,0:T(8,128)S(1)} collective-permute-done((f32[5,32,128]{2,1,0:T(8,128)S(1)}, f32[5,32,128]{2,1,0:T(8,128)S(1)}, u32[]{:S(2)}, u32[]{:S(2)}) %collective-permute-start.4) | collective-permute-done | bytes 81952 | tf_op jit(solution)/shard_map/ppermute | solution.py:664
  43.9 0.3 shard_map.152
  44.2 3.4 %collective-permute-start.6 = (f32[376,128]{1,0:T(8,128)S(1)}, f32[376,128]{1,0:T(8,128)S(1)}, u32[]{:S(2)}, u32[]{:S(2)}) collective-permute-start(f32[376,128]{1,0:T(8,128)S(1)} %get-tuple-element.25), channel_id=1, source_target_pairs={{0,1},{1,2},{2,3},{4,5},{5,6},{6,7},{8,9},{9,10},{10,11},{12,13},{... | collective-permute-start | bytes 577544 | tf_op jit(solution)/shard_map/ppermute | solution.py:664
  47.6 1.3 %collective-permute-start.7 = (f32[376,128]{1,0:T(8,128)S(1)}, f32[376,128]{1,0:T(8,128)S(1)}, u32[]{:S(2)}, u32[]{:S(2)}) collective-permute-start(f32[376,128]{1,0:T(8,128)S(1)} %get-tuple-element.26), channel_id=1, source_target_pairs={{1,0},{2,1},{3,2},{5,4},{6,5},{7,6},{9,8},{10,9},{11,10},{13,12},{... | collective-permute-start | bytes 577544 | tf_op jit(solution)/shard_map/ppermute | solution.py:664
  48.9 26.3 %all-gather = f32[16,1,128]{2,1,0:T(1,128)S(1)} all-gather(f32[1,1,128]{2,1,0:T(1,128)S(1)} %slice_bitcast_fusion.1), channel_id=1, replica_groups=mesh['groups'=2,'wide'=4,'narrow'=4] {'wide','narrow'}, dimensions={0}, use_global_device_ids=true | all-gather | bytes 8704 | tf_op jit(solution)/shard_map/all_gather | solution.py:690
  75.2 1.7 %shard_map.153.inverse = f32[16,128]{1,0:T(8,128)S(1)} custom-call(f32[16,128]{1,0:T(8,128)S(1)} %bitcast.6), custom_call_target="tpu_custom_call" | custom-call | tf_op jit(solution)/shard_map/pallas_call | solution.py:713
  76.9 4.1 %shard_map.156 = (f32[74,48,128]{2,1,0:T(8,128)S(1)}, f32[74,48,128]{2,1,0:T(8,128)S(1)}, f32[74,48,128]{2,1,0:T(8,128)S(1)}, f32[74,48,128]{2,1,0:T(8,128)S(1)}, f32[8,128]{1,0:T(8,128)S(1)}) custom-call(s32[64,32,128]{2,1,0:T(8,128)S(1)} %copy-done.1, f32[64,32,128]{2,1,0:T(8,128)S(1)} %copy-done.3, f32[64,32,128]{2,1,0:T(8,128)S(1)} %get-tuple-element.24.refs_0_.local, ...), custom_call_target="tpu_custom_call" | custom-call | flops 1000000000 | tf_op jit(solution)/shard_map/pallas_call | solution.py:703
  81.0 10.2 %shard_map.157 = (f32[64,32,128]{2,1,0:T(8,128)S(1)}, f32[32,128]{1,0:T(8,128)S(1)}, f32[32,128]{1,0:T(8,128)S(1)}, f32[64,128]{1,0:T(8,128)S(1)}, f32[64,128]{1,0:T(8,128)S(1)}) custom-call(f32[64,32,128]{2,1,0:T(8,128)S(1)} %get-tuple-element.24.refs_0_.local, f32[5,32,128]{2,1,0:T(8,128)S(1)} %collective-permute-done.4.refs_1_.low, ...), custom_call_target="tpu_custom_call" | custom-call | flops 4000000000 | tf_op jit(solution)/shard_map/pallas_call | solution.py:720
  91.2 1.3 %collective-permute-start.12 = (f32[32,128]{1,0:T(8,128)S(1)}, f32[32,128]{1,0:T(8,128)S(1)}, u32[]{:S(2)}, u32[]{:S(2)}) collective-permute-start(f32[32,128]{1,0:T(8,128)S(1)} %get-tuple-element.37), channel_id=1, source_target_pairs={{0,4},{4,8},{8,12},{1,5},{5,9},{9,13},{2,6},{6,10},{10,14},{3,7},{... | collective-permute-start | bytes 49160 | tf_op jit(solution)/shard_map/ppermute | solution.py:664
  92.5 1.3 %collective-permute-start.13 = (f32[32,128]{1,0:T(8,128)S(1)}, f32[32,128]{1,0:T(8,128)S(1)}, u32[]{:S(2)}, u32[]{:S(2)}) collective-permute-start(f32[32,128]{1,0:T(8,128)S(1)} %get-tuple-element.38), channel_id=1, source_target_pairs={{4,0},{8,4},{12,8},{5,1},{9,5},{13,9},{6,2},{10,6},{14,10},{7,3},{... | collective-permute-start | bytes 49160 | tf_op jit(solution)/shard_map/ppermute | solution.py:664
  93.8 2.2 %collective-permute-start.14 = (f32[64,128]{1,0:T(8,128)S(1)}, f32[64,128]{1,0:T(8,128)S(1)}, u32[]{:S(2)}, u32[]{:S(2)}) collective-permute-start(f32[64,128]{1,0:T(8,128)S(1)} %get-tuple-element.39), channel_id=1, source_target_pairs={{0,1},{1,2},{2,3},{4,5},{5,6},{6,7},{8,9},{9,10},{10,11},{12,13},{... | collective-permute-start | bytes 98312 | tf_op jit(solution)/shard_map/ppermute | solution.py:664
  96.0 1.3 %collective-permute-start.15 = (f32[64,128]{1,0:T(8,128)S(1)}, f32[64,128]{1,0:T(8,128)S(1)}, u32[]{:S(2)}, u32[]{:S(2)}) collective-permute-start(f32[64,128]{1,0:T(8,128)S(1)} %get-tuple-element.40), channel_id=1, source_target_pairs={{1,0},{2,1},{3,2},{5,4},{6,5},{7,6},{9,8},{10,9},{11,10},{13,12},{... | collective-permute-start | bytes 98312 | tf_op jit(solution)/shard_map/ppermute | solution.py:664
  97.3 21.7 %all-gather.1 = f32[16,1,128]{2,1,0:T(1,128)S(1)} all-gather(f32[1,1,128]{2,1,0:T(1,128)S(1)} %slice_bitcast_fusion), channel_id=1, replica_groups=mesh['groups'=2,'wide'=4,'narrow'=4] {'wide','narrow'}, dimensions={0}, use_global_device_ids=true | all-gather | bytes 8704 | tf_op jit(solution)/shard_map/all_gather | solution.py:711
  119.1 3.7 %shard_map.158 = (f32[64,32,128]{2,1,0:T(8,128)}, f32[64,32,128]{2,1,0:T(8,128)}) custom-call(f32[64,32,128]{2,1,0:T(8,128)S(1)} %copy-done.5, f32[64,32,128]{2,1,0:T(8,128)S(1)} %get-tuple-element.36.partial, f32[32,128]{1,0:T(8,128)S(1)} %collective-permute-done.12.low, f32[32,128]{1,0:T(8,128)S(1)} %collective-permute-done.13.high, ...), custom_call_target="tpu_custom_call" | custom-call | tf_op jit(solution)/shard_map/pallas_call | solution.py:744
  (50 shorter events, 0.6 us)
Async XLA Ops:
  0.6 19.7 %copy-start.7 = (f32[3]{0:T(128)S(1)}, f32[3]{0:T(128)}, u32[]{:S(2)}) copy-start(f32[3]{0:T(128)} %decay.3) | copy-start | bytes 40
  0.6 19.7 %copy-start.6 = (f32[3,3]{1,0:T(4,128)S(1)}, f32[3,3]{1,0:T(4,128)}, u32[]{:S(2)}) copy-start(f32[3,3]{1,0:T(4,128)} %diffusivity.3) | copy-start | bytes 112
  1.5 14.7 %collective-permute-start.1 = (f32[4,32,128]{2,1,0:T(8,128)S(1)}, f32[4,32,128]{2,1,0:T(8,128)S(1)}, u32[]{:S(2)}, u32[]{:S(2)}) collective-permute-start(f32[4,32,128]{2,1,0:T(8,128)S(1)} %get-tuple-element.44), channel_id=1, source_target_pairs={{4,0},{8,4},{12,8},{5,1},{9,5},{13,9},{6,2},{10,6},{14,10},{7,3},{... | collective-permute-start | bytes 196616 | tf_op jit(solution)/shard_map/ppermute | solution.py:664
  2.8 13.4 %collective-permute-start = (f32[4,32,128]{2,1,0:T(8,128)S(1)}, f32[4,32,128]{2,1,0:T(8,128)S(1)}, u32[]{:S(2)}, u32[]{:S(2)}) collective-permute-start(f32[4,32,128]{2,1,0:T(8,128)S(1)} %get-tuple-element.45), channel_id=1, source_target_pairs={{0,4},{4,8},{8,12},{1,5},{5,9},{9,13},{2,6},{6,10},{10,14},{3,7},{... | collective-permute-start | bytes 196616 | tf_op jit(solution)/shard_map/ppermute | solution.py:664
  8.4 1.2 copy-start
  10.9 9.5 %copy-start.1 = (s32[64,32,128]{2,1,0:T(8,128)S(1)}, s32[64,32,128]{2,1,0:T(8,128)}, u32[]{:S(2)}) copy-start(s32[64,32,128]{2,1,0:T(8,128)} %zone.5) | copy-start | bytes 3145732
  10.9 9.5 %copy-start.3 = (f32[64,32,128]{2,1,0:T(8,128)S(1)}, f32[64,32,128]{2,1,0:T(8,128)}, u32[]{:S(2)}) copy-start(f32[64,32,128]{2,1,0:T(8,128)} %scale.5) | copy-start | bytes 3145732
  10.9 11.1 %collective-permute-start.8 = (f32[10,32,128]{2,1,0:T(8,128)S(1)}, f32[10,32,128]{2,1,0:T(8,128)S(1)}, u32[]{:S(2)}, u32[]{:S(2)}) collective-permute-start(f32[10,32,128]{2,1,0:T(8,128)S(1)} %get-tuple-element.27), channel_id=1, source_target_pairs={{0,4},{4,8},{8,12},{1,5},{5,9},{9,13},{2,6},{6,10},{10,14},{3,7},{... | collective-permute-start | bytes 491528 | tf_op jit(solution)/shard_map/ppermute | solution.py:664
  15.0 7.2 %collective-permute-start.9 = (f32[10,32,128]{2,1,0:T(8,128)S(1)}, f32[10,32,128]{2,1,0:T(8,128)S(1)}, u32[]{:S(2)}, u32[]{:S(2)}) collective-permute-start(f32[10,32,128]{2,1,0:T(8,128)S(1)} %get-tuple-element.28), channel_id=1, source_target_pairs={{4,0},{8,4},{12,8},{5,1},{9,5},{13,9},{6,2},{10,6},{14,10},{7,3},{... | collective-permute-start | bytes 491528 | tf_op jit(solution)/shard_map/ppermute | solution.py:664
  16.3 1.2 copy-start.4
  17.7 10.9 %collective-permute-start.2 = (f32[296,128]{1,0:T(8,128)S(1)}, f32[296,128]{1,0:T(8,128)S(1)}, u32[]{:S(2)}, u32[]{:S(2)}) collective-permute-start(f32[296,128]{1,0:T(8,128)S(1)} %get-tuple-element.22), channel_id=1, source_target_pairs={{0,1},{1,2},{2,3},{4,5},{5,6},{6,7},{8,9},{9,10},{10,11},{12,13},{... | collective-permute-start | bytes 454664 | tf_op jit(solution)/shard_map/ppermute | solution.py:664
  19.0 9.6 %collective-permute-start.3 = (f32[296,128]{1,0:T(8,128)S(1)}, f32[296,128]{1,0:T(8,128)S(1)}, u32[]{:S(2)}, u32[]{:S(2)}) collective-permute-start(f32[296,128]{1,0:T(8,128)S(1)} %get-tuple-element.23), channel_id=1, source_target_pairs={{1,0},{2,1},{3,2},{5,4},{6,5},{7,6},{9,8},{10,9},{11,10},{13,12},{... | collective-permute-start | bytes 454664 | tf_op jit(solution)/shard_map/ppermute | solution.py:664
  21.8 6.7 %copy-start.8 = (bf16[256,256]{1,0:T(8,128)(2,1)S(1)}, bf16[256,256]{1,0:T(8,128)(2,1)}, u32[]{:S(2)}) copy-start(bf16[256,256]{1,0:T(8,128)(2,1)} %constant.22.clone.rest_4_.rest_9_) | copy-start | bytes 393220
  21.9 6.7 %copy-start.9 = (bf16[192,240]{1,0:T(8,128)(2,1)S(1)}, bf16[192,240]{1,0:T(8,128)(2,1)}, u32[]{:S(2)}) copy-start(bf16[192,240]{1,0:T(8,128)(2,1)} %constant.20.clone.rest_2_.rest_7_) | copy-start | bytes 276484
  21.9 6.7 %copy-start.10 = (bf16[144,160]{1,0:T(8,128)(2,1)S(1)}, bf16[144,160]{1,0:T(8,128)(2,1)}, u32[]{:S(2)}) copy-start(bf16[144,160]{1,0:T(8,128)(2,1)} %constant.19.clone.rest_1_.rest_6_) | copy-start | bytes 138244
  21.9 6.7 %copy-start.11 = (bf16[256,128]{1,0:T(8,128)(2,1)S(1)}, bf16[256,128]{1,0:T(8,128)(2,1)}, u32[]{:S(2)}) copy-start(bf16[256,128]{1,0:T(8,128)(2,1)} %constant.23.clone.rest_5_.rest_10_) | copy-start | bytes 196612
  21.9 6.7 %copy-start.12 = (bf16[96,144]{1,0:T(8,128)(2,1)S(1)}, bf16[96,144]{1,0:T(8,128)(2,1)}, u32[]{:S(2)}) copy-start(bf16[96,144]{1,0:T(8,128)(2,1)} %constant.21.clone.rest_3_.rest_8_) | copy-start | bytes 82948
  21.9 6.7 %copy-start.13 = (f32[72,128]{1,0:T(8,128)S(1)}, f32[72,128]{1,0:T(8,128)}, u32[]{:S(2)}) copy-start(f32[72,128]{1,0:T(8,128)} %constant.24.clone.rest_6_.rest_11_) | copy-start | bytes 110596
  21.9 6.7 %copy-start.14 = (bf16[80,96]{1,0:T(8,128)(2,1)S(1)}, bf16[80,96]{1,0:T(8,128)(2,1)}, u32[]{:S(2)}) copy-start(bf16[80,96]{1,0:T(8,128)(2,1)} %constant.18.clone.rest_0_.rest_5_) | copy-start | bytes 46084
  21.9 6.7 %copy-start.15 = (f32[1,40]{1,0:T(1,128)S(1)}, f32[1,40]{1,0:T(1,128)}, u32[]{:S(2)}) copy-start(f32[1,40]{1,0:T(1,128)} %constant.26.clone.rest_8_.rest_13_) | copy-start | bytes 484
  21.9 6.7 %copy-start.16 = (f32[1,128]{1,0:T(1,128)S(1)}, f32[1,128]{1,0:T(1,128)}, u32[]{:S(2)}) copy-start(f32[1,128]{1,0:T(1,128)} %constant.25.clone.rest_7_.rest_12_) | copy-start | bytes 1540
  22.7 54.2 %collective-permute-start.10 = (f32[744,128]{1,0:T(8,128)S(1)}, f32[744,128]{1,0:T(8,128)S(1)}, u32[]{:S(2)}, u32[]{:S(2)}) collective-permute-start(f32[744,128]{1,0:T(8,128)S(1)} %get-tuple-element.29), channel_id=1, source_target_pairs={{0,1},{1,2},{2,3},{4,5},{5,6},{6,7},{8,9},{9,10},{10,11},{12,13},{... | collective-permute-start | bytes 1142792 | tf_op jit(solution)/shard_map/ppermute | solution.py:664
  27.3 49.6 %collective-permute-start.11 = (f32[744,128]{1,0:T(8,128)S(1)}, f32[744,128]{1,0:T(8,128)S(1)}, u32[]{:S(2)}, u32[]{:S(2)}) collective-permute-start(f32[744,128]{1,0:T(8,128)S(1)} %get-tuple-element.30), channel_id=1, source_target_pairs={{1,0},{2,1},{3,2},{5,4},{6,5},{7,6},{9,8},{10,9},{11,10},{13,12},{... | collective-permute-start | bytes 1142792 | tf_op jit(solution)/shard_map/ppermute | solution.py:664
  35.4 7.0 %collective-permute-start.5 = (f32[5,32,128]{2,1,0:T(8,128)S(1)}, f32[5,32,128]{2,1,0:T(8,128)S(1)}, u32[]{:S(2)}, u32[]{:S(2)}) collective-permute-start(f32[5,32,128]{2,1,0:T(8,128)S(1)} %get-tuple-element.42), channel_id=1, source_target_pairs={{4,0},{8,4},{12,8},{5,1},{9,5},{13,9},{6,2},{10,6},{14,10},{7,3},{... | collective-permute-start | bytes 245768 | tf_op jit(solution)/shard_map/ppermute | solution.py:664
  36.7 7.2 %collective-permute-start.4 = (f32[5,32,128]{2,1,0:T(8,128)S(1)}, f32[5,32,128]{2,1,0:T(8,128)S(1)}, u32[]{:S(2)}, u32[]{:S(2)}) collective-permute-start(f32[5,32,128]{2,1,0:T(8,128)S(1)} %get-tuple-element.43), channel_id=1, source_target_pairs={{0,4},{4,8},{8,12},{1,5},{5,9},{9,13},{2,6},{6,10},{10,14},{3,7},{... | collective-permute-start | bytes 245768 | tf_op jit(solution)/shard_map/ppermute | solution.py:664
  44.2 36.8 %collective-permute-start.6 = (f32[376,128]{1,0:T(8,128)S(1)}, f32[376,128]{1,0:T(8,128)S(1)}, u32[]{:S(2)}, u32[]{:S(2)}) collective-permute-start(f32[376,128]{1,0:T(8,128)S(1)} %get-tuple-element.25), channel_id=1, source_target_pairs={{0,1},{1,2},{2,3},{4,5},{5,6},{6,7},{8,9},{9,10},{10,11},{12,13},{... | collective-permute-start | bytes 577544 | tf_op jit(solution)/shard_map/ppermute | solution.py:664
  47.6 33.4 %collective-permute-start.7 = (f32[376,128]{1,0:T(8,128)S(1)}, f32[376,128]{1,0:T(8,128)S(1)}, u32[]{:S(2)}, u32[]{:S(2)}) collective-permute-start(f32[376,128]{1,0:T(8,128)S(1)} %get-tuple-element.26), channel_id=1, source_target_pairs={{1,0},{2,1},{3,2},{5,4},{6,5},{7,6},{9,8},{10,9},{11,10},{13,12},{... | collective-permute-start | bytes 577544 | tf_op jit(solution)/shard_map/ppermute | solution.py:664
  81.0 38.1 %copy-start.5 = (f32[64,32,128]{2,1,0:T(8,128)S(1)}, f32[64,32,128]{2,1,0:T(8,128)}, u32[]{:S(2)}) copy-start(f32[64,32,128]{2,1,0:T(8,128)} %load.5) | copy-start | bytes 3145732
  91.2 27.8 %collective-permute-start.12 = (f32[32,128]{1,0:T(8,128)S(1)}, f32[32,128]{1,0:T(8,128)S(1)}, u32[]{:S(2)}, u32[]{:S(2)}) collective-permute-start(f32[32,128]{1,0:T(8,128)S(1)} %get-tuple-element.37), channel_id=1, source_target_pairs={{0,4},{4,8},{8,12},{1,5},{5,9},{9,13},{2,6},{6,10},{10,14},{3,7},{... | collective-permute-start | bytes 49160 | tf_op jit(solution)/shard_map/ppermute | solution.py:664
  92.5 26.5 %collective-permute-start.13 = (f32[32,128]{1,0:T(8,128)S(1)}, f32[32,128]{1,0:T(8,128)S(1)}, u32[]{:S(2)}, u32[]{:S(2)}) collective-permute-start(f32[32,128]{1,0:T(8,128)S(1)} %get-tuple-element.38), channel_id=1, source_target_pairs={{4,0},{8,4},{12,8},{5,1},{9,5},{13,9},{6,2},{10,6},{14,10},{7,3},{... | collective-permute-start | bytes 49160 | tf_op jit(solution)/shard_map/ppermute | solution.py:664
  93.8 25.2 %collective-permute-start.14 = (f32[64,128]{1,0:T(8,128)S(1)}, f32[64,128]{1,0:T(8,128)S(1)}, u32[]{:S(2)}, u32[]{:S(2)}) collective-permute-start(f32[64,128]{1,0:T(8,128)S(1)} %get-tuple-element.39), channel_id=1, source_target_pairs={{0,1},{1,2},{2,3},{4,5},{5,6},{6,7},{8,9},{9,10},{10,11},{12,13},{... | collective-permute-start | bytes 98312 | tf_op jit(solution)/shard_map/ppermute | solution.py:664
  96.0 23.0 %collective-permute-start.15 = (f32[64,128]{1,0:T(8,128)S(1)}, f32[64,128]{1,0:T(8,128)S(1)}, u32[]{:S(2)}, u32[]{:S(2)}) collective-permute-start(f32[64,128]{1,0:T(8,128)S(1)} %get-tuple-element.40), channel_id=1, source_target_pairs={{1,0},{2,1},{3,2},{5,4},{6,5},{7,6},{9,8},{10,9},{11,10},{13,12},{... | collective-permute-start | bytes 98312 | tf_op jit(solution)/shard_map/ppermute | solution.py:664
  (1 other events, 1.2 us)

commit v5 on v4

--- a/solution.py
+++ b/solution.py
@@ -22,7 +22,7 @@
 
 MEANS = range(4)
 BOX_DIAGONAL, LONG_HIGH, LONG_LOW, ACROSS_HIGH, ACROSS_LOW, LOAD_SUM = range(4, 10)
-IMAGE_SUM, FLOW_LONG_HIGH, FLOW_LONG_LOW, FLOW_ACROSS_HIGH, FLOW_ACROSS_LOW = range(5)
+IMAGE_SUM, FLOW_LONG_HIGH, FLOW_LONG_LOW, FLOW_ACROSS_HIGH, FLOW_ACROSS_LOW = range(16, 21)
 
 VMEM = pl.BlockSpec(memory_space=pltpu.VMEM)
 SMEM = pl.BlockSpec(memory_space=pltpu.SMEM)
@@ -248,26 +248,51 @@
     return -(-(count * (box.long + 2 * REACH)) // 8) * 8
 
 
-def pack_fields(box, wide, *refs):
-    *fields, low, high, up, down = refs
+def pack_fields(box, wide, count, fields, *refs):
+    own, (low, high), tables = refs[:fields], refs[fields : fields + 2], refs[fields + 2 : -3]
+    up, down, table = refs[-3:]
     size = wide * box.across
-    flat = [field.reshape(box.long * box.across, box.deep) for field in fields]
+    flat = [field.reshape(box.long * box.across, box.deep) for field in own]
+    low = low.reshape(low.size // box.deep, box.deep)
+    high = high.reshape(high.size // box.deep, box.deep)
     sides = [
-        [
-            ref.reshape(len(fields) * size, box.deep).at[index * size : (index + 1) * size]
-            for index in range(len(fields))
-        ]
+        [ref.at[index * size : (index + 1) * size] for index in range(fields)]
         for ref in (low, high)
     ]
     pack_columns(box, flat, sides[0], sides[1], wide, up, down)
-
-
-def pack_edges(box, zone, scale, up, down):
+    known = merged(*(ref[ref.shape[0] - count :, :] for ref in tables))
+    table[...] = known
+    up[up.shape[0] - count :, :] = known
+    down[down.shape[0] - count :, :] = known
+
+
+def bring_in(
+    box, zone, scale, load, own_zone, own_scale, own_load, load_up, load_down, up, down, staged, sems
+):
     last = box.long
-    up[:REACH] = scale[last - REACH :]
-    down[:REACH] = scale[:REACH]
-    up[REACH:] = zone[last - REACH :].astype(jnp.float32)
-    down[REACH:] = zone[:REACH].astype(jnp.float32)
+    copies = [
+        (load.at[last - MARGIN :], load_up),
+        (load.at[:MARGIN], load_down),
+        (zone.at[last - REACH :], staged.at[0]),
+        (zone.at[:REACH], staged.at[1]),
+        (scale.at[last - REACH :], up.at[:REACH]),
+        (scale.at[:REACH], down.at[:REACH]),
+        (load, own_load),
+        (scale, own_scale),
+        (zone, own_zone),
+    ]
+    copies = [
+        pltpu.make_async_copy(source, target, sems.at[index])
+        for index, (source, target) in enumerate(copies)
+    ]
+    for copy in copies:
+        copy.start()
+    for copy in copies[:4]:
+        copy.wait()
+    up[REACH:] = staged[0].astype(jnp.float32)
+    down[REACH:] = staged[1].astype(jnp.float32)
+    for copy in copies[4:]:
+        copy.wait()
 
 
 def fill_window(box, window, own, low, high, left, right, wide, place, total, add=None):
@@ -318,6 +343,26 @@
     return jnp.where(labels == 0, values[0], jnp.where(labels == 1, values[1], values[2]))
 
 
+def at_own_row(line, shape):
+    long_pos, across_pos, _, across_count = position()
+    rows = lax.broadcasted_iota(jnp.int32, shape, 0)
+    own = rows == long_pos * across_count + across_pos
+    return jnp.where(own, line[:1], jnp.zeros(shape, jnp.float32))
+
+
+def merged(table, *others):
+    for other in others:
+        table = jnp.where(table != 0.0, table, other)
+    return table
+
+
+def merge(table, low, high, out):
+    count = table.shape[0]
+    out[...] = merged(
+        table[...], low[low.shape[0] - count :, :], high[high.shape[0] - count :, :]
+    )
+
+
 def line_of(numbers, shape):
     lanes = lax.broadcasted_iota(jnp.int32, shape, 1)
     line = jnp.zeros(shape, jnp.float32)
@@ -326,7 +371,7 @@
     return line
 
 
-def box_sums(box, zone, scale, load, diffusivity, decay, out):
+def box_sums(box, zone, scale, load, diffusivity, decay, out, table):
     step = 4
     nothing = jnp.zeros((box.across, box.deep), jnp.float32)
     half = [[0.5 * diffusivity[z, d] for z in range(3)] for d in range(3)]
@@ -360,7 +405,9 @@
         (ACROSS_LOW, total(sums[1][:1])),
         (LOAD_SUM, total(sums[4])),
     ]
-    out[...] = line_of(numbers, out.shape)
+    line = line_of(numbers, out.shape)
+    out[...] = line
+    table[...] = at_own_row(line, table.shape)
 
 
 def means_of(ref):
@@ -370,7 +417,15 @@
 def first_solve(box, load, low, high, left, right, means, *rest):
     tables = rest[:N_TABLES]
     window, local, spectral, middle = rest[N_TABLES:]
-    fill_window(box, window, load, low[...], high[...], left, right, MARGIN, 0, MARGIN)
+    _, across_pos, _, across_count = position()
+    has_left, has_right = as_float(across_pos > 0), as_float(across_pos < across_count - 1)
+
+    def inside(values, row_side, col_side):
+        if col_side == 0:
+            return values
+        return values * (has_left if col_side < 0 else has_right)
+
+    fill_window(box, window, load, low[...], high[...], left, right, MARGIN, 0, MARGIN, inside)
 
     def emit(start, values):
         values = values * (1.0 / cheb_center)
@@ -393,7 +448,6 @@
     box,
     zone,
     scale,
-    local,
     low,
     high,
     left,
@@ -404,7 +458,6 @@
     to_across,
     to_deep,
     mass,
-    told,
     zone_window,
     scale_window,
 ):
@@ -433,38 +486,76 @@
         last_long = one_row(row, last_long)
     to_long[box.rows - 1] = last_long
 
-    first, last = REACH, REACH + box.long
-    inner = slice(EDGE, EDGE + box.across)
+
+def image_sums(
+    box, zone, scale, local, low, high, left, right, table, diffusivity, decay, out, up, down
+):
+    half = [[0.5 * diffusivity[z, d] for z in range(3)] for d in range(3)]
+    rates = [decay[z] for z in range(3)]
+    lane = lax.broadcasted_iota(jnp.int32, (box.across, box.deep), 1)
+    ends = jnp.where((lane == 0) | (lane == box.deep - 1), jnp.float32(1.0), jnp.float32(0.0))
     step = 8
 
     def add_rows(index, total):
         for row in range(step):
             row = index * step + row
-            total = total + mass[first + row, inner] * local[row]
+            labels = zone[row]
+            mass = looked_up(labels, rates) + looked_up(labels, half[2]) * scale[row] * ends
+            total = total + mass * local[row]
         return total
 
     nothing = jnp.zeros((box.across, box.deep), jnp.float32)
-    image_sum = lax.fori_loop(0, box.long // step, add_rows, nothing)
+    image = lax.fori_loop(0, box.long // step, add_rows, nothing)
+    shape = (box.long * box.across, box.deep)
+    zone_flat, scale_flat, local_flat = zone.reshape(shape), scale.reshape(shape), local.reshape(shape)
+    last_col = row_of(box.across, box.across - 1, box.long)
+    first_col = row_of(box.across, 0, box.long)
+
+    def side(ref, place):
+        return ref[place * box.long : (place + 1) * box.long, :]
+
+    faces = [
+        (0, zone[box.long - 1], scale[box.long - 1], local[box.long - 1], high[REACH], high[0]),
+        (0, zone[0], scale[0], local[0], low[2 * REACH - 1], low[REACH - 1]),
+        (
+            1,
+            zone_flat[last_col, :],
+            scale_flat[last_col, :],
+            local_flat[last_col, :],
+            side(right, REACH),
+            side(right, 0),
+        ),
+        (
+            1,
+            zone_flat[first_col, :],
+            scale_flat[first_col, :],
+            local_flat[first_col, :],
+            side(left, 2 * REACH - 1),
+            side(left, REACH - 1),
+        ),
+    ]
+    flows = []
+    for direction, labels, factor, values, far_labels, far_factor in faces:
+        weight = looked_up(labels, half[direction]) * factor
+        weight = weight + looked_up(far_labels, half[direction]) * far_factor
+        flows.append(jnp.sum(weight * values, keepdims=True))
     long_pos, across_pos, long_count, across_count = position()
-    across_flat = to_across.reshape(box.flat, box.deep)
-    local_flat = local.reshape(box.long * box.across, box.deep)
-    flows = [
-        to_long[last - 1, inner] * local[box.long - 1],
-        to_long[first - 1, inner] * local[0],
-        across_flat[row_of(box.cols, EDGE + box.across - 1, box.long, first), :]
-        * local_flat[row_of(box.across, box.across - 1, box.long), :],
-        across_flat[row_of(box.cols, EDGE - 1, box.long, first), :]
-        * local_flat[row_of(box.across, 0, box.long), :],
-    ]
-    flows = [jnp.sum(flow, keepdims=True) for flow in flows]
     numbers = [
-        (IMAGE_SUM, jnp.sum(image_sum, keepdims=True) + sum(flows)),
+        (IMAGE_SUM, jnp.sum(image, keepdims=True) + sum(flows)),
         (FLOW_LONG_HIGH, flows[0] * as_float(long_pos < long_count - 1)),
         (FLOW_LONG_LOW, flows[1] * as_float(long_pos > 0)),
         (FLOW_ACROSS_HIGH, flows[2] * as_float(across_pos < across_count - 1)),
         (FLOW_ACROSS_LOW, flows[3] * as_float(across_pos > 0)),
     ]
-    told[...] = line_of(numbers, told.shape)
+    count = out.shape[0]
+    known = merged(table[...], left[left.shape[0] - count :, :], right[right.shape[0] - count :, :])
+    known = known + at_own_row(line_of(numbers, (8, known.shape[1])), known.shape)
+    out[...] = known
+    edge = REACH * box.across
+    up[:edge] = local_flat[shape[0] - edge :, :]
+    up[edge:] = known
+    down[:edge] = local_flat[:edge, :]
+    down[edge:] = known
 
 
 def column(values, index):
@@ -541,8 +632,7 @@
 def second_solve(box, local, low, high, left, right, inverse, told, means, *rest):
     to_long, to_across, to_deep, mass, load_window = rest[:5]
     tables = rest[5 : 5 + N_TABLES]
-    iterate, top, bottom, last_col, first_col = rest[5 + N_TABLES : 10 + N_TABLES]
-    window, residual, spectral, middle = rest[10 + N_TABLES :]
+    iterate, window, residual, spectral, middle = rest[5 + N_TABLES :]
     long_pos, across_pos, long_count, across_count = position()
     coarse = answer(inverse, column(told, LOAD_SUM)) * (1.0 / cheb_center)
     shifts = {
@@ -557,7 +647,9 @@
             shift = shift.reshape(1, 1, 1)
         return values + shift
 
-    fill_window(box, window, local, low[...], high[...], left, right, REACH, 0, REACH, add)
+    edge = REACH * box.across
+    low, high = (ref[:edge, :].reshape(REACH, box.across, box.deep) for ref in (low, high))
+    fill_window(box, window, local, low, high, left, right, REACH, 0, REACH, add)
     weights = (to_long, to_across, to_deep, mass)
 
     def one_row(row, flow):
@@ -587,11 +679,27 @@
     box_solve(
         box, residual, means_of(means), tables, row_mask, col_mask, spectral, middle, emit
     )
-    top[...] = iterate[box.long - 1]
-    bottom[...] = iterate[0]
-    flat = iterate.reshape(box.long * box.across, box.deep)
-    last_col[...] = flat[row_of(box.across, box.across - 1, box.long), :]
-    first_col[...] = flat[row_of(box.across, 0, box.long), :]
+
+
+def correct_faces(
+    box, partial, inverse, table, more, shift, top, bottom, last_col, first_col
+):
+    count = table.shape[0]
+    across_count = lax.axis_size("narrow")
+    numbers = merged(table[...], more[...])
+    sums = column(numbers, IMAGE_SUM)
+    sums = sums - column(pltpu.roll(numbers, count - across_count, 0), FLOW_LONG_LOW)
+    sums = sums - column(pltpu.roll(numbers, across_count, 0), FLOW_LONG_HIGH)
+    sums = sums - column(pltpu.roll(numbers, count - 1, 0), FLOW_ACROSS_LOW)
+    sums = sums - column(pltpu.roll(numbers, 1, 0), FLOW_ACROSS_HIGH)
+    sums = column(numbers, LOAD_SUM) * (1.0 - 1.0 / cheb_center) - sums
+    own = at_box(answer(inverse, sums) * gain, 0, 0)
+    shift[...] = jnp.broadcast_to(own, shift.shape)
+    top[...] = partial[box.long - 1] + own
+    bottom[...] = partial[0] + own
+    flat = partial.reshape(box.long * box.across, box.deep)
+    last_col[...] = flat[row_of(box.across, box.across - 1, box.long), :] + own
+    first_col[...] = flat[row_of(box.across, 0, box.long), :] + own
 
 
 def last_residual(
@@ -602,9 +710,7 @@
     high,
     left,
     right,
-    inverse,
-    load_told,
-    image_told,
+    shift,
     to_long,
     to_across,
     to_deep,
@@ -615,28 +721,18 @@
     result,
     sems,
 ):
-    count = load_told.shape[0]
-    across_count = lax.axis_size("narrow")
-    numbers = image_told[...]
-    sums = column(numbers, IMAGE_SUM)
-    sums = sums - column(pltpu.roll(numbers, count - across_count, 0), FLOW_LONG_LOW)
-    sums = sums - column(pltpu.roll(numbers, across_count, 0), FLOW_LONG_HIGH)
-    sums = sums - column(pltpu.roll(numbers, count - 1, 0), FLOW_ACROSS_LOW)
-    sums = sums - column(pltpu.roll(numbers, 1, 0), FLOW_ACROSS_HIGH)
-    sums = column(load_told, LOAD_SUM) * (1.0 - 1.0 / cheb_center) - sums
-    coarse = answer(inverse, sums) * gain
     inner = slice(EDGE, EDGE + box.across)
     flat = window.reshape((box.long + 2) * box.cols, box.deep)
     blank = jnp.zeros((box.long + 2, EDGE, box.deep), jnp.float32)
     window[:, :EDGE, :] = blank
     window[:, EDGE + box.across :, :] = blank
-    window[1 : 1 + box.long, inner, :] = partial[...] + at_box(coarse, 0, 0).reshape(1, 1, 1)
+    window[1 : 1 + box.long, inner, :] = partial[...] + shift[0:1, :].reshape(1, 1, box.deep)
     own = pltpu.make_async_copy(window.at[1 : 1 + box.long, inner, :], iterate, sems.at[0])
     own.start()
-    window[0, inner, :] = low[...] + at_box(coarse, -1, 0)
-    window[1 + box.long, inner, :] = high[...] + at_box(coarse, 1, 0)
-    flat[row_of(box.cols, EDGE - 1, box.long, 1), :] = left[...] + at_box(coarse, 0, -1)
-    flat[row_of(box.cols, EDGE + box.across, box.long, 1), :] = right[...] + at_box(coarse, 0, 1)
+    window[0, inner, :] = low[...]
+    window[1 + box.long, inner, :] = high[...]
+    flat[row_of(box.cols, EDGE - 1, box.long, 1), :] = left[...]
+    flat[row_of(box.cols, EDGE + box.across, box.long, 1), :] = right[...]
     weights = (to_long, to_across, to_deep, mass)
 
     def one_row(row, flow):
@@ -657,20 +753,36 @@
         copy.wait()
 
 
-def exchange(axis, last, first):
+def exchange(axis, last, first, around=False):
     size = lax.axis_size(axis)
-    up = [(i, i + 1) for i in range(size - 1)]
+    up = [(i, (i + 1) % size) for i in range(size if around else size - 1)]
     down = [(j, i) for i, j in up]
     return lax.ppermute(last, axis, up), lax.ppermute(first, axis, down)
+
+
+def two_away(axis, table):
+    size = lax.axis_size(axis)
+    return lax.ppermute(table, axis, [(i, (i + 2) % size) for i in range(size)])
+
+
+def tell(table):
+    count = table.shape[0]
+    long_pos, across_pos, _, across_count = position()
+    own = lax.dynamic_slice_in_dim(table, long_pos * across_count + across_pos, 1, axis=0)
+    line = jnp.broadcast_to(own, (count, 1, 128))
+    told = lax.all_to_all(line, ("wide", "narrow"), split_axis=0, concat_axis=0, tiled=True)
+    return told.reshape(count, 128)
 
 
 def on_device(zone, scale, diffusivity, decay, load):
     box = Box(load.shape)
     long, across, deep = load.shape
     count = lax.axis_size("wide") * lax.axis_size("narrow")
+    by_margins = lax.axis_size("wide") == 4 and lax.axis_size("narrow") == 4
     tables = tables_of(box)
     cells = f32(long, across, deep)
     window = f32(box.rows, box.cols, deep)
+    table_shape = f32(count, 128)
 
     def scratch(shape):
         return pltpu.VMEM(shape, jnp.float32)
@@ -678,48 +790,75 @@
     spectral = scratch((box.ey, padded(box.ex), deep))
     middle = scratch((long, padded(box.ey), deep))
 
-    def pack(wide, *fields):
-        message = f32(message_rows(box, wide * (len(fields) - 2)), deep)
-        body = functools.partial(pack_fields, box, wide)
-        return call(body, (message, message), [VMEM] * len(fields))(*fields)
-
-    load_low, load_high = exchange("wide", load[long - MARGIN :], load[:MARGIN])
-    own_told = call(functools.partial(box_sums, box), f32(8, 128), [VMEM] * 3 + [SMEM] * 2)(
-        zone, scale, load, diffusivity, decay
-    )
-    load_told = lax.all_gather(own_told[:1], ("wide", "narrow"), axis=0, tiled=True)
+    def pack(wide, fields, *refs):
+        message = f32(message_rows(box, wide * fields) + count, deep)
+        body = functools.partial(pack_fields, box, wide, count, fields)
+        return call(body, (message, message, table_shape), [VMEM] * len(refs))(*refs)
+
     far = f32(2 * REACH, across, deep)
-    up, down = call(functools.partial(pack_edges, box), (far, far), [VMEM] * 2)(zone, scale)
-    low, high = exchange("wide", up, down)
-    load_left, load_right = exchange("narrow", *pack(MARGIN, load, load_low, load_high))
-    left, right = exchange("narrow", *pack(REACH, scale, zone, low, high))
+    zone, scale, load, load_up, load_down, up, down = call(
+        functools.partial(bring_in, box),
+        (jax.ShapeDtypeStruct(cells.shape, zone.dtype), cells, cells)
+        + (f32(MARGIN, across, deep),) * 2
+        + (far, far),
+        [pl.BlockSpec(memory_space=pltpu.HBM)] * 3,
+        [pltpu.VMEM((2, REACH, across, deep), zone.dtype), pltpu.SemaphoreType.DMA((9,))],
+    )(*(pltpu.with_memory_space_constraint(field, pltpu.HBM) for field in (zone, scale, load)))
+    load_low, load_high = exchange("wide", load_up, load_down)
+    far_low, far_high = exchange("wide", up, down)
+    sums, table = call(
+        functools.partial(box_sums, box), (f32(8, 128), table_shape), [VMEM] * 3 + [SMEM] * 2
+    )(zone, scale, load, diffusivity, decay)
+    own_table = table
+    up, down, _ = pack(MARGIN, 1, load, load_low, load_high, table)
+    load_left, load_right = exchange("narrow", up, down, by_margins)
+    up, down, table = pack(REACH, 2, scale, zone, far_low, far_high, table, load_left, load_right)
+    far_left, far_right = exchange("narrow", up, down)
     load_window, local = call(
         functools.partial(first_solve, box),
         (window, cells),
         [VMEM] * (6 + N_TABLES),
         [spectral, middle],
         flops=4 * 10**9,
-    )(load, load_low, load_high, load_left, load_right, own_told, *tables)
-    to_long, to_across, to_deep, mass, image_told = call(
+    )(load, load_low, load_high, load_left, load_right, sums, *tables)
+    message = f32(REACH * across + count, deep)
+    table, up, down = call(
+        functools.partial(image_sums, box), (table_shape, message, message), [VMEM] * 8 + [SMEM] * 2
+    )(zone, scale, local, far_low, far_high, far_left, far_right, table, diffusivity, decay)
+    image_table = table
+    low, high = exchange("wide", up, down)
+    to_long, to_across, to_deep, mass = call(
         functools.partial(weights_of, box),
-        (window,) * 4 + (f32(8, 128),),
-        [VMEM] * 7 + [SMEM] * 2,
+        (window,) * 4,
+        [VMEM] * 6 + [SMEM] * 2,
         [scratch(window.shape)] * 2,
         flops=10**9,
-    )(zone, scale, local, low, high, left, right, diffusivity, decay)
-    low, high = exchange("wide", local[long - REACH :], local[:REACH])
-    image_told = lax.all_gather(image_told[:1], ("wide", "narrow"), axis=0, tiled=True)
-    left, right = exchange("narrow", *pack(REACH, local, low, high))
+    )(zone, scale, far_low, far_high, far_left, far_right, diffusivity, decay)
+    joined = functools.partial(call, merge, table_shape, [VMEM] * 3)
+    if by_margins:
+        table = joined()(table, low, high)
+        more = two_away("wide", table)
+        up, down, table = pack(REACH, 1, local, low, high, table, more)
+        load_table = table
+    else:
+        up, down, _ = pack(REACH, 1, local, low, high, table)
+        load_table = tell(own_table)
+    left, right = exchange("narrow", up, down)
     inverse = call(
         coarse_inverse,
         f32(count, -(-count // 128) * 128),
         [VMEM],
         [scratch((count, -(-2 * count // 128) * 128))],
-    )(load_told)
+    )(load_table)
+    if by_margins:
+        table = joined()(table, left, right)
+        more = two_away("narrow", table)
+    else:
+        table = more = tell(image_table)
     row, col = f32(across, deep), f32(long, deep)
-    partial, top, bottom, last_col, first_col = call(
+    partial = call(
         functools.partial(second_solve, box),
-        (cells, row, row, col, col),
+        cells,
         [VMEM] * (13 + N_TABLES),
         [scratch(window.shape), scratch((box.ex, box.cols, deep)), spectral, middle],
         flops=4 * 10**9,
@@ -730,8 +869,8 @@
         left,
         right,
         inverse,
-        load_told,
-        own_told,
+        load_table,
+        sums,
         to_long,
         to_across,
         to_deep,
@@ -739,12 +878,15 @@
         load_window,
         *tables,
     )
+    shift, top, bottom, last_col, first_col = call(
+        functools.partial(correct_faces, box), (f32(8, deep), row, row, col, col), [VMEM] * 4
+    )(partial, inverse, table, more)
+    left, right = exchange("narrow", last_col, first_col)
     low, high = exchange("wide", top, bottom)
-    left, right = exchange("narrow", last_col, first_col)
     return call(
         functools.partial(last_residual, box),
         (cells, cells),
-        [VMEM] * 13,
+        [VMEM] * 11,
         [scratch((long + 2, box.cols, deep)), scratch(cells.shape), pltpu.SemaphoreType.DMA((5,))],
         out_spec=pl.BlockSpec(memory_space=pl.ANY),
     )(
@@ -754,9 +896,7 @@
         high,
         left,
         right,
-        inverse,
-        load_told,
-        image_told,
+        shift,
         to_long,
         to_across,
         to_deep,

time: 124 us -> 92.2 us (0.74)
  blocking collectives: 48 us -> 0 us
  waiting for transfers between devices: 2.28 us -> 15.7 us
  local copies, waits for them, and re-layouts: 4.66 us -> 0.07 us
  starting transfers between devices: 37.9 us -> 42.2 us
  Pallas kernels: 28.8 us -> 32.7 us
    all_gather x2 -> x0, blocking collectives: 48 us -> none  [the longest x1 26.3 us: on_device(): lax.all_gather(own_told[:1], ('wide', 'narrow'), axis=0, tiled=True)]
    ppermute x16, waiting for transfers between devices: 2.28 us -> 13.7 us  [exchange(): return (lax.ppermute(last, axis, up), lax.ppermute(first, axis, down))]
    ppermute x0 -> x2, starting transfers between devices: none -> 8.26 us  [two_away(): return lax.ppermute(table, axis, [(i, (i + 2) % size) for i in range(size)])]
    ppermute x16, starting transfers between devices: 37.9 us -> 33.9 us  [exchange(): return (lax.ppermute(last, axis, up), lax.ppermute(first, axis, down))]
    pallas_call x8 -> x12, Pallas kernels: 20.4 us -> 24.2 us  [the longest x1 10.2 us: on_device(): call(functools.partial(second_solve, box), cells, [VMEM] * (13 + N_TABLES...]
    unnamed x36 -> x22, local copies, waits for them, and re-layouts: 3.75 us -> 0.07 us
    ppermute x0 -> x2, waiting for transfers between devices: none -> 1.98 us  [two_away(): return lax.ppermute(table, axis, [(i, (i + 2) % size) for i in range(size)])]
  transfers between devices with their start and end apart: 16 -> 18, of which waited for: 3 -> 8; matrix products, arithmetic and copies ran while one was open for 0% -> 0% of each run, Pallas kernels for 12% -> 27%
where the time goes in v5:
time: 92.2 us; the launch traced here: 91.7 us
  starting transfers between devices  42.2 us (46%)
  Pallas kernels  32.7 us (35%)
  waiting for transfers between devices  15.7 us (17%)
  between operations  1.18 us (1%)
    ppermute x16, starting transfers between devices, exchange(): return (lax.ppermute(last, axis, up), lax.ppermute(first, axis, down))  33.9 us
    ppermute x16, waiting for transfers between devices, exchange(): return (lax.ppermute(last, axis, up), lax.ppermute(first, axis, down))  13.7 us
    pallas_call x1, Pallas kernels, on_device(): call(functools.partial(second_solve, box), cells, [VMEM] * (13 + N_TABLES...  10.2 us
    ppermute x2, starting transfers between devices, two_away(): return lax.ppermute(table, axis, [(i, (i + 2) % size) for i in range(size)])  8.26 us
    pallas_call x1, Pallas kernels, on_device(): call(functools.partial(first_solve, box), (window, cells), [VMEM] * (6 +...  6.72 us
    pallas_call x1, Pallas kernels, on_device(): call(functools.partial(weights_of, box), (window,) * 4, [VMEM] * 6 + [SME...  3.72 us
    pallas_call x1, Pallas kernels, on_device(): call(functools.partial(last_residual, box), (cells, cells), [VMEM] * 11,...  3.43 us
    pallas_call x1, Pallas kernels, on_device(): call(functools.partial(bring_in, box), (jax.ShapeDtypeStruct(cells.shape,...  2.18 us
  transfers between devices with their start and end apart: 18, of which 8 were waited for; matrix products, arithmetic and copies ran while one was open for 0% of the time, Pallas kernels for 27%

profile of v5, /device:TPU:0, one launch (start us, length us, event | category | flops | bytes accessed | tf_op | source)
XLA Modules:
  0.0 91.7 jit_solution(6198190690396175712)
XLA Ops:
  0.7 2.2 %shard_map.149 = (s32[64,32,128]{2,1,0:T(8,128)S(1)}, f32[64,32,128]{2,1,0:T(8,128)S(1)}, f32[64,32,128]{2,1,0:T(8,128)S(1)}, f32[4,32,128]{2,1,0:T(8,128)S(1)},...) custom-call(s32[64,32,128]{2,1,0:T(8,128)} %zone.1, f32[64,32,128]{2,1,0:T(8,128)} %scale.1, ...), custom_call_target="tpu_custom_call" | custom-call | tf_op jit(solution)/shard_map/pallas_call | solution.py:799
  2.8 4.9 %collective-permute-start = (f32[4,32,128]{2,1,0:T(8,128)S(1)}, f32[4,32,128]{2,1,0:T(8,128)S(1)}, u32[]{:S(2)}, u32[]{:S(2)}) collective-permute-start(f32[4,32,128]{2,1,0:T(8,128)S(1)} %get-tuple-element.34), channel_id=1, source_target_pairs={{0,4},{4,8},{8,12},{1,5},{5,9},{9,13},{2,6},{6,10},{10,14},{3,7},{... | collective-permute-start | bytes 196616 | tf_op jit(solution)/shard_map/ppermute | solution.py:760
  7.8 1.3 %collective-permute-start.1 = (f32[4,32,128]{2,1,0:T(8,128)S(1)}, f32[4,32,128]{2,1,0:T(8,128)S(1)}, u32[]{:S(2)}, u32[]{:S(2)}) collective-permute-start(f32[4,32,128]{2,1,0:T(8,128)S(1)} %get-tuple-element.35), channel_id=1, source_target_pairs={{4,0},{8,4},{12,8},{5,1},{9,5},{13,9},{6,2},{10,6},{14,10},{7,3},{... | collective-permute-start | bytes 196616 | tf_op jit(solution)/shard_map/ppermute | solution.py:760
  9.1 4.6 %collective-permute-start.4 = (f32[10,32,128]{2,1,0:T(8,128)S(1)}, f32[10,32,128]{2,1,0:T(8,128)S(1)}, u32[]{:S(2)}, u32[]{:S(2)}) collective-permute-start(f32[10,32,128]{2,1,0:T(8,128)S(1)} %get-tuple-element.43), channel_id=1, source_target_pairs={{0,4},{4,8},{8,12},{1,5},{5,9},{9,13},{2,6},{6,10},{10,14},{3,7},{... | collective-permute-start | bytes 491528 | tf_op jit(solution)/shard_map/ppermute | solution.py:760
  13.6 1.3 %collective-permute-start.5 = (f32[10,32,128]{2,1,0:T(8,128)S(1)}, f32[10,32,128]{2,1,0:T(8,128)S(1)}, u32[]{:S(2)}, u32[]{:S(2)}) collective-permute-start(f32[10,32,128]{2,1,0:T(8,128)S(1)} %get-tuple-element.44), channel_id=1, source_target_pairs={{4,0},{8,4},{12,8},{5,1},{9,5},{13,9},{6,2},{10,6},{14,10},{7,3},{... | collective-permute-start | bytes 491528 | tf_op jit(solution)/shard_map/ppermute | solution.py:760
  15.0 1.5 %shard_map.150 = (f32[8,128]{1,0:T(8,128)S(1)}, f32[16,128]{1,0:T(8,128)S(1)}) custom-call(s32[64,32,128]{2,1,0:T(8,128)S(1)} %get-tuple-element.36.zone.refs_1_, f32[64,32,128]{2,1,0:T(8,128)S(1)} %get-tuple-element.37.scale.refs_0_, f32[64,32,128]{2,1,0:T(8,128)S(1)} %get-tuple-element.33.load.refs_0_, f32[3,3]{1,0:T(4,128)S(1)} %copy-done, f32[3]{0:T(128)S(1)} %copy-done.1), custom_call_target="tpu_custom_call" | custom-call | tf_op jit(solution)/shard_map/pallas_call | solution.py:809
  16.6 0.8 shard_map.151
  17.4 1.7 %collective-permute-start.3 = (f32[312,128]{1,0:T(8,128)S(1)}, f32[312,128]{1,0:T(8,128)S(1)}, u32[]{:S(2)}, u32[]{:S(2)}) collective-permute-start(f32[312,128]{1,0:T(8,128)S(1)} %get-tuple-element.40), channel_id=1, source_target_pairs={{1,0},{2,1},{3,2},{0,3},{5,4},{6,5},{7,6},{4,7},{9,8},{10,9},{11,1... | collective-permute-start | bytes 479240 | tf_op jit(solution)/shard_map/ppermute | solution.py:760
  19.2 1.7 %collective-permute-done.5.refs_3_.high = f32[10,32,128]{2,1,0:T(8,128)S(1)} collective-permute-done((f32[10,32,128]{2,1,0:T(8,128)S(1)}, f32[10,32,128]{2,1,0:T(8,128)S(1)}, u32[]{:S(2)}, u32[]{:S(2)}) %collective-permute-start.5) | collective-permute-done | bytes 163872 | tf_op jit(solution)/shard_map/ppermute | solution.py:760
  20.9 1.2 %collective-permute-done.2.left.refs_5_ = f32[312,128]{1,0:T(8,128)S(1)} collective-permute-done((f32[312,128]{1,0:T(8,128)S(1)}, f32[312,128]{1,0:T(8,128)S(1)}, u32[]{:S(2)}, u32[]{:S(2)}) %collective-permute-start.2) | collective-permute-done | bytes 159776 | tf_op jit(solution)/shard_map/ppermute | solution.py:760
  23.3 2.8 %collective-permute-start.6 = (f32[760,128]{1,0:T(8,128)S(1)}, f32[760,128]{1,0:T(8,128)S(1)}, u32[]{:S(2)}, u32[]{:S(2)}) collective-permute-start(f32[760,128]{1,0:T(8,128)S(1)} %get-tuple-element.45), channel_id=1, source_target_pairs={{0,1},{1,2},{2,3},{4,5},{5,6},{6,7},{8,9},{9,10},{10,11},{12,13},{... | collective-permute-start | bytes 1167368 | tf_op jit(solution)/shard_map/ppermute | solution.py:760
  26.1 1.3 %collective-permute-start.7 = (f32[760,128]{1,0:T(8,128)S(1)}, f32[760,128]{1,0:T(8,128)S(1)}, u32[]{:S(2)}, u32[]{:S(2)}) collective-permute-start(f32[760,128]{1,0:T(8,128)S(1)} %get-tuple-element.46), channel_id=1, source_target_pairs={{1,0},{2,1},{3,2},{5,4},{6,5},{7,6},{9,8},{10,9},{11,10},{13,12},{... | collective-permute-start | bytes 1167368 | tf_op jit(solution)/shard_map/ppermute | solution.py:760
  27.5 6.7 %shard_map.152 = (f32[74,48,128]{2,1,0:T(8,128)S(1)}, f32[64,32,128]{2,1,0:T(8,128)S(1)}) custom-call(f32[64,32,128]{2,1,0:T(8,128)S(1)} %get-tuple-element.33.load.refs_0_, f32[4,32,128]{2,1,0:T(8,128)S(1)} %collective-permute-done.refs_1_.low, f32[4,32,128]{2,1,0:T(8,128)S(1)} %collective-permute-done.1.refs_2_.high, ...), custom_call_target="tpu_custom_call" | custom-call | flops 4000000000 | tf_op jit(solution)/shard_map/pallas_call | solution.py:817
  34.3 1.3 %shard_map.154 = (f32[16,128]{1,0:T(8,128)S(1)}, f32[176,128]{1,0:T(8,128)S(1)}, f32[176,128]{1,0:T(8,128)S(1)}) custom-call(s32[64,32,128]{2,1,0:T(8,128)S(1)} %get-tuple-element.36.zone.refs_1_, f32[64,32,128]{2,1,0:T(8,128)S(1)} %get-tuple-element.37.scale.refs_0_, f32[64,32,128]{2,1,0:T(8,128)S(1)} %get-tuple-element.42.local.refs_0_, ...), custom_call_target="tpu_custom_call" | custom-call | tf_op jit(solution)/shard_map/pallas_call | solution.py:825
  35.6 4.6 %collective-permute-start.8 = (f32[176,128]{1,0:T(8,128)S(1)}, f32[176,128]{1,0:T(8,128)S(1)}, u32[]{:S(2)}, u32[]{:S(2)}) collective-permute-start(f32[176,128]{1,0:T(8,128)S(1)} %get-tuple-element.48), channel_id=1, source_target_pairs={{0,4},{4,8},{8,12},{1,5},{5,9},{9,13},{2,6},{6,10},{10,14},{3,7},{... | collective-permute-start | bytes 270344 | tf_op jit(solution)/shard_map/ppermute | solution.py:760
  40.2 1.3 %collective-permute-start.9 = (f32[176,128]{1,0:T(8,128)S(1)}, f32[176,128]{1,0:T(8,128)S(1)}, u32[]{:S(2)}, u32[]{:S(2)}) collective-permute-start(f32[176,128]{1,0:T(8,128)S(1)} %get-tuple-element.49), channel_id=1, source_target_pairs={{4,0},{8,4},{12,8},{5,1},{9,5},{13,9},{6,2},{10,6},{14,10},{7,3},{... | collective-permute-start | bytes 270344 | tf_op jit(solution)/shard_map/ppermute | solution.py:760
  41.5 0.9 collective-permute-done.8.low.refs_1_
  42.4 4.7 %collective-permute-done.9.high.refs_2_ = f32[176,128]{1,0:T(8,128)S(1)} collective-permute-done((f32[176,128]{1,0:T(8,128)S(1)}, f32[176,128]{1,0:T(8,128)S(1)}, u32[]{:S(2)}, u32[]{:S(2)}) %collective-permute-start.9) | collective-permute-done | bytes 90144 | tf_op jit(solution)/shard_map/ppermute | solution.py:760
  47.1 2.6 %collective-permute-start.10 = (f32[16,128]{1,0:T(8,128)S(1)}, f32[16,128]{1,0:T(8,128)S(1)}, u32[]{:S(2)}, u32[]{:S(2)}) collective-permute-start(f32[16,128]{1,0:T(8,128)S(1)} %shard_map.155.refs_3_), channel_id=1, source_target_pairs={{0,8},{4,12},{8,0},{12,4},{1,9},{5,13},{9,1},{13,5},{2,10},{6,14},... | collective-permute-start | bytes 24584 | tf_op jit(solution)/shard_map/ppermute | solution.py:765
  49.7 2.0 %collective-permute-done.10.refs_4_ = f32[16,128]{1,0:T(8,128)S(1)} collective-permute-done((f32[16,128]{1,0:T(8,128)S(1)}, f32[16,128]{1,0:T(8,128)S(1)}, u32[]{:S(2)}, u32[]{:S(2)}) %collective-permute-start.10) | collective-permute-done | bytes 8224 | tf_op jit(solution)/shard_map/ppermute | solution.py:765
  51.9 1.3 %collective-permute-start.11 = (f32[392,128]{1,0:T(8,128)S(1)}, f32[392,128]{1,0:T(8,128)S(1)}, u32[]{:S(2)}, u32[]{:S(2)}) collective-permute-start(f32[392,128]{1,0:T(8,128)S(1)} %get-tuple-element.51), channel_id=1, source_target_pairs={{0,1},{1,2},{2,3},{4,5},{5,6},{6,7},{8,9},{9,10},{10,11},{12,13},{... | collective-permute-start | bytes 602120 | tf_op jit(solution)/shard_map/ppermute | solution.py:760
  53.2 1.5 %collective-permute-start.12 = (f32[392,128]{1,0:T(8,128)S(1)}, f32[392,128]{1,0:T(8,128)S(1)}, u32[]{:S(2)}, u32[]{:S(2)}) collective-permute-start(f32[392,128]{1,0:T(8,128)S(1)} %get-tuple-element.52), channel_id=1, source_target_pairs={{1,0},{2,1},{3,2},{5,4},{6,5},{7,6},{9,8},{10,9},{11,10},{13,12},{... | collective-permute-start | bytes 602120 | tf_op jit(solution)/shard_map/ppermute | solution.py:760
  54.7 3.7 %shard_map.158 = (f32[74,48,128]{2,1,0:T(8,128)S(1)}, f32[74,48,128]{2,1,0:T(8,128)S(1)}, f32[74,48,128]{2,1,0:T(8,128)S(1)}, f32[74,48,128]{2,1,0:T(8,128)S(1)}) custom-call(s32[64,32,128]{2,1,0:T(8,128)S(1)} %get-tuple-element.36.zone.refs_1_, f32[64,32,128]{2,1,0:T(8,128)S(1)} %get-tuple-element.37.scale.refs_0_, ...), custom_call_target="tpu_custom_call" | custom-call | flops 1000000000 | tf_op jit(solution)/shard_map/pallas_call | solution.py:830
  58.4 1.7 %shard_map.157.inverse = f32[16,128]{1,0:T(8,128)S(1)} custom-call(f32[16,128]{1,0:T(8,128)S(1)} %get-tuple-element.53.told.table), custom_call_target="tpu_custom_call" | custom-call | tf_op jit(solution)/shard_map/pallas_call | solution.py:847
  60.2 5.7 %collective-permute-start.13 = (f32[16,128]{1,0:T(8,128)S(1)}, f32[16,128]{1,0:T(8,128)S(1)}, u32[]{:S(2)}, u32[]{:S(2)}) collective-permute-start(f32[16,128]{1,0:T(8,128)S(1)} %shard_map.160.table), channel_id=1, source_target_pairs={{0,2},{1,3},{2,0},{3,1},{4,6},{5,7},{6,4},{7,5},{8,10},{9,11},{10,... | collective-permute-start | bytes 24584 | tf_op jit(solution)/shard_map/ppermute | solution.py:765
  65.9 10.2 %shard_map.159.partial = f32[64,32,128]{2,1,0:T(8,128)S(1)} custom-call(f32[64,32,128]{2,1,0:T(8,128)S(1)} %get-tuple-element.42.local.refs_0_, f32[176,128]{1,0:T(8,128)S(1)} %collective-permute-done.8.low.refs_1_, f32[176,128]{1,0:T(8,128)S(1)} %collective-permute-done.9.high.refs_2_, f32[392,128]{1,0:T(8,128)S(1)} %collective-permute-done.11.left.low, ...), custom_call_target="tpu_custom_call" | custom-call | flops 4000000000 | tf_op jit(solution)/shard_map/pallas_call | solution.py:859
  76.4 1.3 %collective-permute-start.16 = (f32[64,128]{1,0:T(8,128)S(1)}, f32[64,128]{1,0:T(8,128)S(1)}, u32[]{:S(2)}, u32[]{:S(2)}) collective-permute-start(f32[64,128]{1,0:T(8,128)S(1)} %get-tuple-element.61), channel_id=1, source_target_pairs={{0,1},{1,2},{2,3},{4,5},{5,6},{6,7},{8,9},{9,10},{10,11},{12,13},{... | collective-permute-start | bytes 98312 | tf_op jit(solution)/shard_map/ppermute | solution.py:760
  77.6 1.3 %collective-permute-start.17 = (f32[64,128]{1,0:T(8,128)S(1)}, f32[64,128]{1,0:T(8,128)S(1)}, u32[]{:S(2)}, u32[]{:S(2)}) collective-permute-start(f32[64,128]{1,0:T(8,128)S(1)} %get-tuple-element.62), channel_id=1, source_target_pairs={{1,0},{2,1},{3,2},{5,4},{6,5},{7,6},{9,8},{10,9},{11,10},{13,12},{... | collective-permute-start | bytes 98312 | tf_op jit(solution)/shard_map/ppermute | solution.py:760
  78.9 3.5 %collective-permute-start.14 = (f32[32,128]{1,0:T(8,128)S(1)}, f32[32,128]{1,0:T(8,128)S(1)}, u32[]{:S(2)}, u32[]{:S(2)}) collective-permute-start(f32[32,128]{1,0:T(8,128)S(1)} %get-tuple-element.59), channel_id=1, source_target_pairs={{0,4},{4,8},{8,12},{1,5},{5,9},{9,13},{2,6},{6,10},{10,14},{3,7},{... | collective-permute-start | bytes 49160 | tf_op jit(solution)/shard_map/ppermute | solution.py:760
  82.4 1.3 %collective-permute-start.15 = (f32[32,128]{1,0:T(8,128)S(1)}, f32[32,128]{1,0:T(8,128)S(1)}, u32[]{:S(2)}, u32[]{:S(2)}) collective-permute-start(f32[32,128]{1,0:T(8,128)S(1)} %get-tuple-element.60), channel_id=1, source_target_pairs={{4,0},{8,4},{12,8},{5,1},{9,5},{13,9},{6,2},{10,6},{14,10},{7,3},{... | collective-permute-start | bytes 49160 | tf_op jit(solution)/shard_map/ppermute | solution.py:760
  83.9 4.3 %collective-permute-done.15.high = f32[32,128]{1,0:T(8,128)S(1)} collective-permute-done((f32[32,128]{1,0:T(8,128)S(1)}, f32[32,128]{1,0:T(8,128)S(1)}, u32[]{:S(2)}, u32[]{:S(2)}) %collective-permute-start.15) | collective-permute-done | bytes 16416 | tf_op jit(solution)/shard_map/ppermute | solution.py:760
  88.1 3.4 %shard_map.162 = (f32[64,32,128]{2,1,0:T(8,128)}, f32[64,32,128]{2,1,0:T(8,128)}) custom-call(f32[64,32,128]{2,1,0:T(8,128)S(1)} %get-tuple-element.33.load.refs_0_, f32[64,32,128]{2,1,0:T(8,128)S(1)} %shard_map.159.partial, f32[32,128]{1,0:T(8,128)S(1)} %collective-permute-done.14.low, f32[32,128]{1,0:T(8,128)S(1)} %collective-permute-done.15.high, ...), custom_call_target="tpu_custom_call" | custom-call | tf_op jit(solution)/shard_map/pallas_call | solution.py:886
  (40 shorter events, 2.0 us)
Async XLA Ops:
  0.6 14.3 %copy-start = (f32[3,3]{1,0:T(4,128)S(1)}, f32[3,3]{1,0:T(4,128)}, u32[]{:S(2)}) copy-start(f32[3,3]{1,0:T(4,128)} %diffusivity.5) | copy-start | bytes 112
  0.6 14.3 %copy-start.1 = (f32[3]{0:T(128)S(1)}, f32[3]{0:T(128)}, u32[]{:S(2)}) copy-start(f32[3]{0:T(128)} %decay.5) | copy-start | bytes 40
  2.8 13.6 %collective-permute-start = (f32[4,32,128]{2,1,0:T(8,128)S(1)}, f32[4,32,128]{2,1,0:T(8,128)S(1)}, u32[]{:S(2)}, u32[]{:S(2)}) collective-permute-start(f32[4,32,128]{2,1,0:T(8,128)S(1)} %get-tuple-element.34), channel_id=1, source_target_pairs={{0,4},{4,8},{8,12},{1,5},{5,9},{9,13},{2,6},{6,10},{10,14},{3,7},{... | collective-permute-start | bytes 196616 | tf_op jit(solution)/shard_map/ppermute | solution.py:760
  7.8 8.7 %collective-permute-start.1 = (f32[4,32,128]{2,1,0:T(8,128)S(1)}, f32[4,32,128]{2,1,0:T(8,128)S(1)}, u32[]{:S(2)}, u32[]{:S(2)}) collective-permute-start(f32[4,32,128]{2,1,0:T(8,128)S(1)} %get-tuple-element.35), channel_id=1, source_target_pairs={{4,0},{8,4},{12,8},{5,1},{9,5},{13,9},{6,2},{10,6},{14,10},{7,3},{... | collective-permute-start | bytes 196616 | tf_op jit(solution)/shard_map/ppermute | solution.py:760
  9.1 10.1 %collective-permute-start.4 = (f32[10,32,128]{2,1,0:T(8,128)S(1)}, f32[10,32,128]{2,1,0:T(8,128)S(1)}, u32[]{:S(2)}, u32[]{:S(2)}) collective-permute-start(f32[10,32,128]{2,1,0:T(8,128)S(1)} %get-tuple-element.43), channel_id=1, source_target_pairs={{0,4},{4,8},{8,12},{1,5},{5,9},{9,13},{2,6},{6,10},{10,14},{3,7},{... | collective-permute-start | bytes 491528 | tf_op jit(solution)/shard_map/ppermute | solution.py:760
  13.6 7.2 %collective-permute-start.5 = (f32[10,32,128]{2,1,0:T(8,128)S(1)}, f32[10,32,128]{2,1,0:T(8,128)S(1)}, u32[]{:S(2)}, u32[]{:S(2)}) collective-permute-start(f32[10,32,128]{2,1,0:T(8,128)S(1)} %get-tuple-element.44), channel_id=1, source_target_pairs={{4,0},{8,4},{12,8},{5,1},{9,5},{13,9},{6,2},{10,6},{14,10},{7,3},{... | collective-permute-start | bytes 491528 | tf_op jit(solution)/shard_map/ppermute | solution.py:760
  16.5 11.0 %copy-start.2 = (bf16[256,256]{1,0:T(8,128)(2,1)S(1)}, bf16[256,256]{1,0:T(8,128)(2,1)}, u32[]{:S(2)}) copy-start(bf16[256,256]{1,0:T(8,128)(2,1)} %constant.22.clone.rest_4_.rest_9_) | copy-start | bytes 393220
  16.5 11.0 %copy-start.3 = (bf16[192,240]{1,0:T(8,128)(2,1)S(1)}, bf16[192,240]{1,0:T(8,128)(2,1)}, u32[]{:S(2)}) copy-start(bf16[192,240]{1,0:T(8,128)(2,1)} %constant.20.clone.rest_2_.rest_7_) | copy-start | bytes 276484
  16.5 11.0 %copy-start.4 = (bf16[144,160]{1,0:T(8,128)(2,1)S(1)}, bf16[144,160]{1,0:T(8,128)(2,1)}, u32[]{:S(2)}) copy-start(bf16[144,160]{1,0:T(8,128)(2,1)} %constant.19.clone.rest_1_.rest_6_) | copy-start | bytes 138244
  16.5 10.9 %copy-start.5 = (bf16[256,128]{1,0:T(8,128)(2,1)S(1)}, bf16[256,128]{1,0:T(8,128)(2,1)}, u32[]{:S(2)}) copy-start(bf16[256,128]{1,0:T(8,128)(2,1)} %constant.23.clone.rest_5_.rest_10_) | copy-start | bytes 196612
  16.5 10.9 %copy-start.6 = (bf16[96,144]{1,0:T(8,128)(2,1)S(1)}, bf16[96,144]{1,0:T(8,128)(2,1)}, u32[]{:S(2)}) copy-start(bf16[96,144]{1,0:T(8,128)(2,1)} %constant.21.clone.rest_3_.rest_8_) | copy-start | bytes 82948
  16.6 10.9 %copy-start.7 = (f32[72,128]{1,0:T(8,128)S(1)}, f32[72,128]{1,0:T(8,128)}, u32[]{:S(2)}) copy-start(f32[72,128]{1,0:T(8,128)} %constant.24.clone.rest_6_.rest_11_) | copy-start | bytes 110596
  16.6 10.9 %copy-start.8 = (bf16[80,96]{1,0:T(8,128)(2,1)S(1)}, bf16[80,96]{1,0:T(8,128)(2,1)}, u32[]{:S(2)}) copy-start(bf16[80,96]{1,0:T(8,128)(2,1)} %constant.18.clone.rest_0_.rest_5_) | copy-start | bytes 46084
  16.6 10.9 %copy-start.9 = (f32[1,128]{1,0:T(1,128)S(1)}, f32[1,128]{1,0:T(1,128)}, u32[]{:S(2)}) copy-start(f32[1,128]{1,0:T(1,128)} %constant.25.clone.rest_7_.rest_12_) | copy-start | bytes 1540
  16.6 10.9 %copy-start.10 = (f32[1,40]{1,0:T(1,128)S(1)}, f32[1,40]{1,0:T(1,128)}, u32[]{:S(2)}) copy-start(f32[1,40]{1,0:T(1,128)} %constant.26.clone.rest_8_.rest_13_) | copy-start | bytes 484
  17.4 4.7 %collective-permute-start.2 = (f32[312,128]{1,0:T(8,128)S(1)}, f32[312,128]{1,0:T(8,128)S(1)}, u32[]{:S(2)}, u32[]{:S(2)}) collective-permute-start(f32[312,128]{1,0:T(8,128)S(1)} %get-tuple-element.39), channel_id=1, source_target_pairs={{0,1},{1,2},{2,3},{3,0},{4,5},{5,6},{6,7},{7,4},{8,9},{9,10},{10,1... | collective-permute-start | bytes 479240 | tf_op jit(solution)/shard_map/ppermute | solution.py:760
  17.4 5.4 %collective-permute-start.3 = (f32[312,128]{1,0:T(8,128)S(1)}, f32[312,128]{1,0:T(8,128)S(1)}, u32[]{:S(2)}, u32[]{:S(2)}) collective-permute-start(f32[312,128]{1,0:T(8,128)S(1)} %get-tuple-element.40), channel_id=1, source_target_pairs={{1,0},{2,1},{3,2},{0,3},{5,4},{6,5},{7,6},{4,7},{9,8},{10,9},{11,1... | collective-permute-start | bytes 479240 | tf_op jit(solution)/shard_map/ppermute | solution.py:760
  23.3 10.9 %collective-permute-start.6 = (f32[760,128]{1,0:T(8,128)S(1)}, f32[760,128]{1,0:T(8,128)S(1)}, u32[]{:S(2)}, u32[]{:S(2)}) collective-permute-start(f32[760,128]{1,0:T(8,128)S(1)} %get-tuple-element.45), channel_id=1, source_target_pairs={{0,1},{1,2},{2,3},{4,5},{5,6},{6,7},{8,9},{9,10},{10,11},{12,13},{... | collective-permute-start | bytes 1167368 | tf_op jit(solution)/shard_map/ppermute | solution.py:760
  26.1 8.1 %collective-permute-start.7 = (f32[760,128]{1,0:T(8,128)S(1)}, f32[760,128]{1,0:T(8,128)S(1)}, u32[]{:S(2)}, u32[]{:S(2)}) collective-permute-start(f32[760,128]{1,0:T(8,128)S(1)} %get-tuple-element.46), channel_id=1, source_target_pairs={{1,0},{2,1},{3,2},{5,4},{6,5},{7,6},{9,8},{10,9},{11,10},{13,12},{... | collective-permute-start | bytes 1167368 | tf_op jit(solution)/shard_map/ppermute | solution.py:760
  35.6 6.8 %collective-permute-start.8 = (f32[176,128]{1,0:T(8,128)S(1)}, f32[176,128]{1,0:T(8,128)S(1)}, u32[]{:S(2)}, u32[]{:S(2)}) collective-permute-start(f32[176,128]{1,0:T(8,128)S(1)} %get-tuple-element.48), channel_id=1, source_target_pairs={{0,4},{4,8},{8,12},{1,5},{5,9},{9,13},{2,6},{6,10},{10,14},{3,7},{... | collective-permute-start | bytes 270344 | tf_op jit(solution)/shard_map/ppermute | solution.py:760
  40.2 6.9 %collective-permute-start.9 = (f32[176,128]{1,0:T(8,128)S(1)}, f32[176,128]{1,0:T(8,128)S(1)}, u32[]{:S(2)}, u32[]{:S(2)}) collective-permute-start(f32[176,128]{1,0:T(8,128)S(1)} %get-tuple-element.49), channel_id=1, source_target_pairs={{4,0},{8,4},{12,8},{5,1},{9,5},{13,9},{6,2},{10,6},{14,10},{7,3},{... | collective-permute-start | bytes 270344 | tf_op jit(solution)/shard_map/ppermute | solution.py:760
  47.1 4.5 %collective-permute-start.10 = (f32[16,128]{1,0:T(8,128)S(1)}, f32[16,128]{1,0:T(8,128)S(1)}, u32[]{:S(2)}, u32[]{:S(2)}) collective-permute-start(f32[16,128]{1,0:T(8,128)S(1)} %shard_map.155.refs_3_), channel_id=1, source_target_pairs={{0,8},{4,12},{8,0},{12,4},{1,9},{5,13},{9,1},{13,5},{2,10},{6,14},... | collective-permute-start | bytes 24584 | tf_op jit(solution)/shard_map/ppermute | solution.py:765
  51.9 8.2 %collective-permute-start.11 = (f32[392,128]{1,0:T(8,128)S(1)}, f32[392,128]{1,0:T(8,128)S(1)}, u32[]{:S(2)}, u32[]{:S(2)}) collective-permute-start(f32[392,128]{1,0:T(8,128)S(1)} %get-tuple-element.51), channel_id=1, source_target_pairs={{0,1},{1,2},{2,3},{4,5},{5,6},{6,7},{8,9},{9,10},{10,11},{12,13},{... | collective-permute-start | bytes 602120 | tf_op jit(solution)/shard_map/ppermute | solution.py:760
  53.2 6.9 %collective-permute-start.12 = (f32[392,128]{1,0:T(8,128)S(1)}, f32[392,128]{1,0:T(8,128)S(1)}, u32[]{:S(2)}, u32[]{:S(2)}) collective-permute-start(f32[392,128]{1,0:T(8,128)S(1)} %get-tuple-element.52), channel_id=1, source_target_pairs={{1,0},{2,1},{3,2},{5,4},{6,5},{7,6},{9,8},{10,9},{11,10},{13,12},{... | collective-permute-start | bytes 602120 | tf_op jit(solution)/shard_map/ppermute | solution.py:760
  60.2 15.9 %collective-permute-start.13 = (f32[16,128]{1,0:T(8,128)S(1)}, f32[16,128]{1,0:T(8,128)S(1)}, u32[]{:S(2)}, u32[]{:S(2)}) collective-permute-start(f32[16,128]{1,0:T(8,128)S(1)} %shard_map.160.table), channel_id=1, source_target_pairs={{0,2},{1,3},{2,0},{3,1},{4,6},{5,7},{6,4},{7,5},{8,10},{9,11},{10,... | collective-permute-start | bytes 24584 | tf_op jit(solution)/shard_map/ppermute | solution.py:765
  76.4 11.8 %collective-permute-start.16 = (f32[64,128]{1,0:T(8,128)S(1)}, f32[64,128]{1,0:T(8,128)S(1)}, u32[]{:S(2)}, u32[]{:S(2)}) collective-permute-start(f32[64,128]{1,0:T(8,128)S(1)} %get-tuple-element.61), channel_id=1, source_target_pairs={{0,1},{1,2},{2,3},{4,5},{5,6},{6,7},{8,9},{9,10},{10,11},{12,13},{... | collective-permute-start | bytes 98312 | tf_op jit(solution)/shard_map/ppermute | solution.py:760
  77.6 10.5 %collective-permute-start.17 = (f32[64,128]{1,0:T(8,128)S(1)}, f32[64,128]{1,0:T(8,128)S(1)}, u32[]{:S(2)}, u32[]{:S(2)}) collective-permute-start(f32[64,128]{1,0:T(8,128)S(1)} %get-tuple-element.62), channel_id=1, source_target_pairs={{1,0},{2,1},{3,2},{5,4},{6,5},{7,6},{9,8},{10,9},{11,10},{13,12},{... | collective-permute-start | bytes 98312 | tf_op jit(solution)/shard_map/ppermute | solution.py:760
  78.9 4.9 %collective-permute-start.14 = (f32[32,128]{1,0:T(8,128)S(1)}, f32[32,128]{1,0:T(8,128)S(1)}, u32[]{:S(2)}, u32[]{:S(2)}) collective-permute-start(f32[32,128]{1,0:T(8,128)S(1)} %get-tuple-element.59), channel_id=1, source_target_pairs={{0,4},{4,8},{8,12},{1,5},{5,9},{9,13},{2,6},{6,10},{10,14},{3,7},{... | collective-permute-start | bytes 49160 | tf_op jit(solution)/shard_map/ppermute | solution.py:760
  82.4 5.7 %collective-permute-start.15 = (f32[32,128]{1,0:T(8,128)S(1)}, f32[32,128]{1,0:T(8,128)S(1)}, u32[]{:S(2)}, u32[]{:S(2)}) collective-permute-start(f32[32,128]{1,0:T(8,128)S(1)} %get-tuple-element.60), channel_id=1, source_target_pairs={{4,0},{8,4},{12,8},{5,1},{9,5},{13,9},{6,2},{10,6},{14,10},{7,3},{... | collective-permute-start | bytes 49160 | tf_op jit(solution)/shard_map/ppermute | solution.py:760

commit v6 on v5

--- a/solution.py
+++ b/solution.py
@@ -226,21 +226,48 @@
     return jnp.where(flag, jnp.float32(1.0), jnp.float32(0.0))
 
 
+def is_even(axis):
+    return lax.rem(lax.axis_index(axis), 2) == 0
+
+
+class Sides:
+    def __init__(self, axis, first, second):
+        position = lax.axis_index(axis)
+        self.even = is_even(axis)
+        self.has_low = as_float(position > 0)
+        self.has_high = as_float(position < lax.axis_size(axis) - 1)
+        self.first, self.second = first, second
+
+    def low(self, *index):
+        return jnp.where(self.even, self.second[index], self.first[index]) * self.has_low
+
+    def high(self, *index):
+        return jnp.where(self.even, self.first[index], self.second[index]) * self.has_high
+
+
+def in_order(even, up, down):
+    return jnp.where(even, up, down), jnp.where(even, down, up)
+
+
 def row_of(stride, col, count, first=0):
     return pl.ds(first * stride + col, count, stride=stride)
 
 
-def pack_columns(box, fields, lows, highs, wide, up, down):
+def pack_columns(box, fields, wide_sides, wide, first, second):
     corner = len(fields) * wide * box.long
+    even = is_even("narrow")
     place = 0
-    for field, low, high in zip(fields, lows, highs):
+    for field, sides in zip(fields, wide_sides):
         for step in range(wide):
-            for target, col in ((up, box.across - wide + step), (down, step)):
-                values = field[row_of(box.across, col, box.long), :]
-                target[place * box.long : (place + 1) * box.long, :] = values.astype(jnp.float32)
-                at = corner + 2 * REACH * place
-                target[at : at + wide, :] = low[row_of(box.across, col, wide), :]
-                target[at + REACH : at + REACH + wide, :] = high[row_of(box.across, col, wide), :]
+            cols = (box.across - wide + step, step)
+            values = [field[row_of(box.across, col, box.long), :] for col in cols]
+            low = [sides.low(row_of(box.across, col, wide), slice(None)) for col in cols]
+            high = [sides.high(row_of(box.across, col, wide), slice(None)) for col in cols]
+            at = corner + 2 * REACH * place
+            for start, parts in ((place * box.long, values), (at, low), (at + REACH, high)):
+                parts = in_order(even, *(part.astype(jnp.float32) for part in parts))
+                size = parts[0].shape[0]
+                first[start : start + size, :], second[start : start + size, :] = parts
             place += 1
 
 
@@ -256,10 +283,10 @@
     low = low.reshape(low.size // box.deep, box.deep)
     high = high.reshape(high.size // box.deep, box.deep)
     sides = [
-        [ref.at[index * size : (index + 1) * size] for index in range(fields)]
-        for ref in (low, high)
+        Sides("wide", *(ref.at[index * size : (index + 1) * size] for ref in (low, high)))
+        for index in range(fields)
     ]
-    pack_columns(box, flat, sides[0], sides[1], wide, up, down)
+    pack_columns(box, flat, sides, wide, up, down)
     known = merged(*(ref[ref.shape[0] - count :, :] for ref in tables))
     table[...] = known
     up[up.shape[0] - count :, :] = known
@@ -267,16 +294,22 @@
 
 
 def bring_in(
-    box, zone, scale, load, own_zone, own_scale, own_load, load_up, load_down, up, down, staged, sems
+    box, zone, scale, load, own_zone, own_scale, own_load, load_first, load_second, first, second,
+    staged, sems
 ):
-    last = box.long
+    even = is_even("wide")
+
+    def edges(wide):
+        up, down = box.long - wide, 0
+        return [pl.ds(jnp.where(even, *pair), wide) for pair in ((up, down), (down, up))]
+
     copies = [
-        (load.at[last - MARGIN :], load_up),
-        (load.at[:MARGIN], load_down),
-        (zone.at[last - REACH :], staged.at[0]),
-        (zone.at[:REACH], staged.at[1]),
-        (scale.at[last - REACH :], up.at[:REACH]),
-        (scale.at[:REACH], down.at[:REACH]),
+        (load.at[edges(MARGIN)[0]], load_first),
+        (load.at[edges(MARGIN)[1]], load_second),
+        (zone.at[edges(REACH)[0]], staged.at[0]),
+        (zone.at[edges(REACH)[1]], staged.at[1]),
+        (scale.at[edges(REACH)[0]], first.at[:REACH]),
+        (scale.at[edges(REACH)[1]], second.at[:REACH]),
         (load, own_load),
         (scale, own_scale),
         (zone, own_zone),
@@ -289,13 +322,13 @@
         copy.start()
     for copy in copies[:4]:
         copy.wait()
-    up[REACH:] = staged[0].astype(jnp.float32)
-    down[REACH:] = staged[1].astype(jnp.float32)
+    first[REACH:] = staged[0].astype(jnp.float32)
+    second[REACH:] = staged[1].astype(jnp.float32)
     for copy in copies[4:]:
         copy.wait()
 
 
-def fill_window(box, window, own, low, high, left, right, wide, place, total, add=None):
+def fill_window(box, window, own, wide_sides, narrow_sides, wide, place, total, add=None):
     flat = window.reshape(box.flat, box.deep)
     nothing = jnp.zeros((box.rows, EDGE, box.deep), jnp.float32)
     window[:, :EDGE, :] = nothing
@@ -309,22 +342,21 @@
         window[0:1, inner, :] = blank
         window[box.rows - 1 :, inner, :] = blank
     window[first:last, inner, :] = add(own[...].astype(jnp.float32), 0, 0)
-    window[first - wide : first, inner, :] = add(low, -1, 0)
-    window[last : last + wide, inner, :] = add(high, 1, 0)
+    window[first - wide : first, inner, :] = add(wide_sides.low(Ellipsis), -1, 0)
+    window[last : last + wide, inner, :] = add(wide_sides.high(Ellipsis), 1, 0)
     corner = total * box.long
     for step in range(wide):
         for source, col, side in (
-            (left, EDGE - wide + step, -1),
-            (right, EDGE + box.across + step, 1),
+            (narrow_sides.low, EDGE - wide + step, -1),
+            (narrow_sides.high, EDGE + box.across + step, 1),
         ):
-            at = (place + step) * box.long
-            values = source[at : at + box.long, :]
-            flat[row_of(box.cols, col, box.long, first), :] = add(values, 0, side)
-            at = corner + 2 * REACH * (place + step)
-            values = source[at : at + wide, :]
-            flat[row_of(box.cols, col, wide, first - wide), :] = add(values, -1, side)
-            values = source[at + REACH : at + REACH + wide, :]
-            flat[row_of(box.cols, col, wide, last), :] = add(values, 1, side)
+            for start, size, row, row_side in (
+                ((place + step) * box.long, box.long, first, 0),
+                (corner + 2 * REACH * (place + step), wide, first - wide, -1),
+                (corner + 2 * REACH * (place + step) + REACH, wide, last, 1),
+            ):
+                values = source(slice(start, start + size), slice(None))
+                flat[row_of(box.cols, col, size, row), :] = add(values, row_side, side)
 
 
 def negative_image(row, x, x_next, flow_before, weights):
@@ -417,15 +449,8 @@
 def first_solve(box, load, low, high, left, right, means, *rest):
     tables = rest[:N_TABLES]
     window, local, spectral, middle = rest[N_TABLES:]
-    _, across_pos, _, across_count = position()
-    has_left, has_right = as_float(across_pos > 0), as_float(across_pos < across_count - 1)
-
-    def inside(values, row_side, col_side):
-        if col_side == 0:
-            return values
-        return values * (has_left if col_side < 0 else has_right)
-
-    fill_window(box, window, load, low[...], high[...], left, right, MARGIN, 0, MARGIN, inside)
+    wide_sides, narrow_sides = Sides("wide", low, high), Sides("narrow", left, right)
+    fill_window(box, window, load, wide_sides, narrow_sides, MARGIN, 0, MARGIN)
 
     def emit(start, values):
         values = values * (1.0 / cheb_center)
@@ -462,10 +487,10 @@
     scale_window,
 ):
     for index, (window, own) in enumerate(((scale_window, scale), (zone_window, zone))):
-        part = slice(index * REACH, (index + 1) * REACH)
-        fill_window(
-            box, window, own, low[part], high[part], left, right, REACH, part.start, 2 * REACH
-        )
+        start = index * REACH
+        wide_sides = Sides("wide", *(ref.at[start : start + REACH] for ref in (low, high)))
+        narrow_sides = Sides("narrow", left, right)
+        fill_window(box, window, own, wide_sides, narrow_sides, REACH, start, 2 * REACH)
     half = [[0.5 * diffusivity[z, d] for d in range(3)] for z in range(3)]
     rates = [decay[z] for z in range(3)]
     lane = lax.broadcasted_iota(jnp.int32, (box.cols, box.deep), 1)
@@ -511,27 +536,30 @@
     last_col = row_of(box.across, box.across - 1, box.long)
     first_col = row_of(box.across, 0, box.long)
 
-    def side(ref, place):
-        return ref[place * box.long : (place + 1) * box.long, :]
-
+    wide_sides, narrow_sides = Sides("wide", low, high), Sides("narrow", left, right)
+
+    def side(source, place):
+        return source(slice(place * box.long, (place + 1) * box.long), slice(None))
+
+    above, below = wide_sides.high, wide_sides.low
     faces = [
-        (0, zone[box.long - 1], scale[box.long - 1], local[box.long - 1], high[REACH], high[0]),
-        (0, zone[0], scale[0], local[0], low[2 * REACH - 1], low[REACH - 1]),
+        (0, zone[box.long - 1], scale[box.long - 1], local[box.long - 1], above(REACH), above(0)),
+        (0, zone[0], scale[0], local[0], below(2 * REACH - 1), below(REACH - 1)),
         (
             1,
             zone_flat[last_col, :],
             scale_flat[last_col, :],
             local_flat[last_col, :],
-            side(right, REACH),
-            side(right, 0),
+            side(narrow_sides.high, REACH),
+            side(narrow_sides.high, 0),
         ),
         (
             1,
             zone_flat[first_col, :],
             scale_flat[first_col, :],
             local_flat[first_col, :],
-            side(left, 2 * REACH - 1),
-            side(left, REACH - 1),
+            side(narrow_sides.low, 2 * REACH - 1),
+            side(narrow_sides.low, REACH - 1),
         ),
     ]
     flows = []
@@ -552,10 +580,10 @@
     known = known + at_own_row(line_of(numbers, (8, known.shape[1])), known.shape)
     out[...] = known
     edge = REACH * box.across
-    up[:edge] = local_flat[shape[0] - edge :, :]
-    up[edge:] = known
-    down[:edge] = local_flat[:edge, :]
-    down[edge:] = known
+    even = is_even("wide")
+    for target, pair in ((up, (box.long - REACH, 0)), (down, (0, box.long - REACH))):
+        target[:edge] = local[pl.ds(jnp.where(even, *pair), REACH)].reshape(edge, box.deep)
+        target[edge:] = known
 
 
 def column(values, index):
@@ -648,8 +676,11 @@
         return values + shift
 
     edge = REACH * box.across
-    low, high = (ref[:edge, :].reshape(REACH, box.across, box.deep) for ref in (low, high))
-    fill_window(box, window, local, low, high, left, right, REACH, 0, REACH, add)
+    low, high = (
+        ref.at[:edge].reshape(REACH, box.across, box.deep) for ref in (low, high)
+    )
+    wide_sides, narrow_sides = Sides("wide", low, high), Sides("narrow", left, right)
+    fill_window(box, window, local, wide_sides, narrow_sides, REACH, 0, REACH, add)
     weights = (to_long, to_across, to_deep, mass)
 
     def one_row(row, flow):
@@ -695,11 +726,12 @@
     sums = column(numbers, LOAD_SUM) * (1.0 - 1.0 / cheb_center) - sums
     own = at_box(answer(inverse, sums) * gain, 0, 0)
     shift[...] = jnp.broadcast_to(own, shift.shape)
-    top[...] = partial[box.long - 1] + own
-    bottom[...] = partial[0] + own
+    rows = in_order(is_even("wide"), partial[box.long - 1], partial[0])
+    top[...], bottom[...] = rows[0] + own, rows[1] + own
     flat = partial.reshape(box.long * box.across, box.deep)
-    last_col[...] = flat[row_of(box.across, box.across - 1, box.long), :] + own
-    first_col[...] = flat[row_of(box.across, 0, box.long), :] + own
+    cols = [flat[row_of(box.across, col, box.long), :] for col in (box.across - 1, 0)]
+    cols = in_order(is_even("narrow"), *cols)
+    last_col[...], first_col[...] = cols[0] + own, cols[1] + own
 
 
 def last_residual(
@@ -729,10 +761,11 @@
     window[1 : 1 + box.long, inner, :] = partial[...] + shift[0:1, :].reshape(1, 1, box.deep)
     own = pltpu.make_async_copy(window.at[1 : 1 + box.long, inner, :], iterate, sems.at[0])
     own.start()
-    window[0, inner, :] = low[...]
-    window[1 + box.long, inner, :] = high[...]
-    flat[row_of(box.cols, EDGE - 1, box.long, 1), :] = left[...]
-    flat[row_of(box.cols, EDGE + box.across, box.long, 1), :] = right[...]
+    wide_sides, narrow_sides = Sides("wide", low, high), Sides("narrow", left, right)
+    window[0, inner, :] = wide_sides.low(Ellipsis)
+    window[1 + box.long, inner, :] = wide_sides.high(Ellipsis)
+    flat[row_of(box.cols, EDGE - 1, box.long, 1), :] = narrow_sides.low(Ellipsis)
+    flat[row_of(box.cols, EDGE + box.across, box.long, 1), :] = narrow_sides.high(Ellipsis)
     weights = (to_long, to_across, to_deep, mass)
 
     def one_row(row, flow):
@@ -753,11 +786,18 @@
         copy.wait()
 
 
-def exchange(axis, last, first, around=False):
+def exchange(axis, first, second, around=False):
     size = lax.axis_size(axis)
-    up = [(i, (i + 1) % size) for i in range(size if around else size - 1)]
-    down = [(j, i) for i, j in up]
-    return lax.ppermute(last, axis, up), lax.ppermute(first, axis, down)
+    swaps = []
+    for way in range(2):
+        pairs = []
+        for place in range(size):
+            other = place + 1 if place % 2 == way else place - 1
+            if around and size % 2 == 0:
+                other %= size
+            pairs.append((place, other if 0 <= other < size else place))
+        swaps.append(pairs)
+    return lax.ppermute(first, axis, swaps[0]), lax.ppermute(second, axis, swaps[1])
 
 
 def two_away(axis, table):

time: 92.2 us -> 73.9 us (0.80)
  the two profiles are of different devices: /device:TPU:0 before, /device:TPU:13 now
where the time goes in v6:
time: 73.9 us; the launch traced here: 73.6 us
  Pallas kernels  32.6 us (44%)
  starting transfers between devices  28.1 us (38%)
  waiting for transfers between devices  11.7 us (16%)
  between operations  1.16 us (2%)
    ppermute x8, starting transfers between devices, exchange(): lax.ppermute(second, axis, swaps[1])  25 us
    pallas_call x1, Pallas kernels, on_device(): call(functools.partial(second_solve, box), cells, [VMEM] * (13 + N_TABLES...  10.2 us
    ppermute x8, waiting for transfers between devices, exchange(): lax.ppermute(second, axis, swaps[1])  8.28 us
    pallas_call x1, Pallas kernels, on_device(): call(functools.partial(first_solve, box), (window, cells), [VMEM] * (6 +...  6.71 us
    pallas_call x1, Pallas kernels, on_device(): call(functools.partial(weights_of, box), (window,) * 4, [VMEM] * 6 + [SME...  3.71 us
    pallas_call x1, Pallas kernels, on_device(): call(functools.partial(last_residual, box), (cells, cells), [VMEM] * 11,...  3.43 us
    ppermute x2, waiting for transfers between devices, two_away(): return lax.ppermute(table, axis, [(i, (i + 2) % size) for i in range(size)])  3.4 us
    ppermute x8, starting transfers between devices, exchange(): lax.ppermute(first, axis, swaps[0])  2.99 us
  transfers between devices with their start and end apart: 18, of which 4 were waited for; matrix products, arithmetic and copies ran while one was open for 0% of the time, Pallas kernels for 33%

profile of v6, /device:TPU:13, one launch (start us, length us, event | category | flops | bytes accessed | tf_op | source)
XLA Modules:
  0.0 73.6 jit_solution(10433162845916705562)
XLA Ops:
  0.7 2.2 %shard_map.149 = (s32[64,32,128]{2,1,0:T(8,128)S(1)}, f32[64,32,128]{2,1,0:T(8,128)S(1)}, f32[64,32,128]{2,1,0:T(8,128)S(1)}, f32[4,32,128]{2,1,0:T(8,128)S(1)},...) custom-call(s32[64,32,128]{2,1,0:T(8,128)} %zone.1, f32[64,32,128]{2,1,0:T(8,128)} %scale.1, ...), custom_call_target="tpu_custom_call" | custom-call | tf_op jit(solution)/shard_map/pallas_call | solution.py:839
  2.8 0.2 collective-permute-start
  3.1 4.3 %collective-permute-start.1 = (f32[4,32,128]{2,1,0:T(8,128)S(1)}, f32[4,32,128]{2,1,0:T(8,128)S(1)}, u32[]{:S(2)}, u32[]{:S(2)}) collective-permute-start(f32[4,32,128]{2,1,0:T(8,128)S(1)} %get-tuple-element.35), channel_id=1, source_target_pairs={{0,0},{4,8},{8,4},{12,12},{1,1},{5,9},{9,5},{13,13},{2,2},{6,10},{... | collective-permute-start | bytes 196616 | tf_op jit(solution)/shard_map/ppermute | solution.py:800
  7.4 0.1 collective-permute-start.4
  7.5 1.9 %collective-permute-start.5 = (f32[10,32,128]{2,1,0:T(8,128)S(1)}, f32[10,32,128]{2,1,0:T(8,128)S(1)}, u32[]{:S(2)}, u32[]{:S(2)}) collective-permute-start(f32[10,32,128]{2,1,0:T(8,128)S(1)} %get-tuple-element.44), channel_id=1, source_target_pairs={{0,0},{4,8},{8,4},{12,12},{1,1},{5,9},{9,5},{13,13},{2,2},{6,10},{... | collective-permute-start | bytes 491528 | tf_op jit(solution)/shard_map/ppermute | solution.py:800
  9.4 1.5 %shard_map.150 = (f32[8,128]{1,0:T(8,128)S(1)}, f32[16,128]{1,0:T(8,128)S(1)}) custom-call(s32[64,32,128]{2,1,0:T(8,128)S(1)} %get-tuple-element.36.zone.refs_1_, f32[64,32,128]{2,1,0:T(8,128)S(1)} %get-tuple-element.37.scale.refs_0_, f32[64,32,128]{2,1,0:T(8,128)S(1)} %get-tuple-element.33.load.refs_0_, f32[3,3]{1,0:T(4,128)S(1)} %copy-done, f32[3]{0:T(128)S(1)} %copy-done.1), custom_call_target="tpu_custom_call" | custom-call | tf_op jit(solution)/shard_map/pallas_call | solution.py:849
  11.1 0.8 %shard_map.151 = (f32[312,128]{1,0:T(8,128)S(1)}, f32[312,128]{1,0:T(8,128)S(1)}, f32[16,128]{1,0:T(8,128)}) custom-call(f32[64,32,128]{2,1,0:T(8,128)S(1)} %get-tuple-element.33.load.refs_0_, f32[4,32,128]{2,1,0:T(8,128)S(1)} %collective-permute-done.refs_1_.low, f32[4,32,128]{2,1,0:T(8,128)S(1)} %collective-permute-done.1.refs_2_.high, ...), custom_call_target="tpu_custom_call" | custom-call | tf_op jit(solution)/shard_map/pallas_call | solution.py:836
  11.8 1.2 %collective-permute-start.2 = (f32[312,128]{1,0:T(8,128)S(1)}, f32[312,128]{1,0:T(8,128)S(1)}, u32[]{:S(2)}, u32[]{:S(2)}) collective-permute-start(f32[312,128]{1,0:T(8,128)S(1)} %get-tuple-element.39), channel_id=1, source_target_pairs={{0,1},{1,0},{2,3},{3,2},{4,5},{5,4},{6,7},{7,6},{8,9},{9,8},{10,11... | collective-permute-start | bytes 479240 | tf_op jit(solution)/shard_map/ppermute | solution.py:800
  13.1 1.1 %collective-permute-start.3 = (f32[312,128]{1,0:T(8,128)S(1)}, f32[312,128]{1,0:T(8,128)S(1)}, u32[]{:S(2)}, u32[]{:S(2)}) collective-permute-start(f32[312,128]{1,0:T(8,128)S(1)} %get-tuple-element.40), channel_id=1, source_target_pairs={{0,3},{1,2},{2,1},{3,0},{4,7},{5,6},{6,5},{7,4},{8,11},{9,10},{10,... | collective-permute-start | bytes 479240 | tf_op jit(solution)/shard_map/ppermute | solution.py:800
  14.2 4.6 %collective-permute-done.3.right.refs_6_ = f32[312,128]{1,0:T(8,128)S(1)} collective-permute-done((f32[312,128]{1,0:T(8,128)S(1)}, f32[312,128]{1,0:T(8,128)S(1)}, u32[]{:S(2)}, u32[]{:S(2)}) %collective-permute-start.3) | collective-permute-done | bytes 159776 | tf_op jit(solution)/shard_map/ppermute | solution.py:800
  18.8 0.4 shard_map.153
  19.2 0.1 collective-permute-start.6
  19.4 3.5 %collective-permute-start.7 = (f32[760,128]{1,0:T(8,128)S(1)}, f32[760,128]{1,0:T(8,128)S(1)}, u32[]{:S(2)}, u32[]{:S(2)}) collective-permute-start(f32[760,128]{1,0:T(8,128)S(1)} %get-tuple-element.46), channel_id=1, source_target_pairs={{0,0},{1,2},{2,1},{3,3},{4,4},{5,6},{6,5},{7,7},{8,8},{9,10},{10,9... | collective-permute-start | bytes 1167368 | tf_op jit(solution)/shard_map/ppermute | solution.py:800
  22.9 6.7 %shard_map.152 = (f32[74,48,128]{2,1,0:T(8,128)S(1)}, f32[64,32,128]{2,1,0:T(8,128)S(1)}) custom-call(f32[64,32,128]{2,1,0:T(8,128)S(1)} %get-tuple-element.33.load.refs_0_, f32[4,32,128]{2,1,0:T(8,128)S(1)} %collective-permute-done.refs_1_.low, f32[4,32,128]{2,1,0:T(8,128)S(1)} %collective-permute-done.1.refs_2_.high, ...), custom_call_target="tpu_custom_call" | custom-call | flops 4000000000 | tf_op jit(solution)/shard_map/pallas_call | solution.py:857
  29.6 1.4 %shard_map.154 = (f32[16,128]{1,0:T(8,128)S(1)}, f32[176,128]{1,0:T(8,128)S(1)}, f32[176,128]{1,0:T(8,128)S(1)}) custom-call(s32[64,32,128]{2,1,0:T(8,128)S(1)} %get-tuple-element.36.zone.refs_1_, f32[64,32,128]{2,1,0:T(8,128)S(1)} %get-tuple-element.37.scale.refs_0_, f32[64,32,128]{2,1,0:T(8,128)S(1)} %get-tuple-element.42.local.refs_0_, ...), custom_call_target="tpu_custom_call" | custom-call | tf_op jit(solution)/shard_map/pallas_call | solution.py:865
  31.0 0.5 collective-permute-start.8
  31.6 3.2 %collective-permute-start.9 = (f32[176,128]{1,0:T(8,128)S(1)}, f32[176,128]{1,0:T(8,128)S(1)}, u32[]{:S(2)}, u32[]{:S(2)}) collective-permute-start(f32[176,128]{1,0:T(8,128)S(1)} %get-tuple-element.49), channel_id=1, source_target_pairs={{0,0},{4,8},{8,4},{12,12},{1,1},{5,9},{9,5},{13,13},{2,2},{6,10},{... | collective-permute-start | bytes 270344 | tf_op jit(solution)/shard_map/ppermute | solution.py:800
  34.8 2.0 %collective-permute-done.9.high.refs_2_ = f32[176,128]{1,0:T(8,128)S(1)} collective-permute-done((f32[176,128]{1,0:T(8,128)S(1)}, f32[176,128]{1,0:T(8,128)S(1)}, u32[]{:S(2)}, u32[]{:S(2)}) %collective-permute-start.9) | collective-permute-done | bytes 90144 | tf_op jit(solution)/shard_map/ppermute | solution.py:800
  36.8 3.4 %collective-permute-done.10.refs_4_ = f32[16,128]{1,0:T(8,128)S(1)} collective-permute-done((f32[16,128]{1,0:T(8,128)S(1)}, f32[16,128]{1,0:T(8,128)S(1)}, u32[]{:S(2)}, u32[]{:S(2)}) %collective-permute-start.10) | collective-permute-done | bytes 8224 | tf_op jit(solution)/shard_map/ppermute | solution.py:805
  40.2 0.2 shard_map.156
  40.5 0.3 collective-permute-start.11
  40.8 4.8 %collective-permute-start.12 = (f32[392,128]{1,0:T(8,128)S(1)}, f32[392,128]{1,0:T(8,128)S(1)}, u32[]{:S(2)}, u32[]{:S(2)}) collective-permute-start(f32[392,128]{1,0:T(8,128)S(1)} %get-tuple-element.52), channel_id=1, source_target_pairs={{0,0},{1,2},{2,1},{3,3},{4,4},{5,6},{6,5},{7,7},{8,8},{9,10},{10,9... | collective-permute-start | bytes 602120 | tf_op jit(solution)/shard_map/ppermute | solution.py:800
  45.6 3.7 %shard_map.158 = (f32[74,48,128]{2,1,0:T(8,128)S(1)}, f32[74,48,128]{2,1,0:T(8,128)S(1)}, f32[74,48,128]{2,1,0:T(8,128)S(1)}, f32[74,48,128]{2,1,0:T(8,128)S(1)}) custom-call(s32[64,32,128]{2,1,0:T(8,128)S(1)} %get-tuple-element.36.zone.refs_1_, f32[64,32,128]{2,1,0:T(8,128)S(1)} %get-tuple-element.37.scale.refs_0_, ...), custom_call_target="tpu_custom_call" | custom-call | flops 1000000000 | tf_op jit(solution)/shard_map/pallas_call | solution.py:870
  49.3 1.7 %shard_map.157.inverse = f32[16,128]{1,0:T(8,128)S(1)} custom-call(f32[16,128]{1,0:T(8,128)S(1)} %get-tuple-element.53.told.table), custom_call_target="tpu_custom_call" | custom-call | tf_op jit(solution)/shard_map/pallas_call | solution.py:887
  51.1 0.1 collective-permute-start.13
  51.1 10.2 %shard_map.159.partial = f32[64,32,128]{2,1,0:T(8,128)S(1)} custom-call(f32[64,32,128]{2,1,0:T(8,128)S(1)} %get-tuple-element.42.local.refs_0_, f32[176,128]{1,0:T(8,128)S(1)} %collective-permute-done.8.low.refs_1_, f32[176,128]{1,0:T(8,128)S(1)} %collective-permute-done.9.high.refs_2_, f32[392,128]{1,0:T(8,128)S(1)} %collective-permute-done.11.left.low, ...), custom_call_target="tpu_custom_call" | custom-call | flops 4000000000 | tf_op jit(solution)/shard_map/pallas_call | solution.py:899
  61.3 0.3 shard_map.161
  61.7 0.4 collective-permute-start.16
  62.1 3.4 %collective-permute-start.17 = (f32[64,128]{1,0:T(8,128)S(1)}, f32[64,128]{1,0:T(8,128)S(1)}, u32[]{:S(2)}, u32[]{:S(2)}) collective-permute-start(f32[64,128]{1,0:T(8,128)S(1)} %get-tuple-element.62), channel_id=1, source_target_pairs={{0,0},{1,2},{2,1},{3,3},{4,4},{5,6},{6,5},{7,7},{8,8},{9,10},{10,9... | collective-permute-start | bytes 98312 | tf_op jit(solution)/shard_map/ppermute | solution.py:800
  65.5 2.9 %collective-permute-start.15 = (f32[32,128]{1,0:T(8,128)S(1)}, f32[32,128]{1,0:T(8,128)S(1)}, u32[]{:S(2)}, u32[]{:S(2)}) collective-permute-start(f32[32,128]{1,0:T(8,128)S(1)} %get-tuple-element.60), channel_id=1, source_target_pairs={{0,0},{4,8},{8,4},{12,12},{1,1},{5,9},{9,5},{13,13},{2,2},{6,10},{... | collective-permute-start | bytes 49160 | tf_op jit(solution)/shard_map/ppermute | solution.py:800
  68.4 1.6 %collective-permute-done.15.high = f32[32,128]{1,0:T(8,128)S(1)} collective-permute-done((f32[32,128]{1,0:T(8,128)S(1)}, f32[32,128]{1,0:T(8,128)S(1)}, u32[]{:S(2)}, u32[]{:S(2)}) %collective-permute-start.15) | collective-permute-done | bytes 16416 | tf_op jit(solution)/shard_map/ppermute | solution.py:800
  70.0 3.4 %shard_map.162 = (f32[64,32,128]{2,1,0:T(8,128)}, f32[64,32,128]{2,1,0:T(8,128)}) custom-call(f32[64,32,128]{2,1,0:T(8,128)S(1)} %get-tuple-element.33.load.refs_0_, f32[64,32,128]{2,1,0:T(8,128)S(1)} %shard_map.159.partial, f32[32,128]{1,0:T(8,128)S(1)} %collective-permute-done.14.low, f32[32,128]{1,0:T(8,128)S(1)} %collective-permute-done.15.high, ...), custom_call_target="tpu_custom_call" | custom-call | tf_op jit(solution)/shard_map/pallas_call | solution.py:926
  (40 shorter events, 0.2 us)
Async XLA Ops:
  0.6 8.8 %copy-start = (f32[3,3]{1,0:T(4,128)S(1)}, f32[3,3]{1,0:T(4,128)}, u32[]{:S(2)}) copy-start(f32[3,3]{1,0:T(4,128)} %diffusivity.5) | copy-start | bytes 112
  0.6 8.8 %copy-start.1 = (f32[3]{0:T(128)S(1)}, f32[3]{0:T(128)}, u32[]{:S(2)}) copy-start(f32[3]{0:T(128)} %decay.5) | copy-start | bytes 40
  2.8 8.1 %collective-permute-start = (f32[4,32,128]{2,1,0:T(8,128)S(1)}, f32[4,32,128]{2,1,0:T(8,128)S(1)}, u32[]{:S(2)}, u32[]{:S(2)}) collective-permute-start(f32[4,32,128]{2,1,0:T(8,128)S(1)} %get-tuple-element.34), channel_id=1, source_target_pairs={{0,4},{4,0},{8,12},{12,8},{1,5},{5,1},{9,13},{13,9},{2,6},{6,2},{1... | collective-permute-start | bytes 196616 | tf_op jit(solution)/shard_map/ppermute | solution.py:800
  3.1 7.9 %collective-permute-start.1 = (f32[4,32,128]{2,1,0:T(8,128)S(1)}, f32[4,32,128]{2,1,0:T(8,128)S(1)}, u32[]{:S(2)}, u32[]{:S(2)}) collective-permute-start(f32[4,32,128]{2,1,0:T(8,128)S(1)} %get-tuple-element.35), channel_id=1, source_target_pairs={{0,0},{4,8},{8,4},{12,12},{1,1},{5,9},{9,5},{13,13},{2,2},{6,10},{... | collective-permute-start | bytes 196616 | tf_op jit(solution)/shard_map/ppermute | solution.py:800
  7.4 6.8 %collective-permute-start.4 = (f32[10,32,128]{2,1,0:T(8,128)S(1)}, f32[10,32,128]{2,1,0:T(8,128)S(1)}, u32[]{:S(2)}, u32[]{:S(2)}) collective-permute-start(f32[10,32,128]{2,1,0:T(8,128)S(1)} %get-tuple-element.43), channel_id=1, source_target_pairs={{0,4},{4,0},{8,12},{12,8},{1,5},{5,1},{9,13},{13,9},{2,6},{6,2},{1... | collective-permute-start | bytes 491528 | tf_op jit(solution)/shard_map/ppermute | solution.py:800
  7.5 6.7 %collective-permute-start.5 = (f32[10,32,128]{2,1,0:T(8,128)S(1)}, f32[10,32,128]{2,1,0:T(8,128)S(1)}, u32[]{:S(2)}, u32[]{:S(2)}) collective-permute-start(f32[10,32,128]{2,1,0:T(8,128)S(1)} %get-tuple-element.44), channel_id=1, source_target_pairs={{0,0},{4,8},{8,4},{12,12},{1,1},{5,9},{9,5},{13,13},{2,2},{6,10},{... | collective-permute-start | bytes 491528 | tf_op jit(solution)/shard_map/ppermute | solution.py:800
  11.0 11.9 %copy-start.2 = (bf16[256,256]{1,0:T(8,128)(2,1)S(1)}, bf16[256,256]{1,0:T(8,128)(2,1)}, u32[]{:S(2)}) copy-start(bf16[256,256]{1,0:T(8,128)(2,1)} %constant.22.clone.rest_4_.rest_9_) | copy-start | bytes 393220
  11.0 11.9 %copy-start.3 = (bf16[192,240]{1,0:T(8,128)(2,1)S(1)}, bf16[192,240]{1,0:T(8,128)(2,1)}, u32[]{:S(2)}) copy-start(bf16[192,240]{1,0:T(8,128)(2,1)} %constant.20.clone.rest_2_.rest_7_) | copy-start | bytes 276484
  11.0 11.9 %copy-start.4 = (bf16[144,160]{1,0:T(8,128)(2,1)S(1)}, bf16[144,160]{1,0:T(8,128)(2,1)}, u32[]{:S(2)}) copy-start(bf16[144,160]{1,0:T(8,128)(2,1)} %constant.19.clone.rest_1_.rest_6_) | copy-start | bytes 138244
  11.0 11.9 %copy-start.5 = (bf16[256,128]{1,0:T(8,128)(2,1)S(1)}, bf16[256,128]{1,0:T(8,128)(2,1)}, u32[]{:S(2)}) copy-start(bf16[256,128]{1,0:T(8,128)(2,1)} %constant.23.clone.rest_5_.rest_10_) | copy-start | bytes 196612
  11.0 11.8 %copy-start.6 = (bf16[96,144]{1,0:T(8,128)(2,1)S(1)}, bf16[96,144]{1,0:T(8,128)(2,1)}, u32[]{:S(2)}) copy-start(bf16[96,144]{1,0:T(8,128)(2,1)} %constant.21.clone.rest_3_.rest_8_) | copy-start | bytes 82948
  11.0 11.8 %copy-start.7 = (f32[72,128]{1,0:T(8,128)S(1)}, f32[72,128]{1,0:T(8,128)}, u32[]{:S(2)}) copy-start(f32[72,128]{1,0:T(8,128)} %constant.24.clone.rest_6_.rest_11_) | copy-start | bytes 110596
  11.0 11.8 %copy-start.8 = (bf16[80,96]{1,0:T(8,128)(2,1)S(1)}, bf16[80,96]{1,0:T(8,128)(2,1)}, u32[]{:S(2)}) copy-start(bf16[80,96]{1,0:T(8,128)(2,1)} %constant.18.clone.rest_0_.rest_5_) | copy-start | bytes 46084
  11.1 11.8 %copy-start.9 = (f32[1,128]{1,0:T(1,128)S(1)}, f32[1,128]{1,0:T(1,128)}, u32[]{:S(2)}) copy-start(f32[1,128]{1,0:T(1,128)} %constant.25.clone.rest_7_.rest_12_) | copy-start | bytes 1540
  11.1 11.8 %copy-start.10 = (f32[1,40]{1,0:T(1,128)S(1)}, f32[1,40]{1,0:T(1,128)}, u32[]{:S(2)}) copy-start(f32[1,40]{1,0:T(1,128)} %constant.26.clone.rest_8_.rest_13_) | copy-start | bytes 484
  11.8 2.3 %collective-permute-start.2 = (f32[312,128]{1,0:T(8,128)S(1)}, f32[312,128]{1,0:T(8,128)S(1)}, u32[]{:S(2)}, u32[]{:S(2)}) collective-permute-start(f32[312,128]{1,0:T(8,128)S(1)} %get-tuple-element.39), channel_id=1, source_target_pairs={{0,1},{1,0},{2,3},{3,2},{4,5},{5,4},{6,7},{7,6},{8,9},{9,8},{10,11... | collective-permute-start | bytes 479240 | tf_op jit(solution)/shard_map/ppermute | solution.py:800
  13.1 5.7 %collective-permute-start.3 = (f32[312,128]{1,0:T(8,128)S(1)}, f32[312,128]{1,0:T(8,128)S(1)}, u32[]{:S(2)}, u32[]{:S(2)}) collective-permute-start(f32[312,128]{1,0:T(8,128)S(1)} %get-tuple-element.40), channel_id=1, source_target_pairs={{0,3},{1,2},{2,1},{3,0},{4,7},{5,6},{6,5},{7,4},{8,11},{9,10},{10,... | collective-permute-start | bytes 479240 | tf_op jit(solution)/shard_map/ppermute | solution.py:800
  19.2 10.4 %collective-permute-start.6 = (f32[760,128]{1,0:T(8,128)S(1)}, f32[760,128]{1,0:T(8,128)S(1)}, u32[]{:S(2)}, u32[]{:S(2)}) collective-permute-start(f32[760,128]{1,0:T(8,128)S(1)} %get-tuple-element.45), channel_id=1, source_target_pairs={{0,1},{1,0},{2,3},{3,2},{4,5},{5,4},{6,7},{7,6},{8,9},{9,8},{10,11... | collective-permute-start | bytes 1167368 | tf_op jit(solution)/shard_map/ppermute | solution.py:800
  19.4 10.3 %collective-permute-start.7 = (f32[760,128]{1,0:T(8,128)S(1)}, f32[760,128]{1,0:T(8,128)S(1)}, u32[]{:S(2)}, u32[]{:S(2)}) collective-permute-start(f32[760,128]{1,0:T(8,128)S(1)} %get-tuple-element.46), channel_id=1, source_target_pairs={{0,0},{1,2},{2,1},{3,3},{4,4},{5,6},{6,5},{7,7},{8,8},{9,10},{10,9... | collective-permute-start | bytes 1167368 | tf_op jit(solution)/shard_map/ppermute | solution.py:800
  31.0 3.7 %collective-permute-start.8 = (f32[176,128]{1,0:T(8,128)S(1)}, f32[176,128]{1,0:T(8,128)S(1)}, u32[]{:S(2)}, u32[]{:S(2)}) collective-permute-start(f32[176,128]{1,0:T(8,128)S(1)} %get-tuple-element.48), channel_id=1, source_target_pairs={{0,4},{4,0},{8,12},{12,8},{1,5},{5,1},{9,13},{13,9},{2,6},{6,2},{1... | collective-permute-start | bytes 270344 | tf_op jit(solution)/shard_map/ppermute | solution.py:800
  31.6 5.3 %collective-permute-start.9 = (f32[176,128]{1,0:T(8,128)S(1)}, f32[176,128]{1,0:T(8,128)S(1)}, u32[]{:S(2)}, u32[]{:S(2)}) collective-permute-start(f32[176,128]{1,0:T(8,128)S(1)} %get-tuple-element.49), channel_id=1, source_target_pairs={{0,0},{4,8},{8,4},{12,12},{1,1},{5,9},{9,5},{13,13},{2,2},{6,10},{... | collective-permute-start | bytes 270344 | tf_op jit(solution)/shard_map/ppermute | solution.py:800
  36.8 3.4 %collective-permute-start.10 = (f32[16,128]{1,0:T(8,128)S(1)}, f32[16,128]{1,0:T(8,128)S(1)}, u32[]{:S(2)}, u32[]{:S(2)}) collective-permute-start(f32[16,128]{1,0:T(8,128)S(1)} %shard_map.155.refs_3_), channel_id=1, source_target_pairs={{0,8},{4,12},{8,0},{12,4},{1,9},{5,13},{9,1},{13,5},{2,10},{6,14},... | collective-permute-start | bytes 24584 | tf_op jit(solution)/shard_map/ppermute | solution.py:805
  40.5 10.6 %collective-permute-start.11 = (f32[392,128]{1,0:T(8,128)S(1)}, f32[392,128]{1,0:T(8,128)S(1)}, u32[]{:S(2)}, u32[]{:S(2)}) collective-permute-start(f32[392,128]{1,0:T(8,128)S(1)} %get-tuple-element.51), channel_id=1, source_target_pairs={{0,1},{1,0},{2,3},{3,2},{4,5},{5,4},{6,7},{7,6},{8,9},{9,8},{10,11... | collective-permute-start | bytes 602120 | tf_op jit(solution)/shard_map/ppermute | solution.py:800
  40.8 10.3 %collective-permute-start.12 = (f32[392,128]{1,0:T(8,128)S(1)}, f32[392,128]{1,0:T(8,128)S(1)}, u32[]{:S(2)}, u32[]{:S(2)}) collective-permute-start(f32[392,128]{1,0:T(8,128)S(1)} %get-tuple-element.52), channel_id=1, source_target_pairs={{0,0},{1,2},{2,1},{3,3},{4,4},{5,6},{6,5},{7,7},{8,8},{9,10},{10,9... | collective-permute-start | bytes 602120 | tf_op jit(solution)/shard_map/ppermute | solution.py:800
  51.1 10.3 %collective-permute-start.13 = (f32[16,128]{1,0:T(8,128)S(1)}, f32[16,128]{1,0:T(8,128)S(1)}, u32[]{:S(2)}, u32[]{:S(2)}) collective-permute-start(f32[16,128]{1,0:T(8,128)S(1)} %shard_map.160.table), channel_id=1, source_target_pairs={{0,2},{1,3},{2,0},{3,1},{4,6},{5,7},{6,4},{7,5},{8,10},{9,11},{10,... | collective-permute-start | bytes 24584 | tf_op jit(solution)/shard_map/ppermute | solution.py:805
  61.7 8.3 %collective-permute-start.16 = (f32[64,128]{1,0:T(8,128)S(1)}, f32[64,128]{1,0:T(8,128)S(1)}, u32[]{:S(2)}, u32[]{:S(2)}) collective-permute-start(f32[64,128]{1,0:T(8,128)S(1)} %get-tuple-element.61), channel_id=1, source_target_pairs={{0,1},{1,0},{2,3},{3,2},{4,5},{5,4},{6,7},{7,6},{8,9},{9,8},{10,11... | collective-permute-start | bytes 98312 | tf_op jit(solution)/shard_map/ppermute | solution.py:800
  62.1 7.9 %collective-permute-start.17 = (f32[64,128]{1,0:T(8,128)S(1)}, f32[64,128]{1,0:T(8,128)S(1)}, u32[]{:S(2)}, u32[]{:S(2)}) collective-permute-start(f32[64,128]{1,0:T(8,128)S(1)} %get-tuple-element.62), channel_id=1, source_target_pairs={{0,0},{1,2},{2,1},{3,3},{4,4},{5,6},{6,5},{7,7},{8,8},{9,10},{10,9... | collective-permute-start | bytes 98312 | tf_op jit(solution)/shard_map/ppermute | solution.py:800
  65.4 3.0 %collective-permute-start.14 = (f32[32,128]{1,0:T(8,128)S(1)}, f32[32,128]{1,0:T(8,128)S(1)}, u32[]{:S(2)}, u32[]{:S(2)}) collective-permute-start(f32[32,128]{1,0:T(8,128)S(1)} %get-tuple-element.59), channel_id=1, source_target_pairs={{0,4},{4,0},{8,12},{12,8},{1,5},{5,1},{9,13},{13,9},{2,6},{6,2},{1... | collective-permute-start | bytes 49160 | tf_op jit(solution)/shard_map/ppermute | solution.py:800
  65.5 4.5 %collective-permute-start.15 = (f32[32,128]{1,0:T(8,128)S(1)}, f32[32,128]{1,0:T(8,128)S(1)}, u32[]{:S(2)}, u32[]{:S(2)}) collective-permute-start(f32[32,128]{1,0:T(8,128)S(1)} %get-tuple-element.60), channel_id=1, source_target_pairs={{0,0},{4,8},{8,4},{12,12},{1,1},{5,9},{9,5},{13,13},{2,2},{6,10},{... | collective-permute-start | bytes 49160 | tf_op jit(solution)/shard_map/ppermute | solution.py:800

commit v7 on v6

--- a/solution.py
+++ b/solution.py
@@ -275,9 +275,9 @@
     return -(-(count * (box.long + 2 * REACH)) // 8) * 8
 
 
-def pack_fields(box, wide, count, fields, *refs):
-    own, (low, high), tables = refs[:fields], refs[fields : fields + 2], refs[fields + 2 : -3]
-    up, down, table = refs[-3:]
+def pack_fields(box, wide, fields, tables, after, *refs):
+    own, (low, high), refs = refs[:fields], refs[fields : fields + 2], refs[fields + 2 :]
+    parts, (first, second, *table) = refs[:tables], refs[tables + after :]
     size = wide * box.across
     flat = [field.reshape(box.long * box.across, box.deep) for field in own]
     low = low.reshape(low.size // box.deep, box.deep)
@@ -286,16 +286,16 @@
         Sides("wide", *(ref.at[index * size : (index + 1) * size] for ref in (low, high)))
         for index in range(fields)
     ]
-    pack_columns(box, flat, sides, wide, up, down)
-    known = merged(*(ref[ref.shape[0] - count :, :] for ref in tables))
-    table[...] = known
-    up[up.shape[0] - count :, :] = known
-    down[down.shape[0] - count :, :] = known
-
-
-def bring_in(
-    box, zone, scale, load, own_zone, own_scale, own_load, load_first, load_second, first, second,
-    staged, sems
+    pack_columns(box, flat, sides, wide, first, second)
+    if tables:
+        known = last_rows_merged(parts, table[0].shape[0])
+        table[0][...] = known
+        first[first.shape[0] - known.shape[0] :, :] = known
+        second[second.shape[0] - known.shape[0] :, :] = known
+
+
+def bring_edges(
+    box, zone, scale, load, own_load, load_first, load_second, first, second, staged, sems
 ):
     even = is_even("wide")
 
@@ -311,8 +311,6 @@
         (scale.at[edges(REACH)[0]], first.at[:REACH]),
         (scale.at[edges(REACH)[1]], second.at[:REACH]),
         (load, own_load),
-        (scale, own_scale),
-        (zone, own_zone),
     ]
     copies = [
         pltpu.make_async_copy(source, target, sems.at[index])
@@ -388,11 +386,8 @@
     return table
 
 
-def merge(table, low, high, out):
-    count = table.shape[0]
-    out[...] = merged(
-        table[...], low[low.shape[0] - count :, :], high[high.shape[0] - count :, :]
-    )
+def last_rows_merged(refs, count):
+    return merged(*(ref[ref.shape[0] - count :, :] for ref in refs))
 
 
 def line_of(numbers, shape):
@@ -403,7 +398,21 @@
     return line
 
 
-def box_sums(box, zone, scale, load, diffusivity, decay, out, table):
+def box_sums(
+    box, far_zone, far_scale, load, after, diffusivity, decay, zone, scale, out, table, sems
+):
+    del after
+    parts = 2
+    size = box.long // parts
+    copies = []
+    for part in range(parts):
+        rows = slice(part * size, (part + 1) * size)
+        for index, (source, target) in enumerate(((far_zone, zone), (far_scale, scale))):
+            copy = pltpu.make_async_copy(
+                source.at[rows], target.at[rows], sems.at[2 * part + index]
+            )
+            copy.start()
+            copies.append(copy)
     step = 4
     nothing = jnp.zeros((box.across, box.deep), jnp.float32)
     half = [[0.5 * diffusivity[z, d] for z in range(3)] for d in range(3)]
@@ -419,7 +428,12 @@
             sums = [total + more for total, more in zip(sums, halves(row) + [load[row]])]
         return sums
 
-    sums = lax.fori_loop(0, box.long // step, some_rows, [nothing] * 5)
+    sums = [nothing] * 5
+    for part in range(parts):
+        for copy in copies[2 * part : 2 * part + 2]:
+            copy.wait()
+        per_part = size // step
+        sums = lax.fori_loop(part * per_part, (part + 1) * per_part, some_rows, sums)
 
     def total(values):
         return jnp.sum(values, keepdims=True).reshape(1, 1)
@@ -575,9 +589,7 @@
         (FLOW_ACROSS_HIGH, flows[2] * as_float(across_pos < across_count - 1)),
         (FLOW_ACROSS_LOW, flows[3] * as_float(across_pos > 0)),
     ]
-    count = out.shape[0]
-    known = merged(table[...], left[left.shape[0] - count :, :], right[right.shape[0] - count :, :])
-    known = known + at_own_row(line_of(numbers, (8, known.shape[1])), known.shape)
+    known = table[...] + at_own_row(line_of(numbers, (8, out.shape[1])), out.shape)
     out[...] = known
     edge = REACH * box.across
     even = is_even("wide")
@@ -590,10 +602,9 @@
     return values[:, index : index + 1]
 
 
-def coarse_inverse(told, inverse, work):
+def coarse_inverse(numbers, work):
     count, width = work.shape
     across = lax.axis_size("narrow")
-    numbers = told[...]
     beyond = pltpu.roll(numbers, count - across, 0)
     beside = pltpu.roll(numbers, count - 1, 0)
     before = pltpu.roll(numbers, across, 0)
@@ -619,6 +630,12 @@
     for shift, coupling in zip((across, -across, 1, -1), couplings):
         matrix = matrix - jnp.where((cols == rows + shift) & (cols < count), coupling, blank)
     matrix = jnp.where(cols == rows + count, jnp.ones((count, 1), jnp.float32), matrix)
+    if count <= 16:
+        for step in range(count):
+            pivot_row = matrix[step : step + 1, :] / matrix[step : step + 1, step : step + 1]
+            rest = matrix - matrix[:, step : step + 1] * pivot_row
+            matrix = jnp.where(rows == step, pivot_row, rest)
+        return pltpu.roll(matrix, width - count, 1)
     work[...] = matrix
 
     def eliminate(step, _):
@@ -634,13 +651,12 @@
     lax.fori_loop(0, count, eliminate, 0)
     values = work[...]
     if count % 128:
-        inverse[...] = pltpu.roll(values, width - count, 1)[:, : inverse.shape[1]]
-    else:
-        inverse[...] = values[:, count : 2 * count]
+        return pltpu.roll(values, width - count, 1)
+    return values[:, count : 2 * count]
 
 
 def answer(inverse, sums):
-    return jnp.sum(inverse[...] * sums, axis=0, keepdims=True)
+    return jnp.sum(inverse * sums, axis=0, keepdims=True)
 
 
 def at_box(values, row_side, col_side):
@@ -657,12 +673,30 @@
     return jnp.sum(jnp.where(wanted, values, jnp.zeros_like(values)), axis=1, keepdims=True)
 
 
-def second_solve(box, local, low, high, left, right, inverse, told, means, *rest):
+def coarse_corrections(box, numbers, work):
+    count = numbers.shape[0]
+    across_count = lax.axis_size("narrow")
+    inverse = coarse_inverse(numbers, work)
+    sums = column(numbers, IMAGE_SUM)
+    sums = sums - column(pltpu.roll(numbers, count - across_count, 0), FLOW_LONG_LOW)
+    sums = sums - column(pltpu.roll(numbers, across_count, 0), FLOW_LONG_HIGH)
+    sums = sums - column(pltpu.roll(numbers, count - 1, 0), FLOW_ACROSS_LOW)
+    sums = sums - column(pltpu.roll(numbers, 1, 0), FLOW_ACROSS_HIGH)
+    load_sums = column(numbers, LOAD_SUM)
+    sums = load_sums * (1.0 - 1.0 / cheb_center) - sums
+    return answer(inverse, load_sums) * (1.0 / cheb_center), answer(inverse, sums) * gain
+
+
+def second_solve(box, parts, local, low, high, left, right, means, *rest):
+    table_parts, rest = rest[:parts], rest[parts:]
     to_long, to_across, to_deep, mass, load_window = rest[:5]
     tables = rest[5 : 5 + N_TABLES]
-    iterate, window, residual, spectral, middle = rest[5 + N_TABLES :]
+    iterate, top, bottom, last_col, first_col = rest[5 + N_TABLES : 10 + N_TABLES]
+    window, residual, spectral, middle, work = rest[10 + N_TABLES :]
     long_pos, across_pos, long_count, across_count = position()
-    coarse = answer(inverse, column(told, LOAD_SUM)) * (1.0 / cheb_center)
+    numbers = last_rows_merged(table_parts, work.shape[0])
+    coarse, second_coarse = coarse_corrections(box, numbers, work)
+    own_shift = at_box(second_coarse, 0, 0)
     shifts = {
         (row_side, col_side): at_box(coarse, row_side, col_side)
         for row_side in (-1, 0, 1)
@@ -705,33 +739,17 @@
     def emit(start, values):
         rows = values.reshape(8, box.across, box.deep)
         before = window[first + start : first + start + 8, inner, :]
-        iterate[start : start + 8] = keep * before + gain * rows
+        shift = own_shift.reshape(1, 1, 1)
+        iterate[start : start + 8] = keep * before + (gain * rows + shift)
 
     box_solve(
         box, residual, means_of(means), tables, row_mask, col_mask, spectral, middle, emit
     )
-
-
-def correct_faces(
-    box, partial, inverse, table, more, shift, top, bottom, last_col, first_col
-):
-    count = table.shape[0]
-    across_count = lax.axis_size("narrow")
-    numbers = merged(table[...], more[...])
-    sums = column(numbers, IMAGE_SUM)
-    sums = sums - column(pltpu.roll(numbers, count - across_count, 0), FLOW_LONG_LOW)
-    sums = sums - column(pltpu.roll(numbers, across_count, 0), FLOW_LONG_HIGH)
-    sums = sums - column(pltpu.roll(numbers, count - 1, 0), FLOW_ACROSS_LOW)
-    sums = sums - column(pltpu.roll(numbers, 1, 0), FLOW_ACROSS_HIGH)
-    sums = column(numbers, LOAD_SUM) * (1.0 - 1.0 / cheb_center) - sums
-    own = at_box(answer(inverse, sums) * gain, 0, 0)
-    shift[...] = jnp.broadcast_to(own, shift.shape)
-    rows = in_order(is_even("wide"), partial[box.long - 1], partial[0])
-    top[...], bottom[...] = rows[0] + own, rows[1] + own
-    flat = partial.reshape(box.long * box.across, box.deep)
+    rows = in_order(is_even("wide"), iterate[box.long - 1], iterate[0])
+    top[...], bottom[...] = rows
+    flat = iterate.reshape(box.long * box.across, box.deep)
     cols = [flat[row_of(box.across, col, box.long), :] for col in (box.across - 1, 0)]
-    cols = in_order(is_even("narrow"), *cols)
-    last_col[...], first_col[...] = cols[0] + own, cols[1] + own
+    last_col[...], first_col[...] = in_order(is_even("narrow"), *cols)
 
 
 def last_residual(
@@ -742,7 +760,6 @@
     high,
     left,
     right,
-    shift,
     to_long,
     to_across,
     to_deep,
@@ -758,7 +775,7 @@
     blank = jnp.zeros((box.long + 2, EDGE, box.deep), jnp.float32)
     window[:, :EDGE, :] = blank
     window[:, EDGE + box.across :, :] = blank
-    window[1 : 1 + box.long, inner, :] = partial[...] + shift[0:1, :].reshape(1, 1, box.deep)
+    window[1 : 1 + box.long, inner, :] = partial[...]
     own = pltpu.make_async_copy(window.at[1 : 1 + box.long, inner, :], iterate, sems.at[0])
     own.start()
     wide_sides, narrow_sides = Sides("wide", low, high), Sides("narrow", left, right)
@@ -821,127 +838,102 @@
     by_margins = lax.axis_size("wide") == 4 and lax.axis_size("narrow") == 4
     tables = tables_of(box)
     cells = f32(long, across, deep)
+    whole_zone = jax.ShapeDtypeStruct(cells.shape, zone.dtype)
     window = f32(box.rows, box.cols, deep)
     table_shape = f32(count, 128)
+    anywhere = pl.BlockSpec(memory_space=pl.ANY)
+    in_hbm = pl.BlockSpec(memory_space=pltpu.HBM)
 
     def scratch(shape):
         return pltpu.VMEM(shape, jnp.float32)
 
+    def pinned(field):
+        return pltpu.with_memory_space_constraint(field, pltpu.HBM)
+
     spectral = scratch((box.ey, padded(box.ex), deep))
     middle = scratch((long, padded(box.ey), deep))
 
-    def pack(wide, fields, *refs):
-        message = f32(message_rows(box, wide * fields) + count, deep)
-        body = functools.partial(pack_fields, box, wide, count, fields)
-        return call(body, (message, message, table_shape), [VMEM] * len(refs))(*refs)
+    def pack(wide, fields, sides, parts=(), after=()):
+        rows = message_rows(box, wide * len(fields)) + (count if parts else 0)
+        message = f32(rows, deep)
+        body = functools.partial(pack_fields, box, wide, len(fields), len(parts), len(after))
+        return call(
+            body,
+            (message, message) + ((table_shape,) if parts else ()),
+            [VMEM] * (len(fields) + 2 + len(parts)) + [anywhere] * len(after),
+        )(*fields, *sides, *parts, *after)
 
     far = f32(2 * REACH, across, deep)
-    zone, scale, load, load_up, load_down, up, down = call(
-        functools.partial(bring_in, box),
-        (jax.ShapeDtypeStruct(cells.shape, zone.dtype), cells, cells)
-        + (f32(MARGIN, across, deep),) * 2
-        + (far, far),
-        [pl.BlockSpec(memory_space=pltpu.HBM)] * 3,
-        [pltpu.VMEM((2, REACH, across, deep), zone.dtype), pltpu.SemaphoreType.DMA((9,))],
-    )(*(pltpu.with_memory_space_constraint(field, pltpu.HBM) for field in (zone, scale, load)))
-    load_low, load_high = exchange("wide", load_up, load_down)
-    far_low, far_high = exchange("wide", up, down)
-    sums, table = call(
-        functools.partial(box_sums, box), (f32(8, 128), table_shape), [VMEM] * 3 + [SMEM] * 2
-    )(zone, scale, load, diffusivity, decay)
-    own_table = table
-    up, down, _ = pack(MARGIN, 1, load, load_low, load_high, table)
-    load_left, load_right = exchange("narrow", up, down, by_margins)
-    up, down, table = pack(REACH, 2, scale, zone, far_low, far_high, table, load_left, load_right)
-    far_left, far_right = exchange("narrow", up, down)
+    far_zone, far_scale = zone, scale
+    load, load_first, load_second, first, second = call(
+        functools.partial(bring_edges, box),
+        (cells,) + (f32(MARGIN, across, deep),) * 2 + (far, far),
+        [in_hbm] * 3,
+        [pltpu.VMEM((2, REACH, across, deep), zone.dtype), pltpu.SemaphoreType.DMA((7,))],
+    )(pinned(zone), pinned(scale), pinned(load))
+    load_wide = exchange("wide", load_first, load_second)
+    far_wide = exchange("wide", first, second)
+    load_first, load_second = pack(MARGIN, [load], load_wide)
+    load_narrow = exchange("narrow", load_first, load_second)
+    zone, scale, sums, table = call(
+        functools.partial(box_sums, box),
+        (whole_zone, cells, f32(8, 128), table_shape),
+        [in_hbm] * 2 + [VMEM, anywhere] + [SMEM] * 2,
+        [pltpu.SemaphoreType.DMA((4,))],
+    )(pinned(far_zone), pinned(far_scale), load, load_first, diffusivity, decay)
+    far_narrow = exchange("narrow", *pack(REACH, [scale, zone], far_wide))
     load_window, local = call(
         functools.partial(first_solve, box),
         (window, cells),
         [VMEM] * (6 + N_TABLES),
         [spectral, middle],
         flops=4 * 10**9,
-    )(load, load_low, load_high, load_left, load_right, sums, *tables)
+    )(load, *load_wide, *load_narrow, sums, *tables)
     message = f32(REACH * across + count, deep)
-    table, up, down = call(
+    table, first, second = call(
         functools.partial(image_sums, box), (table_shape, message, message), [VMEM] * 8 + [SMEM] * 2
-    )(zone, scale, local, far_low, far_high, far_left, far_right, table, diffusivity, decay)
-    image_table = table
-    low, high = exchange("wide", up, down)
-    to_long, to_across, to_deep, mass = call(
+    )(zone, scale, local, *far_wide, *far_narrow, table, diffusivity, decay)
+    own_table = table
+    wide = exchange("wide", first, second, by_margins)
+    parts = (table, *wide)
+    if by_margins:
+        parts += (two_away("wide", table),)
+    weights = call(
         functools.partial(weights_of, box),
         (window,) * 4,
         [VMEM] * 6 + [SMEM] * 2,
         [scratch(window.shape)] * 2,
         flops=10**9,
-    )(zone, scale, far_low, far_high, far_left, far_right, diffusivity, decay)
-    joined = functools.partial(call, merge, table_shape, [VMEM] * 3)
+    )(zone, scale, *far_wide, *far_narrow, diffusivity, decay)
+    first, second, table = pack(REACH, [local], wide, parts, weights[3:])
+    narrow = exchange("narrow", first, second, by_margins)
     if by_margins:
-        table = joined()(table, low, high)
-        more = two_away("wide", table)
-        up, down, table = pack(REACH, 1, local, low, high, table, more)
-        load_table = table
+        parts = (table, *narrow, two_away("narrow", table))
     else:
-        up, down, _ = pack(REACH, 1, local, low, high, table)
-        load_table = tell(own_table)
-    left, right = exchange("narrow", up, down)
-    inverse = call(
-        coarse_inverse,
-        f32(count, -(-count // 128) * 128),
-        [VMEM],
-        [scratch((count, -(-2 * count // 128) * 128))],
-    )(load_table)
-    if by_margins:
-        table = joined()(table, left, right)
-        more = two_away("narrow", table)
-    else:
-        table = more = tell(image_table)
+        parts = (tell(own_table),)
     row, col = f32(across, deep), f32(long, deep)
-    partial = call(
-        functools.partial(second_solve, box),
-        cells,
-        [VMEM] * (13 + N_TABLES),
-        [scratch(window.shape), scratch((box.ex, box.cols, deep)), spectral, middle],
+    iterate, first_row, second_row, first_col, second_col = call(
+        functools.partial(second_solve, box, len(parts)),
+        (cells, row, row, col, col),
+        [VMEM] * (11 + len(parts) + N_TABLES),
+        [
+            scratch(window.shape),
+            scratch((box.ex, box.cols, deep)),
+            spectral,
+            middle,
+            scratch((count, -(-2 * count // 128) * 128)),
+        ],
         flops=4 * 10**9,
-    )(
-        local,
-        low,
-        high,
-        left,
-        right,
-        inverse,
-        load_table,
-        sums,
-        to_long,
-        to_across,
-        to_deep,
-        mass,
-        load_window,
-        *tables,
-    )
-    shift, top, bottom, last_col, first_col = call(
-        functools.partial(correct_faces, box), (f32(8, deep), row, row, col, col), [VMEM] * 4
-    )(partial, inverse, table, more)
-    left, right = exchange("narrow", last_col, first_col)
-    low, high = exchange("wide", top, bottom)
+    )(local, *wide, *narrow, sums, *parts, *weights, load_window, *tables)
+    narrow = exchange("narrow", first_col, second_col)
+    wide = exchange("wide", first_row, second_row)
     return call(
         functools.partial(last_residual, box),
         (cells, cells),
-        [VMEM] * 11,
+        [VMEM] * 10,
         [scratch((long + 2, box.cols, deep)), scratch(cells.shape), pltpu.SemaphoreType.DMA((5,))],
-        out_spec=pl.BlockSpec(memory_space=pl.ANY),
-    )(
-        load,
-        partial,
-        low,
-        high,
-        left,
-        right,
-        shift,
-        to_long,
-        to_across,
-        to_deep,
-        mass,
-    )
+        out_spec=anywhere,
+    )(load, iterate, *wide, *narrow, *weights)
 
 
 def solution(mesh):

time: 73.9 us -> 69.2 us (0.936)
  the two profiles are of different devices: /device:TPU:13 before, /device:TPU:10 now
where the time goes in v7:
time: 69.2 us; the launch traced here: 68.9 us
  Pallas kernels  32.1 us (46%)
  starting transfers between devices  24.9 us (36%)
  waiting for transfers between devices  10.7 us (15%)
  between operations  1.16 us (2%)
    ppermute x8, starting transfers between devices, exchange(): lax.ppermute(second, axis, swaps[1])  17.2 us
    pallas_call x1, Pallas kernels, on_device(): call(functools.partial(second_solve, box, len(parts)), (cells, row, row,...  11.6 us
    pallas_call x1, Pallas kernels, on_device(): call(functools.partial(first_solve, box), (window, cells), [VMEM] * (6 +...  6.73 us
    ppermute x8, starting transfers between devices, exchange(): lax.ppermute(first, axis, swaps[0])  5.85 us
    ppermute x2, waiting for transfers between devices, two_away(): return lax.ppermute(table, axis, [(i, (i + 2) % size) for i in range(size)])  5.39 us
    ppermute x8, waiting for transfers between devices, exchange(): lax.ppermute(second, axis, swaps[1])  4.86 us
    pallas_call x1, Pallas kernels, on_device(): call(functools.partial(weights_of, box), (window,) * 4, [VMEM] * 6 + [SME...  3.7 us
    pallas_call x1, Pallas kernels, on_device(): call(functools.partial(last_residual, box), (cells, cells), [VMEM] * 10,...  3.43 us
  transfers between devices with their start and end apart: 18, of which 6 were waited for; matrix products, arithmetic and copies ran while one was open for 0% of the time, Pallas kernels for 20%

profile of v7, /device:TPU:10, one launch (start us, length us, event | category | flops | bytes accessed | tf_op | source)
XLA Modules:
  0.0 68.9 jit_solution(1948384723088784320)
XLA Ops:
  0.7 1.5 %shard_map.149 = (f32[64,32,128]{2,1,0:T(8,128)S(1)}, f32[4,32,128]{2,1,0:T(8,128)S(1)}, f32[4,32,128]{2,1,0:T(8,128)S(1)}, f32[10,32,128]{2,1,0:T(8,128)S(1)}, f32[10,32,128]{2,1,0:T(8,128)S(1)}) custom-call(s32[64,32,128]{2,1,0:T(8,128)} %far_zone.1, f32[64,32,128]{2,1,0:T(8,128)} %far_scale.1, f32[64,32,128]{2,1,0:T(8,128)} %load.1), custom_call_target="tpu_custom_call" | custom-call | tf_op jit(solution)/shard_map/pallas_call | solution.py:868
  2.2 0.5 collective-permute-start
  2.7 4.6 %collective-permute-start.1 = (f32[4,32,128]{2,1,0:T(8,128)S(1)}, f32[4,32,128]{2,1,0:T(8,128)S(1)}, u32[]{:S(2)}, u32[]{:S(2)}) collective-permute-start(f32[4,32,128]{2,1,0:T(8,128)S(1)} %get-tuple-element.34), channel_id=1, source_target_pairs={{0,0},{4,8},{8,4},{12,12},{1,1},{5,9},{9,5},{13,13},{2,2},{6,10},{... | collective-permute-start | bytes 196616 | tf_op jit(solution)/shard_map/ppermute | solution.py:817
  7.3 0.1 collective-permute-start.4
  7.4 1.9 %collective-permute-start.5 = (f32[10,32,128]{2,1,0:T(8,128)S(1)}, f32[10,32,128]{2,1,0:T(8,128)S(1)}, u32[]{:S(2)}, u32[]{:S(2)}) collective-permute-start(f32[10,32,128]{2,1,0:T(8,128)S(1)} %get-tuple-element.42), channel_id=1, source_target_pairs={{0,0},{4,8},{8,4},{12,12},{1,1},{5,9},{9,5},{13,13},{2,2},{6,10},{... | collective-permute-start | bytes 491528 | tf_op jit(solution)/shard_map/ppermute | solution.py:817
  9.3 0.2 collective-permute-done.1.refs_2_.high
  9.5 0.2 shard_map.150
  9.7 1.9 %collective-permute-start.3 = (f32[296,128]{1,0:T(8,128)S(1)}, f32[296,128]{1,0:T(8,128)S(1)}, u32[]{:S(2)}, u32[]{:S(2)}) collective-permute-start(f32[296,128]{1,0:T(8,128)S(1)} %get-tuple-element.36), channel_id=1, source_target_pairs={{0,0},{1,2},{2,1},{3,3},{4,4},{5,6},{6,5},{7,7},{8,8},{9,10},{10,9... | collective-permute-start | bytes 454664 | tf_op jit(solution)/shard_map/ppermute | solution.py:817
  11.7 0.1 collective-permute-start.2
  11.8 2.7 %shard_map.151 = (s32[64,32,128]{2,1,0:T(8,128)S(1)}, f32[64,32,128]{2,1,0:T(8,128)S(1)}, f32[8,128]{1,0:T(8,128)S(1)}, f32[16,128]{1,0:T(8,128)S(1)}) custom-call(s32[64,32,128]{2,1,0:T(8,128)} %far_zone.1, f32[64,32,128]{2,1,0:T(8,128)} %far_scale.1, f32[64,32,128]{2,1,0:T(8,128)S(1)} %get-tuple-element.32.refs_0_.load, ...), custom_call_target="tpu_custom_call" | custom-call | tf_op jit(solution)/shard_map/pallas_call | solution.py:878
  14.6 0.1 collective-permute-done.5.refs_3_.high
  14.7 0.4 shard_map.153
  15.1 0.5 collective-permute-start.6
  15.6 3.6 %collective-permute-start.7 = (f32[744,128]{1,0:T(8,128)S(1)}, f32[744,128]{1,0:T(8,128)S(1)}, u32[]{:S(2)}, u32[]{:S(2)}) collective-permute-start(f32[744,128]{1,0:T(8,128)S(1)} %get-tuple-element.44), channel_id=1, source_target_pairs={{0,0},{1,2},{2,1},{3,3},{4,4},{5,6},{6,5},{7,7},{8,8},{9,10},{10,9... | collective-permute-start | bytes 1142792 | tf_op jit(solution)/shard_map/ppermute | solution.py:817
  19.3 6.7 %shard_map.152 = (f32[74,48,128]{2,1,0:T(8,128)S(1)}, f32[64,32,128]{2,1,0:T(8,128)S(1)}) custom-call(f32[64,32,128]{2,1,0:T(8,128)S(1)} %get-tuple-element.32.refs_0_.load, f32[4,32,128]{2,1,0:T(8,128)S(1)} %collective-permute-done.refs_1_.low, f32[4,32,128]{2,1,0:T(8,128)S(1)} %collective-permute-done.1.refs_2_.high, ...), custom_call_target="tpu_custom_call" | custom-call | flops 4000000000 | tf_op jit(solution)/shard_map/pallas_call | solution.py:885
  26.1 1.6 %shard_map.154 = (f32[16,128]{1,0:T(8,128)S(1)}, f32[176,128]{1,0:T(8,128)S(1)}, f32[176,128]{1,0:T(8,128)S(1)}) custom-call(s32[64,32,128]{2,1,0:T(8,128)S(1)} %get-tuple-element.39.refs_1_.zone, f32[64,32,128]{2,1,0:T(8,128)S(1)} %get-tuple-element.40.refs_0_.scale, f32[64,32,128]{2,1,0:T(8,128)S(1)} %get-tuple-element.38.local.refs_0_, ...), custom_call_target="tpu_custom_call" | custom-call | tf_op jit(solution)/shard_map/pallas_call | solution.py:893
  27.6 0.1 collective-permute-start.10
  27.7 3.6 %collective-permute-start.8 = (f32[176,128]{1,0:T(8,128)S(1)}, f32[176,128]{1,0:T(8,128)S(1)}, u32[]{:S(2)}, u32[]{:S(2)}) collective-permute-start(f32[176,128]{1,0:T(8,128)S(1)} %get-tuple-element.46), channel_id=1, source_target_pairs={{0,4},{4,0},{8,12},{12,8},{1,5},{5,1},{9,13},{13,9},{2,6},{6,2},{1... | collective-permute-start | bytes 270344 | tf_op jit(solution)/shard_map/ppermute | solution.py:817
  31.3 3.7 %shard_map.155 = (f32[74,48,128]{2,1,0:T(8,128)S(1)}, f32[74,48,128]{2,1,0:T(8,128)S(1)}, f32[74,48,128]{2,1,0:T(8,128)S(1)}, f32[74,48,128]{2,1,0:T(8,128)S(1)}) custom-call(s32[64,32,128]{2,1,0:T(8,128)S(1)} %get-tuple-element.39.refs_1_.zone, f32[64,32,128]{2,1,0:T(8,128)S(1)} %get-tuple-element.40.refs_0_.scale, ...), custom_call_target="tpu_custom_call" | custom-call | flops 1000000000 | tf_op jit(solution)/shard_map/pallas_call | solution.py:901
  35.1 1.8 %collective-permute-done.9.refs_2_.refs_5_.high = f32[176,128]{1,0:T(8,128)S(1)} collective-permute-done((f32[176,128]{1,0:T(8,128)S(1)}, f32[176,128]{1,0:T(8,128)S(1)}, u32[]{:S(2)}, u32[]{:S(2)}) %collective-permute-start.9) | collective-permute-done | bytes 90144 | tf_op jit(solution)/shard_map/ppermute | solution.py:817
  36.8 0.2 shard_map.156
  37.1 0.1 collective-permute-start.11
  37.1 0.4 collective-permute-start.12
  37.5 1.8 %collective-permute-start.13 = (f32[16,128]{1,0:T(8,128)S(1)}, f32[16,128]{1,0:T(8,128)S(1)}, u32[]{:S(2)}, u32[]{:S(2)}) collective-permute-start(f32[16,128]{1,0:T(8,128)S(1)} %get-tuple-element.52.rest_0_), channel_id=1, source_target_pairs={{0,2},{1,3},{2,0},{3,1},{4,6},{5,7},{6,4},{7,5},{8,10},{9,11},{10,... | collective-permute-start | bytes 24584 | tf_op jit(solution)/shard_map/ppermute | solution.py:822
  39.3 5.4 %collective-permute-done.13.rest_3_ = f32[16,128]{1,0:T(8,128)S(1)} collective-permute-done((f32[16,128]{1,0:T(8,128)S(1)}, f32[16,128]{1,0:T(8,128)S(1)}, u32[]{:S(2)}, u32[]{:S(2)}) %collective-permute-start.13) | collective-permute-done | bytes 8224 | tf_op jit(solution)/shard_map/ppermute | solution.py:822
  44.7 11.6 %shard_map.157 = (f32[64,32,128]{2,1,0:T(8,128)S(1)}, f32[32,128]{1,0:T(8,128)S(1)}, f32[32,128]{1,0:T(8,128)S(1)}, f32[64,128]{1,0:T(8,128)S(1)}, f32[64,128]{1,0:T(8,128)S(1)}) custom-call(f32[64,32,128]{2,1,0:T(8,128)S(1)} %get-tuple-element.38.local.refs_0_, f32[176,128]{1,0:T(8,128)S(1)} %collective-permute-done.8.refs_1_.refs_4_.low, ...), custom_call_target="tpu_custom_call" | custom-call | flops 4000000000 | tf_op jit(solution)/shard_map/pallas_call | solution.py:915
  56.4 2.4 %collective-permute-start.17 = (f32[64,128]{1,0:T(8,128)S(1)}, f32[64,128]{1,0:T(8,128)S(1)}, u32[]{:S(2)}, u32[]{:S(2)}) collective-permute-start(f32[64,128]{1,0:T(8,128)S(1)} %get-tuple-element.61), channel_id=1, source_target_pairs={{0,0},{1,2},{2,1},{3,3},{4,4},{5,6},{6,5},{7,7},{8,8},{9,10},{10,9... | collective-permute-start | bytes 98312 | tf_op jit(solution)/shard_map/ppermute | solution.py:817
  58.8 1.0 %collective-permute-start.14 = (f32[32,128]{1,0:T(8,128)S(1)}, f32[32,128]{1,0:T(8,128)S(1)}, u32[]{:S(2)}, u32[]{:S(2)}) collective-permute-start(f32[32,128]{1,0:T(8,128)S(1)} %get-tuple-element.58), channel_id=1, source_target_pairs={{0,4},{4,0},{8,12},{12,8},{1,5},{5,1},{9,13},{13,9},{2,6},{6,2},{1... | collective-permute-start | bytes 49160 | tf_op jit(solution)/shard_map/ppermute | solution.py:817
  59.7 2.4 %collective-permute-start.15 = (f32[32,128]{1,0:T(8,128)S(1)}, f32[32,128]{1,0:T(8,128)S(1)}, u32[]{:S(2)}, u32[]{:S(2)}) collective-permute-start(f32[32,128]{1,0:T(8,128)S(1)} %get-tuple-element.59), channel_id=1, source_target_pairs={{0,0},{4,8},{8,4},{12,12},{1,1},{5,9},{9,5},{13,13},{2,2},{6,10},{... | collective-permute-start | bytes 49160 | tf_op jit(solution)/shard_map/ppermute | solution.py:817
  62.1 0.4 collective-permute-done.14.low
  62.6 2.8 %collective-permute-done.15.high = f32[32,128]{1,0:T(8,128)S(1)} collective-permute-done((f32[32,128]{1,0:T(8,128)S(1)}, f32[32,128]{1,0:T(8,128)S(1)}, u32[]{:S(2)}, u32[]{:S(2)}) %collective-permute-start.15) | collective-permute-done | bytes 16416 | tf_op jit(solution)/shard_map/ppermute | solution.py:817
  65.3 3.4 %shard_map.158 = (f32[64,32,128]{2,1,0:T(8,128)}, f32[64,32,128]{2,1,0:T(8,128)}) custom-call(f32[64,32,128]{2,1,0:T(8,128)S(1)} %get-tuple-element.32.refs_0_.load, f32[64,32,128]{2,1,0:T(8,128)S(1)} %get-tuple-element.57.partial, f32[32,128]{1,0:T(8,128)S(1)} %collective-permute-done.14.low, f32[32,128]{1,0:T(8,128)S(1)} %collective-permute-done.15.high, ...), custom_call_target="tpu_custom_call" | custom-call | tf_op jit(solution)/shard_map/pallas_call | solution.py:930
  (36 shorter events, 0.2 us)
Async XLA Ops:
  0.6 11.1 %copy-start.1 = (f32[3]{0:T(128)S(1)}, f32[3]{0:T(128)}, u32[]{:S(2)}) copy-start(f32[3]{0:T(128)} %decay.5) | copy-start | bytes 40
  0.6 11.1 %copy-start = (f32[3,3]{1,0:T(4,128)S(1)}, f32[3,3]{1,0:T(4,128)}, u32[]{:S(2)}) copy-start(f32[3,3]{1,0:T(4,128)} %diffusivity.5) | copy-start | bytes 112
  2.2 7.1 %collective-permute-start = (f32[4,32,128]{2,1,0:T(8,128)S(1)}, f32[4,32,128]{2,1,0:T(8,128)S(1)}, u32[]{:S(2)}, u32[]{:S(2)}) collective-permute-start(f32[4,32,128]{2,1,0:T(8,128)S(1)} %get-tuple-element.33), channel_id=1, source_target_pairs={{0,4},{4,0},{8,12},{12,8},{1,5},{5,1},{9,13},{13,9},{2,6},{6,2},{1... | collective-permute-start | bytes 196616 | tf_op jit(solution)/shard_map/ppermute | solution.py:817
  2.7 6.8 %collective-permute-start.1 = (f32[4,32,128]{2,1,0:T(8,128)S(1)}, f32[4,32,128]{2,1,0:T(8,128)S(1)}, u32[]{:S(2)}, u32[]{:S(2)}) collective-permute-start(f32[4,32,128]{2,1,0:T(8,128)S(1)} %get-tuple-element.34), channel_id=1, source_target_pairs={{0,0},{4,8},{8,4},{12,12},{1,1},{5,9},{9,5},{13,13},{2,2},{6,10},{... | collective-permute-start | bytes 196616 | tf_op jit(solution)/shard_map/ppermute | solution.py:817
  7.3 7.2 %collective-permute-start.4 = (f32[10,32,128]{2,1,0:T(8,128)S(1)}, f32[10,32,128]{2,1,0:T(8,128)S(1)}, u32[]{:S(2)}, u32[]{:S(2)}) collective-permute-start(f32[10,32,128]{2,1,0:T(8,128)S(1)} %get-tuple-element.41), channel_id=1, source_target_pairs={{0,4},{4,0},{8,12},{12,8},{1,5},{5,1},{9,13},{13,9},{2,6},{6,2},{1... | collective-permute-start | bytes 491528 | tf_op jit(solution)/shard_map/ppermute | solution.py:817
  7.4 7.3 %collective-permute-start.5 = (f32[10,32,128]{2,1,0:T(8,128)S(1)}, f32[10,32,128]{2,1,0:T(8,128)S(1)}, u32[]{:S(2)}, u32[]{:S(2)}) collective-permute-start(f32[10,32,128]{2,1,0:T(8,128)S(1)} %get-tuple-element.42), channel_id=1, source_target_pairs={{0,0},{4,8},{8,4},{12,12},{1,1},{5,9},{9,5},{13,13},{2,2},{6,10},{... | collective-permute-start | bytes 491528 | tf_op jit(solution)/shard_map/ppermute | solution.py:817
  9.7 9.5 %collective-permute-start.3 = (f32[296,128]{1,0:T(8,128)S(1)}, f32[296,128]{1,0:T(8,128)S(1)}, u32[]{:S(2)}, u32[]{:S(2)}) collective-permute-start(f32[296,128]{1,0:T(8,128)S(1)} %get-tuple-element.36), channel_id=1, source_target_pairs={{0,0},{1,2},{2,1},{3,3},{4,4},{5,6},{6,5},{7,7},{8,8},{9,10},{10,9... | collective-permute-start | bytes 454664 | tf_op jit(solution)/shard_map/ppermute | solution.py:817
  11.7 7.6 %collective-permute-start.2 = (f32[296,128]{1,0:T(8,128)S(1)}, f32[296,128]{1,0:T(8,128)S(1)}, u32[]{:S(2)}, u32[]{:S(2)}) collective-permute-start(f32[296,128]{1,0:T(8,128)S(1)} %get-tuple-element.35.after), channel_id=1, source_target_pairs={{0,1},{1,0},{2,3},{3,2},{4,5},{5,4},{6,7},{7,6},{8,9},{9,8},{10,11... | collective-permute-start | bytes 454664 | tf_op jit(solution)/shard_map/ppermute | solution.py:817
  14.4 4.8 %copy-start.2 = (bf16[256,256]{1,0:T(8,128)(2,1)S(1)}, bf16[256,256]{1,0:T(8,128)(2,1)}, u32[]{:S(2)}) copy-start(bf16[256,256]{1,0:T(8,128)(2,1)} %constant.22.clone.rest_4_.rest_13_) | copy-start | bytes 393220
  14.5 4.8 %copy-start.3 = (bf16[192,240]{1,0:T(8,128)(2,1)S(1)}, bf16[192,240]{1,0:T(8,128)(2,1)}, u32[]{:S(2)}) copy-start(bf16[192,240]{1,0:T(8,128)(2,1)} %constant.20.clone.rest_2_.rest_11_) | copy-start | bytes 276484
  14.5 4.8 %copy-start.4 = (bf16[144,160]{1,0:T(8,128)(2,1)S(1)}, bf16[144,160]{1,0:T(8,128)(2,1)}, u32[]{:S(2)}) copy-start(bf16[144,160]{1,0:T(8,128)(2,1)} %constant.19.clone.rest_1_.rest_10_) | copy-start | bytes 138244
  14.5 4.8 %copy-start.5 = (bf16[256,128]{1,0:T(8,128)(2,1)S(1)}, bf16[256,128]{1,0:T(8,128)(2,1)}, u32[]{:S(2)}) copy-start(bf16[256,128]{1,0:T(8,128)(2,1)} %constant.23.clone.rest_5_.rest_14_) | copy-start | bytes 196612
  14.5 4.8 %copy-start.6 = (bf16[96,144]{1,0:T(8,128)(2,1)S(1)}, bf16[96,144]{1,0:T(8,128)(2,1)}, u32[]{:S(2)}) copy-start(bf16[96,144]{1,0:T(8,128)(2,1)} %constant.21.clone.rest_3_.rest_12_) | copy-start | bytes 82948
  14.5 4.8 %copy-start.7 = (f32[72,128]{1,0:T(8,128)S(1)}, f32[72,128]{1,0:T(8,128)}, u32[]{:S(2)}) copy-start(f32[72,128]{1,0:T(8,128)} %constant.24.clone.rest_6_.rest_15_) | copy-start | bytes 110596
  14.5 4.8 %copy-start.8 = (bf16[80,96]{1,0:T(8,128)(2,1)S(1)}, bf16[80,96]{1,0:T(8,128)(2,1)}, u32[]{:S(2)}) copy-start(bf16[80,96]{1,0:T(8,128)(2,1)} %constant.18.clone.rest_0_.rest_9_) | copy-start | bytes 46084
  14.5 4.8 %copy-start.9 = (f32[1,40]{1,0:T(1,128)S(1)}, f32[1,40]{1,0:T(1,128)}, u32[]{:S(2)}) copy-start(f32[1,40]{1,0:T(1,128)} %constant.26.clone.rest_8_.rest_17_) | copy-start | bytes 484
  14.5 4.8 %copy-start.10 = (f32[1,128]{1,0:T(1,128)S(1)}, f32[1,128]{1,0:T(1,128)}, u32[]{:S(2)}) copy-start(f32[1,128]{1,0:T(1,128)} %constant.25.clone.rest_7_.rest_16_) | copy-start | bytes 1540
  15.1 10.9 %collective-permute-start.6 = (f32[744,128]{1,0:T(8,128)S(1)}, f32[744,128]{1,0:T(8,128)S(1)}, u32[]{:S(2)}, u32[]{:S(2)}) collective-permute-start(f32[744,128]{1,0:T(8,128)S(1)} %get-tuple-element.43), channel_id=1, source_target_pairs={{0,1},{1,0},{2,3},{3,2},{4,5},{5,4},{6,7},{7,6},{8,9},{9,8},{10,11... | collective-permute-start | bytes 1142792 | tf_op jit(solution)/shard_map/ppermute | solution.py:817
  15.6 10.5 %collective-permute-start.7 = (f32[744,128]{1,0:T(8,128)S(1)}, f32[744,128]{1,0:T(8,128)S(1)}, u32[]{:S(2)}, u32[]{:S(2)}) collective-permute-start(f32[744,128]{1,0:T(8,128)S(1)} %get-tuple-element.44), channel_id=1, source_target_pairs={{0,0},{1,2},{2,1},{3,3},{4,4},{5,6},{6,5},{7,7},{8,8},{9,10},{10,9... | collective-permute-start | bytes 1142792 | tf_op jit(solution)/shard_map/ppermute | solution.py:817
  27.6 7.4 %collective-permute-start.10 = (f32[16,128]{1,0:T(8,128)S(1)}, f32[16,128]{1,0:T(8,128)S(1)}, u32[]{:S(2)}, u32[]{:S(2)}) collective-permute-start(f32[16,128]{1,0:T(8,128)S(1)} %get-tuple-element.48.refs_3_), channel_id=1, source_target_pairs={{0,8},{4,12},{8,0},{12,4},{1,9},{5,13},{9,1},{13,5},{2,10},{6,14},... | collective-permute-start | bytes 24584 | tf_op jit(solution)/shard_map/ppermute | solution.py:822
  27.7 7.4 %collective-permute-start.8 = (f32[176,128]{1,0:T(8,128)S(1)}, f32[176,128]{1,0:T(8,128)S(1)}, u32[]{:S(2)}, u32[]{:S(2)}) collective-permute-start(f32[176,128]{1,0:T(8,128)S(1)} %get-tuple-element.46), channel_id=1, source_target_pairs={{0,4},{4,0},{8,12},{12,8},{1,5},{5,1},{9,13},{13,9},{2,6},{6,2},{1... | collective-permute-start | bytes 270344 | tf_op jit(solution)/shard_map/ppermute | solution.py:817
  31.3 5.5 %collective-permute-start.9 = (f32[176,128]{1,0:T(8,128)S(1)}, f32[176,128]{1,0:T(8,128)S(1)}, u32[]{:S(2)}, u32[]{:S(2)}) collective-permute-start(f32[176,128]{1,0:T(8,128)S(1)} %get-tuple-element.47), channel_id=1, source_target_pairs={{0,12},{4,8},{8,4},{12,0},{1,13},{5,9},{9,5},{13,1},{2,14},{6,10},... | collective-permute-start | bytes 270344 | tf_op jit(solution)/shard_map/ppermute | solution.py:817
  37.1 7.6 %collective-permute-start.11 = (f32[392,128]{1,0:T(8,128)S(1)}, f32[392,128]{1,0:T(8,128)S(1)}, u32[]{:S(2)}, u32[]{:S(2)}) collective-permute-start(f32[392,128]{1,0:T(8,128)S(1)} %get-tuple-element.50), channel_id=1, source_target_pairs={{0,1},{1,0},{2,3},{3,2},{4,5},{5,4},{6,7},{7,6},{8,9},{9,8},{10,11... | collective-permute-start | bytes 602120 | tf_op jit(solution)/shard_map/ppermute | solution.py:817
  37.1 7.5 %collective-permute-start.12 = (f32[392,128]{1,0:T(8,128)S(1)}, f32[392,128]{1,0:T(8,128)S(1)}, u32[]{:S(2)}, u32[]{:S(2)}) collective-permute-start(f32[392,128]{1,0:T(8,128)S(1)} %get-tuple-element.51), channel_id=1, source_target_pairs={{0,3},{1,2},{2,1},{3,0},{4,7},{5,6},{6,5},{7,4},{8,11},{9,10},{10,... | collective-permute-start | bytes 602120 | tf_op jit(solution)/shard_map/ppermute | solution.py:817
  37.5 7.2 %collective-permute-start.13 = (f32[16,128]{1,0:T(8,128)S(1)}, f32[16,128]{1,0:T(8,128)S(1)}, u32[]{:S(2)}, u32[]{:S(2)}) collective-permute-start(f32[16,128]{1,0:T(8,128)S(1)} %get-tuple-element.52.rest_0_), channel_id=1, source_target_pairs={{0,2},{1,3},{2,0},{3,1},{4,6},{5,7},{6,4},{7,5},{8,10},{9,11},{10,... | collective-permute-start | bytes 24584 | tf_op jit(solution)/shard_map/ppermute | solution.py:822
  56.3 9.0 %collective-permute-start.16 = (f32[64,128]{1,0:T(8,128)S(1)}, f32[64,128]{1,0:T(8,128)S(1)}, u32[]{:S(2)}, u32[]{:S(2)}) collective-permute-start(f32[64,128]{1,0:T(8,128)S(1)} %get-tuple-element.60), channel_id=1, source_target_pairs={{0,1},{1,0},{2,3},{3,2},{4,5},{5,4},{6,7},{7,6},{8,9},{9,8},{10,11... | collective-permute-start | bytes 98312 | tf_op jit(solution)/shard_map/ppermute | solution.py:817
  56.4 9.0 %collective-permute-start.17 = (f32[64,128]{1,0:T(8,128)S(1)}, f32[64,128]{1,0:T(8,128)S(1)}, u32[]{:S(2)}, u32[]{:S(2)}) collective-permute-start(f32[64,128]{1,0:T(8,128)S(1)} %get-tuple-element.61), channel_id=1, source_target_pairs={{0,0},{1,2},{2,1},{3,3},{4,4},{5,6},{6,5},{7,7},{8,8},{9,10},{10,9... | collective-permute-start | bytes 98312 | tf_op jit(solution)/shard_map/ppermute | solution.py:817
  58.8 3.8 %collective-permute-start.14 = (f32[32,128]{1,0:T(8,128)S(1)}, f32[32,128]{1,0:T(8,128)S(1)}, u32[]{:S(2)}, u32[]{:S(2)}) collective-permute-start(f32[32,128]{1,0:T(8,128)S(1)} %get-tuple-element.58), channel_id=1, source_target_pairs={{0,4},{4,0},{8,12},{12,8},{1,5},{5,1},{9,13},{13,9},{2,6},{6,2},{1... | collective-permute-start | bytes 49160 | tf_op jit(solution)/shard_map/ppermute | solution.py:817
  59.7 5.6 %collective-permute-start.15 = (f32[32,128]{1,0:T(8,128)S(1)}, f32[32,128]{1,0:T(8,128)S(1)}, u32[]{:S(2)}, u32[]{:S(2)}) collective-permute-start(f32[32,128]{1,0:T(8,128)S(1)} %get-tuple-element.59), channel_id=1, source_target_pairs={{0,0},{4,8},{8,4},{12,12},{1,1},{5,9},{9,5},{13,13},{2,2},{6,10},{... | collective-permute-start | bytes 49160 | tf_op jit(solution)/shard_map/ppermute | solution.py:817

commit v8 on v7

--- a/solution.py
+++ b/solution.py
@@ -110,9 +110,6 @@
     sine_x, eig_x = sine_basis(box.ex)
     sine_y, eig_y = sine_basis(box.ey)
     sine_z, eig_z = sine_basis(box.deep)
-    skip = EDGE - MARGIN
-    into_y = np.zeros((box.ey, box.cols), np.float32)
-    into_y[:, skip : skip + box.ey] = sine_y
     from_y = sine_y[MARGIN : MARGIN + box.across]
     from_x = sine_x[MARGIN : MARGIN + box.long]
     spread = np.broadcast_to(eig_x[:, None], (box.ex, box.deep))
@@ -120,7 +117,7 @@
     return [
         jnp.asarray(np.ascontiguousarray(t))
         for t in (
-            left_table(into_y, box.cols, FORWARD),
+            left_table(sine_y, padded(box.ey), FORWARD),
             left_table(sine_x, padded(box.ex), FORWARD),
             left_table(from_x, padded(box.ex), BACKWARD),
             left_table(from_y, padded(box.ey), BACKWARD),
@@ -164,7 +161,7 @@
     return jnp.concatenate([values, blank], axis=0)
 
 
-def box_solve(box, source, means, tables, row_mask, col_mask, spectral, middle, emit):
+def box_solve(box, source, skip, means, tables, row_mask, col_mask, spectral, middle, emit):
     into_y, into_x, from_x, from_y, main_z, rest_z, spread, eig_z, eig_y = tables
     deep = box.deep
     deep_x, deep_y = padded(box.ex), padded(box.ey)
@@ -182,11 +179,11 @@
     if deep_y > box.ey:
         middle[:, box.ey :, :] = jnp.zeros((box.long, deep_y - box.ey, deep), jnp.float32)
     for start in range(0, box.ex, 8):
-        block = source[start : start + 8].reshape(8 * box.cols, deep)
-        block = dot_right(block, main_z, rest_z, FORWARD).reshape(8, box.cols, deep)
+        block = source[start : start + 8, skip : skip + box.ey].reshape(8 * box.ey, deep)
+        block = dot_right(block, main_z, rest_z, FORWARD).reshape(8, box.ey, deep)
         for row in range(0, 8, 2):
             pair = jnp.concatenate([block[row], block[row + 1]], axis=1)
-            pair = dot_left(into_y, pair, FORWARD, box.ey)
+            pair = dot_left(into_y, with_rows(pair, deep_y), FORWARD, box.ey)
             for part in range(2):
                 spectral_flat[pl.ds(start + row + part, box.ey, stride=deep_x), :] = pair[
                     :, part * deep : (part + 1) * deep
@@ -357,14 +354,16 @@
                 flat[row_of(box.cols, col, size, row), :] = add(values, row_side, side)
 
 
-def negative_image(row, x, x_next, flow_before, weights):
+def negative_image(window, row, at, first, last, flow_before, weights):
     to_long, to_across, to_deep, mass = weights
-    rows, lanes = x.shape
-    flow_long = to_long[row] * (x_next - x)
-    flow_across = to_across[row] * (pltpu.roll(x, rows - 1, 0) - x)
-    flow_deep = to_deep[row] * (pltpu.roll(x, lanes - 1, 1) - x)
-    total = flow_long - flow_before - mass[row] * x
-    total = total + (flow_across - pltpu.roll(flow_across, 1, 0))
+    x = window[row, first:last]
+    flow_long = to_long[at, first:last] * (window[row + 1, first:last] - x)
+    flow_across = to_across[at, first:last] * (window[row, first + 1 : last + 1] - x)
+    flow_from = to_across[at, first - 1 : last - 1] * (x - window[row, first - 1 : last - 1])
+    lanes = x.shape[1]
+    flow_deep = to_deep[at, first:last] * (pltpu.roll(x, lanes - 1, 1) - x)
+    total = flow_long - flow_before - mass[at, first:last] * x
+    total = total + (flow_across - flow_from)
     total = total + (flow_deep - pltpu.roll(flow_deep, 1, 1))
     return total, flow_long
 
@@ -388,6 +387,10 @@
 
 def last_rows_merged(refs, count):
     return merged(*(ref[ref.shape[0] - count :, :] for ref in refs))
+
+
+def join_rows(table, message, out):
+    out[...] = last_rows_merged((table, message), out.shape[0])
 
 
 def line_of(numbers, shape):
@@ -460,19 +463,32 @@
     return [ref[0:1, index : index + 1] for index in range(4)]
 
 
-def first_solve(box, load, low, high, left, right, means, *rest):
+def first_solve(box, load, low, high, left, right, means, zone, scale, diffusivity, decay, *rest):
     tables = rest[:N_TABLES]
-    window, local, spectral, middle = rest[N_TABLES:]
+    window, local, image, spectral, middle = rest[N_TABLES:]
+    half = [0.5 * diffusivity[z, 2] for z in range(3)]
+    rates = [decay[z] for z in range(3)]
+    lane = lax.broadcasted_iota(jnp.int32, (box.across, box.deep), 1)
+    ends = jnp.where((lane == 0) | (lane == box.deep - 1), jnp.float32(1.0), jnp.float32(0.0))
+    image[...] = jnp.zeros((box.across, box.deep), jnp.float32)
     wide_sides, narrow_sides = Sides("wide", low, high), Sides("narrow", left, right)
     fill_window(box, window, load, wide_sides, narrow_sides, MARGIN, 0, MARGIN)
 
     def emit(start, values):
         values = values * (1.0 / cheb_center)
-        local[start : start + 8] = values.reshape(8, box.across, box.deep)
+        values = values.reshape(8, box.across, box.deep)
+        local[start : start + 8] = values
+        total = image[...]
+        for row in range(8):
+            labels = zone[start + row]
+            mass = looked_up(labels, rates) + looked_up(labels, half) * scale[start + row] * ends
+            total = total + mass * values[row]
+        image[...] = total
 
     box_solve(
         box,
         window.at[1 : 1 + box.ex],
+        EDGE - MARGIN,
         means_of(means),
         tables,
         None,
@@ -527,24 +543,9 @@
 
 
 def image_sums(
-    box, zone, scale, local, low, high, left, right, table, diffusivity, decay, out, up, down
+    box, zone, scale, local, image, low, high, left, right, table, diffusivity, out, up, down
 ):
     half = [[0.5 * diffusivity[z, d] for z in range(3)] for d in range(3)]
-    rates = [decay[z] for z in range(3)]
-    lane = lax.broadcasted_iota(jnp.int32, (box.across, box.deep), 1)
-    ends = jnp.where((lane == 0) | (lane == box.deep - 1), jnp.float32(1.0), jnp.float32(0.0))
-    step = 8
-
-    def add_rows(index, total):
-        for row in range(step):
-            row = index * step + row
-            labels = zone[row]
-            mass = looked_up(labels, rates) + looked_up(labels, half[2]) * scale[row] * ends
-            total = total + mass * local[row]
-        return total
-
-    nothing = jnp.zeros((box.across, box.deep), jnp.float32)
-    image = lax.fori_loop(0, box.long // step, add_rows, nothing)
     shape = (box.long * box.across, box.deep)
     zone_flat, scale_flat, local_flat = zone.reshape(shape), scale.reshape(shape), local.reshape(shape)
     last_col = row_of(box.across, box.across - 1, box.long)
@@ -583,7 +584,7 @@
         flows.append(jnp.sum(weight * values, keepdims=True))
     long_pos, across_pos, long_count, across_count = position()
     numbers = [
-        (IMAGE_SUM, jnp.sum(image, keepdims=True) + sum(flows)),
+        (IMAGE_SUM, jnp.sum(image[...], keepdims=True) + sum(flows)),
         (FLOW_LONG_HIGH, flows[0] * as_float(long_pos < long_count - 1)),
         (FLOW_LONG_LOW, flows[1] * as_float(long_pos > 0)),
         (FLOW_ACROSS_HIGH, flows[2] * as_float(across_pos < across_count - 1)),
@@ -717,22 +718,24 @@
     fill_window(box, window, local, wide_sides, narrow_sides, REACH, 0, REACH, add)
     weights = (to_long, to_across, to_deep, mass)
 
+    start, stop = EDGE - MARGIN, EDGE + box.across + MARGIN
+
     def one_row(row, flow):
-        image, flow = negative_image(row, window[row], window[row + 1], flow, weights)
-        residual[row - 1] = load_window[row] + image
+        image, flow = negative_image(window, row, row, start, stop, flow, weights)
+        residual[row - 1] = load_window[row, start:stop] + image
         return flow
 
-    flow = to_long[0] * (window[1] - window[0])
+    flow = to_long[0, start:stop] * (window[1, start:stop] - window[0, start:stop])
     lax.fori_loop(1, 1 + box.ex, one_row, flow, unroll=4)
     inner = slice(EDGE, EDGE + box.across)
     first = REACH
     row_ids = lax.broadcasted_iota(jnp.int32, (1, padded(box.ex)), 1)
-    col_ids = lax.broadcasted_iota(jnp.int32, (1, box.cols), 1)
+    col_ids = lax.broadcasted_iota(jnp.int32, (1, padded(box.ey)), 1)
     row_mask = jnp.where(row_ids < MARGIN, as_float(long_pos > 0), 1.0)
     row_mask = jnp.where(row_ids >= MARGIN + box.long, as_float(long_pos < long_count - 1), row_mask)
-    col_mask = jnp.where(col_ids < EDGE, as_float(across_pos > 0), 1.0)
+    col_mask = jnp.where(col_ids < MARGIN, as_float(across_pos > 0), 1.0)
     col_mask = jnp.where(
-        col_ids >= EDGE + box.across, as_float(across_pos < across_count - 1), col_mask
+        col_ids >= MARGIN + box.across, as_float(across_pos < across_count - 1), col_mask
     )
     keep = 1.0 + rho_second * rho_first
 
@@ -743,7 +746,7 @@
         iterate[start : start + 8] = keep * before + (gain * rows + shift)
 
     box_solve(
-        box, residual, means_of(means), tables, row_mask, col_mask, spectral, middle, emit
+        box, residual, 0, means_of(means), tables, row_mask, col_mask, spectral, middle, emit
     )
     rows = in_order(is_even("wide"), iterate[box.long - 1], iterate[0])
     top[...], bottom[...] = rows
@@ -786,11 +789,13 @@
     weights = (to_long, to_across, to_deep, mass)
 
     def one_row(row, flow):
-        image, flow = negative_image(REACH + row, window[row + 1], window[row + 2], flow, weights)
-        result[row] = load[row] + image[inner]
+        image, flow = negative_image(
+            window, row + 1, REACH + row, inner.start, inner.stop, flow, weights
+        )
+        result[row] = load[row] + image
         return flow
 
-    flow = to_long[REACH - 1] * (window[1] - window[0])
+    flow = to_long[REACH - 1, inner] * (window[1, inner] - window[0, inner])
     chunk = box.long // 4
     copies = [own]
     for index in range(4):
@@ -882,17 +887,17 @@
         [pltpu.SemaphoreType.DMA((4,))],
     )(pinned(far_zone), pinned(far_scale), load, load_first, diffusivity, decay)
     far_narrow = exchange("narrow", *pack(REACH, [scale, zone], far_wide))
-    load_window, local = call(
+    load_window, local, image = call(
         functools.partial(first_solve, box),
-        (window, cells),
-        [VMEM] * (6 + N_TABLES),
+        (window, cells, f32(across, deep)),
+        [VMEM] * 8 + [SMEM] * 2 + [VMEM] * N_TABLES,
         [spectral, middle],
         flops=4 * 10**9,
-    )(load, *load_wide, *load_narrow, sums, *tables)
+    )(load, *load_wide, *load_narrow, sums, zone, scale, diffusivity, decay, *tables)
     message = f32(REACH * across + count, deep)
     table, first, second = call(
-        functools.partial(image_sums, box), (table_shape, message, message), [VMEM] * 8 + [SMEM] * 2
-    )(zone, scale, local, *far_wide, *far_narrow, table, diffusivity, decay)
+        functools.partial(image_sums, box), (table_shape, message, message), [VMEM] * 9 + [SMEM]
+    )(zone, scale, local, image, *far_wide, *far_narrow, table, diffusivity)
     own_table = table
     wide = exchange("wide", first, second, by_margins)
     parts = (table, *wide)
@@ -906,9 +911,10 @@
         flops=10**9,
     )(zone, scale, *far_wide, *far_narrow, diffusivity, decay)
     first, second, table = pack(REACH, [local], wide, parts, weights[3:])
-    narrow = exchange("narrow", first, second, by_margins)
+    narrow = exchange("narrow", first, second)
     if by_margins:
-        parts = (table, *narrow, two_away("narrow", table))
+        table = call(join_rows, table_shape, [VMEM] * 2)(table, narrow[0])
+        parts = (table, two_away("narrow", table))
     else:
         parts = (tell(own_table),)
     row, col = f32(across, deep), f32(long, deep)
@@ -918,7 +924,7 @@
         [VMEM] * (11 + len(parts) + N_TABLES),
         [
             scratch(window.shape),
-            scratch((box.ex, box.cols, deep)),
+            scratch((box.ex, box.ey, deep)),
             spectral,
             middle,
             scratch((count, -(-2 * count // 128) * 128)),

time: 69.2 us -> 69.1 us (level)
  waiting for transfers between devices: 10.7 us -> 9.68 us
  starting transfers between devices: 24.9 us -> 25.8 us
    ppermute x2, waiting for transfers between devices: 5.39 us -> 0.01 us  [two_away(): return lax.ppermute(table, axis, [(i, (i + 2) % size) for i in range(size)])]
    ppermute x8, waiting for transfers between devices: 4.86 us -> 8.78 us  [exchange(): lax.ppermute(second, axis, swaps[1])]
    ppermute x8, starting transfers between devices: 17.2 us -> 20.2 us  [exchange(): lax.ppermute(second, axis, swaps[1])]
    ppermute x2, starting transfers between devices: 1.83 us -> 0.15 us  [two_away(): return lax.ppermute(table, axis, [(i, (i + 2) % size) for i in range(size)])]
    pallas_call x1 -> x2, Pallas kernels: 6.73 us -> 7.3 us  [the longest x1 7.3 us: on_device(): call(functools.partial(first_solve, box), (window, cells, f32(across, dee...]
  transfers between devices with their start and end apart: 18 -> 18, of which waited for: 6 -> 6; matrix products, arithmetic and copies ran while one was open for 0% -> 0% of each run, Pallas kernels for 20% -> 21%
where the time goes in v8:
time: 69.1 us; the launch traced here: 68.7 us
  Pallas kernels  32 us (46%)
  starting transfers between devices  25.8 us (37%)
  waiting for transfers between devices  9.68 us (14%)
  between operations  1.18 us (2%)
    ppermute x8, starting transfers between devices, exchange(): lax.ppermute(second, axis, swaps[1])  20.2 us
    pallas_call x1, Pallas kernels, on_device(): call(functools.partial(second_solve, box, len(parts)), (cells, row, row,...  11.5 us
    ppermute x8, waiting for transfers between devices, exchange(): lax.ppermute(second, axis, swaps[1])  8.78 us
    pallas_call x1, Pallas kernels, on_device(): call(functools.partial(first_solve, box), (window, cells, f32(across, dee...  7.3 us
    ppermute x8, starting transfers between devices, exchange(): lax.ppermute(first, axis, swaps[0])  5.49 us
    pallas_call x1, Pallas kernels, on_device(): call(functools.partial(weights_of, box), (window,) * 4, [VMEM] * 6 + [SME...  3.71 us
    pallas_call x1, Pallas kernels, on_device(): call(functools.partial(last_residual, box), (cells, cells), [VMEM] * 10,...  3.46 us
    pallas_call x1, Pallas kernels, on_device(): call(functools.partial(box_sums, box), (whole_zone, cells, f32(8, 128), t...  2.69 us
  transfers between devices with their start and end apart: 18, of which 6 were waited for; matrix products, arithmetic and copies ran while one was open for 0% of the time, Pallas kernels for 21%

profile of v8, /device:TPU:10, one launch (start us, length us, event | category | flops | bytes accessed | tf_op | source)
XLA Modules:
  0.0 68.7 jit_solution(7290728513641757470)
XLA Ops:
  0.7 1.5 %shard_map.149 = (f32[64,32,128]{2,1,0:T(8,128)S(1)}, f32[4,32,128]{2,1,0:T(8,128)S(1)}, f32[4,32,128]{2,1,0:T(8,128)S(1)}, f32[10,32,128]{2,1,0:T(8,128)S(1)}, f32[10,32,128]{2,1,0:T(8,128)S(1)}) custom-call(s32[64,32,128]{2,1,0:T(8,128)} %far_zone.1, f32[64,32,128]{2,1,0:T(8,128)} %far_scale.1, f32[64,32,128]{2,1,0:T(8,128)} %load.1), custom_call_target="tpu_custom_call" | custom-call | tf_op jit(solution)/shard_map/pallas_call | solution.py:873
  2.2 0.5 collective-permute-start
  2.7 4.6 %collective-permute-start.1 = (f32[4,32,128]{2,1,0:T(8,128)S(1)}, f32[4,32,128]{2,1,0:T(8,128)S(1)}, u32[]{:S(2)}, u32[]{:S(2)}) collective-permute-start(f32[4,32,128]{2,1,0:T(8,128)S(1)} %get-tuple-element.35), channel_id=1, source_target_pairs={{0,0},{4,8},{8,4},{12,12},{1,1},{5,9},{9,5},{13,13},{2,2},{6,10},{... | collective-permute-start | bytes 196616 | tf_op jit(solution)/shard_map/ppermute | solution.py:822
  7.3 0.1 collective-permute-start.4
  7.4 1.9 %collective-permute-start.5 = (f32[10,32,128]{2,1,0:T(8,128)S(1)}, f32[10,32,128]{2,1,0:T(8,128)S(1)}, u32[]{:S(2)}, u32[]{:S(2)}) collective-permute-start(f32[10,32,128]{2,1,0:T(8,128)S(1)} %get-tuple-element.44), channel_id=1, source_target_pairs={{0,0},{4,8},{8,4},{12,12},{1,1},{5,9},{9,5},{13,13},{2,2},{6,10},{... | collective-permute-start | bytes 491528 | tf_op jit(solution)/shard_map/ppermute | solution.py:822
  9.3 0.2 collective-permute-done.1.refs_2_.high
  9.5 0.2 shard_map.150
  9.7 1.9 %collective-permute-start.3 = (f32[296,128]{1,0:T(8,128)S(1)}, f32[296,128]{1,0:T(8,128)S(1)}, u32[]{:S(2)}, u32[]{:S(2)}) collective-permute-start(f32[296,128]{1,0:T(8,128)S(1)} %get-tuple-element.37), channel_id=1, source_target_pairs={{0,0},{1,2},{2,1},{3,3},{4,4},{5,6},{6,5},{7,7},{8,8},{9,10},{10,9... | collective-permute-start | bytes 454664 | tf_op jit(solution)/shard_map/ppermute | solution.py:822
  11.7 0.1 collective-permute-start.2
  11.8 2.7 %shard_map.151 = (s32[64,32,128]{2,1,0:T(8,128)S(1)}, f32[64,32,128]{2,1,0:T(8,128)S(1)}, f32[8,128]{1,0:T(8,128)S(1)}, f32[16,128]{1,0:T(8,128)S(1)}) custom-call(s32[64,32,128]{2,1,0:T(8,128)} %far_zone.1, f32[64,32,128]{2,1,0:T(8,128)} %far_scale.1, f32[64,32,128]{2,1,0:T(8,128)S(1)} %get-tuple-element.33.refs_0_.load, ...), custom_call_target="tpu_custom_call" | custom-call | tf_op jit(solution)/shard_map/pallas_call | solution.py:883
  14.6 0.1 collective-permute-done.5.refs_3_.high
  14.7 0.4 shard_map.153
  15.1 0.5 collective-permute-start.6
  15.6 3.6 %collective-permute-start.7 = (f32[744,128]{1,0:T(8,128)S(1)}, f32[744,128]{1,0:T(8,128)S(1)}, u32[]{:S(2)}, u32[]{:S(2)}) collective-permute-start(f32[744,128]{1,0:T(8,128)S(1)} %get-tuple-element.46), channel_id=1, source_target_pairs={{0,0},{1,2},{2,1},{3,3},{4,4},{5,6},{6,5},{7,7},{8,8},{9,10},{10,9... | collective-permute-start | bytes 1142792 | tf_op jit(solution)/shard_map/ppermute | solution.py:822
  19.3 7.3 %shard_map.152 = (f32[74,48,128]{2,1,0:T(8,128)S(1)}, f32[64,32,128]{2,1,0:T(8,128)S(1)}, f32[32,128]{1,0:T(8,128)S(1)}) custom-call(f32[64,32,128]{2,1,0:T(8,128)S(1)} %get-tuple-element.33.refs_0_.load, f32[4,32,128]{2,1,0:T(8,128)S(1)} %collective-permute-done.refs_1_.low, f32[4,32,128]{2,1,0:T(8,128)S(1)} %collective-permute-done.1.refs_2_.high, ...), custom_call_target="tpu_custom_call" | custom-call | flops 4000000000 | tf_op jit(solution)/shard_map/pallas_call | solution.py:890
  26.6 1.0 %shard_map.154 = (f32[16,128]{1,0:T(8,128)S(1)}, f32[176,128]{1,0:T(8,128)S(1)}, f32[176,128]{1,0:T(8,128)S(1)}) custom-call(s32[64,32,128]{2,1,0:T(8,128)S(1)} %get-tuple-element.39.zone.refs_1_, f32[64,32,128]{2,1,0:T(8,128)S(1)} %get-tuple-element.40.scale.refs_0_, f32[64,32,128]{2,1,0:T(8,128)S(1)} %get-tuple-element.41.local.refs_0_, ...), custom_call_target="tpu_custom_call" | custom-call | tf_op jit(solution)/shard_map/pallas_call | solution.py:898
  27.6 0.1 collective-permute-start.10
  27.7 3.6 %collective-permute-start.8 = (f32[176,128]{1,0:T(8,128)S(1)}, f32[176,128]{1,0:T(8,128)S(1)}, u32[]{:S(2)}, u32[]{:S(2)}) collective-permute-start(f32[176,128]{1,0:T(8,128)S(1)} %get-tuple-element.48), channel_id=1, source_target_pairs={{0,4},{4,0},{8,12},{12,8},{1,5},{5,1},{9,13},{13,9},{2,6},{6,2},{1... | collective-permute-start | bytes 270344 | tf_op jit(solution)/shard_map/ppermute | solution.py:822
  31.3 3.7 %shard_map.155 = (f32[74,48,128]{2,1,0:T(8,128)S(1)}, f32[74,48,128]{2,1,0:T(8,128)S(1)}, f32[74,48,128]{2,1,0:T(8,128)S(1)}, f32[74,48,128]{2,1,0:T(8,128)S(1)}) custom-call(s32[64,32,128]{2,1,0:T(8,128)S(1)} %get-tuple-element.39.zone.refs_1_, f32[64,32,128]{2,1,0:T(8,128)S(1)} %get-tuple-element.40.scale.refs_0_, ...), custom_call_target="tpu_custom_call" | custom-call | flops 1000000000 | tf_op jit(solution)/shard_map/pallas_call | solution.py:906
  35.0 1.8 %collective-permute-done.9.refs_2_.refs_5_.high = f32[176,128]{1,0:T(8,128)S(1)} collective-permute-done((f32[176,128]{1,0:T(8,128)S(1)}, f32[176,128]{1,0:T(8,128)S(1)}, u32[]{:S(2)}, u32[]{:S(2)}) %collective-permute-start.9) | collective-permute-done | bytes 90144 | tf_op jit(solution)/shard_map/ppermute | solution.py:822
  36.8 0.2 shard_map.156
  37.0 0.1 collective-permute-start.11
  37.1 2.6 %collective-permute-start.12 = (f32[392,128]{1,0:T(8,128)S(1)}, f32[392,128]{1,0:T(8,128)S(1)}, u32[]{:S(2)}, u32[]{:S(2)}) collective-permute-start(f32[392,128]{1,0:T(8,128)S(1)} %get-tuple-element.53), channel_id=1, source_target_pairs={{0,0},{1,2},{2,1},{3,3},{4,4},{5,6},{6,5},{7,7},{8,8},{9,10},{10,9... | collective-permute-start | bytes 602120 | tf_op jit(solution)/shard_map/ppermute | solution.py:822
  39.8 4.4 %collective-permute-done.12.right = f32[392,128]{1,0:T(8,128)S(1)} collective-permute-done((f32[392,128]{1,0:T(8,128)S(1)}, f32[392,128]{1,0:T(8,128)S(1)}, u32[]{:S(2)}, u32[]{:S(2)}) %collective-permute-start.12) | collective-permute-done | bytes 200736 | tf_op jit(solution)/shard_map/ppermute | solution.py:822
  44.2 11.5 %shard_map.158 = (f32[64,32,128]{2,1,0:T(8,128)S(1)}, f32[32,128]{1,0:T(8,128)S(1)}, f32[32,128]{1,0:T(8,128)S(1)}, f32[64,128]{1,0:T(8,128)S(1)}, f32[64,128]{1,0:T(8,128)S(1)}) custom-call(f32[64,32,128]{2,1,0:T(8,128)S(1)} %get-tuple-element.41.local.refs_0_, f32[176,128]{1,0:T(8,128)S(1)} %collective-permute-done.8.refs_1_.refs_4_.low, ...), custom_call_target="tpu_custom_call" | custom-call | flops 4000000000 | tf_op jit(solution)/shard_map/pallas_call | solution.py:921
  55.7 0.2 collective-permute-start.16
  55.9 3.1 %collective-permute-start.17 = (f32[64,128]{1,0:T(8,128)S(1)}, f32[64,128]{1,0:T(8,128)S(1)}, u32[]{:S(2)}, u32[]{:S(2)}) collective-permute-start(f32[64,128]{1,0:T(8,128)S(1)} %get-tuple-element.63), channel_id=1, source_target_pairs={{0,0},{1,2},{2,1},{3,3},{4,4},{5,6},{6,5},{7,7},{8,8},{9,10},{10,9... | collective-permute-start | bytes 98312 | tf_op jit(solution)/shard_map/ppermute | solution.py:822
  59.0 0.5 collective-permute-start.14
  59.5 2.4 %collective-permute-start.15 = (f32[32,128]{1,0:T(8,128)S(1)}, f32[32,128]{1,0:T(8,128)S(1)}, u32[]{:S(2)}, u32[]{:S(2)}) collective-permute-start(f32[32,128]{1,0:T(8,128)S(1)} %get-tuple-element.61), channel_id=1, source_target_pairs={{0,0},{4,8},{8,4},{12,12},{1,1},{5,9},{9,5},{13,13},{2,2},{6,10},{... | collective-permute-start | bytes 49160 | tf_op jit(solution)/shard_map/ppermute | solution.py:822
  61.9 0.9 %collective-permute-done.14.low = f32[32,128]{1,0:T(8,128)S(1)} collective-permute-done((f32[32,128]{1,0:T(8,128)S(1)}, f32[32,128]{1,0:T(8,128)S(1)}, u32[]{:S(2)}, u32[]{:S(2)}) %collective-permute-start.14) | collective-permute-done | bytes 16416 | tf_op jit(solution)/shard_map/ppermute | solution.py:822
  62.8 2.3 %collective-permute-done.15.high = f32[32,128]{1,0:T(8,128)S(1)} collective-permute-done((f32[32,128]{1,0:T(8,128)S(1)}, f32[32,128]{1,0:T(8,128)S(1)}, u32[]{:S(2)}, u32[]{:S(2)}) %collective-permute-start.15) | collective-permute-done | bytes 16416 | tf_op jit(solution)/shard_map/ppermute | solution.py:822
  65.1 3.5 %shard_map.159 = (f32[64,32,128]{2,1,0:T(8,128)}, f32[64,32,128]{2,1,0:T(8,128)}) custom-call(f32[64,32,128]{2,1,0:T(8,128)S(1)} %get-tuple-element.33.refs_0_.load, f32[64,32,128]{2,1,0:T(8,128)S(1)} %get-tuple-element.59.partial, f32[32,128]{1,0:T(8,128)S(1)} %collective-permute-done.14.low, f32[32,128]{1,0:T(8,128)S(1)} %collective-permute-done.15.high, ...), custom_call_target="tpu_custom_call" | custom-call | tf_op jit(solution)/shard_map/pallas_call | solution.py:936
  (37 shorter events, 0.2 us)
Async XLA Ops:
  0.6 11.1 %copy-start = (f32[3,3]{1,0:T(4,128)S(1)}, f32[3,3]{1,0:T(4,128)}, u32[]{:S(2)}) copy-start(f32[3,3]{1,0:T(4,128)} %diffusivity.7) | copy-start | bytes 112
  0.6 11.1 %copy-start.1 = (f32[3]{0:T(128)S(1)}, f32[3]{0:T(128)}, u32[]{:S(2)}) copy-start(f32[3]{0:T(128)} %decay.5) | copy-start | bytes 40
  2.2 7.1 %collective-permute-start = (f32[4,32,128]{2,1,0:T(8,128)S(1)}, f32[4,32,128]{2,1,0:T(8,128)S(1)}, u32[]{:S(2)}, u32[]{:S(2)}) collective-permute-start(f32[4,32,128]{2,1,0:T(8,128)S(1)} %get-tuple-element.34), channel_id=1, source_target_pairs={{0,4},{4,0},{8,12},{12,8},{1,5},{5,1},{9,13},{13,9},{2,6},{6,2},{1... | collective-permute-start | bytes 196616 | tf_op jit(solution)/shard_map/ppermute | solution.py:822
  2.7 6.8 %collective-permute-start.1 = (f32[4,32,128]{2,1,0:T(8,128)S(1)}, f32[4,32,128]{2,1,0:T(8,128)S(1)}, u32[]{:S(2)}, u32[]{:S(2)}) collective-permute-start(f32[4,32,128]{2,1,0:T(8,128)S(1)} %get-tuple-element.35), channel_id=1, source_target_pairs={{0,0},{4,8},{8,4},{12,12},{1,1},{5,9},{9,5},{13,13},{2,2},{6,10},{... | collective-permute-start | bytes 196616 | tf_op jit(solution)/shard_map/ppermute | solution.py:822
  7.3 7.2 %collective-permute-start.4 = (f32[10,32,128]{2,1,0:T(8,128)S(1)}, f32[10,32,128]{2,1,0:T(8,128)S(1)}, u32[]{:S(2)}, u32[]{:S(2)}) collective-permute-start(f32[10,32,128]{2,1,0:T(8,128)S(1)} %get-tuple-element.43), channel_id=1, source_target_pairs={{0,4},{4,0},{8,12},{12,8},{1,5},{5,1},{9,13},{13,9},{2,6},{6,2},{1... | collective-permute-start | bytes 491528 | tf_op jit(solution)/shard_map/ppermute | solution.py:822
  7.4 7.3 %collective-permute-start.5 = (f32[10,32,128]{2,1,0:T(8,128)S(1)}, f32[10,32,128]{2,1,0:T(8,128)S(1)}, u32[]{:S(2)}, u32[]{:S(2)}) collective-permute-start(f32[10,32,128]{2,1,0:T(8,128)S(1)} %get-tuple-element.44), channel_id=1, source_target_pairs={{0,0},{4,8},{8,4},{12,12},{1,1},{5,9},{9,5},{13,13},{2,2},{6,10},{... | collective-permute-start | bytes 491528 | tf_op jit(solution)/shard_map/ppermute | solution.py:822
  9.7 9.5 %collective-permute-start.3 = (f32[296,128]{1,0:T(8,128)S(1)}, f32[296,128]{1,0:T(8,128)S(1)}, u32[]{:S(2)}, u32[]{:S(2)}) collective-permute-start(f32[296,128]{1,0:T(8,128)S(1)} %get-tuple-element.37), channel_id=1, source_target_pairs={{0,0},{1,2},{2,1},{3,3},{4,4},{5,6},{6,5},{7,7},{8,8},{9,10},{10,9... | collective-permute-start | bytes 454664 | tf_op jit(solution)/shard_map/ppermute | solution.py:822
  11.7 7.6 %collective-permute-start.2 = (f32[296,128]{1,0:T(8,128)S(1)}, f32[296,128]{1,0:T(8,128)S(1)}, u32[]{:S(2)}, u32[]{:S(2)}) collective-permute-start(f32[296,128]{1,0:T(8,128)S(1)} %get-tuple-element.36.after), channel_id=1, source_target_pairs={{0,1},{1,0},{2,3},{3,2},{4,5},{5,4},{6,7},{7,6},{8,9},{9,8},{10,11... | collective-permute-start | bytes 454664 | tf_op jit(solution)/shard_map/ppermute | solution.py:822
  14.4 4.8 %copy-start.2 = (bf16[256,256]{1,0:T(8,128)(2,1)S(1)}, bf16[256,256]{1,0:T(8,128)(2,1)}, u32[]{:S(2)}) copy-start(bf16[256,256]{1,0:T(8,128)(2,1)} %constant.22.clone.rest_4_.rest_11_) | copy-start | bytes 393220
  14.5 4.8 %copy-start.3 = (bf16[192,240]{1,0:T(8,128)(2,1)S(1)}, bf16[192,240]{1,0:T(8,128)(2,1)}, u32[]{:S(2)}) copy-start(bf16[192,240]{1,0:T(8,128)(2,1)} %constant.20.clone.rest_2_.rest_9_) | copy-start | bytes 276484
  14.5 4.8 %copy-start.4 = (bf16[144,160]{1,0:T(8,128)(2,1)S(1)}, bf16[144,160]{1,0:T(8,128)(2,1)}, u32[]{:S(2)}) copy-start(bf16[144,160]{1,0:T(8,128)(2,1)} %constant.19.clone.rest_1_.rest_8_) | copy-start | bytes 138244
  14.5 4.8 %copy-start.5 = (bf16[256,128]{1,0:T(8,128)(2,1)S(1)}, bf16[256,128]{1,0:T(8,128)(2,1)}, u32[]{:S(2)}) copy-start(bf16[256,128]{1,0:T(8,128)(2,1)} %constant.23.clone.rest_5_.rest_12_) | copy-start | bytes 196612
  14.5 4.8 %copy-start.6 = (bf16[96,144]{1,0:T(8,128)(2,1)S(1)}, bf16[96,144]{1,0:T(8,128)(2,1)}, u32[]{:S(2)}) copy-start(bf16[96,144]{1,0:T(8,128)(2,1)} %constant.21.clone.rest_3_.rest_10_) | copy-start | bytes 82948
  14.5 4.8 %copy-start.7 = (f32[72,128]{1,0:T(8,128)S(1)}, f32[72,128]{1,0:T(8,128)}, u32[]{:S(2)}) copy-start(f32[72,128]{1,0:T(8,128)} %constant.24.clone.rest_6_.rest_13_) | copy-start | bytes 110596
  14.5 4.8 %copy-start.8 = (bf16[80,96]{1,0:T(8,128)(2,1)S(1)}, bf16[80,96]{1,0:T(8,128)(2,1)}, u32[]{:S(2)}) copy-start(bf16[80,96]{1,0:T(8,128)(2,1)} %constant.18.clone.rest_0_.rest_7_) | copy-start | bytes 46084
  14.5 4.8 %copy-start.9 = (f32[1,40]{1,0:T(1,128)S(1)}, f32[1,40]{1,0:T(1,128)}, u32[]{:S(2)}) copy-start(f32[1,40]{1,0:T(1,128)} %constant.26.clone.rest_8_.rest_15_) | copy-start | bytes 484
  14.5 4.8 %copy-start.10 = (f32[1,128]{1,0:T(1,128)S(1)}, f32[1,128]{1,0:T(1,128)}, u32[]{:S(2)}) copy-start(f32[1,128]{1,0:T(1,128)} %constant.25.clone.rest_7_.rest_14_) | copy-start | bytes 1540
  15.1 11.5 %collective-permute-start.6 = (f32[744,128]{1,0:T(8,128)S(1)}, f32[744,128]{1,0:T(8,128)S(1)}, u32[]{:S(2)}, u32[]{:S(2)}) collective-permute-start(f32[744,128]{1,0:T(8,128)S(1)} %get-tuple-element.45), channel_id=1, source_target_pairs={{0,1},{1,0},{2,3},{3,2},{4,5},{5,4},{6,7},{7,6},{8,9},{9,8},{10,11... | collective-permute-start | bytes 1142792 | tf_op jit(solution)/shard_map/ppermute | solution.py:822
  15.6 11.1 %collective-permute-start.7 = (f32[744,128]{1,0:T(8,128)S(1)}, f32[744,128]{1,0:T(8,128)S(1)}, u32[]{:S(2)}, u32[]{:S(2)}) collective-permute-start(f32[744,128]{1,0:T(8,128)S(1)} %get-tuple-element.46), channel_id=1, source_target_pairs={{0,0},{1,2},{2,1},{3,3},{4,4},{5,6},{6,5},{7,7},{8,8},{9,10},{10,9... | collective-permute-start | bytes 1142792 | tf_op jit(solution)/shard_map/ppermute | solution.py:822
  27.6 7.4 %collective-permute-start.10 = (f32[16,128]{1,0:T(8,128)S(1)}, f32[16,128]{1,0:T(8,128)S(1)}, u32[]{:S(2)}, u32[]{:S(2)}) collective-permute-start(f32[16,128]{1,0:T(8,128)S(1)} %get-tuple-element.50.refs_3_), channel_id=1, source_target_pairs={{0,8},{4,12},{8,0},{12,4},{1,9},{5,13},{9,1},{13,5},{2,10},{6,14},... | collective-permute-start | bytes 24584 | tf_op jit(solution)/shard_map/ppermute | solution.py:827
  27.7 7.4 %collective-permute-start.8 = (f32[176,128]{1,0:T(8,128)S(1)}, f32[176,128]{1,0:T(8,128)S(1)}, u32[]{:S(2)}, u32[]{:S(2)}) collective-permute-start(f32[176,128]{1,0:T(8,128)S(1)} %get-tuple-element.48), channel_id=1, source_target_pairs={{0,4},{4,0},{8,12},{12,8},{1,5},{5,1},{9,13},{13,9},{2,6},{6,2},{1... | collective-permute-start | bytes 270344 | tf_op jit(solution)/shard_map/ppermute | solution.py:822
  31.3 5.5 %collective-permute-start.9 = (f32[176,128]{1,0:T(8,128)S(1)}, f32[176,128]{1,0:T(8,128)S(1)}, u32[]{:S(2)}, u32[]{:S(2)}) collective-permute-start(f32[176,128]{1,0:T(8,128)S(1)} %get-tuple-element.49), channel_id=1, source_target_pairs={{0,12},{4,8},{8,4},{12,0},{1,13},{5,9},{9,5},{13,1},{2,14},{6,10},... | collective-permute-start | bytes 270344 | tf_op jit(solution)/shard_map/ppermute | solution.py:822
  37.0 2.7 %collective-permute-start.11 = (f32[392,128]{1,0:T(8,128)S(1)}, f32[392,128]{1,0:T(8,128)S(1)}, u32[]{:S(2)}, u32[]{:S(2)}) collective-permute-start(f32[392,128]{1,0:T(8,128)S(1)} %get-tuple-element.52), channel_id=1, source_target_pairs={{0,1},{1,0},{2,3},{3,2},{4,5},{5,4},{6,7},{7,6},{8,9},{9,8},{10,11... | collective-permute-start | bytes 602120 | tf_op jit(solution)/shard_map/ppermute | solution.py:822
  37.1 7.1 %collective-permute-start.12 = (f32[392,128]{1,0:T(8,128)S(1)}, f32[392,128]{1,0:T(8,128)S(1)}, u32[]{:S(2)}, u32[]{:S(2)}) collective-permute-start(f32[392,128]{1,0:T(8,128)S(1)} %get-tuple-element.53), channel_id=1, source_target_pairs={{0,0},{1,2},{2,1},{3,3},{4,4},{5,6},{6,5},{7,7},{8,8},{9,10},{10,9... | collective-permute-start | bytes 602120 | tf_op jit(solution)/shard_map/ppermute | solution.py:822
  39.8 4.5 %collective-permute-start.13 = (f32[16,128]{1,0:T(8,128)S(1)}, f32[16,128]{1,0:T(8,128)S(1)}, u32[]{:S(2)}, u32[]{:S(2)}) collective-permute-start(f32[16,128]{1,0:T(8,128)S(1)} %shard_map.157.rest_0_), channel_id=1, source_target_pairs={{0,2},{1,3},{2,0},{3,1},{4,6},{5,7},{6,4},{7,5},{8,10},{9,11},{10,... | collective-permute-start | bytes 24584 | tf_op jit(solution)/shard_map/ppermute | solution.py:827
  55.7 9.4 %collective-permute-start.16 = (f32[64,128]{1,0:T(8,128)S(1)}, f32[64,128]{1,0:T(8,128)S(1)}, u32[]{:S(2)}, u32[]{:S(2)}) collective-permute-start(f32[64,128]{1,0:T(8,128)S(1)} %get-tuple-element.62), channel_id=1, source_target_pairs={{0,1},{1,0},{2,3},{3,2},{4,5},{5,4},{6,7},{7,6},{8,9},{9,8},{10,11... | collective-permute-start | bytes 98312 | tf_op jit(solution)/shard_map/ppermute | solution.py:822
  55.9 9.2 %collective-permute-start.17 = (f32[64,128]{1,0:T(8,128)S(1)}, f32[64,128]{1,0:T(8,128)S(1)}, u32[]{:S(2)}, u32[]{:S(2)}) collective-permute-start(f32[64,128]{1,0:T(8,128)S(1)} %get-tuple-element.63), channel_id=1, source_target_pairs={{0,0},{1,2},{2,1},{3,3},{4,4},{5,6},{6,5},{7,7},{8,8},{9,10},{10,9... | collective-permute-start | bytes 98312 | tf_op jit(solution)/shard_map/ppermute | solution.py:822
  59.0 3.8 %collective-permute-start.14 = (f32[32,128]{1,0:T(8,128)S(1)}, f32[32,128]{1,0:T(8,128)S(1)}, u32[]{:S(2)}, u32[]{:S(2)}) collective-permute-start(f32[32,128]{1,0:T(8,128)S(1)} %get-tuple-element.60), channel_id=1, source_target_pairs={{0,4},{4,0},{8,12},{12,8},{1,5},{5,1},{9,13},{13,9},{2,6},{6,2},{1... | collective-permute-start | bytes 49160 | tf_op jit(solution)/shard_map/ppermute | solution.py:822
  59.5 5.6 %collective-permute-start.15 = (f32[32,128]{1,0:T(8,128)S(1)}, f32[32,128]{1,0:T(8,128)S(1)}, u32[]{:S(2)}, u32[]{:S(2)}) collective-permute-start(f32[32,128]{1,0:T(8,128)S(1)} %get-tuple-element.61), channel_id=1, source_target_pairs={{0,0},{4,8},{8,4},{12,12},{1,1},{5,9},{9,5},{13,13},{2,2},{6,10},{... | collective-permute-start | bytes 49160 | tf_op jit(solution)/shard_map/ppermute | solution.py:822

commit v9 on v8

--- a/solution.py
+++ b/solution.py
@@ -36,12 +36,12 @@
     return table.astype(np.float32), eigvals.astype(np.float32)
 
 
-def call(body, out_shape, in_specs, scratch=(), flops=0, moved=0, out_spec=VMEM):
+def call(body, out_shape, in_specs, scratch=(), flops=0, moved=0, out_spec=None):
     return pl.pallas_call(
         body,
         out_shape=out_shape,
         in_specs=in_specs,
-        out_specs=jax.tree.map(lambda _: out_spec, out_shape),
+        out_specs=out_spec or jax.tree.map(lambda _: VMEM, out_shape),
         scratch_shapes=list(scratch),
         compiler_params=pltpu.CompilerParams(vmem_limit_bytes=30 * 2**20),
         cost_estimate=pl.CostEstimate(flops=flops, bytes_accessed=moved, transcendentals=0),
@@ -161,7 +161,7 @@
     return jnp.concatenate([values, blank], axis=0)
 
 
-def box_solve(box, source, skip, means, tables, row_mask, col_mask, spectral, middle, emit):
+def box_solve(box, source, means, tables, row_mask, col_mask, spectral, middle, emit):
     into_y, into_x, from_x, from_y, main_z, rest_z, spread, eig_z, eig_y = tables
     deep = box.deep
     deep_x, deep_y = padded(box.ex), padded(box.ey)
@@ -179,7 +179,7 @@
     if deep_y > box.ey:
         middle[:, box.ey :, :] = jnp.zeros((box.long, deep_y - box.ey, deep), jnp.float32)
     for start in range(0, box.ex, 8):
-        block = source[start : start + 8, skip : skip + box.ey].reshape(8 * box.ey, deep)
+        block = source(start).reshape(8 * box.ey, deep)
         block = dot_right(block, main_z, rest_z, FORWARD).reshape(8, box.ey, deep)
         for row in range(0, 8, 2):
             pair = jnp.concatenate([block[row], block[row + 1]], axis=1)
@@ -487,8 +487,7 @@
 
     box_solve(
         box,
-        window.at[1 : 1 + box.ex],
-        EDGE - MARGIN,
+        lambda row: window[1 + row : 9 + row, EDGE - MARGIN : EDGE + box.across + MARGIN],
         means_of(means),
         tables,
         None,
@@ -674,8 +673,10 @@
     return jnp.sum(jnp.where(wanted, values, jnp.zeros_like(values)), axis=1, keepdims=True)
 
 
-def coarse_corrections(box, numbers, work):
-    count = numbers.shape[0]
+def coarse_corrections(parts, *refs):
+    table_parts, (out, work) = refs[:parts], refs[parts:]
+    count = work.shape[0]
+    numbers = last_rows_merged(table_parts, count)
     across_count = lax.axis_size("narrow")
     inverse = coarse_inverse(numbers, work)
     sums = column(numbers, IMAGE_SUM)
@@ -685,19 +686,18 @@
     sums = sums - column(pltpu.roll(numbers, 1, 0), FLOW_ACROSS_HIGH)
     load_sums = column(numbers, LOAD_SUM)
     sums = load_sums * (1.0 - 1.0 / cheb_center) - sums
-    return answer(inverse, load_sums) * (1.0 / cheb_center), answer(inverse, sums) * gain
-
-
-def second_solve(box, parts, local, low, high, left, right, means, *rest):
-    table_parts, rest = rest[:parts], rest[parts:]
+    out[0:1, :] = answer(inverse, load_sums) * (1.0 / cheb_center)
+    out[1:2, :] = answer(inverse, sums) * gain
+
+
+def second_solve(box, local, low, high, left, right, means, answers, *rest):
     to_long, to_across, to_deep, mass, load_window = rest[:5]
     tables = rest[5 : 5 + N_TABLES]
-    iterate, top, bottom, last_col, first_col = rest[5 + N_TABLES : 10 + N_TABLES]
-    window, residual, spectral, middle, work = rest[10 + N_TABLES :]
+    iterate, top, bottom, last_col, first_col, out = rest[5 + N_TABLES : 11 + N_TABLES]
+    window, spectral, middle, sems = rest[11 + N_TABLES :]
     long_pos, across_pos, long_count, across_count = position()
-    numbers = last_rows_merged(table_parts, work.shape[0])
-    coarse, second_coarse = coarse_corrections(box, numbers, work)
-    own_shift = at_box(second_coarse, 0, 0)
+    coarse = answers[0:1, :]
+    own_shift = at_box(answers[1:2, :], 0, 0)
     shifts = {
         (row_side, col_side): at_box(coarse, row_side, col_side)
         for row_side in (-1, 0, 1)
@@ -720,13 +720,15 @@
 
     start, stop = EDGE - MARGIN, EDGE + box.across + MARGIN
 
-    def one_row(row, flow):
-        image, flow = negative_image(window, row, row, start, stop, flow, weights)
-        residual[row - 1] = load_window[row, start:stop] + image
-        return flow
-
-    flow = to_long[0, start:stop] * (window[1, start:stop] - window[0, start:stop])
-    lax.fori_loop(1, 1 + box.ex, one_row, flow, unroll=4)
+    flow = [to_long[0, start:stop] * (window[1, start:stop] - window[0, start:stop])]
+
+    def residual(start_row):
+        rows = []
+        for row in range(start_row + 1, start_row + 9):
+            image, flow[0] = negative_image(window, row, row, start, stop, flow[0], weights)
+            rows.append((load_window[row, start:stop] + image)[None])
+        return jnp.concatenate(rows, axis=0)
+
     inner = slice(EDGE, EDGE + box.across)
     first = REACH
     row_ids = lax.broadcasted_iota(jnp.int32, (1, padded(box.ex)), 1)
@@ -738,21 +740,30 @@
         col_ids >= MARGIN + box.across, as_float(across_pos < across_count - 1), col_mask
     )
     keep = 1.0 + rho_second * rho_first
+    copies = []
 
     def emit(start, values):
         rows = values.reshape(8, box.across, box.deep)
         before = window[first + start : first + start + 8, inner, :]
         shift = own_shift.reshape(1, 1, 1)
         iterate[start : start + 8] = keep * before + (gain * rows + shift)
+        copies.append(
+            pltpu.make_async_copy(
+                iterate.at[start : start + 8], out.at[start : start + 8], sems.at[len(copies)]
+            )
+        )
+        copies[-1].start()
 
     box_solve(
-        box, residual, 0, means_of(means), tables, row_mask, col_mask, spectral, middle, emit
+        box, residual, means_of(means), tables, row_mask, col_mask, spectral, middle, emit
     )
     rows = in_order(is_even("wide"), iterate[box.long - 1], iterate[0])
     top[...], bottom[...] = rows
     flat = iterate.reshape(box.long * box.across, box.deep)
     cols = [flat[row_of(box.across, col, box.long), :] for col in (box.across - 1, 0)]
     last_col[...], first_col[...] = in_order(is_even("narrow"), *cols)
+    for copy in copies:
+        copy.wait()
 
 
 def last_residual(
@@ -767,7 +778,6 @@
     to_across,
     to_deep,
     mass,
-    iterate,
     out,
     window,
     result,
@@ -779,8 +789,6 @@
     window[:, :EDGE, :] = blank
     window[:, EDGE + box.across :, :] = blank
     window[1 : 1 + box.long, inner, :] = partial[...]
-    own = pltpu.make_async_copy(window.at[1 : 1 + box.long, inner, :], iterate, sems.at[0])
-    own.start()
     wide_sides, narrow_sides = Sides("wide", low, high), Sides("narrow", left, right)
     window[0, inner, :] = wide_sides.low(Ellipsis)
     window[1 + box.long, inner, :] = wide_sides.high(Ellipsis)
@@ -797,29 +805,47 @@
 
     flow = to_long[REACH - 1, inner] * (window[1, inner] - window[0, inner])
     chunk = box.long // 4
-    copies = [own]
+    copies = []
     for index in range(4):
         rows = slice(index * chunk, (index + 1) * chunk)
         flow = lax.fori_loop(rows.start, rows.stop, one_row, flow, unroll=4)
-        copy = pltpu.make_async_copy(result.at[rows], out.at[rows], sems.at[1 + index])
+        copy = pltpu.make_async_copy(result.at[rows], out.at[rows], sems.at[index])
         copy.start()
         copies.append(copy)
     for copy in copies:
         copy.wait()
 
 
-def exchange(axis, first, second, around=False):
-    size = lax.axis_size(axis)
-    swaps = []
+def swaps(axis, around):
+    sizes = (lax.axis_size("wide"), lax.axis_size("narrow"))
+    along = ("wide", "narrow").index(axis)
+    size, beside = sizes[along], sizes[1 - along]
+
+    def number(place, other_place):
+        pair = (place, other_place) if along == 0 else (other_place, place)
+        return pair[0] * sizes[1] + pair[1]
+
+    ways = []
     for way in range(2):
         pairs = []
         for place in range(size):
-            other = place + 1 if place % 2 == way else place - 1
-            if around and size % 2 == 0:
-                other %= size
-            pairs.append((place, other if 0 <= other < size else place))
-        swaps.append(pairs)
-    return lax.ppermute(first, axis, swaps[0]), lax.ppermute(second, axis, swaps[1])
+            for other_place in range(beside):
+                partner = place + 1 if place % 2 == way else place - 1
+                there = other_place
+                if around and size % 2 == 0:
+                    partner %= size
+                if not 0 <= partner < size:
+                    partner = place
+                    there = other_place ^ 1 if beside % 2 == 0 else other_place
+                pairs.append((number(place, other_place), number(partner, there)))
+        ways.append(pairs)
+    return ways
+
+
+def exchange(axis, first, second, around=False):
+    ways = swaps(axis, around)
+    axes = ("wide", "narrow")
+    return lax.ppermute(first, axes, ways[0]), lax.ppermute(second, axes, ways[1])
 
 
 def two_away(axis, table):
@@ -918,28 +944,30 @@
     else:
         parts = (tell(own_table),)
     row, col = f32(across, deep), f32(long, deep)
-    iterate, first_row, second_row, first_col, second_col = call(
-        functools.partial(second_solve, box, len(parts)),
-        (cells, row, row, col, col),
-        [VMEM] * (11 + len(parts) + N_TABLES),
-        [
-            scratch(window.shape),
-            scratch((box.ex, box.ey, deep)),
-            spectral,
-            middle,
-            scratch((count, -(-2 * count // 128) * 128)),
-        ],
+    answers = call(
+        functools.partial(coarse_corrections, len(parts)),
+        f32(8, -(-count // 128) * 128),
+        [VMEM] * len(parts),
+        [scratch((count, -(-2 * count // 128) * 128))],
+    )(*parts)
+    iterate, first_row, second_row, first_col, second_col, result = call(
+        functools.partial(second_solve, box),
+        (cells, row, row, col, col, cells),
+        [VMEM] * (12 + N_TABLES),
+        [scratch(window.shape), spectral, middle, pltpu.SemaphoreType.DMA((long // 8,))],
         flops=4 * 10**9,
-    )(local, *wide, *narrow, sums, *parts, *weights, load_window, *tables)
+        out_spec=(VMEM,) * 5 + (anywhere,),
+    )(local, *wide, *narrow, sums, answers, *weights, load_window, *tables)
     narrow = exchange("narrow", first_col, second_col)
     wide = exchange("wide", first_row, second_row)
-    return call(
+    residual = call(
         functools.partial(last_residual, box),
-        (cells, cells),
+        cells,
         [VMEM] * 10,
-        [scratch((long + 2, box.cols, deep)), scratch(cells.shape), pltpu.SemaphoreType.DMA((5,))],
+        [scratch((long + 2, box.cols, deep)), scratch(cells.shape), pltpu.SemaphoreType.DMA((4,))],
         out_spec=anywhere,
     )(load, iterate, *wide, *narrow, *weights)
+    return result, residual
 
 
 def solution(mesh):

time: 69.1 us -> 60.4 us (0.87)
  the two profiles are of different devices: /device:TPU:10 before, /device:TPU:0 now
where the time goes in v9:
time: 60.4 us; the launch traced here: 60.2 us
  Pallas kernels  31.8 us (53%)
  starting transfers between devices  18.1 us (30%)
  waiting for transfers between devices  9.16 us (15%)
  between operations  1.1 us (2%)
    ppermute x8, starting transfers between devices, exchange(): lax.ppermute(first, axes, ways[0])  10.1 us
    pallas_call x1, Pallas kernels, on_device(): call(functools.partial(second_solve, box), (cells, row, row, col, col, ce...  9.62 us
    pallas_call x1, Pallas kernels, on_device(): call(functools.partial(first_solve, box), (window, cells, f32(across, dee...  7.3 us
    ppermute x8, starting transfers between devices, exchange(): lax.ppermute(second, axes, ways[1])  4.56 us
    pallas_call x1, Pallas kernels, on_device(): call(functools.partial(weights_of, box), (window,) * 4, [VMEM] * 6 + [SME...  3.89 us
    ppermute x2, waiting for transfers between devices, two_away(): return lax.ppermute(table, axis, [(i, (i + 2) % size) for i in range(size)])  3.86 us
    pallas_call x1, Pallas kernels, on_device(): call(functools.partial(last_residual, box), cells, [VMEM] * 10, [scratch(...  3.47 us
    ppermute x8, waiting for transfers between devices, exchange(): lax.ppermute(first, axes, ways[0])  3.43 us
  transfers between devices with their start and end apart: 18, of which 4 were waited for; matrix products, arithmetic and copies ran while one was open for 0% of the time, Pallas kernels for 27%

profile of v9, /device:TPU:0, one launch (start us, length us, event | category | flops | bytes accessed | tf_op | source)
XLA Modules:
  0.0 60.2 jit_solution(5382654747284438201)
XLA Ops:
  0.7 1.5 %shard_map.149 = (f32[64,32,128]{2,1,0:T(8,128)S(1)}, f32[4,32,128]{2,1,0:T(8,128)S(1)}, f32[4,32,128]{2,1,0:T(8,128)S(1)}, f32[10,32,128]{2,1,0:T(8,128)S(1)}, f32[10,32,128]{2,1,0:T(8,128)S(1)}) custom-call(s32[64,32,128]{2,1,0:T(8,128)} %far_zone.1, f32[64,32,128]{2,1,0:T(8,128)} %far_scale.1, f32[64,32,128]{2,1,0:T(8,128)} %load.1), custom_call_target="tpu_custom_call" | custom-call | tf_op jit(solution)/shard_map/pallas_call | solution.py:899
  2.2 3.1 %collective-permute-start = (f32[4,32,128]{2,1,0:T(8,128)S(1)}, f32[4,32,128]{2,1,0:T(8,128)S(1)}, u32[]{:S(2)}, u32[]{:S(2)}) collective-permute-start(f32[4,32,128]{2,1,0:T(8,128)S(1)} %get-tuple-element.35), channel_id=1, source_target_pairs={{0,4},{1,5},{2,6},{3,7},{4,0},{5,1},{6,2},{7,3},{8,12},{9,13},{10,... | collective-permute-start | bytes 196616 | tf_op jit(solution)/shard_map/ppermute | solution.py:848
  5.3 3.1 %collective-permute-start.4 = (f32[10,32,128]{2,1,0:T(8,128)S(1)}, f32[10,32,128]{2,1,0:T(8,128)S(1)}, u32[]{:S(2)}, u32[]{:S(2)}) collective-permute-start(f32[10,32,128]{2,1,0:T(8,128)S(1)} %get-tuple-element.44), channel_id=1, source_target_pairs={{0,4},{1,5},{2,6},{3,7},{4,0},{5,1},{6,2},{7,3},{8,12},{9,13},{10,... | collective-permute-start | bytes 491528 | tf_op jit(solution)/shard_map/ppermute | solution.py:848
  8.4 0.2 shard_map.150
  8.6 2.7 %collective-permute-start.3 = (f32[296,128]{1,0:T(8,128)S(1)}, f32[296,128]{1,0:T(8,128)S(1)}, u32[]{:S(2)}, u32[]{:S(2)}) collective-permute-start(f32[296,128]{1,0:T(8,128)S(1)} %get-tuple-element.38), channel_id=1, source_target_pairs={{0,4},{4,0},{8,12},{12,8},{1,2},{5,6},{9,10},{13,14},{2,1},{6,5},{... | collective-permute-start | bytes 454664 | tf_op jit(solution)/shard_map/ppermute | solution.py:848
  11.3 2.7 %shard_map.151 = (s32[64,32,128]{2,1,0:T(8,128)S(1)}, f32[64,32,128]{2,1,0:T(8,128)S(1)}, f32[8,128]{1,0:T(8,128)S(1)}, f32[16,128]{1,0:T(8,128)S(1)}) custom-call(s32[64,32,128]{2,1,0:T(8,128)} %far_zone.1, f32[64,32,128]{2,1,0:T(8,128)} %far_scale.1, f32[64,32,128]{2,1,0:T(8,128)S(1)} %get-tuple-element.34.refs_0_.load, ...), custom_call_target="tpu_custom_call" | custom-call | tf_op jit(solution)/shard_map/pallas_call | solution.py:909
  14.0 0.0 copy-start.2
  14.0 0.0 copy-start.3
  14.1 0.4 shard_map.153
  14.6 0.6 collective-permute-start.6
  15.1 1.2 %collective-permute-start.7 = (f32[744,128]{1,0:T(8,128)S(1)}, f32[744,128]{1,0:T(8,128)S(1)}, u32[]{:S(2)}, u32[]{:S(2)}) collective-permute-start(f32[744,128]{1,0:T(8,128)S(1)} %get-tuple-element.47), channel_id=1, source_target_pairs={{0,4},{4,0},{8,12},{12,8},{1,2},{5,6},{9,10},{13,14},{2,1},{6,5},{... | collective-permute-start | bytes 1142792 | tf_op jit(solution)/shard_map/ppermute | solution.py:848
  16.4 7.3 %shard_map.152 = (f32[74,48,128]{2,1,0:T(8,128)S(1)}, f32[64,32,128]{2,1,0:T(8,128)S(1)}, f32[32,128]{1,0:T(8,128)S(1)}) custom-call(f32[64,32,128]{2,1,0:T(8,128)S(1)} %get-tuple-element.34.refs_0_.load, f32[4,32,128]{2,1,0:T(8,128)S(1)} %collective-permute-done.refs_1_.low, f32[4,32,128]{2,1,0:T(8,128)S(1)} %collective-permute-done.1.refs_2_.high, ...), custom_call_target="tpu_custom_call" | custom-call | flops 4000000000 | tf_op jit(solution)/shard_map/pallas_call | solution.py:916
  23.7 1.0 %shard_map.154 = (f32[16,128]{1,0:T(8,128)S(1)}, f32[176,128]{1,0:T(8,128)S(1)}, f32[176,128]{1,0:T(8,128)S(1)}) custom-call(s32[64,32,128]{2,1,0:T(8,128)S(1)} %get-tuple-element.40.zone.refs_1_, f32[64,32,128]{2,1,0:T(8,128)S(1)} %get-tuple-element.41.scale.refs_0_, f32[64,32,128]{2,1,0:T(8,128)S(1)} %get-tuple-element.42.local.refs_0_, ...), custom_call_target="tpu_custom_call" | custom-call | tf_op jit(solution)/shard_map/pallas_call | solution.py:924
  24.7 2.7 %collective-permute-start.10 = (f32[16,128]{1,0:T(8,128)S(1)}, f32[16,128]{1,0:T(8,128)S(1)}, u32[]{:S(2)}, u32[]{:S(2)}) collective-permute-start(f32[16,128]{1,0:T(8,128)S(1)} %get-tuple-element.51.refs_3_), channel_id=1, source_target_pairs={{0,8},{4,12},{8,0},{12,4},{1,9},{5,13},{9,1},{13,5},{2,10},{6,14},... | collective-permute-start | bytes 24584 | tf_op jit(solution)/shard_map/ppermute | solution.py:853
  27.4 1.2 %collective-permute-start.8 = (f32[176,128]{1,0:T(8,128)S(1)}, f32[176,128]{1,0:T(8,128)S(1)}, u32[]{:S(2)}, u32[]{:S(2)}) collective-permute-start(f32[176,128]{1,0:T(8,128)S(1)} %get-tuple-element.49), channel_id=1, source_target_pairs={{0,4},{1,5},{2,6},{3,7},{4,0},{5,1},{6,2},{7,3},{8,12},{9,13},{10,... | collective-permute-start | bytes 270344 | tf_op jit(solution)/shard_map/ppermute | solution.py:848
  28.6 0.6 collective-permute-start.9
  29.1 3.9 %shard_map.155 = (f32[74,48,128]{2,1,0:T(8,128)S(1)}, f32[74,48,128]{2,1,0:T(8,128)S(1)}, f32[74,48,128]{2,1,0:T(8,128)S(1)}, f32[74,48,128]{2,1,0:T(8,128)S(1)}) custom-call(s32[64,32,128]{2,1,0:T(8,128)S(1)} %get-tuple-element.40.zone.refs_1_, f32[64,32,128]{2,1,0:T(8,128)S(1)} %get-tuple-element.41.scale.refs_0_, ...), custom_call_target="tpu_custom_call" | custom-call | flops 1000000000 | tf_op jit(solution)/shard_map/pallas_call | solution.py:932
  33.1 1.8 %collective-permute-done.9.refs_2_.refs_5_.high = f32[176,128]{1,0:T(8,128)S(1)} collective-permute-done((f32[176,128]{1,0:T(8,128)S(1)}, f32[176,128]{1,0:T(8,128)S(1)}, u32[]{:S(2)}, u32[]{:S(2)}) %collective-permute-start.9) | collective-permute-done | bytes 90144 | tf_op jit(solution)/shard_map/ppermute | solution.py:848
  34.9 0.2 shard_map.156
  35.1 0.1 collective-permute-start.11
  35.2 0.1 collective-permute-start.12
  35.3 1.4 %collective-permute-done.11.message.left = f32[392,128]{1,0:T(8,128)S(1)} collective-permute-done((f32[392,128]{1,0:T(8,128)S(1)}, f32[392,128]{1,0:T(8,128)S(1)}, u32[]{:S(2)}, u32[]{:S(2)}) %collective-permute-start.11) | collective-permute-done | bytes 200736 | tf_op jit(solution)/shard_map/ppermute | solution.py:848
  36.6 0.7 %collective-permute-start.13 = (f32[16,128]{1,0:T(8,128)S(1)}, f32[16,128]{1,0:T(8,128)S(1)}, u32[]{:S(2)}, u32[]{:S(2)}) collective-permute-start(f32[16,128]{1,0:T(8,128)S(1)} %shard_map.157.refs_0_), channel_id=1, source_target_pairs={{0,2},{1,3},{2,0},{3,1},{4,6},{5,7},{6,4},{7,5},{8,10},{9,11},{10,... | collective-permute-start | bytes 24584 | tf_op jit(solution)/shard_map/ppermute | solution.py:853
  37.3 3.9 %collective-permute-done.13.refs_1_ = f32[16,128]{1,0:T(8,128)S(1)} collective-permute-done((f32[16,128]{1,0:T(8,128)S(1)}, f32[16,128]{1,0:T(8,128)S(1)}, u32[]{:S(2)}, u32[]{:S(2)}) %collective-permute-start.13) | collective-permute-done | bytes 8224 | tf_op jit(solution)/shard_map/ppermute | solution.py:853
  41.2 1.5 %shard_map.158.answers = f32[8,128]{1,0:T(8,128)S(1)} custom-call(f32[16,128]{1,0:T(8,128)S(1)} %shard_map.157.refs_0_, f32[16,128]{1,0:T(8,128)S(1)} %collective-permute-done.13.refs_1_), custom_call_target="tpu_custom_call" | custom-call | tf_op jit(solution)/shard_map/pallas_call | solution.py:947
  42.7 0.0 collective-permute-done.12.right
  42.7 9.6 %shard_map.159 = (f32[64,32,128]{2,1,0:T(8,128)S(1)}, f32[32,128]{1,0:T(8,128)S(1)}, f32[32,128]{1,0:T(8,128)S(1)}, f32[64,128]{1,0:T(8,128)S(1)}, f32[64,128]{1,0:T(8,128)S(1)}, /*index=5*/f32[64,32,128]{2,1,0:T(8,128)}) custom-call(f32[64,32,128]{2,1,0:T(8,128)S(1)} %get-tuple-element.42.local.refs_0_, ...), custom_call_target="tpu_custom_call" | custom-call | flops 4000000000 | tf_op jit(solution)/shard_map/pallas_call | solution.py:953
  52.3 0.1 collective-permute-start.16
  52.4 0.1 collective-permute-start.17
  52.5 2.0 %collective-permute-start.14 = (f32[32,128]{1,0:T(8,128)S(1)}, f32[32,128]{1,0:T(8,128)S(1)}, u32[]{:S(2)}, u32[]{:S(2)}) collective-permute-start(f32[32,128]{1,0:T(8,128)S(1)} %get-tuple-element.62), channel_id=1, source_target_pairs={{0,4},{1,5},{2,6},{3,7},{4,0},{5,1},{6,2},{7,3},{8,12},{9,13},{10,... | collective-permute-start | bytes 49160 | tf_op jit(solution)/shard_map/ppermute | solution.py:848
  54.5 2.1 %collective-permute-done.14.low = f32[32,128]{1,0:T(8,128)S(1)} collective-permute-done((f32[32,128]{1,0:T(8,128)S(1)}, f32[32,128]{1,0:T(8,128)S(1)}, u32[]{:S(2)}, u32[]{:S(2)}) %collective-permute-start.14) | collective-permute-done | bytes 16416 | tf_op jit(solution)/shard_map/ppermute | solution.py:848
  56.6 3.5 %shard_map.160 = f32[64,32,128]{2,1,0:T(8,128)} custom-call(f32[64,32,128]{2,1,0:T(8,128)S(1)} %get-tuple-element.34.refs_0_.load, f32[64,32,128]{2,1,0:T(8,128)S(1)} %get-tuple-element.61.partial, f32[32,128]{1,0:T(8,128)S(1)} %collective-permute-done.14.low, f32[32,128]{1,0:T(8,128)S(1)} %collective-permute-done.15.high, ...), custom_call_target="tpu_custom_call" | custom-call | tf_op jit(solution)/shard_map/pallas_call | solution.py:963
  (38 shorter events, 0.1 us)
Async XLA Ops:
  0.6 10.7 %copy-start = (f32[3,3]{1,0:T(4,128)S(1)}, f32[3,3]{1,0:T(4,128)}, u32[]{:S(2)}) copy-start(f32[3,3]{1,0:T(4,128)} %diffusivity.7) | copy-start | bytes 112
  0.6 10.7 %copy-start.1 = (f32[3]{0:T(128)S(1)}, f32[3]{0:T(128)}, u32[]{:S(2)}) copy-start(f32[3]{0:T(128)} %decay.5) | copy-start | bytes 40
  2.2 6.2 %collective-permute-start = (f32[4,32,128]{2,1,0:T(8,128)S(1)}, f32[4,32,128]{2,1,0:T(8,128)S(1)}, u32[]{:S(2)}, u32[]{:S(2)}) collective-permute-start(f32[4,32,128]{2,1,0:T(8,128)S(1)} %get-tuple-element.35), channel_id=1, source_target_pairs={{0,4},{1,5},{2,6},{3,7},{4,0},{5,1},{6,2},{7,3},{8,12},{9,13},{10,... | collective-permute-start | bytes 196616 | tf_op jit(solution)/shard_map/ppermute | solution.py:848
  5.3 3.2 %collective-permute-start.1 = (f32[4,32,128]{2,1,0:T(8,128)S(1)}, f32[4,32,128]{2,1,0:T(8,128)S(1)}, u32[]{:S(2)}, u32[]{:S(2)}) collective-permute-start(f32[4,32,128]{2,1,0:T(8,128)S(1)} %get-tuple-element.36), channel_id=1, source_target_pairs={{0,1},{1,0},{2,3},{3,2},{4,8},{5,9},{6,10},{7,11},{8,4},{9,5},{10,... | collective-permute-start | bytes 196616 | tf_op jit(solution)/shard_map/ppermute | solution.py:848
  5.3 8.8 %collective-permute-start.4 = (f32[10,32,128]{2,1,0:T(8,128)S(1)}, f32[10,32,128]{2,1,0:T(8,128)S(1)}, u32[]{:S(2)}, u32[]{:S(2)}) collective-permute-start(f32[10,32,128]{2,1,0:T(8,128)S(1)} %get-tuple-element.44), channel_id=1, source_target_pairs={{0,4},{1,5},{2,6},{3,7},{4,0},{5,1},{6,2},{7,3},{8,12},{9,13},{10,... | collective-permute-start | bytes 491528 | tf_op jit(solution)/shard_map/ppermute | solution.py:848
  8.4 5.7 %collective-permute-start.5 = (f32[10,32,128]{2,1,0:T(8,128)S(1)}, f32[10,32,128]{2,1,0:T(8,128)S(1)}, u32[]{:S(2)}, u32[]{:S(2)}) collective-permute-start(f32[10,32,128]{2,1,0:T(8,128)S(1)} %get-tuple-element.45), channel_id=1, source_target_pairs={{0,1},{1,0},{2,3},{3,2},{4,8},{5,9},{6,10},{7,11},{8,4},{9,5},{10,... | collective-permute-start | bytes 491528 | tf_op jit(solution)/shard_map/ppermute | solution.py:848
  8.6 7.7 %collective-permute-start.3 = (f32[296,128]{1,0:T(8,128)S(1)}, f32[296,128]{1,0:T(8,128)S(1)}, u32[]{:S(2)}, u32[]{:S(2)}) collective-permute-start(f32[296,128]{1,0:T(8,128)S(1)} %get-tuple-element.38), channel_id=1, source_target_pairs={{0,4},{4,0},{8,12},{12,8},{1,2},{5,6},{9,10},{13,14},{2,1},{6,5},{... | collective-permute-start | bytes 454664 | tf_op jit(solution)/shard_map/ppermute | solution.py:848
  11.3 5.0 %collective-permute-start.2 = (f32[296,128]{1,0:T(8,128)S(1)}, f32[296,128]{1,0:T(8,128)S(1)}, u32[]{:S(2)}, u32[]{:S(2)}) collective-permute-start(f32[296,128]{1,0:T(8,128)S(1)} %get-tuple-element.37.after), channel_id=1, source_target_pairs={{0,1},{4,5},{8,9},{12,13},{1,0},{5,4},{9,8},{13,12},{2,3},{6,7},{1... | collective-permute-start | bytes 454664 | tf_op jit(solution)/shard_map/ppermute | solution.py:848
  14.0 2.3 %copy-start.2 = (bf16[256,256]{1,0:T(8,128)(2,1)S(1)}, bf16[256,256]{1,0:T(8,128)(2,1)}, u32[]{:S(2)}) copy-start(bf16[256,256]{1,0:T(8,128)(2,1)} %constant.22.clone.rest_4_.rest_9_) | copy-start | bytes 393220
  14.0 2.3 %copy-start.3 = (bf16[192,240]{1,0:T(8,128)(2,1)S(1)}, bf16[192,240]{1,0:T(8,128)(2,1)}, u32[]{:S(2)}) copy-start(bf16[192,240]{1,0:T(8,128)(2,1)} %constant.20.clone.rest_2_.rest_7_) | copy-start | bytes 276484
  14.0 2.3 %copy-start.4 = (bf16[144,160]{1,0:T(8,128)(2,1)S(1)}, bf16[144,160]{1,0:T(8,128)(2,1)}, u32[]{:S(2)}) copy-start(bf16[144,160]{1,0:T(8,128)(2,1)} %constant.19.clone.rest_1_.rest_6_) | copy-start | bytes 138244
  14.0 2.3 %copy-start.5 = (bf16[256,128]{1,0:T(8,128)(2,1)S(1)}, bf16[256,128]{1,0:T(8,128)(2,1)}, u32[]{:S(2)}) copy-start(bf16[256,128]{1,0:T(8,128)(2,1)} %constant.23.clone.rest_5_.rest_10_) | copy-start | bytes 196612
  14.0 2.3 %copy-start.6 = (bf16[96,144]{1,0:T(8,128)(2,1)S(1)}, bf16[96,144]{1,0:T(8,128)(2,1)}, u32[]{:S(2)}) copy-start(bf16[96,144]{1,0:T(8,128)(2,1)} %constant.21.clone.rest_3_.rest_8_) | copy-start | bytes 82948
  14.1 2.3 %copy-start.7 = (f32[72,128]{1,0:T(8,128)S(1)}, f32[72,128]{1,0:T(8,128)}, u32[]{:S(2)}) copy-start(f32[72,128]{1,0:T(8,128)} %constant.24.clone.rest_6_.rest_11_) | copy-start | bytes 110596
  14.1 2.3 %copy-start.8 = (bf16[80,96]{1,0:T(8,128)(2,1)S(1)}, bf16[80,96]{1,0:T(8,128)(2,1)}, u32[]{:S(2)}) copy-start(bf16[80,96]{1,0:T(8,128)(2,1)} %constant.18.clone.rest_0_.rest_5_) | copy-start | bytes 46084
  14.1 2.3 %copy-start.9 = (f32[1,40]{1,0:T(1,128)S(1)}, f32[1,40]{1,0:T(1,128)}, u32[]{:S(2)}) copy-start(f32[1,40]{1,0:T(1,128)} %constant.26.clone.rest_8_.rest_13_) | copy-start | bytes 484
  14.1 2.3 %copy-start.10 = (f32[1,128]{1,0:T(1,128)S(1)}, f32[1,128]{1,0:T(1,128)}, u32[]{:S(2)}) copy-start(f32[1,128]{1,0:T(1,128)} %constant.25.clone.rest_7_.rest_12_) | copy-start | bytes 1540
  14.6 9.1 %collective-permute-start.6 = (f32[744,128]{1,0:T(8,128)S(1)}, f32[744,128]{1,0:T(8,128)S(1)}, u32[]{:S(2)}, u32[]{:S(2)}) collective-permute-start(f32[744,128]{1,0:T(8,128)S(1)} %get-tuple-element.46), channel_id=1, source_target_pairs={{0,1},{4,5},{8,9},{12,13},{1,0},{5,4},{9,8},{13,12},{2,3},{6,7},{1... | collective-permute-start | bytes 1142792 | tf_op jit(solution)/shard_map/ppermute | solution.py:848
  15.1 8.6 %collective-permute-start.7 = (f32[744,128]{1,0:T(8,128)S(1)}, f32[744,128]{1,0:T(8,128)S(1)}, u32[]{:S(2)}, u32[]{:S(2)}) collective-permute-start(f32[744,128]{1,0:T(8,128)S(1)} %get-tuple-element.47), channel_id=1, source_target_pairs={{0,4},{4,0},{8,12},{12,8},{1,2},{5,6},{9,10},{13,14},{2,1},{6,5},{... | collective-permute-start | bytes 1142792 | tf_op jit(solution)/shard_map/ppermute | solution.py:848
  24.7 8.3 %collective-permute-start.10 = (f32[16,128]{1,0:T(8,128)S(1)}, f32[16,128]{1,0:T(8,128)S(1)}, u32[]{:S(2)}, u32[]{:S(2)}) collective-permute-start(f32[16,128]{1,0:T(8,128)S(1)} %get-tuple-element.51.refs_3_), channel_id=1, source_target_pairs={{0,8},{4,12},{8,0},{12,4},{1,9},{5,13},{9,1},{13,5},{2,10},{6,14},... | collective-permute-start | bytes 24584 | tf_op jit(solution)/shard_map/ppermute | solution.py:853
  27.4 5.6 %collective-permute-start.8 = (f32[176,128]{1,0:T(8,128)S(1)}, f32[176,128]{1,0:T(8,128)S(1)}, u32[]{:S(2)}, u32[]{:S(2)}) collective-permute-start(f32[176,128]{1,0:T(8,128)S(1)} %get-tuple-element.49), channel_id=1, source_target_pairs={{0,4},{1,5},{2,6},{3,7},{4,0},{5,1},{6,2},{7,3},{8,12},{9,13},{10,... | collective-permute-start | bytes 270344 | tf_op jit(solution)/shard_map/ppermute | solution.py:848
  28.6 6.3 %collective-permute-start.9 = (f32[176,128]{1,0:T(8,128)S(1)}, f32[176,128]{1,0:T(8,128)S(1)}, u32[]{:S(2)}, u32[]{:S(2)}) collective-permute-start(f32[176,128]{1,0:T(8,128)S(1)} %get-tuple-element.50), channel_id=1, source_target_pairs={{0,12},{1,13},{2,14},{3,15},{4,8},{5,9},{6,10},{7,11},{8,4},{9,5},... | collective-permute-start | bytes 270344 | tf_op jit(solution)/shard_map/ppermute | solution.py:848
  35.1 1.5 %collective-permute-start.11 = (f32[392,128]{1,0:T(8,128)S(1)}, f32[392,128]{1,0:T(8,128)S(1)}, u32[]{:S(2)}, u32[]{:S(2)}) collective-permute-start(f32[392,128]{1,0:T(8,128)S(1)} %get-tuple-element.53), channel_id=1, source_target_pairs={{0,1},{4,5},{8,9},{12,13},{1,0},{5,4},{9,8},{13,12},{2,3},{6,7},{1... | collective-permute-start | bytes 602120 | tf_op jit(solution)/shard_map/ppermute | solution.py:848
  35.2 7.5 %collective-permute-start.12 = (f32[392,128]{1,0:T(8,128)S(1)}, f32[392,128]{1,0:T(8,128)S(1)}, u32[]{:S(2)}, u32[]{:S(2)}) collective-permute-start(f32[392,128]{1,0:T(8,128)S(1)} %get-tuple-element.54), channel_id=1, source_target_pairs={{0,4},{4,0},{8,12},{12,8},{1,2},{5,6},{9,10},{13,14},{2,1},{6,5},{... | collective-permute-start | bytes 602120 | tf_op jit(solution)/shard_map/ppermute | solution.py:848
  36.6 4.6 %collective-permute-start.13 = (f32[16,128]{1,0:T(8,128)S(1)}, f32[16,128]{1,0:T(8,128)S(1)}, u32[]{:S(2)}, u32[]{:S(2)}) collective-permute-start(f32[16,128]{1,0:T(8,128)S(1)} %shard_map.157.refs_0_), channel_id=1, source_target_pairs={{0,2},{1,3},{2,0},{3,1},{4,6},{5,7},{6,4},{7,5},{8,10},{9,11},{10,... | collective-permute-start | bytes 24584 | tf_op jit(solution)/shard_map/ppermute | solution.py:853
  52.3 4.2 %collective-permute-start.16 = (f32[64,128]{1,0:T(8,128)S(1)}, f32[64,128]{1,0:T(8,128)S(1)}, u32[]{:S(2)}, u32[]{:S(2)}) collective-permute-start(f32[64,128]{1,0:T(8,128)S(1)} %get-tuple-element.64), channel_id=1, source_target_pairs={{0,1},{4,5},{8,9},{12,13},{1,0},{5,4},{9,8},{13,12},{2,3},{6,7},{1... | collective-permute-start | bytes 98312 | tf_op jit(solution)/shard_map/ppermute | solution.py:848
  52.4 4.2 %collective-permute-start.17 = (f32[64,128]{1,0:T(8,128)S(1)}, f32[64,128]{1,0:T(8,128)S(1)}, u32[]{:S(2)}, u32[]{:S(2)}) collective-permute-start(f32[64,128]{1,0:T(8,128)S(1)} %get-tuple-element.65), channel_id=1, source_target_pairs={{0,4},{4,0},{8,12},{12,8},{1,2},{5,6},{9,10},{13,14},{2,1},{6,5},{... | collective-permute-start | bytes 98312 | tf_op jit(solution)/shard_map/ppermute | solution.py:848
  52.5 4.1 %collective-permute-start.14 = (f32[32,128]{1,0:T(8,128)S(1)}, f32[32,128]{1,0:T(8,128)S(1)}, u32[]{:S(2)}, u32[]{:S(2)}) collective-permute-start(f32[32,128]{1,0:T(8,128)S(1)} %get-tuple-element.62), channel_id=1, source_target_pairs={{0,4},{1,5},{2,6},{3,7},{4,0},{5,1},{6,2},{7,3},{8,12},{9,13},{10,... | collective-permute-start | bytes 49160 | tf_op jit(solution)/shard_map/ppermute | solution.py:848
  54.5 2.1 %collective-permute-start.15 = (f32[32,128]{1,0:T(8,128)S(1)}, f32[32,128]{1,0:T(8,128)S(1)}, u32[]{:S(2)}, u32[]{:S(2)}) collective-permute-start(f32[32,128]{1,0:T(8,128)S(1)} %get-tuple-element.63), channel_id=1, source_target_pairs={{0,1},{1,0},{2,3},{3,2},{4,8},{5,9},{6,10},{7,11},{8,4},{9,5},{10,... | collective-permute-start | bytes 49160 | tf_op jit(solution)/shard_map/ppermute | solution.py:848

commit v10 on v9

--- a/solution.py
+++ b/solution.py
@@ -172,8 +172,6 @@
         mask = jnp.concatenate([row_mask] * FORWARD, axis=1)
         into_x = (into_x.astype(jnp.float32) * mask).astype(jnp.bfloat16)
     from_x, from_y, main_z, rest_z = from_x[...], from_y[...], main_z[...], rest_z[...]
-    spectral_flat = spectral.reshape(box.ey * deep_x, deep)
-    middle_flat = middle.reshape(box.long * deep_y, deep)
     if deep_x > box.ex:
         spectral[:, box.ex :, :] = jnp.zeros((box.ey, deep_x - box.ex, deep), jnp.float32)
     if deep_y > box.ey:
@@ -181,14 +179,14 @@
     for start in range(0, box.ex, 8):
         block = source(start).reshape(8 * box.ey, deep)
         block = dot_right(block, main_z, rest_z, FORWARD).reshape(8, box.ey, deep)
+        rows = []
         for row in range(0, 8, 2):
             pair = jnp.concatenate([block[row], block[row + 1]], axis=1)
             pair = dot_left(into_y, with_rows(pair, deep_y), FORWARD, box.ey)
-            for part in range(2):
-                spectral_flat[pl.ds(start + row + part, box.ey, stride=deep_x), :] = pair[
-                    :, part * deep : (part + 1) * deep
-                ]
+            rows += [pair[:, :deep], pair[:, deep:]]
+        spectral[:, start : start + 8, :] = jnp.swapaxes(jnp.stack(rows), 0, 1)
     base = means[3] + means[0] * spread[...] + means[2] * eig_z[...]
+    cols = []
     for col in range(0, box.ey, 2):
         pair = jnp.concatenate([spectral[col], spectral[col + 1]], axis=1)
         pair = dot_left(into_x, pair, FORWARD, box.ex)
@@ -201,10 +199,10 @@
             axis=1,
         )
         pair = dot_left(from_x, with_rows(pair, deep_x), BACKWARD, box.long)
-        for part in range(2):
-            middle_flat[pl.ds(col + part, box.long, stride=deep_y), :] = pair[
-                :, part * deep : (part + 1) * deep
-            ]
+        cols += [pair[:, :deep], pair[:, deep:]]
+        if len(cols) == 8:
+            middle[:, col - 6 : col + 2, :] = jnp.swapaxes(jnp.stack(cols), 0, 1)
+            cols = []
     for start in range(0, box.long, 8):
         parts = []
         for row in range(start, start + 8, 2):

time: 60.4 us -> 60.2 us (level)
  transfers between devices with their start and end apart: 18 -> 18, of which waited for: 4 -> 4; matrix products, arithmetic and copies ran while one was open for 0% -> 0% of each run, Pallas kernels for 27% -> 26%
where the time goes in v10:
time: 60.2 us; the launch traced here: 60 us
  Pallas kernels  31.6 us (52%)
  starting transfers between devices  18.1 us (30%)
  waiting for transfers between devices  9.17 us (15%)
  between operations  1.1 us (2%)
    ppermute x8, starting transfers between devices, exchange(): lax.ppermute(first, axes, ways[0])  10.1 us
    pallas_call x1, Pallas kernels, on_device(): call(functools.partial(second_solve, box), (cells, row, row, col, col, ce...  9.53 us
    pallas_call x1, Pallas kernels, on_device(): call(functools.partial(first_solve, box), (window, cells, f32(across, dee...  7.18 us
    ppermute x8, starting transfers between devices, exchange(): lax.ppermute(second, axes, ways[1])  4.55 us
    pallas_call x1, Pallas kernels, on_device(): call(functools.partial(weights_of, box), (window,) * 4, [VMEM] * 6 + [SME...  3.89 us
    ppermute x2, waiting for transfers between devices, two_away(): return lax.ppermute(table, axis, [(i, (i + 2) % size) for i in range(size)])  3.86 us
    pallas_call x1, Pallas kernels, on_device(): call(functools.partial(last_residual, box), cells, [VMEM] * 10, [scratch(...  3.47 us
    ppermute x8, waiting for transfers between devices, exchange(): lax.ppermute(first, axes, ways[0])  3.43 us
  transfers between devices with their start and end apart: 18, of which 4 were waited for; matrix products, arithmetic and copies ran while one was open for 0% of the time, Pallas kernels for 26%

profile of v10, /device:TPU:0, one launch (start us, length us, event | category | flops | bytes accessed | tf_op | source)
XLA Modules:
  0.0 60.0 jit_solution(2661316705769525665)
XLA Ops:
  0.7 1.5 %shard_map.149 = (f32[64,32,128]{2,1,0:T(8,128)S(1)}, f32[4,32,128]{2,1,0:T(8,128)S(1)}, f32[4,32,128]{2,1,0:T(8,128)S(1)}, f32[10,32,128]{2,1,0:T(8,128)S(1)}, f32[10,32,128]{2,1,0:T(8,128)S(1)}) custom-call(s32[64,32,128]{2,1,0:T(8,128)} %far_zone.1, f32[64,32,128]{2,1,0:T(8,128)} %far_scale.1, f32[64,32,128]{2,1,0:T(8,128)} %load.1), custom_call_target="tpu_custom_call" | custom-call | tf_op jit(solution)/shard_map/pallas_call | solution.py:897
  2.2 3.1 %collective-permute-start = (f32[4,32,128]{2,1,0:T(8,128)S(1)}, f32[4,32,128]{2,1,0:T(8,128)S(1)}, u32[]{:S(2)}, u32[]{:S(2)}) collective-permute-start(f32[4,32,128]{2,1,0:T(8,128)S(1)} %get-tuple-element.35), channel_id=1, source_target_pairs={{0,4},{1,5},{2,6},{3,7},{4,0},{5,1},{6,2},{7,3},{8,12},{9,13},{10,... | collective-permute-start | bytes 196616 | tf_op jit(solution)/shard_map/ppermute | solution.py:846
  5.3 3.1 %collective-permute-start.4 = (f32[10,32,128]{2,1,0:T(8,128)S(1)}, f32[10,32,128]{2,1,0:T(8,128)S(1)}, u32[]{:S(2)}, u32[]{:S(2)}) collective-permute-start(f32[10,32,128]{2,1,0:T(8,128)S(1)} %get-tuple-element.44), channel_id=1, source_target_pairs={{0,4},{1,5},{2,6},{3,7},{4,0},{5,1},{6,2},{7,3},{8,12},{9,13},{10,... | collective-permute-start | bytes 491528 | tf_op jit(solution)/shard_map/ppermute | solution.py:846
  8.4 0.2 shard_map.150
  8.6 2.7 %collective-permute-start.3 = (f32[296,128]{1,0:T(8,128)S(1)}, f32[296,128]{1,0:T(8,128)S(1)}, u32[]{:S(2)}, u32[]{:S(2)}) collective-permute-start(f32[296,128]{1,0:T(8,128)S(1)} %get-tuple-element.38), channel_id=1, source_target_pairs={{0,4},{4,0},{8,12},{12,8},{1,2},{5,6},{9,10},{13,14},{2,1},{6,5},{... | collective-permute-start | bytes 454664 | tf_op jit(solution)/shard_map/ppermute | solution.py:846
  11.3 2.7 %shard_map.151 = (s32[64,32,128]{2,1,0:T(8,128)S(1)}, f32[64,32,128]{2,1,0:T(8,128)S(1)}, f32[8,128]{1,0:T(8,128)S(1)}, f32[16,128]{1,0:T(8,128)S(1)}) custom-call(s32[64,32,128]{2,1,0:T(8,128)} %far_zone.1, f32[64,32,128]{2,1,0:T(8,128)} %far_scale.1, f32[64,32,128]{2,1,0:T(8,128)S(1)} %get-tuple-element.34.refs_0_.load, ...), custom_call_target="tpu_custom_call" | custom-call | tf_op jit(solution)/shard_map/pallas_call | solution.py:907
  14.0 0.0 copy-start.2
  14.0 0.0 copy-start.3
  14.1 0.4 shard_map.153
  14.6 0.6 collective-permute-start.6
  15.1 1.2 %collective-permute-start.7 = (f32[744,128]{1,0:T(8,128)S(1)}, f32[744,128]{1,0:T(8,128)S(1)}, u32[]{:S(2)}, u32[]{:S(2)}) collective-permute-start(f32[744,128]{1,0:T(8,128)S(1)} %get-tuple-element.47), channel_id=1, source_target_pairs={{0,4},{4,0},{8,12},{12,8},{1,2},{5,6},{9,10},{13,14},{2,1},{6,5},{... | collective-permute-start | bytes 1142792 | tf_op jit(solution)/shard_map/ppermute | solution.py:846
  16.4 7.2 %shard_map.152 = (f32[74,48,128]{2,1,0:T(8,128)S(1)}, f32[64,32,128]{2,1,0:T(8,128)S(1)}, f32[32,128]{1,0:T(8,128)S(1)}) custom-call(f32[64,32,128]{2,1,0:T(8,128)S(1)} %get-tuple-element.34.refs_0_.load, f32[4,32,128]{2,1,0:T(8,128)S(1)} %collective-permute-done.refs_1_.low, f32[4,32,128]{2,1,0:T(8,128)S(1)} %collective-permute-done.1.refs_2_.high, ...), custom_call_target="tpu_custom_call" | custom-call | flops 4000000000 | tf_op jit(solution)/shard_map/pallas_call | solution.py:914
  23.6 1.0 %shard_map.154 = (f32[16,128]{1,0:T(8,128)S(1)}, f32[176,128]{1,0:T(8,128)S(1)}, f32[176,128]{1,0:T(8,128)S(1)}) custom-call(s32[64,32,128]{2,1,0:T(8,128)S(1)} %get-tuple-element.40.zone.refs_1_, f32[64,32,128]{2,1,0:T(8,128)S(1)} %get-tuple-element.41.scale.refs_0_, f32[64,32,128]{2,1,0:T(8,128)S(1)} %get-tuple-element.42.local.refs_0_, ...), custom_call_target="tpu_custom_call" | custom-call | tf_op jit(solution)/shard_map/pallas_call | solution.py:922
  24.6 2.7 %collective-permute-start.10 = (f32[16,128]{1,0:T(8,128)S(1)}, f32[16,128]{1,0:T(8,128)S(1)}, u32[]{:S(2)}, u32[]{:S(2)}) collective-permute-start(f32[16,128]{1,0:T(8,128)S(1)} %get-tuple-element.51.refs_3_), channel_id=1, source_target_pairs={{0,8},{4,12},{8,0},{12,4},{1,9},{5,13},{9,1},{13,5},{2,10},{6,14},... | collective-permute-start | bytes 24584 | tf_op jit(solution)/shard_map/ppermute | solution.py:851
  27.3 1.2 %collective-permute-start.8 = (f32[176,128]{1,0:T(8,128)S(1)}, f32[176,128]{1,0:T(8,128)S(1)}, u32[]{:S(2)}, u32[]{:S(2)}) collective-permute-start(f32[176,128]{1,0:T(8,128)S(1)} %get-tuple-element.49), channel_id=1, source_target_pairs={{0,4},{1,5},{2,6},{3,7},{4,0},{5,1},{6,2},{7,3},{8,12},{9,13},{10,... | collective-permute-start | bytes 270344 | tf_op jit(solution)/shard_map/ppermute | solution.py:846
  28.5 0.6 collective-permute-start.9
  29.0 3.9 %shard_map.155 = (f32[74,48,128]{2,1,0:T(8,128)S(1)}, f32[74,48,128]{2,1,0:T(8,128)S(1)}, f32[74,48,128]{2,1,0:T(8,128)S(1)}, f32[74,48,128]{2,1,0:T(8,128)S(1)}) custom-call(s32[64,32,128]{2,1,0:T(8,128)S(1)} %get-tuple-element.40.zone.refs_1_, f32[64,32,128]{2,1,0:T(8,128)S(1)} %get-tuple-element.41.scale.refs_0_, ...), custom_call_target="tpu_custom_call" | custom-call | flops 1000000000 | tf_op jit(solution)/shard_map/pallas_call | solution.py:930
  32.9 1.8 %collective-permute-done.9.refs_2_.refs_5_.high = f32[176,128]{1,0:T(8,128)S(1)} collective-permute-done((f32[176,128]{1,0:T(8,128)S(1)}, f32[176,128]{1,0:T(8,128)S(1)}, u32[]{:S(2)}, u32[]{:S(2)}) %collective-permute-start.9) | collective-permute-done | bytes 90144 | tf_op jit(solution)/shard_map/ppermute | solution.py:846
  34.8 0.2 shard_map.156
  35.0 0.1 collective-permute-start.11
  35.1 0.1 collective-permute-start.12
  35.2 1.4 %collective-permute-done.11.message.left = f32[392,128]{1,0:T(8,128)S(1)} collective-permute-done((f32[392,128]{1,0:T(8,128)S(1)}, f32[392,128]{1,0:T(8,128)S(1)}, u32[]{:S(2)}, u32[]{:S(2)}) %collective-permute-start.11) | collective-permute-done | bytes 200736 | tf_op jit(solution)/shard_map/ppermute | solution.py:846
  36.5 0.7 %collective-permute-start.13 = (f32[16,128]{1,0:T(8,128)S(1)}, f32[16,128]{1,0:T(8,128)S(1)}, u32[]{:S(2)}, u32[]{:S(2)}) collective-permute-start(f32[16,128]{1,0:T(8,128)S(1)} %shard_map.157.refs_0_), channel_id=1, source_target_pairs={{0,2},{1,3},{2,0},{3,1},{4,6},{5,7},{6,4},{7,5},{8,10},{9,11},{10,... | collective-permute-start | bytes 24584 | tf_op jit(solution)/shard_map/ppermute | solution.py:851
  37.2 3.9 %collective-permute-done.13.refs_1_ = f32[16,128]{1,0:T(8,128)S(1)} collective-permute-done((f32[16,128]{1,0:T(8,128)S(1)}, f32[16,128]{1,0:T(8,128)S(1)}, u32[]{:S(2)}, u32[]{:S(2)}) %collective-permute-start.13) | collective-permute-done | bytes 8224 | tf_op jit(solution)/shard_map/ppermute | solution.py:851
  41.1 1.5 %shard_map.158.answers = f32[8,128]{1,0:T(8,128)S(1)} custom-call(f32[16,128]{1,0:T(8,128)S(1)} %shard_map.157.refs_0_, f32[16,128]{1,0:T(8,128)S(1)} %collective-permute-done.13.refs_1_), custom_call_target="tpu_custom_call" | custom-call | tf_op jit(solution)/shard_map/pallas_call | solution.py:945
  42.6 0.0 collective-permute-done.12.right
  42.6 9.5 %shard_map.159 = (f32[64,32,128]{2,1,0:T(8,128)S(1)}, f32[32,128]{1,0:T(8,128)S(1)}, f32[32,128]{1,0:T(8,128)S(1)}, f32[64,128]{1,0:T(8,128)S(1)}, f32[64,128]{1,0:T(8,128)S(1)}, /*index=5*/f32[64,32,128]{2,1,0:T(8,128)}) custom-call(f32[64,32,128]{2,1,0:T(8,128)S(1)} %get-tuple-element.42.local.refs_0_, ...), custom_call_target="tpu_custom_call" | custom-call | flops 4000000000 | tf_op jit(solution)/shard_map/pallas_call | solution.py:951
  52.1 0.1 collective-permute-start.16
  52.2 0.1 collective-permute-start.17
  52.3 2.0 %collective-permute-start.14 = (f32[32,128]{1,0:T(8,128)S(1)}, f32[32,128]{1,0:T(8,128)S(1)}, u32[]{:S(2)}, u32[]{:S(2)}) collective-permute-start(f32[32,128]{1,0:T(8,128)S(1)} %get-tuple-element.62), channel_id=1, source_target_pairs={{0,4},{1,5},{2,6},{3,7},{4,0},{5,1},{6,2},{7,3},{8,12},{9,13},{10,... | collective-permute-start | bytes 49160 | tf_op jit(solution)/shard_map/ppermute | solution.py:846
  54.3 2.1 %collective-permute-done.14.low = f32[32,128]{1,0:T(8,128)S(1)} collective-permute-done((f32[32,128]{1,0:T(8,128)S(1)}, f32[32,128]{1,0:T(8,128)S(1)}, u32[]{:S(2)}, u32[]{:S(2)}) %collective-permute-start.14) | collective-permute-done | bytes 16416 | tf_op jit(solution)/shard_map/ppermute | solution.py:846
  56.4 3.5 %shard_map.160 = f32[64,32,128]{2,1,0:T(8,128)} custom-call(f32[64,32,128]{2,1,0:T(8,128)S(1)} %get-tuple-element.34.refs_0_.load, f32[64,32,128]{2,1,0:T(8,128)S(1)} %get-tuple-element.61.partial, f32[32,128]{1,0:T(8,128)S(1)} %collective-permute-done.14.low, f32[32,128]{1,0:T(8,128)S(1)} %collective-permute-done.15.high, ...), custom_call_target="tpu_custom_call" | custom-call | tf_op jit(solution)/shard_map/pallas_call | solution.py:961
  (38 shorter events, 0.1 us)
Async XLA Ops:
  0.6 10.7 %copy-start = (f32[3,3]{1,0:T(4,128)S(1)}, f32[3,3]{1,0:T(4,128)}, u32[]{:S(2)}) copy-start(f32[3,3]{1,0:T(4,128)} %diffusivity.7) | copy-start | bytes 112
  0.6 10.7 %copy-start.1 = (f32[3]{0:T(128)S(1)}, f32[3]{0:T(128)}, u32[]{:S(2)}) copy-start(f32[3]{0:T(128)} %decay.5) | copy-start | bytes 40
  2.2 6.2 %collective-permute-start = (f32[4,32,128]{2,1,0:T(8,128)S(1)}, f32[4,32,128]{2,1,0:T(8,128)S(1)}, u32[]{:S(2)}, u32[]{:S(2)}) collective-permute-start(f32[4,32,128]{2,1,0:T(8,128)S(1)} %get-tuple-element.35), channel_id=1, source_target_pairs={{0,4},{1,5},{2,6},{3,7},{4,0},{5,1},{6,2},{7,3},{8,12},{9,13},{10,... | collective-permute-start | bytes 196616 | tf_op jit(solution)/shard_map/ppermute | solution.py:846
  5.3 3.2 %collective-permute-start.1 = (f32[4,32,128]{2,1,0:T(8,128)S(1)}, f32[4,32,128]{2,1,0:T(8,128)S(1)}, u32[]{:S(2)}, u32[]{:S(2)}) collective-permute-start(f32[4,32,128]{2,1,0:T(8,128)S(1)} %get-tuple-element.36), channel_id=1, source_target_pairs={{0,1},{1,0},{2,3},{3,2},{4,8},{5,9},{6,10},{7,11},{8,4},{9,5},{10,... | collective-permute-start | bytes 196616 | tf_op jit(solution)/shard_map/ppermute | solution.py:846
  5.3 8.8 %collective-permute-start.4 = (f32[10,32,128]{2,1,0:T(8,128)S(1)}, f32[10,32,128]{2,1,0:T(8,128)S(1)}, u32[]{:S(2)}, u32[]{:S(2)}) collective-permute-start(f32[10,32,128]{2,1,0:T(8,128)S(1)} %get-tuple-element.44), channel_id=1, source_target_pairs={{0,4},{1,5},{2,6},{3,7},{4,0},{5,1},{6,2},{7,3},{8,12},{9,13},{10,... | collective-permute-start | bytes 491528 | tf_op jit(solution)/shard_map/ppermute | solution.py:846
  8.4 5.7 %collective-permute-start.5 = (f32[10,32,128]{2,1,0:T(8,128)S(1)}, f32[10,32,128]{2,1,0:T(8,128)S(1)}, u32[]{:S(2)}, u32[]{:S(2)}) collective-permute-start(f32[10,32,128]{2,1,0:T(8,128)S(1)} %get-tuple-element.45), channel_id=1, source_target_pairs={{0,1},{1,0},{2,3},{3,2},{4,8},{5,9},{6,10},{7,11},{8,4},{9,5},{10,... | collective-permute-start | bytes 491528 | tf_op jit(solution)/shard_map/ppermute | solution.py:846
  8.6 7.7 %collective-permute-start.3 = (f32[296,128]{1,0:T(8,128)S(1)}, f32[296,128]{1,0:T(8,128)S(1)}, u32[]{:S(2)}, u32[]{:S(2)}) collective-permute-start(f32[296,128]{1,0:T(8,128)S(1)} %get-tuple-element.38), channel_id=1, source_target_pairs={{0,4},{4,0},{8,12},{12,8},{1,2},{5,6},{9,10},{13,14},{2,1},{6,5},{... | collective-permute-start | bytes 454664 | tf_op jit(solution)/shard_map/ppermute | solution.py:846
  11.3 5.0 %collective-permute-start.2 = (f32[296,128]{1,0:T(8,128)S(1)}, f32[296,128]{1,0:T(8,128)S(1)}, u32[]{:S(2)}, u32[]{:S(2)}) collective-permute-start(f32[296,128]{1,0:T(8,128)S(1)} %get-tuple-element.37.after), channel_id=1, source_target_pairs={{0,1},{4,5},{8,9},{12,13},{1,0},{5,4},{9,8},{13,12},{2,3},{6,7},{1... | collective-permute-start | bytes 454664 | tf_op jit(solution)/shard_map/ppermute | solution.py:846
  14.0 2.3 %copy-start.2 = (bf16[256,256]{1,0:T(8,128)(2,1)S(1)}, bf16[256,256]{1,0:T(8,128)(2,1)}, u32[]{:S(2)}) copy-start(bf16[256,256]{1,0:T(8,128)(2,1)} %constant.22.clone.rest_4_.rest_9_) | copy-start | bytes 393220
  14.0 2.3 %copy-start.3 = (bf16[192,240]{1,0:T(8,128)(2,1)S(1)}, bf16[192,240]{1,0:T(8,128)(2,1)}, u32[]{:S(2)}) copy-start(bf16[192,240]{1,0:T(8,128)(2,1)} %constant.20.clone.rest_2_.rest_7_) | copy-start | bytes 276484
  14.0 2.3 %copy-start.4 = (bf16[144,160]{1,0:T(8,128)(2,1)S(1)}, bf16[144,160]{1,0:T(8,128)(2,1)}, u32[]{:S(2)}) copy-start(bf16[144,160]{1,0:T(8,128)(2,1)} %constant.19.clone.rest_1_.rest_6_) | copy-start | bytes 138244
  14.0 2.3 %copy-start.5 = (bf16[256,128]{1,0:T(8,128)(2,1)S(1)}, bf16[256,128]{1,0:T(8,128)(2,1)}, u32[]{:S(2)}) copy-start(bf16[256,128]{1,0:T(8,128)(2,1)} %constant.23.clone.rest_5_.rest_10_) | copy-start | bytes 196612
  14.0 2.3 %copy-start.6 = (bf16[96,144]{1,0:T(8,128)(2,1)S(1)}, bf16[96,144]{1,0:T(8,128)(2,1)}, u32[]{:S(2)}) copy-start(bf16[96,144]{1,0:T(8,128)(2,1)} %constant.21.clone.rest_3_.rest_8_) | copy-start | bytes 82948
  14.1 2.3 %copy-start.7 = (f32[72,128]{1,0:T(8,128)S(1)}, f32[72,128]{1,0:T(8,128)}, u32[]{:S(2)}) copy-start(f32[72,128]{1,0:T(8,128)} %constant.24.clone.rest_6_.rest_11_) | copy-start | bytes 110596
  14.1 2.3 %copy-start.8 = (bf16[80,96]{1,0:T(8,128)(2,1)S(1)}, bf16[80,96]{1,0:T(8,128)(2,1)}, u32[]{:S(2)}) copy-start(bf16[80,96]{1,0:T(8,128)(2,1)} %constant.18.clone.rest_0_.rest_5_) | copy-start | bytes 46084
  14.1 2.3 %copy-start.9 = (f32[1,40]{1,0:T(1,128)S(1)}, f32[1,40]{1,0:T(1,128)}, u32[]{:S(2)}) copy-start(f32[1,40]{1,0:T(1,128)} %constant.26.clone.rest_8_.rest_13_) | copy-start | bytes 484
  14.1 2.3 %copy-start.10 = (f32[1,128]{1,0:T(1,128)S(1)}, f32[1,128]{1,0:T(1,128)}, u32[]{:S(2)}) copy-start(f32[1,128]{1,0:T(1,128)} %constant.25.clone.rest_7_.rest_12_) | copy-start | bytes 1540
  14.6 9.0 %collective-permute-start.6 = (f32[744,128]{1,0:T(8,128)S(1)}, f32[744,128]{1,0:T(8,128)S(1)}, u32[]{:S(2)}, u32[]{:S(2)}) collective-permute-start(f32[744,128]{1,0:T(8,128)S(1)} %get-tuple-element.46), channel_id=1, source_target_pairs={{0,1},{4,5},{8,9},{12,13},{1,0},{5,4},{9,8},{13,12},{2,3},{6,7},{1... | collective-permute-start | bytes 1142792 | tf_op jit(solution)/shard_map/ppermute | solution.py:846
  15.1 8.5 %collective-permute-start.7 = (f32[744,128]{1,0:T(8,128)S(1)}, f32[744,128]{1,0:T(8,128)S(1)}, u32[]{:S(2)}, u32[]{:S(2)}) collective-permute-start(f32[744,128]{1,0:T(8,128)S(1)} %get-tuple-element.47), channel_id=1, source_target_pairs={{0,4},{4,0},{8,12},{12,8},{1,2},{5,6},{9,10},{13,14},{2,1},{6,5},{... | collective-permute-start | bytes 1142792 | tf_op jit(solution)/shard_map/ppermute | solution.py:846
  24.6 8.3 %collective-permute-start.10 = (f32[16,128]{1,0:T(8,128)S(1)}, f32[16,128]{1,0:T(8,128)S(1)}, u32[]{:S(2)}, u32[]{:S(2)}) collective-permute-start(f32[16,128]{1,0:T(8,128)S(1)} %get-tuple-element.51.refs_3_), channel_id=1, source_target_pairs={{0,8},{4,12},{8,0},{12,4},{1,9},{5,13},{9,1},{13,5},{2,10},{6,14},... | collective-permute-start | bytes 24584 | tf_op jit(solution)/shard_map/ppermute | solution.py:851
  27.3 5.6 %collective-permute-start.8 = (f32[176,128]{1,0:T(8,128)S(1)}, f32[176,128]{1,0:T(8,128)S(1)}, u32[]{:S(2)}, u32[]{:S(2)}) collective-permute-start(f32[176,128]{1,0:T(8,128)S(1)} %get-tuple-element.49), channel_id=1, source_target_pairs={{0,4},{1,5},{2,6},{3,7},{4,0},{5,1},{6,2},{7,3},{8,12},{9,13},{10,... | collective-permute-start | bytes 270344 | tf_op jit(solution)/shard_map/ppermute | solution.py:846
  28.5 6.3 %collective-permute-start.9 = (f32[176,128]{1,0:T(8,128)S(1)}, f32[176,128]{1,0:T(8,128)S(1)}, u32[]{:S(2)}, u32[]{:S(2)}) collective-permute-start(f32[176,128]{1,0:T(8,128)S(1)} %get-tuple-element.50), channel_id=1, source_target_pairs={{0,12},{1,13},{2,14},{3,15},{4,8},{5,9},{6,10},{7,11},{8,4},{9,5},... | collective-permute-start | bytes 270344 | tf_op jit(solution)/shard_map/ppermute | solution.py:846
  35.0 1.5 %collective-permute-start.11 = (f32[392,128]{1,0:T(8,128)S(1)}, f32[392,128]{1,0:T(8,128)S(1)}, u32[]{:S(2)}, u32[]{:S(2)}) collective-permute-start(f32[392,128]{1,0:T(8,128)S(1)} %get-tuple-element.53), channel_id=1, source_target_pairs={{0,1},{4,5},{8,9},{12,13},{1,0},{5,4},{9,8},{13,12},{2,3},{6,7},{1... | collective-permute-start | bytes 602120 | tf_op jit(solution)/shard_map/ppermute | solution.py:846
  35.1 7.5 %collective-permute-start.12 = (f32[392,128]{1,0:T(8,128)S(1)}, f32[392,128]{1,0:T(8,128)S(1)}, u32[]{:S(2)}, u32[]{:S(2)}) collective-permute-start(f32[392,128]{1,0:T(8,128)S(1)} %get-tuple-element.54), channel_id=1, source_target_pairs={{0,4},{4,0},{8,12},{12,8},{1,2},{5,6},{9,10},{13,14},{2,1},{6,5},{... | collective-permute-start | bytes 602120 | tf_op jit(solution)/shard_map/ppermute | solution.py:846
  36.5 4.6 %collective-permute-start.13 = (f32[16,128]{1,0:T(8,128)S(1)}, f32[16,128]{1,0:T(8,128)S(1)}, u32[]{:S(2)}, u32[]{:S(2)}) collective-permute-start(f32[16,128]{1,0:T(8,128)S(1)} %shard_map.157.refs_0_), channel_id=1, source_target_pairs={{0,2},{1,3},{2,0},{3,1},{4,6},{5,7},{6,4},{7,5},{8,10},{9,11},{10,... | collective-permute-start | bytes 24584 | tf_op jit(solution)/shard_map/ppermute | solution.py:851
  52.1 4.2 %collective-permute-start.16 = (f32[64,128]{1,0:T(8,128)S(1)}, f32[64,128]{1,0:T(8,128)S(1)}, u32[]{:S(2)}, u32[]{:S(2)}) collective-permute-start(f32[64,128]{1,0:T(8,128)S(1)} %get-tuple-element.64), channel_id=1, source_target_pairs={{0,1},{4,5},{8,9},{12,13},{1,0},{5,4},{9,8},{13,12},{2,3},{6,7},{1... | collective-permute-start | bytes 98312 | tf_op jit(solution)/shard_map/ppermute | solution.py:846
  52.2 4.2 %collective-permute-start.17 = (f32[64,128]{1,0:T(8,128)S(1)}, f32[64,128]{1,0:T(8,128)S(1)}, u32[]{:S(2)}, u32[]{:S(2)}) collective-permute-start(f32[64,128]{1,0:T(8,128)S(1)} %get-tuple-element.65), channel_id=1, source_target_pairs={{0,4},{4,0},{8,12},{12,8},{1,2},{5,6},{9,10},{13,14},{2,1},{6,5},{... | collective-permute-start | bytes 98312 | tf_op jit(solution)/shard_map/ppermute | solution.py:846
  52.3 4.1 %collective-permute-start.14 = (f32[32,128]{1,0:T(8,128)S(1)}, f32[32,128]{1,0:T(8,128)S(1)}, u32[]{:S(2)}, u32[]{:S(2)}) collective-permute-start(f32[32,128]{1,0:T(8,128)S(1)} %get-tuple-element.62), channel_id=1, source_target_pairs={{0,4},{1,5},{2,6},{3,7},{4,0},{5,1},{6,2},{7,3},{8,12},{9,13},{10,... | collective-permute-start | bytes 49160 | tf_op jit(solution)/shard_map/ppermute | solution.py:846
  54.3 2.1 %collective-permute-start.15 = (f32[32,128]{1,0:T(8,128)S(1)}, f32[32,128]{1,0:T(8,128)S(1)}, u32[]{:S(2)}, u32[]{:S(2)}) collective-permute-start(f32[32,128]{1,0:T(8,128)S(1)} %get-tuple-element.63), channel_id=1, source_target_pairs={{0,1},{1,0},{2,3},{3,2},{4,8},{5,9},{6,10},{7,11},{8,4},{9,5},{10,... | collective-permute-start | bytes 49160 | tf_op jit(solution)/shard_map/ppermute | solution.py:846

commit v11 on v9

--- a/solution.py
+++ b/solution.py
@@ -36,7 +36,7 @@
     return table.astype(np.float32), eigvals.astype(np.float32)
 
 
-def call(body, out_shape, in_specs, scratch=(), flops=0, moved=0, out_spec=None):
+def call(body, out_shape, in_specs, scratch=(), flops=0, out_spec=None, aliases=None):
     return pl.pallas_call(
         body,
         out_shape=out_shape,
@@ -44,7 +44,8 @@
         out_specs=out_spec or jax.tree.map(lambda _: VMEM, out_shape),
         scratch_shapes=list(scratch),
         compiler_params=pltpu.CompilerParams(vmem_limit_bytes=30 * 2**20),
-        cost_estimate=pl.CostEstimate(flops=flops, bytes_accessed=moved, transcendentals=0),
+        cost_estimate=pl.CostEstimate(flops=flops, bytes_accessed=0, transcendentals=0),
+        input_output_aliases=aliases or {},
     )
 
 
@@ -161,8 +162,8 @@
     return jnp.concatenate([values, blank], axis=0)
 
 
-def box_solve(box, source, means, tables, row_mask, col_mask, spectral, middle, emit):
-    into_y, into_x, from_x, from_y, main_z, rest_z, spread, eig_z, eig_y = tables
+def box_solve(box, source, divided, tables, row_mask, col_mask, spectral, middle, emit):
+    into_y, into_x, from_x, from_y, main_z, rest_z = tables[:6]
     deep = box.deep
     deep_x, deep_y = padded(box.ex), padded(box.ey)
     into_y, into_x = into_y[...], into_x[...]
@@ -188,14 +189,12 @@
                 spectral_flat[pl.ds(start + row + part, box.ey, stride=deep_x), :] = pair[
                     :, part * deep : (part + 1) * deep
                 ]
-    base = means[3] + means[0] * spread[...] + means[2] * eig_z[...]
     for col in range(0, box.ey, 2):
         pair = jnp.concatenate([spectral[col], spectral[col + 1]], axis=1)
         pair = dot_left(into_x, pair, FORWARD, box.ex)
         pair = jnp.concatenate(
             [
-                pair[:, part * deep : (part + 1) * deep]
-                / (base + means[1] * eig_y[0, col + part])
+                divided(pair[:, part * deep : (part + 1) * deep], col + part)
                 for part in range(2)
             ],
             axis=1,
@@ -405,8 +404,8 @@
     box, far_zone, far_scale, load, after, diffusivity, decay, zone, scale, out, table, sems
 ):
     del after
-    parts = 2
-    size = box.long // parts
+    size = 8
+    parts = box.long // size
     copies = []
     for part in range(parts):
         rows = slice(part * size, (part + 1) * size)
@@ -416,7 +415,6 @@
             )
             copy.start()
             copies.append(copy)
-    step = 4
     nothing = jnp.zeros((box.across, box.deep), jnp.float32)
     half = [[0.5 * diffusivity[z, d] for z in range(3)] for d in range(3)]
     rates = [decay[z] for z in range(3)]
@@ -424,19 +422,13 @@
     def halves(row):
         labels, factor = zone[row], scale[row]
         return [looked_up(labels, half[d]) * factor for d in range(3)] + [looked_up(labels, rates)]
-
-    def some_rows(index, sums):
-        for row in range(step):
-            row = index * step + row
-            sums = [total + more for total, more in zip(sums, halves(row) + [load[row]])]
-        return sums
 
     sums = [nothing] * 5
     for part in range(parts):
         for copy in copies[2 * part : 2 * part + 2]:
             copy.wait()
-        per_part = size // step
-        sums = lax.fori_loop(part * per_part, (part + 1) * per_part, some_rows, sums)
+        for row in range(part * size, (part + 1) * size):
+            sums = [total + more for total, more in zip(sums, halves(row) + [load[row]])]
 
     def total(values):
         return jnp.sum(values, keepdims=True).reshape(1, 1)
@@ -465,7 +457,16 @@
 
 def first_solve(box, load, low, high, left, right, means, zone, scale, diffusivity, decay, *rest):
     tables = rest[:N_TABLES]
-    window, local, image, spectral, middle = rest[N_TABLES:]
+    window, local, image, inverses, spectral, middle = rest[N_TABLES:]
+    spread, eig_z, eig_y = tables[6:]
+    means = means_of(means)
+    base = means[3] + means[0] * spread[...] + means[2] * eig_z[...]
+
+    def divided(values, col):
+        inverse = 1.0 / (base + means[1] * eig_y[0, col])
+        inverses[col] = inverse
+        return values * inverse
+
     half = [0.5 * diffusivity[z, 2] for z in range(3)]
     rates = [decay[z] for z in range(3)]
     lane = lax.broadcasted_iota(jnp.int32, (box.across, box.deep), 1)
@@ -488,7 +489,7 @@
     box_solve(
         box,
         lambda row: window[1 + row : 9 + row, EDGE - MARGIN : EDGE + box.across + MARGIN],
-        means_of(means),
+        divided,
         tables,
         None,
         None,
@@ -498,47 +499,57 @@
     )
 
 
-def weights_of(
-    box,
-    zone,
-    scale,
-    low,
-    high,
-    left,
-    right,
-    diffusivity,
-    decay,
-    to_long,
-    to_across,
-    to_deep,
-    mass,
-    zone_window,
-    scale_window,
+def side_weights(
+    box, zone, scale, low, high, left, right, diffusivity, to_long, to_across, zone_window,
+    scale_window
 ):
     for index, (window, own) in enumerate(((scale_window, scale), (zone_window, zone))):
         start = index * REACH
         wide_sides = Sides("wide", *(ref.at[start : start + REACH] for ref in (low, high)))
         narrow_sides = Sides("narrow", left, right)
         fill_window(box, window, own, wide_sides, narrow_sides, REACH, start, 2 * REACH)
-    half = [[0.5 * diffusivity[z, d] for d in range(3)] for z in range(3)]
+    half = [[0.5 * diffusivity[z, d] for z in range(3)] for d in range(2)]
+
+    def one_row(row, before):
+        labels, factor = zone_window[row], scale_window[row]
+        now = [looked_up(labels, half[d]) * factor for d in range(2)]
+        to_across[row] = now[1] + pltpu.roll(now[1], box.cols - 1, 0)
+        to_long[jnp.maximum(row - 1, 0)] = before + now[0]
+        return now[0]
+
+    def some_rows(index, before):
+        for row in range(8):
+            before = one_row(index * 8 + row, before)
+        return before
+
+    before = jnp.zeros((box.cols, box.deep), jnp.float32)
+    before = lax.fori_loop(0, box.rows // 8, some_rows, before)
+    for row in range(box.rows // 8 * 8, box.rows):
+        before = one_row(row, before)
+    to_long[box.rows - 1] = before
+
+
+def deep_weights(box, zone_window, scale_window, diffusivity, decay, to_deep, mass):
+    half = [0.5 * diffusivity[z, 2] for z in range(3)]
     rates = [decay[z] for z in range(3)]
     lane = lax.broadcasted_iota(jnp.int32, (box.cols, box.deep), 1)
     ends = jnp.where((lane == 0) | (lane == box.deep - 1), jnp.float32(1.0), jnp.float32(0.0))
     not_last = jnp.where(lane == box.deep - 1, jnp.float32(0.0), jnp.float32(1.0))
 
-    def one_row(row, before):
-        labels, factor = zone_window[row], scale_window[row]
-        now = [looked_up(labels, [half[z][d] for z in range(3)]) * factor for d in range(3)]
-        to_across[row] = now[1] + pltpu.roll(now[1], box.cols - 1, 0)
-        to_deep[row] = (now[2] + pltpu.roll(now[2], box.deep - 1, 1)) * not_last
-        mass[row] = looked_up(labels, rates) + now[2] * ends
-        to_long[jnp.maximum(row - 1, 0)] = before + now[0]
-        return now[0]
-
-    last_long = lax.fori_loop(0, box.rows - 2, one_row, jnp.zeros_like(ends), unroll=4)
-    for row in range(box.rows - 2, box.rows):
-        last_long = one_row(row, last_long)
-    to_long[box.rows - 1] = last_long
+    def one_row(row):
+        labels = zone_window[row]
+        now = looked_up(labels, half) * scale_window[row]
+        to_deep[row] = (now + pltpu.roll(now, box.deep - 1, 1)) * not_last
+        mass[row] = looked_up(labels, rates) + now * ends
+
+    def some_rows(index, _):
+        for row in range(8):
+            one_row(index * 8 + row)
+        return 0
+
+    lax.fori_loop(0, box.rows // 8, some_rows, 0)
+    for row in range(box.rows // 8 * 8, box.rows):
+        one_row(row)
 
 
 def image_sums(
@@ -690,7 +701,7 @@
     out[1:2, :] = answer(inverse, sums) * gain
 
 
-def second_solve(box, local, low, high, left, right, means, answers, *rest):
+def second_solve(box, local, low, high, left, right, inverses, answers, *rest):
     to_long, to_across, to_deep, mass, load_window = rest[:5]
     tables = rest[5 : 5 + N_TABLES]
     iterate, top, bottom, last_col, first_col, out = rest[5 + N_TABLES : 11 + N_TABLES]
@@ -722,6 +733,9 @@
 
     flow = [to_long[0, start:stop] * (window[1, start:stop] - window[0, start:stop])]
 
+    def divided(values, col):
+        return values * inverses[col]
+
     def residual(start_row):
         rows = []
         for row in range(start_row + 1, start_row + 9):
@@ -755,7 +769,7 @@
         copies[-1].start()
 
     box_solve(
-        box, residual, means_of(means), tables, row_mask, col_mask, spectral, middle, emit
+        box, residual, divided, tables, row_mask, col_mask, spectral, middle, emit
     )
     rows = in_order(is_even("wide"), iterate[box.long - 1], iterate[0])
     top[...], bottom[...] = rows
@@ -766,50 +780,82 @@
         copy.wait()
 
 
-def last_residual(
-    box,
-    load,
-    partial,
-    low,
-    high,
-    left,
-    right,
-    to_long,
-    to_across,
-    to_deep,
-    mass,
-    out,
-    window,
-    result,
-    sems,
+def inner_residual(
+    box, load, iterate, to_long, to_across, to_deep, mass, rows, cols, out, window, result, sems
 ):
     inner = slice(EDGE, EDGE + box.across)
     flat = window.reshape((box.long + 2) * box.cols, box.deep)
-    blank = jnp.zeros((box.long + 2, EDGE, box.deep), jnp.float32)
-    window[:, :EDGE, :] = blank
-    window[:, EDGE + box.across :, :] = blank
-    window[1 : 1 + box.long, inner, :] = partial[...]
-    wide_sides, narrow_sides = Sides("wide", low, high), Sides("narrow", left, right)
-    window[0, inner, :] = wide_sides.low(Ellipsis)
-    window[1 + box.long, inner, :] = wide_sides.high(Ellipsis)
-    flat[row_of(box.cols, EDGE - 1, box.long, 1), :] = narrow_sides.low(Ellipsis)
-    flat[row_of(box.cols, EDGE + box.across, box.long, 1), :] = narrow_sides.high(Ellipsis)
+    iterate_flat = iterate.reshape(box.long * box.across, box.deep)
+    window[1 : 1 + box.long, inner, :] = iterate[...]
+    window[0, inner, :] = iterate[0]
+    window[1 + box.long, inner, :] = iterate[box.long - 1]
+    for col, place in ((0, EDGE - 1), (box.across - 1, EDGE + box.across)):
+        values = iterate_flat[row_of(box.across, col, box.long), :]
+        flat[row_of(box.cols, place, box.long, 1), :] = values
     weights = (to_long, to_across, to_deep, mass)
-
-    def one_row(row, flow):
+    flow = jnp.zeros((box.across, box.deep), jnp.float32)
+    middle = slice(8, box.across - 8)
+    copies = []
+    for row in range(box.long):
         image, flow = negative_image(
             window, row + 1, REACH + row, inner.start, inner.stop, flow, weights
         )
-        result[row] = load[row] + image
-        return flow
-
-    flow = to_long[REACH - 1, inner] * (window[1, inner] - window[0, inner])
-    chunk = box.long // 4
-    copies = []
-    for index in range(4):
-        rows = slice(index * chunk, (index + 1) * chunk)
-        flow = lax.fori_loop(rows.start, rows.stop, one_row, flow, unroll=4)
-        copy = pltpu.make_async_copy(result.at[rows], out.at[rows], sems.at[index])
+        values = load[row] + image
+        result[row] = values[middle]
+        cols[0, row] = values[:8]
+        cols[1, row] = values[box.across - 8 :]
+        if row == 0:
+            rows[0] = values
+        if row == box.long - 1:
+            rows[1] = values
+        if row % 8 == 7:
+            part = slice(row - 7, row + 1)
+            copy = pltpu.make_async_copy(result.at[part], out.at[part, middle], sems.at[row // 8])
+            copy.start()
+            copies.append(copy)
+    for copy in copies:
+        copy.wait()
+
+
+def outer_residual(
+    box, iterate, low, high, left, right, to_long, to_across, rows, cols, inner_out, out,
+    row_part, col_part, sems
+):
+    del inner_out
+    inner = slice(EDGE, EDGE + box.across)
+    middle = slice(8, box.across - 8)
+    wide_sides, narrow_sides = Sides("wide", low, high), Sides("narrow", left, right)
+    last = box.long - 1
+    iterate_flat = iterate.reshape(box.long * box.across, box.deep)
+    across_flat = to_across.reshape(box.flat, box.deep)
+    below = to_long[REACH - 1, inner] * (wide_sides.low(Ellipsis) - iterate[0])
+    above = to_long[REACH + last, inner] * (wide_sides.high(Ellipsis) - iterate[last])
+    row_part[0] = (rows[0] + below)[middle]
+    row_part[1] = (rows[1] + above)[middle]
+    copies = [
+        pltpu.make_async_copy(row_part.at[0], out.at[0, middle], sems.at[0]),
+        pltpu.make_async_copy(row_part.at[1], out.at[last, middle], sems.at[1]),
+    ]
+    for copy in copies:
+        copy.start()
+    col_part[...] = cols[...]
+    flat = col_part.reshape(2 * box.long * 8, box.deep)
+    for side, (from_side, col, face, tile) in enumerate(
+        (
+            (narrow_sides.low, 0, EDGE - 1, slice(0, 8)),
+            (narrow_sides.high, box.across - 1, EDGE + box.across - 1, slice(box.across - 8, None)),
+        )
+    ):
+        weight = across_flat[row_of(box.cols, face, box.long, REACH), :]
+        own = iterate_flat[row_of(box.across, col, box.long), :]
+        place = pl.ds(side * box.long * 8 + side * 7, box.long, stride=8)
+        flat[place, :] = flat[place, :] + weight * (from_side(Ellipsis) - own)
+        col_part[side, 0] = col_part[side, 0] + below[tile]
+        col_part[side, last] = col_part[side, last] + above[tile]
+        first_col = side * (box.across - 8)
+        copy = pltpu.make_async_copy(
+            col_part.at[side], out.at[:, first_col : first_col + 8], sems.at[2 + side]
+        )
         copy.start()
         copies.append(copy)
     for copy in copies:
@@ -910,12 +956,12 @@
         functools.partial(box_sums, box),
         (whole_zone, cells, f32(8, 128), table_shape),
         [in_hbm] * 2 + [VMEM, anywhere] + [SMEM] * 2,
-        [pltpu.SemaphoreType.DMA((4,))],
+        [pltpu.SemaphoreType.DMA((2 * (long // 8),))],
     )(pinned(far_zone), pinned(far_scale), load, load_first, diffusivity, decay)
     far_narrow = exchange("narrow", *pack(REACH, [scale, zone], far_wide))
-    load_window, local, image = call(
+    load_window, local, image, inverses = call(
         functools.partial(first_solve, box),
-        (window, cells, f32(across, deep)),
+        (window, cells, f32(across, deep), f32(box.ey, box.ex, deep)),
         [VMEM] * 8 + [SMEM] * 2 + [VMEM] * N_TABLES,
         [spectral, middle],
         flops=4 * 10**9,
@@ -929,14 +975,20 @@
     parts = (table, *wide)
     if by_margins:
         parts += (two_away("wide", table),)
-    weights = call(
-        functools.partial(weights_of, box),
+    to_long, to_across, *windows = call(
+        functools.partial(side_weights, box),
         (window,) * 4,
-        [VMEM] * 6 + [SMEM] * 2,
-        [scratch(window.shape)] * 2,
+        [VMEM] * 6 + [SMEM],
         flops=10**9,
-    )(zone, scale, *far_wide, *far_narrow, diffusivity, decay)
-    first, second, table = pack(REACH, [local], wide, parts, weights[3:])
+    )(zone, scale, *far_wide, *far_narrow, diffusivity)
+    to_deep, mass = call(
+        functools.partial(deep_weights, box),
+        (window,) * 2,
+        [VMEM] * 2 + [SMEM] * 2,
+        flops=10**9,
+    )(*windows, diffusivity, decay)
+    weights = (to_long, to_across, to_deep, mass)
+    first, second, table = pack(REACH, [local], wide, parts, [to_long])
     narrow = exchange("narrow", first, second)
     if by_margins:
         table = call(join_rows, table_shape, [VMEM] * 2)(table, narrow[0])
@@ -957,16 +1009,33 @@
         [scratch(window.shape), spectral, middle, pltpu.SemaphoreType.DMA((long // 8,))],
         flops=4 * 10**9,
         out_spec=(VMEM,) * 5 + (anywhere,),
-    )(local, *wide, *narrow, sums, answers, *weights, load_window, *tables)
+    )(local, *wide, *narrow, inverses, answers, *weights, load_window, *tables)
     narrow = exchange("narrow", first_col, second_col)
     wide = exchange("wide", first_row, second_row)
+    rows, cols, inner = call(
+        functools.partial(inner_residual, box),
+        (f32(2, across, deep), f32(2, long, 8, deep), cells),
+        [VMEM] * 6,
+        [
+            scratch((long + 2, box.cols, deep)),
+            scratch((long, across - 16, deep)),
+            pltpu.SemaphoreType.DMA((long // 8,)),
+        ],
+        flops=10**9,
+        out_spec=(VMEM, VMEM, anywhere),
+    )(load, iterate, *weights)
     residual = call(
-        functools.partial(last_residual, box),
+        functools.partial(outer_residual, box),
         cells,
-        [VMEM] * 10,
-        [scratch((long + 2, box.cols, deep)), scratch(cells.shape), pltpu.SemaphoreType.DMA((4,))],
+        [VMEM] * 9 + [anywhere],
+        [
+            scratch((2, across - 16, deep)),
+            scratch((2, long, 8, deep)),
+            pltpu.SemaphoreType.DMA((4,)),
+        ],
         out_spec=anywhere,
-    )(load, iterate, *wide, *narrow, *weights)
+        aliases={9: 0},
+    )(iterate, *wide, *narrow, to_long, to_across, rows, cols, inner)
     return result, residual
 
 

time: 60.4 us -> 57.3 us (0.949)
  waiting for transfers between devices: 9.16 us -> 5.28 us
    ppermute x8, starting transfers between devices: 4.56 us -> 8.08 us  [exchange(): lax.ppermute(second, axes, ways[1])]
    ppermute x8, waiting for transfers between devices: 3.43 us -> 0.92 us  [exchange(): lax.ppermute(first, axes, ways[0])]
    ppermute x2, starting transfers between devices: 3.4 us -> 1.11 us  [two_away(): return lax.ppermute(table, axis, [(i, (i + 2) % size) for i in range(size)])]
    pallas_call x2 -> x4, Pallas kernels: 7.36 us -> 9.53 us  [the longest x1 4.48 us: on_device(): call(functools.partial(inner_residual, box), (f32(2, across, deep), f32(2...]
    ppermute x8, waiting for transfers between devices: 1.87 us -> 0.04 us  [exchange(): lax.ppermute(second, axes, ways[1])]
    pallas_call x1, Pallas kernels: 9.62 us -> 8.03 us  [on_device(): call(functools.partial(second_solve, box), (cells, row, row, col, col, ce...]
    ppermute x8, starting transfers between devices: 10.1 us -> 9.15 us  [exchange(): lax.ppermute(first, axes, ways[0])]
  transfers between devices with their start and end apart: 18 -> 18, of which waited for: 4 -> 3; matrix products, arithmetic and copies ran while one was open for 0% -> 0% of each run, Pallas kernels for 27% -> 36%
where the time goes in v11:
time: 57.3 us; the launch traced here: 57.1 us
  Pallas kernels  32.2 us (56%)
  starting transfers between devices  18.3 us (32%)
  waiting for transfers between devices  5.28 us (9%)
  between operations  1.12 us (2%)
    ppermute x8, starting transfers between devices, exchange(): lax.ppermute(first, axes, ways[0])  9.15 us
    ppermute x8, starting transfers between devices, exchange(): lax.ppermute(second, axes, ways[1])  8.08 us
    pallas_call x1, Pallas kernels, on_device(): call(functools.partial(second_solve, box), (cells, row, row, col, col, ce...  8.03 us
    pallas_call x1, Pallas kernels, on_device(): call(functools.partial(first_solve, box), (window, cells, f32(across, dee...  7.33 us
    pallas_call x1, Pallas kernels, on_device(): call(functools.partial(inner_residual, box), (f32(2, across, deep), f32(2...  4.48 us
    ppermute x2, waiting for transfers between devices, two_away(): return lax.ppermute(table, axis, [(i, (i + 2) % size) for i in range(size)])  4.32 us
    pallas_call x1, Pallas kernels, on_device(): call(functools.partial(box_sums, box), (whole_zone, cells, f32(8, 128), t...  2.55 us
    pallas_call x1, Pallas kernels, on_device(): call(functools.partial(side_weights, box), (window,) * 4, [VMEM] * 6 + [S...  2.27 us
  transfers between devices with their start and end apart: 18, of which 3 were waited for; matrix products, arithmetic and copies ran while one was open for 0% of the time, Pallas kernels for 36%

profile of v11, /device:TPU:0, one launch (start us, length us, event | category | flops | bytes accessed | tf_op | source)
XLA Modules:
  0.0 57.1 jit_solution(4049581877854604141)
XLA Ops:
  0.7 1.5 %shard_map.149 = (f32[64,32,128]{2,1,0:T(8,128)S(1)}, f32[4,32,128]{2,1,0:T(8,128)S(1)}, f32[4,32,128]{2,1,0:T(8,128)S(1)}, f32[10,32,128]{2,1,0:T(8,128)S(1)}, f32[10,32,128]{2,1,0:T(8,128)S(1)}) custom-call(s32[64,32,128]{2,1,0:T(8,128)} %far_zone.1, f32[64,32,128]{2,1,0:T(8,128)} %far_scale.1, f32[64,32,128]{2,1,0:T(8,128)} %load.1), custom_call_target="tpu_custom_call" | custom-call | tf_op jit(solution)/shard_map/pallas_call | solution.py:945
  2.2 3.1 %collective-permute-start = (f32[4,32,128]{2,1,0:T(8,128)S(1)}, f32[4,32,128]{2,1,0:T(8,128)S(1)}, u32[]{:S(2)}, u32[]{:S(2)}) collective-permute-start(f32[4,32,128]{2,1,0:T(8,128)S(1)} %get-tuple-element.41), channel_id=1, source_target_pairs={{0,4},{1,5},{2,6},{3,7},{4,0},{5,1},{6,2},{7,3},{8,12},{9,13},{10,... | collective-permute-start | bytes 196616 | tf_op jit(solution)/shard_map/ppermute | solution.py:894
  5.3 3.1 %collective-permute-start.4 = (f32[10,32,128]{2,1,0:T(8,128)S(1)}, f32[10,32,128]{2,1,0:T(8,128)S(1)}, u32[]{:S(2)}, u32[]{:S(2)}) collective-permute-start(f32[10,32,128]{2,1,0:T(8,128)S(1)} %get-tuple-element.50), channel_id=1, source_target_pairs={{0,4},{1,5},{2,6},{3,7},{4,0},{5,1},{6,2},{7,3},{8,12},{9,13},{10,... | collective-permute-start | bytes 491528 | tf_op jit(solution)/shard_map/ppermute | solution.py:894
  8.4 0.2 shard_map.150
  8.6 0.6 collective-permute-start.2
  9.2 2.2 %collective-permute-start.3 = (f32[296,128]{1,0:T(8,128)S(1)}, f32[296,128]{1,0:T(8,128)S(1)}, u32[]{:S(2)}, u32[]{:S(2)}) collective-permute-start(f32[296,128]{1,0:T(8,128)S(1)} %get-tuple-element.44), channel_id=1, source_target_pairs={{0,4},{4,0},{8,12},{12,8},{1,2},{5,6},{9,10},{13,14},{2,1},{6,5},{... | collective-permute-start | bytes 454664 | tf_op jit(solution)/shard_map/ppermute | solution.py:894
  11.4 2.5 %shard_map.151 = (s32[64,32,128]{2,1,0:T(8,128)S(1)}, f32[64,32,128]{2,1,0:T(8,128)S(1)}, f32[8,128]{1,0:T(8,128)S(1)}, f32[16,128]{1,0:T(8,128)S(1)}) custom-call(s32[64,32,128]{2,1,0:T(8,128)} %far_zone.1, f32[64,32,128]{2,1,0:T(8,128)} %far_scale.1, f32[64,32,128]{2,1,0:T(8,128)S(1)} %get-tuple-element.40.refs_0_.load, ...), custom_call_target="tpu_custom_call" | custom-call | tf_op jit(solution)/shard_map/pallas_call | solution.py:955
  14.1 0.4 shard_map.153
  14.5 0.1 collective-permute-start.6
  14.6 1.6 %collective-permute-start.7 = (f32[744,128]{1,0:T(8,128)S(1)}, f32[744,128]{1,0:T(8,128)S(1)}, u32[]{:S(2)}, u32[]{:S(2)}) collective-permute-start(f32[744,128]{1,0:T(8,128)S(1)} %get-tuple-element.53), channel_id=1, source_target_pairs={{0,4},{4,0},{8,12},{12,8},{1,2},{5,6},{9,10},{13,14},{2,1},{6,5},{... | collective-permute-start | bytes 1142792 | tf_op jit(solution)/shard_map/ppermute | solution.py:894
  16.3 7.3 %shard_map.152 = (f32[74,48,128]{2,1,0:T(8,128)S(1)}, f32[64,32,128]{2,1,0:T(8,128)S(1)}, f32[32,128]{1,0:T(8,128)S(1)}, f32[40,72,128]{2,1,0:T(8,128)S(1)}) custom-call(f32[64,32,128]{2,1,0:T(8,128)S(1)} %get-tuple-element.40.refs_0_.load, f32[4,32,128]{2,1,0:T(8,128)S(1)} %collective-permute-done.refs_1_.low, ...), custom_call_target="tpu_custom_call" | custom-call | flops 4000000000 | tf_op jit(solution)/shard_map/pallas_call | solution.py:962
  23.6 1.0 %shard_map.154 = (f32[16,128]{1,0:T(8,128)S(1)}, f32[176,128]{1,0:T(8,128)S(1)}, f32[176,128]{1,0:T(8,128)S(1)}) custom-call(s32[64,32,128]{2,1,0:T(8,128)S(1)} %get-tuple-element.46.zone.refs_1_, f32[64,32,128]{2,1,0:T(8,128)S(1)} %get-tuple-element.47.scale.refs_0_, f32[64,32,128]{2,1,0:T(8,128)S(1)} %get-tuple-element.48.local.refs_0_, ...), custom_call_target="tpu_custom_call" | custom-call | tf_op jit(solution)/shard_map/pallas_call | solution.py:970
  24.6 0.6 collective-permute-start.8
  25.2 3.2 %collective-permute-start.9 = (f32[176,128]{1,0:T(8,128)S(1)}, f32[176,128]{1,0:T(8,128)S(1)}, u32[]{:S(2)}, u32[]{:S(2)}) collective-permute-start(f32[176,128]{1,0:T(8,128)S(1)} %get-tuple-element.56), channel_id=1, source_target_pairs={{0,12},{1,13},{2,14},{3,15},{4,8},{5,9},{6,10},{7,11},{8,4},{9,5},... | collective-permute-start | bytes 270344 | tf_op jit(solution)/shard_map/ppermute | solution.py:894
  28.4 0.1 collective-permute-start.10
  28.5 2.3 %shard_map.155 = (f32[74,48,128]{2,1,0:T(8,128)S(1)}, f32[74,48,128]{2,1,0:T(8,128)S(1)}, f32[74,48,128]{2,1,0:T(8,128)S(1)}, f32[74,48,128]{2,1,0:T(8,128)S(1)}) custom-call(s32[64,32,128]{2,1,0:T(8,128)S(1)} %get-tuple-element.46.zone.refs_1_, f32[64,32,128]{2,1,0:T(8,128)S(1)} %get-tuple-element.47.scale.refs_0_, ...), custom_call_target="tpu_custom_call" | custom-call | flops 1000000000 | tf_op jit(solution)/shard_map/pallas_call | solution.py:978
  30.7 2.7 %collective-permute-done.10.refs_6_ = f32[16,128]{1,0:T(8,128)S(1)} collective-permute-done((f32[16,128]{1,0:T(8,128)S(1)}, f32[16,128]{1,0:T(8,128)S(1)}, u32[]{:S(2)}, u32[]{:S(2)}) %collective-permute-start.10) | collective-permute-done | bytes 8224 | tf_op jit(solution)/shard_map/ppermute | solution.py:899
  33.4 0.2 shard_map.156
  33.6 0.1 collective-permute-start.11
  33.7 0.5 collective-permute-start.12
  34.3 0.9 %collective-permute-done.11.message.left = f32[392,128]{1,0:T(8,128)S(1)} collective-permute-done((f32[392,128]{1,0:T(8,128)S(1)}, f32[392,128]{1,0:T(8,128)S(1)}, u32[]{:S(2)}, u32[]{:S(2)}) %collective-permute-start.11) | collective-permute-done | bytes 200736 | tf_op jit(solution)/shard_map/ppermute | solution.py:894
  35.2 1.0 %collective-permute-start.13 = (f32[16,128]{1,0:T(8,128)S(1)}, f32[16,128]{1,0:T(8,128)S(1)}, u32[]{:S(2)}, u32[]{:S(2)}) collective-permute-start(f32[16,128]{1,0:T(8,128)S(1)} %shard_map.157.refs_0_), channel_id=1, source_target_pairs={{0,2},{1,3},{2,0},{3,1},{4,6},{5,7},{6,4},{7,5},{8,10},{9,11},{10,... | collective-permute-start | bytes 24584 | tf_op jit(solution)/shard_map/ppermute | solution.py:899
  36.2 1.8 %shard_map.159 = (f32[74,48,128]{2,1,0:T(8,128)S(1)}, f32[74,48,128]{2,1,0:T(8,128)S(1)}) custom-call(f32[74,48,128]{2,1,0:T(8,128)S(1)} %get-tuple-element.64.zone_window, f32[74,48,128]{2,1,0:T(8,128)S(1)} %get-tuple-element.65.scale_window, f32[3,3]{1,0:T(4,128)S(1)} %copy-done, f32[3]{0:T(128)S(1)} %copy-done.1), custom_call_target="tpu_custom_call" | custom-call | flops 1000000000 | tf_op jit(solution)/shard_map/pallas_call | solution.py:984
  38.0 1.7 %collective-permute-done.13.refs_1_ = f32[16,128]{1,0:T(8,128)S(1)} collective-permute-done((f32[16,128]{1,0:T(8,128)S(1)}, f32[16,128]{1,0:T(8,128)S(1)}, u32[]{:S(2)}, u32[]{:S(2)}) %collective-permute-start.13) | collective-permute-done | bytes 8224 | tf_op jit(solution)/shard_map/ppermute | solution.py:899
  39.7 1.5 %shard_map.158.answers = f32[8,128]{1,0:T(8,128)S(1)} custom-call(f32[16,128]{1,0:T(8,128)S(1)} %shard_map.157.refs_0_, f32[16,128]{1,0:T(8,128)S(1)} %collective-permute-done.13.refs_1_), custom_call_target="tpu_custom_call" | custom-call | tf_op jit(solution)/shard_map/pallas_call | solution.py:999
  41.2 0.0 collective-permute-done.12.right
  41.2 8.0 %shard_map.160 = (f32[64,32,128]{2,1,0:T(8,128)S(1)}, f32[32,128]{1,0:T(8,128)S(1)}, f32[32,128]{1,0:T(8,128)S(1)}, f32[64,128]{1,0:T(8,128)S(1)}, f32[64,128]{1,0:T(8,128)S(1)}, /*index=5*/f32[64,32,128]{2,1,0:T(8,128)}) custom-call(f32[64,32,128]{2,1,0:T(8,128)S(1)} %get-tuple-element.48.local.refs_0_, ...), custom_call_target="tpu_custom_call" | custom-call | flops 4000000000 | tf_op jit(solution)/shard_map/pallas_call | solution.py:1005
  49.3 0.1 collective-permute-start.16
  49.3 0.5 collective-permute-start.17
  49.9 1.6 %collective-permute-start.14 = (f32[32,128]{1,0:T(8,128)S(1)}, f32[32,128]{1,0:T(8,128)S(1)}, u32[]{:S(2)}, u32[]{:S(2)}) collective-permute-start(f32[32,128]{1,0:T(8,128)S(1)} %get-tuple-element.71), channel_id=1, source_target_pairs={{0,4},{1,5},{2,6},{3,7},{4,0},{5,1},{6,2},{7,3},{8,12},{9,13},{10,... | collective-permute-start | bytes 49160 | tf_op jit(solution)/shard_map/ppermute | solution.py:894
  51.4 4.5 %shard_map.161 = (f32[2,32,128]{2,1,0:T(8,128)S(1)}, f32[2,64,8,128]{3,2,1,0:T(8,128)S(1)}, f32[64,32,128]{2,1,0:T(8,128)}) custom-call(f32[64,32,128]{2,1,0:T(8,128)S(1)} %get-tuple-element.40.refs_0_.load, f32[64,32,128]{2,1,0:T(8,128)S(1)} %get-tuple-element.70.iterate, f32[74,48,128]{2,1,0:T(8,128)S(1)} %get-tuple-element.58.refs_7_.rest_0_.to_long, ...), custom_call_target="tpu_custom_call" | custom-call | flops 1000000000 | tf_op jit(solution)/shard_map/pallas_call | solution.py:1015
  56.0 0.9 %shard_map.162 = f32[64,32,128]{2,1,0:T(8,128)} custom-call(f32[64,32,128]{2,1,0:T(8,128)S(1)} %get-tuple-element.70.iterate, f32[32,128]{1,0:T(8,128)S(1)} %collective-permute-done.14.low, f32[32,128]{1,0:T(8,128)S(1)} %collective-permute-done.15.high, f32[64,128]{1,0:T(8,128)S(1)} %collective-permute-done.16.left, ...), custom_call_target="tpu_custom_call", output_to_operand_aliasing={{}: (9, {})} | custom-call | tf_op jit(solution)/shard_map/pallas_call | solution.py:1027
  (40 shorter events, 0.1 us)
Async XLA Ops:
  0.6 10.7 %copy-start = (f32[3,3]{1,0:T(4,128)S(1)}, f32[3,3]{1,0:T(4,128)}, u32[]{:S(2)}) copy-start(f32[3,3]{1,0:T(4,128)} %diffusivity.9) | copy-start | bytes 112
  0.6 10.7 %copy-start.1 = (f32[3]{0:T(128)S(1)}, f32[3]{0:T(128)}, u32[]{:S(2)}) copy-start(f32[3]{0:T(128)} %decay.5) | copy-start | bytes 40
  2.2 6.2 %collective-permute-start = (f32[4,32,128]{2,1,0:T(8,128)S(1)}, f32[4,32,128]{2,1,0:T(8,128)S(1)}, u32[]{:S(2)}, u32[]{:S(2)}) collective-permute-start(f32[4,32,128]{2,1,0:T(8,128)S(1)} %get-tuple-element.41), channel_id=1, source_target_pairs={{0,4},{1,5},{2,6},{3,7},{4,0},{5,1},{6,2},{7,3},{8,12},{9,13},{10,... | collective-permute-start | bytes 196616 | tf_op jit(solution)/shard_map/ppermute | solution.py:894
  5.3 3.2 %collective-permute-start.1 = (f32[4,32,128]{2,1,0:T(8,128)S(1)}, f32[4,32,128]{2,1,0:T(8,128)S(1)}, u32[]{:S(2)}, u32[]{:S(2)}) collective-permute-start(f32[4,32,128]{2,1,0:T(8,128)S(1)} %get-tuple-element.42), channel_id=1, source_target_pairs={{0,1},{1,0},{2,3},{3,2},{4,8},{5,9},{6,10},{7,11},{8,4},{9,5},{10,... | collective-permute-start | bytes 196616 | tf_op jit(solution)/shard_map/ppermute | solution.py:894
  5.3 8.8 %collective-permute-start.4 = (f32[10,32,128]{2,1,0:T(8,128)S(1)}, f32[10,32,128]{2,1,0:T(8,128)S(1)}, u32[]{:S(2)}, u32[]{:S(2)}) collective-permute-start(f32[10,32,128]{2,1,0:T(8,128)S(1)} %get-tuple-element.50), channel_id=1, source_target_pairs={{0,4},{1,5},{2,6},{3,7},{4,0},{5,1},{6,2},{7,3},{8,12},{9,13},{10,... | collective-permute-start | bytes 491528 | tf_op jit(solution)/shard_map/ppermute | solution.py:894
  8.4 5.6 %collective-permute-start.5 = (f32[10,32,128]{2,1,0:T(8,128)S(1)}, f32[10,32,128]{2,1,0:T(8,128)S(1)}, u32[]{:S(2)}, u32[]{:S(2)}) collective-permute-start(f32[10,32,128]{2,1,0:T(8,128)S(1)} %get-tuple-element.51), channel_id=1, source_target_pairs={{0,1},{1,0},{2,3},{3,2},{4,8},{5,9},{6,10},{7,11},{8,4},{9,5},{10,... | collective-permute-start | bytes 491528 | tf_op jit(solution)/shard_map/ppermute | solution.py:894
  8.6 7.5 %collective-permute-start.2 = (f32[296,128]{1,0:T(8,128)S(1)}, f32[296,128]{1,0:T(8,128)S(1)}, u32[]{:S(2)}, u32[]{:S(2)}) collective-permute-start(f32[296,128]{1,0:T(8,128)S(1)} %get-tuple-element.43.after), channel_id=1, source_target_pairs={{0,1},{4,5},{8,9},{12,13},{1,0},{5,4},{9,8},{13,12},{2,3},{6,7},{1... | collective-permute-start | bytes 454664 | tf_op jit(solution)/shard_map/ppermute | solution.py:894
  9.2 7.0 %collective-permute-start.3 = (f32[296,128]{1,0:T(8,128)S(1)}, f32[296,128]{1,0:T(8,128)S(1)}, u32[]{:S(2)}, u32[]{:S(2)}) collective-permute-start(f32[296,128]{1,0:T(8,128)S(1)} %get-tuple-element.44), channel_id=1, source_target_pairs={{0,4},{4,0},{8,12},{12,8},{1,2},{5,6},{9,10},{13,14},{2,1},{6,5},{... | collective-permute-start | bytes 454664 | tf_op jit(solution)/shard_map/ppermute | solution.py:894
  13.9 2.3 %copy-start.2 = (bf16[256,256]{1,0:T(8,128)(2,1)S(1)}, bf16[256,256]{1,0:T(8,128)(2,1)}, u32[]{:S(2)}) copy-start(bf16[256,256]{1,0:T(8,128)(2,1)} %constant.22.clone.rest_4_.rest_9_) | copy-start | bytes 393220
  13.9 2.2 %copy-start.3 = (bf16[192,240]{1,0:T(8,128)(2,1)S(1)}, bf16[192,240]{1,0:T(8,128)(2,1)}, u32[]{:S(2)}) copy-start(bf16[192,240]{1,0:T(8,128)(2,1)} %constant.20.clone.rest_2_.rest_7_) | copy-start | bytes 276484
  14.0 2.2 %copy-start.4 = (bf16[144,160]{1,0:T(8,128)(2,1)S(1)}, bf16[144,160]{1,0:T(8,128)(2,1)}, u32[]{:S(2)}) copy-start(bf16[144,160]{1,0:T(8,128)(2,1)} %constant.19.clone.rest_1_.rest_6_) | copy-start | bytes 138244
  14.0 2.2 %copy-start.5 = (bf16[256,128]{1,0:T(8,128)(2,1)S(1)}, bf16[256,128]{1,0:T(8,128)(2,1)}, u32[]{:S(2)}) copy-start(bf16[256,128]{1,0:T(8,128)(2,1)} %constant.23.clone.rest_5_.rest_10_) | copy-start | bytes 196612
  14.0 2.2 %copy-start.6 = (bf16[96,144]{1,0:T(8,128)(2,1)S(1)}, bf16[96,144]{1,0:T(8,128)(2,1)}, u32[]{:S(2)}) copy-start(bf16[96,144]{1,0:T(8,128)(2,1)} %constant.21.clone.rest_3_.rest_8_) | copy-start | bytes 82948
  14.0 2.2 %copy-start.7 = (f32[72,128]{1,0:T(8,128)S(1)}, f32[72,128]{1,0:T(8,128)}, u32[]{:S(2)}) copy-start(f32[72,128]{1,0:T(8,128)} %constant.24.clone.rest_6_.rest_11_) | copy-start | bytes 110596
  14.0 2.2 %copy-start.8 = (bf16[80,96]{1,0:T(8,128)(2,1)S(1)}, bf16[80,96]{1,0:T(8,128)(2,1)}, u32[]{:S(2)}) copy-start(bf16[80,96]{1,0:T(8,128)(2,1)} %constant.18.clone.rest_0_.rest_5_) | copy-start | bytes 46084
  14.0 2.2 %copy-start.9 = (f32[1,128]{1,0:T(1,128)S(1)}, f32[1,128]{1,0:T(1,128)}, u32[]{:S(2)}) copy-start(f32[1,128]{1,0:T(1,128)} %constant.25.clone.rest_7_.rest_12_) | copy-start | bytes 1540
  14.0 2.2 %copy-start.10 = (f32[1,40]{1,0:T(1,128)S(1)}, f32[1,40]{1,0:T(1,128)}, u32[]{:S(2)}) copy-start(f32[1,40]{1,0:T(1,128)} %constant.26.clone.rest_8_.rest_13_) | copy-start | bytes 484
  14.5 9.1 %collective-permute-start.6 = (f32[744,128]{1,0:T(8,128)S(1)}, f32[744,128]{1,0:T(8,128)S(1)}, u32[]{:S(2)}, u32[]{:S(2)}) collective-permute-start(f32[744,128]{1,0:T(8,128)S(1)} %get-tuple-element.52), channel_id=1, source_target_pairs={{0,1},{4,5},{8,9},{12,13},{1,0},{5,4},{9,8},{13,12},{2,3},{6,7},{1... | collective-permute-start | bytes 1142792 | tf_op jit(solution)/shard_map/ppermute | solution.py:894
  14.6 9.0 %collective-permute-start.7 = (f32[744,128]{1,0:T(8,128)S(1)}, f32[744,128]{1,0:T(8,128)S(1)}, u32[]{:S(2)}, u32[]{:S(2)}) collective-permute-start(f32[744,128]{1,0:T(8,128)S(1)} %get-tuple-element.53), channel_id=1, source_target_pairs={{0,4},{4,0},{8,12},{12,8},{1,2},{5,6},{9,10},{13,14},{2,1},{6,5},{... | collective-permute-start | bytes 1142792 | tf_op jit(solution)/shard_map/ppermute | solution.py:894
  24.6 8.8 %collective-permute-start.8 = (f32[176,128]{1,0:T(8,128)S(1)}, f32[176,128]{1,0:T(8,128)S(1)}, u32[]{:S(2)}, u32[]{:S(2)}) collective-permute-start(f32[176,128]{1,0:T(8,128)S(1)} %get-tuple-element.55), channel_id=1, source_target_pairs={{0,4},{1,5},{2,6},{3,7},{4,0},{5,1},{6,2},{7,3},{8,12},{9,13},{10,... | collective-permute-start | bytes 270344 | tf_op jit(solution)/shard_map/ppermute | solution.py:894
  25.2 8.3 %collective-permute-start.9 = (f32[176,128]{1,0:T(8,128)S(1)}, f32[176,128]{1,0:T(8,128)S(1)}, u32[]{:S(2)}, u32[]{:S(2)}) collective-permute-start(f32[176,128]{1,0:T(8,128)S(1)} %get-tuple-element.56), channel_id=1, source_target_pairs={{0,12},{1,13},{2,14},{3,15},{4,8},{5,9},{6,10},{7,11},{8,4},{9,5},... | collective-permute-start | bytes 270344 | tf_op jit(solution)/shard_map/ppermute | solution.py:894
  28.4 5.0 %collective-permute-start.10 = (f32[16,128]{1,0:T(8,128)S(1)}, f32[16,128]{1,0:T(8,128)S(1)}, u32[]{:S(2)}, u32[]{:S(2)}) collective-permute-start(f32[16,128]{1,0:T(8,128)S(1)} %get-tuple-element.57.refs_3_), channel_id=1, source_target_pairs={{0,8},{4,12},{8,0},{12,4},{1,9},{5,13},{9,1},{13,5},{2,10},{6,14},... | collective-permute-start | bytes 24584 | tf_op jit(solution)/shard_map/ppermute | solution.py:899
  33.6 1.5 %collective-permute-start.11 = (f32[392,128]{1,0:T(8,128)S(1)}, f32[392,128]{1,0:T(8,128)S(1)}, u32[]{:S(2)}, u32[]{:S(2)}) collective-permute-start(f32[392,128]{1,0:T(8,128)S(1)} %get-tuple-element.59), channel_id=1, source_target_pairs={{0,1},{4,5},{8,9},{12,13},{1,0},{5,4},{9,8},{13,12},{2,3},{6,7},{1... | collective-permute-start | bytes 602120 | tf_op jit(solution)/shard_map/ppermute | solution.py:894
  33.7 7.5 %collective-permute-start.12 = (f32[392,128]{1,0:T(8,128)S(1)}, f32[392,128]{1,0:T(8,128)S(1)}, u32[]{:S(2)}, u32[]{:S(2)}) collective-permute-start(f32[392,128]{1,0:T(8,128)S(1)} %get-tuple-element.60), channel_id=1, source_target_pairs={{0,4},{4,0},{8,12},{12,8},{1,2},{5,6},{9,10},{13,14},{2,1},{6,5},{... | collective-permute-start | bytes 602120 | tf_op jit(solution)/shard_map/ppermute | solution.py:894
  35.2 4.6 %collective-permute-start.13 = (f32[16,128]{1,0:T(8,128)S(1)}, f32[16,128]{1,0:T(8,128)S(1)}, u32[]{:S(2)}, u32[]{:S(2)}) collective-permute-start(f32[16,128]{1,0:T(8,128)S(1)} %shard_map.157.refs_0_), channel_id=1, source_target_pairs={{0,2},{1,3},{2,0},{3,1},{4,6},{5,7},{6,4},{7,5},{8,10},{9,11},{10,... | collective-permute-start | bytes 24584 | tf_op jit(solution)/shard_map/ppermute | solution.py:899
  49.3 6.7 %collective-permute-start.16 = (f32[64,128]{1,0:T(8,128)S(1)}, f32[64,128]{1,0:T(8,128)S(1)}, u32[]{:S(2)}, u32[]{:S(2)}) collective-permute-start(f32[64,128]{1,0:T(8,128)S(1)} %get-tuple-element.73), channel_id=1, source_target_pairs={{0,1},{4,5},{8,9},{12,13},{1,0},{5,4},{9,8},{13,12},{2,3},{6,7},{1... | collective-permute-start | bytes 98312 | tf_op jit(solution)/shard_map/ppermute | solution.py:894
  49.3 6.6 %collective-permute-start.17 = (f32[64,128]{1,0:T(8,128)S(1)}, f32[64,128]{1,0:T(8,128)S(1)}, u32[]{:S(2)}, u32[]{:S(2)}) collective-permute-start(f32[64,128]{1,0:T(8,128)S(1)} %get-tuple-element.74), channel_id=1, source_target_pairs={{0,4},{4,0},{8,12},{12,8},{1,2},{5,6},{9,10},{13,14},{2,1},{6,5},{... | collective-permute-start | bytes 98312 | tf_op jit(solution)/shard_map/ppermute | solution.py:894
  49.9 6.1 %collective-permute-start.14 = (f32[32,128]{1,0:T(8,128)S(1)}, f32[32,128]{1,0:T(8,128)S(1)}, u32[]{:S(2)}, u32[]{:S(2)}) collective-permute-start(f32[32,128]{1,0:T(8,128)S(1)} %get-tuple-element.71), channel_id=1, source_target_pairs={{0,4},{1,5},{2,6},{3,7},{4,0},{5,1},{6,2},{7,3},{8,12},{9,13},{10,... | collective-permute-start | bytes 49160 | tf_op jit(solution)/shard_map/ppermute | solution.py:894
  51.4 4.5 %collective-permute-start.15 = (f32[32,128]{1,0:T(8,128)S(1)}, f32[32,128]{1,0:T(8,128)S(1)}, u32[]{:S(2)}, u32[]{:S(2)}) collective-permute-start(f32[32,128]{1,0:T(8,128)S(1)} %get-tuple-element.72), channel_id=1, source_target_pairs={{0,1},{1,0},{2,3},{3,2},{4,8},{5,9},{6,10},{7,11},{8,4},{9,5},{10,... | collective-permute-start | bytes 49160 | tf_op jit(solution)/shard_map/ppermute | solution.py:894

commit v12 on v11

--- a/solution.py
+++ b/solution.py
@@ -111,6 +111,7 @@
     sine_x, eig_x = sine_basis(box.ex)
     sine_y, eig_y = sine_basis(box.ey)
     sine_z, eig_z = sine_basis(box.deep)
+    in_order_of_steps = np.arange(box.ey).reshape(8, box.ey // 8).T.reshape(-1)
     from_y = sine_y[MARGIN : MARGIN + box.across]
     from_x = sine_x[MARGIN : MARGIN + box.long]
     spread = np.broadcast_to(eig_x[:, None], (box.ex, box.deep))
@@ -118,7 +119,7 @@
     return [
         jnp.asarray(np.ascontiguousarray(t))
         for t in (
-            left_table(sine_y, padded(box.ey), FORWARD),
+            left_table(sine_y[:, in_order_of_steps], padded(box.ey), FORWARD),
             left_table(sine_x, padded(box.ex), FORWARD),
             left_table(from_x, padded(box.ex), BACKWARD),
             left_table(from_y, padded(box.ey), BACKWARD),
@@ -291,7 +292,8 @@
 
 
 def bring_edges(
-    box, zone, scale, load, own_load, load_first, load_second, first, second, staged, sems
+    box, zone, scale, load, own_zone, own_scale, own_load, load_first, load_second, first, second,
+    staged, sems
 ):
     even = is_even("wide")
 
@@ -307,6 +309,8 @@
         (scale.at[edges(REACH)[0]], first.at[:REACH]),
         (scale.at[edges(REACH)[1]], second.at[:REACH]),
         (load, own_load),
+        (scale, own_scale),
+        (zone, own_zone),
     ]
     copies = [
         pltpu.make_async_copy(source, target, sems.at[index])
@@ -353,18 +357,40 @@
                 flat[row_of(box.cols, col, size, row), :] = add(values, row_side, side)
 
 
-def negative_image(window, row, at, first, last, flow_before, weights):
+def some_cols(box, ref, row, step):
+    stride = box.ey // 8
+    return ref[row, pl.ds(EDGE - MARGIN + step, 8, stride=stride), :]
+
+
+def negative_image(box, window, row, at, x, flow_before, weights):
     to_long, to_across, to_deep, mass = weights
-    x = window[row, first:last]
-    flow_long = to_long[at, first:last] * (window[row + 1, first:last] - x)
-    flow_across = to_across[at, first:last] * (window[row, first + 1 : last + 1] - x)
-    flow_from = to_across[at, first - 1 : last - 1] * (x - window[row, first - 1 : last - 1])
-    lanes = x.shape[1]
-    flow_deep = to_deep[at, first:last] * (pltpu.roll(x, lanes - 1, 1) - x)
-    total = flow_long - flow_before - mass[at, first:last] * x
-    total = total + (flow_across - flow_from)
-    total = total + (flow_deep - pltpu.roll(flow_deep, 1, 1))
-    return total, flow_long
+    steps = range(box.ey // 8)
+    x_next = [some_cols(box, window, row + 1, step) for step in range(-1, len(steps) + 1)]
+    flow_long = [
+        some_cols(box, to_long, at, step) * (x_next[step + 1] - x[step + 1]) for step in steps
+    ]
+    flow_across = [
+        some_cols(box, to_across, at, step) * (x[step + 2] - x[step + 1])
+        for step in range(-1, len(steps))
+    ]
+    totals = []
+    for step in steps:
+        here = x[step + 1]
+        lanes = here.shape[1]
+        flow_deep = some_cols(box, to_deep, at, step) * (pltpu.roll(here, lanes - 1, 1) - here)
+        total = flow_long[step] - flow_before[step] - some_cols(box, mass, at, step) * here
+        total = total + (flow_across[step + 1] - flow_across[step])
+        totals.append(total + (flow_deep - pltpu.roll(flow_deep, 1, 1)))
+    return totals, x_next, flow_long
+
+
+def in_steps(box, refs, rows):
+    return jnp.stack(
+        [
+            jnp.concatenate([some_cols(box, ref, row, step) for step in range(box.ey // 8)], axis=0)
+            for ref, row in zip(refs, rows)
+        ]
+    )
 
 
 def looked_up(labels, values):
@@ -400,21 +426,8 @@
     return line
 
 
-def box_sums(
-    box, far_zone, far_scale, load, after, diffusivity, decay, zone, scale, out, table, sems
-):
+def box_sums(box, zone, scale, load, after, diffusivity, decay, out, table):
     del after
-    size = 8
-    parts = box.long // size
-    copies = []
-    for part in range(parts):
-        rows = slice(part * size, (part + 1) * size)
-        for index, (source, target) in enumerate(((far_zone, zone), (far_scale, scale))):
-            copy = pltpu.make_async_copy(
-                source.at[rows], target.at[rows], sems.at[2 * part + index]
-            )
-            copy.start()
-            copies.append(copy)
     nothing = jnp.zeros((box.across, box.deep), jnp.float32)
     half = [[0.5 * diffusivity[z, d] for z in range(3)] for d in range(3)]
     rates = [decay[z] for z in range(3)]
@@ -424,11 +437,8 @@
         return [looked_up(labels, half[d]) * factor for d in range(3)] + [looked_up(labels, rates)]
 
     sums = [nothing] * 5
-    for part in range(parts):
-        for copy in copies[2 * part : 2 * part + 2]:
-            copy.wait()
-        for row in range(part * size, (part + 1) * size):
-            sums = [total + more for total, more in zip(sums, halves(row) + [load[row]])]
+    for row in range(box.long):
+        sums = [total + more for total, more in zip(sums, halves(row) + [load[row]])]
 
     def total(values):
         return jnp.sum(values, keepdims=True).reshape(1, 1)
@@ -463,7 +473,10 @@
     base = means[3] + means[0] * spread[...] + means[2] * eig_z[...]
 
     def divided(values, col):
-        inverse = 1.0 / (base + means[1] * eig_y[0, col])
+        divisor = base + means[1] * eig_y[0, col]
+        inverse = pl.reciprocal(divisor, approx=True)
+        for _ in range(2):
+            inverse = inverse * (2.0 - divisor * inverse)
         inverses[col] = inverse
         return values * inverse
 
@@ -488,7 +501,7 @@
 
     box_solve(
         box,
-        lambda row: window[1 + row : 9 + row, EDGE - MARGIN : EDGE + box.across + MARGIN],
+        lambda start: in_steps(box, [window] * 8, range(1 + start, 9 + start)),
         divided,
         tables,
         None,
@@ -729,9 +742,13 @@
     fill_window(box, window, local, wide_sides, narrow_sides, REACH, 0, REACH, add)
     weights = (to_long, to_across, to_deep, mass)
 
-    start, stop = EDGE - MARGIN, EDGE + box.across + MARGIN
-
-    flow = [to_long[0, start:stop] * (window[1, start:stop] - window[0, start:stop])]
+    steps = range(box.ey // 8)
+    x = [some_cols(box, window, 1, step) for step in range(-1, len(steps) + 1)]
+    flow = [
+        some_cols(box, to_long, 0, step) * (x[step + 1] - some_cols(box, window, 0, step))
+        for step in steps
+    ]
+    state = [x, flow]
 
     def divided(values, col):
         return values * inverses[col]
@@ -739,14 +756,16 @@
     def residual(start_row):
         rows = []
         for row in range(start_row + 1, start_row + 9):
-            image, flow[0] = negative_image(window, row, row, start, stop, flow[0], weights)
-            rows.append((load_window[row, start:stop] + image)[None])
-        return jnp.concatenate(rows, axis=0)
+            image, *state[:] = negative_image(box, window, row, row, *state, weights)
+            image = [some_cols(box, load_window, row, step) + image[step] for step in steps]
+            rows.append(jnp.concatenate(image, axis=0))
+        return jnp.stack(rows)
 
     inner = slice(EDGE, EDGE + box.across)
     first = REACH
     row_ids = lax.broadcasted_iota(jnp.int32, (1, padded(box.ex)), 1)
     col_ids = lax.broadcasted_iota(jnp.int32, (1, padded(box.ey)), 1)
+    col_ids = (col_ids & 7) * (box.ey // 8) + lax.shift_right_logical(col_ids, 3)
     row_mask = jnp.where(row_ids < MARGIN, as_float(long_pos > 0), 1.0)
     row_mask = jnp.where(row_ids >= MARGIN + box.long, as_float(long_pos < long_count - 1), row_mask)
     col_mask = jnp.where(col_ids < MARGIN, as_float(across_pos > 0), 1.0)
@@ -786,6 +805,9 @@
     inner = slice(EDGE, EDGE + box.across)
     flat = window.reshape((box.long + 2) * box.cols, box.deep)
     iterate_flat = iterate.reshape(box.long * box.across, box.deep)
+    blank = jnp.zeros((box.long + 2, EDGE, box.deep), jnp.float32)
+    window[:, :EDGE, :] = blank
+    window[:, EDGE + box.across :, :] = blank
     window[1 : 1 + box.long, inner, :] = iterate[...]
     window[0, inner, :] = iterate[0]
     window[1 + box.long, inner, :] = iterate[box.long - 1]
@@ -793,15 +815,18 @@
         values = iterate_flat[row_of(box.across, col, box.long), :]
         flat[row_of(box.cols, place, box.long, 1), :] = values
     weights = (to_long, to_across, to_deep, mass)
-    flow = jnp.zeros((box.across, box.deep), jnp.float32)
+    steps = range(box.ey // 8)
+    x = [some_cols(box, window, 1, step) for step in range(-1, len(steps) + 1)]
+    flow = [jnp.zeros((8, box.deep), jnp.float32) for _ in steps]
     middle = slice(8, box.across - 8)
     copies = []
     for row in range(box.long):
-        image, flow = negative_image(
-            window, row + 1, REACH + row, inner.start, inner.stop, flow, weights
-        )
-        values = load[row] + image
-        result[row] = values[middle]
+        image, x, flow = negative_image(box, window, row + 1, REACH + row, x, flow, weights)
+        for step in steps:
+            place = pl.ds(EDGE - MARGIN + step, 8, stride=box.ey // 8)
+            result[row, place, :] = image[step]
+        values = load[row] + result[row, inner]
+        result[row, inner] = values
         cols[0, row] = values[:8]
         cols[1, row] = values[box.across - 8 :]
         if row == 0:
@@ -810,7 +835,11 @@
             rows[1] = values
         if row % 8 == 7:
             part = slice(row - 7, row + 1)
-            copy = pltpu.make_async_copy(result.at[part], out.at[part, middle], sems.at[row // 8])
+            copy = pltpu.make_async_copy(
+                result.at[part, EDGE + 8 : EDGE + box.across - 8],
+                out.at[part, middle],
+                sems.at[row // 8],
+            )
             copy.start()
             copies.append(copy)
     for copy in copies:
@@ -941,23 +970,21 @@
         )(*fields, *sides, *parts, *after)
 
     far = f32(2 * REACH, across, deep)
-    far_zone, far_scale = zone, scale
-    load, load_first, load_second, first, second = call(
+    zone, scale, load, load_first, load_second, first, second = call(
         functools.partial(bring_edges, box),
-        (cells,) + (f32(MARGIN, across, deep),) * 2 + (far, far),
+        (whole_zone, cells, cells) + (f32(MARGIN, across, deep),) * 2 + (far, far),
         [in_hbm] * 3,
-        [pltpu.VMEM((2, REACH, across, deep), zone.dtype), pltpu.SemaphoreType.DMA((7,))],
+        [pltpu.VMEM((2, REACH, across, deep), zone.dtype), pltpu.SemaphoreType.DMA((9,))],
     )(pinned(zone), pinned(scale), pinned(load))
     load_wide = exchange("wide", load_first, load_second)
     far_wide = exchange("wide", first, second)
     load_first, load_second = pack(MARGIN, [load], load_wide)
     load_narrow = exchange("narrow", load_first, load_second)
-    zone, scale, sums, table = call(
+    sums, table = call(
         functools.partial(box_sums, box),
-        (whole_zone, cells, f32(8, 128), table_shape),
-        [in_hbm] * 2 + [VMEM, anywhere] + [SMEM] * 2,
-        [pltpu.SemaphoreType.DMA((2 * (long // 8),))],
-    )(pinned(far_zone), pinned(far_scale), load, load_first, diffusivity, decay)
+        (f32(8, 128), table_shape),
+        [VMEM] * 3 + [anywhere] + [SMEM] * 2,
+    )(zone, scale, load, load_first, diffusivity, decay)
     far_narrow = exchange("narrow", *pack(REACH, [scale, zone], far_wide))
     load_window, local, image, inverses = call(
         functools.partial(first_solve, box),
@@ -1018,7 +1045,7 @@
         [VMEM] * 6,
         [
             scratch((long + 2, box.cols, deep)),
-            scratch((long, across - 16, deep)),
+            scratch((long, box.cols, deep)),
             pltpu.SemaphoreType.DMA((long // 8,)),
         ],
         flops=10**9,

time: 57.3 us -> 55.9 us (0.976)
  Pallas kernels: 32.2 us -> 29.3 us
  waiting for transfers between devices: 5.28 us -> 7.05 us
    pallas_call x1, Pallas kernels: 4.48 us -> 2.05 us  [on_device(): call(functools.partial(inner_residual, box), (f32(2, across, deep), f32(2...]
    ppermute x2, waiting for transfers between devices: 4.32 us -> 5.27 us  [two_away(): return lax.ppermute(table, axis, [(i, (i + 2) % size) for i in range(size)])]
    ppermute x8, waiting for transfers between devices: 0.92 us -> 1.74 us  [exchange(): lax.ppermute(first, axes, ways[0])]
    ppermute x8, starting transfers between devices: 8.08 us -> 8.66 us  [exchange(): lax.ppermute(second, axes, ways[1])]
  transfers between devices with their start and end apart: 18 -> 18, of which waited for: 3 -> 5; matrix products, arithmetic and copies ran while one was open for 0% -> 0% of each run, Pallas kernels for 36% -> 31%
where the time goes in v12:
time: 55.9 us; the launch traced here: 55.8 us
  Pallas kernels  29.3 us (52%)
  starting transfers between devices  18.3 us (33%)
  waiting for transfers between devices  7.05 us (13%)
  between operations  1.09 us (2%)
    ppermute x8, starting transfers between devices, exchange(): lax.ppermute(first, axes, ways[0])  8.71 us
    ppermute x8, starting transfers between devices, exchange(): lax.ppermute(second, axes, ways[1])  8.66 us
    pallas_call x1, Pallas kernels, on_device(): call(functools.partial(second_solve, box), (cells, row, row, col, col, ce...  7.85 us
    pallas_call x1, Pallas kernels, on_device(): call(functools.partial(first_solve, box), (window, cells, f32(across, dee...  7.3 us
    ppermute x2, waiting for transfers between devices, two_away(): return lax.ppermute(table, axis, [(i, (i + 2) % size) for i in range(size)])  5.27 us
    pallas_call x1, Pallas kernels, on_device(): call(functools.partial(side_weights, box), (window,) * 4, [VMEM] * 6 + [S...  2.27 us
    pallas_call x1, Pallas kernels, on_device(): call(functools.partial(bring_edges, box), (whole_zone, cells, cells) + (f...  2.19 us
    pallas_call x1, Pallas kernels, on_device(): call(functools.partial(inner_residual, box), (f32(2, across, deep), f32(2...  2.05 us
  transfers between devices with their start and end apart: 18, of which 5 were waited for; matrix products, arithmetic and copies ran while one was open for 0% of the time, Pallas kernels for 31%

profile of v12, /device:TPU:0, one launch (start us, length us, event | category | flops | bytes accessed | tf_op | source)
XLA Modules:
  0.0 55.8 jit_solution(1203405248287936832)
XLA Ops:
  0.6 2.2 %shard_map.149 = (s32[64,32,128]{2,1,0:T(8,128)S(1)}, f32[64,32,128]{2,1,0:T(8,128)S(1)}, f32[64,32,128]{2,1,0:T(8,128)S(1)}, f32[4,32,128]{2,1,0:T(8,128)S(1)},...) custom-call(s32[64,32,128]{2,1,0:T(8,128)} %zone.1, f32[64,32,128]{2,1,0:T(8,128)} %scale.1, ...), custom_call_target="tpu_custom_call" | custom-call | tf_op jit(solution)/shard_map/pallas_call | solution.py:973
  2.8 3.1 %collective-permute-start = (f32[4,32,128]{2,1,0:T(8,128)S(1)}, f32[4,32,128]{2,1,0:T(8,128)S(1)}, u32[]{:S(2)}, u32[]{:S(2)}) collective-permute-start(f32[4,32,128]{2,1,0:T(8,128)S(1)} %get-tuple-element.41), channel_id=1, source_target_pairs={{0,4},{1,5},{2,6},{3,7},{4,0},{5,1},{6,2},{7,3},{8,12},{9,13},{10,... | collective-permute-start | bytes 196616 | tf_op jit(solution)/shard_map/ppermute | solution.py:923
  5.9 3.1 %collective-permute-start.4 = (f32[10,32,128]{2,1,0:T(8,128)S(1)}, f32[10,32,128]{2,1,0:T(8,128)S(1)}, u32[]{:S(2)}, u32[]{:S(2)}) collective-permute-start(f32[10,32,128]{2,1,0:T(8,128)S(1)} %get-tuple-element.50), channel_id=1, source_target_pairs={{0,4},{1,5},{2,6},{3,7},{4,0},{5,1},{6,2},{7,3},{8,12},{9,13},{10,... | collective-permute-start | bytes 491528 | tf_op jit(solution)/shard_map/ppermute | solution.py:923
  9.1 0.2 shard_map.150
  9.3 0.6 %collective-permute-start.2 = (f32[296,128]{1,0:T(8,128)S(1)}, f32[296,128]{1,0:T(8,128)S(1)}, u32[]{:S(2)}, u32[]{:S(2)}) collective-permute-start(f32[296,128]{1,0:T(8,128)S(1)} %get-tuple-element.43.after), channel_id=1, source_target_pairs={{0,1},{4,5},{8,9},{12,13},{1,0},{5,4},{9,8},{13,12},{2,3},{6,7},{1... | collective-permute-start | bytes 454664 | tf_op jit(solution)/shard_map/ppermute | solution.py:923
  9.8 2.2 %collective-permute-start.3 = (f32[296,128]{1,0:T(8,128)S(1)}, f32[296,128]{1,0:T(8,128)S(1)}, u32[]{:S(2)}, u32[]{:S(2)}) collective-permute-start(f32[296,128]{1,0:T(8,128)S(1)} %get-tuple-element.44), channel_id=1, source_target_pairs={{0,4},{4,0},{8,12},{12,8},{1,2},{5,6},{9,10},{13,14},{2,1},{6,5},{... | collective-permute-start | bytes 454664 | tf_op jit(solution)/shard_map/ppermute | solution.py:923
  12.0 0.7 %collective-permute-done.4.refs_2_.low = f32[10,32,128]{2,1,0:T(8,128)S(1)} collective-permute-done((f32[10,32,128]{2,1,0:T(8,128)S(1)}, f32[10,32,128]{2,1,0:T(8,128)S(1)}, u32[]{:S(2)}, u32[]{:S(2)}) %collective-permute-start.4) | collective-permute-done | bytes 163872 | tf_op jit(solution)/shard_map/ppermute | solution.py:923
  12.7 0.4 shard_map.153
  13.3 0.1 collective-permute-start.6
  13.4 2.2 %collective-permute-start.7 = (f32[744,128]{1,0:T(8,128)S(1)}, f32[744,128]{1,0:T(8,128)S(1)}, u32[]{:S(2)}, u32[]{:S(2)}) collective-permute-start(f32[744,128]{1,0:T(8,128)S(1)} %get-tuple-element.53), channel_id=1, source_target_pairs={{0,4},{4,0},{8,12},{12,8},{1,2},{5,6},{9,10},{13,14},{2,1},{6,5},{... | collective-permute-start | bytes 1142792 | tf_op jit(solution)/shard_map/ppermute | solution.py:923
  15.5 1.6 %shard_map.151 = (f32[8,128]{1,0:T(8,128)S(1)}, f32[16,128]{1,0:T(8,128)S(1)}) custom-call(s32[64,32,128]{2,1,0:T(8,128)S(1)} %get-tuple-element.45.zone.refs_1_, f32[64,32,128]{2,1,0:T(8,128)S(1)} %get-tuple-element.46.scale.refs_0_, f32[64,32,128]{2,1,0:T(8,128)S(1)} %get-tuple-element.40.refs_0_.load, f32[296,128]{1,0:T(8,128)S(1)} %get-tuple-element.43.after, ...), custom_call_target="tpu_custom_call" | custom-call | tf_op jit(solution)/shard_map/pallas_call | solution.py:983
  17.3 7.3 %shard_map.152 = (f32[74,48,128]{2,1,0:T(8,128)S(1)}, f32[64,32,128]{2,1,0:T(8,128)S(1)}, f32[32,128]{1,0:T(8,128)S(1)}, f32[40,72,128]{2,1,0:T(8,128)S(1)}) custom-call(f32[64,32,128]{2,1,0:T(8,128)S(1)} %get-tuple-element.40.refs_0_.load, f32[4,32,128]{2,1,0:T(8,128)S(1)} %collective-permute-done.refs_1_.low, ...), custom_call_target="tpu_custom_call" | custom-call | flops 4000000000 | tf_op jit(solution)/shard_map/pallas_call | solution.py:989
  24.6 1.0 %shard_map.154 = (f32[16,128]{1,0:T(8,128)S(1)}, f32[176,128]{1,0:T(8,128)S(1)}, f32[176,128]{1,0:T(8,128)S(1)}) custom-call(s32[64,32,128]{2,1,0:T(8,128)S(1)} %get-tuple-element.45.zone.refs_1_, f32[64,32,128]{2,1,0:T(8,128)S(1)} %get-tuple-element.46.scale.refs_0_, f32[64,32,128]{2,1,0:T(8,128)S(1)} %get-tuple-element.48.local.refs_0_, ...), custom_call_target="tpu_custom_call" | custom-call | tf_op jit(solution)/shard_map/pallas_call | solution.py:997
  25.5 0.1 collective-permute-start.8
  25.6 3.3 %collective-permute-start.9 = (f32[176,128]{1,0:T(8,128)S(1)}, f32[176,128]{1,0:T(8,128)S(1)}, u32[]{:S(2)}, u32[]{:S(2)}) collective-permute-start(f32[176,128]{1,0:T(8,128)S(1)} %get-tuple-element.56), channel_id=1, source_target_pairs={{0,12},{1,13},{2,14},{3,15},{4,8},{5,9},{6,10},{7,11},{8,4},{9,5},... | collective-permute-start | bytes 270344 | tf_op jit(solution)/shard_map/ppermute | solution.py:923
  28.9 0.2 collective-permute-start.10
  29.1 2.3 %shard_map.155 = (f32[74,48,128]{2,1,0:T(8,128)S(1)}, f32[74,48,128]{2,1,0:T(8,128)S(1)}, f32[74,48,128]{2,1,0:T(8,128)S(1)}, f32[74,48,128]{2,1,0:T(8,128)S(1)}) custom-call(s32[64,32,128]{2,1,0:T(8,128)S(1)} %get-tuple-element.45.zone.refs_1_, f32[64,32,128]{2,1,0:T(8,128)S(1)} %get-tuple-element.46.scale.refs_0_, ...), custom_call_target="tpu_custom_call" | custom-call | flops 1000000000 | tf_op jit(solution)/shard_map/pallas_call | solution.py:1005
  31.4 3.3 %collective-permute-done.10.refs_6_ = f32[16,128]{1,0:T(8,128)S(1)} collective-permute-done((f32[16,128]{1,0:T(8,128)S(1)}, f32[16,128]{1,0:T(8,128)S(1)}, u32[]{:S(2)}, u32[]{:S(2)}) %collective-permute-start.10) | collective-permute-done | bytes 8224 | tf_op jit(solution)/shard_map/ppermute | solution.py:928
  34.6 0.2 shard_map.156
  34.9 0.1 collective-permute-start.11
  35.0 0.5 collective-permute-start.12
  35.5 0.9 %collective-permute-done.11.message.left = f32[392,128]{1,0:T(8,128)S(1)} collective-permute-done((f32[392,128]{1,0:T(8,128)S(1)}, f32[392,128]{1,0:T(8,128)S(1)}, u32[]{:S(2)}, u32[]{:S(2)}) %collective-permute-start.11) | collective-permute-done | bytes 200736 | tf_op jit(solution)/shard_map/ppermute | solution.py:923
  36.4 0.7 %collective-permute-start.13 = (f32[16,128]{1,0:T(8,128)S(1)}, f32[16,128]{1,0:T(8,128)S(1)}, u32[]{:S(2)}, u32[]{:S(2)}) collective-permute-start(f32[16,128]{1,0:T(8,128)S(1)} %shard_map.157.refs_0_), channel_id=1, source_target_pairs={{0,2},{1,3},{2,0},{3,1},{4,6},{5,7},{6,4},{7,5},{8,10},{9,11},{10,... | collective-permute-start | bytes 24584 | tf_op jit(solution)/shard_map/ppermute | solution.py:928
  37.1 1.8 %shard_map.159 = (f32[74,48,128]{2,1,0:T(8,128)S(1)}, f32[74,48,128]{2,1,0:T(8,128)S(1)}) custom-call(f32[74,48,128]{2,1,0:T(8,128)S(1)} %get-tuple-element.64.zone_window, f32[74,48,128]{2,1,0:T(8,128)S(1)} %get-tuple-element.65.scale_window, f32[3,3]{1,0:T(4,128)S(1)} %copy-done, f32[3]{0:T(128)S(1)} %copy-done.1), custom_call_target="tpu_custom_call" | custom-call | flops 1000000000 | tf_op jit(solution)/shard_map/pallas_call | solution.py:1011
  38.9 2.0 %collective-permute-done.13.refs_1_ = f32[16,128]{1,0:T(8,128)S(1)} collective-permute-done((f32[16,128]{1,0:T(8,128)S(1)}, f32[16,128]{1,0:T(8,128)S(1)}, u32[]{:S(2)}, u32[]{:S(2)}) %collective-permute-start.13) | collective-permute-done | bytes 8224 | tf_op jit(solution)/shard_map/ppermute | solution.py:928
  40.9 1.5 %shard_map.158.answers = f32[8,128]{1,0:T(8,128)S(1)} custom-call(f32[16,128]{1,0:T(8,128)S(1)} %shard_map.157.refs_0_, f32[16,128]{1,0:T(8,128)S(1)} %collective-permute-done.13.refs_1_), custom_call_target="tpu_custom_call" | custom-call | tf_op jit(solution)/shard_map/pallas_call | solution.py:1026
  42.4 7.8 %shard_map.160 = (f32[64,32,128]{2,1,0:T(8,128)S(1)}, f32[32,128]{1,0:T(8,128)S(1)}, f32[32,128]{1,0:T(8,128)S(1)}, f32[64,128]{1,0:T(8,128)S(1)}, f32[64,128]{1,0:T(8,128)S(1)}, /*index=5*/f32[64,32,128]{2,1,0:T(8,128)}) custom-call(f32[64,32,128]{2,1,0:T(8,128)S(1)} %get-tuple-element.48.local.refs_0_, ...), custom_call_target="tpu_custom_call" | custom-call | flops 4000000000 | tf_op jit(solution)/shard_map/pallas_call | solution.py:1032
  50.4 0.6 collective-permute-start.17
  50.9 1.5 %collective-permute-start.14 = (f32[32,128]{1,0:T(8,128)S(1)}, f32[32,128]{1,0:T(8,128)S(1)}, u32[]{:S(2)}, u32[]{:S(2)}) collective-permute-start(f32[32,128]{1,0:T(8,128)S(1)} %get-tuple-element.71), channel_id=1, source_target_pairs={{0,4},{1,5},{2,6},{3,7},{4,0},{5,1},{6,2},{7,3},{8,12},{9,13},{10,... | collective-permute-start | bytes 49160 | tf_op jit(solution)/shard_map/ppermute | solution.py:923
  52.5 2.0 %shard_map.161 = (f32[2,32,128]{2,1,0:T(8,128)S(1)}, f32[2,64,8,128]{3,2,1,0:T(8,128)S(1)}, f32[64,32,128]{2,1,0:T(8,128)}) custom-call(f32[64,32,128]{2,1,0:T(8,128)S(1)} %get-tuple-element.40.refs_0_.load, f32[64,32,128]{2,1,0:T(8,128)S(1)} %get-tuple-element.70.iterate, f32[74,48,128]{2,1,0:T(8,128)S(1)} %get-tuple-element.58.refs_7_.rest_0_.to_long, ...), custom_call_target="tpu_custom_call" | custom-call | flops 1000000000 | tf_op jit(solution)/shard_map/pallas_call | solution.py:1042
  54.5 0.1 collective-permute-done.14.low
  54.7 0.9 %shard_map.162 = f32[64,32,128]{2,1,0:T(8,128)} custom-call(f32[64,32,128]{2,1,0:T(8,128)S(1)} %get-tuple-element.70.iterate, f32[32,128]{1,0:T(8,128)S(1)} %collective-permute-done.14.low, f32[32,128]{1,0:T(8,128)S(1)} %collective-permute-done.15.high, f32[64,128]{1,0:T(8,128)S(1)} %collective-permute-done.16.left, ...), custom_call_target="tpu_custom_call", output_to_operand_aliasing={{}: (9, {})} | custom-call | tf_op jit(solution)/shard_map/pallas_call | solution.py:1054
  (40 shorter events, 0.2 us)
Async XLA Ops:
  2.8 12.7 %copy-start = (f32[3,3]{1,0:T(4,128)S(1)}, f32[3,3]{1,0:T(4,128)}, u32[]{:S(2)}) copy-start(f32[3,3]{1,0:T(4,128)} %diffusivity.9) | copy-start | bytes 112
  2.8 12.7 %copy-start.1 = (f32[3]{0:T(128)S(1)}, f32[3]{0:T(128)}, u32[]{:S(2)}) copy-start(f32[3]{0:T(128)} %decay.5) | copy-start | bytes 40
  2.8 6.2 %collective-permute-start = (f32[4,32,128]{2,1,0:T(8,128)S(1)}, f32[4,32,128]{2,1,0:T(8,128)S(1)}, u32[]{:S(2)}, u32[]{:S(2)}) collective-permute-start(f32[4,32,128]{2,1,0:T(8,128)S(1)} %get-tuple-element.41), channel_id=1, source_target_pairs={{0,4},{1,5},{2,6},{3,7},{4,0},{5,1},{6,2},{7,3},{8,12},{9,13},{10,... | collective-permute-start | bytes 196616 | tf_op jit(solution)/shard_map/ppermute | solution.py:923
  5.9 3.2 %collective-permute-start.1 = (f32[4,32,128]{2,1,0:T(8,128)S(1)}, f32[4,32,128]{2,1,0:T(8,128)S(1)}, u32[]{:S(2)}, u32[]{:S(2)}) collective-permute-start(f32[4,32,128]{2,1,0:T(8,128)S(1)} %get-tuple-element.42), channel_id=1, source_target_pairs={{0,1},{1,0},{2,3},{3,2},{4,8},{5,9},{6,10},{7,11},{8,4},{9,5},{10,... | collective-permute-start | bytes 196616 | tf_op jit(solution)/shard_map/ppermute | solution.py:923
  5.9 6.8 %collective-permute-start.4 = (f32[10,32,128]{2,1,0:T(8,128)S(1)}, f32[10,32,128]{2,1,0:T(8,128)S(1)}, u32[]{:S(2)}, u32[]{:S(2)}) collective-permute-start(f32[10,32,128]{2,1,0:T(8,128)S(1)} %get-tuple-element.50), channel_id=1, source_target_pairs={{0,4},{1,5},{2,6},{3,7},{4,0},{5,1},{6,2},{7,3},{8,12},{9,13},{10,... | collective-permute-start | bytes 491528 | tf_op jit(solution)/shard_map/ppermute | solution.py:923
  9.1 3.6 %collective-permute-start.5 = (f32[10,32,128]{2,1,0:T(8,128)S(1)}, f32[10,32,128]{2,1,0:T(8,128)S(1)}, u32[]{:S(2)}, u32[]{:S(2)}) collective-permute-start(f32[10,32,128]{2,1,0:T(8,128)S(1)} %get-tuple-element.51), channel_id=1, source_target_pairs={{0,1},{1,0},{2,3},{3,2},{4,8},{5,9},{6,10},{7,11},{8,4},{9,5},{10,... | collective-permute-start | bytes 491528 | tf_op jit(solution)/shard_map/ppermute | solution.py:923
  9.3 7.9 %collective-permute-start.2 = (f32[296,128]{1,0:T(8,128)S(1)}, f32[296,128]{1,0:T(8,128)S(1)}, u32[]{:S(2)}, u32[]{:S(2)}) collective-permute-start(f32[296,128]{1,0:T(8,128)S(1)} %get-tuple-element.43.after), channel_id=1, source_target_pairs={{0,1},{4,5},{8,9},{12,13},{1,0},{5,4},{9,8},{13,12},{2,3},{6,7},{1... | collective-permute-start | bytes 454664 | tf_op jit(solution)/shard_map/ppermute | solution.py:923
  9.8 7.3 %collective-permute-start.3 = (f32[296,128]{1,0:T(8,128)S(1)}, f32[296,128]{1,0:T(8,128)S(1)}, u32[]{:S(2)}, u32[]{:S(2)}) collective-permute-start(f32[296,128]{1,0:T(8,128)S(1)} %get-tuple-element.44), channel_id=1, source_target_pairs={{0,4},{4,0},{8,12},{12,8},{1,2},{5,6},{9,10},{13,14},{2,1},{6,5},{... | collective-permute-start | bytes 454664 | tf_op jit(solution)/shard_map/ppermute | solution.py:923
  13.2 4.0 %copy-start.2 = (bf16[256,256]{1,0:T(8,128)(2,1)S(1)}, bf16[256,256]{1,0:T(8,128)(2,1)}, u32[]{:S(2)}) copy-start(bf16[256,256]{1,0:T(8,128)(2,1)} %constant.22.clone.rest_4_.rest_9_) | copy-start | bytes 393220
  13.2 4.0 %copy-start.3 = (bf16[192,240]{1,0:T(8,128)(2,1)S(1)}, bf16[192,240]{1,0:T(8,128)(2,1)}, u32[]{:S(2)}) copy-start(bf16[192,240]{1,0:T(8,128)(2,1)} %constant.20.clone.rest_2_.rest_7_) | copy-start | bytes 276484
  13.2 4.0 %copy-start.4 = (bf16[144,160]{1,0:T(8,128)(2,1)S(1)}, bf16[144,160]{1,0:T(8,128)(2,1)}, u32[]{:S(2)}) copy-start(bf16[144,160]{1,0:T(8,128)(2,1)} %constant.19.clone.rest_1_.rest_6_) | copy-start | bytes 138244
  13.2 4.0 %copy-start.5 = (bf16[256,128]{1,0:T(8,128)(2,1)S(1)}, bf16[256,128]{1,0:T(8,128)(2,1)}, u32[]{:S(2)}) copy-start(bf16[256,128]{1,0:T(8,128)(2,1)} %constant.23.clone.rest_5_.rest_10_) | copy-start | bytes 196612
  13.2 4.0 %copy-start.6 = (bf16[96,144]{1,0:T(8,128)(2,1)S(1)}, bf16[96,144]{1,0:T(8,128)(2,1)}, u32[]{:S(2)}) copy-start(bf16[96,144]{1,0:T(8,128)(2,1)} %constant.21.clone.rest_3_.rest_8_) | copy-start | bytes 82948
  13.2 4.0 %copy-start.7 = (f32[72,128]{1,0:T(8,128)S(1)}, f32[72,128]{1,0:T(8,128)}, u32[]{:S(2)}) copy-start(f32[72,128]{1,0:T(8,128)} %constant.24.clone.rest_6_.rest_11_) | copy-start | bytes 110596
  13.2 4.0 %copy-start.8 = (bf16[80,96]{1,0:T(8,128)(2,1)S(1)}, bf16[80,96]{1,0:T(8,128)(2,1)}, u32[]{:S(2)}) copy-start(bf16[80,96]{1,0:T(8,128)(2,1)} %constant.18.clone.rest_0_.rest_5_) | copy-start | bytes 46084
  13.3 4.0 %copy-start.9 = (f32[1,128]{1,0:T(1,128)S(1)}, f32[1,128]{1,0:T(1,128)}, u32[]{:S(2)}) copy-start(f32[1,128]{1,0:T(1,128)} %constant.25.clone.rest_7_.rest_12_) | copy-start | bytes 1540
  13.3 4.0 %copy-start.10 = (f32[1,40]{1,0:T(1,128)S(1)}, f32[1,40]{1,0:T(1,128)}, u32[]{:S(2)}) copy-start(f32[1,40]{1,0:T(1,128)} %constant.26.clone.rest_8_.rest_13_) | copy-start | bytes 484
  13.3 11.3 %collective-permute-start.6 = (f32[744,128]{1,0:T(8,128)S(1)}, f32[744,128]{1,0:T(8,128)S(1)}, u32[]{:S(2)}, u32[]{:S(2)}) collective-permute-start(f32[744,128]{1,0:T(8,128)S(1)} %get-tuple-element.52), channel_id=1, source_target_pairs={{0,1},{4,5},{8,9},{12,13},{1,0},{5,4},{9,8},{13,12},{2,3},{6,7},{1... | collective-permute-start | bytes 1142792 | tf_op jit(solution)/shard_map/ppermute | solution.py:923
  13.4 11.2 %collective-permute-start.7 = (f32[744,128]{1,0:T(8,128)S(1)}, f32[744,128]{1,0:T(8,128)S(1)}, u32[]{:S(2)}, u32[]{:S(2)}) collective-permute-start(f32[744,128]{1,0:T(8,128)S(1)} %get-tuple-element.53), channel_id=1, source_target_pairs={{0,4},{4,0},{8,12},{12,8},{1,2},{5,6},{9,10},{13,14},{2,1},{6,5},{... | collective-permute-start | bytes 1142792 | tf_op jit(solution)/shard_map/ppermute | solution.py:923
  25.5 9.1 %collective-permute-start.8 = (f32[176,128]{1,0:T(8,128)S(1)}, f32[176,128]{1,0:T(8,128)S(1)}, u32[]{:S(2)}, u32[]{:S(2)}) collective-permute-start(f32[176,128]{1,0:T(8,128)S(1)} %get-tuple-element.55), channel_id=1, source_target_pairs={{0,4},{1,5},{2,6},{3,7},{4,0},{5,1},{6,2},{7,3},{8,12},{9,13},{10,... | collective-permute-start | bytes 270344 | tf_op jit(solution)/shard_map/ppermute | solution.py:923
  25.6 9.0 %collective-permute-start.9 = (f32[176,128]{1,0:T(8,128)S(1)}, f32[176,128]{1,0:T(8,128)S(1)}, u32[]{:S(2)}, u32[]{:S(2)}) collective-permute-start(f32[176,128]{1,0:T(8,128)S(1)} %get-tuple-element.56), channel_id=1, source_target_pairs={{0,12},{1,13},{2,14},{3,15},{4,8},{5,9},{6,10},{7,11},{8,4},{9,5},... | collective-permute-start | bytes 270344 | tf_op jit(solution)/shard_map/ppermute | solution.py:923
  28.9 5.7 %collective-permute-start.10 = (f32[16,128]{1,0:T(8,128)S(1)}, f32[16,128]{1,0:T(8,128)S(1)}, u32[]{:S(2)}, u32[]{:S(2)}) collective-permute-start(f32[16,128]{1,0:T(8,128)S(1)} %get-tuple-element.57.refs_3_), channel_id=1, source_target_pairs={{0,8},{4,12},{8,0},{12,4},{1,9},{5,13},{9,1},{13,5},{2,10},{6,14},... | collective-permute-start | bytes 24584 | tf_op jit(solution)/shard_map/ppermute | solution.py:928
  34.9 1.5 %collective-permute-start.11 = (f32[392,128]{1,0:T(8,128)S(1)}, f32[392,128]{1,0:T(8,128)S(1)}, u32[]{:S(2)}, u32[]{:S(2)}) collective-permute-start(f32[392,128]{1,0:T(8,128)S(1)} %get-tuple-element.59), channel_id=1, source_target_pairs={{0,1},{4,5},{8,9},{12,13},{1,0},{5,4},{9,8},{13,12},{2,3},{6,7},{1... | collective-permute-start | bytes 602120 | tf_op jit(solution)/shard_map/ppermute | solution.py:923
  35.0 7.4 %collective-permute-start.12 = (f32[392,128]{1,0:T(8,128)S(1)}, f32[392,128]{1,0:T(8,128)S(1)}, u32[]{:S(2)}, u32[]{:S(2)}) collective-permute-start(f32[392,128]{1,0:T(8,128)S(1)} %get-tuple-element.60), channel_id=1, source_target_pairs={{0,4},{4,0},{8,12},{12,8},{1,2},{5,6},{9,10},{13,14},{2,1},{6,5},{... | collective-permute-start | bytes 602120 | tf_op jit(solution)/shard_map/ppermute | solution.py:923
  36.4 4.6 %collective-permute-start.13 = (f32[16,128]{1,0:T(8,128)S(1)}, f32[16,128]{1,0:T(8,128)S(1)}, u32[]{:S(2)}, u32[]{:S(2)}) collective-permute-start(f32[16,128]{1,0:T(8,128)S(1)} %shard_map.157.refs_0_), channel_id=1, source_target_pairs={{0,2},{1,3},{2,0},{3,1},{4,6},{5,7},{6,4},{7,5},{8,10},{9,11},{10,... | collective-permute-start | bytes 24584 | tf_op jit(solution)/shard_map/ppermute | solution.py:928
  50.3 4.4 %collective-permute-start.16 = (f32[64,128]{1,0:T(8,128)S(1)}, f32[64,128]{1,0:T(8,128)S(1)}, u32[]{:S(2)}, u32[]{:S(2)}) collective-permute-start(f32[64,128]{1,0:T(8,128)S(1)} %get-tuple-element.73), channel_id=1, source_target_pairs={{0,1},{4,5},{8,9},{12,13},{1,0},{5,4},{9,8},{13,12},{2,3},{6,7},{1... | collective-permute-start | bytes 98312 | tf_op jit(solution)/shard_map/ppermute | solution.py:923
  50.4 4.3 %collective-permute-start.17 = (f32[64,128]{1,0:T(8,128)S(1)}, f32[64,128]{1,0:T(8,128)S(1)}, u32[]{:S(2)}, u32[]{:S(2)}) collective-permute-start(f32[64,128]{1,0:T(8,128)S(1)} %get-tuple-element.74), channel_id=1, source_target_pairs={{0,4},{4,0},{8,12},{12,8},{1,2},{5,6},{9,10},{13,14},{2,1},{6,5},{... | collective-permute-start | bytes 98312 | tf_op jit(solution)/shard_map/ppermute | solution.py:923
  50.9 3.7 %collective-permute-start.14 = (f32[32,128]{1,0:T(8,128)S(1)}, f32[32,128]{1,0:T(8,128)S(1)}, u32[]{:S(2)}, u32[]{:S(2)}) collective-permute-start(f32[32,128]{1,0:T(8,128)S(1)} %get-tuple-element.71), channel_id=1, source_target_pairs={{0,4},{1,5},{2,6},{3,7},{4,0},{5,1},{6,2},{7,3},{8,12},{9,13},{10,... | collective-permute-start | bytes 49160 | tf_op jit(solution)/shard_map/ppermute | solution.py:923
  52.5 2.2 %collective-permute-start.15 = (f32[32,128]{1,0:T(8,128)S(1)}, f32[32,128]{1,0:T(8,128)S(1)}, u32[]{:S(2)}, u32[]{:S(2)}) collective-permute-start(f32[32,128]{1,0:T(8,128)S(1)} %get-tuple-element.72), channel_id=1, source_target_pairs={{0,1},{1,0},{2,3},{3,2},{4,8},{5,9},{6,10},{7,11},{8,4},{9,5},{10,... | collective-permute-start | bytes 49160 | tf_op jit(solution)/shard_map/ppermute | solution.py:923

commit v13 on v12

--- a/solution.py
+++ b/solution.py
@@ -65,11 +65,12 @@
 
 def pieces(values, count):
     parts = []
-    for _ in range(count):
-        part = values.astype(jnp.bfloat16)
+    for _ in range(count - 1):
+        scaled = values * 65537.0
+        part = scaled - (scaled - values)
         parts.append(part)
-        values = values - part.astype(jnp.float32)
-    return parts
+        values = values - part
+    return parts + [values]
 
 
 def left_table(table, depth, count):
@@ -79,9 +80,9 @@
     parts = []
     rest = wide
     for _ in range(count):
-        part = rest.astype(ml_dtypes.bfloat16)
+        part = rest.astype(ml_dtypes.bfloat16).astype(np.float32)
         parts.append(part)
-        rest = rest - part.astype(np.float32)
+        rest = rest - part
     blank = np.zeros_like(parts[0])
     lines = []
     for index in range(count):
@@ -93,15 +94,15 @@
 def right_tables(table):
     rest, parts = table, []
     for _ in range(3):
-        part = rest.astype(ml_dtypes.bfloat16)
+        part = rest.astype(ml_dtypes.bfloat16).astype(np.float32)
         parts.append(part)
-        rest = rest - part.astype(np.float32)
+        rest = rest - part
     both = np.concatenate([parts[0], parts[1]], axis=1)
     return np.concatenate([both, both], axis=0), np.concatenate([parts[2], parts[0]], axis=0)
 
 
 def padded(size):
-    return -(-size // 16) * 16
+    return -(-size // 8) * 8
 
 
 FORWARD, BACKWARD = 2, 3
@@ -135,24 +136,28 @@
 N_TABLES = 9
 
 
-def bf16_dot(left, right):
+def one_pass(left, right):
     return lax.dot_general(
-        left, right, (((1,), (0,)), ((), ())), preferred_element_type=jnp.float32
+        left,
+        right,
+        (((1,), (0,)), ((), ())),
+        precision=lax.Precision.DEFAULT,
+        preferred_element_type=jnp.float32,
     )
 
 
 def dot_left(table, values, count, rows):
-    total = bf16_dot(table, jnp.concatenate(pieces(values, count), axis=0))
+    total = one_pass(table, jnp.concatenate(pieces(values, count), axis=0))
     return sum(total[index * rows : (index + 1) * rows] for index in range(1, count)) + total[:rows]
 
 
 def dot_right(values, main, rest, count):
     deep = values.shape[1]
     parts = pieces(values, count)
-    total = bf16_dot(jnp.concatenate(parts[:2], axis=1), main)
+    total = one_pass(jnp.concatenate(parts[:2], axis=1), main)
     result = total[:, :deep] + total[:, deep:]
     if count == 3:
-        result = result + bf16_dot(jnp.concatenate([parts[0], parts[2]], axis=1), rest)
+        result = result + one_pass(jnp.concatenate([parts[0], parts[2]], axis=1), rest)
     return result
 
 
@@ -170,9 +175,9 @@
     into_y, into_x = into_y[...], into_x[...]
     if col_mask is not None:
         mask = jnp.concatenate([col_mask] * FORWARD, axis=1)
-        into_y = (into_y.astype(jnp.float32) * mask).astype(jnp.bfloat16)
+        into_y = into_y * mask
         mask = jnp.concatenate([row_mask] * FORWARD, axis=1)
-        into_x = (into_x.astype(jnp.float32) * mask).astype(jnp.bfloat16)
+        into_x = into_x * mask
     from_x, from_y, main_z, rest_z = from_x[...], from_y[...], main_z[...], rest_z[...]
     spectral_flat = spectral.reshape(box.ey * deep_x, deep)
     middle_flat = middle.reshape(box.long * deep_y, deep)

time: 55.9 us -> 55.4 us (level)
  Pallas kernels: 29.3 us -> 28.5 us
where the time goes in v13:
time: 55.4 us; the launch traced here: 55.2 us
  Pallas kernels  28.5 us (51%)
  starting transfers between devices  18.3 us (33%)
  waiting for transfers between devices  7.25 us (13%)
  between operations  1.09 us (2%)
    ppermute x8, starting transfers between devices, exchange(): lax.ppermute(first, axes, ways[0])  8.72 us
    ppermute x8, starting transfers between devices, exchange(): lax.ppermute(second, axes, ways[1])  8.66 us
    pallas_call x1, Pallas kernels, on_device(): call(functools.partial(second_solve, box), (cells, row, row, col, col, ce...  7.4 us
    pallas_call x1, Pallas kernels, on_device(): call(functools.partial(first_solve, box), (window, cells, f32(across, dee...  7.19 us
    ppermute x2, waiting for transfers between devices, two_away(): return lax.ppermute(table, axis, [(i, (i + 2) % size) for i in range(size)])  5.27 us
    pallas_call x1, Pallas kernels, on_device(): call(functools.partial(side_weights, box), (window,) * 4, [VMEM] * 6 + [S...  2.25 us
    pallas_call x1, Pallas kernels, on_device(): call(functools.partial(bring_edges, box), (whole_zone, cells, cells) + (f...  2.19 us
    ppermute x8, waiting for transfers between devices, exchange(): lax.ppermute(first, axes, ways[0])  1.94 us
  transfers between devices with their start and end apart: 18, of which 5 were waited for; matrix products, arithmetic and copies ran while one was open for 0% of the time, Pallas kernels for 31%

profile of v13, /device:TPU:0, one launch (start us, length us, event | category | flops | bytes accessed | tf_op | source)
XLA Modules:
  0.0 55.2 jit_solution(1012888790341749740)
XLA Ops:
  0.6 2.2 %shard_map.149 = (s32[64,32,128]{2,1,0:T(8,128)S(1)}, f32[64,32,128]{2,1,0:T(8,128)S(1)}, f32[64,32,128]{2,1,0:T(8,128)S(1)}, f32[4,32,128]{2,1,0:T(8,128)S(1)},...) custom-call(s32[64,32,128]{2,1,0:T(8,128)} %zone.1, f32[64,32,128]{2,1,0:T(8,128)} %scale.1, ...), custom_call_target="tpu_custom_call" | custom-call | tf_op jit(solution)/shard_map/pallas_call | solution.py:978
  2.8 3.1 %collective-permute-start = (f32[4,32,128]{2,1,0:T(8,128)S(1)}, f32[4,32,128]{2,1,0:T(8,128)S(1)}, u32[]{:S(2)}, u32[]{:S(2)}) collective-permute-start(f32[4,32,128]{2,1,0:T(8,128)S(1)} %get-tuple-element.41), channel_id=1, source_target_pairs={{0,4},{1,5},{2,6},{3,7},{4,0},{5,1},{6,2},{7,3},{8,12},{9,13},{10,... | collective-permute-start | bytes 196616 | tf_op jit(solution)/shard_map/ppermute | solution.py:928
  5.9 3.1 %collective-permute-start.4 = (f32[10,32,128]{2,1,0:T(8,128)S(1)}, f32[10,32,128]{2,1,0:T(8,128)S(1)}, u32[]{:S(2)}, u32[]{:S(2)}) collective-permute-start(f32[10,32,128]{2,1,0:T(8,128)S(1)} %get-tuple-element.50), channel_id=1, source_target_pairs={{0,4},{1,5},{2,6},{3,7},{4,0},{5,1},{6,2},{7,3},{8,12},{9,13},{10,... | collective-permute-start | bytes 491528 | tf_op jit(solution)/shard_map/ppermute | solution.py:928
  9.1 0.2 shard_map.150
  9.3 0.6 %collective-permute-start.2 = (f32[296,128]{1,0:T(8,128)S(1)}, f32[296,128]{1,0:T(8,128)S(1)}, u32[]{:S(2)}, u32[]{:S(2)}) collective-permute-start(f32[296,128]{1,0:T(8,128)S(1)} %get-tuple-element.43.after), channel_id=1, source_target_pairs={{0,1},{4,5},{8,9},{12,13},{1,0},{5,4},{9,8},{13,12},{2,3},{6,7},{1... | collective-permute-start | bytes 454664 | tf_op jit(solution)/shard_map/ppermute | solution.py:928
  9.8 2.2 %collective-permute-start.3 = (f32[296,128]{1,0:T(8,128)S(1)}, f32[296,128]{1,0:T(8,128)S(1)}, u32[]{:S(2)}, u32[]{:S(2)}) collective-permute-start(f32[296,128]{1,0:T(8,128)S(1)} %get-tuple-element.44), channel_id=1, source_target_pairs={{0,4},{4,0},{8,12},{12,8},{1,2},{5,6},{9,10},{13,14},{2,1},{6,5},{... | collective-permute-start | bytes 454664 | tf_op jit(solution)/shard_map/ppermute | solution.py:928
  12.0 0.7 %collective-permute-done.4.refs_2_.low = f32[10,32,128]{2,1,0:T(8,128)S(1)} collective-permute-done((f32[10,32,128]{2,1,0:T(8,128)S(1)}, f32[10,32,128]{2,1,0:T(8,128)S(1)}, u32[]{:S(2)}, u32[]{:S(2)}) %collective-permute-start.4) | collective-permute-done | bytes 163872 | tf_op jit(solution)/shard_map/ppermute | solution.py:928
  12.7 0.4 shard_map.153
  13.3 0.1 collective-permute-start.6
  13.4 2.2 %collective-permute-start.7 = (f32[744,128]{1,0:T(8,128)S(1)}, f32[744,128]{1,0:T(8,128)S(1)}, u32[]{:S(2)}, u32[]{:S(2)}) collective-permute-start(f32[744,128]{1,0:T(8,128)S(1)} %get-tuple-element.53), channel_id=1, source_target_pairs={{0,4},{4,0},{8,12},{12,8},{1,2},{5,6},{9,10},{13,14},{2,1},{6,5},{... | collective-permute-start | bytes 1142792 | tf_op jit(solution)/shard_map/ppermute | solution.py:928
  15.5 1.6 %shard_map.151 = (f32[8,128]{1,0:T(8,128)S(1)}, f32[16,128]{1,0:T(8,128)S(1)}) custom-call(s32[64,32,128]{2,1,0:T(8,128)S(1)} %get-tuple-element.45.zone.refs_1_, f32[64,32,128]{2,1,0:T(8,128)S(1)} %get-tuple-element.46.scale.refs_0_, f32[64,32,128]{2,1,0:T(8,128)S(1)} %get-tuple-element.40.refs_0_.load, f32[296,128]{1,0:T(8,128)S(1)} %get-tuple-element.43.after, ...), custom_call_target="tpu_custom_call" | custom-call | tf_op jit(solution)/shard_map/pallas_call | solution.py:988
  17.2 7.2 %shard_map.152 = (f32[74,48,128]{2,1,0:T(8,128)S(1)}, f32[64,32,128]{2,1,0:T(8,128)S(1)}, f32[32,128]{1,0:T(8,128)S(1)}, f32[40,72,128]{2,1,0:T(8,128)S(1)}) custom-call(f32[64,32,128]{2,1,0:T(8,128)S(1)} %get-tuple-element.40.refs_0_.load, f32[4,32,128]{2,1,0:T(8,128)S(1)} %collective-permute-done.refs_1_.low, ...), custom_call_target="tpu_custom_call" | custom-call | flops 4000000000 | tf_op jit(solution)/shard_map/pallas_call | solution.py:994
  24.5 1.0 %shard_map.154 = (f32[16,128]{1,0:T(8,128)S(1)}, f32[176,128]{1,0:T(8,128)S(1)}, f32[176,128]{1,0:T(8,128)S(1)}) custom-call(s32[64,32,128]{2,1,0:T(8,128)S(1)} %get-tuple-element.45.zone.refs_1_, f32[64,32,128]{2,1,0:T(8,128)S(1)} %get-tuple-element.46.scale.refs_0_, f32[64,32,128]{2,1,0:T(8,128)S(1)} %get-tuple-element.48.local.refs_0_, ...), custom_call_target="tpu_custom_call" | custom-call | tf_op jit(solution)/shard_map/pallas_call | solution.py:1002
  25.4 0.1 collective-permute-start.8
  25.5 3.3 %collective-permute-start.9 = (f32[176,128]{1,0:T(8,128)S(1)}, f32[176,128]{1,0:T(8,128)S(1)}, u32[]{:S(2)}, u32[]{:S(2)}) collective-permute-start(f32[176,128]{1,0:T(8,128)S(1)} %get-tuple-element.56), channel_id=1, source_target_pairs={{0,12},{1,13},{2,14},{3,15},{4,8},{5,9},{6,10},{7,11},{8,4},{9,5},... | collective-permute-start | bytes 270344 | tf_op jit(solution)/shard_map/ppermute | solution.py:928
  28.8 0.2 collective-permute-start.10
  29.0 2.3 %shard_map.155 = (f32[74,48,128]{2,1,0:T(8,128)S(1)}, f32[74,48,128]{2,1,0:T(8,128)S(1)}, f32[74,48,128]{2,1,0:T(8,128)S(1)}, f32[74,48,128]{2,1,0:T(8,128)S(1)}) custom-call(s32[64,32,128]{2,1,0:T(8,128)S(1)} %get-tuple-element.45.zone.refs_1_, f32[64,32,128]{2,1,0:T(8,128)S(1)} %get-tuple-element.46.scale.refs_0_, ...), custom_call_target="tpu_custom_call" | custom-call | flops 1000000000 | tf_op jit(solution)/shard_map/pallas_call | solution.py:1010
  31.2 3.3 %collective-permute-done.10.refs_6_ = f32[16,128]{1,0:T(8,128)S(1)} collective-permute-done((f32[16,128]{1,0:T(8,128)S(1)}, f32[16,128]{1,0:T(8,128)S(1)}, u32[]{:S(2)}, u32[]{:S(2)}) %collective-permute-start.10) | collective-permute-done | bytes 8224 | tf_op jit(solution)/shard_map/ppermute | solution.py:933
  34.5 0.2 shard_map.156
  34.8 0.1 collective-permute-start.11
  34.9 0.5 collective-permute-start.12
  35.4 0.9 %collective-permute-done.11.message.left = f32[392,128]{1,0:T(8,128)S(1)} collective-permute-done((f32[392,128]{1,0:T(8,128)S(1)}, f32[392,128]{1,0:T(8,128)S(1)}, u32[]{:S(2)}, u32[]{:S(2)}) %collective-permute-start.11) | collective-permute-done | bytes 200736 | tf_op jit(solution)/shard_map/ppermute | solution.py:928
  36.3 0.7 %collective-permute-start.13 = (f32[16,128]{1,0:T(8,128)S(1)}, f32[16,128]{1,0:T(8,128)S(1)}, u32[]{:S(2)}, u32[]{:S(2)}) collective-permute-start(f32[16,128]{1,0:T(8,128)S(1)} %shard_map.157.refs_0_), channel_id=1, source_target_pairs={{0,2},{1,3},{2,0},{3,1},{4,6},{5,7},{6,4},{7,5},{8,10},{9,11},{10,... | collective-permute-start | bytes 24584 | tf_op jit(solution)/shard_map/ppermute | solution.py:933
  37.0 1.9 %shard_map.159 = (f32[74,48,128]{2,1,0:T(8,128)S(1)}, f32[74,48,128]{2,1,0:T(8,128)S(1)}) custom-call(f32[74,48,128]{2,1,0:T(8,128)S(1)} %get-tuple-element.64.zone_window, f32[74,48,128]{2,1,0:T(8,128)S(1)} %get-tuple-element.65.scale_window, f32[3,3]{1,0:T(4,128)S(1)} %copy-done, f32[3]{0:T(128)S(1)} %copy-done.1), custom_call_target="tpu_custom_call" | custom-call | flops 1000000000 | tf_op jit(solution)/shard_map/pallas_call | solution.py:1016
  38.8 2.0 %collective-permute-done.13.refs_1_ = f32[16,128]{1,0:T(8,128)S(1)} collective-permute-done((f32[16,128]{1,0:T(8,128)S(1)}, f32[16,128]{1,0:T(8,128)S(1)}, u32[]{:S(2)}, u32[]{:S(2)}) %collective-permute-start.13) | collective-permute-done | bytes 8224 | tf_op jit(solution)/shard_map/ppermute | solution.py:933
  40.8 1.5 %shard_map.158.answers = f32[8,128]{1,0:T(8,128)S(1)} custom-call(f32[16,128]{1,0:T(8,128)S(1)} %shard_map.157.refs_0_, f32[16,128]{1,0:T(8,128)S(1)} %collective-permute-done.13.refs_1_), custom_call_target="tpu_custom_call" | custom-call | tf_op jit(solution)/shard_map/pallas_call | solution.py:1031
  42.3 7.4 %shard_map.160 = (f32[64,32,128]{2,1,0:T(8,128)S(1)}, f32[32,128]{1,0:T(8,128)S(1)}, f32[32,128]{1,0:T(8,128)S(1)}, f32[64,128]{1,0:T(8,128)S(1)}, f32[64,128]{1,0:T(8,128)S(1)}, /*index=5*/f32[64,32,128]{2,1,0:T(8,128)}) custom-call(f32[64,32,128]{2,1,0:T(8,128)S(1)} %get-tuple-element.48.local.refs_0_, ...), custom_call_target="tpu_custom_call" | custom-call | flops 4000000000 | tf_op jit(solution)/shard_map/pallas_call | solution.py:1037
  49.8 0.6 %collective-permute-start.17 = (f32[64,128]{1,0:T(8,128)S(1)}, f32[64,128]{1,0:T(8,128)S(1)}, u32[]{:S(2)}, u32[]{:S(2)}) collective-permute-start(f32[64,128]{1,0:T(8,128)S(1)} %get-tuple-element.74), channel_id=1, source_target_pairs={{0,4},{4,0},{8,12},{12,8},{1,2},{5,6},{9,10},{13,14},{2,1},{6,5},{... | collective-permute-start | bytes 98312 | tf_op jit(solution)/shard_map/ppermute | solution.py:928
  50.4 1.5 %collective-permute-start.14 = (f32[32,128]{1,0:T(8,128)S(1)}, f32[32,128]{1,0:T(8,128)S(1)}, u32[]{:S(2)}, u32[]{:S(2)}) collective-permute-start(f32[32,128]{1,0:T(8,128)S(1)} %get-tuple-element.71), channel_id=1, source_target_pairs={{0,4},{1,5},{2,6},{3,7},{4,0},{5,1},{6,2},{7,3},{8,12},{9,13},{10,... | collective-permute-start | bytes 49160 | tf_op jit(solution)/shard_map/ppermute | solution.py:928
  51.9 1.9 %shard_map.161 = (f32[2,32,128]{2,1,0:T(8,128)S(1)}, f32[2,64,8,128]{3,2,1,0:T(8,128)S(1)}, f32[64,32,128]{2,1,0:T(8,128)}) custom-call(f32[64,32,128]{2,1,0:T(8,128)S(1)} %get-tuple-element.40.refs_0_.load, f32[64,32,128]{2,1,0:T(8,128)S(1)} %get-tuple-element.70.iterate, f32[74,48,128]{2,1,0:T(8,128)S(1)} %get-tuple-element.58.refs_7_.rest_0_.to_long, ...), custom_call_target="tpu_custom_call" | custom-call | flops 1000000000 | tf_op jit(solution)/shard_map/pallas_call | solution.py:1047
  53.8 0.3 collective-permute-done.14.low
  54.1 0.9 %shard_map.162 = f32[64,32,128]{2,1,0:T(8,128)} custom-call(f32[64,32,128]{2,1,0:T(8,128)S(1)} %get-tuple-element.70.iterate, f32[32,128]{1,0:T(8,128)S(1)} %collective-permute-done.14.low, f32[32,128]{1,0:T(8,128)S(1)} %collective-permute-done.15.high, f32[64,128]{1,0:T(8,128)S(1)} %collective-permute-done.16.left, ...), custom_call_target="tpu_custom_call", output_to_operand_aliasing={{}: (9, {})} | custom-call | tf_op jit(solution)/shard_map/pallas_call | solution.py:1059
  (40 shorter events, 0.2 us)
Async XLA Ops:
  2.8 12.7 %copy-start = (f32[3,3]{1,0:T(4,128)S(1)}, f32[3,3]{1,0:T(4,128)}, u32[]{:S(2)}) copy-start(f32[3,3]{1,0:T(4,128)} %diffusivity.9) | copy-start | bytes 112
  2.8 12.7 %copy-start.1 = (f32[3]{0:T(128)S(1)}, f32[3]{0:T(128)}, u32[]{:S(2)}) copy-start(f32[3]{0:T(128)} %decay.5) | copy-start | bytes 40
  2.8 6.2 %collective-permute-start = (f32[4,32,128]{2,1,0:T(8,128)S(1)}, f32[4,32,128]{2,1,0:T(8,128)S(1)}, u32[]{:S(2)}, u32[]{:S(2)}) collective-permute-start(f32[4,32,128]{2,1,0:T(8,128)S(1)} %get-tuple-element.41), channel_id=1, source_target_pairs={{0,4},{1,5},{2,6},{3,7},{4,0},{5,1},{6,2},{7,3},{8,12},{9,13},{10,... | collective-permute-start | bytes 196616 | tf_op jit(solution)/shard_map/ppermute | solution.py:928
  5.9 3.2 %collective-permute-start.1 = (f32[4,32,128]{2,1,0:T(8,128)S(1)}, f32[4,32,128]{2,1,0:T(8,128)S(1)}, u32[]{:S(2)}, u32[]{:S(2)}) collective-permute-start(f32[4,32,128]{2,1,0:T(8,128)S(1)} %get-tuple-element.42), channel_id=1, source_target_pairs={{0,1},{1,0},{2,3},{3,2},{4,8},{5,9},{6,10},{7,11},{8,4},{9,5},{10,... | collective-permute-start | bytes 196616 | tf_op jit(solution)/shard_map/ppermute | solution.py:928
  5.9 6.8 %collective-permute-start.4 = (f32[10,32,128]{2,1,0:T(8,128)S(1)}, f32[10,32,128]{2,1,0:T(8,128)S(1)}, u32[]{:S(2)}, u32[]{:S(2)}) collective-permute-start(f32[10,32,128]{2,1,0:T(8,128)S(1)} %get-tuple-element.50), channel_id=1, source_target_pairs={{0,4},{1,5},{2,6},{3,7},{4,0},{5,1},{6,2},{7,3},{8,12},{9,13},{10,... | collective-permute-start | bytes 491528 | tf_op jit(solution)/shard_map/ppermute | solution.py:928
  9.1 3.6 %collective-permute-start.5 = (f32[10,32,128]{2,1,0:T(8,128)S(1)}, f32[10,32,128]{2,1,0:T(8,128)S(1)}, u32[]{:S(2)}, u32[]{:S(2)}) collective-permute-start(f32[10,32,128]{2,1,0:T(8,128)S(1)} %get-tuple-element.51), channel_id=1, source_target_pairs={{0,1},{1,0},{2,3},{3,2},{4,8},{5,9},{6,10},{7,11},{8,4},{9,5},{10,... | collective-permute-start | bytes 491528 | tf_op jit(solution)/shard_map/ppermute | solution.py:928
  9.3 7.9 %collective-permute-start.2 = (f32[296,128]{1,0:T(8,128)S(1)}, f32[296,128]{1,0:T(8,128)S(1)}, u32[]{:S(2)}, u32[]{:S(2)}) collective-permute-start(f32[296,128]{1,0:T(8,128)S(1)} %get-tuple-element.43.after), channel_id=1, source_target_pairs={{0,1},{4,5},{8,9},{12,13},{1,0},{5,4},{9,8},{13,12},{2,3},{6,7},{1... | collective-permute-start | bytes 454664 | tf_op jit(solution)/shard_map/ppermute | solution.py:928
  9.8 7.3 %collective-permute-start.3 = (f32[296,128]{1,0:T(8,128)S(1)}, f32[296,128]{1,0:T(8,128)S(1)}, u32[]{:S(2)}, u32[]{:S(2)}) collective-permute-start(f32[296,128]{1,0:T(8,128)S(1)} %get-tuple-element.44), channel_id=1, source_target_pairs={{0,4},{4,0},{8,12},{12,8},{1,2},{5,6},{9,10},{13,14},{2,1},{6,5},{... | collective-permute-start | bytes 454664 | tf_op jit(solution)/shard_map/ppermute | solution.py:928
  13.2 4.0 %copy-start.2 = (f32[256,256]{1,0:T(8,128)S(1)}, f32[256,256]{1,0:T(8,128)}, u32[]{:S(2)}) copy-start(f32[256,256]{1,0:T(8,128)} %constant.22.clone.rest_4_.rest_9_) | copy-start | bytes 786436
  13.2 4.0 %copy-start.3 = (f32[192,216]{1,0:T(8,128)S(1)}, f32[192,216]{1,0:T(8,128)}, u32[]{:S(2)}) copy-start(f32[192,216]{1,0:T(8,128)} %constant.20.clone.rest_2_.rest_7_) | copy-start | bytes 497668
  13.2 4.0 %copy-start.4 = (f32[144,144]{1,0:T(8,128)S(1)}, f32[144,144]{1,0:T(8,128)}, u32[]{:S(2)}) copy-start(f32[144,144]{1,0:T(8,128)} %constant.19.clone.rest_1_.rest_6_) | copy-start | bytes 248836
  13.2 4.0 %copy-start.5 = (f32[256,128]{1,0:T(8,128)S(1)}, f32[256,128]{1,0:T(8,128)}, u32[]{:S(2)}) copy-start(f32[256,128]{1,0:T(8,128)} %constant.23.clone.rest_5_.rest_10_) | copy-start | bytes 393220
  13.2 4.0 %copy-start.6 = (f32[96,120]{1,0:T(8,128)S(1)}, f32[96,120]{1,0:T(8,128)}, u32[]{:S(2)}) copy-start(f32[96,120]{1,0:T(8,128)} %constant.21.clone.rest_3_.rest_8_) | copy-start | bytes 138244
  13.2 4.0 %copy-start.7 = (f32[80,80]{1,0:T(8,128)S(1)}, f32[80,80]{1,0:T(8,128)}, u32[]{:S(2)}) copy-start(f32[80,80]{1,0:T(8,128)} %constant.18.clone.rest_0_.rest_5_) | copy-start | bytes 76804
  13.2 4.0 %copy-start.8 = (f32[72,128]{1,0:T(8,128)S(1)}, f32[72,128]{1,0:T(8,128)}, u32[]{:S(2)}) copy-start(f32[72,128]{1,0:T(8,128)} %constant.24.clone.rest_6_.rest_11_) | copy-start | bytes 110596
  13.3 4.0 %copy-start.9 = (f32[1,128]{1,0:T(1,128)S(1)}, f32[1,128]{1,0:T(1,128)}, u32[]{:S(2)}) copy-start(f32[1,128]{1,0:T(1,128)} %constant.25.clone.rest_7_.rest_12_) | copy-start | bytes 1540
  13.3 4.0 %copy-start.10 = (f32[1,40]{1,0:T(1,128)S(1)}, f32[1,40]{1,0:T(1,128)}, u32[]{:S(2)}) copy-start(f32[1,40]{1,0:T(1,128)} %constant.26.clone.rest_8_.rest_13_) | copy-start | bytes 484
  13.3 11.2 %collective-permute-start.6 = (f32[744,128]{1,0:T(8,128)S(1)}, f32[744,128]{1,0:T(8,128)S(1)}, u32[]{:S(2)}, u32[]{:S(2)}) collective-permute-start(f32[744,128]{1,0:T(8,128)S(1)} %get-tuple-element.52), channel_id=1, source_target_pairs={{0,1},{4,5},{8,9},{12,13},{1,0},{5,4},{9,8},{13,12},{2,3},{6,7},{1... | collective-permute-start | bytes 1142792 | tf_op jit(solution)/shard_map/ppermute | solution.py:928
  13.4 11.1 %collective-permute-start.7 = (f32[744,128]{1,0:T(8,128)S(1)}, f32[744,128]{1,0:T(8,128)S(1)}, u32[]{:S(2)}, u32[]{:S(2)}) collective-permute-start(f32[744,128]{1,0:T(8,128)S(1)} %get-tuple-element.53), channel_id=1, source_target_pairs={{0,4},{4,0},{8,12},{12,8},{1,2},{5,6},{9,10},{13,14},{2,1},{6,5},{... | collective-permute-start | bytes 1142792 | tf_op jit(solution)/shard_map/ppermute | solution.py:928
  25.4 9.1 %collective-permute-start.8 = (f32[176,128]{1,0:T(8,128)S(1)}, f32[176,128]{1,0:T(8,128)S(1)}, u32[]{:S(2)}, u32[]{:S(2)}) collective-permute-start(f32[176,128]{1,0:T(8,128)S(1)} %get-tuple-element.55), channel_id=1, source_target_pairs={{0,4},{1,5},{2,6},{3,7},{4,0},{5,1},{6,2},{7,3},{8,12},{9,13},{10,... | collective-permute-start | bytes 270344 | tf_op jit(solution)/shard_map/ppermute | solution.py:928
  25.5 9.0 %collective-permute-start.9 = (f32[176,128]{1,0:T(8,128)S(1)}, f32[176,128]{1,0:T(8,128)S(1)}, u32[]{:S(2)}, u32[]{:S(2)}) collective-permute-start(f32[176,128]{1,0:T(8,128)S(1)} %get-tuple-element.56), channel_id=1, source_target_pairs={{0,12},{1,13},{2,14},{3,15},{4,8},{5,9},{6,10},{7,11},{8,4},{9,5},... | collective-permute-start | bytes 270344 | tf_op jit(solution)/shard_map/ppermute | solution.py:928
  28.8 5.7 %collective-permute-start.10 = (f32[16,128]{1,0:T(8,128)S(1)}, f32[16,128]{1,0:T(8,128)S(1)}, u32[]{:S(2)}, u32[]{:S(2)}) collective-permute-start(f32[16,128]{1,0:T(8,128)S(1)} %get-tuple-element.57.refs_3_), channel_id=1, source_target_pairs={{0,8},{4,12},{8,0},{12,4},{1,9},{5,13},{9,1},{13,5},{2,10},{6,14},... | collective-permute-start | bytes 24584 | tf_op jit(solution)/shard_map/ppermute | solution.py:933
  34.8 1.5 %collective-permute-start.11 = (f32[392,128]{1,0:T(8,128)S(1)}, f32[392,128]{1,0:T(8,128)S(1)}, u32[]{:S(2)}, u32[]{:S(2)}) collective-permute-start(f32[392,128]{1,0:T(8,128)S(1)} %get-tuple-element.59), channel_id=1, source_target_pairs={{0,1},{4,5},{8,9},{12,13},{1,0},{5,4},{9,8},{13,12},{2,3},{6,7},{1... | collective-permute-start | bytes 602120 | tf_op jit(solution)/shard_map/ppermute | solution.py:928
  34.9 7.4 %collective-permute-start.12 = (f32[392,128]{1,0:T(8,128)S(1)}, f32[392,128]{1,0:T(8,128)S(1)}, u32[]{:S(2)}, u32[]{:S(2)}) collective-permute-start(f32[392,128]{1,0:T(8,128)S(1)} %get-tuple-element.60), channel_id=1, source_target_pairs={{0,4},{4,0},{8,12},{12,8},{1,2},{5,6},{9,10},{13,14},{2,1},{6,5},{... | collective-permute-start | bytes 602120 | tf_op jit(solution)/shard_map/ppermute | solution.py:928
  36.3 4.6 %collective-permute-start.13 = (f32[16,128]{1,0:T(8,128)S(1)}, f32[16,128]{1,0:T(8,128)S(1)}, u32[]{:S(2)}, u32[]{:S(2)}) collective-permute-start(f32[16,128]{1,0:T(8,128)S(1)} %shard_map.157.refs_0_), channel_id=1, source_target_pairs={{0,2},{1,3},{2,0},{3,1},{4,6},{5,7},{6,4},{7,5},{8,10},{9,11},{10,... | collective-permute-start | bytes 24584 | tf_op jit(solution)/shard_map/ppermute | solution.py:933
  49.7 4.4 %collective-permute-start.16 = (f32[64,128]{1,0:T(8,128)S(1)}, f32[64,128]{1,0:T(8,128)S(1)}, u32[]{:S(2)}, u32[]{:S(2)}) collective-permute-start(f32[64,128]{1,0:T(8,128)S(1)} %get-tuple-element.73), channel_id=1, source_target_pairs={{0,1},{4,5},{8,9},{12,13},{1,0},{5,4},{9,8},{13,12},{2,3},{6,7},{1... | collective-permute-start | bytes 98312 | tf_op jit(solution)/shard_map/ppermute | solution.py:928
  49.8 4.3 %collective-permute-start.17 = (f32[64,128]{1,0:T(8,128)S(1)}, f32[64,128]{1,0:T(8,128)S(1)}, u32[]{:S(2)}, u32[]{:S(2)}) collective-permute-start(f32[64,128]{1,0:T(8,128)S(1)} %get-tuple-element.74), channel_id=1, source_target_pairs={{0,4},{4,0},{8,12},{12,8},{1,2},{5,6},{9,10},{13,14},{2,1},{6,5},{... | collective-permute-start | bytes 98312 | tf_op jit(solution)/shard_map/ppermute | solution.py:928
  50.4 3.7 %collective-permute-start.14 = (f32[32,128]{1,0:T(8,128)S(1)}, f32[32,128]{1,0:T(8,128)S(1)}, u32[]{:S(2)}, u32[]{:S(2)}) collective-permute-start(f32[32,128]{1,0:T(8,128)S(1)} %get-tuple-element.71), channel_id=1, source_target_pairs={{0,4},{1,5},{2,6},{3,7},{4,0},{5,1},{6,2},{7,3},{8,12},{9,13},{10,... | collective-permute-start | bytes 49160 | tf_op jit(solution)/shard_map/ppermute | solution.py:928
  51.9 2.2 %collective-permute-start.15 = (f32[32,128]{1,0:T(8,128)S(1)}, f32[32,128]{1,0:T(8,128)S(1)}, u32[]{:S(2)}, u32[]{:S(2)}) collective-permute-start(f32[32,128]{1,0:T(8,128)S(1)} %get-tuple-element.72), channel_id=1, source_target_pairs={{0,1},{1,0},{2,3},{3,2},{4,8},{5,9},{6,10},{7,11},{8,4},{9,5},{10,... | collective-permute-start | bytes 49160 | tf_op jit(solution)/shard_map/ppermute | solution.py:928

commit v14 on v13

--- a/solution.py
+++ b/solution.py
@@ -73,22 +73,20 @@
     return parts + [values]
 
 
+def products(count):
+    return [(a, b) for a in range(count) for b in range(count - a)]
+
+
 def left_table(table, depth, count):
     rows, cols = table.shape
-    wide = np.zeros((rows, depth), np.float32)
-    wide[:, :cols] = table
+    rest = np.zeros((rows, depth), np.float32)
+    rest[:, :cols] = table
     parts = []
-    rest = wide
     for _ in range(count):
         part = rest.astype(ml_dtypes.bfloat16).astype(np.float32)
         parts.append(part)
         rest = rest - part
-    blank = np.zeros_like(parts[0])
-    lines = []
-    for index in range(count):
-        used = count - index if count > 2 else count
-        lines.append(np.concatenate([parts[index]] * used + [blank] * (count - used), axis=1))
-    return np.concatenate(lines, axis=0)
+    return np.concatenate([parts[a] for a, _ in products(count)], axis=1)
 
 
 def right_tables(table):
@@ -146,9 +144,9 @@
     )
 
 
-def dot_left(table, values, count, rows):
-    total = one_pass(table, jnp.concatenate(pieces(values, count), axis=0))
-    return sum(total[index * rows : (index + 1) * rows] for index in range(1, count)) + total[:rows]
+def dot_left(table, values, count):
+    parts = pieces(values, count)
+    return one_pass(table, jnp.concatenate([parts[b] for _, b in products(count)], axis=0))
 
 
 def dot_right(values, main, rest, count):
@@ -174,9 +172,9 @@
     deep_x, deep_y = padded(box.ex), padded(box.ey)
     into_y, into_x = into_y[...], into_x[...]
     if col_mask is not None:
-        mask = jnp.concatenate([col_mask] * FORWARD, axis=1)
+        mask = jnp.concatenate([col_mask] * len(products(FORWARD)), axis=1)
         into_y = into_y * mask
-        mask = jnp.concatenate([row_mask] * FORWARD, axis=1)
+        mask = jnp.concatenate([row_mask] * len(products(FORWARD)), axis=1)
         into_x = into_x * mask
     from_x, from_y, main_z, rest_z = from_x[...], from_y[...], main_z[...], rest_z[...]
     spectral_flat = spectral.reshape(box.ey * deep_x, deep)
@@ -190,14 +188,14 @@
         block = dot_right(block, main_z, rest_z, FORWARD).reshape(8, box.ey, deep)
         for row in range(0, 8, 2):
             pair = jnp.concatenate([block[row], block[row + 1]], axis=1)
-            pair = dot_left(into_y, with_rows(pair, deep_y), FORWARD, box.ey)
+            pair = dot_left(into_y, with_rows(pair, deep_y), FORWARD)
             for part in range(2):
                 spectral_flat[pl.ds(start + row + part, box.ey, stride=deep_x), :] = pair[
                     :, part * deep : (part + 1) * deep
                 ]
     for col in range(0, box.ey, 2):
         pair = jnp.concatenate([spectral[col], spectral[col + 1]], axis=1)
-        pair = dot_left(into_x, pair, FORWARD, box.ex)
+        pair = dot_left(into_x, pair, FORWARD)
         pair = jnp.concatenate(
             [
                 divided(pair[:, part * deep : (part + 1) * deep], col + part)
@@ -205,7 +203,7 @@
             ],
             axis=1,
         )
-        pair = dot_left(from_x, with_rows(pair, deep_x), BACKWARD, box.long)
+        pair = dot_left(from_x, with_rows(pair, deep_x), BACKWARD)
         for part in range(2):
             middle_flat[pl.ds(col + part, box.long, stride=deep_y), :] = pair[
                 :, part * deep : (part + 1) * deep
@@ -214,7 +212,7 @@
         parts = []
         for row in range(start, start + 8, 2):
             pair = jnp.concatenate([middle[row], middle[row + 1]], axis=1)
-            pair = dot_left(from_y, pair, BACKWARD, box.across)
+            pair = dot_left(from_y, pair, BACKWARD)
             parts += [pair[:, :deep], pair[:, deep:]]
         emit(start, dot_right(jnp.concatenate(parts, axis=0), main_z, rest_z, BACKWARD))
 

time: 55.4 us -> 55.5 us (level)
  no operation moved by 1% of the time
where the time goes in v14:
time: 55.5 us; the launch traced here: 55.4 us
  Pallas kernels  28.8 us (52%)
  starting transfers between devices  18.3 us (33%)
  waiting for transfers between devices  7.08 us (13%)
  between operations  1.09 us (2%)
    ppermute x8, starting transfers between devices, exchange(): lax.ppermute(first, axes, ways[0])  8.71 us
    ppermute x8, starting transfers between devices, exchange(): lax.ppermute(second, axes, ways[1])  8.65 us
    pallas_call x1, Pallas kernels, on_device(): call(functools.partial(second_solve, box), (cells, row, row, col, col, ce...  7.6 us
    pallas_call x1, Pallas kernels, on_device(): call(functools.partial(first_solve, box), (window, cells, f32(across, dee...  7.14 us
    ppermute x2, waiting for transfers between devices, two_away(): return lax.ppermute(table, axis, [(i, (i + 2) % size) for i in range(size)])  5.31 us
    pallas_call x1, Pallas kernels, on_device(): call(functools.partial(side_weights, box), (window,) * 4, [VMEM] * 6 + [S...  2.23 us
    pallas_call x1, Pallas kernels, on_device(): call(functools.partial(bring_edges, box), (whole_zone, cells, cells) + (f...  2.19 us
    pallas_call x1, Pallas kernels, on_device(): call(functools.partial(inner_residual, box), (f32(2, across, deep), f32(2...  2.05 us
  transfers between devices with their start and end apart: 18, of which 5 were waited for; matrix products, arithmetic and copies ran while one was open for 0% of the time, Pallas kernels for 31%

profile of v14, /device:TPU:0, one launch (start us, length us, event | category | flops | bytes accessed | tf_op | source)
XLA Modules:
  0.0 55.4 jit_solution(9208517294008033342)
XLA Ops:
  0.6 2.2 %shard_map.149 = (s32[64,32,128]{2,1,0:T(8,128)S(1)}, f32[64,32,128]{2,1,0:T(8,128)S(1)}, f32[64,32,128]{2,1,0:T(8,128)S(1)}, f32[4,32,128]{2,1,0:T(8,128)S(1)},...) custom-call(s32[64,32,128]{2,1,0:T(8,128)} %zone.1, f32[64,32,128]{2,1,0:T(8,128)} %scale.1, ...), custom_call_target="tpu_custom_call" | custom-call | tf_op jit(solution)/shard_map/pallas_call | solution.py:976
  2.8 3.1 %collective-permute-start = (f32[4,32,128]{2,1,0:T(8,128)S(1)}, f32[4,32,128]{2,1,0:T(8,128)S(1)}, u32[]{:S(2)}, u32[]{:S(2)}) collective-permute-start(f32[4,32,128]{2,1,0:T(8,128)S(1)} %get-tuple-element.41), channel_id=1, source_target_pairs={{0,4},{1,5},{2,6},{3,7},{4,0},{5,1},{6,2},{7,3},{8,12},{9,13},{10,... | collective-permute-start | bytes 196616 | tf_op jit(solution)/shard_map/ppermute | solution.py:926
  5.9 3.1 %collective-permute-start.4 = (f32[10,32,128]{2,1,0:T(8,128)S(1)}, f32[10,32,128]{2,1,0:T(8,128)S(1)}, u32[]{:S(2)}, u32[]{:S(2)}) collective-permute-start(f32[10,32,128]{2,1,0:T(8,128)S(1)} %get-tuple-element.50), channel_id=1, source_target_pairs={{0,4},{1,5},{2,6},{3,7},{4,0},{5,1},{6,2},{7,3},{8,12},{9,13},{10,... | collective-permute-start | bytes 491528 | tf_op jit(solution)/shard_map/ppermute | solution.py:926
  9.1 0.2 shard_map.150
  9.3 0.6 %collective-permute-start.2 = (f32[296,128]{1,0:T(8,128)S(1)}, f32[296,128]{1,0:T(8,128)S(1)}, u32[]{:S(2)}, u32[]{:S(2)}) collective-permute-start(f32[296,128]{1,0:T(8,128)S(1)} %get-tuple-element.43.after), channel_id=1, source_target_pairs={{0,1},{4,5},{8,9},{12,13},{1,0},{5,4},{9,8},{13,12},{2,3},{6,7},{1... | collective-permute-start | bytes 454664 | tf_op jit(solution)/shard_map/ppermute | solution.py:926
  9.8 2.2 %collective-permute-start.3 = (f32[296,128]{1,0:T(8,128)S(1)}, f32[296,128]{1,0:T(8,128)S(1)}, u32[]{:S(2)}, u32[]{:S(2)}) collective-permute-start(f32[296,128]{1,0:T(8,128)S(1)} %get-tuple-element.44), channel_id=1, source_target_pairs={{0,4},{4,0},{8,12},{12,8},{1,2},{5,6},{9,10},{13,14},{2,1},{6,5},{... | collective-permute-start | bytes 454664 | tf_op jit(solution)/shard_map/ppermute | solution.py:926
  12.0 0.7 %collective-permute-done.4.refs_2_.low = f32[10,32,128]{2,1,0:T(8,128)S(1)} collective-permute-done((f32[10,32,128]{2,1,0:T(8,128)S(1)}, f32[10,32,128]{2,1,0:T(8,128)S(1)}, u32[]{:S(2)}, u32[]{:S(2)}) %collective-permute-start.4) | collective-permute-done | bytes 163872 | tf_op jit(solution)/shard_map/ppermute | solution.py:926
  12.7 0.4 shard_map.153
  13.3 0.1 collective-permute-start.6
  13.4 2.2 %collective-permute-start.7 = (f32[744,128]{1,0:T(8,128)S(1)}, f32[744,128]{1,0:T(8,128)S(1)}, u32[]{:S(2)}, u32[]{:S(2)}) collective-permute-start(f32[744,128]{1,0:T(8,128)S(1)} %get-tuple-element.53), channel_id=1, source_target_pairs={{0,4},{4,0},{8,12},{12,8},{1,2},{5,6},{9,10},{13,14},{2,1},{6,5},{... | collective-permute-start | bytes 1142792 | tf_op jit(solution)/shard_map/ppermute | solution.py:926
  15.5 1.6 %shard_map.151 = (f32[8,128]{1,0:T(8,128)S(1)}, f32[16,128]{1,0:T(8,128)S(1)}) custom-call(s32[64,32,128]{2,1,0:T(8,128)S(1)} %get-tuple-element.45.zone.refs_1_, f32[64,32,128]{2,1,0:T(8,128)S(1)} %get-tuple-element.46.scale.refs_0_, f32[64,32,128]{2,1,0:T(8,128)S(1)} %get-tuple-element.40.refs_0_.load, f32[296,128]{1,0:T(8,128)S(1)} %get-tuple-element.43.after, ...), custom_call_target="tpu_custom_call" | custom-call | tf_op jit(solution)/shard_map/pallas_call | solution.py:986
  17.3 7.1 %shard_map.152 = (f32[74,48,128]{2,1,0:T(8,128)S(1)}, f32[64,32,128]{2,1,0:T(8,128)S(1)}, f32[32,128]{1,0:T(8,128)S(1)}, f32[40,72,128]{2,1,0:T(8,128)S(1)}) custom-call(f32[64,32,128]{2,1,0:T(8,128)S(1)} %get-tuple-element.40.refs_0_.load, f32[4,32,128]{2,1,0:T(8,128)S(1)} %collective-permute-done.refs_1_.low, ...), custom_call_target="tpu_custom_call" | custom-call | flops 4000000000 | tf_op jit(solution)/shard_map/pallas_call | solution.py:992
  24.4 1.0 %shard_map.154 = (f32[16,128]{1,0:T(8,128)S(1)}, f32[176,128]{1,0:T(8,128)S(1)}, f32[176,128]{1,0:T(8,128)S(1)}) custom-call(s32[64,32,128]{2,1,0:T(8,128)S(1)} %get-tuple-element.45.zone.refs_1_, f32[64,32,128]{2,1,0:T(8,128)S(1)} %get-tuple-element.46.scale.refs_0_, f32[64,32,128]{2,1,0:T(8,128)S(1)} %get-tuple-element.48.local.refs_0_, ...), custom_call_target="tpu_custom_call" | custom-call | tf_op jit(solution)/shard_map/pallas_call | solution.py:1000
  25.4 0.1 collective-permute-start.8
  25.5 3.3 %collective-permute-start.9 = (f32[176,128]{1,0:T(8,128)S(1)}, f32[176,128]{1,0:T(8,128)S(1)}, u32[]{:S(2)}, u32[]{:S(2)}) collective-permute-start(f32[176,128]{1,0:T(8,128)S(1)} %get-tuple-element.56), channel_id=1, source_target_pairs={{0,12},{1,13},{2,14},{3,15},{4,8},{5,9},{6,10},{7,11},{8,4},{9,5},... | collective-permute-start | bytes 270344 | tf_op jit(solution)/shard_map/ppermute | solution.py:926
  28.7 0.2 collective-permute-start.10
  28.9 2.2 %shard_map.155 = (f32[74,48,128]{2,1,0:T(8,128)S(1)}, f32[74,48,128]{2,1,0:T(8,128)S(1)}, f32[74,48,128]{2,1,0:T(8,128)S(1)}, f32[74,48,128]{2,1,0:T(8,128)S(1)}) custom-call(s32[64,32,128]{2,1,0:T(8,128)S(1)} %get-tuple-element.45.zone.refs_1_, f32[64,32,128]{2,1,0:T(8,128)S(1)} %get-tuple-element.46.scale.refs_0_, ...), custom_call_target="tpu_custom_call" | custom-call | flops 1000000000 | tf_op jit(solution)/shard_map/pallas_call | solution.py:1008
  31.2 3.3 %collective-permute-done.10.refs_6_ = f32[16,128]{1,0:T(8,128)S(1)} collective-permute-done((f32[16,128]{1,0:T(8,128)S(1)}, f32[16,128]{1,0:T(8,128)S(1)}, u32[]{:S(2)}, u32[]{:S(2)}) %collective-permute-start.10) | collective-permute-done | bytes 8224 | tf_op jit(solution)/shard_map/ppermute | solution.py:931
  34.5 0.2 shard_map.156
  34.7 0.1 collective-permute-start.11
  34.8 0.5 collective-permute-start.12
  35.3 0.9 %collective-permute-done.11.message.left = f32[392,128]{1,0:T(8,128)S(1)} collective-permute-done((f32[392,128]{1,0:T(8,128)S(1)}, f32[392,128]{1,0:T(8,128)S(1)}, u32[]{:S(2)}, u32[]{:S(2)}) %collective-permute-start.11) | collective-permute-done | bytes 200736 | tf_op jit(solution)/shard_map/ppermute | solution.py:926
  36.2 0.7 %collective-permute-start.13 = (f32[16,128]{1,0:T(8,128)S(1)}, f32[16,128]{1,0:T(8,128)S(1)}, u32[]{:S(2)}, u32[]{:S(2)}) collective-permute-start(f32[16,128]{1,0:T(8,128)S(1)} %shard_map.157.refs_0_), channel_id=1, source_target_pairs={{0,2},{1,3},{2,0},{3,1},{4,6},{5,7},{6,4},{7,5},{8,10},{9,11},{10,... | collective-permute-start | bytes 24584 | tf_op jit(solution)/shard_map/ppermute | solution.py:931
  36.9 1.8 %shard_map.159 = (f32[74,48,128]{2,1,0:T(8,128)S(1)}, f32[74,48,128]{2,1,0:T(8,128)S(1)}) custom-call(f32[74,48,128]{2,1,0:T(8,128)S(1)} %get-tuple-element.64.zone_window, f32[74,48,128]{2,1,0:T(8,128)S(1)} %get-tuple-element.65.scale_window, f32[3,3]{1,0:T(4,128)S(1)} %copy-done, f32[3]{0:T(128)S(1)} %copy-done.1), custom_call_target="tpu_custom_call" | custom-call | flops 1000000000 | tf_op jit(solution)/shard_map/pallas_call | solution.py:1014
  38.8 2.0 %collective-permute-done.13.refs_1_ = f32[16,128]{1,0:T(8,128)S(1)} collective-permute-done((f32[16,128]{1,0:T(8,128)S(1)}, f32[16,128]{1,0:T(8,128)S(1)}, u32[]{:S(2)}, u32[]{:S(2)}) %collective-permute-start.13) | collective-permute-done | bytes 8224 | tf_op jit(solution)/shard_map/ppermute | solution.py:931
  40.8 1.5 %shard_map.158.answers = f32[8,128]{1,0:T(8,128)S(1)} custom-call(f32[16,128]{1,0:T(8,128)S(1)} %shard_map.157.refs_0_, f32[16,128]{1,0:T(8,128)S(1)} %collective-permute-done.13.refs_1_), custom_call_target="tpu_custom_call" | custom-call | tf_op jit(solution)/shard_map/pallas_call | solution.py:1029
  42.3 7.6 %shard_map.160 = (f32[64,32,128]{2,1,0:T(8,128)S(1)}, f32[32,128]{1,0:T(8,128)S(1)}, f32[32,128]{1,0:T(8,128)S(1)}, f32[64,128]{1,0:T(8,128)S(1)}, f32[64,128]{1,0:T(8,128)S(1)}, /*index=5*/f32[64,32,128]{2,1,0:T(8,128)}) custom-call(f32[64,32,128]{2,1,0:T(8,128)S(1)} %get-tuple-element.48.local.refs_0_, ...), custom_call_target="tpu_custom_call" | custom-call | flops 4000000000 | tf_op jit(solution)/shard_map/pallas_call | solution.py:1035
  50.0 0.5 collective-permute-start.17
  50.5 1.5 %collective-permute-start.14 = (f32[32,128]{1,0:T(8,128)S(1)}, f32[32,128]{1,0:T(8,128)S(1)}, u32[]{:S(2)}, u32[]{:S(2)}) collective-permute-start(f32[32,128]{1,0:T(8,128)S(1)} %get-tuple-element.71), channel_id=1, source_target_pairs={{0,4},{1,5},{2,6},{3,7},{4,0},{5,1},{6,2},{7,3},{8,12},{9,13},{10,... | collective-permute-start | bytes 49160 | tf_op jit(solution)/shard_map/ppermute | solution.py:926
  52.1 2.0 %shard_map.161 = (f32[2,32,128]{2,1,0:T(8,128)S(1)}, f32[2,64,8,128]{3,2,1,0:T(8,128)S(1)}, f32[64,32,128]{2,1,0:T(8,128)}) custom-call(f32[64,32,128]{2,1,0:T(8,128)S(1)} %get-tuple-element.40.refs_0_.load, f32[64,32,128]{2,1,0:T(8,128)S(1)} %get-tuple-element.70.iterate, f32[74,48,128]{2,1,0:T(8,128)S(1)} %get-tuple-element.58.refs_7_.rest_0_.to_long, ...), custom_call_target="tpu_custom_call" | custom-call | flops 1000000000 | tf_op jit(solution)/shard_map/pallas_call | solution.py:1045
  54.1 0.1 collective-permute-done.14.low
  54.3 0.9 %shard_map.162 = f32[64,32,128]{2,1,0:T(8,128)} custom-call(f32[64,32,128]{2,1,0:T(8,128)S(1)} %get-tuple-element.70.iterate, f32[32,128]{1,0:T(8,128)S(1)} %collective-permute-done.14.low, f32[32,128]{1,0:T(8,128)S(1)} %collective-permute-done.15.high, f32[64,128]{1,0:T(8,128)S(1)} %collective-permute-done.16.left, ...), custom_call_target="tpu_custom_call", output_to_operand_aliasing={{}: (9, {})} | custom-call | tf_op jit(solution)/shard_map/pallas_call | solution.py:1057
  (40 shorter events, 0.2 us)
Async XLA Ops:
  2.8 12.7 %copy-start = (f32[3,3]{1,0:T(4,128)S(1)}, f32[3,3]{1,0:T(4,128)}, u32[]{:S(2)}) copy-start(f32[3,3]{1,0:T(4,128)} %diffusivity.9) | copy-start | bytes 112
  2.8 12.7 %copy-start.1 = (f32[3]{0:T(128)S(1)}, f32[3]{0:T(128)}, u32[]{:S(2)}) copy-start(f32[3]{0:T(128)} %decay.5) | copy-start | bytes 40
  2.8 6.2 %collective-permute-start = (f32[4,32,128]{2,1,0:T(8,128)S(1)}, f32[4,32,128]{2,1,0:T(8,128)S(1)}, u32[]{:S(2)}, u32[]{:S(2)}) collective-permute-start(f32[4,32,128]{2,1,0:T(8,128)S(1)} %get-tuple-element.41), channel_id=1, source_target_pairs={{0,4},{1,5},{2,6},{3,7},{4,0},{5,1},{6,2},{7,3},{8,12},{9,13},{10,... | collective-permute-start | bytes 196616 | tf_op jit(solution)/shard_map/ppermute | solution.py:926
  5.9 3.2 %collective-permute-start.1 = (f32[4,32,128]{2,1,0:T(8,128)S(1)}, f32[4,32,128]{2,1,0:T(8,128)S(1)}, u32[]{:S(2)}, u32[]{:S(2)}) collective-permute-start(f32[4,32,128]{2,1,0:T(8,128)S(1)} %get-tuple-element.42), channel_id=1, source_target_pairs={{0,1},{1,0},{2,3},{3,2},{4,8},{5,9},{6,10},{7,11},{8,4},{9,5},{10,... | collective-permute-start | bytes 196616 | tf_op jit(solution)/shard_map/ppermute | solution.py:926
  5.9 6.8 %collective-permute-start.4 = (f32[10,32,128]{2,1,0:T(8,128)S(1)}, f32[10,32,128]{2,1,0:T(8,128)S(1)}, u32[]{:S(2)}, u32[]{:S(2)}) collective-permute-start(f32[10,32,128]{2,1,0:T(8,128)S(1)} %get-tuple-element.50), channel_id=1, source_target_pairs={{0,4},{1,5},{2,6},{3,7},{4,0},{5,1},{6,2},{7,3},{8,12},{9,13},{10,... | collective-permute-start | bytes 491528 | tf_op jit(solution)/shard_map/ppermute | solution.py:926
  9.1 3.6 %collective-permute-start.5 = (f32[10,32,128]{2,1,0:T(8,128)S(1)}, f32[10,32,128]{2,1,0:T(8,128)S(1)}, u32[]{:S(2)}, u32[]{:S(2)}) collective-permute-start(f32[10,32,128]{2,1,0:T(8,128)S(1)} %get-tuple-element.51), channel_id=1, source_target_pairs={{0,1},{1,0},{2,3},{3,2},{4,8},{5,9},{6,10},{7,11},{8,4},{9,5},{10,... | collective-permute-start | bytes 491528 | tf_op jit(solution)/shard_map/ppermute | solution.py:926
  9.3 7.9 %collective-permute-start.2 = (f32[296,128]{1,0:T(8,128)S(1)}, f32[296,128]{1,0:T(8,128)S(1)}, u32[]{:S(2)}, u32[]{:S(2)}) collective-permute-start(f32[296,128]{1,0:T(8,128)S(1)} %get-tuple-element.43.after), channel_id=1, source_target_pairs={{0,1},{4,5},{8,9},{12,13},{1,0},{5,4},{9,8},{13,12},{2,3},{6,7},{1... | collective-permute-start | bytes 454664 | tf_op jit(solution)/shard_map/ppermute | solution.py:926
  9.8 7.3 %collective-permute-start.3 = (f32[296,128]{1,0:T(8,128)S(1)}, f32[296,128]{1,0:T(8,128)S(1)}, u32[]{:S(2)}, u32[]{:S(2)}) collective-permute-start(f32[296,128]{1,0:T(8,128)S(1)} %get-tuple-element.44), channel_id=1, source_target_pairs={{0,4},{4,0},{8,12},{12,8},{1,2},{5,6},{9,10},{13,14},{2,1},{6,5},{... | collective-permute-start | bytes 454664 | tf_op jit(solution)/shard_map/ppermute | solution.py:926
  13.2 4.0 %copy-start.2 = (f32[256,256]{1,0:T(8,128)S(1)}, f32[256,256]{1,0:T(8,128)}, u32[]{:S(2)}) copy-start(f32[256,256]{1,0:T(8,128)} %constant.22.clone.rest_4_.rest_9_) | copy-start | bytes 786436
  13.2 4.0 %copy-start.3 = (f32[64,432]{1,0:T(8,128)S(1)}, f32[64,432]{1,0:T(8,128)}, u32[]{:S(2)}) copy-start(f32[64,432]{1,0:T(8,128)} %constant.20.clone.rest_2_.rest_7_) | copy-start | bytes 331780
  13.2 4.0 %copy-start.4 = (f32[256,128]{1,0:T(8,128)S(1)}, f32[256,128]{1,0:T(8,128)}, u32[]{:S(2)}) copy-start(f32[256,128]{1,0:T(8,128)} %constant.23.clone.rest_5_.rest_10_) | copy-start | bytes 393220
  13.2 4.0 %copy-start.5 = (f32[72,216]{1,0:T(8,128)S(1)}, f32[72,216]{1,0:T(8,128)}, u32[]{:S(2)}) copy-start(f32[72,216]{1,0:T(8,128)} %constant.19.clone.rest_1_.rest_6_) | copy-start | bytes 186628
  13.2 4.0 %copy-start.6 = (f32[72,128]{1,0:T(8,128)S(1)}, f32[72,128]{1,0:T(8,128)}, u32[]{:S(2)}) copy-start(f32[72,128]{1,0:T(8,128)} %constant.24.clone.rest_6_.rest_11_) | copy-start | bytes 110596
  13.2 4.0 %copy-start.7 = (f32[32,240]{1,0:T(8,128)S(1)}, f32[32,240]{1,0:T(8,128)}, u32[]{:S(2)}) copy-start(f32[32,240]{1,0:T(8,128)} %constant.21.clone.rest_3_.rest_8_) | copy-start | bytes 92164
  13.2 4.0 %copy-start.8 = (f32[40,120]{1,0:T(8,128)S(1)}, f32[40,120]{1,0:T(8,128)}, u32[]{:S(2)}) copy-start(f32[40,120]{1,0:T(8,128)} %constant.18.clone.rest_0_.rest_5_) | copy-start | bytes 57604
  13.3 4.0 %copy-start.9 = (f32[1,128]{1,0:T(1,128)S(1)}, f32[1,128]{1,0:T(1,128)}, u32[]{:S(2)}) copy-start(f32[1,128]{1,0:T(1,128)} %constant.25.clone.rest_7_.rest_12_) | copy-start | bytes 1540
  13.3 4.0 %copy-start.10 = (f32[1,40]{1,0:T(1,128)S(1)}, f32[1,40]{1,0:T(1,128)}, u32[]{:S(2)}) copy-start(f32[1,40]{1,0:T(1,128)} %constant.26.clone.rest_8_.rest_13_) | copy-start | bytes 484
  13.3 11.1 %collective-permute-start.6 = (f32[744,128]{1,0:T(8,128)S(1)}, f32[744,128]{1,0:T(8,128)S(1)}, u32[]{:S(2)}, u32[]{:S(2)}) collective-permute-start(f32[744,128]{1,0:T(8,128)S(1)} %get-tuple-element.52), channel_id=1, source_target_pairs={{0,1},{4,5},{8,9},{12,13},{1,0},{5,4},{9,8},{13,12},{2,3},{6,7},{1... | collective-permute-start | bytes 1142792 | tf_op jit(solution)/shard_map/ppermute | solution.py:926
  13.4 11.1 %collective-permute-start.7 = (f32[744,128]{1,0:T(8,128)S(1)}, f32[744,128]{1,0:T(8,128)S(1)}, u32[]{:S(2)}, u32[]{:S(2)}) collective-permute-start(f32[744,128]{1,0:T(8,128)S(1)} %get-tuple-element.53), channel_id=1, source_target_pairs={{0,4},{4,0},{8,12},{12,8},{1,2},{5,6},{9,10},{13,14},{2,1},{6,5},{... | collective-permute-start | bytes 1142792 | tf_op jit(solution)/shard_map/ppermute | solution.py:926
  25.4 9.1 %collective-permute-start.8 = (f32[176,128]{1,0:T(8,128)S(1)}, f32[176,128]{1,0:T(8,128)S(1)}, u32[]{:S(2)}, u32[]{:S(2)}) collective-permute-start(f32[176,128]{1,0:T(8,128)S(1)} %get-tuple-element.55), channel_id=1, source_target_pairs={{0,4},{1,5},{2,6},{3,7},{4,0},{5,1},{6,2},{7,3},{8,12},{9,13},{10,... | collective-permute-start | bytes 270344 | tf_op jit(solution)/shard_map/ppermute | solution.py:926
  25.5 9.0 %collective-permute-start.9 = (f32[176,128]{1,0:T(8,128)S(1)}, f32[176,128]{1,0:T(8,128)S(1)}, u32[]{:S(2)}, u32[]{:S(2)}) collective-permute-start(f32[176,128]{1,0:T(8,128)S(1)} %get-tuple-element.56), channel_id=1, source_target_pairs={{0,12},{1,13},{2,14},{3,15},{4,8},{5,9},{6,10},{7,11},{8,4},{9,5},... | collective-permute-start | bytes 270344 | tf_op jit(solution)/shard_map/ppermute | solution.py:926
  28.7 5.7 %collective-permute-start.10 = (f32[16,128]{1,0:T(8,128)S(1)}, f32[16,128]{1,0:T(8,128)S(1)}, u32[]{:S(2)}, u32[]{:S(2)}) collective-permute-start(f32[16,128]{1,0:T(8,128)S(1)} %get-tuple-element.57.refs_3_), channel_id=1, source_target_pairs={{0,8},{4,12},{8,0},{12,4},{1,9},{5,13},{9,1},{13,5},{2,10},{6,14},... | collective-permute-start | bytes 24584 | tf_op jit(solution)/shard_map/ppermute | solution.py:931
  34.7 1.5 %collective-permute-start.11 = (f32[392,128]{1,0:T(8,128)S(1)}, f32[392,128]{1,0:T(8,128)S(1)}, u32[]{:S(2)}, u32[]{:S(2)}) collective-permute-start(f32[392,128]{1,0:T(8,128)S(1)} %get-tuple-element.59), channel_id=1, source_target_pairs={{0,1},{4,5},{8,9},{12,13},{1,0},{5,4},{9,8},{13,12},{2,3},{6,7},{1... | collective-permute-start | bytes 602120 | tf_op jit(solution)/shard_map/ppermute | solution.py:926
  34.8 7.4 %collective-permute-start.12 = (f32[392,128]{1,0:T(8,128)S(1)}, f32[392,128]{1,0:T(8,128)S(1)}, u32[]{:S(2)}, u32[]{:S(2)}) collective-permute-start(f32[392,128]{1,0:T(8,128)S(1)} %get-tuple-element.60), channel_id=1, source_target_pairs={{0,4},{4,0},{8,12},{12,8},{1,2},{5,6},{9,10},{13,14},{2,1},{6,5},{... | collective-permute-start | bytes 602120 | tf_op jit(solution)/shard_map/ppermute | solution.py:926
  36.2 4.6 %collective-permute-start.13 = (f32[16,128]{1,0:T(8,128)S(1)}, f32[16,128]{1,0:T(8,128)S(1)}, u32[]{:S(2)}, u32[]{:S(2)}) collective-permute-start(f32[16,128]{1,0:T(8,128)S(1)} %shard_map.157.refs_0_), channel_id=1, source_target_pairs={{0,2},{1,3},{2,0},{3,1},{4,6},{5,7},{6,4},{7,5},{8,10},{9,11},{10,... | collective-permute-start | bytes 24584 | tf_op jit(solution)/shard_map/ppermute | solution.py:931
  49.9 4.4 %collective-permute-start.16 = (f32[64,128]{1,0:T(8,128)S(1)}, f32[64,128]{1,0:T(8,128)S(1)}, u32[]{:S(2)}, u32[]{:S(2)}) collective-permute-start(f32[64,128]{1,0:T(8,128)S(1)} %get-tuple-element.73), channel_id=1, source_target_pairs={{0,1},{4,5},{8,9},{12,13},{1,0},{5,4},{9,8},{13,12},{2,3},{6,7},{1... | collective-permute-start | bytes 98312 | tf_op jit(solution)/shard_map/ppermute | solution.py:926
  50.0 4.3 %collective-permute-start.17 = (f32[64,128]{1,0:T(8,128)S(1)}, f32[64,128]{1,0:T(8,128)S(1)}, u32[]{:S(2)}, u32[]{:S(2)}) collective-permute-start(f32[64,128]{1,0:T(8,128)S(1)} %get-tuple-element.74), channel_id=1, source_target_pairs={{0,4},{4,0},{8,12},{12,8},{1,2},{5,6},{9,10},{13,14},{2,1},{6,5},{... | collective-permute-start | bytes 98312 | tf_op jit(solution)/shard_map/ppermute | solution.py:926
  50.5 3.7 %collective-permute-start.14 = (f32[32,128]{1,0:T(8,128)S(1)}, f32[32,128]{1,0:T(8,128)S(1)}, u32[]{:S(2)}, u32[]{:S(2)}) collective-permute-start(f32[32,128]{1,0:T(8,128)S(1)} %get-tuple-element.71), channel_id=1, source_target_pairs={{0,4},{1,5},{2,6},{3,7},{4,0},{5,1},{6,2},{7,3},{8,12},{9,13},{10,... | collective-permute-start | bytes 49160 | tf_op jit(solution)/shard_map/ppermute | solution.py:926
  52.1 2.2 %collective-permute-start.15 = (f32[32,128]{1,0:T(8,128)S(1)}, f32[32,128]{1,0:T(8,128)S(1)}, u32[]{:S(2)}, u32[]{:S(2)}) collective-permute-start(f32[32,128]{1,0:T(8,128)S(1)} %get-tuple-element.72), channel_id=1, source_target_pairs={{0,1},{1,0},{2,3},{3,2},{4,8},{5,9},{6,10},{7,11},{8,4},{9,5},{10,... | collective-permute-start | bytes 49160 | tf_op jit(solution)/shard_map/ppermute | solution.py:926

commit v15 on v13

--- a/solution.py
+++ b/solution.py
@@ -168,6 +168,17 @@
     return jnp.concatenate([values, blank], axis=0)
 
 
+ABREAST = 8
+
+
+def beside(values):
+    return jnp.concatenate(values, axis=1)
+
+
+def apart(values, lanes):
+    return [values[:, start : start + lanes] for start in range(0, values.shape[1], lanes)]
+
+
 def box_solve(box, source, divided, tables, row_mask, col_mask, spectral, middle, emit):
     into_y, into_x, from_x, from_y, main_z, rest_z = tables[:6]
     deep = box.deep
@@ -188,34 +199,24 @@
     for start in range(0, box.ex, 8):
         block = source(start).reshape(8 * box.ey, deep)
         block = dot_right(block, main_z, rest_z, FORWARD).reshape(8, box.ey, deep)
-        for row in range(0, 8, 2):
-            pair = jnp.concatenate([block[row], block[row + 1]], axis=1)
-            pair = dot_left(into_y, with_rows(pair, deep_y), FORWARD, box.ey)
-            for part in range(2):
-                spectral_flat[pl.ds(start + row + part, box.ey, stride=deep_x), :] = pair[
-                    :, part * deep : (part + 1) * deep
-                ]
-    for col in range(0, box.ey, 2):
-        pair = jnp.concatenate([spectral[col], spectral[col + 1]], axis=1)
-        pair = dot_left(into_x, pair, FORWARD, box.ex)
-        pair = jnp.concatenate(
-            [
-                divided(pair[:, part * deep : (part + 1) * deep], col + part)
-                for part in range(2)
-            ],
-            axis=1,
-        )
-        pair = dot_left(from_x, with_rows(pair, deep_x), BACKWARD, box.long)
-        for part in range(2):
-            middle_flat[pl.ds(col + part, box.long, stride=deep_y), :] = pair[
-                :, part * deep : (part + 1) * deep
-            ]
+        for row in range(0, 8, ABREAST):
+            wide = beside([block[row + part] for part in range(ABREAST)])
+            wide = dot_left(into_y, with_rows(wide, deep_y), FORWARD, box.ey)
+            for part, values in enumerate(apart(wide, deep)):
+                place = pl.ds(start + row + part, box.ey, stride=deep_x)
+                spectral_flat[place, :] = values
+    for col in range(0, box.ey, ABREAST):
+        wide = beside([spectral[col + part] for part in range(ABREAST)])
+        wide = apart(dot_left(into_x, wide, FORWARD, box.ex), deep)
+        wide = beside([divided(values, col + part) for part, values in enumerate(wide)])
+        wide = dot_left(from_x, with_rows(wide, deep_x), BACKWARD, box.long)
+        for part, values in enumerate(apart(wide, deep)):
+            middle_flat[pl.ds(col + part, box.long, stride=deep_y), :] = values
     for start in range(0, box.long, 8):
         parts = []
-        for row in range(start, start + 8, 2):
-            pair = jnp.concatenate([middle[row], middle[row + 1]], axis=1)
-            pair = dot_left(from_y, pair, BACKWARD, box.across)
-            parts += [pair[:, :deep], pair[:, deep:]]
+        for row in range(start, start + 8, ABREAST):
+            wide = beside([middle[row + part] for part in range(ABREAST)])
+            parts += apart(dot_left(from_y, wide, BACKWARD, box.across), deep)
         emit(start, dot_right(jnp.concatenate(parts, axis=0), main_z, rest_z, BACKWARD))
 
 

time: 55.4 us -> 54.8 us (0.989)
    pallas_call x1, Pallas kernels: 7.4 us -> 6.7 us  [on_device(): call(functools.partial(second_solve, box), (cells, row, row, col, col, ce...]
where the time goes in v15:
time: 54.8 us; the launch traced here: 54.7 us
  Pallas kernels  28 us (51%)
  starting transfers between devices  18.3 us (33%)
  waiting for transfers between devices  7.23 us (13%)
  between operations  1.09 us (2%)
    ppermute x8, starting transfers between devices, exchange(): lax.ppermute(first, axes, ways[0])  8.7 us
    ppermute x8, starting transfers between devices, exchange(): lax.ppermute(second, axes, ways[1])  8.66 us
    pallas_call x1, Pallas kernels, on_device(): call(functools.partial(first_solve, box), (window, cells, f32(across, dee...  7.38 us
    pallas_call x1, Pallas kernels, on_device(): call(functools.partial(second_solve, box), (cells, row, row, col, col, ce...  6.7 us
    ppermute x2, waiting for transfers between devices, two_away(): return lax.ppermute(table, axis, [(i, (i + 2) % size) for i in range(size)])  5.25 us
    pallas_call x1, Pallas kernels, on_device(): call(functools.partial(side_weights, box), (window,) * 4, [VMEM] * 6 + [S...  2.25 us
    pallas_call x1, Pallas kernels, on_device(): call(functools.partial(bring_edges, box), (whole_zone, cells, cells) + (f...  2.19 us
    ppermute x8, waiting for transfers between devices, exchange(): lax.ppermute(first, axes, ways[0])  1.94 us
  transfers between devices with their start and end apart: 18, of which 5 were waited for; matrix products, arithmetic and copies ran while one was open for 0% of the time, Pallas kernels for 31%

profile of v15, /device:TPU:0, one launch (start us, length us, event | category | flops | bytes accessed | tf_op | source)
XLA Modules:
  0.0 54.7 jit_solution(3593615953625537339)
XLA Ops:
  0.6 2.2 %shard_map.149 = (s32[64,32,128]{2,1,0:T(8,128)S(1)}, f32[64,32,128]{2,1,0:T(8,128)S(1)}, f32[64,32,128]{2,1,0:T(8,128)S(1)}, f32[4,32,128]{2,1,0:T(8,128)S(1)},...) custom-call(s32[64,32,128]{2,1,0:T(8,128)} %zone.1, f32[64,32,128]{2,1,0:T(8,128)} %scale.1, ...), custom_call_target="tpu_custom_call" | custom-call | tf_op jit(solution)/shard_map/pallas_call | solution.py:979
  2.8 3.1 %collective-permute-start = (f32[4,32,128]{2,1,0:T(8,128)S(1)}, f32[4,32,128]{2,1,0:T(8,128)S(1)}, u32[]{:S(2)}, u32[]{:S(2)}) collective-permute-start(f32[4,32,128]{2,1,0:T(8,128)S(1)} %get-tuple-element.41), channel_id=1, source_target_pairs={{0,4},{1,5},{2,6},{3,7},{4,0},{5,1},{6,2},{7,3},{8,12},{9,13},{10,... | collective-permute-start | bytes 196616 | tf_op jit(solution)/shard_map/ppermute | solution.py:929
  5.9 3.1 %collective-permute-start.4 = (f32[10,32,128]{2,1,0:T(8,128)S(1)}, f32[10,32,128]{2,1,0:T(8,128)S(1)}, u32[]{:S(2)}, u32[]{:S(2)}) collective-permute-start(f32[10,32,128]{2,1,0:T(8,128)S(1)} %get-tuple-element.50), channel_id=1, source_target_pairs={{0,4},{1,5},{2,6},{3,7},{4,0},{5,1},{6,2},{7,3},{8,12},{9,13},{10,... | collective-permute-start | bytes 491528 | tf_op jit(solution)/shard_map/ppermute | solution.py:929
  9.1 0.2 shard_map.150
  9.3 0.6 %collective-permute-start.2 = (f32[296,128]{1,0:T(8,128)S(1)}, f32[296,128]{1,0:T(8,128)S(1)}, u32[]{:S(2)}, u32[]{:S(2)}) collective-permute-start(f32[296,128]{1,0:T(8,128)S(1)} %get-tuple-element.43.after), channel_id=1, source_target_pairs={{0,1},{4,5},{8,9},{12,13},{1,0},{5,4},{9,8},{13,12},{2,3},{6,7},{1... | collective-permute-start | bytes 454664 | tf_op jit(solution)/shard_map/ppermute | solution.py:929
  9.8 2.2 %collective-permute-start.3 = (f32[296,128]{1,0:T(8,128)S(1)}, f32[296,128]{1,0:T(8,128)S(1)}, u32[]{:S(2)}, u32[]{:S(2)}) collective-permute-start(f32[296,128]{1,0:T(8,128)S(1)} %get-tuple-element.44), channel_id=1, source_target_pairs={{0,4},{4,0},{8,12},{12,8},{1,2},{5,6},{9,10},{13,14},{2,1},{6,5},{... | collective-permute-start | bytes 454664 | tf_op jit(solution)/shard_map/ppermute | solution.py:929
  12.0 0.7 %collective-permute-done.4.refs_2_.low = f32[10,32,128]{2,1,0:T(8,128)S(1)} collective-permute-done((f32[10,32,128]{2,1,0:T(8,128)S(1)}, f32[10,32,128]{2,1,0:T(8,128)S(1)}, u32[]{:S(2)}, u32[]{:S(2)}) %collective-permute-start.4) | collective-permute-done | bytes 163872 | tf_op jit(solution)/shard_map/ppermute | solution.py:929
  12.7 0.4 shard_map.153
  13.3 0.1 collective-permute-start.6
  13.4 2.2 %collective-permute-start.7 = (f32[744,128]{1,0:T(8,128)S(1)}, f32[744,128]{1,0:T(8,128)S(1)}, u32[]{:S(2)}, u32[]{:S(2)}) collective-permute-start(f32[744,128]{1,0:T(8,128)S(1)} %get-tuple-element.53), channel_id=1, source_target_pairs={{0,4},{4,0},{8,12},{12,8},{1,2},{5,6},{9,10},{13,14},{2,1},{6,5},{... | collective-permute-start | bytes 1142792 | tf_op jit(solution)/shard_map/ppermute | solution.py:929
  15.5 1.6 %shard_map.151 = (f32[8,128]{1,0:T(8,128)S(1)}, f32[16,128]{1,0:T(8,128)S(1)}) custom-call(s32[64,32,128]{2,1,0:T(8,128)S(1)} %get-tuple-element.45.zone.refs_1_, f32[64,32,128]{2,1,0:T(8,128)S(1)} %get-tuple-element.46.scale.refs_0_, f32[64,32,128]{2,1,0:T(8,128)S(1)} %get-tuple-element.40.refs_0_.load, f32[296,128]{1,0:T(8,128)S(1)} %get-tuple-element.43.after, ...), custom_call_target="tpu_custom_call" | custom-call | tf_op jit(solution)/shard_map/pallas_call | solution.py:989
  17.2 7.4 %shard_map.152 = (f32[74,48,128]{2,1,0:T(8,128)S(1)}, f32[64,32,128]{2,1,0:T(8,128)S(1)}, f32[32,128]{1,0:T(8,128)S(1)}, f32[40,72,128]{2,1,0:T(8,128)S(1)}) custom-call(f32[64,32,128]{2,1,0:T(8,128)S(1)} %get-tuple-element.40.refs_0_.load, f32[4,32,128]{2,1,0:T(8,128)S(1)} %collective-permute-done.refs_1_.low, ...), custom_call_target="tpu_custom_call" | custom-call | flops 4000000000 | tf_op jit(solution)/shard_map/pallas_call | solution.py:995
  24.7 1.0 %shard_map.154 = (f32[16,128]{1,0:T(8,128)S(1)}, f32[176,128]{1,0:T(8,128)S(1)}, f32[176,128]{1,0:T(8,128)S(1)}) custom-call(s32[64,32,128]{2,1,0:T(8,128)S(1)} %get-tuple-element.45.zone.refs_1_, f32[64,32,128]{2,1,0:T(8,128)S(1)} %get-tuple-element.46.scale.refs_0_, f32[64,32,128]{2,1,0:T(8,128)S(1)} %get-tuple-element.48.local.refs_0_, ...), custom_call_target="tpu_custom_call" | custom-call | tf_op jit(solution)/shard_map/pallas_call | solution.py:1003
  25.6 0.1 collective-permute-start.8
  25.7 3.3 %collective-permute-start.9 = (f32[176,128]{1,0:T(8,128)S(1)}, f32[176,128]{1,0:T(8,128)S(1)}, u32[]{:S(2)}, u32[]{:S(2)}) collective-permute-start(f32[176,128]{1,0:T(8,128)S(1)} %get-tuple-element.56), channel_id=1, source_target_pairs={{0,12},{1,13},{2,14},{3,15},{4,8},{5,9},{6,10},{7,11},{8,4},{9,5},... | collective-permute-start | bytes 270344 | tf_op jit(solution)/shard_map/ppermute | solution.py:929
  28.9 0.2 collective-permute-start.10
  29.2 2.3 %shard_map.155 = (f32[74,48,128]{2,1,0:T(8,128)S(1)}, f32[74,48,128]{2,1,0:T(8,128)S(1)}, f32[74,48,128]{2,1,0:T(8,128)S(1)}, f32[74,48,128]{2,1,0:T(8,128)S(1)}) custom-call(s32[64,32,128]{2,1,0:T(8,128)S(1)} %get-tuple-element.45.zone.refs_1_, f32[64,32,128]{2,1,0:T(8,128)S(1)} %get-tuple-element.46.scale.refs_0_, ...), custom_call_target="tpu_custom_call" | custom-call | flops 1000000000 | tf_op jit(solution)/shard_map/pallas_call | solution.py:1011
  31.4 3.3 %collective-permute-done.10.refs_6_ = f32[16,128]{1,0:T(8,128)S(1)} collective-permute-done((f32[16,128]{1,0:T(8,128)S(1)}, f32[16,128]{1,0:T(8,128)S(1)}, u32[]{:S(2)}, u32[]{:S(2)}) %collective-permute-start.10) | collective-permute-done | bytes 8224 | tf_op jit(solution)/shard_map/ppermute | solution.py:934
  34.7 0.2 shard_map.156
  34.9 0.1 collective-permute-start.11
  35.1 0.5 collective-permute-start.12
  35.6 0.9 %collective-permute-done.11.message.left = f32[392,128]{1,0:T(8,128)S(1)} collective-permute-done((f32[392,128]{1,0:T(8,128)S(1)}, f32[392,128]{1,0:T(8,128)S(1)}, u32[]{:S(2)}, u32[]{:S(2)}) %collective-permute-start.11) | collective-permute-done | bytes 200736 | tf_op jit(solution)/shard_map/ppermute | solution.py:929
  36.4 0.7 %collective-permute-start.13 = (f32[16,128]{1,0:T(8,128)S(1)}, f32[16,128]{1,0:T(8,128)S(1)}, u32[]{:S(2)}, u32[]{:S(2)}) collective-permute-start(f32[16,128]{1,0:T(8,128)S(1)} %shard_map.157.refs_0_), channel_id=1, source_target_pairs={{0,2},{1,3},{2,0},{3,1},{4,6},{5,7},{6,4},{7,5},{8,10},{9,11},{10,... | collective-permute-start | bytes 24584 | tf_op jit(solution)/shard_map/ppermute | solution.py:934
  37.1 1.9 %shard_map.159 = (f32[74,48,128]{2,1,0:T(8,128)S(1)}, f32[74,48,128]{2,1,0:T(8,128)S(1)}) custom-call(f32[74,48,128]{2,1,0:T(8,128)S(1)} %get-tuple-element.64.zone_window, f32[74,48,128]{2,1,0:T(8,128)S(1)} %get-tuple-element.65.scale_window, f32[3,3]{1,0:T(4,128)S(1)} %copy-done, f32[3]{0:T(128)S(1)} %copy-done.1), custom_call_target="tpu_custom_call" | custom-call | flops 1000000000 | tf_op jit(solution)/shard_map/pallas_call | solution.py:1017
  39.0 2.0 %collective-permute-done.13.refs_1_ = f32[16,128]{1,0:T(8,128)S(1)} collective-permute-done((f32[16,128]{1,0:T(8,128)S(1)}, f32[16,128]{1,0:T(8,128)S(1)}, u32[]{:S(2)}, u32[]{:S(2)}) %collective-permute-start.13) | collective-permute-done | bytes 8224 | tf_op jit(solution)/shard_map/ppermute | solution.py:934
  41.0 1.5 %shard_map.158.answers = f32[8,128]{1,0:T(8,128)S(1)} custom-call(f32[16,128]{1,0:T(8,128)S(1)} %shard_map.157.refs_0_, f32[16,128]{1,0:T(8,128)S(1)} %collective-permute-done.13.refs_1_), custom_call_target="tpu_custom_call" | custom-call | tf_op jit(solution)/shard_map/pallas_call | solution.py:1032
  42.5 6.7 %shard_map.160 = (f32[64,32,128]{2,1,0:T(8,128)S(1)}, f32[32,128]{1,0:T(8,128)S(1)}, f32[32,128]{1,0:T(8,128)S(1)}, f32[64,128]{1,0:T(8,128)S(1)}, f32[64,128]{1,0:T(8,128)S(1)}, /*index=5*/f32[64,32,128]{2,1,0:T(8,128)}) custom-call(f32[64,32,128]{2,1,0:T(8,128)S(1)} %get-tuple-element.48.local.refs_0_, ...), custom_call_target="tpu_custom_call" | custom-call | flops 4000000000 | tf_op jit(solution)/shard_map/pallas_call | solution.py:1038
  49.3 0.6 %collective-permute-start.17 = (f32[64,128]{1,0:T(8,128)S(1)}, f32[64,128]{1,0:T(8,128)S(1)}, u32[]{:S(2)}, u32[]{:S(2)}) collective-permute-start(f32[64,128]{1,0:T(8,128)S(1)} %get-tuple-element.74), channel_id=1, source_target_pairs={{0,4},{4,0},{8,12},{12,8},{1,2},{5,6},{9,10},{13,14},{2,1},{6,5},{... | collective-permute-start | bytes 98312 | tf_op jit(solution)/shard_map/ppermute | solution.py:929
  49.8 1.5 %collective-permute-start.14 = (f32[32,128]{1,0:T(8,128)S(1)}, f32[32,128]{1,0:T(8,128)S(1)}, u32[]{:S(2)}, u32[]{:S(2)}) collective-permute-start(f32[32,128]{1,0:T(8,128)S(1)} %get-tuple-element.71), channel_id=1, source_target_pairs={{0,4},{1,5},{2,6},{3,7},{4,0},{5,1},{6,2},{7,3},{8,12},{9,13},{10,... | collective-permute-start | bytes 49160 | tf_op jit(solution)/shard_map/ppermute | solution.py:929
  51.4 1.9 %shard_map.161 = (f32[2,32,128]{2,1,0:T(8,128)S(1)}, f32[2,64,8,128]{3,2,1,0:T(8,128)S(1)}, f32[64,32,128]{2,1,0:T(8,128)}) custom-call(f32[64,32,128]{2,1,0:T(8,128)S(1)} %get-tuple-element.40.refs_0_.load, f32[64,32,128]{2,1,0:T(8,128)S(1)} %get-tuple-element.70.iterate, f32[74,48,128]{2,1,0:T(8,128)S(1)} %get-tuple-element.58.refs_7_.rest_0_.to_long, ...), custom_call_target="tpu_custom_call" | custom-call | flops 1000000000 | tf_op jit(solution)/shard_map/pallas_call | solution.py:1048
  53.2 0.3 collective-permute-done.14.low
  53.6 0.9 %shard_map.162 = f32[64,32,128]{2,1,0:T(8,128)} custom-call(f32[64,32,128]{2,1,0:T(8,128)S(1)} %get-tuple-element.70.iterate, f32[32,128]{1,0:T(8,128)S(1)} %collective-permute-done.14.low, f32[32,128]{1,0:T(8,128)S(1)} %collective-permute-done.15.high, f32[64,128]{1,0:T(8,128)S(1)} %collective-permute-done.16.left, ...), custom_call_target="tpu_custom_call", output_to_operand_aliasing={{}: (9, {})} | custom-call | tf_op jit(solution)/shard_map/pallas_call | solution.py:1060
  (40 shorter events, 0.2 us)
Async XLA Ops:
  2.8 12.7 %copy-start = (f32[3,3]{1,0:T(4,128)S(1)}, f32[3,3]{1,0:T(4,128)}, u32[]{:S(2)}) copy-start(f32[3,3]{1,0:T(4,128)} %diffusivity.9) | copy-start | bytes 112
  2.8 12.7 %copy-start.1 = (f32[3]{0:T(128)S(1)}, f32[3]{0:T(128)}, u32[]{:S(2)}) copy-start(f32[3]{0:T(128)} %decay.5) | copy-start | bytes 40
  2.8 6.2 %collective-permute-start = (f32[4,32,128]{2,1,0:T(8,128)S(1)}, f32[4,32,128]{2,1,0:T(8,128)S(1)}, u32[]{:S(2)}, u32[]{:S(2)}) collective-permute-start(f32[4,32,128]{2,1,0:T(8,128)S(1)} %get-tuple-element.41), channel_id=1, source_target_pairs={{0,4},{1,5},{2,6},{3,7},{4,0},{5,1},{6,2},{7,3},{8,12},{9,13},{10,... | collective-permute-start | bytes 196616 | tf_op jit(solution)/shard_map/ppermute | solution.py:929
  5.9 3.2 %collective-permute-start.1 = (f32[4,32,128]{2,1,0:T(8,128)S(1)}, f32[4,32,128]{2,1,0:T(8,128)S(1)}, u32[]{:S(2)}, u32[]{:S(2)}) collective-permute-start(f32[4,32,128]{2,1,0:T(8,128)S(1)} %get-tuple-element.42), channel_id=1, source_target_pairs={{0,1},{1,0},{2,3},{3,2},{4,8},{5,9},{6,10},{7,11},{8,4},{9,5},{10,... | collective-permute-start | bytes 196616 | tf_op jit(solution)/shard_map/ppermute | solution.py:929
  5.9 6.8 %collective-permute-start.4 = (f32[10,32,128]{2,1,0:T(8,128)S(1)}, f32[10,32,128]{2,1,0:T(8,128)S(1)}, u32[]{:S(2)}, u32[]{:S(2)}) collective-permute-start(f32[10,32,128]{2,1,0:T(8,128)S(1)} %get-tuple-element.50), channel_id=1, source_target_pairs={{0,4},{1,5},{2,6},{3,7},{4,0},{5,1},{6,2},{7,3},{8,12},{9,13},{10,... | collective-permute-start | bytes 491528 | tf_op jit(solution)/shard_map/ppermute | solution.py:929
  9.1 3.6 %collective-permute-start.5 = (f32[10,32,128]{2,1,0:T(8,128)S(1)}, f32[10,32,128]{2,1,0:T(8,128)S(1)}, u32[]{:S(2)}, u32[]{:S(2)}) collective-permute-start(f32[10,32,128]{2,1,0:T(8,128)S(1)} %get-tuple-element.51), channel_id=1, source_target_pairs={{0,1},{1,0},{2,3},{3,2},{4,8},{5,9},{6,10},{7,11},{8,4},{9,5},{10,... | collective-permute-start | bytes 491528 | tf_op jit(solution)/shard_map/ppermute | solution.py:929
  9.3 7.9 %collective-permute-start.2 = (f32[296,128]{1,0:T(8,128)S(1)}, f32[296,128]{1,0:T(8,128)S(1)}, u32[]{:S(2)}, u32[]{:S(2)}) collective-permute-start(f32[296,128]{1,0:T(8,128)S(1)} %get-tuple-element.43.after), channel_id=1, source_target_pairs={{0,1},{4,5},{8,9},{12,13},{1,0},{5,4},{9,8},{13,12},{2,3},{6,7},{1... | collective-permute-start | bytes 454664 | tf_op jit(solution)/shard_map/ppermute | solution.py:929
  9.8 7.3 %collective-permute-start.3 = (f32[296,128]{1,0:T(8,128)S(1)}, f32[296,128]{1,0:T(8,128)S(1)}, u32[]{:S(2)}, u32[]{:S(2)}) collective-permute-start(f32[296,128]{1,0:T(8,128)S(1)} %get-tuple-element.44), channel_id=1, source_target_pairs={{0,4},{4,0},{8,12},{12,8},{1,2},{5,6},{9,10},{13,14},{2,1},{6,5},{... | collective-permute-start | bytes 454664 | tf_op jit(solution)/shard_map/ppermute | solution.py:929
  13.2 4.0 %copy-start.2 = (f32[256,256]{1,0:T(8,128)S(1)}, f32[256,256]{1,0:T(8,128)}, u32[]{:S(2)}) copy-start(f32[256,256]{1,0:T(8,128)} %constant.22.clone.rest_4_.rest_9_) | copy-start | bytes 786436
  13.2 4.0 %copy-start.3 = (f32[192,216]{1,0:T(8,128)S(1)}, f32[192,216]{1,0:T(8,128)}, u32[]{:S(2)}) copy-start(f32[192,216]{1,0:T(8,128)} %constant.20.clone.rest_2_.rest_7_) | copy-start | bytes 497668
  13.2 4.0 %copy-start.4 = (f32[144,144]{1,0:T(8,128)S(1)}, f32[144,144]{1,0:T(8,128)}, u32[]{:S(2)}) copy-start(f32[144,144]{1,0:T(8,128)} %constant.19.clone.rest_1_.rest_6_) | copy-start | bytes 248836
  13.2 4.0 %copy-start.5 = (f32[256,128]{1,0:T(8,128)S(1)}, f32[256,128]{1,0:T(8,128)}, u32[]{:S(2)}) copy-start(f32[256,128]{1,0:T(8,128)} %constant.23.clone.rest_5_.rest_10_) | copy-start | bytes 393220
  13.2 4.0 %copy-start.6 = (f32[96,120]{1,0:T(8,128)S(1)}, f32[96,120]{1,0:T(8,128)}, u32[]{:S(2)}) copy-start(f32[96,120]{1,0:T(8,128)} %constant.21.clone.rest_3_.rest_8_) | copy-start | bytes 138244
  13.2 4.0 %copy-start.7 = (f32[80,80]{1,0:T(8,128)S(1)}, f32[80,80]{1,0:T(8,128)}, u32[]{:S(2)}) copy-start(f32[80,80]{1,0:T(8,128)} %constant.18.clone.rest_0_.rest_5_) | copy-start | bytes 76804
  13.2 4.0 %copy-start.8 = (f32[72,128]{1,0:T(8,128)S(1)}, f32[72,128]{1,0:T(8,128)}, u32[]{:S(2)}) copy-start(f32[72,128]{1,0:T(8,128)} %constant.24.clone.rest_6_.rest_11_) | copy-start | bytes 110596
  13.3 4.0 %copy-start.9 = (f32[1,128]{1,0:T(1,128)S(1)}, f32[1,128]{1,0:T(1,128)}, u32[]{:S(2)}) copy-start(f32[1,128]{1,0:T(1,128)} %constant.25.clone.rest_7_.rest_12_) | copy-start | bytes 1540
  13.3 4.0 %copy-start.10 = (f32[1,40]{1,0:T(1,128)S(1)}, f32[1,40]{1,0:T(1,128)}, u32[]{:S(2)}) copy-start(f32[1,40]{1,0:T(1,128)} %constant.26.clone.rest_8_.rest_13_) | copy-start | bytes 484
  13.3 11.4 %collective-permute-start.6 = (f32[744,128]{1,0:T(8,128)S(1)}, f32[744,128]{1,0:T(8,128)S(1)}, u32[]{:S(2)}, u32[]{:S(2)}) collective-permute-start(f32[744,128]{1,0:T(8,128)S(1)} %get-tuple-element.52), channel_id=1, source_target_pairs={{0,1},{4,5},{8,9},{12,13},{1,0},{5,4},{9,8},{13,12},{2,3},{6,7},{1... | collective-permute-start | bytes 1142792 | tf_op jit(solution)/shard_map/ppermute | solution.py:929
  13.4 11.3 %collective-permute-start.7 = (f32[744,128]{1,0:T(8,128)S(1)}, f32[744,128]{1,0:T(8,128)S(1)}, u32[]{:S(2)}, u32[]{:S(2)}) collective-permute-start(f32[744,128]{1,0:T(8,128)S(1)} %get-tuple-element.53), channel_id=1, source_target_pairs={{0,4},{4,0},{8,12},{12,8},{1,2},{5,6},{9,10},{13,14},{2,1},{6,5},{... | collective-permute-start | bytes 1142792 | tf_op jit(solution)/shard_map/ppermute | solution.py:929
  25.6 9.1 %collective-permute-start.8 = (f32[176,128]{1,0:T(8,128)S(1)}, f32[176,128]{1,0:T(8,128)S(1)}, u32[]{:S(2)}, u32[]{:S(2)}) collective-permute-start(f32[176,128]{1,0:T(8,128)S(1)} %get-tuple-element.55), channel_id=1, source_target_pairs={{0,4},{1,5},{2,6},{3,7},{4,0},{5,1},{6,2},{7,3},{8,12},{9,13},{10,... | collective-permute-start | bytes 270344 | tf_op jit(solution)/shard_map/ppermute | solution.py:929
  25.7 9.0 %collective-permute-start.9 = (f32[176,128]{1,0:T(8,128)S(1)}, f32[176,128]{1,0:T(8,128)S(1)}, u32[]{:S(2)}, u32[]{:S(2)}) collective-permute-start(f32[176,128]{1,0:T(8,128)S(1)} %get-tuple-element.56), channel_id=1, source_target_pairs={{0,12},{1,13},{2,14},{3,15},{4,8},{5,9},{6,10},{7,11},{8,4},{9,5},... | collective-permute-start | bytes 270344 | tf_op jit(solution)/shard_map/ppermute | solution.py:929
  28.9 5.7 %collective-permute-start.10 = (f32[16,128]{1,0:T(8,128)S(1)}, f32[16,128]{1,0:T(8,128)S(1)}, u32[]{:S(2)}, u32[]{:S(2)}) collective-permute-start(f32[16,128]{1,0:T(8,128)S(1)} %get-tuple-element.57.refs_3_), channel_id=1, source_target_pairs={{0,8},{4,12},{8,0},{12,4},{1,9},{5,13},{9,1},{13,5},{2,10},{6,14},... | collective-permute-start | bytes 24584 | tf_op jit(solution)/shard_map/ppermute | solution.py:934
  34.9 1.5 %collective-permute-start.11 = (f32[392,128]{1,0:T(8,128)S(1)}, f32[392,128]{1,0:T(8,128)S(1)}, u32[]{:S(2)}, u32[]{:S(2)}) collective-permute-start(f32[392,128]{1,0:T(8,128)S(1)} %get-tuple-element.59), channel_id=1, source_target_pairs={{0,1},{4,5},{8,9},{12,13},{1,0},{5,4},{9,8},{13,12},{2,3},{6,7},{1... | collective-permute-start | bytes 602120 | tf_op jit(solution)/shard_map/ppermute | solution.py:929
  35.1 7.4 %collective-permute-start.12 = (f32[392,128]{1,0:T(8,128)S(1)}, f32[392,128]{1,0:T(8,128)S(1)}, u32[]{:S(2)}, u32[]{:S(2)}) collective-permute-start(f32[392,128]{1,0:T(8,128)S(1)} %get-tuple-element.60), channel_id=1, source_target_pairs={{0,4},{4,0},{8,12},{12,8},{1,2},{5,6},{9,10},{13,14},{2,1},{6,5},{... | collective-permute-start | bytes 602120 | tf_op jit(solution)/shard_map/ppermute | solution.py:929
  36.4 4.6 %collective-permute-start.13 = (f32[16,128]{1,0:T(8,128)S(1)}, f32[16,128]{1,0:T(8,128)S(1)}, u32[]{:S(2)}, u32[]{:S(2)}) collective-permute-start(f32[16,128]{1,0:T(8,128)S(1)} %shard_map.157.refs_0_), channel_id=1, source_target_pairs={{0,2},{1,3},{2,0},{3,1},{4,6},{5,7},{6,4},{7,5},{8,10},{9,11},{10,... | collective-permute-start | bytes 24584 | tf_op jit(solution)/shard_map/ppermute | solution.py:934
  49.2 4.4 %collective-permute-start.16 = (f32[64,128]{1,0:T(8,128)S(1)}, f32[64,128]{1,0:T(8,128)S(1)}, u32[]{:S(2)}, u32[]{:S(2)}) collective-permute-start(f32[64,128]{1,0:T(8,128)S(1)} %get-tuple-element.73), channel_id=1, source_target_pairs={{0,1},{4,5},{8,9},{12,13},{1,0},{5,4},{9,8},{13,12},{2,3},{6,7},{1... | collective-permute-start | bytes 98312 | tf_op jit(solution)/shard_map/ppermute | solution.py:929
  49.3 4.3 %collective-permute-start.17 = (f32[64,128]{1,0:T(8,128)S(1)}, f32[64,128]{1,0:T(8,128)S(1)}, u32[]{:S(2)}, u32[]{:S(2)}) collective-permute-start(f32[64,128]{1,0:T(8,128)S(1)} %get-tuple-element.74), channel_id=1, source_target_pairs={{0,4},{4,0},{8,12},{12,8},{1,2},{5,6},{9,10},{13,14},{2,1},{6,5},{... | collective-permute-start | bytes 98312 | tf_op jit(solution)/shard_map/ppermute | solution.py:929
  49.8 3.7 %collective-permute-start.14 = (f32[32,128]{1,0:T(8,128)S(1)}, f32[32,128]{1,0:T(8,128)S(1)}, u32[]{:S(2)}, u32[]{:S(2)}) collective-permute-start(f32[32,128]{1,0:T(8,128)S(1)} %get-tuple-element.71), channel_id=1, source_target_pairs={{0,4},{1,5},{2,6},{3,7},{4,0},{5,1},{6,2},{7,3},{8,12},{9,13},{10,... | collective-permute-start | bytes 49160 | tf_op jit(solution)/shard_map/ppermute | solution.py:929
  51.4 2.2 %collective-permute-start.15 = (f32[32,128]{1,0:T(8,128)S(1)}, f32[32,128]{1,0:T(8,128)S(1)}, u32[]{:S(2)}, u32[]{:S(2)}) collective-permute-start(f32[32,128]{1,0:T(8,128)S(1)} %get-tuple-element.72), channel_id=1, source_target_pairs={{0,1},{1,0},{2,3},{3,2},{4,8},{5,9},{6,10},{7,11},{8,4},{9,5},{10,... | collective-permute-start | bytes 49160 | tf_op jit(solution)/shard_map/ppermute | solution.py:929

commit v16 on v15

--- a/solution.py
+++ b/solution.py
@@ -115,7 +115,8 @@
     in_order_of_steps = np.arange(box.ey).reshape(8, box.ey // 8).T.reshape(-1)
     from_y = sine_y[MARGIN : MARGIN + box.across]
     from_x = sine_x[MARGIN : MARGIN + box.long]
-    spread = np.broadcast_to(eig_x[:, None], (box.ex, box.deep))
+    spread_x = np.broadcast_to(eig_x[:, None], (box.ex, box.deep))
+    spread_y = np.broadcast_to(eig_y[:, None], (box.ey, box.deep))
     main_z, rest_z = right_tables(sine_z)
     return [
         jnp.asarray(np.ascontiguousarray(t))
@@ -126,9 +127,9 @@
             left_table(from_y, padded(box.ey), BACKWARD),
             main_z,
             rest_z,
-            spread,
+            spread_x,
+            spread_y,
             eig_z[None, :],
-            eig_y[None, :],
         )
     ]
 
@@ -425,11 +426,17 @@
 
 
 def line_of(numbers, shape):
-    lanes = lax.broadcasted_iota(jnp.int32, shape, 1)
-    line = jnp.zeros(shape, jnp.float32)
-    for index, number in numbers:
-        line = jnp.where(lanes == index, number, line)
-    return line
+    count = -(-len(numbers) // 8) * 8
+    rows = lax.broadcasted_iota(jnp.int32, (count, shape[1]), 0)
+    lanes = lax.broadcasted_iota(jnp.int32, (count, shape[1]), 1)
+    stacked = jnp.zeros((count, shape[1]), jnp.float32)
+    place = jnp.zeros((count, shape[1]), jnp.bool_)
+    for row, (index, values) in enumerate(numbers):
+        stacked = jnp.where(rows == row, values, stacked)
+        place = place | ((rows == row) & (lanes == index))
+    sums = jnp.sum(stacked, axis=1, keepdims=True)
+    line = jnp.sum(jnp.where(place, sums, jnp.zeros_like(stacked)), axis=0, keepdims=True)
+    return jnp.broadcast_to(line, shape)
 
 
 def box_sums(box, zone, scale, load, after, diffusivity, decay, out, table):
@@ -447,19 +454,20 @@
         sums = [total + more for total, more in zip(sums, halves(row) + [load[row]])]
 
     def total(values):
-        return jnp.sum(values, keepdims=True).reshape(1, 1)
+        return jnp.sum(values, axis=0, keepdims=True)
 
     cells = box.long * box.across * box.deep
     numbers = [(index, total(sums[index]) * (2.0 / cells)) for index in range(3)]
     mass = total(sums[3])
     numbers += [(3, mass / cells)]
-    ends = total(sums[2][:, :1]) + total(sums[2][:, box.deep - 1 :])
+    lane = lax.broadcasted_iota(jnp.int32, (1, box.deep), 1)
+    ends = jnp.where((lane == 0) | (lane == box.deep - 1), total(sums[2]), 0.0)
     numbers += [
         (BOX_DIAGONAL, mass + ends),
         (LONG_HIGH, total(halves(box.long - 1)[0])),
         (LONG_LOW, total(halves(0)[0])),
-        (ACROSS_HIGH, total(sums[1][box.across - 1 :])),
-        (ACROSS_LOW, total(sums[1][:1])),
+        (ACROSS_HIGH, sums[1][box.across - 1 :]),
+        (ACROSS_LOW, sums[1][:1]),
         (LOAD_SUM, total(sums[4])),
     ]
     line = line_of(numbers, out.shape)
@@ -474,12 +482,12 @@
 def first_solve(box, load, low, high, left, right, means, zone, scale, diffusivity, decay, *rest):
     tables = rest[:N_TABLES]
     window, local, image, inverses, spectral, middle = rest[N_TABLES:]
-    spread, eig_z, eig_y = tables[6:]
+    spread_x, spread_y, eig_z = tables[6:]
     means = means_of(means)
-    base = means[3] + means[0] * spread[...] + means[2] * eig_z[...]
+    base = means[3] + means[0] * spread_x[...] + means[2] * eig_z[...]
 
     def divided(values, col):
-        divisor = base + means[1] * eig_y[0, col]
+        divisor = base + means[1] * spread_y[col : col + 1, :]
         inverse = pl.reciprocal(divisor, approx=True)
         for _ in range(2):
             inverse = inverse * (2.0 - divisor * inverse)
@@ -610,10 +618,10 @@
     for direction, labels, factor, values, far_labels, far_factor in faces:
         weight = looked_up(labels, half[direction]) * factor
         weight = weight + looked_up(far_labels, half[direction]) * far_factor
-        flows.append(jnp.sum(weight * values, keepdims=True))
+        flows.append(jnp.sum(weight * values, axis=0, keepdims=True))
     long_pos, across_pos, long_count, across_count = position()
     numbers = [
-        (IMAGE_SUM, jnp.sum(image[...], keepdims=True) + sum(flows)),
+        (IMAGE_SUM, jnp.sum(image[...], axis=0, keepdims=True) + sum(flows)),
         (FLOW_LONG_HIGH, flows[0] * as_float(long_pos < long_count - 1)),
         (FLOW_LONG_LOW, flows[1] * as_float(long_pos > 0)),
         (FLOW_ACROSS_HIGH, flows[2] * as_float(across_pos < across_count - 1)),
@@ -630,6 +638,28 @@
 
 def column(values, index):
     return values[:, index : index + 1]
+
+
+def uncoupled_groups(count, across):
+    places = np.arange(count)
+    long_step = np.abs(places[:, None] // across - places[None, :] // across)
+    across_step = np.abs(places[:, None] % across - places[None, :] % across)
+    coupled = long_step + across_step == 1
+    left = list(range(count))
+    groups = []
+    while left:
+        group = []
+        for place in sorted(left, key=lambda p: (coupled[p][left].sum(), p)):
+            if not coupled[place][group].any():
+                group.append(place)
+        left = [place for place in left if place not in group]
+        for place in group:
+            beside = [other for other in left if coupled[place][other]]
+            for other in beside:
+                coupled[other][beside] = True
+                coupled[other][other] = False
+        groups.append(group)
+    return groups
 
 
 def coarse_inverse(numbers, work):
@@ -661,10 +691,13 @@
         matrix = matrix - jnp.where((cols == rows + shift) & (cols < count), coupling, blank)
     matrix = jnp.where(cols == rows + count, jnp.ones((count, 1), jnp.float32), matrix)
     if count <= 16:
-        for step in range(count):
-            pivot_row = matrix[step : step + 1, :] / matrix[step : step + 1, step : step + 1]
-            rest = matrix - matrix[:, step : step + 1] * pivot_row
-            matrix = jnp.where(rows == step, pivot_row, rest)
+        for group in uncoupled_groups(count, across):
+            rest = matrix
+            for step in group:
+                pivot_row = matrix[step : step + 1, :] / matrix[step : step + 1, step : step + 1]
+                rest = rest - matrix[:, step : step + 1] * pivot_row
+                rest = jnp.where(rows == step, pivot_row, rest)
+            matrix = rest
         return pltpu.roll(matrix, width - count, 1)
     work[...] = matrix
 

time: 54.8 us -> 52.2 us (0.953)
  Pallas kernels: 28 us -> 25.4 us
    pallas_call x1, Pallas kernels: 7.38 us -> 5.75 us  [on_device(): call(functools.partial(first_solve, box), (window, cells, f32(across, dee...]
    pallas_call x1, Pallas kernels: 1.48 us -> 0.86 us  [on_device(): call(functools.partial(coarse_corrections, len(parts)), f32(8, -(-count /...]
  transfers between devices with their start and end apart: 18 -> 18, of which waited for: 5 -> 5; matrix products, arithmetic and copies ran while one was open for 0% -> 0% of each run, Pallas kernels for 31% -> 28%
where the time goes in v16:
time: 52.2 us; the launch traced here: 52 us
  Pallas kernels  25.4 us (49%)
  starting transfers between devices  18.3 us (35%)
  waiting for transfers between devices  7.14 us (14%)
  between operations  1.08 us (2%)
    ppermute x8, starting transfers between devices, exchange(): lax.ppermute(first, axes, ways[0])  9 us
    ppermute x8, starting transfers between devices, exchange(): lax.ppermute(second, axes, ways[1])  8.61 us
    pallas_call x1, Pallas kernels, on_device(): call(functools.partial(second_solve, box), (cells, row, row, col, col, ce...  6.7 us
    pallas_call x1, Pallas kernels, on_device(): call(functools.partial(first_solve, box), (window, cells, f32(across, dee...  5.75 us
    ppermute x2, waiting for transfers between devices, two_away(): return lax.ppermute(table, axis, [(i, (i + 2) % size) for i in range(size)])  5.18 us
    pallas_call x1, Pallas kernels, on_device(): call(functools.partial(side_weights, box), (window,) * 4, [VMEM] * 6 + [S...  2.25 us
    pallas_call x1, Pallas kernels, on_device(): call(functools.partial(bring_edges, box), (whole_zone, cells, cells) + (f...  2.19 us
    ppermute x8, waiting for transfers between devices, exchange(): lax.ppermute(first, axes, ways[0])  1.93 us
  transfers between devices with their start and end apart: 18, of which 5 were waited for; matrix products, arithmetic and copies ran while one was open for 0% of the time, Pallas kernels for 28%

profile of v16, /device:TPU:0, one launch (start us, length us, event | category | flops | bytes accessed | tf_op | source)
XLA Modules:
  0.0 52.0 jit_solution(10884278909357788580)
XLA Ops:
  0.6 2.2 %shard_map.149 = (s32[64,32,128]{2,1,0:T(8,128)S(1)}, f32[64,32,128]{2,1,0:T(8,128)S(1)}, f32[64,32,128]{2,1,0:T(8,128)S(1)}, f32[4,32,128]{2,1,0:T(8,128)S(1)},...) custom-call(s32[64,32,128]{2,1,0:T(8,128)} %zone.1, f32[64,32,128]{2,1,0:T(8,128)} %scale.1, ...), custom_call_target="tpu_custom_call" | custom-call | tf_op jit(solution)/shard_map/pallas_call | solution.py:1012
  2.8 3.1 %collective-permute-start = (f32[4,32,128]{2,1,0:T(8,128)S(1)}, f32[4,32,128]{2,1,0:T(8,128)S(1)}, u32[]{:S(2)}, u32[]{:S(2)}) collective-permute-start(f32[4,32,128]{2,1,0:T(8,128)S(1)} %get-tuple-element.41), channel_id=1, source_target_pairs={{0,4},{1,5},{2,6},{3,7},{4,0},{5,1},{6,2},{7,3},{8,12},{9,13},{10,... | collective-permute-start | bytes 196616 | tf_op jit(solution)/shard_map/ppermute | solution.py:962
  5.9 3.1 %collective-permute-start.4 = (f32[10,32,128]{2,1,0:T(8,128)S(1)}, f32[10,32,128]{2,1,0:T(8,128)S(1)}, u32[]{:S(2)}, u32[]{:S(2)}) collective-permute-start(f32[10,32,128]{2,1,0:T(8,128)S(1)} %get-tuple-element.50), channel_id=1, source_target_pairs={{0,4},{1,5},{2,6},{3,7},{4,0},{5,1},{6,2},{7,3},{8,12},{9,13},{10,... | collective-permute-start | bytes 491528 | tf_op jit(solution)/shard_map/ppermute | solution.py:962
  9.1 0.2 shard_map.150
  9.3 0.6 %collective-permute-start.2 = (f32[296,128]{1,0:T(8,128)S(1)}, f32[296,128]{1,0:T(8,128)S(1)}, u32[]{:S(2)}, u32[]{:S(2)}) collective-permute-start(f32[296,128]{1,0:T(8,128)S(1)} %get-tuple-element.43.after), channel_id=1, source_target_pairs={{0,1},{4,5},{8,9},{12,13},{1,0},{5,4},{9,8},{13,12},{2,3},{6,7},{1... | collective-permute-start | bytes 454664 | tf_op jit(solution)/shard_map/ppermute | solution.py:962
  9.8 2.2 %collective-permute-start.3 = (f32[296,128]{1,0:T(8,128)S(1)}, f32[296,128]{1,0:T(8,128)S(1)}, u32[]{:S(2)}, u32[]{:S(2)}) collective-permute-start(f32[296,128]{1,0:T(8,128)S(1)} %get-tuple-element.44), channel_id=1, source_target_pairs={{0,4},{4,0},{8,12},{12,8},{1,2},{5,6},{9,10},{13,14},{2,1},{6,5},{... | collective-permute-start | bytes 454664 | tf_op jit(solution)/shard_map/ppermute | solution.py:962
  12.0 0.7 %collective-permute-done.4.refs_2_.low = f32[10,32,128]{2,1,0:T(8,128)S(1)} collective-permute-done((f32[10,32,128]{2,1,0:T(8,128)S(1)}, f32[10,32,128]{2,1,0:T(8,128)S(1)}, u32[]{:S(2)}, u32[]{:S(2)}) %collective-permute-start.4) | collective-permute-done | bytes 163872 | tf_op jit(solution)/shard_map/ppermute | solution.py:962
  12.7 0.4 shard_map.153
  13.3 0.1 collective-permute-start.6
  13.4 2.2 %collective-permute-start.7 = (f32[744,128]{1,0:T(8,128)S(1)}, f32[744,128]{1,0:T(8,128)S(1)}, u32[]{:S(2)}, u32[]{:S(2)}) collective-permute-start(f32[744,128]{1,0:T(8,128)S(1)} %get-tuple-element.53), channel_id=1, source_target_pairs={{0,4},{4,0},{8,12},{12,8},{1,2},{5,6},{9,10},{13,14},{2,1},{6,5},{... | collective-permute-start | bytes 1142792 | tf_op jit(solution)/shard_map/ppermute | solution.py:962
  15.5 1.3 %shard_map.151 = (f32[8,128]{1,0:T(8,128)S(1)}, f32[16,128]{1,0:T(8,128)S(1)}) custom-call(s32[64,32,128]{2,1,0:T(8,128)S(1)} %get-tuple-element.45.zone.refs_1_, f32[64,32,128]{2,1,0:T(8,128)S(1)} %get-tuple-element.46.scale.refs_0_, f32[64,32,128]{2,1,0:T(8,128)S(1)} %get-tuple-element.40.refs_0_.load, f32[296,128]{1,0:T(8,128)S(1)} %get-tuple-element.43.after, ...), custom_call_target="tpu_custom_call" | custom-call | tf_op jit(solution)/shard_map/pallas_call | solution.py:1022
  17.0 5.7 %shard_map.152 = (f32[74,48,128]{2,1,0:T(8,128)S(1)}, f32[64,32,128]{2,1,0:T(8,128)S(1)}, f32[32,128]{1,0:T(8,128)S(1)}, f32[40,72,128]{2,1,0:T(8,128)S(1)}) custom-call(f32[64,32,128]{2,1,0:T(8,128)S(1)} %get-tuple-element.40.refs_0_.load, f32[4,32,128]{2,1,0:T(8,128)S(1)} %collective-permute-done.refs_1_.low, ...), custom_call_target="tpu_custom_call" | custom-call | flops 4000000000 | tf_op jit(solution)/shard_map/pallas_call | solution.py:1028
  22.7 0.9 %shard_map.154 = (f32[16,128]{1,0:T(8,128)S(1)}, f32[176,128]{1,0:T(8,128)S(1)}, f32[176,128]{1,0:T(8,128)S(1)}) custom-call(s32[64,32,128]{2,1,0:T(8,128)S(1)} %get-tuple-element.45.zone.refs_1_, f32[64,32,128]{2,1,0:T(8,128)S(1)} %get-tuple-element.46.scale.refs_0_, f32[64,32,128]{2,1,0:T(8,128)S(1)} %get-tuple-element.48.local.refs_0_, ...), custom_call_target="tpu_custom_call" | custom-call | tf_op jit(solution)/shard_map/pallas_call | solution.py:1036
  23.7 0.4 collective-permute-start.8
  24.1 3.2 %collective-permute-start.9 = (f32[176,128]{1,0:T(8,128)S(1)}, f32[176,128]{1,0:T(8,128)S(1)}, u32[]{:S(2)}, u32[]{:S(2)}) collective-permute-start(f32[176,128]{1,0:T(8,128)S(1)} %get-tuple-element.56), channel_id=1, source_target_pairs={{0,12},{1,13},{2,14},{3,15},{4,8},{5,9},{6,10},{7,11},{8,4},{9,5},... | collective-permute-start | bytes 270344 | tf_op jit(solution)/shard_map/ppermute | solution.py:962
  27.3 2.3 %shard_map.155 = (f32[74,48,128]{2,1,0:T(8,128)S(1)}, f32[74,48,128]{2,1,0:T(8,128)S(1)}, f32[74,48,128]{2,1,0:T(8,128)S(1)}, f32[74,48,128]{2,1,0:T(8,128)S(1)}) custom-call(s32[64,32,128]{2,1,0:T(8,128)S(1)} %get-tuple-element.45.zone.refs_1_, f32[64,32,128]{2,1,0:T(8,128)S(1)} %get-tuple-element.46.scale.refs_0_, ...), custom_call_target="tpu_custom_call" | custom-call | flops 1000000000 | tf_op jit(solution)/shard_map/pallas_call | solution.py:1044
  29.5 3.2 %collective-permute-done.10.refs_6_ = f32[16,128]{1,0:T(8,128)S(1)} collective-permute-done((f32[16,128]{1,0:T(8,128)S(1)}, f32[16,128]{1,0:T(8,128)S(1)}, u32[]{:S(2)}, u32[]{:S(2)}) %collective-permute-start.10) | collective-permute-done | bytes 8224 | tf_op jit(solution)/shard_map/ppermute | solution.py:967
  32.7 0.2 shard_map.156
  32.9 0.1 collective-permute-start.11
  33.0 0.6 %collective-permute-start.12 = (f32[392,128]{1,0:T(8,128)S(1)}, f32[392,128]{1,0:T(8,128)S(1)}, u32[]{:S(2)}, u32[]{:S(2)}) collective-permute-start(f32[392,128]{1,0:T(8,128)S(1)} %get-tuple-element.60), channel_id=1, source_target_pairs={{0,4},{4,0},{8,12},{12,8},{1,2},{5,6},{9,10},{13,14},{2,1},{6,5},{... | collective-permute-start | bytes 602120 | tf_op jit(solution)/shard_map/ppermute | solution.py:962
  33.5 0.9 %collective-permute-done.11.message.left = f32[392,128]{1,0:T(8,128)S(1)} collective-permute-done((f32[392,128]{1,0:T(8,128)S(1)}, f32[392,128]{1,0:T(8,128)S(1)}, u32[]{:S(2)}, u32[]{:S(2)}) %collective-permute-start.11) | collective-permute-done | bytes 200736 | tf_op jit(solution)/shard_map/ppermute | solution.py:962
  34.4 0.7 %collective-permute-start.13 = (f32[16,128]{1,0:T(8,128)S(1)}, f32[16,128]{1,0:T(8,128)S(1)}, u32[]{:S(2)}, u32[]{:S(2)}) collective-permute-start(f32[16,128]{1,0:T(8,128)S(1)} %shard_map.157.refs_0_), channel_id=1, source_target_pairs={{0,2},{1,3},{2,0},{3,1},{4,6},{5,7},{6,4},{7,5},{8,10},{9,11},{10,... | collective-permute-start | bytes 24584 | tf_op jit(solution)/shard_map/ppermute | solution.py:967
  35.1 1.8 %shard_map.159 = (f32[74,48,128]{2,1,0:T(8,128)S(1)}, f32[74,48,128]{2,1,0:T(8,128)S(1)}) custom-call(f32[74,48,128]{2,1,0:T(8,128)S(1)} %get-tuple-element.64.zone_window, f32[74,48,128]{2,1,0:T(8,128)S(1)} %get-tuple-element.65.scale_window, f32[3,3]{1,0:T(4,128)S(1)} %copy-done, f32[3]{0:T(128)S(1)} %copy-done.1), custom_call_target="tpu_custom_call" | custom-call | flops 1000000000 | tf_op jit(solution)/shard_map/pallas_call | solution.py:1050
  37.0 2.0 %collective-permute-done.13.refs_1_ = f32[16,128]{1,0:T(8,128)S(1)} collective-permute-done((f32[16,128]{1,0:T(8,128)S(1)}, f32[16,128]{1,0:T(8,128)S(1)}, u32[]{:S(2)}, u32[]{:S(2)}) %collective-permute-start.13) | collective-permute-done | bytes 8224 | tf_op jit(solution)/shard_map/ppermute | solution.py:967
  39.0 0.9 %shard_map.158.answers = f32[8,128]{1,0:T(8,128)S(1)} custom-call(f32[16,128]{1,0:T(8,128)S(1)} %shard_map.157.refs_0_, f32[16,128]{1,0:T(8,128)S(1)} %collective-permute-done.13.refs_1_), custom_call_target="tpu_custom_call" | custom-call | tf_op jit(solution)/shard_map/pallas_call | solution.py:1065
  39.9 6.7 %shard_map.160 = (f32[64,32,128]{2,1,0:T(8,128)S(1)}, f32[32,128]{1,0:T(8,128)S(1)}, f32[32,128]{1,0:T(8,128)S(1)}, f32[64,128]{1,0:T(8,128)S(1)}, f32[64,128]{1,0:T(8,128)S(1)}, /*index=5*/f32[64,32,128]{2,1,0:T(8,128)}) custom-call(f32[64,32,128]{2,1,0:T(8,128)S(1)} %get-tuple-element.48.local.refs_0_, ...), custom_call_target="tpu_custom_call" | custom-call | flops 4000000000 | tf_op jit(solution)/shard_map/pallas_call | solution.py:1071
  46.6 0.1 collective-permute-start.16
  46.7 0.5 %collective-permute-start.17 = (f32[64,128]{1,0:T(8,128)S(1)}, f32[64,128]{1,0:T(8,128)S(1)}, u32[]{:S(2)}, u32[]{:S(2)}) collective-permute-start(f32[64,128]{1,0:T(8,128)S(1)} %get-tuple-element.74), channel_id=1, source_target_pairs={{0,4},{4,0},{8,12},{12,8},{1,2},{5,6},{9,10},{13,14},{2,1},{6,5},{... | collective-permute-start | bytes 98312 | tf_op jit(solution)/shard_map/ppermute | solution.py:962
  47.2 1.5 %collective-permute-start.14 = (f32[32,128]{1,0:T(8,128)S(1)}, f32[32,128]{1,0:T(8,128)S(1)}, u32[]{:S(2)}, u32[]{:S(2)}) collective-permute-start(f32[32,128]{1,0:T(8,128)S(1)} %get-tuple-element.71), channel_id=1, source_target_pairs={{0,4},{1,5},{2,6},{3,7},{4,0},{5,1},{6,2},{7,3},{8,12},{9,13},{10,... | collective-permute-start | bytes 49160 | tf_op jit(solution)/shard_map/ppermute | solution.py:962
  48.7 1.9 %shard_map.161 = (f32[2,32,128]{2,1,0:T(8,128)S(1)}, f32[2,64,8,128]{3,2,1,0:T(8,128)S(1)}, f32[64,32,128]{2,1,0:T(8,128)}) custom-call(f32[64,32,128]{2,1,0:T(8,128)S(1)} %get-tuple-element.40.refs_0_.load, f32[64,32,128]{2,1,0:T(8,128)S(1)} %get-tuple-element.70.iterate, f32[74,48,128]{2,1,0:T(8,128)S(1)} %get-tuple-element.58.refs_7_.rest_0_.to_long, ...), custom_call_target="tpu_custom_call" | custom-call | flops 1000000000 | tf_op jit(solution)/shard_map/pallas_call | solution.py:1081
  50.6 0.3 collective-permute-done.14.low
  51.0 0.9 %shard_map.162 = f32[64,32,128]{2,1,0:T(8,128)} custom-call(f32[64,32,128]{2,1,0:T(8,128)S(1)} %get-tuple-element.70.iterate, f32[32,128]{1,0:T(8,128)S(1)} %collective-permute-done.14.low, f32[32,128]{1,0:T(8,128)S(1)} %collective-permute-done.15.high, f32[64,128]{1,0:T(8,128)S(1)} %collective-permute-done.16.left, ...), custom_call_target="tpu_custom_call", output_to_operand_aliasing={{}: (9, {})} | custom-call | tf_op jit(solution)/shard_map/pallas_call | solution.py:1093
  (40 shorter events, 0.1 us)
Async XLA Ops:
  2.8 12.7 %copy-start = (f32[3,3]{1,0:T(4,128)S(1)}, f32[3,3]{1,0:T(4,128)}, u32[]{:S(2)}) copy-start(f32[3,3]{1,0:T(4,128)} %diffusivity.9) | copy-start | bytes 112
  2.8 12.7 %copy-start.1 = (f32[3]{0:T(128)S(1)}, f32[3]{0:T(128)}, u32[]{:S(2)}) copy-start(f32[3]{0:T(128)} %decay.5) | copy-start | bytes 40
  2.8 6.2 %collective-permute-start = (f32[4,32,128]{2,1,0:T(8,128)S(1)}, f32[4,32,128]{2,1,0:T(8,128)S(1)}, u32[]{:S(2)}, u32[]{:S(2)}) collective-permute-start(f32[4,32,128]{2,1,0:T(8,128)S(1)} %get-tuple-element.41), channel_id=1, source_target_pairs={{0,4},{1,5},{2,6},{3,7},{4,0},{5,1},{6,2},{7,3},{8,12},{9,13},{10,... | collective-permute-start | bytes 196616 | tf_op jit(solution)/shard_map/ppermute | solution.py:962
  5.9 3.2 %collective-permute-start.1 = (f32[4,32,128]{2,1,0:T(8,128)S(1)}, f32[4,32,128]{2,1,0:T(8,128)S(1)}, u32[]{:S(2)}, u32[]{:S(2)}) collective-permute-start(f32[4,32,128]{2,1,0:T(8,128)S(1)} %get-tuple-element.42), channel_id=1, source_target_pairs={{0,1},{1,0},{2,3},{3,2},{4,8},{5,9},{6,10},{7,11},{8,4},{9,5},{10,... | collective-permute-start | bytes 196616 | tf_op jit(solution)/shard_map/ppermute | solution.py:962
  5.9 6.8 %collective-permute-start.4 = (f32[10,32,128]{2,1,0:T(8,128)S(1)}, f32[10,32,128]{2,1,0:T(8,128)S(1)}, u32[]{:S(2)}, u32[]{:S(2)}) collective-permute-start(f32[10,32,128]{2,1,0:T(8,128)S(1)} %get-tuple-element.50), channel_id=1, source_target_pairs={{0,4},{1,5},{2,6},{3,7},{4,0},{5,1},{6,2},{7,3},{8,12},{9,13},{10,... | collective-permute-start | bytes 491528 | tf_op jit(solution)/shard_map/ppermute | solution.py:962
  9.1 3.6 %collective-permute-start.5 = (f32[10,32,128]{2,1,0:T(8,128)S(1)}, f32[10,32,128]{2,1,0:T(8,128)S(1)}, u32[]{:S(2)}, u32[]{:S(2)}) collective-permute-start(f32[10,32,128]{2,1,0:T(8,128)S(1)} %get-tuple-element.51), channel_id=1, source_target_pairs={{0,1},{1,0},{2,3},{3,2},{4,8},{5,9},{6,10},{7,11},{8,4},{9,5},{10,... | collective-permute-start | bytes 491528 | tf_op jit(solution)/shard_map/ppermute | solution.py:962
  9.3 7.6 %collective-permute-start.2 = (f32[296,128]{1,0:T(8,128)S(1)}, f32[296,128]{1,0:T(8,128)S(1)}, u32[]{:S(2)}, u32[]{:S(2)}) collective-permute-start(f32[296,128]{1,0:T(8,128)S(1)} %get-tuple-element.43.after), channel_id=1, source_target_pairs={{0,1},{4,5},{8,9},{12,13},{1,0},{5,4},{9,8},{13,12},{2,3},{6,7},{1... | collective-permute-start | bytes 454664 | tf_op jit(solution)/shard_map/ppermute | solution.py:962
  9.8 7.0 %collective-permute-start.3 = (f32[296,128]{1,0:T(8,128)S(1)}, f32[296,128]{1,0:T(8,128)S(1)}, u32[]{:S(2)}, u32[]{:S(2)}) collective-permute-start(f32[296,128]{1,0:T(8,128)S(1)} %get-tuple-element.44), channel_id=1, source_target_pairs={{0,4},{4,0},{8,12},{12,8},{1,2},{5,6},{9,10},{13,14},{2,1},{6,5},{... | collective-permute-start | bytes 454664 | tf_op jit(solution)/shard_map/ppermute | solution.py:962
  13.2 3.7 %copy-start.2 = (f32[256,256]{1,0:T(8,128)S(1)}, f32[256,256]{1,0:T(8,128)}, u32[]{:S(2)}) copy-start(f32[256,256]{1,0:T(8,128)} %constant.22.clone.rest_4_.rest_9_) | copy-start | bytes 786436
  13.2 3.7 %copy-start.3 = (f32[192,216]{1,0:T(8,128)S(1)}, f32[192,216]{1,0:T(8,128)}, u32[]{:S(2)}) copy-start(f32[192,216]{1,0:T(8,128)} %constant.20.clone.rest_2_.rest_7_) | copy-start | bytes 497668
  13.2 3.7 %copy-start.4 = (f32[144,144]{1,0:T(8,128)S(1)}, f32[144,144]{1,0:T(8,128)}, u32[]{:S(2)}) copy-start(f32[144,144]{1,0:T(8,128)} %constant.19.clone.rest_1_.rest_6_) | copy-start | bytes 248836
  13.2 3.7 %copy-start.5 = (f32[256,128]{1,0:T(8,128)S(1)}, f32[256,128]{1,0:T(8,128)}, u32[]{:S(2)}) copy-start(f32[256,128]{1,0:T(8,128)} %constant.23.clone.rest_5_.rest_10_) | copy-start | bytes 393220
  13.2 3.7 %copy-start.6 = (f32[96,120]{1,0:T(8,128)S(1)}, f32[96,120]{1,0:T(8,128)}, u32[]{:S(2)}) copy-start(f32[96,120]{1,0:T(8,128)} %constant.21.clone.rest_3_.rest_8_) | copy-start | bytes 138244
  13.2 3.7 %copy-start.7 = (f32[80,80]{1,0:T(8,128)S(1)}, f32[80,80]{1,0:T(8,128)}, u32[]{:S(2)}) copy-start(f32[80,80]{1,0:T(8,128)} %constant.18.clone.rest_0_.rest_5_) | copy-start | bytes 76804
  13.2 3.7 %copy-start.8 = (f32[72,128]{1,0:T(8,128)S(1)}, f32[72,128]{1,0:T(8,128)}, u32[]{:S(2)}) copy-start(f32[72,128]{1,0:T(8,128)} %constant.24.clone.rest_6_.rest_11_) | copy-start | bytes 110596
  13.3 3.7 %copy-start.9 = (f32[40,128]{1,0:T(8,128)S(1)}, f32[40,128]{1,0:T(8,128)}, u32[]{:S(2)}) copy-start(f32[40,128]{1,0:T(8,128)} %constant.25.clone.rest_7_.rest_12_) | copy-start | bytes 61444
  13.3 3.7 %copy-start.10 = (f32[1,128]{1,0:T(1,128)S(1)}, f32[1,128]{1,0:T(1,128)}, u32[]{:S(2)}) copy-start(f32[1,128]{1,0:T(1,128)} %constant.26.clone.rest_8_.rest_13_) | copy-start | bytes 1540
  13.3 9.4 %collective-permute-start.6 = (f32[744,128]{1,0:T(8,128)S(1)}, f32[744,128]{1,0:T(8,128)S(1)}, u32[]{:S(2)}, u32[]{:S(2)}) collective-permute-start(f32[744,128]{1,0:T(8,128)S(1)} %get-tuple-element.52), channel_id=1, source_target_pairs={{0,1},{4,5},{8,9},{12,13},{1,0},{5,4},{9,8},{13,12},{2,3},{6,7},{1... | collective-permute-start | bytes 1142792 | tf_op jit(solution)/shard_map/ppermute | solution.py:962
  13.4 9.4 %collective-permute-start.7 = (f32[744,128]{1,0:T(8,128)S(1)}, f32[744,128]{1,0:T(8,128)S(1)}, u32[]{:S(2)}, u32[]{:S(2)}) collective-permute-start(f32[744,128]{1,0:T(8,128)S(1)} %get-tuple-element.53), channel_id=1, source_target_pairs={{0,4},{4,0},{8,12},{12,8},{1,2},{5,6},{9,10},{13,14},{2,1},{6,5},{... | collective-permute-start | bytes 1142792 | tf_op jit(solution)/shard_map/ppermute | solution.py:962
  23.7 9.0 %collective-permute-start.8 = (f32[176,128]{1,0:T(8,128)S(1)}, f32[176,128]{1,0:T(8,128)S(1)}, u32[]{:S(2)}, u32[]{:S(2)}) collective-permute-start(f32[176,128]{1,0:T(8,128)S(1)} %get-tuple-element.55), channel_id=1, source_target_pairs={{0,4},{1,5},{2,6},{3,7},{4,0},{5,1},{6,2},{7,3},{8,12},{9,13},{10,... | collective-permute-start | bytes 270344 | tf_op jit(solution)/shard_map/ppermute | solution.py:962
  24.1 8.6 %collective-permute-start.9 = (f32[176,128]{1,0:T(8,128)S(1)}, f32[176,128]{1,0:T(8,128)S(1)}, u32[]{:S(2)}, u32[]{:S(2)}) collective-permute-start(f32[176,128]{1,0:T(8,128)S(1)} %get-tuple-element.56), channel_id=1, source_target_pairs={{0,12},{1,13},{2,14},{3,15},{4,8},{5,9},{6,10},{7,11},{8,4},{9,5},... | collective-permute-start | bytes 270344 | tf_op jit(solution)/shard_map/ppermute | solution.py:962
  27.3 5.4 %collective-permute-start.10 = (f32[16,128]{1,0:T(8,128)S(1)}, f32[16,128]{1,0:T(8,128)S(1)}, u32[]{:S(2)}, u32[]{:S(2)}) collective-permute-start(f32[16,128]{1,0:T(8,128)S(1)} %get-tuple-element.57.refs_3_), channel_id=1, source_target_pairs={{0,8},{4,12},{8,0},{12,4},{1,9},{5,13},{9,1},{13,5},{2,10},{6,14},... | collective-permute-start | bytes 24584 | tf_op jit(solution)/shard_map/ppermute | solution.py:967
  32.9 1.5 %collective-permute-start.11 = (f32[392,128]{1,0:T(8,128)S(1)}, f32[392,128]{1,0:T(8,128)S(1)}, u32[]{:S(2)}, u32[]{:S(2)}) collective-permute-start(f32[392,128]{1,0:T(8,128)S(1)} %get-tuple-element.59), channel_id=1, source_target_pairs={{0,1},{4,5},{8,9},{12,13},{1,0},{5,4},{9,8},{13,12},{2,3},{6,7},{1... | collective-permute-start | bytes 602120 | tf_op jit(solution)/shard_map/ppermute | solution.py:962
  33.0 6.9 %collective-permute-start.12 = (f32[392,128]{1,0:T(8,128)S(1)}, f32[392,128]{1,0:T(8,128)S(1)}, u32[]{:S(2)}, u32[]{:S(2)}) collective-permute-start(f32[392,128]{1,0:T(8,128)S(1)} %get-tuple-element.60), channel_id=1, source_target_pairs={{0,4},{4,0},{8,12},{12,8},{1,2},{5,6},{9,10},{13,14},{2,1},{6,5},{... | collective-permute-start | bytes 602120 | tf_op jit(solution)/shard_map/ppermute | solution.py:962
  34.4 4.6 %collective-permute-start.13 = (f32[16,128]{1,0:T(8,128)S(1)}, f32[16,128]{1,0:T(8,128)S(1)}, u32[]{:S(2)}, u32[]{:S(2)}) collective-permute-start(f32[16,128]{1,0:T(8,128)S(1)} %shard_map.157.refs_0_), channel_id=1, source_target_pairs={{0,2},{1,3},{2,0},{3,1},{4,6},{5,7},{6,4},{7,5},{8,10},{9,11},{10,... | collective-permute-start | bytes 24584 | tf_op jit(solution)/shard_map/ppermute | solution.py:967
  46.6 4.4 %collective-permute-start.16 = (f32[64,128]{1,0:T(8,128)S(1)}, f32[64,128]{1,0:T(8,128)S(1)}, u32[]{:S(2)}, u32[]{:S(2)}) collective-permute-start(f32[64,128]{1,0:T(8,128)S(1)} %get-tuple-element.73), channel_id=1, source_target_pairs={{0,1},{4,5},{8,9},{12,13},{1,0},{5,4},{9,8},{13,12},{2,3},{6,7},{1... | collective-permute-start | bytes 98312 | tf_op jit(solution)/shard_map/ppermute | solution.py:962
  46.7 4.3 %collective-permute-start.17 = (f32[64,128]{1,0:T(8,128)S(1)}, f32[64,128]{1,0:T(8,128)S(1)}, u32[]{:S(2)}, u32[]{:S(2)}) collective-permute-start(f32[64,128]{1,0:T(8,128)S(1)} %get-tuple-element.74), channel_id=1, source_target_pairs={{0,4},{4,0},{8,12},{12,8},{1,2},{5,6},{9,10},{13,14},{2,1},{6,5},{... | collective-permute-start | bytes 98312 | tf_op jit(solution)/shard_map/ppermute | solution.py:962
  47.2 3.7 %collective-permute-start.14 = (f32[32,128]{1,0:T(8,128)S(1)}, f32[32,128]{1,0:T(8,128)S(1)}, u32[]{:S(2)}, u32[]{:S(2)}) collective-permute-start(f32[32,128]{1,0:T(8,128)S(1)} %get-tuple-element.71), channel_id=1, source_target_pairs={{0,4},{1,5},{2,6},{3,7},{4,0},{5,1},{6,2},{7,3},{8,12},{9,13},{10,... | collective-permute-start | bytes 49160 | tf_op jit(solution)/shard_map/ppermute | solution.py:962
  48.7 2.2 %collective-permute-start.15 = (f32[32,128]{1,0:T(8,128)S(1)}, f32[32,128]{1,0:T(8,128)S(1)}, u32[]{:S(2)}, u32[]{:S(2)}) collective-permute-start(f32[32,128]{1,0:T(8,128)S(1)} %get-tuple-element.72), channel_id=1, source_target_pairs={{0,1},{1,0},{2,3},{3,2},{4,8},{5,9},{6,10},{7,11},{8,4},{9,5},{10,... | collective-permute-start | bytes 49160 | tf_op jit(solution)/shard_map/ppermute | solution.py:962

commit v17 on v16

--- a/solution.py
+++ b/solution.py
@@ -25,7 +25,6 @@
 IMAGE_SUM, FLOW_LONG_HIGH, FLOW_LONG_LOW, FLOW_ACROSS_HIGH, FLOW_ACROSS_LOW = range(16, 21)
 
 VMEM = pl.BlockSpec(memory_space=pltpu.VMEM)
-SMEM = pl.BlockSpec(memory_space=pltpu.SMEM)
 
 
 def sine_basis(length):
@@ -298,10 +297,7 @@
         second[second.shape[0] - known.shape[0] :, :] = known
 
 
-def bring_edges(
-    box, zone, scale, load, own_zone, own_scale, own_load, load_first, load_second, first, second,
-    staged, sems
-):
+def bring_edges(box, zone, scale, load, load_first, load_second, first, second, staged, sems):
     even = is_even("wide")
 
     def edges(wide):
@@ -309,15 +305,12 @@
         return [pl.ds(jnp.where(even, *pair), wide) for pair in ((up, down), (down, up))]
 
     copies = [
+        (zone.at[edges(REACH)[0]], staged.at[0]),
+        (zone.at[edges(REACH)[1]], staged.at[1]),
         (load.at[edges(MARGIN)[0]], load_first),
         (load.at[edges(MARGIN)[1]], load_second),
-        (zone.at[edges(REACH)[0]], staged.at[0]),
-        (zone.at[edges(REACH)[1]], staged.at[1]),
         (scale.at[edges(REACH)[0]], first.at[:REACH]),
         (scale.at[edges(REACH)[1]], second.at[:REACH]),
-        (load, own_load),
-        (scale, own_scale),
-        (zone, own_zone),
     ]
     copies = [
         pltpu.make_async_copy(source, target, sems.at[index])
@@ -325,11 +318,24 @@
     ]
     for copy in copies:
         copy.start()
-    for copy in copies[:4]:
+    for copy in copies[:2]:
         copy.wait()
     first[REACH:] = staged[0].astype(jnp.float32)
     second[REACH:] = staged[1].astype(jnp.float32)
-    for copy in copies[4:]:
+    for copy in copies[2:]:
+        copy.wait()
+
+
+def bring_box(load, scale, zone, after, own_load, own_scale, own_zone, sems):
+    del after
+    pairs = ((load, own_load), (scale, own_scale), (zone, own_zone))
+    copies = [
+        pltpu.make_async_copy(source, target, sems.at[index])
+        for index, (source, target) in enumerate(pairs)
+    ]
+    for copy in copies:
+        copy.start()
+    for copy in copies:
         copy.wait()
 
 
@@ -442,8 +448,8 @@
 def box_sums(box, zone, scale, load, after, diffusivity, decay, out, table):
     del after
     nothing = jnp.zeros((box.across, box.deep), jnp.float32)
-    half = [[0.5 * diffusivity[z, d] for z in range(3)] for d in range(3)]
-    rates = [decay[z] for z in range(3)]
+    half = [[0.5 * diffusivity[z : z + 1, d : d + 1] for z in range(3)] for d in range(3)]
+    rates = [decay[0:1, z : z + 1] for z in range(3)]
 
     def halves(row):
         labels, factor = zone[row], scale[row]
@@ -494,8 +500,8 @@
         inverses[col] = inverse
         return values * inverse
 
-    half = [0.5 * diffusivity[z, 2] for z in range(3)]
-    rates = [decay[z] for z in range(3)]
+    half = [0.5 * diffusivity[z : z + 1, 2:3] for z in range(3)]
+    rates = [decay[0:1, z : z + 1] for z in range(3)]
     lane = lax.broadcasted_iota(jnp.int32, (box.across, box.deep), 1)
     ends = jnp.where((lane == 0) | (lane == box.deep - 1), jnp.float32(1.0), jnp.float32(0.0))
     image[...] = jnp.zeros((box.across, box.deep), jnp.float32)
@@ -535,7 +541,7 @@
         wide_sides = Sides("wide", *(ref.at[start : start + REACH] for ref in (low, high)))
         narrow_sides = Sides("narrow", left, right)
         fill_window(box, window, own, wide_sides, narrow_sides, REACH, start, 2 * REACH)
-    half = [[0.5 * diffusivity[z, d] for z in range(3)] for d in range(2)]
+    half = [[0.5 * diffusivity[z : z + 1, d : d + 1] for z in range(3)] for d in range(2)]
 
     def one_row(row, before):
         labels, factor = zone_window[row], scale_window[row]
@@ -557,8 +563,8 @@
 
 
 def deep_weights(box, zone_window, scale_window, diffusivity, decay, to_deep, mass):
-    half = [0.5 * diffusivity[z, 2] for z in range(3)]
-    rates = [decay[z] for z in range(3)]
+    half = [0.5 * diffusivity[z : z + 1, 2:3] for z in range(3)]
+    rates = [decay[0:1, z : z + 1] for z in range(3)]
     lane = lax.broadcasted_iota(jnp.int32, (box.cols, box.deep), 1)
     ends = jnp.where((lane == 0) | (lane == box.deep - 1), jnp.float32(1.0), jnp.float32(0.0))
     not_last = jnp.where(lane == box.deep - 1, jnp.float32(0.0), jnp.float32(1.0))
@@ -582,7 +588,7 @@
 def image_sums(
     box, zone, scale, local, image, low, high, left, right, table, diffusivity, out, up, down
 ):
-    half = [[0.5 * diffusivity[z, d] for z in range(3)] for d in range(3)]
+    half = [[0.5 * diffusivity[z : z + 1, d : d + 1] for z in range(3)] for d in range(3)]
     shape = (box.long * box.across, box.deep)
     zone_flat, scale_flat, local_flat = zone.reshape(shape), scale.reshape(shape), local.reshape(shape)
     last_col = row_of(box.across, box.across - 1, box.long)
@@ -930,7 +936,7 @@
         copy.wait()
 
 
-def swaps(axis, around):
+def swaps(axis):
     sizes = (lax.axis_size("wide"), lax.axis_size("narrow"))
     along = ("wide", "narrow").index(axis)
     size, beside = sizes[along], sizes[1 - along]
@@ -946,8 +952,6 @@
             for other_place in range(beside):
                 partner = place + 1 if place % 2 == way else place - 1
                 there = other_place
-                if around and size % 2 == 0:
-                    partner %= size
                 if not 0 <= partner < size:
                     partner = place
                     there = other_place ^ 1 if beside % 2 == 0 else other_place
@@ -956,10 +960,15 @@
     return ways
 
 
-def exchange(axis, first, second, around=False):
-    ways = swaps(axis, around)
+def exchange(axis, first, second):
+    ways = swaps(axis)
     axes = ("wide", "narrow")
     return lax.ppermute(first, axes, ways[0]), lax.ppermute(second, axes, ways[1])
+
+
+def from_other_end(axis, table):
+    size = lax.axis_size(axis)
+    return lax.ppermute(table, axis, [(i, size - 1 - i) for i in range(size)])
 
 
 def two_away(axis, table):
@@ -982,6 +991,7 @@
     count = lax.axis_size("wide") * lax.axis_size("narrow")
     by_margins = lax.axis_size("wide") == 4 and lax.axis_size("narrow") == 4
     tables = tables_of(box)
+    decay = decay.reshape(1, -1)
     cells = f32(long, across, deep)
     whole_zone = jax.ShapeDtypeStruct(cells.shape, zone.dtype)
     window = f32(box.rows, box.cols, deep)
@@ -1009,12 +1019,19 @@
         )(*fields, *sides, *parts, *after)
 
     far = f32(2 * REACH, across, deep)
-    zone, scale, load, load_first, load_second, first, second = call(
+    far_zone, far_scale, far_load = pinned(zone), pinned(scale), pinned(load)
+    load_first, load_second, first, second = call(
         functools.partial(bring_edges, box),
-        (whole_zone, cells, cells) + (f32(MARGIN, across, deep),) * 2 + (far, far),
+        (f32(MARGIN, across, deep),) * 2 + (far, far),
         [in_hbm] * 3,
-        [pltpu.VMEM((2, REACH, across, deep), zone.dtype), pltpu.SemaphoreType.DMA((9,))],
-    )(pinned(zone), pinned(scale), pinned(load))
+        [pltpu.VMEM((2, REACH, across, deep), zone.dtype), pltpu.SemaphoreType.DMA((6,))],
+    )(far_zone, far_scale, far_load)
+    load, scale, zone = call(
+        bring_box,
+        (cells, cells, whole_zone),
+        [in_hbm] * 3 + [anywhere],
+        [pltpu.SemaphoreType.DMA((3,))],
+    )(far_load, far_scale, far_zone, load_first)
     load_wide = exchange("wide", load_first, load_second)
     far_wide = exchange("wide", first, second)
     load_first, load_second = pack(MARGIN, [load], load_wide)
@@ -1022,35 +1039,35 @@
     sums, table = call(
         functools.partial(box_sums, box),
         (f32(8, 128), table_shape),
-        [VMEM] * 3 + [anywhere] + [SMEM] * 2,
+        [VMEM] * 3 + [anywhere] + [VMEM] * 2,
     )(zone, scale, load, load_first, diffusivity, decay)
     far_narrow = exchange("narrow", *pack(REACH, [scale, zone], far_wide))
     load_window, local, image, inverses = call(
         functools.partial(first_solve, box),
         (window, cells, f32(across, deep), f32(box.ey, box.ex, deep)),
-        [VMEM] * 8 + [SMEM] * 2 + [VMEM] * N_TABLES,
+        [VMEM] * 8 + [VMEM] * 2 + [VMEM] * N_TABLES,
         [spectral, middle],
         flops=4 * 10**9,
     )(load, *load_wide, *load_narrow, sums, zone, scale, diffusivity, decay, *tables)
     message = f32(REACH * across + count, deep)
     table, first, second = call(
-        functools.partial(image_sums, box), (table_shape, message, message), [VMEM] * 9 + [SMEM]
+        functools.partial(image_sums, box), (table_shape, message, message), [VMEM] * 9 + [VMEM]
     )(zone, scale, local, image, *far_wide, *far_narrow, table, diffusivity)
     own_table = table
-    wide = exchange("wide", first, second, by_margins)
-    parts = (table, *wide)
+    wide = exchange("wide", first, second)
+    parts = (table, wide[0])
     if by_margins:
-        parts += (two_away("wide", table),)
+        parts += (two_away("wide", table), from_other_end("wide", table))
     to_long, to_across, *windows = call(
         functools.partial(side_weights, box),
         (window,) * 4,
-        [VMEM] * 6 + [SMEM],
+        [VMEM] * 6 + [VMEM],
         flops=10**9,
     )(zone, scale, *far_wide, *far_narrow, diffusivity)
     to_deep, mass = call(
         functools.partial(deep_weights, box),
         (window,) * 2,
-        [VMEM] * 2 + [SMEM] * 2,
+        [VMEM] * 2 + [VMEM] * 2,
         flops=10**9,
     )(*windows, diffusivity, decay)
     weights = (to_long, to_across, to_deep, mass)

time: 52.2 us -> 50.6 us (0.969)
  starting transfers between devices: 18.3 us -> 17.4 us
  waiting for transfers between devices: 7.14 us -> 6.44 us
    ppermute x2, waiting for transfers between devices: 5.18 us -> 1.38 us  [two_away(): return lax.ppermute(table, axis, [(i, (i + 2) % size) for i in range(size)])]
    ppermute x8, starting transfers between devices: 8.61 us -> 5.84 us  [exchange(): lax.ppermute(second, axes, ways[1])]
    ppermute x0 -> x1, waiting for transfers between devices: none -> 1.76 us  [from_other_end(): return lax.ppermute(table, axis, [(i, size - 1 - i) for i in range(size)])]
    ppermute x2, starting transfers between devices: 0.7 us -> 2.43 us  [two_away(): return lax.ppermute(table, axis, [(i, (i + 2) % size) for i in range(size)])]
    pallas_call x3 -> x4, Pallas kernels: 6.28 us -> 7.63 us  [the longest x1 2.36 us: on_device(): call(functools.partial(side_weights, box), (window,) * 4, [VMEM] * 6 + [V...]
    ppermute x0 -> x1, starting transfers between devices: none -> 1.19 us  [from_other_end(): return lax.ppermute(table, axis, [(i, size - 1 - i) for i in range(size)])]
    ppermute x8, starting transfers between devices: 9 us -> 7.99 us  [exchange(): lax.ppermute(first, axes, ways[0])]
    ppermute x8, waiting for transfers between devices: 1.93 us -> 2.68 us  [exchange(): lax.ppermute(first, axes, ways[0])]
  transfers between devices with their start and end apart: 18 -> 19, of which waited for: 5 -> 6; matrix products, arithmetic and copies ran while one was open for 0% -> 0% of each run, Pallas kernels for 28% -> 31%
where the time goes in v17:
time: 50.6 us; the launch traced here: 50.4 us
  Pallas kernels  25.4 us (50%)
  starting transfers between devices  17.4 us (34%)
  waiting for transfers between devices  6.44 us (13%)
  between operations  1.08 us (2%)
    ppermute x8, starting transfers between devices, exchange(): lax.ppermute(first, axes, ways[0])  7.99 us
    pallas_call x1, Pallas kernels, on_device(): call(functools.partial(second_solve, box), (cells, row, row, col, col, ce...  6.82 us
    ppermute x8, starting transfers between devices, exchange(): lax.ppermute(second, axes, ways[1])  5.84 us
    pallas_call x1, Pallas kernels, on_device(): call(functools.partial(first_solve, box), (window, cells, f32(across, dee...  5.2 us
    ppermute x8, waiting for transfers between devices, exchange(): lax.ppermute(first, axes, ways[0])  2.68 us
    ppermute x2, starting transfers between devices, two_away(): return lax.ppermute(table, axis, [(i, (i + 2) % size) for i in range(size)])  2.43 us
    pallas_call x1, Pallas kernels, on_device(): call(functools.partial(side_weights, box), (window,) * 4, [VMEM] * 6 + [V...  2.36 us
    pallas_call x1, Pallas kernels, on_device(): call(functools.partial(deep_weights, box), (window,) * 2, [VMEM] * 2 + [V...  2.25 us
  transfers between devices with their start and end apart: 19, of which 6 were waited for; matrix products, arithmetic and copies ran while one was open for 0% of the time, Pallas kernels for 31%

profile of v17, /device:TPU:0, one launch (start us, length us, event | category | flops | bytes accessed | tf_op | source)
XLA Modules:
  0.0 50.4 jit_solution(2992870511411082189)
XLA Ops:
  0.6 1.1 %shard_map.149 = (f32[4,32,128]{2,1,0:T(8,128)S(1)}, f32[4,32,128]{2,1,0:T(8,128)S(1)}, f32[10,32,128]{2,1,0:T(8,128)S(1)}, f32[10,32,128]{2,1,0:T(8,128)S(1)}) custom-call(s32[64,32,128]{2,1,0:T(8,128)} %zone.3, f32[64,32,128]{2,1,0:T(8,128)} %scale.3, f32[64,32,128]{2,1,0:T(8,128)} %load.3), custom_call_target="tpu_custom_call" | custom-call | tf_op jit(solution)/shard_map/pallas_call | solution.py:1023
  1.8 3.1 %collective-permute-start = (f32[4,32,128]{2,1,0:T(8,128)S(1)}, f32[4,32,128]{2,1,0:T(8,128)S(1)}, u32[]{:S(2)}, u32[]{:S(2)}) collective-permute-start(f32[4,32,128]{2,1,0:T(8,128)S(1)} %get-tuple-element.40.after), channel_id=1, source_target_pairs={{0,4},{1,5},{2,6},{3,7},{4,0},{5,1},{6,2},{7,3},{8,12},{9,13},{10,... | collective-permute-start | bytes 196616 | tf_op jit(solution)/shard_map/ppermute | solution.py:966
  4.9 3.1 %collective-permute-start.4 = (f32[10,32,128]{2,1,0:T(8,128)S(1)}, f32[10,32,128]{2,1,0:T(8,128)S(1)}, u32[]{:S(2)}, u32[]{:S(2)}) collective-permute-start(f32[10,32,128]{2,1,0:T(8,128)S(1)} %get-tuple-element.50), channel_id=1, source_target_pairs={{0,4},{1,5},{2,6},{3,7},{4,0},{5,1},{6,2},{7,3},{8,12},{9,13},{10,... | collective-permute-start | bytes 491528 | tf_op jit(solution)/shard_map/ppermute | solution.py:966
  8.0 1.9 %shard_map.150 = (f32[64,32,128]{2,1,0:T(8,128)S(1)}, f32[64,32,128]{2,1,0:T(8,128)S(1)}, s32[64,32,128]{2,1,0:T(8,128)S(1)}) custom-call(f32[64,32,128]{2,1,0:T(8,128)} %load.3, f32[64,32,128]{2,1,0:T(8,128)} %scale.3, s32[64,32,128]{2,1,0:T(8,128)} %zone.3, f32[4,32,128]{2,1,0:T(8,128)S(1)} %get-tuple-element.40.after), custom_call_target="tpu_custom_call" | custom-call | tf_op jit(solution)/shard_map/pallas_call | solution.py:1029
  10.0 0.2 shard_map.151
  10.1 0.6 %collective-permute-start.2 = (f32[296,128]{1,0:T(8,128)S(1)}, f32[296,128]{1,0:T(8,128)S(1)}, u32[]{:S(2)}, u32[]{:S(2)}) collective-permute-start(f32[296,128]{1,0:T(8,128)S(1)} %get-tuple-element.43.after), channel_id=1, source_target_pairs={{0,1},{4,5},{8,9},{12,13},{1,0},{5,4},{9,8},{13,12},{2,3},{6,7},{1... | collective-permute-start | bytes 454664 | tf_op jit(solution)/shard_map/ppermute | solution.py:966
  10.7 0.2 collective-permute-start.3
  10.9 0.7 %collective-permute-done.4.refs_2_.low = f32[10,32,128]{2,1,0:T(8,128)S(1)} collective-permute-done((f32[10,32,128]{2,1,0:T(8,128)S(1)}, f32[10,32,128]{2,1,0:T(8,128)S(1)}, u32[]{:S(2)}, u32[]{:S(2)}) %collective-permute-start.4) | collective-permute-done | bytes 163872 | tf_op jit(solution)/shard_map/ppermute | solution.py:966
  11.7 0.4 shard_map.154
  12.2 0.7 %collective-permute-start.6 = (f32[744,128]{1,0:T(8,128)S(1)}, f32[744,128]{1,0:T(8,128)S(1)}, u32[]{:S(2)}, u32[]{:S(2)}) collective-permute-start(f32[744,128]{1,0:T(8,128)S(1)} %get-tuple-element.52), channel_id=1, source_target_pairs={{0,1},{4,5},{8,9},{12,13},{1,0},{5,4},{9,8},{13,12},{2,3},{6,7},{1... | collective-permute-start | bytes 1142792 | tf_op jit(solution)/shard_map/ppermute | solution.py:966
  12.9 1.5 %collective-permute-start.7 = (f32[744,128]{1,0:T(8,128)S(1)}, f32[744,128]{1,0:T(8,128)S(1)}, u32[]{:S(2)}, u32[]{:S(2)}) collective-permute-start(f32[744,128]{1,0:T(8,128)S(1)} %get-tuple-element.53), channel_id=1, source_target_pairs={{0,4},{4,0},{8,12},{12,8},{1,2},{5,6},{9,10},{13,14},{2,1},{6,5},{... | collective-permute-start | bytes 1142792 | tf_op jit(solution)/shard_map/ppermute | solution.py:966
  14.5 0.8 %shard_map.152 = (f32[8,128]{1,0:T(8,128)S(1)}, f32[16,128]{1,0:T(8,128)S(1)}) custom-call(s32[64,32,128]{2,1,0:T(8,128)S(1)} %get-tuple-element.45.zone.refs_1_, f32[64,32,128]{2,1,0:T(8,128)S(1)} %get-tuple-element.46.scale.refs_0_, f32[64,32,128]{2,1,0:T(8,128)S(1)} %get-tuple-element.41.refs_0_.load, f32[296,128]{1,0:T(8,128)S(1)} %get-tuple-element.43.after, ...), custom_call_target="tpu_custom_call" | custom-call | tf_op jit(solution)/shard_map/pallas_call | solution.py:1039
  15.3 0.6 %collective-permute-done.3.right = f32[296,128]{1,0:T(8,128)S(1)} collective-permute-done((f32[296,128]{1,0:T(8,128)S(1)}, f32[296,128]{1,0:T(8,128)S(1)}, u32[]{:S(2)}, u32[]{:S(2)}) %collective-permute-start.3) | collective-permute-done | bytes 151584 | tf_op jit(solution)/shard_map/ppermute | solution.py:966
  16.0 5.2 %shard_map.153 = (f32[74,48,128]{2,1,0:T(8,128)S(1)}, f32[64,32,128]{2,1,0:T(8,128)S(1)}, f32[32,128]{1,0:T(8,128)S(1)}, f32[40,72,128]{2,1,0:T(8,128)S(1)}) custom-call(f32[64,32,128]{2,1,0:T(8,128)S(1)} %get-tuple-element.41.refs_0_.load, f32[4,32,128]{2,1,0:T(8,128)S(1)} %collective-permute-done.refs_1_.low, ...), custom_call_target="tpu_custom_call" | custom-call | flops 4000000000 | tf_op jit(solution)/shard_map/pallas_call | solution.py:1045
  21.2 0.4 shard_map.155
  21.6 2.1 %collective-permute-start.10 = (f32[16,128]{1,0:T(8,128)S(1)}, f32[16,128]{1,0:T(8,128)S(1)}, u32[]{:S(2)}, u32[]{:S(2)}) collective-permute-start(f32[16,128]{1,0:T(8,128)S(1)} %get-tuple-element.57.refs_3_), channel_id=1, source_target_pairs={{0,8},{4,12},{8,0},{12,4},{1,9},{5,13},{9,1},{13,5},{2,10},{6,14},... | collective-permute-start | bytes 24584 | tf_op jit(solution)/shard_map/ppermute | solution.py:976
  23.7 1.2 %collective-permute-start.11 = (f32[16,128]{1,0:T(8,128)S(1)}, f32[16,128]{1,0:T(8,128)S(1)}, u32[]{:S(2)}, u32[]{:S(2)}) collective-permute-start(f32[16,128]{1,0:T(8,128)S(1)} %get-tuple-element.57.refs_3_), channel_id=1, source_target_pairs={{0,12},{4,8},{8,4},{12,0},{1,13},{5,9},{9,5},{13,1},{2,14},{6,10},... | collective-permute-start | bytes 24584 | tf_op jit(solution)/shard_map/ppermute | solution.py:971
  24.9 0.2 collective-permute-start.8
  25.1 2.4 %shard_map.156 = (f32[74,48,128]{2,1,0:T(8,128)S(1)}, f32[74,48,128]{2,1,0:T(8,128)S(1)}, f32[74,48,128]{2,1,0:T(8,128)S(1)}, f32[74,48,128]{2,1,0:T(8,128)S(1)}) custom-call(s32[64,32,128]{2,1,0:T(8,128)S(1)} %get-tuple-element.45.zone.refs_1_, f32[64,32,128]{2,1,0:T(8,128)S(1)} %get-tuple-element.46.scale.refs_0_, ...), custom_call_target="tpu_custom_call" | custom-call | flops 1000000000 | tf_op jit(solution)/shard_map/pallas_call | solution.py:1061
  27.5 1.8 %collective-permute-done.11.refs_6_ = f32[16,128]{1,0:T(8,128)S(1)} collective-permute-done((f32[16,128]{1,0:T(8,128)S(1)}, f32[16,128]{1,0:T(8,128)S(1)}, u32[]{:S(2)}, u32[]{:S(2)}) %collective-permute-start.11) | collective-permute-done | bytes 8224 | tf_op jit(solution)/shard_map/ppermute | solution.py:971
  29.2 0.2 collective-permute-done.8.refs_1_.refs_4_.low
  29.5 0.2 shard_map.157
  29.8 2.0 %collective-permute-start.13 = (f32[392,128]{1,0:T(8,128)S(1)}, f32[392,128]{1,0:T(8,128)S(1)}, u32[]{:S(2)}, u32[]{:S(2)}) collective-permute-start(f32[392,128]{1,0:T(8,128)S(1)} %get-tuple-element.60), channel_id=1, source_target_pairs={{0,4},{4,0},{8,12},{12,8},{1,2},{5,6},{9,10},{13,14},{2,1},{6,5},{... | collective-permute-start | bytes 602120 | tf_op jit(solution)/shard_map/ppermute | solution.py:966
  31.8 0.3 collective-permute-start.14
  32.1 2.2 %shard_map.160 = (f32[74,48,128]{2,1,0:T(8,128)S(1)}, f32[74,48,128]{2,1,0:T(8,128)S(1)}) custom-call(f32[74,48,128]{2,1,0:T(8,128)S(1)} %get-tuple-element.64.zone_window, f32[74,48,128]{2,1,0:T(8,128)S(1)} %get-tuple-element.65.scale_window, f32[3,3]{1,0:T(4,128)S(1)} %copy-done, f32[1,3]{1,0:T(1,128)S(1)} %bitcast.3), custom_call_target="tpu_custom_call" | custom-call | flops 1000000000 | tf_op jit(solution)/shard_map/pallas_call | solution.py:1067
  34.4 1.4 %collective-permute-done.14.refs_1_ = f32[16,128]{1,0:T(8,128)S(1)} collective-permute-done((f32[16,128]{1,0:T(8,128)S(1)}, f32[16,128]{1,0:T(8,128)S(1)}, u32[]{:S(2)}, u32[]{:S(2)}) %collective-permute-start.14) | collective-permute-done | bytes 8224 | tf_op jit(solution)/shard_map/ppermute | solution.py:976
  35.8 0.9 %shard_map.159.answers = f32[8,128]{1,0:T(8,128)S(1)} custom-call(f32[16,128]{1,0:T(8,128)S(1)} %shard_map.158.refs_0_, f32[16,128]{1,0:T(8,128)S(1)} %collective-permute-done.14.refs_1_), custom_call_target="tpu_custom_call" | custom-call | tf_op jit(solution)/shard_map/pallas_call | solution.py:1082
  36.7 6.8 %shard_map.161 = (f32[64,32,128]{2,1,0:T(8,128)S(1)}, f32[32,128]{1,0:T(8,128)S(1)}, f32[32,128]{1,0:T(8,128)S(1)}, f32[64,128]{1,0:T(8,128)S(1)}, f32[64,128]{1,0:T(8,128)S(1)}, /*index=5*/f32[64,32,128]{2,1,0:T(8,128)}) custom-call(f32[64,32,128]{2,1,0:T(8,128)S(1)} %get-tuple-element.48.local.refs_0_, ...), custom_call_target="tpu_custom_call" | custom-call | flops 4000000000 | tf_op jit(solution)/shard_map/pallas_call | solution.py:1088
  43.6 2.0 %collective-permute-start.18 = (f32[64,128]{1,0:T(8,128)S(1)}, f32[64,128]{1,0:T(8,128)S(1)}, u32[]{:S(2)}, u32[]{:S(2)}) collective-permute-start(f32[64,128]{1,0:T(8,128)S(1)} %get-tuple-element.74), channel_id=1, source_target_pairs={{0,4},{4,0},{8,12},{12,8},{1,2},{5,6},{9,10},{13,14},{2,1},{6,5},{... | collective-permute-start | bytes 98312 | tf_op jit(solution)/shard_map/ppermute | solution.py:966
  45.7 1.9 %shard_map.162 = (f32[2,32,128]{2,1,0:T(8,128)S(1)}, f32[2,64,8,128]{3,2,1,0:T(8,128)S(1)}, f32[64,32,128]{2,1,0:T(8,128)}) custom-call(f32[64,32,128]{2,1,0:T(8,128)S(1)} %get-tuple-element.41.refs_0_.load, f32[64,32,128]{2,1,0:T(8,128)S(1)} %get-tuple-element.70.iterate, f32[74,48,128]{2,1,0:T(8,128)S(1)} %get-tuple-element.58.refs_7_.rest_0_.to_long, ...), custom_call_target="tpu_custom_call" | custom-call | flops 1000000000 | tf_op jit(solution)/shard_map/pallas_call | solution.py:1098
  47.6 1.7 %collective-permute-done.15.low = f32[32,128]{1,0:T(8,128)S(1)} collective-permute-done((f32[32,128]{1,0:T(8,128)S(1)}, f32[32,128]{1,0:T(8,128)S(1)}, u32[]{:S(2)}, u32[]{:S(2)}) %collective-permute-start.15) | collective-permute-done | bytes 16416 | tf_op jit(solution)/shard_map/ppermute | solution.py:966
  49.3 0.9 %shard_map.163 = f32[64,32,128]{2,1,0:T(8,128)} custom-call(f32[64,32,128]{2,1,0:T(8,128)S(1)} %get-tuple-element.70.iterate, f32[32,128]{1,0:T(8,128)S(1)} %collective-permute-done.15.low, f32[32,128]{1,0:T(8,128)S(1)} %collective-permute-done.16.high, f32[64,128]{1,0:T(8,128)S(1)} %collective-permute-done.17.left, ...), custom_call_target="tpu_custom_call", output_to_operand_aliasing={{}: (9, {})} | custom-call | tf_op jit(solution)/shard_map/pallas_call | solution.py:1110
  (43 shorter events, 0.4 us)
Async XLA Ops:
  1.8 8.2 %collective-permute-start = (f32[4,32,128]{2,1,0:T(8,128)S(1)}, f32[4,32,128]{2,1,0:T(8,128)S(1)}, u32[]{:S(2)}, u32[]{:S(2)}) collective-permute-start(f32[4,32,128]{2,1,0:T(8,128)S(1)} %get-tuple-element.40.after), channel_id=1, source_target_pairs={{0,4},{1,5},{2,6},{3,7},{4,0},{5,1},{6,2},{7,3},{8,12},{9,13},{10,... | collective-permute-start | bytes 196616 | tf_op jit(solution)/shard_map/ppermute | solution.py:966
  4.9 5.1 %collective-permute-start.1 = (f32[4,32,128]{2,1,0:T(8,128)S(1)}, f32[4,32,128]{2,1,0:T(8,128)S(1)}, u32[]{:S(2)}, u32[]{:S(2)}) collective-permute-start(f32[4,32,128]{2,1,0:T(8,128)S(1)} %get-tuple-element.42), channel_id=1, source_target_pairs={{0,1},{1,0},{2,3},{3,2},{4,8},{5,9},{6,10},{7,11},{8,4},{9,5},{10,... | collective-permute-start | bytes 196616 | tf_op jit(solution)/shard_map/ppermute | solution.py:966
  4.9 6.8 %collective-permute-start.4 = (f32[10,32,128]{2,1,0:T(8,128)S(1)}, f32[10,32,128]{2,1,0:T(8,128)S(1)}, u32[]{:S(2)}, u32[]{:S(2)}) collective-permute-start(f32[10,32,128]{2,1,0:T(8,128)S(1)} %get-tuple-element.50), channel_id=1, source_target_pairs={{0,4},{1,5},{2,6},{3,7},{4,0},{5,1},{6,2},{7,3},{8,12},{9,13},{10,... | collective-permute-start | bytes 491528 | tf_op jit(solution)/shard_map/ppermute | solution.py:966
  8.0 3.6 %collective-permute-start.5 = (f32[10,32,128]{2,1,0:T(8,128)S(1)}, f32[10,32,128]{2,1,0:T(8,128)S(1)}, u32[]{:S(2)}, u32[]{:S(2)}) collective-permute-start(f32[10,32,128]{2,1,0:T(8,128)S(1)} %get-tuple-element.51), channel_id=1, source_target_pairs={{0,1},{1,0},{2,3},{3,2},{4,8},{5,9},{6,10},{7,11},{8,4},{9,5},{10,... | collective-permute-start | bytes 491528 | tf_op jit(solution)/shard_map/ppermute | solution.py:966
  9.9 4.6 %copy-start = (f32[3,3]{1,0:T(4,128)S(1)}, f32[3,3]{1,0:T(4,128)}, u32[]{:S(2)}) copy-start(f32[3,3]{1,0:T(4,128)} %diffusivity.9) | copy-start | bytes 112
  9.9 4.5 %copy-start.1 = (f32[3]{0:T(128)S(1)}, f32[3]{0:T(128)}, u32[]{:S(2)}) copy-start(f32[3]{0:T(128)} %param.17) | copy-start | bytes 40
  10.1 5.2 %collective-permute-start.2 = (f32[296,128]{1,0:T(8,128)S(1)}, f32[296,128]{1,0:T(8,128)S(1)}, u32[]{:S(2)}, u32[]{:S(2)}) collective-permute-start(f32[296,128]{1,0:T(8,128)S(1)} %get-tuple-element.43.after), channel_id=1, source_target_pairs={{0,1},{4,5},{8,9},{12,13},{1,0},{5,4},{9,8},{13,12},{2,3},{6,7},{1... | collective-permute-start | bytes 454664 | tf_op jit(solution)/shard_map/ppermute | solution.py:966
  10.7 5.2 %collective-permute-start.3 = (f32[296,128]{1,0:T(8,128)S(1)}, f32[296,128]{1,0:T(8,128)S(1)}, u32[]{:S(2)}, u32[]{:S(2)}) collective-permute-start(f32[296,128]{1,0:T(8,128)S(1)} %get-tuple-element.44), channel_id=1, source_target_pairs={{0,4},{4,0},{8,12},{12,8},{1,2},{5,6},{9,10},{13,14},{2,1},{6,5},{... | collective-permute-start | bytes 454664 | tf_op jit(solution)/shard_map/ppermute | solution.py:966
  12.1 3.8 %copy-start.2 = (f32[256,256]{1,0:T(8,128)S(1)}, f32[256,256]{1,0:T(8,128)}, u32[]{:S(2)}) copy-start(f32[256,256]{1,0:T(8,128)} %constant.22.clone.rest_4_.rest_9_) | copy-start | bytes 786436
  12.1 3.8 %copy-start.3 = (f32[192,216]{1,0:T(8,128)S(1)}, f32[192,216]{1,0:T(8,128)}, u32[]{:S(2)}) copy-start(f32[192,216]{1,0:T(8,128)} %constant.20.clone.rest_2_.rest_7_) | copy-start | bytes 497668
  12.1 3.8 %copy-start.4 = (f32[144,144]{1,0:T(8,128)S(1)}, f32[144,144]{1,0:T(8,128)}, u32[]{:S(2)}) copy-start(f32[144,144]{1,0:T(8,128)} %constant.19.clone.rest_1_.rest_6_) | copy-start | bytes 248836
  12.1 3.8 %copy-start.5 = (f32[256,128]{1,0:T(8,128)S(1)}, f32[256,128]{1,0:T(8,128)}, u32[]{:S(2)}) copy-start(f32[256,128]{1,0:T(8,128)} %constant.23.clone.rest_5_.rest_10_) | copy-start | bytes 393220
  12.1 3.8 %copy-start.6 = (f32[96,120]{1,0:T(8,128)S(1)}, f32[96,120]{1,0:T(8,128)}, u32[]{:S(2)}) copy-start(f32[96,120]{1,0:T(8,128)} %constant.21.clone.rest_3_.rest_8_) | copy-start | bytes 138244
  12.2 3.8 %copy-start.7 = (f32[80,80]{1,0:T(8,128)S(1)}, f32[80,80]{1,0:T(8,128)}, u32[]{:S(2)}) copy-start(f32[80,80]{1,0:T(8,128)} %constant.18.clone.rest_0_.rest_5_) | copy-start | bytes 76804
  12.2 3.8 %copy-start.8 = (f32[72,128]{1,0:T(8,128)S(1)}, f32[72,128]{1,0:T(8,128)}, u32[]{:S(2)}) copy-start(f32[72,128]{1,0:T(8,128)} %constant.24.clone.rest_6_.rest_11_) | copy-start | bytes 110596
  12.2 3.8 %copy-start.9 = (f32[40,128]{1,0:T(8,128)S(1)}, f32[40,128]{1,0:T(8,128)}, u32[]{:S(2)}) copy-start(f32[40,128]{1,0:T(8,128)} %constant.25.clone.rest_7_.rest_12_) | copy-start | bytes 61444
  12.2 3.8 %copy-start.10 = (f32[1,128]{1,0:T(1,128)S(1)}, f32[1,128]{1,0:T(1,128)}, u32[]{:S(2)}) copy-start(f32[1,128]{1,0:T(1,128)} %constant.26.clone.rest_8_.rest_13_) | copy-start | bytes 1540
  12.2 9.0 %collective-permute-start.6 = (f32[744,128]{1,0:T(8,128)S(1)}, f32[744,128]{1,0:T(8,128)S(1)}, u32[]{:S(2)}, u32[]{:S(2)}) collective-permute-start(f32[744,128]{1,0:T(8,128)S(1)} %get-tuple-element.52), channel_id=1, source_target_pairs={{0,1},{4,5},{8,9},{12,13},{1,0},{5,4},{9,8},{13,12},{2,3},{6,7},{1... | collective-permute-start | bytes 1142792 | tf_op jit(solution)/shard_map/ppermute | solution.py:966
  12.9 8.3 %collective-permute-start.7 = (f32[744,128]{1,0:T(8,128)S(1)}, f32[744,128]{1,0:T(8,128)S(1)}, u32[]{:S(2)}, u32[]{:S(2)}) collective-permute-start(f32[744,128]{1,0:T(8,128)S(1)} %get-tuple-element.53), channel_id=1, source_target_pairs={{0,4},{4,0},{8,12},{12,8},{1,2},{5,6},{9,10},{13,14},{2,1},{6,5},{... | collective-permute-start | bytes 1142792 | tf_op jit(solution)/shard_map/ppermute | solution.py:966
  21.6 5.9 %collective-permute-start.10 = (f32[16,128]{1,0:T(8,128)S(1)}, f32[16,128]{1,0:T(8,128)S(1)}, u32[]{:S(2)}, u32[]{:S(2)}) collective-permute-start(f32[16,128]{1,0:T(8,128)S(1)} %get-tuple-element.57.refs_3_), channel_id=1, source_target_pairs={{0,8},{4,12},{8,0},{12,4},{1,9},{5,13},{9,1},{13,5},{2,10},{6,14},... | collective-permute-start | bytes 24584 | tf_op jit(solution)/shard_map/ppermute | solution.py:976
  23.7 5.6 %collective-permute-start.11 = (f32[16,128]{1,0:T(8,128)S(1)}, f32[16,128]{1,0:T(8,128)S(1)}, u32[]{:S(2)}, u32[]{:S(2)}) collective-permute-start(f32[16,128]{1,0:T(8,128)S(1)} %get-tuple-element.57.refs_3_), channel_id=1, source_target_pairs={{0,12},{4,8},{8,4},{12,0},{1,13},{5,9},{9,5},{13,1},{2,14},{6,10},... | collective-permute-start | bytes 24584 | tf_op jit(solution)/shard_map/ppermute | solution.py:971
  24.9 4.6 %collective-permute-start.8 = (f32[176,128]{1,0:T(8,128)S(1)}, f32[176,128]{1,0:T(8,128)S(1)}, u32[]{:S(2)}, u32[]{:S(2)}) collective-permute-start(f32[176,128]{1,0:T(8,128)S(1)} %get-tuple-element.55), channel_id=1, source_target_pairs={{0,4},{1,5},{2,6},{3,7},{4,0},{5,1},{6,2},{7,3},{8,12},{9,13},{10,... | collective-permute-start | bytes 270344 | tf_op jit(solution)/shard_map/ppermute | solution.py:966
  25.1 4.4 %collective-permute-start.9 = (f32[176,128]{1,0:T(8,128)S(1)}, f32[176,128]{1,0:T(8,128)S(1)}, u32[]{:S(2)}, u32[]{:S(2)}) collective-permute-start(f32[176,128]{1,0:T(8,128)S(1)} %get-tuple-element.56), channel_id=1, source_target_pairs={{0,1},{1,0},{2,3},{3,2},{4,8},{5,9},{6,10},{7,11},{8,4},{9,5},{10,... | collective-permute-start | bytes 270344 | tf_op jit(solution)/shard_map/ppermute | solution.py:966
  29.7 2.1 %collective-permute-start.12 = (f32[392,128]{1,0:T(8,128)S(1)}, f32[392,128]{1,0:T(8,128)S(1)}, u32[]{:S(2)}, u32[]{:S(2)}) collective-permute-start(f32[392,128]{1,0:T(8,128)S(1)} %get-tuple-element.59), channel_id=1, source_target_pairs={{0,1},{4,5},{8,9},{12,13},{1,0},{5,4},{9,8},{13,12},{2,3},{6,7},{1... | collective-permute-start | bytes 602120 | tf_op jit(solution)/shard_map/ppermute | solution.py:966
  29.8 6.9 %collective-permute-start.13 = (f32[392,128]{1,0:T(8,128)S(1)}, f32[392,128]{1,0:T(8,128)S(1)}, u32[]{:S(2)}, u32[]{:S(2)}) collective-permute-start(f32[392,128]{1,0:T(8,128)S(1)} %get-tuple-element.60), channel_id=1, source_target_pairs={{0,4},{4,0},{8,12},{12,8},{1,2},{5,6},{9,10},{13,14},{2,1},{6,5},{... | collective-permute-start | bytes 602120 | tf_op jit(solution)/shard_map/ppermute | solution.py:966
  31.8 4.0 %collective-permute-start.14 = (f32[16,128]{1,0:T(8,128)S(1)}, f32[16,128]{1,0:T(8,128)S(1)}, u32[]{:S(2)}, u32[]{:S(2)}) collective-permute-start(f32[16,128]{1,0:T(8,128)S(1)} %shard_map.158.refs_0_), channel_id=1, source_target_pairs={{0,2},{1,3},{2,0},{3,1},{4,6},{5,7},{6,4},{7,5},{8,10},{9,11},{10,... | collective-permute-start | bytes 24584 | tf_op jit(solution)/shard_map/ppermute | solution.py:976
  43.5 5.8 %collective-permute-start.17 = (f32[64,128]{1,0:T(8,128)S(1)}, f32[64,128]{1,0:T(8,128)S(1)}, u32[]{:S(2)}, u32[]{:S(2)}) collective-permute-start(f32[64,128]{1,0:T(8,128)S(1)} %get-tuple-element.73), channel_id=1, source_target_pairs={{0,1},{4,5},{8,9},{12,13},{1,0},{5,4},{9,8},{13,12},{2,3},{6,7},{1... | collective-permute-start | bytes 98312 | tf_op jit(solution)/shard_map/ppermute | solution.py:966
  43.6 5.8 %collective-permute-start.18 = (f32[64,128]{1,0:T(8,128)S(1)}, f32[64,128]{1,0:T(8,128)S(1)}, u32[]{:S(2)}, u32[]{:S(2)}) collective-permute-start(f32[64,128]{1,0:T(8,128)S(1)} %get-tuple-element.74), channel_id=1, source_target_pairs={{0,4},{4,0},{8,12},{12,8},{1,2},{5,6},{9,10},{13,14},{2,1},{6,5},{... | collective-permute-start | bytes 98312 | tf_op jit(solution)/shard_map/ppermute | solution.py:966
  45.6 3.7 %collective-permute-start.15 = (f32[32,128]{1,0:T(8,128)S(1)}, f32[32,128]{1,0:T(8,128)S(1)}, u32[]{:S(2)}, u32[]{:S(2)}) collective-permute-start(f32[32,128]{1,0:T(8,128)S(1)} %get-tuple-element.71), channel_id=1, source_target_pairs={{0,4},{1,5},{2,6},{3,7},{4,0},{5,1},{6,2},{7,3},{8,12},{9,13},{10,... | collective-permute-start | bytes 49160 | tf_op jit(solution)/shard_map/ppermute | solution.py:966
  45.7 3.7 %collective-permute-start.16 = (f32[32,128]{1,0:T(8,128)S(1)}, f32[32,128]{1,0:T(8,128)S(1)}, u32[]{:S(2)}, u32[]{:S(2)}) collective-permute-start(f32[32,128]{1,0:T(8,128)S(1)} %get-tuple-element.72), channel_id=1, source_target_pairs={{0,1},{1,0},{2,3},{3,2},{4,8},{5,9},{6,10},{7,11},{8,4},{9,5},{10,... | collective-permute-start | bytes 49160 | tf_op jit(solution)/shard_map/ppermute | solution.py:966

commit v18 on v17

--- a/solution.py
+++ b/solution.py
@@ -168,7 +168,11 @@
     return jnp.concatenate([values, blank], axis=0)
 
 
-ABREAST = 8
+FORWARD_ROWS, COLS_ABREAST, BACKWARD_ROWS = 24, 40, 32
+
+
+def fitting(size, wanted):
+    return max(part for part in range(8, wanted + 1, 8) if size % part == 0)
 
 
 def beside(values):
@@ -196,28 +200,30 @@
         spectral[:, box.ex :, :] = jnp.zeros((box.ey, deep_x - box.ex, deep), jnp.float32)
     if deep_y > box.ey:
         middle[:, box.ey :, :] = jnp.zeros((box.long, deep_y - box.ey, deep), jnp.float32)
-    for start in range(0, box.ex, 8):
-        block = source(start).reshape(8 * box.ey, deep)
-        block = dot_right(block, main_z, rest_z, FORWARD).reshape(8, box.ey, deep)
-        for row in range(0, 8, ABREAST):
-            wide = beside([block[row + part] for part in range(ABREAST)])
-            wide = dot_left(into_y, with_rows(wide, deep_y), FORWARD, box.ey)
-            for part, values in enumerate(apart(wide, deep)):
-                place = pl.ds(start + row + part, box.ey, stride=deep_x)
-                spectral_flat[place, :] = values
-    for col in range(0, box.ey, ABREAST):
-        wide = beside([spectral[col + part] for part in range(ABREAST)])
+    step = fitting(box.ex, FORWARD_ROWS)
+    for start in range(0, box.ex, step):
+        block = jnp.concatenate([source(row) for row in range(start, start + step, 8)], axis=0)
+        block = dot_right(block.reshape(step * box.ey, deep), main_z, rest_z, FORWARD)
+        block = block.reshape(step, box.ey, deep)
+        wide = beside([block[row] for row in range(step)])
+        wide = dot_left(into_y, with_rows(wide, deep_y), FORWARD, box.ey)
+        for row, values in enumerate(apart(wide, deep)):
+            spectral_flat[pl.ds(start + row, box.ey, stride=deep_x), :] = values
+    step = fitting(box.ey, COLS_ABREAST)
+    for start in range(0, box.ey, step):
+        wide = beside([spectral[col] for col in range(start, start + step)])
         wide = apart(dot_left(into_x, wide, FORWARD, box.ex), deep)
-        wide = beside([divided(values, col + part) for part, values in enumerate(wide)])
+        wide = beside([divided(values, start + part) for part, values in enumerate(wide)])
         wide = dot_left(from_x, with_rows(wide, deep_x), BACKWARD, box.long)
         for part, values in enumerate(apart(wide, deep)):
-            middle_flat[pl.ds(col + part, box.long, stride=deep_y), :] = values
-    for start in range(0, box.long, 8):
-        parts = []
-        for row in range(start, start + 8, ABREAST):
-            wide = beside([middle[row + part] for part in range(ABREAST)])
-            parts += apart(dot_left(from_y, wide, BACKWARD, box.across), deep)
-        emit(start, dot_right(jnp.concatenate(parts, axis=0), main_z, rest_z, BACKWARD))
+            middle_flat[pl.ds(start + part, box.long, stride=deep_y), :] = values
+    step = fitting(box.long, BACKWARD_ROWS)
+    for start in range(0, box.long, step):
+        wide = beside([middle[row] for row in range(start, start + step)])
+        parts = apart(dot_left(from_y, wide, BACKWARD, box.across), deep)
+        values = dot_right(jnp.concatenate(parts, axis=0), main_z, rest_z, BACKWARD)
+        for row in range(0, step, 8):
+            emit(start + row, values[row * box.across : (row + 8) * box.across])
 
 
 def position():
@@ -328,13 +334,16 @@
 
 def bring_box(load, scale, zone, after, own_load, own_scale, own_zone, sems):
     del after
-    pairs = ((load, own_load), (scale, own_scale), (zone, own_zone))
-    copies = [
-        pltpu.make_async_copy(source, target, sems.at[index])
-        for index, (source, target) in enumerate(pairs)
-    ]
-    for copy in copies:
-        copy.start()
+    parts = 4
+    size = own_load.shape[0] // parts
+    copies = []
+    for part in range(parts):
+        rows = slice(part * size, (part + 1) * size)
+        for source, target in ((load, own_load), (scale, own_scale), (zone, own_zone)):
+            copies.append(
+                pltpu.make_async_copy(source.at[rows], target.at[rows], sems.at[len(copies)])
+            )
+            copies[-1].start()
     for copy in copies:
         copy.wait()
 
@@ -1030,7 +1039,7 @@
         bring_box,
         (cells, cells, whole_zone),
         [in_hbm] * 3 + [anywhere],
-        [pltpu.SemaphoreType.DMA((3,))],
+        [pltpu.SemaphoreType.DMA((12,))],
     )(far_load, far_scale, far_zone, load_first)
     load_wide = exchange("wide", load_first, load_second)
     far_wide = exchange("wide", first, second)

time: 50.6 us -> 49.3 us (0.974)
  Pallas kernels: 25.4 us -> 23.1 us
  waiting for transfers between devices: 6.44 us -> 7.17 us
    pallas_call x1, Pallas kernels: 6.82 us -> 5.57 us  [on_device(): call(functools.partial(second_solve, box), (cells, row, row, col, col, ce...]
    pallas_call x1, Pallas kernels: 5.2 us -> 4.12 us  [on_device(): call(functools.partial(first_solve, box), (window, cells, f32(across, dee...]
    ppermute x2, starting transfers between devices: 2.43 us -> 3 us  [two_away(): return lax.ppermute(table, axis, [(i, (i + 2) % size) for i in range(size)])]
    ppermute x8, waiting for transfers between devices: 0.61 us -> 1.13 us  [exchange(): lax.ppermute(second, axes, ways[1])]
  transfers between devices with their start and end apart: 19 -> 19, of which waited for: 6 -> 7; matrix products, arithmetic and copies ran while one was open for 0% -> 0% of each run, Pallas kernels for 31% -> 30%
where the time goes in v18:
time: 49.3 us; the launch traced here: 49.2 us
  Pallas kernels  23.1 us (47%)
  starting transfers between devices  17.8 us (36%)
  waiting for transfers between devices  7.17 us (15%)
  between operations  1.07 us (2%)
    ppermute x8, starting transfers between devices, exchange(): lax.ppermute(first, axes, ways[0])  7.81 us
    ppermute x8, starting transfers between devices, exchange(): lax.ppermute(second, axes, ways[1])  5.77 us
    pallas_call x1, Pallas kernels, on_device(): call(functools.partial(second_solve, box), (cells, row, row, col, col, ce...  5.57 us
    pallas_call x1, Pallas kernels, on_device(): call(functools.partial(first_solve, box), (window, cells, f32(across, dee...  4.12 us
    ppermute x2, starting transfers between devices, two_away(): return lax.ppermute(table, axis, [(i, (i + 2) % size) for i in range(size)])  3 us
    ppermute x8, waiting for transfers between devices, exchange(): lax.ppermute(first, axes, ways[0])  2.69 us
    pallas_call x1, Pallas kernels, on_device(): call(functools.partial(side_weights, box), (window,) * 4, [VMEM] * 6 + [V...  2.36 us
    pallas_call x1, Pallas kernels, on_device(): call(functools.partial(deep_weights, box), (window,) * 2, [VMEM] * 2 + [V...  2.25 us
  transfers between devices with their start and end apart: 19, of which 7 were waited for; matrix products, arithmetic and copies ran while one was open for 0% of the time, Pallas kernels for 30%

profile of v18, /device:TPU:0, one launch (start us, length us, event | category | flops | bytes accessed | tf_op | source)
XLA Modules:
  0.0 49.2 jit_solution(775800857879821295)
XLA Ops:
  0.6 1.1 %shard_map.149 = (f32[4,32,128]{2,1,0:T(8,128)S(1)}, f32[4,32,128]{2,1,0:T(8,128)S(1)}, f32[10,32,128]{2,1,0:T(8,128)S(1)}, f32[10,32,128]{2,1,0:T(8,128)S(1)}) custom-call(s32[64,32,128]{2,1,0:T(8,128)} %zone.3, f32[64,32,128]{2,1,0:T(8,128)} %scale.3, f32[64,32,128]{2,1,0:T(8,128)} %load.3), custom_call_target="tpu_custom_call" | custom-call | tf_op jit(solution)/shard_map/pallas_call | solution.py:1032
  1.8 3.1 %collective-permute-start = (f32[4,32,128]{2,1,0:T(8,128)S(1)}, f32[4,32,128]{2,1,0:T(8,128)S(1)}, u32[]{:S(2)}, u32[]{:S(2)}) collective-permute-start(f32[4,32,128]{2,1,0:T(8,128)S(1)} %get-tuple-element.40.after), channel_id=1, source_target_pairs={{0,4},{1,5},{2,6},{3,7},{4,0},{5,1},{6,2},{7,3},{8,12},{9,13},{10,... | collective-permute-start | bytes 196616 | tf_op jit(solution)/shard_map/ppermute | solution.py:975
  4.9 3.1 %collective-permute-start.4 = (f32[10,32,128]{2,1,0:T(8,128)S(1)}, f32[10,32,128]{2,1,0:T(8,128)S(1)}, u32[]{:S(2)}, u32[]{:S(2)}) collective-permute-start(f32[10,32,128]{2,1,0:T(8,128)S(1)} %get-tuple-element.50), channel_id=1, source_target_pairs={{0,4},{1,5},{2,6},{3,7},{4,0},{5,1},{6,2},{7,3},{8,12},{9,13},{10,... | collective-permute-start | bytes 491528 | tf_op jit(solution)/shard_map/ppermute | solution.py:975
  8.0 1.9 %shard_map.150 = (f32[64,32,128]{2,1,0:T(8,128)S(1)}, f32[64,32,128]{2,1,0:T(8,128)S(1)}, s32[64,32,128]{2,1,0:T(8,128)S(1)}) custom-call(f32[64,32,128]{2,1,0:T(8,128)} %load.3, f32[64,32,128]{2,1,0:T(8,128)} %scale.3, s32[64,32,128]{2,1,0:T(8,128)} %zone.3, f32[4,32,128]{2,1,0:T(8,128)S(1)} %get-tuple-element.40.after), custom_call_target="tpu_custom_call" | custom-call | tf_op jit(solution)/shard_map/pallas_call | solution.py:1038
  10.0 0.2 shard_map.151
  10.2 0.6 %collective-permute-start.2 = (f32[296,128]{1,0:T(8,128)S(1)}, f32[296,128]{1,0:T(8,128)S(1)}, u32[]{:S(2)}, u32[]{:S(2)}) collective-permute-start(f32[296,128]{1,0:T(8,128)S(1)} %get-tuple-element.43.after), channel_id=1, source_target_pairs={{0,1},{4,5},{8,9},{12,13},{1,0},{5,4},{9,8},{13,12},{2,3},{6,7},{1... | collective-permute-start | bytes 454664 | tf_op jit(solution)/shard_map/ppermute | solution.py:975
  10.7 0.2 collective-permute-start.3
  10.9 0.7 %collective-permute-done.4.refs_2_.low = f32[10,32,128]{2,1,0:T(8,128)S(1)} collective-permute-done((f32[10,32,128]{2,1,0:T(8,128)S(1)}, f32[10,32,128]{2,1,0:T(8,128)S(1)}, u32[]{:S(2)}, u32[]{:S(2)}) %collective-permute-start.4) | collective-permute-done | bytes 163872 | tf_op jit(solution)/shard_map/ppermute | solution.py:975
  11.7 0.4 shard_map.154
  12.2 0.8 %collective-permute-start.6 = (f32[744,128]{1,0:T(8,128)S(1)}, f32[744,128]{1,0:T(8,128)S(1)}, u32[]{:S(2)}, u32[]{:S(2)}) collective-permute-start(f32[744,128]{1,0:T(8,128)S(1)} %get-tuple-element.52), channel_id=1, source_target_pairs={{0,1},{4,5},{8,9},{12,13},{1,0},{5,4},{9,8},{13,12},{2,3},{6,7},{1... | collective-permute-start | bytes 1142792 | tf_op jit(solution)/shard_map/ppermute | solution.py:975
  13.0 1.5 %collective-permute-start.7 = (f32[744,128]{1,0:T(8,128)S(1)}, f32[744,128]{1,0:T(8,128)S(1)}, u32[]{:S(2)}, u32[]{:S(2)}) collective-permute-start(f32[744,128]{1,0:T(8,128)S(1)} %get-tuple-element.53), channel_id=1, source_target_pairs={{0,4},{4,0},{8,12},{12,8},{1,2},{5,6},{9,10},{13,14},{2,1},{6,5},{... | collective-permute-start | bytes 1142792 | tf_op jit(solution)/shard_map/ppermute | solution.py:975
  14.5 0.8 %shard_map.152 = (f32[8,128]{1,0:T(8,128)S(1)}, f32[16,128]{1,0:T(8,128)S(1)}) custom-call(s32[64,32,128]{2,1,0:T(8,128)S(1)} %get-tuple-element.45.zone.refs_1_, f32[64,32,128]{2,1,0:T(8,128)S(1)} %get-tuple-element.46.scale.refs_0_, f32[64,32,128]{2,1,0:T(8,128)S(1)} %get-tuple-element.41.refs_0_.load, f32[296,128]{1,0:T(8,128)S(1)} %get-tuple-element.43.after, ...), custom_call_target="tpu_custom_call" | custom-call | tf_op jit(solution)/shard_map/pallas_call | solution.py:1048
  15.3 0.6 %collective-permute-done.3.right = f32[296,128]{1,0:T(8,128)S(1)} collective-permute-done((f32[296,128]{1,0:T(8,128)S(1)}, f32[296,128]{1,0:T(8,128)S(1)}, u32[]{:S(2)}, u32[]{:S(2)}) %collective-permute-start.3) | collective-permute-done | bytes 151584 | tf_op jit(solution)/shard_map/ppermute | solution.py:975
  16.0 4.1 %shard_map.153 = (f32[74,48,128]{2,1,0:T(8,128)S(1)}, f32[64,32,128]{2,1,0:T(8,128)S(1)}, f32[32,128]{1,0:T(8,128)S(1)}, f32[40,72,128]{2,1,0:T(8,128)S(1)}) custom-call(f32[64,32,128]{2,1,0:T(8,128)S(1)} %get-tuple-element.41.refs_0_.load, f32[4,32,128]{2,1,0:T(8,128)S(1)} %collective-permute-done.refs_1_.low, ...), custom_call_target="tpu_custom_call" | custom-call | flops 4000000000 | tf_op jit(solution)/shard_map/pallas_call | solution.py:1054
  20.1 0.5 collective-permute-done.7.right
  20.6 0.4 shard_map.155
  21.0 2.7 %collective-permute-start.10 = (f32[16,128]{1,0:T(8,128)S(1)}, f32[16,128]{1,0:T(8,128)S(1)}, u32[]{:S(2)}, u32[]{:S(2)}) collective-permute-start(f32[16,128]{1,0:T(8,128)S(1)} %get-tuple-element.57.refs_3_), channel_id=1, source_target_pairs={{0,8},{4,12},{8,0},{12,4},{1,9},{5,13},{9,1},{13,5},{2,10},{6,14},... | collective-permute-start | bytes 24584 | tf_op jit(solution)/shard_map/ppermute | solution.py:985
  23.7 1.2 %collective-permute-start.11 = (f32[16,128]{1,0:T(8,128)S(1)}, f32[16,128]{1,0:T(8,128)S(1)}, u32[]{:S(2)}, u32[]{:S(2)}) collective-permute-start(f32[16,128]{1,0:T(8,128)S(1)} %get-tuple-element.57.refs_3_), channel_id=1, source_target_pairs={{0,12},{4,8},{8,4},{12,0},{1,13},{5,9},{9,5},{13,1},{2,14},{6,10},... | collective-permute-start | bytes 24584 | tf_op jit(solution)/shard_map/ppermute | solution.py:980
  24.9 2.4 %shard_map.156 = (f32[74,48,128]{2,1,0:T(8,128)S(1)}, f32[74,48,128]{2,1,0:T(8,128)S(1)}, f32[74,48,128]{2,1,0:T(8,128)S(1)}, f32[74,48,128]{2,1,0:T(8,128)S(1)}) custom-call(s32[64,32,128]{2,1,0:T(8,128)S(1)} %get-tuple-element.45.zone.refs_1_, f32[64,32,128]{2,1,0:T(8,128)S(1)} %get-tuple-element.46.scale.refs_0_, ...), custom_call_target="tpu_custom_call" | custom-call | flops 1000000000 | tf_op jit(solution)/shard_map/pallas_call | solution.py:1070
  27.2 2.0 %collective-permute-done.11.refs_6_ = f32[16,128]{1,0:T(8,128)S(1)} collective-permute-done((f32[16,128]{1,0:T(8,128)S(1)}, f32[16,128]{1,0:T(8,128)S(1)}, u32[]{:S(2)}, u32[]{:S(2)}) %collective-permute-start.11) | collective-permute-done | bytes 8224 | tf_op jit(solution)/shard_map/ppermute | solution.py:980
  29.2 0.3 collective-permute-done.8.refs_1_.refs_4_.low
  29.5 0.2 shard_map.157
  29.8 2.0 %collective-permute-start.13 = (f32[392,128]{1,0:T(8,128)S(1)}, f32[392,128]{1,0:T(8,128)S(1)}, u32[]{:S(2)}, u32[]{:S(2)}) collective-permute-start(f32[392,128]{1,0:T(8,128)S(1)} %get-tuple-element.60), channel_id=1, source_target_pairs={{0,4},{4,0},{8,12},{12,8},{1,2},{5,6},{9,10},{13,14},{2,1},{6,5},{... | collective-permute-start | bytes 602120 | tf_op jit(solution)/shard_map/ppermute | solution.py:975
  31.8 0.3 collective-permute-start.14
  32.1 2.2 %shard_map.160 = (f32[74,48,128]{2,1,0:T(8,128)S(1)}, f32[74,48,128]{2,1,0:T(8,128)S(1)}) custom-call(f32[74,48,128]{2,1,0:T(8,128)S(1)} %get-tuple-element.64.zone_window, f32[74,48,128]{2,1,0:T(8,128)S(1)} %get-tuple-element.65.scale_window, f32[3,3]{1,0:T(4,128)S(1)} %copy-done, f32[1,3]{1,0:T(1,128)S(1)} %bitcast.3), custom_call_target="tpu_custom_call" | custom-call | flops 1000000000 | tf_op jit(solution)/shard_map/pallas_call | solution.py:1076
  34.4 1.4 %collective-permute-done.14.refs_1_ = f32[16,128]{1,0:T(8,128)S(1)} collective-permute-done((f32[16,128]{1,0:T(8,128)S(1)}, f32[16,128]{1,0:T(8,128)S(1)}, u32[]{:S(2)}, u32[]{:S(2)}) %collective-permute-start.14) | collective-permute-done | bytes 8224 | tf_op jit(solution)/shard_map/ppermute | solution.py:985
  35.8 0.9 %shard_map.159.answers = f32[8,128]{1,0:T(8,128)S(1)} custom-call(f32[16,128]{1,0:T(8,128)S(1)} %shard_map.158.refs_0_, f32[16,128]{1,0:T(8,128)S(1)} %collective-permute-done.14.refs_1_), custom_call_target="tpu_custom_call" | custom-call | tf_op jit(solution)/shard_map/pallas_call | solution.py:1091
  36.7 5.6 %shard_map.161 = (f32[64,32,128]{2,1,0:T(8,128)S(1)}, f32[32,128]{1,0:T(8,128)S(1)}, f32[32,128]{1,0:T(8,128)S(1)}, f32[64,128]{1,0:T(8,128)S(1)}, f32[64,128]{1,0:T(8,128)S(1)}, /*index=5*/f32[64,32,128]{2,1,0:T(8,128)}) custom-call(f32[64,32,128]{2,1,0:T(8,128)S(1)} %get-tuple-element.48.local.refs_0_, ...), custom_call_target="tpu_custom_call" | custom-call | flops 4000000000 | tf_op jit(solution)/shard_map/pallas_call | solution.py:1097
  42.3 2.0 %collective-permute-start.18 = (f32[64,128]{1,0:T(8,128)S(1)}, f32[64,128]{1,0:T(8,128)S(1)}, u32[]{:S(2)}, u32[]{:S(2)}) collective-permute-start(f32[64,128]{1,0:T(8,128)S(1)} %get-tuple-element.74), channel_id=1, source_target_pairs={{0,4},{4,0},{8,12},{12,8},{1,2},{5,6},{9,10},{13,14},{2,1},{6,5},{... | collective-permute-start | bytes 98312 | tf_op jit(solution)/shard_map/ppermute | solution.py:975
  44.5 1.9 %shard_map.162 = (f32[2,32,128]{2,1,0:T(8,128)S(1)}, f32[2,64,8,128]{3,2,1,0:T(8,128)S(1)}, f32[64,32,128]{2,1,0:T(8,128)}) custom-call(f32[64,32,128]{2,1,0:T(8,128)S(1)} %get-tuple-element.41.refs_0_.load, f32[64,32,128]{2,1,0:T(8,128)S(1)} %get-tuple-element.70.iterate, f32[74,48,128]{2,1,0:T(8,128)S(1)} %get-tuple-element.58.refs_7_.rest_0_.to_long, ...), custom_call_target="tpu_custom_call" | custom-call | flops 1000000000 | tf_op jit(solution)/shard_map/pallas_call | solution.py:1107
  46.3 1.7 %collective-permute-done.15.low = f32[32,128]{1,0:T(8,128)S(1)} collective-permute-done((f32[32,128]{1,0:T(8,128)S(1)}, f32[32,128]{1,0:T(8,128)S(1)}, u32[]{:S(2)}, u32[]{:S(2)}) %collective-permute-start.15) | collective-permute-done | bytes 16416 | tf_op jit(solution)/shard_map/ppermute | solution.py:975
  48.1 0.9 %shard_map.163 = f32[64,32,128]{2,1,0:T(8,128)} custom-call(f32[64,32,128]{2,1,0:T(8,128)S(1)} %get-tuple-element.70.iterate, f32[32,128]{1,0:T(8,128)S(1)} %collective-permute-done.15.low, f32[32,128]{1,0:T(8,128)S(1)} %collective-permute-done.16.high, f32[64,128]{1,0:T(8,128)S(1)} %collective-permute-done.17.left, ...), custom_call_target="tpu_custom_call", output_to_operand_aliasing={{}: (9, {})} | custom-call | tf_op jit(solution)/shard_map/pallas_call | solution.py:1119
  (43 shorter events, 0.4 us)
Async XLA Ops:
  1.8 8.2 %collective-permute-start = (f32[4,32,128]{2,1,0:T(8,128)S(1)}, f32[4,32,128]{2,1,0:T(8,128)S(1)}, u32[]{:S(2)}, u32[]{:S(2)}) collective-permute-start(f32[4,32,128]{2,1,0:T(8,128)S(1)} %get-tuple-element.40.after), channel_id=1, source_target_pairs={{0,4},{1,5},{2,6},{3,7},{4,0},{5,1},{6,2},{7,3},{8,12},{9,13},{10,... | collective-permute-start | bytes 196616 | tf_op jit(solution)/shard_map/ppermute | solution.py:975
  4.9 5.1 %collective-permute-start.1 = (f32[4,32,128]{2,1,0:T(8,128)S(1)}, f32[4,32,128]{2,1,0:T(8,128)S(1)}, u32[]{:S(2)}, u32[]{:S(2)}) collective-permute-start(f32[4,32,128]{2,1,0:T(8,128)S(1)} %get-tuple-element.42), channel_id=1, source_target_pairs={{0,1},{1,0},{2,3},{3,2},{4,8},{5,9},{6,10},{7,11},{8,4},{9,5},{10,... | collective-permute-start | bytes 196616 | tf_op jit(solution)/shard_map/ppermute | solution.py:975
  4.9 6.8 %collective-permute-start.4 = (f32[10,32,128]{2,1,0:T(8,128)S(1)}, f32[10,32,128]{2,1,0:T(8,128)S(1)}, u32[]{:S(2)}, u32[]{:S(2)}) collective-permute-start(f32[10,32,128]{2,1,0:T(8,128)S(1)} %get-tuple-element.50), channel_id=1, source_target_pairs={{0,4},{1,5},{2,6},{3,7},{4,0},{5,1},{6,2},{7,3},{8,12},{9,13},{10,... | collective-permute-start | bytes 491528 | tf_op jit(solution)/shard_map/ppermute | solution.py:975
  8.0 3.6 %collective-permute-start.5 = (f32[10,32,128]{2,1,0:T(8,128)S(1)}, f32[10,32,128]{2,1,0:T(8,128)S(1)}, u32[]{:S(2)}, u32[]{:S(2)}) collective-permute-start(f32[10,32,128]{2,1,0:T(8,128)S(1)} %get-tuple-element.51), channel_id=1, source_target_pairs={{0,1},{1,0},{2,3},{3,2},{4,8},{5,9},{6,10},{7,11},{8,4},{9,5},{10,... | collective-permute-start | bytes 491528 | tf_op jit(solution)/shard_map/ppermute | solution.py:975
  9.9 4.5 %copy-start = (f32[3,3]{1,0:T(4,128)S(1)}, f32[3,3]{1,0:T(4,128)}, u32[]{:S(2)}) copy-start(f32[3,3]{1,0:T(4,128)} %diffusivity.9) | copy-start | bytes 112
  10.0 4.5 %copy-start.1 = (f32[3]{0:T(128)S(1)}, f32[3]{0:T(128)}, u32[]{:S(2)}) copy-start(f32[3]{0:T(128)} %param.17) | copy-start | bytes 40
  10.2 5.1 %collective-permute-start.2 = (f32[296,128]{1,0:T(8,128)S(1)}, f32[296,128]{1,0:T(8,128)S(1)}, u32[]{:S(2)}, u32[]{:S(2)}) collective-permute-start(f32[296,128]{1,0:T(8,128)S(1)} %get-tuple-element.43.after), channel_id=1, source_target_pairs={{0,1},{4,5},{8,9},{12,13},{1,0},{5,4},{9,8},{13,12},{2,3},{6,7},{1... | collective-permute-start | bytes 454664 | tf_op jit(solution)/shard_map/ppermute | solution.py:975
  10.7 5.2 %collective-permute-start.3 = (f32[296,128]{1,0:T(8,128)S(1)}, f32[296,128]{1,0:T(8,128)S(1)}, u32[]{:S(2)}, u32[]{:S(2)}) collective-permute-start(f32[296,128]{1,0:T(8,128)S(1)} %get-tuple-element.44), channel_id=1, source_target_pairs={{0,4},{4,0},{8,12},{12,8},{1,2},{5,6},{9,10},{13,14},{2,1},{6,5},{... | collective-permute-start | bytes 454664 | tf_op jit(solution)/shard_map/ppermute | solution.py:975
  12.1 3.8 %copy-start.2 = (f32[256,256]{1,0:T(8,128)S(1)}, f32[256,256]{1,0:T(8,128)}, u32[]{:S(2)}) copy-start(f32[256,256]{1,0:T(8,128)} %constant.22.clone.rest_4_.rest_9_) | copy-start | bytes 786436
  12.1 3.8 %copy-start.3 = (f32[192,216]{1,0:T(8,128)S(1)}, f32[192,216]{1,0:T(8,128)}, u32[]{:S(2)}) copy-start(f32[192,216]{1,0:T(8,128)} %constant.20.clone.rest_2_.rest_7_) | copy-start | bytes 497668
  12.1 3.8 %copy-start.4 = (f32[144,144]{1,0:T(8,128)S(1)}, f32[144,144]{1,0:T(8,128)}, u32[]{:S(2)}) copy-start(f32[144,144]{1,0:T(8,128)} %constant.19.clone.rest_1_.rest_6_) | copy-start | bytes 248836
  12.1 3.8 %copy-start.5 = (f32[256,128]{1,0:T(8,128)S(1)}, f32[256,128]{1,0:T(8,128)}, u32[]{:S(2)}) copy-start(f32[256,128]{1,0:T(8,128)} %constant.23.clone.rest_5_.rest_10_) | copy-start | bytes 393220
  12.1 3.8 %copy-start.6 = (f32[96,120]{1,0:T(8,128)S(1)}, f32[96,120]{1,0:T(8,128)}, u32[]{:S(2)}) copy-start(f32[96,120]{1,0:T(8,128)} %constant.21.clone.rest_3_.rest_8_) | copy-start | bytes 138244
  12.2 3.8 %copy-start.7 = (f32[80,80]{1,0:T(8,128)S(1)}, f32[80,80]{1,0:T(8,128)}, u32[]{:S(2)}) copy-start(f32[80,80]{1,0:T(8,128)} %constant.18.clone.rest_0_.rest_5_) | copy-start | bytes 76804
  12.2 3.8 %copy-start.8 = (f32[72,128]{1,0:T(8,128)S(1)}, f32[72,128]{1,0:T(8,128)}, u32[]{:S(2)}) copy-start(f32[72,128]{1,0:T(8,128)} %constant.24.clone.rest_6_.rest_11_) | copy-start | bytes 110596
  12.2 3.8 %copy-start.9 = (f32[40,128]{1,0:T(8,128)S(1)}, f32[40,128]{1,0:T(8,128)}, u32[]{:S(2)}) copy-start(f32[40,128]{1,0:T(8,128)} %constant.25.clone.rest_7_.rest_12_) | copy-start | bytes 61444
  12.2 3.8 %copy-start.10 = (f32[1,128]{1,0:T(1,128)S(1)}, f32[1,128]{1,0:T(1,128)}, u32[]{:S(2)}) copy-start(f32[1,128]{1,0:T(1,128)} %constant.26.clone.rest_8_.rest_13_) | copy-start | bytes 1540
  12.2 7.9 %collective-permute-start.6 = (f32[744,128]{1,0:T(8,128)S(1)}, f32[744,128]{1,0:T(8,128)S(1)}, u32[]{:S(2)}, u32[]{:S(2)}) collective-permute-start(f32[744,128]{1,0:T(8,128)S(1)} %get-tuple-element.52), channel_id=1, source_target_pairs={{0,1},{4,5},{8,9},{12,13},{1,0},{5,4},{9,8},{13,12},{2,3},{6,7},{1... | collective-permute-start | bytes 1142792 | tf_op jit(solution)/shard_map/ppermute | solution.py:975
  13.0 7.6 %collective-permute-start.7 = (f32[744,128]{1,0:T(8,128)S(1)}, f32[744,128]{1,0:T(8,128)S(1)}, u32[]{:S(2)}, u32[]{:S(2)}) collective-permute-start(f32[744,128]{1,0:T(8,128)S(1)} %get-tuple-element.53), channel_id=1, source_target_pairs={{0,4},{4,0},{8,12},{12,8},{1,2},{5,6},{9,10},{13,14},{2,1},{6,5},{... | collective-permute-start | bytes 1142792 | tf_op jit(solution)/shard_map/ppermute | solution.py:975
  21.0 6.2 %collective-permute-start.10 = (f32[16,128]{1,0:T(8,128)S(1)}, f32[16,128]{1,0:T(8,128)S(1)}, u32[]{:S(2)}, u32[]{:S(2)}) collective-permute-start(f32[16,128]{1,0:T(8,128)S(1)} %get-tuple-element.57.refs_3_), channel_id=1, source_target_pairs={{0,8},{4,12},{8,0},{12,4},{1,9},{5,13},{9,1},{13,5},{2,10},{6,14},... | collective-permute-start | bytes 24584 | tf_op jit(solution)/shard_map/ppermute | solution.py:985
  23.7 5.6 %collective-permute-start.11 = (f32[16,128]{1,0:T(8,128)S(1)}, f32[16,128]{1,0:T(8,128)S(1)}, u32[]{:S(2)}, u32[]{:S(2)}) collective-permute-start(f32[16,128]{1,0:T(8,128)S(1)} %get-tuple-element.57.refs_3_), channel_id=1, source_target_pairs={{0,12},{4,8},{8,4},{12,0},{1,13},{5,9},{9,5},{13,1},{2,14},{6,10},... | collective-permute-start | bytes 24584 | tf_op jit(solution)/shard_map/ppermute | solution.py:980
  24.9 4.6 %collective-permute-start.8 = (f32[176,128]{1,0:T(8,128)S(1)}, f32[176,128]{1,0:T(8,128)S(1)}, u32[]{:S(2)}, u32[]{:S(2)}) collective-permute-start(f32[176,128]{1,0:T(8,128)S(1)} %get-tuple-element.55), channel_id=1, source_target_pairs={{0,4},{1,5},{2,6},{3,7},{4,0},{5,1},{6,2},{7,3},{8,12},{9,13},{10,... | collective-permute-start | bytes 270344 | tf_op jit(solution)/shard_map/ppermute | solution.py:975
  24.9 4.6 %collective-permute-start.9 = (f32[176,128]{1,0:T(8,128)S(1)}, f32[176,128]{1,0:T(8,128)S(1)}, u32[]{:S(2)}, u32[]{:S(2)}) collective-permute-start(f32[176,128]{1,0:T(8,128)S(1)} %get-tuple-element.56), channel_id=1, source_target_pairs={{0,1},{1,0},{2,3},{3,2},{4,8},{5,9},{6,10},{7,11},{8,4},{9,5},{10,... | collective-permute-start | bytes 270344 | tf_op jit(solution)/shard_map/ppermute | solution.py:975
  29.7 2.1 %collective-permute-start.12 = (f32[392,128]{1,0:T(8,128)S(1)}, f32[392,128]{1,0:T(8,128)S(1)}, u32[]{:S(2)}, u32[]{:S(2)}) collective-permute-start(f32[392,128]{1,0:T(8,128)S(1)} %get-tuple-element.59), channel_id=1, source_target_pairs={{0,1},{4,5},{8,9},{12,13},{1,0},{5,4},{9,8},{13,12},{2,3},{6,7},{1... | collective-permute-start | bytes 602120 | tf_op jit(solution)/shard_map/ppermute | solution.py:975
  29.8 6.9 %collective-permute-start.13 = (f32[392,128]{1,0:T(8,128)S(1)}, f32[392,128]{1,0:T(8,128)S(1)}, u32[]{:S(2)}, u32[]{:S(2)}) collective-permute-start(f32[392,128]{1,0:T(8,128)S(1)} %get-tuple-element.60), channel_id=1, source_target_pairs={{0,4},{4,0},{8,12},{12,8},{1,2},{5,6},{9,10},{13,14},{2,1},{6,5},{... | collective-permute-start | bytes 602120 | tf_op jit(solution)/shard_map/ppermute | solution.py:975
  31.8 4.0 %collective-permute-start.14 = (f32[16,128]{1,0:T(8,128)S(1)}, f32[16,128]{1,0:T(8,128)S(1)}, u32[]{:S(2)}, u32[]{:S(2)}) collective-permute-start(f32[16,128]{1,0:T(8,128)S(1)} %shard_map.158.refs_0_), channel_id=1, source_target_pairs={{0,2},{1,3},{2,0},{3,1},{4,6},{5,7},{6,4},{7,5},{8,10},{9,11},{10,... | collective-permute-start | bytes 24584 | tf_op jit(solution)/shard_map/ppermute | solution.py:985
  42.2 5.8 %collective-permute-start.17 = (f32[64,128]{1,0:T(8,128)S(1)}, f32[64,128]{1,0:T(8,128)S(1)}, u32[]{:S(2)}, u32[]{:S(2)}) collective-permute-start(f32[64,128]{1,0:T(8,128)S(1)} %get-tuple-element.73), channel_id=1, source_target_pairs={{0,1},{4,5},{8,9},{12,13},{1,0},{5,4},{9,8},{13,12},{2,3},{6,7},{1... | collective-permute-start | bytes 98312 | tf_op jit(solution)/shard_map/ppermute | solution.py:975
  42.3 5.8 %collective-permute-start.18 = (f32[64,128]{1,0:T(8,128)S(1)}, f32[64,128]{1,0:T(8,128)S(1)}, u32[]{:S(2)}, u32[]{:S(2)}) collective-permute-start(f32[64,128]{1,0:T(8,128)S(1)} %get-tuple-element.74), channel_id=1, source_target_pairs={{0,4},{4,0},{8,12},{12,8},{1,2},{5,6},{9,10},{13,14},{2,1},{6,5},{... | collective-permute-start | bytes 98312 | tf_op jit(solution)/shard_map/ppermute | solution.py:975
  44.3 3.7 %collective-permute-start.15 = (f32[32,128]{1,0:T(8,128)S(1)}, f32[32,128]{1,0:T(8,128)S(1)}, u32[]{:S(2)}, u32[]{:S(2)}) collective-permute-start(f32[32,128]{1,0:T(8,128)S(1)} %get-tuple-element.71), channel_id=1, source_target_pairs={{0,4},{1,5},{2,6},{3,7},{4,0},{5,1},{6,2},{7,3},{8,12},{9,13},{10,... | collective-permute-start | bytes 49160 | tf_op jit(solution)/shard_map/ppermute | solution.py:975
  44.4 3.7 %collective-permute-start.16 = (f32[32,128]{1,0:T(8,128)S(1)}, f32[32,128]{1,0:T(8,128)S(1)}, u32[]{:S(2)}, u32[]{:S(2)}) collective-permute-start(f32[32,128]{1,0:T(8,128)S(1)} %get-tuple-element.72), channel_id=1, source_target_pairs={{0,1},{1,0},{2,3},{3,2},{4,8},{5,9},{6,10},{7,11},{8,4},{9,5},{10,... | collective-permute-start | bytes 49160 | tf_op jit(solution)/shard_map/ppermute | solution.py:975

commit v19 on v18

--- a/solution.py
+++ b/solution.py
@@ -72,22 +72,20 @@
     return parts + [values]
 
 
+def products(count):
+    return [(a, b) for a in range(count) for b in range(count - a)]
+
+
 def left_table(table, depth, count):
     rows, cols = table.shape
-    wide = np.zeros((rows, depth), np.float32)
-    wide[:, :cols] = table
+    rest = np.zeros((rows, depth), np.float32)
+    rest[:, :cols] = table
     parts = []
-    rest = wide
     for _ in range(count):
         part = rest.astype(ml_dtypes.bfloat16).astype(np.float32)
         parts.append(part)
         rest = rest - part
-    blank = np.zeros_like(parts[0])
-    lines = []
-    for index in range(count):
-        used = count - index if count > 2 else count
-        lines.append(np.concatenate([parts[index]] * used + [blank] * (count - used), axis=1))
-    return np.concatenate(lines, axis=0)
+    return np.concatenate([parts[a] for a, _ in products(count)], axis=1)
 
 
 def right_tables(table):
@@ -146,9 +144,9 @@
     )
 
 
-def dot_left(table, values, count, rows):
-    total = one_pass(table, jnp.concatenate(pieces(values, count), axis=0))
-    return sum(total[index * rows : (index + 1) * rows] for index in range(1, count)) + total[:rows]
+def dot_left(table, values, count):
+    parts = pieces(values, count)
+    return one_pass(table, jnp.concatenate([parts[b] for _, b in products(count)], axis=0))
 
 
 def dot_right(values, main, rest, count):
@@ -189,9 +187,9 @@
     deep_x, deep_y = padded(box.ex), padded(box.ey)
     into_y, into_x = into_y[...], into_x[...]
     if col_mask is not None:
-        mask = jnp.concatenate([col_mask] * FORWARD, axis=1)
+        mask = jnp.concatenate([col_mask] * len(products(FORWARD)), axis=1)
         into_y = into_y * mask
-        mask = jnp.concatenate([row_mask] * FORWARD, axis=1)
+        mask = jnp.concatenate([row_mask] * len(products(FORWARD)), axis=1)
         into_x = into_x * mask
     from_x, from_y, main_z, rest_z = from_x[...], from_y[...], main_z[...], rest_z[...]
     spectral_flat = spectral.reshape(box.ey * deep_x, deep)
@@ -206,21 +204,21 @@
         block = dot_right(block.reshape(step * box.ey, deep), main_z, rest_z, FORWARD)
         block = block.reshape(step, box.ey, deep)
         wide = beside([block[row] for row in range(step)])
-        wide = dot_left(into_y, with_rows(wide, deep_y), FORWARD, box.ey)
+        wide = dot_left(into_y, with_rows(wide, deep_y), FORWARD)
         for row, values in enumerate(apart(wide, deep)):
             spectral_flat[pl.ds(start + row, box.ey, stride=deep_x), :] = values
     step = fitting(box.ey, COLS_ABREAST)
     for start in range(0, box.ey, step):
         wide = beside([spectral[col] for col in range(start, start + step)])
-        wide = apart(dot_left(into_x, wide, FORWARD, box.ex), deep)
+        wide = apart(dot_left(into_x, wide, FORWARD), deep)
         wide = beside([divided(values, start + part) for part, values in enumerate(wide)])
-        wide = dot_left(from_x, with_rows(wide, deep_x), BACKWARD, box.long)
+        wide = dot_left(from_x, with_rows(wide, deep_x), BACKWARD)
         for part, values in enumerate(apart(wide, deep)):
             middle_flat[pl.ds(start + part, box.long, stride=deep_y), :] = values
     step = fitting(box.long, BACKWARD_ROWS)
     for start in range(0, box.long, step):
         wide = beside([middle[row] for row in range(start, start + step)])
-        parts = apart(dot_left(from_y, wide, BACKWARD, box.across), deep)
+        parts = apart(dot_left(from_y, wide, BACKWARD), deep)
         values = dot_right(jnp.concatenate(parts, axis=0), main_z, rest_z, BACKWARD)
         for row in range(0, step, 8):
             emit(start + row, values[row * box.across : (row + 8) * box.across])
@@ -556,17 +554,11 @@
         labels, factor = zone_window[row], scale_window[row]
         now = [looked_up(labels, half[d]) * factor for d in range(2)]
         to_across[row] = now[1] + pltpu.roll(now[1], box.cols - 1, 0)
-        to_long[jnp.maximum(row - 1, 0)] = before + now[0]
+        to_long[max(row - 1, 0)] = before + now[0]
         return now[0]
 
-    def some_rows(index, before):
-        for row in range(8):
-            before = one_row(index * 8 + row, before)
-        return before
-
     before = jnp.zeros((box.cols, box.deep), jnp.float32)
-    before = lax.fori_loop(0, box.rows // 8, some_rows, before)
-    for row in range(box.rows // 8 * 8, box.rows):
+    for row in range(box.rows):
         before = one_row(row, before)
     to_long[box.rows - 1] = before
 
@@ -584,13 +576,7 @@
         to_deep[row] = (now + pltpu.roll(now, box.deep - 1, 1)) * not_last
         mass[row] = looked_up(labels, rates) + now * ends
 
-    def some_rows(index, _):
-        for row in range(8):
-            one_row(index * 8 + row)
-        return 0
-
-    lax.fori_loop(0, box.rows // 8, some_rows, 0)
-    for row in range(box.rows // 8 * 8, box.rows):
+    for row in range(box.rows):
         one_row(row)
 
 
@@ -751,8 +737,7 @@
     return jnp.sum(jnp.where(wanted, values, jnp.zeros_like(values)), axis=1, keepdims=True)
 
 
-def coarse_corrections(parts, *refs):
-    table_parts, (out, work) = refs[:parts], refs[parts:]
+def coarse_corrections(table_parts, work):
     count = work.shape[0]
     numbers = last_rows_merged(table_parts, count)
     across_count = lax.axis_size("narrow")
@@ -764,25 +749,27 @@
     sums = sums - column(pltpu.roll(numbers, 1, 0), FLOW_ACROSS_HIGH)
     load_sums = column(numbers, LOAD_SUM)
     sums = load_sums * (1.0 - 1.0 / cheb_center) - sums
-    out[0:1, :] = answer(inverse, load_sums) * (1.0 / cheb_center)
-    out[1:2, :] = answer(inverse, sums) * gain
-
-
-def second_solve(box, local, low, high, left, right, inverses, answers, *rest):
+    return answer(inverse, load_sums) * (1.0 / cheb_center), answer(inverse, sums) * gain
+
+
+def second_solve(box, parts, local, low, high, left, right, inverses, *rest):
+    table_parts, rest = rest[:parts], rest[parts:]
     to_long, to_across, to_deep, mass, load_window = rest[:5]
     tables = rest[5 : 5 + N_TABLES]
     iterate, top, bottom, last_col, first_col, out = rest[5 + N_TABLES : 11 + N_TABLES]
-    window, spectral, middle, sems = rest[11 + N_TABLES :]
+    window, spectral, middle, sems, work = rest[11 + N_TABLES :]
     long_pos, across_pos, long_count, across_count = position()
-    coarse = answers[0:1, :]
-    own_shift = at_box(answers[1:2, :], 0, 0)
+    coarse, second_coarse = coarse_corrections(table_parts, work)
+    own_coarse = at_box(coarse, 0, 0)
     shifts = {
-        (row_side, col_side): at_box(coarse, row_side, col_side)
+        (row_side, col_side): at_box(coarse, row_side, col_side) - own_coarse
         for row_side in (-1, 0, 1)
         for col_side in (-1, 0, 1)
     }
 
     def add(values, row_side, col_side):
+        if row_side == 0 and col_side == 0:
+            return values
         shift = shifts[row_side, col_side]
         if values.ndim == 3:
             shift = shift.reshape(1, 1, 1)
@@ -811,7 +798,11 @@
         rows = []
         for row in range(start_row + 1, start_row + 9):
             image, *state[:] = negative_image(box, window, row, row, *state, weights)
-            image = [some_cols(box, load_window, row, step) + image[step] for step in steps]
+            image = [
+                some_cols(box, load_window, row, step)
+                + (image[step] - some_cols(box, mass, row, step) * own_coarse)
+                for step in steps
+            ]
             rows.append(jnp.concatenate(image, axis=0))
         return jnp.stack(rows)
 
@@ -827,12 +818,12 @@
         col_ids >= MARGIN + box.across, as_float(across_pos < across_count - 1), col_mask
     )
     keep = 1.0 + rho_second * rho_first
+    shift = (at_box(second_coarse, 0, 0) + keep * own_coarse).reshape(1, 1, 1)
     copies = []
 
     def emit(start, values):
         rows = values.reshape(8, box.across, box.deep)
         before = window[first + start : first + start + 8, inner, :]
-        shift = own_shift.reshape(1, 1, 1)
         iterate[start : start + 8] = keep * before + (gain * rows + shift)
         copies.append(
             pltpu.make_async_copy(
@@ -1088,20 +1079,20 @@
     else:
         parts = (tell(own_table),)
     row, col = f32(across, deep), f32(long, deep)
-    answers = call(
-        functools.partial(coarse_corrections, len(parts)),
-        f32(8, -(-count // 128) * 128),
-        [VMEM] * len(parts),
-        [scratch((count, -(-2 * count // 128) * 128))],
-    )(*parts)
     iterate, first_row, second_row, first_col, second_col, result = call(
-        functools.partial(second_solve, box),
+        functools.partial(second_solve, box, len(parts)),
         (cells, row, row, col, col, cells),
-        [VMEM] * (12 + N_TABLES),
-        [scratch(window.shape), spectral, middle, pltpu.SemaphoreType.DMA((long // 8,))],
+        [VMEM] * (11 + len(parts) + N_TABLES),
+        [
+            scratch(window.shape),
+            spectral,
+            middle,
+            pltpu.SemaphoreType.DMA((long // 8,)),
+            scratch((count, -(-2 * count // 128) * 128)),
+        ],
         flops=4 * 10**9,
         out_spec=(VMEM,) * 5 + (anywhere,),
-    )(local, *wide, *narrow, inverses, answers, *weights, load_window, *tables)
+    )(local, *wide, *narrow, inverses, *parts, *weights, load_window, *tables)
     narrow = exchange("narrow", first_col, second_col)
     wide = exchange("wide", first_row, second_row)
     rows, cols, inner = call(

time: 49.3 us -> 50 us (1.014)
  waiting for transfers between devices: 7.17 us -> 9.11 us
  Pallas kernels: 23.1 us -> 21.9 us
    ppermute x8, waiting for transfers between devices: 1.13 us -> 3.2 us  [exchange(): lax.ppermute(second, axes, ways[1])]
    pallas_call x1, Pallas kernels: 2.25 us -> 0.86 us  [on_device(): call(functools.partial(deep_weights, box), (window,) * 2, [VMEM] * 2 + [V...]
    ppermute x2, waiting for transfers between devices: 1.38 us -> 0.21 us  [two_away(): return lax.ppermute(table, axis, [(i, (i + 2) % size) for i in range(size)])]
    ppermute x1, waiting for transfers between devices: 1.98 us -> 3.01 us  [from_other_end(): return lax.ppermute(table, axis, [(i, size - 1 - i) for i in range(size)])]
    pallas_call x1, Pallas kernels: 2.36 us -> 1.33 us  [on_device(): call(functools.partial(side_weights, box), (window,) * 4, [VMEM] * 6 + [V...]
    pallas_call x2 -> x1, Pallas kernels: 6.43 us -> 7.07 us  [on_device(): call(functools.partial(second_solve, box, len(parts)), (cells, row, row,...]
    pallas_call x1, Pallas kernels: 4.12 us -> 4.72 us  [on_device(): call(functools.partial(first_solve, box), (window, cells, f32(across, dee...]
  transfers between devices with their start and end apart: 19 -> 19, of which waited for: 7 -> 7; matrix products, arithmetic and copies ran while one was open for 0% -> 0% of each run, Pallas kernels for 30% -> 24%
where the time goes in v19:
time: 50 us; the launch traced here: 49.8 us
  Pallas kernels  21.9 us (44%)
  starting transfers between devices  17.6 us (35%)
  waiting for transfers between devices  9.11 us (18%)
  between operations  1.07 us (2%)
    ppermute x8, starting transfers between devices, exchange(): lax.ppermute(first, axes, ways[0])  7.81 us
    pallas_call x1, Pallas kernels, on_device(): call(functools.partial(second_solve, box, len(parts)), (cells, row, row,...  7.07 us
    ppermute x8, starting transfers between devices, exchange(): lax.ppermute(second, axes, ways[1])  5.77 us
    pallas_call x1, Pallas kernels, on_device(): call(functools.partial(first_solve, box), (window, cells, f32(across, dee...  4.72 us
    ppermute x8, waiting for transfers between devices, exchange(): lax.ppermute(second, axes, ways[1])  3.2 us
    ppermute x1, waiting for transfers between devices, from_other_end(): return lax.ppermute(table, axis, [(i, size - 1 - i) for i in range(size)])  3.01 us
    ppermute x2, starting transfers between devices, two_away(): return lax.ppermute(table, axis, [(i, (i + 2) % size) for i in range(size)])  2.87 us
    ppermute x8, waiting for transfers between devices, exchange(): lax.ppermute(first, axes, ways[0])  2.69 us
  transfers between devices with their start and end apart: 19, of which 7 were waited for; matrix products, arithmetic and copies ran while one was open for 0% of the time, Pallas kernels for 24%

profile of v19, /device:TPU:0, one launch (start us, length us, event | category | flops | bytes accessed | tf_op | source)
XLA Modules:
  0.0 49.8 jit_solution(15303948278440388784)
XLA Ops:
  0.6 1.1 %shard_map.149 = (f32[4,32,128]{2,1,0:T(8,128)S(1)}, f32[4,32,128]{2,1,0:T(8,128)S(1)}, f32[10,32,128]{2,1,0:T(8,128)S(1)}, f32[10,32,128]{2,1,0:T(8,128)S(1)}) custom-call(s32[64,32,128]{2,1,0:T(8,128)} %zone.3, f32[64,32,128]{2,1,0:T(8,128)} %scale.3, f32[64,32,128]{2,1,0:T(8,128)} %load.3), custom_call_target="tpu_custom_call" | custom-call | tf_op jit(solution)/shard_map/pallas_call | solution.py:1023
  1.8 3.1 %collective-permute-start = (f32[4,32,128]{2,1,0:T(8,128)S(1)}, f32[4,32,128]{2,1,0:T(8,128)S(1)}, u32[]{:S(2)}, u32[]{:S(2)}) collective-permute-start(f32[4,32,128]{2,1,0:T(8,128)S(1)} %get-tuple-element.40.after), channel_id=1, source_target_pairs={{0,4},{1,5},{2,6},{3,7},{4,0},{5,1},{6,2},{7,3},{8,12},{9,13},{10,... | collective-permute-start | bytes 196616 | tf_op jit(solution)/shard_map/ppermute | solution.py:966
  4.9 3.1 %collective-permute-start.4 = (f32[10,32,128]{2,1,0:T(8,128)S(1)}, f32[10,32,128]{2,1,0:T(8,128)S(1)}, u32[]{:S(2)}, u32[]{:S(2)}) collective-permute-start(f32[10,32,128]{2,1,0:T(8,128)S(1)} %get-tuple-element.50), channel_id=1, source_target_pairs={{0,4},{1,5},{2,6},{3,7},{4,0},{5,1},{6,2},{7,3},{8,12},{9,13},{10,... | collective-permute-start | bytes 491528 | tf_op jit(solution)/shard_map/ppermute | solution.py:966
  8.0 1.9 %shard_map.150 = (f32[64,32,128]{2,1,0:T(8,128)S(1)}, f32[64,32,128]{2,1,0:T(8,128)S(1)}, s32[64,32,128]{2,1,0:T(8,128)S(1)}) custom-call(f32[64,32,128]{2,1,0:T(8,128)} %load.3, f32[64,32,128]{2,1,0:T(8,128)} %scale.3, s32[64,32,128]{2,1,0:T(8,128)} %zone.3, f32[4,32,128]{2,1,0:T(8,128)S(1)} %get-tuple-element.40.after), custom_call_target="tpu_custom_call" | custom-call | tf_op jit(solution)/shard_map/pallas_call | solution.py:1029
  10.0 0.2 shard_map.151
  10.2 0.6 %collective-permute-start.2 = (f32[296,128]{1,0:T(8,128)S(1)}, f32[296,128]{1,0:T(8,128)S(1)}, u32[]{:S(2)}, u32[]{:S(2)}) collective-permute-start(f32[296,128]{1,0:T(8,128)S(1)} %get-tuple-element.43.after), channel_id=1, source_target_pairs={{0,1},{4,5},{8,9},{12,13},{1,0},{5,4},{9,8},{13,12},{2,3},{6,7},{1... | collective-permute-start | bytes 454664 | tf_op jit(solution)/shard_map/ppermute | solution.py:966
  10.7 0.2 collective-permute-start.3
  10.9 0.7 %collective-permute-done.4.refs_2_.low = f32[10,32,128]{2,1,0:T(8,128)S(1)} collective-permute-done((f32[10,32,128]{2,1,0:T(8,128)S(1)}, f32[10,32,128]{2,1,0:T(8,128)S(1)}, u32[]{:S(2)}, u32[]{:S(2)}) %collective-permute-start.4) | collective-permute-done | bytes 163872 | tf_op jit(solution)/shard_map/ppermute | solution.py:966
  11.7 0.4 shard_map.154
  12.2 0.8 %collective-permute-start.6 = (f32[744,128]{1,0:T(8,128)S(1)}, f32[744,128]{1,0:T(8,128)S(1)}, u32[]{:S(2)}, u32[]{:S(2)}) collective-permute-start(f32[744,128]{1,0:T(8,128)S(1)} %get-tuple-element.52), channel_id=1, source_target_pairs={{0,1},{4,5},{8,9},{12,13},{1,0},{5,4},{9,8},{13,12},{2,3},{6,7},{1... | collective-permute-start | bytes 1142792 | tf_op jit(solution)/shard_map/ppermute | solution.py:966
  13.0 1.5 %collective-permute-start.7 = (f32[744,128]{1,0:T(8,128)S(1)}, f32[744,128]{1,0:T(8,128)S(1)}, u32[]{:S(2)}, u32[]{:S(2)}) collective-permute-start(f32[744,128]{1,0:T(8,128)S(1)} %get-tuple-element.53), channel_id=1, source_target_pairs={{0,4},{4,0},{8,12},{12,8},{1,2},{5,6},{9,10},{13,14},{2,1},{6,5},{... | collective-permute-start | bytes 1142792 | tf_op jit(solution)/shard_map/ppermute | solution.py:966
  14.5 0.8 %shard_map.152 = (f32[8,128]{1,0:T(8,128)S(1)}, f32[16,128]{1,0:T(8,128)S(1)}) custom-call(s32[64,32,128]{2,1,0:T(8,128)S(1)} %get-tuple-element.45.zone.refs_1_, f32[64,32,128]{2,1,0:T(8,128)S(1)} %get-tuple-element.46.scale.refs_0_, f32[64,32,128]{2,1,0:T(8,128)S(1)} %get-tuple-element.41.refs_0_.load, f32[296,128]{1,0:T(8,128)S(1)} %get-tuple-element.43.after, ...), custom_call_target="tpu_custom_call" | custom-call | tf_op jit(solution)/shard_map/pallas_call | solution.py:1039
  15.3 0.6 %collective-permute-done.3.right = f32[296,128]{1,0:T(8,128)S(1)} collective-permute-done((f32[296,128]{1,0:T(8,128)S(1)}, f32[296,128]{1,0:T(8,128)S(1)}, u32[]{:S(2)}, u32[]{:S(2)}) %collective-permute-start.3) | collective-permute-done | bytes 151584 | tf_op jit(solution)/shard_map/ppermute | solution.py:966
  16.0 4.7 %shard_map.153 = (f32[74,48,128]{2,1,0:T(8,128)S(1)}, f32[64,32,128]{2,1,0:T(8,128)S(1)}, f32[32,128]{1,0:T(8,128)S(1)}, f32[40,72,128]{2,1,0:T(8,128)S(1)}) custom-call(f32[64,32,128]{2,1,0:T(8,128)S(1)} %get-tuple-element.41.refs_0_.load, f32[4,32,128]{2,1,0:T(8,128)S(1)} %collective-permute-done.refs_1_.low, ...), custom_call_target="tpu_custom_call" | custom-call | flops 4000000000 | tf_op jit(solution)/shard_map/pallas_call | solution.py:1045
  20.7 0.4 shard_map.155
  21.1 2.5 %collective-permute-start.10 = (f32[16,128]{1,0:T(8,128)S(1)}, f32[16,128]{1,0:T(8,128)S(1)}, u32[]{:S(2)}, u32[]{:S(2)}) collective-permute-start(f32[16,128]{1,0:T(8,128)S(1)} %get-tuple-element.57.refs_3_), channel_id=1, source_target_pairs={{0,8},{4,12},{8,0},{12,4},{1,9},{5,13},{9,1},{13,5},{2,10},{6,14},... | collective-permute-start | bytes 24584 | tf_op jit(solution)/shard_map/ppermute | solution.py:976
  23.7 1.2 %collective-permute-start.11 = (f32[16,128]{1,0:T(8,128)S(1)}, f32[16,128]{1,0:T(8,128)S(1)}, u32[]{:S(2)}, u32[]{:S(2)}) collective-permute-start(f32[16,128]{1,0:T(8,128)S(1)} %get-tuple-element.57.refs_3_), channel_id=1, source_target_pairs={{0,12},{4,8},{8,4},{12,0},{1,13},{5,9},{9,5},{13,1},{2,14},{6,10},... | collective-permute-start | bytes 24584 | tf_op jit(solution)/shard_map/ppermute | solution.py:971
  24.9 1.3 %shard_map.156 = (f32[74,48,128]{2,1,0:T(8,128)S(1)}, f32[74,48,128]{2,1,0:T(8,128)S(1)}, f32[74,48,128]{2,1,0:T(8,128)S(1)}, f32[74,48,128]{2,1,0:T(8,128)S(1)}) custom-call(s32[64,32,128]{2,1,0:T(8,128)S(1)} %get-tuple-element.45.zone.refs_1_, f32[64,32,128]{2,1,0:T(8,128)S(1)} %get-tuple-element.46.scale.refs_0_, ...), custom_call_target="tpu_custom_call" | custom-call | flops 1000000000 | tf_op jit(solution)/shard_map/pallas_call | solution.py:1061
  26.2 3.0 %collective-permute-done.11.refs_6_ = f32[16,128]{1,0:T(8,128)S(1)} collective-permute-done((f32[16,128]{1,0:T(8,128)S(1)}, f32[16,128]{1,0:T(8,128)S(1)}, u32[]{:S(2)}, u32[]{:S(2)}) %collective-permute-start.11) | collective-permute-done | bytes 8224 | tf_op jit(solution)/shard_map/ppermute | solution.py:971
  29.2 0.3 collective-permute-done.8.refs_1_.refs_4_.low
  29.5 0.2 shard_map.157
  29.8 2.0 %collective-permute-start.13 = (f32[392,128]{1,0:T(8,128)S(1)}, f32[392,128]{1,0:T(8,128)S(1)}, u32[]{:S(2)}, u32[]{:S(2)}) collective-permute-start(f32[392,128]{1,0:T(8,128)S(1)} %get-tuple-element.60), channel_id=1, source_target_pairs={{0,4},{4,0},{8,12},{12,8},{1,2},{5,6},{9,10},{13,14},{2,1},{6,5},{... | collective-permute-start | bytes 602120 | tf_op jit(solution)/shard_map/ppermute | solution.py:966
  31.8 0.3 collective-permute-start.14
  32.1 0.9 %shard_map.159 = (f32[74,48,128]{2,1,0:T(8,128)S(1)}, f32[74,48,128]{2,1,0:T(8,128)S(1)}) custom-call(f32[74,48,128]{2,1,0:T(8,128)S(1)} %get-tuple-element.64.zone_window, f32[74,48,128]{2,1,0:T(8,128)S(1)} %get-tuple-element.65.scale_window, f32[3,3]{1,0:T(4,128)S(1)} %copy-done, f32[1,3]{1,0:T(1,128)S(1)} %bitcast.3), custom_call_target="tpu_custom_call" | custom-call | flops 1000000000 | tf_op jit(solution)/shard_map/pallas_call | solution.py:1067
  33.0 2.6 %collective-permute-done.13.right = f32[392,128]{1,0:T(8,128)S(1)} collective-permute-done((f32[392,128]{1,0:T(8,128)S(1)}, f32[392,128]{1,0:T(8,128)S(1)}, u32[]{:S(2)}, u32[]{:S(2)}) %collective-permute-start.13) | collective-permute-done | bytes 200736 | tf_op jit(solution)/shard_map/ppermute | solution.py:966
  35.6 0.2 collective-permute-done.14.rest_1_
  35.8 7.1 %shard_map.160 = (f32[64,32,128]{2,1,0:T(8,128)S(1)}, f32[32,128]{1,0:T(8,128)S(1)}, f32[32,128]{1,0:T(8,128)S(1)}, f32[64,128]{1,0:T(8,128)S(1)}, f32[64,128]{1,0:T(8,128)S(1)}, /*index=5*/f32[64,32,128]{2,1,0:T(8,128)}) custom-call(f32[64,32,128]{2,1,0:T(8,128)S(1)} %get-tuple-element.48.local.refs_0_, ...), custom_call_target="tpu_custom_call" | custom-call | flops 4000000000 | tf_op jit(solution)/shard_map/pallas_call | solution.py:1082
  42.9 2.0 %collective-permute-start.18 = (f32[64,128]{1,0:T(8,128)S(1)}, f32[64,128]{1,0:T(8,128)S(1)}, u32[]{:S(2)}, u32[]{:S(2)}) collective-permute-start(f32[64,128]{1,0:T(8,128)S(1)} %get-tuple-element.74), channel_id=1, source_target_pairs={{0,4},{4,0},{8,12},{12,8},{1,2},{5,6},{9,10},{13,14},{2,1},{6,5},{... | collective-permute-start | bytes 98312 | tf_op jit(solution)/shard_map/ppermute | solution.py:966
  44.9 0.1 collective-permute-start.15
  45.1 1.9 %shard_map.161 = (f32[2,32,128]{2,1,0:T(8,128)S(1)}, f32[2,64,8,128]{3,2,1,0:T(8,128)S(1)}, f32[64,32,128]{2,1,0:T(8,128)}) custom-call(f32[64,32,128]{2,1,0:T(8,128)S(1)} %get-tuple-element.41.refs_0_.load, f32[64,32,128]{2,1,0:T(8,128)S(1)} %get-tuple-element.70.iterate, f32[74,48,128]{2,1,0:T(8,128)S(1)} %get-tuple-element.58.refs_7_.rest_2_.to_long, ...), custom_call_target="tpu_custom_call" | custom-call | flops 1000000000 | tf_op jit(solution)/shard_map/pallas_call | solution.py:1098
  47.0 1.7 %collective-permute-done.15.low = f32[32,128]{1,0:T(8,128)S(1)} collective-permute-done((f32[32,128]{1,0:T(8,128)S(1)}, f32[32,128]{1,0:T(8,128)S(1)}, u32[]{:S(2)}, u32[]{:S(2)}) %collective-permute-start.15) | collective-permute-done | bytes 16416 | tf_op jit(solution)/shard_map/ppermute | solution.py:966
  48.7 0.9 %shard_map.162 = f32[64,32,128]{2,1,0:T(8,128)} custom-call(f32[64,32,128]{2,1,0:T(8,128)S(1)} %get-tuple-element.70.iterate, f32[32,128]{1,0:T(8,128)S(1)} %collective-permute-done.15.low, f32[32,128]{1,0:T(8,128)S(1)} %collective-permute-done.16.high, f32[64,128]{1,0:T(8,128)S(1)} %collective-permute-done.17.left, ...), custom_call_target="tpu_custom_call", output_to_operand_aliasing={{}: (9, {})} | custom-call | tf_op jit(solution)/shard_map/pallas_call | solution.py:1110
  (42 shorter events, 0.3 us)
Async XLA Ops:
  1.8 8.2 %collective-permute-start = (f32[4,32,128]{2,1,0:T(8,128)S(1)}, f32[4,32,128]{2,1,0:T(8,128)S(1)}, u32[]{:S(2)}, u32[]{:S(2)}) collective-permute-start(f32[4,32,128]{2,1,0:T(8,128)S(1)} %get-tuple-element.40.after), channel_id=1, source_target_pairs={{0,4},{1,5},{2,6},{3,7},{4,0},{5,1},{6,2},{7,3},{8,12},{9,13},{10,... | collective-permute-start | bytes 196616 | tf_op jit(solution)/shard_map/ppermute | solution.py:966
  4.9 5.1 %collective-permute-start.1 = (f32[4,32,128]{2,1,0:T(8,128)S(1)}, f32[4,32,128]{2,1,0:T(8,128)S(1)}, u32[]{:S(2)}, u32[]{:S(2)}) collective-permute-start(f32[4,32,128]{2,1,0:T(8,128)S(1)} %get-tuple-element.42), channel_id=1, source_target_pairs={{0,1},{1,0},{2,3},{3,2},{4,8},{5,9},{6,10},{7,11},{8,4},{9,5},{10,... | collective-permute-start | bytes 196616 | tf_op jit(solution)/shard_map/ppermute | solution.py:966
  4.9 6.8 %collective-permute-start.4 = (f32[10,32,128]{2,1,0:T(8,128)S(1)}, f32[10,32,128]{2,1,0:T(8,128)S(1)}, u32[]{:S(2)}, u32[]{:S(2)}) collective-permute-start(f32[10,32,128]{2,1,0:T(8,128)S(1)} %get-tuple-element.50), channel_id=1, source_target_pairs={{0,4},{1,5},{2,6},{3,7},{4,0},{5,1},{6,2},{7,3},{8,12},{9,13},{10,... | collective-permute-start | bytes 491528 | tf_op jit(solution)/shard_map/ppermute | solution.py:966
  8.0 3.6 %collective-permute-start.5 = (f32[10,32,128]{2,1,0:T(8,128)S(1)}, f32[10,32,128]{2,1,0:T(8,128)S(1)}, u32[]{:S(2)}, u32[]{:S(2)}) collective-permute-start(f32[10,32,128]{2,1,0:T(8,128)S(1)} %get-tuple-element.51), channel_id=1, source_target_pairs={{0,1},{1,0},{2,3},{3,2},{4,8},{5,9},{6,10},{7,11},{8,4},{9,5},{10,... | collective-permute-start | bytes 491528 | tf_op jit(solution)/shard_map/ppermute | solution.py:966
  9.9 4.5 %copy-start = (f32[3,3]{1,0:T(4,128)S(1)}, f32[3,3]{1,0:T(4,128)}, u32[]{:S(2)}) copy-start(f32[3,3]{1,0:T(4,128)} %diffusivity.9) | copy-start | bytes 112
  10.0 4.5 %copy-start.1 = (f32[3]{0:T(128)S(1)}, f32[3]{0:T(128)}, u32[]{:S(2)}) copy-start(f32[3]{0:T(128)} %param.17) | copy-start | bytes 40
  10.2 5.1 %collective-permute-start.2 = (f32[296,128]{1,0:T(8,128)S(1)}, f32[296,128]{1,0:T(8,128)S(1)}, u32[]{:S(2)}, u32[]{:S(2)}) collective-permute-start(f32[296,128]{1,0:T(8,128)S(1)} %get-tuple-element.43.after), channel_id=1, source_target_pairs={{0,1},{4,5},{8,9},{12,13},{1,0},{5,4},{9,8},{13,12},{2,3},{6,7},{1... | collective-permute-start | bytes 454664 | tf_op jit(solution)/shard_map/ppermute | solution.py:966
  10.7 5.2 %collective-permute-start.3 = (f32[296,128]{1,0:T(8,128)S(1)}, f32[296,128]{1,0:T(8,128)S(1)}, u32[]{:S(2)}, u32[]{:S(2)}) collective-permute-start(f32[296,128]{1,0:T(8,128)S(1)} %get-tuple-element.44), channel_id=1, source_target_pairs={{0,4},{4,0},{8,12},{12,8},{1,2},{5,6},{9,10},{13,14},{2,1},{6,5},{... | collective-permute-start | bytes 454664 | tf_op jit(solution)/shard_map/ppermute | solution.py:966
  12.1 3.8 %copy-start.2 = (f32[256,256]{1,0:T(8,128)S(1)}, f32[256,256]{1,0:T(8,128)}, u32[]{:S(2)}) copy-start(f32[256,256]{1,0:T(8,128)} %constant.22.clone.rest_4_.rest_11_) | copy-start | bytes 786436
  12.1 3.8 %copy-start.3 = (f32[64,432]{1,0:T(8,128)S(1)}, f32[64,432]{1,0:T(8,128)}, u32[]{:S(2)}) copy-start(f32[64,432]{1,0:T(8,128)} %constant.20.clone.rest_2_.rest_9_) | copy-start | bytes 331780
  12.1 3.8 %copy-start.4 = (f32[256,128]{1,0:T(8,128)S(1)}, f32[256,128]{1,0:T(8,128)}, u32[]{:S(2)}) copy-start(f32[256,128]{1,0:T(8,128)} %constant.23.clone.rest_5_.rest_12_) | copy-start | bytes 393220
  12.1 3.8 %copy-start.5 = (f32[72,216]{1,0:T(8,128)S(1)}, f32[72,216]{1,0:T(8,128)}, u32[]{:S(2)}) copy-start(f32[72,216]{1,0:T(8,128)} %constant.19.clone.rest_1_.rest_8_) | copy-start | bytes 186628
  12.1 3.8 %copy-start.6 = (f32[72,128]{1,0:T(8,128)S(1)}, f32[72,128]{1,0:T(8,128)}, u32[]{:S(2)}) copy-start(f32[72,128]{1,0:T(8,128)} %constant.24.clone.rest_6_.rest_13_) | copy-start | bytes 110596
  12.2 3.8 %copy-start.7 = (f32[32,240]{1,0:T(8,128)S(1)}, f32[32,240]{1,0:T(8,128)}, u32[]{:S(2)}) copy-start(f32[32,240]{1,0:T(8,128)} %constant.21.clone.rest_3_.rest_10_) | copy-start | bytes 92164
  12.2 3.8 %copy-start.8 = (f32[40,120]{1,0:T(8,128)S(1)}, f32[40,120]{1,0:T(8,128)}, u32[]{:S(2)}) copy-start(f32[40,120]{1,0:T(8,128)} %constant.18.clone.rest_0_.rest_7_) | copy-start | bytes 57604
  12.2 3.8 %copy-start.9 = (f32[40,128]{1,0:T(8,128)S(1)}, f32[40,128]{1,0:T(8,128)}, u32[]{:S(2)}) copy-start(f32[40,128]{1,0:T(8,128)} %constant.25.clone.rest_7_.rest_14_) | copy-start | bytes 61444
  12.2 3.8 %copy-start.10 = (f32[1,128]{1,0:T(1,128)S(1)}, f32[1,128]{1,0:T(1,128)}, u32[]{:S(2)}) copy-start(f32[1,128]{1,0:T(1,128)} %constant.26.clone.rest_8_.rest_15_) | copy-start | bytes 1540
  12.2 8.5 %collective-permute-start.6 = (f32[744,128]{1,0:T(8,128)S(1)}, f32[744,128]{1,0:T(8,128)S(1)}, u32[]{:S(2)}, u32[]{:S(2)}) collective-permute-start(f32[744,128]{1,0:T(8,128)S(1)} %get-tuple-element.52), channel_id=1, source_target_pairs={{0,1},{4,5},{8,9},{12,13},{1,0},{5,4},{9,8},{13,12},{2,3},{6,7},{1... | collective-permute-start | bytes 1142792 | tf_op jit(solution)/shard_map/ppermute | solution.py:966
  13.0 7.8 %collective-permute-start.7 = (f32[744,128]{1,0:T(8,128)S(1)}, f32[744,128]{1,0:T(8,128)S(1)}, u32[]{:S(2)}, u32[]{:S(2)}) collective-permute-start(f32[744,128]{1,0:T(8,128)S(1)} %get-tuple-element.53), channel_id=1, source_target_pairs={{0,4},{4,0},{8,12},{12,8},{1,2},{5,6},{9,10},{13,14},{2,1},{6,5},{... | collective-permute-start | bytes 1142792 | tf_op jit(solution)/shard_map/ppermute | solution.py:966
  21.1 5.1 %collective-permute-start.10 = (f32[16,128]{1,0:T(8,128)S(1)}, f32[16,128]{1,0:T(8,128)S(1)}, u32[]{:S(2)}, u32[]{:S(2)}) collective-permute-start(f32[16,128]{1,0:T(8,128)S(1)} %get-tuple-element.57.refs_3_), channel_id=1, source_target_pairs={{0,8},{4,12},{8,0},{12,4},{1,9},{5,13},{9,1},{13,5},{2,10},{6,14},... | collective-permute-start | bytes 24584 | tf_op jit(solution)/shard_map/ppermute | solution.py:976
  23.7 5.6 %collective-permute-start.11 = (f32[16,128]{1,0:T(8,128)S(1)}, f32[16,128]{1,0:T(8,128)S(1)}, u32[]{:S(2)}, u32[]{:S(2)}) collective-permute-start(f32[16,128]{1,0:T(8,128)S(1)} %get-tuple-element.57.refs_3_), channel_id=1, source_target_pairs={{0,12},{4,8},{8,4},{12,0},{1,13},{5,9},{9,5},{13,1},{2,14},{6,10},... | collective-permute-start | bytes 24584 | tf_op jit(solution)/shard_map/ppermute | solution.py:971
  24.9 4.6 %collective-permute-start.8 = (f32[176,128]{1,0:T(8,128)S(1)}, f32[176,128]{1,0:T(8,128)S(1)}, u32[]{:S(2)}, u32[]{:S(2)}) collective-permute-start(f32[176,128]{1,0:T(8,128)S(1)} %get-tuple-element.55), channel_id=1, source_target_pairs={{0,4},{1,5},{2,6},{3,7},{4,0},{5,1},{6,2},{7,3},{8,12},{9,13},{10,... | collective-permute-start | bytes 270344 | tf_op jit(solution)/shard_map/ppermute | solution.py:966
  24.9 4.6 %collective-permute-start.9 = (f32[176,128]{1,0:T(8,128)S(1)}, f32[176,128]{1,0:T(8,128)S(1)}, u32[]{:S(2)}, u32[]{:S(2)}) collective-permute-start(f32[176,128]{1,0:T(8,128)S(1)} %get-tuple-element.56), channel_id=1, source_target_pairs={{0,1},{1,0},{2,3},{3,2},{4,8},{5,9},{6,10},{7,11},{8,4},{9,5},{10,... | collective-permute-start | bytes 270344 | tf_op jit(solution)/shard_map/ppermute | solution.py:966
  29.7 2.1 %collective-permute-start.12 = (f32[392,128]{1,0:T(8,128)S(1)}, f32[392,128]{1,0:T(8,128)S(1)}, u32[]{:S(2)}, u32[]{:S(2)}) collective-permute-start(f32[392,128]{1,0:T(8,128)S(1)} %get-tuple-element.59), channel_id=1, source_target_pairs={{0,1},{4,5},{8,9},{12,13},{1,0},{5,4},{9,8},{13,12},{2,3},{6,7},{1... | collective-permute-start | bytes 602120 | tf_op jit(solution)/shard_map/ppermute | solution.py:966
  29.8 5.8 %collective-permute-start.13 = (f32[392,128]{1,0:T(8,128)S(1)}, f32[392,128]{1,0:T(8,128)S(1)}, u32[]{:S(2)}, u32[]{:S(2)}) collective-permute-start(f32[392,128]{1,0:T(8,128)S(1)} %get-tuple-element.60), channel_id=1, source_target_pairs={{0,4},{4,0},{8,12},{12,8},{1,2},{5,6},{9,10},{13,14},{2,1},{6,5},{... | collective-permute-start | bytes 602120 | tf_op jit(solution)/shard_map/ppermute | solution.py:966
  31.8 4.0 %collective-permute-start.14 = (f32[16,128]{1,0:T(8,128)S(1)}, f32[16,128]{1,0:T(8,128)S(1)}, u32[]{:S(2)}, u32[]{:S(2)}) collective-permute-start(f32[16,128]{1,0:T(8,128)S(1)} %shard_map.158.rest_0_), channel_id=1, source_target_pairs={{0,2},{1,3},{2,0},{3,1},{4,6},{5,7},{6,4},{7,5},{8,10},{9,11},{10,... | collective-permute-start | bytes 24584 | tf_op jit(solution)/shard_map/ppermute | solution.py:976
  42.9 5.8 %collective-permute-start.17 = (f32[64,128]{1,0:T(8,128)S(1)}, f32[64,128]{1,0:T(8,128)S(1)}, u32[]{:S(2)}, u32[]{:S(2)}) collective-permute-start(f32[64,128]{1,0:T(8,128)S(1)} %get-tuple-element.73), channel_id=1, source_target_pairs={{0,1},{4,5},{8,9},{12,13},{1,0},{5,4},{9,8},{13,12},{2,3},{6,7},{1... | collective-permute-start | bytes 98312 | tf_op jit(solution)/shard_map/ppermute | solution.py:966
  42.9 5.8 %collective-permute-start.18 = (f32[64,128]{1,0:T(8,128)S(1)}, f32[64,128]{1,0:T(8,128)S(1)}, u32[]{:S(2)}, u32[]{:S(2)}) collective-permute-start(f32[64,128]{1,0:T(8,128)S(1)} %get-tuple-element.74), channel_id=1, source_target_pairs={{0,4},{4,0},{8,12},{12,8},{1,2},{5,6},{9,10},{13,14},{2,1},{6,5},{... | collective-permute-start | bytes 98312 | tf_op jit(solution)/shard_map/ppermute | solution.py:966
  44.9 3.7 %collective-permute-start.15 = (f32[32,128]{1,0:T(8,128)S(1)}, f32[32,128]{1,0:T(8,128)S(1)}, u32[]{:S(2)}, u32[]{:S(2)}) collective-permute-start(f32[32,128]{1,0:T(8,128)S(1)} %get-tuple-element.71), channel_id=1, source_target_pairs={{0,4},{1,5},{2,6},{3,7},{4,0},{5,1},{6,2},{7,3},{8,12},{9,13},{10,... | collective-permute-start | bytes 49160 | tf_op jit(solution)/shard_map/ppermute | solution.py:966
  45.0 3.7 %collective-permute-start.16 = (f32[32,128]{1,0:T(8,128)S(1)}, f32[32,128]{1,0:T(8,128)S(1)}, u32[]{:S(2)}, u32[]{:S(2)}) collective-permute-start(f32[32,128]{1,0:T(8,128)S(1)} %get-tuple-element.72), channel_id=1, source_target_pairs={{0,1},{1,0},{2,3},{3,2},{4,8},{5,9},{6,10},{7,11},{8,4},{9,5},{10,... | collective-permute-start | bytes 49160 | tf_op jit(solution)/shard_map/ppermute | solution.py:966

commit v20 on v18

--- a/solution.py
+++ b/solution.py
@@ -168,7 +168,7 @@
     return jnp.concatenate([values, blank], axis=0)
 
 
-FORWARD_ROWS, COLS_ABREAST, BACKWARD_ROWS = 24, 40, 32
+FORWARD_ROWS, COLS_ABREAST, BACKWARD_ROWS = 72, 40, 64
 
 
 def fitting(size, wanted):
@@ -556,17 +556,11 @@
         labels, factor = zone_window[row], scale_window[row]
         now = [looked_up(labels, half[d]) * factor for d in range(2)]
         to_across[row] = now[1] + pltpu.roll(now[1], box.cols - 1, 0)
-        to_long[jnp.maximum(row - 1, 0)] = before + now[0]
+        to_long[max(row - 1, 0)] = before + now[0]
         return now[0]
 
-    def some_rows(index, before):
-        for row in range(8):
-            before = one_row(index * 8 + row, before)
-        return before
-
     before = jnp.zeros((box.cols, box.deep), jnp.float32)
-    before = lax.fori_loop(0, box.rows // 8, some_rows, before)
-    for row in range(box.rows // 8 * 8, box.rows):
+    for row in range(box.rows):
         before = one_row(row, before)
     to_long[box.rows - 1] = before
 
@@ -584,13 +578,7 @@
         to_deep[row] = (now + pltpu.roll(now, box.deep - 1, 1)) * not_last
         mass[row] = looked_up(labels, rates) + now * ends
 
-    def some_rows(index, _):
-        for row in range(8):
-            one_row(index * 8 + row)
-        return 0
-
-    lax.fori_loop(0, box.rows // 8, some_rows, 0)
-    for row in range(box.rows // 8 * 8, box.rows):
+    for row in range(box.rows):
         one_row(row)
 
 

time: 49.3 us -> 49.5 us (level)
  waiting for transfers between devices: 7.17 us -> 9.69 us
  Pallas kernels: 23.1 us -> 20.7 us
    ppermute x2, waiting for transfers between devices: 1.38 us -> 2.82 us  [two_away(): return lax.ppermute(table, axis, [(i, (i + 2) % size) for i in range(size)])]
    pallas_call x1, Pallas kernels: 2.25 us -> 0.81 us  [on_device(): call(functools.partial(deep_weights, box), (window,) * 2, [VMEM] * 2 + [V...]
    ppermute x1, waiting for transfers between devices: 1.98 us -> 3.01 us  [from_other_end(): return lax.ppermute(table, axis, [(i, size - 1 - i) for i in range(size)])]
    pallas_call x1, Pallas kernels: 2.36 us -> 1.33 us  [on_device(): call(functools.partial(side_weights, box), (window,) * 4, [VMEM] * 6 + [V...]
  transfers between devices with their start and end apart: 19 -> 19, of which waited for: 7 -> 7; matrix products, arithmetic and copies ran while one was open for 0% -> 0% of each run, Pallas kernels for 30% -> 25%
where the time goes in v20:
time: 49.5 us; the launch traced here: 49.3 us
  Pallas kernels  20.7 us (42%)
  starting transfers between devices  17.8 us (36%)
  waiting for transfers between devices  9.69 us (20%)
  between operations  1.07 us (2%)
    ppermute x8, starting transfers between devices, exchange(): lax.ppermute(first, axes, ways[0])  7.81 us
    ppermute x8, starting transfers between devices, exchange(): lax.ppermute(second, axes, ways[1])  5.76 us
    pallas_call x1, Pallas kernels, on_device(): call(functools.partial(second_solve, box), (cells, row, row, col, col, ce...  5.69 us
    pallas_call x1, Pallas kernels, on_device(): call(functools.partial(first_solve, box), (window, cells, f32(across, dee...  4.08 us
    ppermute x1, waiting for transfers between devices, from_other_end(): return lax.ppermute(table, axis, [(i, size - 1 - i) for i in range(size)])  3.01 us
    ppermute x2, starting transfers between devices, two_away(): return lax.ppermute(table, axis, [(i, (i + 2) % size) for i in range(size)])  3 us
    ppermute x2, waiting for transfers between devices, two_away(): return lax.ppermute(table, axis, [(i, (i + 2) % size) for i in range(size)])  2.82 us
    ppermute x8, waiting for transfers between devices, exchange(): lax.ppermute(first, axes, ways[0])  2.69 us
  transfers between devices with their start and end apart: 19, of which 7 were waited for; matrix products, arithmetic and copies ran while one was open for 0% of the time, Pallas kernels for 25%

profile of v20, /device:TPU:0, one launch (start us, length us, event | category | flops | bytes accessed | tf_op | source)
XLA Modules:
  0.0 49.3 jit_solution(12617475926656781210)
XLA Ops:
  0.6 1.1 %shard_map.149 = (f32[4,32,128]{2,1,0:T(8,128)S(1)}, f32[4,32,128]{2,1,0:T(8,128)S(1)}, f32[10,32,128]{2,1,0:T(8,128)S(1)}, f32[10,32,128]{2,1,0:T(8,128)S(1)}) custom-call(s32[64,32,128]{2,1,0:T(8,128)} %zone.3, f32[64,32,128]{2,1,0:T(8,128)} %scale.3, f32[64,32,128]{2,1,0:T(8,128)} %load.3), custom_call_target="tpu_custom_call" | custom-call | tf_op jit(solution)/shard_map/pallas_call | solution.py:1020
  1.8 3.1 %collective-permute-start = (f32[4,32,128]{2,1,0:T(8,128)S(1)}, f32[4,32,128]{2,1,0:T(8,128)S(1)}, u32[]{:S(2)}, u32[]{:S(2)}) collective-permute-start(f32[4,32,128]{2,1,0:T(8,128)S(1)} %get-tuple-element.40.after), channel_id=1, source_target_pairs={{0,4},{1,5},{2,6},{3,7},{4,0},{5,1},{6,2},{7,3},{8,12},{9,13},{10,... | collective-permute-start | bytes 196616 | tf_op jit(solution)/shard_map/ppermute | solution.py:963
  4.9 3.1 %collective-permute-start.4 = (f32[10,32,128]{2,1,0:T(8,128)S(1)}, f32[10,32,128]{2,1,0:T(8,128)S(1)}, u32[]{:S(2)}, u32[]{:S(2)}) collective-permute-start(f32[10,32,128]{2,1,0:T(8,128)S(1)} %get-tuple-element.50), channel_id=1, source_target_pairs={{0,4},{1,5},{2,6},{3,7},{4,0},{5,1},{6,2},{7,3},{8,12},{9,13},{10,... | collective-permute-start | bytes 491528 | tf_op jit(solution)/shard_map/ppermute | solution.py:963
  8.0 1.9 %shard_map.150 = (f32[64,32,128]{2,1,0:T(8,128)S(1)}, f32[64,32,128]{2,1,0:T(8,128)S(1)}, s32[64,32,128]{2,1,0:T(8,128)S(1)}) custom-call(f32[64,32,128]{2,1,0:T(8,128)} %load.3, f32[64,32,128]{2,1,0:T(8,128)} %scale.3, s32[64,32,128]{2,1,0:T(8,128)} %zone.3, f32[4,32,128]{2,1,0:T(8,128)S(1)} %get-tuple-element.40.after), custom_call_target="tpu_custom_call" | custom-call | tf_op jit(solution)/shard_map/pallas_call | solution.py:1026
  10.0 0.2 shard_map.151
  10.2 0.6 %collective-permute-start.2 = (f32[296,128]{1,0:T(8,128)S(1)}, f32[296,128]{1,0:T(8,128)S(1)}, u32[]{:S(2)}, u32[]{:S(2)}) collective-permute-start(f32[296,128]{1,0:T(8,128)S(1)} %get-tuple-element.43.after), channel_id=1, source_target_pairs={{0,1},{4,5},{8,9},{12,13},{1,0},{5,4},{9,8},{13,12},{2,3},{6,7},{1... | collective-permute-start | bytes 454664 | tf_op jit(solution)/shard_map/ppermute | solution.py:963
  10.7 0.2 collective-permute-start.3
  10.9 0.7 %collective-permute-done.4.refs_2_.low = f32[10,32,128]{2,1,0:T(8,128)S(1)} collective-permute-done((f32[10,32,128]{2,1,0:T(8,128)S(1)}, f32[10,32,128]{2,1,0:T(8,128)S(1)}, u32[]{:S(2)}, u32[]{:S(2)}) %collective-permute-start.4) | collective-permute-done | bytes 163872 | tf_op jit(solution)/shard_map/ppermute | solution.py:963
  11.7 0.4 shard_map.154
  12.2 0.8 %collective-permute-start.6 = (f32[744,128]{1,0:T(8,128)S(1)}, f32[744,128]{1,0:T(8,128)S(1)}, u32[]{:S(2)}, u32[]{:S(2)}) collective-permute-start(f32[744,128]{1,0:T(8,128)S(1)} %get-tuple-element.52), channel_id=1, source_target_pairs={{0,1},{4,5},{8,9},{12,13},{1,0},{5,4},{9,8},{13,12},{2,3},{6,7},{1... | collective-permute-start | bytes 1142792 | tf_op jit(solution)/shard_map/ppermute | solution.py:963
  13.0 1.5 %collective-permute-start.7 = (f32[744,128]{1,0:T(8,128)S(1)}, f32[744,128]{1,0:T(8,128)S(1)}, u32[]{:S(2)}, u32[]{:S(2)}) collective-permute-start(f32[744,128]{1,0:T(8,128)S(1)} %get-tuple-element.53), channel_id=1, source_target_pairs={{0,4},{4,0},{8,12},{12,8},{1,2},{5,6},{9,10},{13,14},{2,1},{6,5},{... | collective-permute-start | bytes 1142792 | tf_op jit(solution)/shard_map/ppermute | solution.py:963
  14.5 0.8 %shard_map.152 = (f32[8,128]{1,0:T(8,128)S(1)}, f32[16,128]{1,0:T(8,128)S(1)}) custom-call(s32[64,32,128]{2,1,0:T(8,128)S(1)} %get-tuple-element.45.zone.refs_1_, f32[64,32,128]{2,1,0:T(8,128)S(1)} %get-tuple-element.46.scale.refs_0_, f32[64,32,128]{2,1,0:T(8,128)S(1)} %get-tuple-element.41.refs_0_.load, f32[296,128]{1,0:T(8,128)S(1)} %get-tuple-element.43.after, ...), custom_call_target="tpu_custom_call" | custom-call | tf_op jit(solution)/shard_map/pallas_call | solution.py:1036
  15.3 0.6 %collective-permute-done.3.right = f32[296,128]{1,0:T(8,128)S(1)} collective-permute-done((f32[296,128]{1,0:T(8,128)S(1)}, f32[296,128]{1,0:T(8,128)S(1)}, u32[]{:S(2)}, u32[]{:S(2)}) %collective-permute-start.3) | collective-permute-done | bytes 151584 | tf_op jit(solution)/shard_map/ppermute | solution.py:963
  16.0 4.1 %shard_map.153 = (f32[74,48,128]{2,1,0:T(8,128)S(1)}, f32[64,32,128]{2,1,0:T(8,128)S(1)}, f32[32,128]{1,0:T(8,128)S(1)}, f32[40,72,128]{2,1,0:T(8,128)S(1)}) custom-call(f32[64,32,128]{2,1,0:T(8,128)S(1)} %get-tuple-element.41.refs_0_.load, f32[4,32,128]{2,1,0:T(8,128)S(1)} %collective-permute-done.refs_1_.low, ...), custom_call_target="tpu_custom_call" | custom-call | flops 4000000000 | tf_op jit(solution)/shard_map/pallas_call | solution.py:1042
  20.1 0.5 %collective-permute-done.7.right = f32[744,128]{1,0:T(8,128)S(1)} collective-permute-done((f32[744,128]{1,0:T(8,128)S(1)}, f32[744,128]{1,0:T(8,128)S(1)}, u32[]{:S(2)}, u32[]{:S(2)}) %collective-permute-start.7) | collective-permute-done | bytes 380960 | tf_op jit(solution)/shard_map/ppermute | solution.py:963
  20.6 0.4 shard_map.155
  21.0 2.7 %collective-permute-start.10 = (f32[16,128]{1,0:T(8,128)S(1)}, f32[16,128]{1,0:T(8,128)S(1)}, u32[]{:S(2)}, u32[]{:S(2)}) collective-permute-start(f32[16,128]{1,0:T(8,128)S(1)} %get-tuple-element.57.refs_3_), channel_id=1, source_target_pairs={{0,8},{4,12},{8,0},{12,4},{1,9},{5,13},{9,1},{13,5},{2,10},{6,14},... | collective-permute-start | bytes 24584 | tf_op jit(solution)/shard_map/ppermute | solution.py:973
  23.7 1.2 %collective-permute-start.11 = (f32[16,128]{1,0:T(8,128)S(1)}, f32[16,128]{1,0:T(8,128)S(1)}, u32[]{:S(2)}, u32[]{:S(2)}) collective-permute-start(f32[16,128]{1,0:T(8,128)S(1)} %get-tuple-element.57.refs_3_), channel_id=1, source_target_pairs={{0,12},{4,8},{8,4},{12,0},{1,13},{5,9},{9,5},{13,1},{2,14},{6,10},... | collective-permute-start | bytes 24584 | tf_op jit(solution)/shard_map/ppermute | solution.py:968
  24.9 1.3 %shard_map.156 = (f32[74,48,128]{2,1,0:T(8,128)S(1)}, f32[74,48,128]{2,1,0:T(8,128)S(1)}, f32[74,48,128]{2,1,0:T(8,128)S(1)}, f32[74,48,128]{2,1,0:T(8,128)S(1)}) custom-call(s32[64,32,128]{2,1,0:T(8,128)S(1)} %get-tuple-element.45.zone.refs_1_, f32[64,32,128]{2,1,0:T(8,128)S(1)} %get-tuple-element.46.scale.refs_0_, ...), custom_call_target="tpu_custom_call" | custom-call | flops 1000000000 | tf_op jit(solution)/shard_map/pallas_call | solution.py:1058
  26.2 3.0 %collective-permute-done.11.refs_6_ = f32[16,128]{1,0:T(8,128)S(1)} collective-permute-done((f32[16,128]{1,0:T(8,128)S(1)}, f32[16,128]{1,0:T(8,128)S(1)}, u32[]{:S(2)}, u32[]{:S(2)}) %collective-permute-start.11) | collective-permute-done | bytes 8224 | tf_op jit(solution)/shard_map/ppermute | solution.py:968
  29.2 0.3 collective-permute-done.8.refs_1_.refs_4_.low
  29.5 0.2 shard_map.157
  29.8 2.0 %collective-permute-start.13 = (f32[392,128]{1,0:T(8,128)S(1)}, f32[392,128]{1,0:T(8,128)S(1)}, u32[]{:S(2)}, u32[]{:S(2)}) collective-permute-start(f32[392,128]{1,0:T(8,128)S(1)} %get-tuple-element.60), channel_id=1, source_target_pairs={{0,4},{4,0},{8,12},{12,8},{1,2},{5,6},{9,10},{13,14},{2,1},{6,5},{... | collective-permute-start | bytes 602120 | tf_op jit(solution)/shard_map/ppermute | solution.py:963
  31.8 0.3 collective-permute-start.14
  32.1 0.8 %shard_map.160 = (f32[74,48,128]{2,1,0:T(8,128)S(1)}, f32[74,48,128]{2,1,0:T(8,128)S(1)}) custom-call(f32[74,48,128]{2,1,0:T(8,128)S(1)} %get-tuple-element.64.zone_window, f32[74,48,128]{2,1,0:T(8,128)S(1)} %get-tuple-element.65.scale_window, f32[3,3]{1,0:T(4,128)S(1)} %copy-done, f32[1,3]{1,0:T(1,128)S(1)} %bitcast.3), custom_call_target="tpu_custom_call" | custom-call | flops 1000000000 | tf_op jit(solution)/shard_map/pallas_call | solution.py:1064
  33.0 2.8 %collective-permute-done.14.refs_1_ = f32[16,128]{1,0:T(8,128)S(1)} collective-permute-done((f32[16,128]{1,0:T(8,128)S(1)}, f32[16,128]{1,0:T(8,128)S(1)}, u32[]{:S(2)}, u32[]{:S(2)}) %collective-permute-start.14) | collective-permute-done | bytes 8224 | tf_op jit(solution)/shard_map/ppermute | solution.py:973
  35.8 0.9 %shard_map.159.answers = f32[8,128]{1,0:T(8,128)S(1)} custom-call(f32[16,128]{1,0:T(8,128)S(1)} %shard_map.158.refs_0_, f32[16,128]{1,0:T(8,128)S(1)} %collective-permute-done.14.refs_1_), custom_call_target="tpu_custom_call" | custom-call | tf_op jit(solution)/shard_map/pallas_call | solution.py:1079
  36.7 5.7 %shard_map.161 = (f32[64,32,128]{2,1,0:T(8,128)S(1)}, f32[32,128]{1,0:T(8,128)S(1)}, f32[32,128]{1,0:T(8,128)S(1)}, f32[64,128]{1,0:T(8,128)S(1)}, f32[64,128]{1,0:T(8,128)S(1)}, /*index=5*/f32[64,32,128]{2,1,0:T(8,128)}) custom-call(f32[64,32,128]{2,1,0:T(8,128)S(1)} %get-tuple-element.48.local.refs_0_, ...), custom_call_target="tpu_custom_call" | custom-call | flops 4000000000 | tf_op jit(solution)/shard_map/pallas_call | solution.py:1085
  42.4 2.0 %collective-permute-start.18 = (f32[64,128]{1,0:T(8,128)S(1)}, f32[64,128]{1,0:T(8,128)S(1)}, u32[]{:S(2)}, u32[]{:S(2)}) collective-permute-start(f32[64,128]{1,0:T(8,128)S(1)} %get-tuple-element.74), channel_id=1, source_target_pairs={{0,4},{4,0},{8,12},{12,8},{1,2},{5,6},{9,10},{13,14},{2,1},{6,5},{... | collective-permute-start | bytes 98312 | tf_op jit(solution)/shard_map/ppermute | solution.py:963
  44.6 1.9 %shard_map.162 = (f32[2,32,128]{2,1,0:T(8,128)S(1)}, f32[2,64,8,128]{3,2,1,0:T(8,128)S(1)}, f32[64,32,128]{2,1,0:T(8,128)}) custom-call(f32[64,32,128]{2,1,0:T(8,128)S(1)} %get-tuple-element.41.refs_0_.load, f32[64,32,128]{2,1,0:T(8,128)S(1)} %get-tuple-element.70.iterate, f32[74,48,128]{2,1,0:T(8,128)S(1)} %get-tuple-element.58.refs_7_.rest_0_.to_long, ...), custom_call_target="tpu_custom_call" | custom-call | flops 1000000000 | tf_op jit(solution)/shard_map/pallas_call | solution.py:1095
  46.5 1.7 %collective-permute-done.15.low = f32[32,128]{1,0:T(8,128)S(1)} collective-permute-done((f32[32,128]{1,0:T(8,128)S(1)}, f32[32,128]{1,0:T(8,128)S(1)}, u32[]{:S(2)}, u32[]{:S(2)}) %collective-permute-start.15) | collective-permute-done | bytes 16416 | tf_op jit(solution)/shard_map/ppermute | solution.py:963
  48.2 0.9 %shard_map.163 = f32[64,32,128]{2,1,0:T(8,128)} custom-call(f32[64,32,128]{2,1,0:T(8,128)S(1)} %get-tuple-element.70.iterate, f32[32,128]{1,0:T(8,128)S(1)} %collective-permute-done.15.low, f32[32,128]{1,0:T(8,128)S(1)} %collective-permute-done.16.high, f32[64,128]{1,0:T(8,128)S(1)} %collective-permute-done.17.left, ...), custom_call_target="tpu_custom_call", output_to_operand_aliasing={{}: (9, {})} | custom-call | tf_op jit(solution)/shard_map/pallas_call | solution.py:1107
  (43 shorter events, 0.4 us)
Async XLA Ops:
  1.8 8.2 %collective-permute-start = (f32[4,32,128]{2,1,0:T(8,128)S(1)}, f32[4,32,128]{2,1,0:T(8,128)S(1)}, u32[]{:S(2)}, u32[]{:S(2)}) collective-permute-start(f32[4,32,128]{2,1,0:T(8,128)S(1)} %get-tuple-element.40.after), channel_id=1, source_target_pairs={{0,4},{1,5},{2,6},{3,7},{4,0},{5,1},{6,2},{7,3},{8,12},{9,13},{10,... | collective-permute-start | bytes 196616 | tf_op jit(solution)/shard_map/ppermute | solution.py:963
  4.9 5.1 %collective-permute-start.1 = (f32[4,32,128]{2,1,0:T(8,128)S(1)}, f32[4,32,128]{2,1,0:T(8,128)S(1)}, u32[]{:S(2)}, u32[]{:S(2)}) collective-permute-start(f32[4,32,128]{2,1,0:T(8,128)S(1)} %get-tuple-element.42), channel_id=1, source_target_pairs={{0,1},{1,0},{2,3},{3,2},{4,8},{5,9},{6,10},{7,11},{8,4},{9,5},{10,... | collective-permute-start | bytes 196616 | tf_op jit(solution)/shard_map/ppermute | solution.py:963
  4.9 6.8 %collective-permute-start.4 = (f32[10,32,128]{2,1,0:T(8,128)S(1)}, f32[10,32,128]{2,1,0:T(8,128)S(1)}, u32[]{:S(2)}, u32[]{:S(2)}) collective-permute-start(f32[10,32,128]{2,1,0:T(8,128)S(1)} %get-tuple-element.50), channel_id=1, source_target_pairs={{0,4},{1,5},{2,6},{3,7},{4,0},{5,1},{6,2},{7,3},{8,12},{9,13},{10,... | collective-permute-start | bytes 491528 | tf_op jit(solution)/shard_map/ppermute | solution.py:963
  8.0 3.6 %collective-permute-start.5 = (f32[10,32,128]{2,1,0:T(8,128)S(1)}, f32[10,32,128]{2,1,0:T(8,128)S(1)}, u32[]{:S(2)}, u32[]{:S(2)}) collective-permute-start(f32[10,32,128]{2,1,0:T(8,128)S(1)} %get-tuple-element.51), channel_id=1, source_target_pairs={{0,1},{1,0},{2,3},{3,2},{4,8},{5,9},{6,10},{7,11},{8,4},{9,5},{10,... | collective-permute-start | bytes 491528 | tf_op jit(solution)/shard_map/ppermute | solution.py:963
  9.9 4.5 %copy-start = (f32[3,3]{1,0:T(4,128)S(1)}, f32[3,3]{1,0:T(4,128)}, u32[]{:S(2)}) copy-start(f32[3,3]{1,0:T(4,128)} %diffusivity.9) | copy-start | bytes 112
  10.0 4.5 %copy-start.1 = (f32[3]{0:T(128)S(1)}, f32[3]{0:T(128)}, u32[]{:S(2)}) copy-start(f32[3]{0:T(128)} %param.17) | copy-start | bytes 40
  10.2 5.1 %collective-permute-start.2 = (f32[296,128]{1,0:T(8,128)S(1)}, f32[296,128]{1,0:T(8,128)S(1)}, u32[]{:S(2)}, u32[]{:S(2)}) collective-permute-start(f32[296,128]{1,0:T(8,128)S(1)} %get-tuple-element.43.after), channel_id=1, source_target_pairs={{0,1},{4,5},{8,9},{12,13},{1,0},{5,4},{9,8},{13,12},{2,3},{6,7},{1... | collective-permute-start | bytes 454664 | tf_op jit(solution)/shard_map/ppermute | solution.py:963
  10.7 5.2 %collective-permute-start.3 = (f32[296,128]{1,0:T(8,128)S(1)}, f32[296,128]{1,0:T(8,128)S(1)}, u32[]{:S(2)}, u32[]{:S(2)}) collective-permute-start(f32[296,128]{1,0:T(8,128)S(1)} %get-tuple-element.44), channel_id=1, source_target_pairs={{0,4},{4,0},{8,12},{12,8},{1,2},{5,6},{9,10},{13,14},{2,1},{6,5},{... | collective-permute-start | bytes 454664 | tf_op jit(solution)/shard_map/ppermute | solution.py:963
  12.1 3.8 %copy-start.2 = (f32[256,256]{1,0:T(8,128)S(1)}, f32[256,256]{1,0:T(8,128)}, u32[]{:S(2)}) copy-start(f32[256,256]{1,0:T(8,128)} %constant.22.clone.rest_4_.rest_9_) | copy-start | bytes 786436
  12.1 3.8 %copy-start.3 = (f32[192,216]{1,0:T(8,128)S(1)}, f32[192,216]{1,0:T(8,128)}, u32[]{:S(2)}) copy-start(f32[192,216]{1,0:T(8,128)} %constant.20.clone.rest_2_.rest_7_) | copy-start | bytes 497668
  12.1 3.8 %copy-start.4 = (f32[144,144]{1,0:T(8,128)S(1)}, f32[144,144]{1,0:T(8,128)}, u32[]{:S(2)}) copy-start(f32[144,144]{1,0:T(8,128)} %constant.19.clone.rest_1_.rest_6_) | copy-start | bytes 248836
  12.1 3.8 %copy-start.5 = (f32[256,128]{1,0:T(8,128)S(1)}, f32[256,128]{1,0:T(8,128)}, u32[]{:S(2)}) copy-start(f32[256,128]{1,0:T(8,128)} %constant.23.clone.rest_5_.rest_10_) | copy-start | bytes 393220
  12.1 3.8 %copy-start.6 = (f32[96,120]{1,0:T(8,128)S(1)}, f32[96,120]{1,0:T(8,128)}, u32[]{:S(2)}) copy-start(f32[96,120]{1,0:T(8,128)} %constant.21.clone.rest_3_.rest_8_) | copy-start | bytes 138244
  12.2 3.8 %copy-start.7 = (f32[80,80]{1,0:T(8,128)S(1)}, f32[80,80]{1,0:T(8,128)}, u32[]{:S(2)}) copy-start(f32[80,80]{1,0:T(8,128)} %constant.18.clone.rest_0_.rest_5_) | copy-start | bytes 76804
  12.2 3.8 %copy-start.8 = (f32[72,128]{1,0:T(8,128)S(1)}, f32[72,128]{1,0:T(8,128)}, u32[]{:S(2)}) copy-start(f32[72,128]{1,0:T(8,128)} %constant.24.clone.rest_6_.rest_11_) | copy-start | bytes 110596
  12.2 3.8 %copy-start.9 = (f32[40,128]{1,0:T(8,128)S(1)}, f32[40,128]{1,0:T(8,128)}, u32[]{:S(2)}) copy-start(f32[40,128]{1,0:T(8,128)} %constant.25.clone.rest_7_.rest_12_) | copy-start | bytes 61444
  12.2 3.8 %copy-start.10 = (f32[1,128]{1,0:T(1,128)S(1)}, f32[1,128]{1,0:T(1,128)}, u32[]{:S(2)}) copy-start(f32[1,128]{1,0:T(1,128)} %constant.26.clone.rest_8_.rest_13_) | copy-start | bytes 1540
  12.2 7.9 %collective-permute-start.6 = (f32[744,128]{1,0:T(8,128)S(1)}, f32[744,128]{1,0:T(8,128)S(1)}, u32[]{:S(2)}, u32[]{:S(2)}) collective-permute-start(f32[744,128]{1,0:T(8,128)S(1)} %get-tuple-element.52), channel_id=1, source_target_pairs={{0,1},{4,5},{8,9},{12,13},{1,0},{5,4},{9,8},{13,12},{2,3},{6,7},{1... | collective-permute-start | bytes 1142792 | tf_op jit(solution)/shard_map/ppermute | solution.py:963
  13.0 7.6 %collective-permute-start.7 = (f32[744,128]{1,0:T(8,128)S(1)}, f32[744,128]{1,0:T(8,128)S(1)}, u32[]{:S(2)}, u32[]{:S(2)}) collective-permute-start(f32[744,128]{1,0:T(8,128)S(1)} %get-tuple-element.53), channel_id=1, source_target_pairs={{0,4},{4,0},{8,12},{12,8},{1,2},{5,6},{9,10},{13,14},{2,1},{6,5},{... | collective-permute-start | bytes 1142792 | tf_op jit(solution)/shard_map/ppermute | solution.py:963
  21.0 5.2 %collective-permute-start.10 = (f32[16,128]{1,0:T(8,128)S(1)}, f32[16,128]{1,0:T(8,128)S(1)}, u32[]{:S(2)}, u32[]{:S(2)}) collective-permute-start(f32[16,128]{1,0:T(8,128)S(1)} %get-tuple-element.57.refs_3_), channel_id=1, source_target_pairs={{0,8},{4,12},{8,0},{12,4},{1,9},{5,13},{9,1},{13,5},{2,10},{6,14},... | collective-permute-start | bytes 24584 | tf_op jit(solution)/shard_map/ppermute | solution.py:973
  23.7 5.6 %collective-permute-start.11 = (f32[16,128]{1,0:T(8,128)S(1)}, f32[16,128]{1,0:T(8,128)S(1)}, u32[]{:S(2)}, u32[]{:S(2)}) collective-permute-start(f32[16,128]{1,0:T(8,128)S(1)} %get-tuple-element.57.refs_3_), channel_id=1, source_target_pairs={{0,12},{4,8},{8,4},{12,0},{1,13},{5,9},{9,5},{13,1},{2,14},{6,10},... | collective-permute-start | bytes 24584 | tf_op jit(solution)/shard_map/ppermute | solution.py:968
  24.9 4.6 %collective-permute-start.8 = (f32[176,128]{1,0:T(8,128)S(1)}, f32[176,128]{1,0:T(8,128)S(1)}, u32[]{:S(2)}, u32[]{:S(2)}) collective-permute-start(f32[176,128]{1,0:T(8,128)S(1)} %get-tuple-element.55), channel_id=1, source_target_pairs={{0,4},{1,5},{2,6},{3,7},{4,0},{5,1},{6,2},{7,3},{8,12},{9,13},{10,... | collective-permute-start | bytes 270344 | tf_op jit(solution)/shard_map/ppermute | solution.py:963
  24.9 4.6 %collective-permute-start.9 = (f32[176,128]{1,0:T(8,128)S(1)}, f32[176,128]{1,0:T(8,128)S(1)}, u32[]{:S(2)}, u32[]{:S(2)}) collective-permute-start(f32[176,128]{1,0:T(8,128)S(1)} %get-tuple-element.56), channel_id=1, source_target_pairs={{0,1},{1,0},{2,3},{3,2},{4,8},{5,9},{6,10},{7,11},{8,4},{9,5},{10,... | collective-permute-start | bytes 270344 | tf_op jit(solution)/shard_map/ppermute | solution.py:963
  29.7 2.1 %collective-permute-start.12 = (f32[392,128]{1,0:T(8,128)S(1)}, f32[392,128]{1,0:T(8,128)S(1)}, u32[]{:S(2)}, u32[]{:S(2)}) collective-permute-start(f32[392,128]{1,0:T(8,128)S(1)} %get-tuple-element.59), channel_id=1, source_target_pairs={{0,1},{4,5},{8,9},{12,13},{1,0},{5,4},{9,8},{13,12},{2,3},{6,7},{1... | collective-permute-start | bytes 602120 | tf_op jit(solution)/shard_map/ppermute | solution.py:963
  29.8 6.9 %collective-permute-start.13 = (f32[392,128]{1,0:T(8,128)S(1)}, f32[392,128]{1,0:T(8,128)S(1)}, u32[]{:S(2)}, u32[]{:S(2)}) collective-permute-start(f32[392,128]{1,0:T(8,128)S(1)} %get-tuple-element.60), channel_id=1, source_target_pairs={{0,4},{4,0},{8,12},{12,8},{1,2},{5,6},{9,10},{13,14},{2,1},{6,5},{... | collective-permute-start | bytes 602120 | tf_op jit(solution)/shard_map/ppermute | solution.py:963
  31.8 4.0 %collective-permute-start.14 = (f32[16,128]{1,0:T(8,128)S(1)}, f32[16,128]{1,0:T(8,128)S(1)}, u32[]{:S(2)}, u32[]{:S(2)}) collective-permute-start(f32[16,128]{1,0:T(8,128)S(1)} %shard_map.158.refs_0_), channel_id=1, source_target_pairs={{0,2},{1,3},{2,0},{3,1},{4,6},{5,7},{6,4},{7,5},{8,10},{9,11},{10,... | collective-permute-start | bytes 24584 | tf_op jit(solution)/shard_map/ppermute | solution.py:973
  42.4 5.8 %collective-permute-start.17 = (f32[64,128]{1,0:T(8,128)S(1)}, f32[64,128]{1,0:T(8,128)S(1)}, u32[]{:S(2)}, u32[]{:S(2)}) collective-permute-start(f32[64,128]{1,0:T(8,128)S(1)} %get-tuple-element.73), channel_id=1, source_target_pairs={{0,1},{4,5},{8,9},{12,13},{1,0},{5,4},{9,8},{13,12},{2,3},{6,7},{1... | collective-permute-start | bytes 98312 | tf_op jit(solution)/shard_map/ppermute | solution.py:963
  42.4 5.8 %collective-permute-start.18 = (f32[64,128]{1,0:T(8,128)S(1)}, f32[64,128]{1,0:T(8,128)S(1)}, u32[]{:S(2)}, u32[]{:S(2)}) collective-permute-start(f32[64,128]{1,0:T(8,128)S(1)} %get-tuple-element.74), channel_id=1, source_target_pairs={{0,4},{4,0},{8,12},{12,8},{1,2},{5,6},{9,10},{13,14},{2,1},{6,5},{... | collective-permute-start | bytes 98312 | tf_op jit(solution)/shard_map/ppermute | solution.py:963
  44.4 3.7 %collective-permute-start.15 = (f32[32,128]{1,0:T(8,128)S(1)}, f32[32,128]{1,0:T(8,128)S(1)}, u32[]{:S(2)}, u32[]{:S(2)}) collective-permute-start(f32[32,128]{1,0:T(8,128)S(1)} %get-tuple-element.71), channel_id=1, source_target_pairs={{0,4},{1,5},{2,6},{3,7},{4,0},{5,1},{6,2},{7,3},{8,12},{9,13},{10,... | collective-permute-start | bytes 49160 | tf_op jit(solution)/shard_map/ppermute | solution.py:963
  44.5 3.7 %collective-permute-start.16 = (f32[32,128]{1,0:T(8,128)S(1)}, f32[32,128]{1,0:T(8,128)S(1)}, u32[]{:S(2)}, u32[]{:S(2)}) collective-permute-start(f32[32,128]{1,0:T(8,128)S(1)} %get-tuple-element.72), channel_id=1, source_target_pairs={{0,1},{1,0},{2,3},{3,2},{4,8},{5,9},{6,10},{7,11},{8,4},{9,5},{10,... | collective-permute-start | bytes 49160 | tf_op jit(solution)/shard_map/ppermute | solution.py:963

commit v21 on v20

--- a/solution.py
+++ b/solution.py
@@ -168,7 +168,7 @@
     return jnp.concatenate([values, blank], axis=0)
 
 
-FORWARD_ROWS, COLS_ABREAST, BACKWARD_ROWS = 72, 40, 64
+FORWARD_ROWS, COLS_ABREAST, BACKWARD_ROWS = 24, 40, 32
 
 
 def fitting(size, wanted):
@@ -332,22 +332,6 @@
         copy.wait()
 
 
-def bring_box(load, scale, zone, after, own_load, own_scale, own_zone, sems):
-    del after
-    parts = 4
-    size = own_load.shape[0] // parts
-    copies = []
-    for part in range(parts):
-        rows = slice(part * size, (part + 1) * size)
-        for source, target in ((load, own_load), (scale, own_scale), (zone, own_zone)):
-            copies.append(
-                pltpu.make_async_copy(source.at[rows], target.at[rows], sems.at[len(copies)])
-            )
-            copies[-1].start()
-    for copy in copies:
-        copy.wait()
-
-
 def fill_window(box, window, own, wide_sides, narrow_sides, wide, place, total, add=None):
     flat = window.reshape(box.flat, box.deep)
     nothing = jnp.zeros((box.rows, EDGE, box.deep), jnp.float32)
@@ -454,8 +438,19 @@
     return jnp.broadcast_to(line, shape)
 
 
-def box_sums(box, zone, scale, load, after, diffusivity, decay, out, table):
+def bring_box(
+    box, far_load, far_scale, far_zone, after, diffusivity, decay, load, scale, zone, out, table, sems
+):
     del after
+    size = 8
+    copies = []
+    for start in range(0, box.long, size):
+        rows = slice(start, start + size)
+        for source, target in ((far_load, load), (far_scale, scale), (far_zone, zone)):
+            copies.append(
+                pltpu.make_async_copy(source.at[rows], target.at[rows], sems.at[len(copies)])
+            )
+            copies[-1].start()
     nothing = jnp.zeros((box.across, box.deep), jnp.float32)
     half = [[0.5 * diffusivity[z : z + 1, d : d + 1] for z in range(3)] for d in range(3)]
     rates = [decay[0:1, z : z + 1] for z in range(3)]
@@ -465,8 +460,11 @@
         return [looked_up(labels, half[d]) * factor for d in range(3)] + [looked_up(labels, rates)]
 
     sums = [nothing] * 5
-    for row in range(box.long):
-        sums = [total + more for total, more in zip(sums, halves(row) + [load[row]])]
+    for start in range(0, box.long, size):
+        for copy in copies[start // size * 3 : start // size * 3 + 3]:
+            copy.wait()
+        for row in range(start, start + size):
+            sums = [total + more for total, more in zip(sums, halves(row) + [load[row]])]
 
     def total(values):
         return jnp.sum(values, axis=0, keepdims=True)
@@ -1023,21 +1021,16 @@
         [in_hbm] * 3,
         [pltpu.VMEM((2, REACH, across, deep), zone.dtype), pltpu.SemaphoreType.DMA((6,))],
     )(far_zone, far_scale, far_load)
-    load, scale, zone = call(
-        bring_box,
-        (cells, cells, whole_zone),
-        [in_hbm] * 3 + [anywhere],
-        [pltpu.SemaphoreType.DMA((12,))],
-    )(far_load, far_scale, far_zone, load_first)
+    load, scale, zone, sums, table = call(
+        functools.partial(bring_box, box),
+        (cells, cells, whole_zone, f32(8, 128), table_shape),
+        [in_hbm] * 3 + [anywhere] + [VMEM] * 2,
+        [pltpu.SemaphoreType.DMA((3 * (long // 8),))],
+    )(far_load, far_scale, far_zone, load_first, diffusivity, decay)
     load_wide = exchange("wide", load_first, load_second)
     far_wide = exchange("wide", first, second)
     load_first, load_second = pack(MARGIN, [load], load_wide)
     load_narrow = exchange("narrow", load_first, load_second)
-    sums, table = call(
-        functools.partial(box_sums, box),
-        (f32(8, 128), table_shape),
-        [VMEM] * 3 + [anywhere] + [VMEM] * 2,
-    )(zone, scale, load, load_first, diffusivity, decay)
     far_narrow = exchange("narrow", *pack(REACH, [scale, zone], far_wide))
     load_window, local, image, inverses = call(
         functools.partial(first_solve, box),

time: 49.5 us -> 49.4 us (level)
  waiting for transfers between devices: 9.69 us -> 10.5 us
  starting transfers between devices: 17.8 us -> 17.2 us
    ppermute x8, waiting for transfers between devices: 1.17 us -> 2.46 us  [exchange(): lax.ppermute(second, axes, ways[1])]
    ppermute x8, starting transfers between devices: 5.76 us -> 5.08 us  [exchange(): lax.ppermute(second, axes, ways[1])]
    ppermute x8, starting transfers between devices: 7.81 us -> 8.42 us  [exchange(): lax.ppermute(first, axes, ways[0])]
    pallas_call x2 -> x1, Pallas kernels: 2.76 us -> 2.31 us  [on_device(): call(functools.partial(bring_box, box), (cells, cells, whole_zone, f32(8,...]
  transfers between devices with their start and end apart: 19 -> 19, of which waited for: 7 -> 7; matrix products, arithmetic and copies ran while one was open for 0% -> 0% of each run, Pallas kernels for 25% -> 24%
where the time goes in v21:
time: 49.4 us; the launch traced here: 49.3 us
  Pallas kernels  20.4 us (41%)
  starting transfers between devices  17.2 us (35%)
  waiting for transfers between devices  10.5 us (21%)
  between operations  1.07 us (2%)
    ppermute x8, starting transfers between devices, exchange(): lax.ppermute(first, axes, ways[0])  8.42 us
    pallas_call x1, Pallas kernels, on_device(): call(functools.partial(second_solve, box), (cells, row, row, col, col, ce...  5.76 us
    ppermute x8, starting transfers between devices, exchange(): lax.ppermute(second, axes, ways[1])  5.08 us
    pallas_call x1, Pallas kernels, on_device(): call(functools.partial(first_solve, box), (window, cells, f32(across, dee...  4.12 us
    ppermute x1, waiting for transfers between devices, from_other_end(): return lax.ppermute(table, axis, [(i, size - 1 - i) for i in range(size)])  2.89 us
    ppermute x2, waiting for transfers between devices, two_away(): return lax.ppermute(table, axis, [(i, (i + 2) % size) for i in range(size)])  2.78 us
    ppermute x2, starting transfers between devices, two_away(): return lax.ppermute(table, axis, [(i, (i + 2) % size) for i in range(size)])  2.52 us
    ppermute x8, waiting for transfers between devices, exchange(): lax.ppermute(second, axes, ways[1])  2.46 us
  transfers between devices with their start and end apart: 19, of which 7 were waited for; matrix products, arithmetic and copies ran while one was open for 0% of the time, Pallas kernels for 24%

profile of v21, /device:TPU:0, one launch (start us, length us, event | category | flops | bytes accessed | tf_op | source)
XLA Modules:
  0.0 49.3 jit_solution(8450017876011016335)
XLA Ops:
  0.6 1.1 %shard_map.149 = (f32[4,32,128]{2,1,0:T(8,128)S(1)}, f32[4,32,128]{2,1,0:T(8,128)S(1)}, f32[10,32,128]{2,1,0:T(8,128)S(1)}, f32[10,32,128]{2,1,0:T(8,128)S(1)}) custom-call(s32[64,32,128]{2,1,0:T(8,128)} %far_zone.1, f32[64,32,128]{2,1,0:T(8,128)} %far_scale.1, f32[64,32,128]{2,1,0:T(8,128)} %far_load.1), custom_call_target="tpu_custom_call" | custom-call | tf_op jit(solution)/shard_map/pallas_call | solution.py:1018
  1.8 3.1 %collective-permute-start = (f32[4,32,128]{2,1,0:T(8,128)S(1)}, f32[4,32,128]{2,1,0:T(8,128)S(1)}, u32[]{:S(2)}, u32[]{:S(2)}) collective-permute-start(f32[4,32,128]{2,1,0:T(8,128)S(1)} %get-tuple-element.40.after), channel_id=1, source_target_pairs={{0,4},{1,5},{2,6},{3,7},{4,0},{5,1},{6,2},{7,3},{8,12},{9,13},{10,... | collective-permute-start | bytes 196616 | tf_op jit(solution)/shard_map/ppermute | solution.py:961
  4.9 3.1 %collective-permute-start.4 = (f32[10,32,128]{2,1,0:T(8,128)S(1)}, f32[10,32,128]{2,1,0:T(8,128)S(1)}, u32[]{:S(2)}, u32[]{:S(2)}) collective-permute-start(f32[10,32,128]{2,1,0:T(8,128)S(1)} %get-tuple-element.50), channel_id=1, source_target_pairs={{0,4},{1,5},{2,6},{3,7},{4,0},{5,1},{6,2},{7,3},{8,12},{9,13},{10,... | collective-permute-start | bytes 491528 | tf_op jit(solution)/shard_map/ppermute | solution.py:961
  8.0 2.3 %shard_map.150 = (f32[64,32,128]{2,1,0:T(8,128)S(1)}, f32[64,32,128]{2,1,0:T(8,128)S(1)}, s32[64,32,128]{2,1,0:T(8,128)S(1)}, f32[8,128]{1,0:T(8,128)S(1)}, f32[16,128]{1,0:T(8,128)S(1)}) custom-call(f32[64,32,128]{2,1,0:T(8,128)} %far_load.1, f32[64,32,128]{2,1,0:T(8,128)} %far_scale.1, s32[64,32,128]{2,1,0:T(8,128)} %far_zone.1, ...), custom_call_target="tpu_custom_call" | custom-call | tf_op jit(solution)/shard_map/pallas_call | solution.py:1024
  10.5 0.2 shard_map.151
  10.7 0.6 %collective-permute-start.2 = (f32[296,128]{1,0:T(8,128)S(1)}, f32[296,128]{1,0:T(8,128)S(1)}, u32[]{:S(2)}, u32[]{:S(2)}) collective-permute-start(f32[296,128]{1,0:T(8,128)S(1)} %get-tuple-element.43), channel_id=1, source_target_pairs={{0,1},{4,5},{8,9},{12,13},{1,0},{5,4},{9,8},{13,12},{2,3},{6,7},{1... | collective-permute-start | bytes 454664 | tf_op jit(solution)/shard_map/ppermute | solution.py:961
  11.3 0.4 collective-permute-done.4.refs_2_.low
  11.7 0.4 shard_map.153
  12.1 1.3 %collective-permute-start.6 = (f32[744,128]{1,0:T(8,128)S(1)}, f32[744,128]{1,0:T(8,128)S(1)}, u32[]{:S(2)}, u32[]{:S(2)}) collective-permute-start(f32[744,128]{1,0:T(8,128)S(1)} %get-tuple-element.52), channel_id=1, source_target_pairs={{0,1},{4,5},{8,9},{12,13},{1,0},{5,4},{9,8},{13,12},{2,3},{6,7},{1... | collective-permute-start | bytes 1142792 | tf_op jit(solution)/shard_map/ppermute | solution.py:961
  13.4 1.0 %collective-permute-start.7 = (f32[744,128]{1,0:T(8,128)S(1)}, f32[744,128]{1,0:T(8,128)S(1)}, u32[]{:S(2)}, u32[]{:S(2)}) collective-permute-start(f32[744,128]{1,0:T(8,128)S(1)} %get-tuple-element.53), channel_id=1, source_target_pairs={{0,4},{4,0},{8,12},{12,8},{1,2},{5,6},{9,10},{13,14},{2,1},{6,5},{... | collective-permute-start | bytes 1142792 | tf_op jit(solution)/shard_map/ppermute | solution.py:961
  14.4 2.1 %collective-permute-done.3.right = f32[296,128]{1,0:T(8,128)S(1)} collective-permute-done((f32[296,128]{1,0:T(8,128)S(1)}, f32[296,128]{1,0:T(8,128)S(1)}, u32[]{:S(2)}, u32[]{:S(2)}) %collective-permute-start.3) | collective-permute-done | bytes 151584 | tf_op jit(solution)/shard_map/ppermute | solution.py:961
  16.5 4.1 %shard_map.152 = (f32[74,48,128]{2,1,0:T(8,128)S(1)}, f32[64,32,128]{2,1,0:T(8,128)S(1)}, f32[32,128]{1,0:T(8,128)S(1)}, f32[40,72,128]{2,1,0:T(8,128)S(1)}) custom-call(f32[64,32,128]{2,1,0:T(8,128)S(1)} %get-tuple-element.41.refs_0_.load, f32[4,32,128]{2,1,0:T(8,128)S(1)} %collective-permute-done.refs_1_.low, ...), custom_call_target="tpu_custom_call" | custom-call | flops 4000000000 | tf_op jit(solution)/shard_map/pallas_call | solution.py:1035
  20.6 0.4 collective-permute-done.7.right
  21.0 0.4 shard_map.154
  21.4 2.2 %collective-permute-start.10 = (f32[16,128]{1,0:T(8,128)S(1)}, f32[16,128]{1,0:T(8,128)S(1)}, u32[]{:S(2)}, u32[]{:S(2)}) collective-permute-start(f32[16,128]{1,0:T(8,128)S(1)} %get-tuple-element.57.refs_3_), channel_id=1, source_target_pairs={{0,8},{4,12},{8,0},{12,4},{1,9},{5,13},{9,1},{13,5},{2,10},{6,14},... | collective-permute-start | bytes 24584 | tf_op jit(solution)/shard_map/ppermute | solution.py:971
  23.6 1.2 %collective-permute-start.11 = (f32[16,128]{1,0:T(8,128)S(1)}, f32[16,128]{1,0:T(8,128)S(1)}, u32[]{:S(2)}, u32[]{:S(2)}) collective-permute-start(f32[16,128]{1,0:T(8,128)S(1)} %get-tuple-element.57.refs_3_), channel_id=1, source_target_pairs={{0,12},{4,8},{8,4},{12,0},{1,13},{5,9},{9,5},{13,1},{2,14},{6,10},... | collective-permute-start | bytes 24584 | tf_op jit(solution)/shard_map/ppermute | solution.py:966
  24.8 0.1 collective-permute-start.8
  24.9 1.3 %shard_map.155 = (f32[74,48,128]{2,1,0:T(8,128)S(1)}, f32[74,48,128]{2,1,0:T(8,128)S(1)}, f32[74,48,128]{2,1,0:T(8,128)S(1)}, f32[74,48,128]{2,1,0:T(8,128)S(1)}) custom-call(s32[64,32,128]{2,1,0:T(8,128)S(1)} %get-tuple-element.46.zone.refs_1_, f32[64,32,128]{2,1,0:T(8,128)S(1)} %get-tuple-element.47.scale.refs_0_, ...), custom_call_target="tpu_custom_call" | custom-call | flops 1000000000 | tf_op jit(solution)/shard_map/pallas_call | solution.py:1051
  26.2 2.9 %collective-permute-done.11.refs_6_ = f32[16,128]{1,0:T(8,128)S(1)} collective-permute-done((f32[16,128]{1,0:T(8,128)S(1)}, f32[16,128]{1,0:T(8,128)S(1)}, u32[]{:S(2)}, u32[]{:S(2)}) %collective-permute-start.11) | collective-permute-done | bytes 8224 | tf_op jit(solution)/shard_map/ppermute | solution.py:966
  29.1 0.3 collective-permute-done.8.refs_1_.refs_4_.low
  29.4 0.2 shard_map.156
  29.7 2.0 %collective-permute-start.13 = (f32[392,128]{1,0:T(8,128)S(1)}, f32[392,128]{1,0:T(8,128)S(1)}, u32[]{:S(2)}, u32[]{:S(2)}) collective-permute-start(f32[392,128]{1,0:T(8,128)S(1)} %get-tuple-element.60), channel_id=1, source_target_pairs={{0,4},{4,0},{8,12},{12,8},{1,2},{5,6},{9,10},{13,14},{2,1},{6,5},{... | collective-permute-start | bytes 602120 | tf_op jit(solution)/shard_map/ppermute | solution.py:961
  31.7 0.3 collective-permute-start.14
  32.0 0.9 %shard_map.159 = (f32[74,48,128]{2,1,0:T(8,128)S(1)}, f32[74,48,128]{2,1,0:T(8,128)S(1)}) custom-call(f32[74,48,128]{2,1,0:T(8,128)S(1)} %get-tuple-element.64.zone_window, f32[74,48,128]{2,1,0:T(8,128)S(1)} %get-tuple-element.65.scale_window, f32[3,3]{1,0:T(4,128)S(1)} %copy-done, f32[1,3]{1,0:T(1,128)S(1)} %bitcast.3), custom_call_target="tpu_custom_call" | custom-call | flops 1000000000 | tf_op jit(solution)/shard_map/pallas_call | solution.py:1057
  32.9 2.8 %collective-permute-done.14.refs_1_ = f32[16,128]{1,0:T(8,128)S(1)} collective-permute-done((f32[16,128]{1,0:T(8,128)S(1)}, f32[16,128]{1,0:T(8,128)S(1)}, u32[]{:S(2)}, u32[]{:S(2)}) %collective-permute-start.14) | collective-permute-done | bytes 8224 | tf_op jit(solution)/shard_map/ppermute | solution.py:971
  35.7 0.9 %shard_map.158.answers = f32[8,128]{1,0:T(8,128)S(1)} custom-call(f32[16,128]{1,0:T(8,128)S(1)} %shard_map.157.refs_0_, f32[16,128]{1,0:T(8,128)S(1)} %collective-permute-done.14.refs_1_), custom_call_target="tpu_custom_call" | custom-call | tf_op jit(solution)/shard_map/pallas_call | solution.py:1072
  36.6 5.8 %shard_map.160 = (f32[64,32,128]{2,1,0:T(8,128)S(1)}, f32[32,128]{1,0:T(8,128)S(1)}, f32[32,128]{1,0:T(8,128)S(1)}, f32[64,128]{1,0:T(8,128)S(1)}, f32[64,128]{1,0:T(8,128)S(1)}, /*index=5*/f32[64,32,128]{2,1,0:T(8,128)}) custom-call(f32[64,32,128]{2,1,0:T(8,128)S(1)} %get-tuple-element.48.local.refs_0_, ...), custom_call_target="tpu_custom_call" | custom-call | flops 4000000000 | tf_op jit(solution)/shard_map/pallas_call | solution.py:1078
  42.4 2.0 %collective-permute-start.18 = (f32[64,128]{1,0:T(8,128)S(1)}, f32[64,128]{1,0:T(8,128)S(1)}, u32[]{:S(2)}, u32[]{:S(2)}) collective-permute-start(f32[64,128]{1,0:T(8,128)S(1)} %get-tuple-element.74), channel_id=1, source_target_pairs={{0,4},{4,0},{8,12},{12,8},{1,2},{5,6},{9,10},{13,14},{2,1},{6,5},{... | collective-permute-start | bytes 98312 | tf_op jit(solution)/shard_map/ppermute | solution.py:961
  44.4 0.1 collective-permute-start.15
  44.6 1.9 %shard_map.161 = (f32[2,32,128]{2,1,0:T(8,128)S(1)}, f32[2,64,8,128]{3,2,1,0:T(8,128)S(1)}, f32[64,32,128]{2,1,0:T(8,128)}) custom-call(f32[64,32,128]{2,1,0:T(8,128)S(1)} %get-tuple-element.41.refs_0_.load, f32[64,32,128]{2,1,0:T(8,128)S(1)} %get-tuple-element.70.iterate, f32[74,48,128]{2,1,0:T(8,128)S(1)} %get-tuple-element.58.refs_7_.rest_0_.to_long, ...), custom_call_target="tpu_custom_call" | custom-call | flops 1000000000 | tf_op jit(solution)/shard_map/pallas_call | solution.py:1088
  46.4 1.7 %collective-permute-done.15.low = f32[32,128]{1,0:T(8,128)S(1)} collective-permute-done((f32[32,128]{1,0:T(8,128)S(1)}, f32[32,128]{1,0:T(8,128)S(1)}, u32[]{:S(2)}, u32[]{:S(2)}) %collective-permute-start.15) | collective-permute-done | bytes 16416 | tf_op jit(solution)/shard_map/ppermute | solution.py:961
  48.2 0.9 %shard_map.162 = f32[64,32,128]{2,1,0:T(8,128)} custom-call(f32[64,32,128]{2,1,0:T(8,128)S(1)} %get-tuple-element.70.iterate, f32[32,128]{1,0:T(8,128)S(1)} %collective-permute-done.15.low, f32[32,128]{1,0:T(8,128)S(1)} %collective-permute-done.16.high, f32[64,128]{1,0:T(8,128)S(1)} %collective-permute-done.17.left, ...), custom_call_target="tpu_custom_call", output_to_operand_aliasing={{}: (9, {})} | custom-call | tf_op jit(solution)/shard_map/pallas_call | solution.py:1100
  (42 shorter events, 0.3 us)
Async XLA Ops:
  0.6 7.4 %copy-start.1 = (f32[3]{0:T(128)S(1)}, f32[3]{0:T(128)}, u32[]{:S(2)}) copy-start(f32[3]{0:T(128)} %param.17) | copy-start | bytes 40
  0.6 7.4 %copy-start = (f32[3,3]{1,0:T(4,128)S(1)}, f32[3,3]{1,0:T(4,128)}, u32[]{:S(2)}) copy-start(f32[3,3]{1,0:T(4,128)} %diffusivity.9) | copy-start | bytes 112
  1.8 8.7 %collective-permute-start = (f32[4,32,128]{2,1,0:T(8,128)S(1)}, f32[4,32,128]{2,1,0:T(8,128)S(1)}, u32[]{:S(2)}, u32[]{:S(2)}) collective-permute-start(f32[4,32,128]{2,1,0:T(8,128)S(1)} %get-tuple-element.40.after), channel_id=1, source_target_pairs={{0,4},{1,5},{2,6},{3,7},{4,0},{5,1},{6,2},{7,3},{8,12},{9,13},{10,... | collective-permute-start | bytes 196616 | tf_op jit(solution)/shard_map/ppermute | solution.py:961
  4.9 5.6 %collective-permute-start.1 = (f32[4,32,128]{2,1,0:T(8,128)S(1)}, f32[4,32,128]{2,1,0:T(8,128)S(1)}, u32[]{:S(2)}, u32[]{:S(2)}) collective-permute-start(f32[4,32,128]{2,1,0:T(8,128)S(1)} %get-tuple-element.42), channel_id=1, source_target_pairs={{0,1},{1,0},{2,3},{3,2},{4,8},{5,9},{6,10},{7,11},{8,4},{9,5},{10,... | collective-permute-start | bytes 196616 | tf_op jit(solution)/shard_map/ppermute | solution.py:961
  4.9 6.8 %collective-permute-start.4 = (f32[10,32,128]{2,1,0:T(8,128)S(1)}, f32[10,32,128]{2,1,0:T(8,128)S(1)}, u32[]{:S(2)}, u32[]{:S(2)}) collective-permute-start(f32[10,32,128]{2,1,0:T(8,128)S(1)} %get-tuple-element.50), channel_id=1, source_target_pairs={{0,4},{1,5},{2,6},{3,7},{4,0},{5,1},{6,2},{7,3},{8,12},{9,13},{10,... | collective-permute-start | bytes 491528 | tf_op jit(solution)/shard_map/ppermute | solution.py:961
  8.0 3.6 %collective-permute-start.5 = (f32[10,32,128]{2,1,0:T(8,128)S(1)}, f32[10,32,128]{2,1,0:T(8,128)S(1)}, u32[]{:S(2)}, u32[]{:S(2)}) collective-permute-start(f32[10,32,128]{2,1,0:T(8,128)S(1)} %get-tuple-element.51), channel_id=1, source_target_pairs={{0,1},{1,0},{2,3},{3,2},{4,8},{5,9},{6,10},{7,11},{8,4},{9,5},{10,... | collective-permute-start | bytes 491528 | tf_op jit(solution)/shard_map/ppermute | solution.py:961
  10.4 6.1 %copy-start.2 = (f32[256,256]{1,0:T(8,128)S(1)}, f32[256,256]{1,0:T(8,128)}, u32[]{:S(2)}) copy-start(f32[256,256]{1,0:T(8,128)} %constant.22.clone.rest_4_.rest_9_) | copy-start | bytes 786436
  10.4 6.1 %copy-start.3 = (f32[192,216]{1,0:T(8,128)S(1)}, f32[192,216]{1,0:T(8,128)}, u32[]{:S(2)}) copy-start(f32[192,216]{1,0:T(8,128)} %constant.20.clone.rest_2_.rest_7_) | copy-start | bytes 497668
  10.4 6.1 %copy-start.4 = (f32[144,144]{1,0:T(8,128)S(1)}, f32[144,144]{1,0:T(8,128)}, u32[]{:S(2)}) copy-start(f32[144,144]{1,0:T(8,128)} %constant.19.clone.rest_1_.rest_6_) | copy-start | bytes 248836
  10.4 6.0 %copy-start.5 = (f32[256,128]{1,0:T(8,128)S(1)}, f32[256,128]{1,0:T(8,128)}, u32[]{:S(2)}) copy-start(f32[256,128]{1,0:T(8,128)} %constant.23.clone.rest_5_.rest_10_) | copy-start | bytes 393220
  10.4 6.0 %copy-start.6 = (f32[96,120]{1,0:T(8,128)S(1)}, f32[96,120]{1,0:T(8,128)}, u32[]{:S(2)}) copy-start(f32[96,120]{1,0:T(8,128)} %constant.21.clone.rest_3_.rest_8_) | copy-start | bytes 138244
  10.4 6.0 %copy-start.7 = (f32[80,80]{1,0:T(8,128)S(1)}, f32[80,80]{1,0:T(8,128)}, u32[]{:S(2)}) copy-start(f32[80,80]{1,0:T(8,128)} %constant.18.clone.rest_0_.rest_5_) | copy-start | bytes 76804
  10.4 6.0 %copy-start.8 = (f32[72,128]{1,0:T(8,128)S(1)}, f32[72,128]{1,0:T(8,128)}, u32[]{:S(2)}) copy-start(f32[72,128]{1,0:T(8,128)} %constant.24.clone.rest_6_.rest_11_) | copy-start | bytes 110596
  10.5 6.0 %copy-start.9 = (f32[40,128]{1,0:T(8,128)S(1)}, f32[40,128]{1,0:T(8,128)}, u32[]{:S(2)}) copy-start(f32[40,128]{1,0:T(8,128)} %constant.25.clone.rest_7_.rest_12_) | copy-start | bytes 61444
  10.5 6.0 %copy-start.10 = (f32[1,128]{1,0:T(1,128)S(1)}, f32[1,128]{1,0:T(1,128)}, u32[]{:S(2)}) copy-start(f32[1,128]{1,0:T(1,128)} %constant.26.clone.rest_8_.rest_13_) | copy-start | bytes 1540
  10.7 3.7 %collective-permute-start.2 = (f32[296,128]{1,0:T(8,128)S(1)}, f32[296,128]{1,0:T(8,128)S(1)}, u32[]{:S(2)}, u32[]{:S(2)}) collective-permute-start(f32[296,128]{1,0:T(8,128)S(1)} %get-tuple-element.43), channel_id=1, source_target_pairs={{0,1},{4,5},{8,9},{12,13},{1,0},{5,4},{9,8},{13,12},{2,3},{6,7},{1... | collective-permute-start | bytes 454664 | tf_op jit(solution)/shard_map/ppermute | solution.py:961
  11.3 5.2 %collective-permute-start.3 = (f32[296,128]{1,0:T(8,128)S(1)}, f32[296,128]{1,0:T(8,128)S(1)}, u32[]{:S(2)}, u32[]{:S(2)}) collective-permute-start(f32[296,128]{1,0:T(8,128)S(1)} %get-tuple-element.44), channel_id=1, source_target_pairs={{0,4},{4,0},{8,12},{12,8},{1,2},{5,6},{9,10},{13,14},{2,1},{6,5},{... | collective-permute-start | bytes 454664 | tf_op jit(solution)/shard_map/ppermute | solution.py:961
  12.1 8.5 %collective-permute-start.6 = (f32[744,128]{1,0:T(8,128)S(1)}, f32[744,128]{1,0:T(8,128)S(1)}, u32[]{:S(2)}, u32[]{:S(2)}) collective-permute-start(f32[744,128]{1,0:T(8,128)S(1)} %get-tuple-element.52), channel_id=1, source_target_pairs={{0,1},{4,5},{8,9},{12,13},{1,0},{5,4},{9,8},{13,12},{2,3},{6,7},{1... | collective-permute-start | bytes 1142792 | tf_op jit(solution)/shard_map/ppermute | solution.py:961
  13.4 7.6 %collective-permute-start.7 = (f32[744,128]{1,0:T(8,128)S(1)}, f32[744,128]{1,0:T(8,128)S(1)}, u32[]{:S(2)}, u32[]{:S(2)}) collective-permute-start(f32[744,128]{1,0:T(8,128)S(1)} %get-tuple-element.53), channel_id=1, source_target_pairs={{0,4},{4,0},{8,12},{12,8},{1,2},{5,6},{9,10},{13,14},{2,1},{6,5},{... | collective-permute-start | bytes 1142792 | tf_op jit(solution)/shard_map/ppermute | solution.py:961
  21.4 4.8 %collective-permute-start.10 = (f32[16,128]{1,0:T(8,128)S(1)}, f32[16,128]{1,0:T(8,128)S(1)}, u32[]{:S(2)}, u32[]{:S(2)}) collective-permute-start(f32[16,128]{1,0:T(8,128)S(1)} %get-tuple-element.57.refs_3_), channel_id=1, source_target_pairs={{0,8},{4,12},{8,0},{12,4},{1,9},{5,13},{9,1},{13,5},{2,10},{6,14},... | collective-permute-start | bytes 24584 | tf_op jit(solution)/shard_map/ppermute | solution.py:971
  23.6 5.6 %collective-permute-start.11 = (f32[16,128]{1,0:T(8,128)S(1)}, f32[16,128]{1,0:T(8,128)S(1)}, u32[]{:S(2)}, u32[]{:S(2)}) collective-permute-start(f32[16,128]{1,0:T(8,128)S(1)} %get-tuple-element.57.refs_3_), channel_id=1, source_target_pairs={{0,12},{4,8},{8,4},{12,0},{1,13},{5,9},{9,5},{13,1},{2,14},{6,10},... | collective-permute-start | bytes 24584 | tf_op jit(solution)/shard_map/ppermute | solution.py:966
  24.8 4.6 %collective-permute-start.8 = (f32[176,128]{1,0:T(8,128)S(1)}, f32[176,128]{1,0:T(8,128)S(1)}, u32[]{:S(2)}, u32[]{:S(2)}) collective-permute-start(f32[176,128]{1,0:T(8,128)S(1)} %get-tuple-element.55), channel_id=1, source_target_pairs={{0,4},{1,5},{2,6},{3,7},{4,0},{5,1},{6,2},{7,3},{8,12},{9,13},{10,... | collective-permute-start | bytes 270344 | tf_op jit(solution)/shard_map/ppermute | solution.py:961
  24.9 4.5 %collective-permute-start.9 = (f32[176,128]{1,0:T(8,128)S(1)}, f32[176,128]{1,0:T(8,128)S(1)}, u32[]{:S(2)}, u32[]{:S(2)}) collective-permute-start(f32[176,128]{1,0:T(8,128)S(1)} %get-tuple-element.56), channel_id=1, source_target_pairs={{0,1},{1,0},{2,3},{3,2},{4,8},{5,9},{6,10},{7,11},{8,4},{9,5},{10,... | collective-permute-start | bytes 270344 | tf_op jit(solution)/shard_map/ppermute | solution.py:961
  29.6 2.1 %collective-permute-start.12 = (f32[392,128]{1,0:T(8,128)S(1)}, f32[392,128]{1,0:T(8,128)S(1)}, u32[]{:S(2)}, u32[]{:S(2)}) collective-permute-start(f32[392,128]{1,0:T(8,128)S(1)} %get-tuple-element.59), channel_id=1, source_target_pairs={{0,1},{4,5},{8,9},{12,13},{1,0},{5,4},{9,8},{13,12},{2,3},{6,7},{1... | collective-permute-start | bytes 602120 | tf_op jit(solution)/shard_map/ppermute | solution.py:961
  29.7 6.9 %collective-permute-start.13 = (f32[392,128]{1,0:T(8,128)S(1)}, f32[392,128]{1,0:T(8,128)S(1)}, u32[]{:S(2)}, u32[]{:S(2)}) collective-permute-start(f32[392,128]{1,0:T(8,128)S(1)} %get-tuple-element.60), channel_id=1, source_target_pairs={{0,4},{4,0},{8,12},{12,8},{1,2},{5,6},{9,10},{13,14},{2,1},{6,5},{... | collective-permute-start | bytes 602120 | tf_op jit(solution)/shard_map/ppermute | solution.py:961
  31.7 4.0 %collective-permute-start.14 = (f32[16,128]{1,0:T(8,128)S(1)}, f32[16,128]{1,0:T(8,128)S(1)}, u32[]{:S(2)}, u32[]{:S(2)}) collective-permute-start(f32[16,128]{1,0:T(8,128)S(1)} %shard_map.157.refs_0_), channel_id=1, source_target_pairs={{0,2},{1,3},{2,0},{3,1},{4,6},{5,7},{6,4},{7,5},{8,10},{9,11},{10,... | collective-permute-start | bytes 24584 | tf_op jit(solution)/shard_map/ppermute | solution.py:971
  42.3 5.8 %collective-permute-start.17 = (f32[64,128]{1,0:T(8,128)S(1)}, f32[64,128]{1,0:T(8,128)S(1)}, u32[]{:S(2)}, u32[]{:S(2)}) collective-permute-start(f32[64,128]{1,0:T(8,128)S(1)} %get-tuple-element.73), channel_id=1, source_target_pairs={{0,1},{4,5},{8,9},{12,13},{1,0},{5,4},{9,8},{13,12},{2,3},{6,7},{1... | collective-permute-start | bytes 98312 | tf_op jit(solution)/shard_map/ppermute | solution.py:961
  42.4 5.7 %collective-permute-start.18 = (f32[64,128]{1,0:T(8,128)S(1)}, f32[64,128]{1,0:T(8,128)S(1)}, u32[]{:S(2)}, u32[]{:S(2)}) collective-permute-start(f32[64,128]{1,0:T(8,128)S(1)} %get-tuple-element.74), channel_id=1, source_target_pairs={{0,4},{4,0},{8,12},{12,8},{1,2},{5,6},{9,10},{13,14},{2,1},{6,5},{... | collective-permute-start | bytes 98312 | tf_op jit(solution)/shard_map/ppermute | solution.py:961
  44.4 3.7 %collective-permute-start.15 = (f32[32,128]{1,0:T(8,128)S(1)}, f32[32,128]{1,0:T(8,128)S(1)}, u32[]{:S(2)}, u32[]{:S(2)}) collective-permute-start(f32[32,128]{1,0:T(8,128)S(1)} %get-tuple-element.71), channel_id=1, source_target_pairs={{0,4},{1,5},{2,6},{3,7},{4,0},{5,1},{6,2},{7,3},{8,12},{9,13},{10,... | collective-permute-start | bytes 49160 | tf_op jit(solution)/shard_map/ppermute | solution.py:961
  44.5 3.6 %collective-permute-start.16 = (f32[32,128]{1,0:T(8,128)S(1)}, f32[32,128]{1,0:T(8,128)S(1)}, u32[]{:S(2)}, u32[]{:S(2)}) collective-permute-start(f32[32,128]{1,0:T(8,128)S(1)} %get-tuple-element.72), channel_id=1, source_target_pairs={{0,1},{1,0},{2,3},{3,2},{4,8},{5,9},{6,10},{7,11},{8,4},{9,5},{10,... | collective-permute-start | bytes 49160 | tf_op jit(solution)/shard_map/ppermute | solution.py:961

commit v22 on v21

--- a/solution.py
+++ b/solution.py
@@ -494,7 +494,7 @@
 
 def first_solve(box, load, low, high, left, right, means, zone, scale, diffusivity, decay, *rest):
     tables = rest[:N_TABLES]
-    window, local, image, inverses, spectral, middle = rest[N_TABLES:]
+    window, local, image, inverses, first, second, spectral, middle = rest[N_TABLES:]
     spread_x, spread_y, eig_z = tables[6:]
     means = means_of(means)
     base = means[3] + means[0] * spread_x[...] + means[2] * eig_z[...]
@@ -537,6 +537,10 @@
         middle,
         emit,
     )
+    even = is_even("wide")
+    for target, pair in ((first, (box.long - REACH, 0)), (second, (0, box.long - REACH))):
+        rows = local[pl.ds(jnp.where(even, *pair), REACH)]
+        target[...] = rows.reshape(REACH * box.across, box.deep)
 
 
 def side_weights(
@@ -581,7 +585,7 @@
 
 
 def image_sums(
-    box, zone, scale, local, image, low, high, left, right, table, diffusivity, out, up, down
+    box, zone, scale, local, image, low, high, left, right, table, diffusivity, out
 ):
     half = [[0.5 * diffusivity[z : z + 1, d : d + 1] for z in range(3)] for d in range(3)]
     shape = (box.long * box.across, box.deep)
@@ -630,12 +634,6 @@
     ]
     known = table[...] + at_own_row(line_of(numbers, (8, out.shape[1])), out.shape)
     out[...] = known
-    edge = REACH * box.across
-    even = is_even("wide")
-    for target, pair in ((up, (box.long - REACH, 0)), (down, (0, box.long - REACH))):
-        target[:edge] = local[pl.ds(jnp.where(even, *pair), REACH)].reshape(edge, box.deep)
-        target[edge:] = known
-
 
 def column(values, index):
     return values[:, index : index + 1]
@@ -1032,22 +1030,23 @@
     load_first, load_second = pack(MARGIN, [load], load_wide)
     load_narrow = exchange("narrow", load_first, load_second)
     far_narrow = exchange("narrow", *pack(REACH, [scale, zone], far_wide))
-    load_window, local, image, inverses = call(
+    message = f32(REACH * across, deep)
+    load_window, local, image, inverses, first, second = call(
         functools.partial(first_solve, box),
-        (window, cells, f32(across, deep), f32(box.ey, box.ex, deep)),
+        (window, cells, f32(across, deep), f32(box.ey, box.ex, deep), message, message),
         [VMEM] * 8 + [VMEM] * 2 + [VMEM] * N_TABLES,
         [spectral, middle],
         flops=4 * 10**9,
     )(load, *load_wide, *load_narrow, sums, zone, scale, diffusivity, decay, *tables)
-    message = f32(REACH * across + count, deep)
-    table, first, second = call(
-        functools.partial(image_sums, box), (table_shape, message, message), [VMEM] * 9 + [VMEM]
-    )(zone, scale, local, image, *far_wide, *far_narrow, table, diffusivity)
+    wide = exchange("wide", first, second)
+    table = call(functools.partial(image_sums, box), table_shape, [VMEM] * 10)(
+        zone, scale, local, image, *far_wide, *far_narrow, table, diffusivity
+    )
     own_table = table
-    wide = exchange("wide", first, second)
-    parts = (table, wide[0])
+    parts = (table,)
     if by_margins:
-        parts += (two_away("wide", table), from_other_end("wide", table))
+        partner = lax.ppermute(table, ("wide", "narrow"), swaps("wide")[0])
+        parts += (partner, two_away("wide", table), from_other_end("wide", table))
     to_long, to_across, *windows = call(
         functools.partial(side_weights, box),
         (window,) * 4,

time: 49.4 us -> 48.6 us (0.984)
  waiting for transfers between devices: 10.5 us -> 9.54 us
    ppermute x8, starting transfers between devices: 5.08 us -> 1.55 us  [exchange(): lax.ppermute(second, axes, ways[1])]
    ppermute x0 -> x1, starting transfers between devices: none -> 1.89 us  [on_device(): partner = lax.ppermute(table, ('wide', 'narrow'), swaps('wide')[0])]
    ppermute x8, starting transfers between devices: 8.42 us -> 10.1 us  [exchange(): lax.ppermute(first, axes, ways[0])]
    ppermute x1, waiting for transfers between devices: 2.89 us -> 2.25 us  [from_other_end(): return lax.ppermute(table, axis, [(i, size - 1 - i) for i in range(size)])]
    ppermute x8, waiting for transfers between devices: 2.38 us -> 1.83 us  [exchange(): lax.ppermute(first, axes, ways[0])]
  transfers between devices with their start and end apart: 19 -> 20, of which waited for: 7 -> 8; matrix products, arithmetic and copies ran while one was open for 0% -> 0% of each run, Pallas kernels for 24% -> 26%
where the time goes in v22:
time: 48.6 us; the launch traced here: 48.4 us
  Pallas kernels  20.4 us (42%)
  starting transfers between devices  17.3 us (36%)
  waiting for transfers between devices  9.54 us (20%)
  between operations  1.09 us (2%)
    ppermute x8, starting transfers between devices, exchange(): lax.ppermute(first, axes, ways[0])  10.1 us
    pallas_call x1, Pallas kernels, on_device(): call(functools.partial(second_solve, box), (cells, row, row, col, col, ce...  5.7 us
    pallas_call x1, Pallas kernels, on_device(): call(functools.partial(first_solve, box), (window, cells, f32(across, dee...  4.17 us
    ppermute x2, waiting for transfers between devices, two_away(): return lax.ppermute(table, axis, [(i, (i + 2) % size) for i in range(size)])  3.2 us
    ppermute x2, starting transfers between devices, two_away(): return lax.ppermute(table, axis, [(i, (i + 2) % size) for i in range(size)])  2.33 us
    pallas_call x1, Pallas kernels, on_device(): call(functools.partial(bring_box, box), (cells, cells, whole_zone, f32(8,...  2.31 us
    ppermute x8, waiting for transfers between devices, exchange(): lax.ppermute(second, axes, ways[1])  2.26 us
    ppermute x1, waiting for transfers between devices, from_other_end(): return lax.ppermute(table, axis, [(i, size - 1 - i) for i in range(size)])  2.25 us
  transfers between devices with their start and end apart: 20, of which 8 were waited for; matrix products, arithmetic and copies ran while one was open for 0% of the time, Pallas kernels for 26%

profile of v22, /device:TPU:0, one launch (start us, length us, event | category | flops | bytes accessed | tf_op | source)
XLA Modules:
  0.0 48.4 jit_solution(1118457806180069031)
XLA Ops:
  0.6 1.1 %shard_map.149 = (f32[4,32,128]{2,1,0:T(8,128)S(1)}, f32[4,32,128]{2,1,0:T(8,128)S(1)}, f32[10,32,128]{2,1,0:T(8,128)S(1)}, f32[10,32,128]{2,1,0:T(8,128)S(1)}) custom-call(s32[64,32,128]{2,1,0:T(8,128)} %far_zone.1, f32[64,32,128]{2,1,0:T(8,128)} %far_scale.1, f32[64,32,128]{2,1,0:T(8,128)} %far_load.1), custom_call_target="tpu_custom_call" | custom-call | tf_op jit(solution)/shard_map/pallas_call | solution.py:1016
  1.8 3.1 %collective-permute-start = (f32[4,32,128]{2,1,0:T(8,128)S(1)}, f32[4,32,128]{2,1,0:T(8,128)S(1)}, u32[]{:S(2)}, u32[]{:S(2)}) collective-permute-start(f32[4,32,128]{2,1,0:T(8,128)S(1)} %get-tuple-element.39.after), channel_id=1, source_target_pairs={{0,4},{1,5},{2,6},{3,7},{4,0},{5,1},{6,2},{7,3},{8,12},{9,13},{10,... | collective-permute-start | bytes 196616 | tf_op jit(solution)/shard_map/ppermute | solution.py:959
  4.9 3.1 %collective-permute-start.6 = (f32[10,32,128]{2,1,0:T(8,128)S(1)}, f32[10,32,128]{2,1,0:T(8,128)S(1)}, u32[]{:S(2)}, u32[]{:S(2)}) collective-permute-start(f32[10,32,128]{2,1,0:T(8,128)S(1)} %get-tuple-element.51), channel_id=1, source_target_pairs={{0,4},{1,5},{2,6},{3,7},{4,0},{5,1},{6,2},{7,3},{8,12},{9,13},{10,... | collective-permute-start | bytes 491528 | tf_op jit(solution)/shard_map/ppermute | solution.py:959
  8.0 2.3 %shard_map.150 = (f32[64,32,128]{2,1,0:T(8,128)S(1)}, f32[64,32,128]{2,1,0:T(8,128)S(1)}, s32[64,32,128]{2,1,0:T(8,128)S(1)}, f32[8,128]{1,0:T(8,128)S(1)}, f32[16,128]{1,0:T(8,128)S(1)}) custom-call(f32[64,32,128]{2,1,0:T(8,128)} %far_load.1, f32[64,32,128]{2,1,0:T(8,128)} %far_scale.1, s32[64,32,128]{2,1,0:T(8,128)} %far_zone.1, ...), custom_call_target="tpu_custom_call" | custom-call | tf_op jit(solution)/shard_map/pallas_call | solution.py:1022
  10.5 0.2 shard_map.151
  10.7 0.6 %collective-permute-start.2 = (f32[296,128]{1,0:T(8,128)S(1)}, f32[296,128]{1,0:T(8,128)S(1)}, u32[]{:S(2)}, u32[]{:S(2)}) collective-permute-start(f32[296,128]{1,0:T(8,128)S(1)} %get-tuple-element.42), channel_id=1, source_target_pairs={{0,1},{4,5},{8,9},{12,13},{1,0},{5,4},{9,8},{13,12},{2,3},{6,7},{1... | collective-permute-start | bytes 454664 | tf_op jit(solution)/shard_map/ppermute | solution.py:959
  11.3 0.4 collective-permute-done.6.refs_2_.low
  11.7 0.4 shard_map.153
  12.1 1.3 %collective-permute-start.8 = (f32[744,128]{1,0:T(8,128)S(1)}, f32[744,128]{1,0:T(8,128)S(1)}, u32[]{:S(2)}, u32[]{:S(2)}) collective-permute-start(f32[744,128]{1,0:T(8,128)S(1)} %get-tuple-element.53), channel_id=1, source_target_pairs={{0,1},{4,5},{8,9},{12,13},{1,0},{5,4},{9,8},{13,12},{2,3},{6,7},{1... | collective-permute-start | bytes 1142792 | tf_op jit(solution)/shard_map/ppermute | solution.py:959
  13.4 1.0 %collective-permute-start.9 = (f32[744,128]{1,0:T(8,128)S(1)}, f32[744,128]{1,0:T(8,128)S(1)}, u32[]{:S(2)}, u32[]{:S(2)}) collective-permute-start(f32[744,128]{1,0:T(8,128)S(1)} %get-tuple-element.54), channel_id=1, source_target_pairs={{0,4},{4,0},{8,12},{12,8},{1,2},{5,6},{9,10},{13,14},{2,1},{6,5},{... | collective-permute-start | bytes 1142792 | tf_op jit(solution)/shard_map/ppermute | solution.py:959
  14.4 2.1 %collective-permute-done.3.right = f32[296,128]{1,0:T(8,128)S(1)} collective-permute-done((f32[296,128]{1,0:T(8,128)S(1)}, f32[296,128]{1,0:T(8,128)S(1)}, u32[]{:S(2)}, u32[]{:S(2)}) %collective-permute-start.3) | collective-permute-done | bytes 151584 | tf_op jit(solution)/shard_map/ppermute | solution.py:959
  16.5 4.2 %shard_map.152 = (f32[74,48,128]{2,1,0:T(8,128)S(1)}, f32[64,32,128]{2,1,0:T(8,128)S(1)}, f32[32,128]{1,0:T(8,128)S(1)}, f32[40,72,128]{2,1,0:T(8,128)S(1)}, f32...) custom-call(f32[64,32,128]{2,1,0:T(8,128)S(1)} %get-tuple-element.40.refs_0_.load, ...), custom_call_target="tpu_custom_call" | custom-call | flops 4000000000 | tf_op jit(solution)/shard_map/pallas_call | solution.py:1034
  21.0 0.4 shard_map.154.refs_3_
  21.4 1.9 %collective-permute-start.10 = (f32[16,128]{1,0:T(8,128)S(1)}, f32[16,128]{1,0:T(8,128)S(1)}, u32[]{:S(2)}, u32[]{:S(2)}) collective-permute-start(f32[16,128]{1,0:T(8,128)S(1)} %shard_map.154.refs_3_), channel_id=1, source_target_pairs={{0,4},{1,5},{2,6},{3,7},{4,0},{5,1},{6,2},{7,3},{8,12},{9,13},{10,... | collective-permute-start | bytes 24584 | tf_op jit(solution)/shard_map/ppermute | solution.py:1048
  23.3 1.4 %collective-permute-start.11 = (f32[16,128]{1,0:T(8,128)S(1)}, f32[16,128]{1,0:T(8,128)S(1)}, u32[]{:S(2)}, u32[]{:S(2)}) collective-permute-start(f32[16,128]{1,0:T(8,128)S(1)} %shard_map.154.refs_3_), channel_id=1, source_target_pairs={{0,8},{4,12},{8,0},{12,4},{1,9},{5,13},{9,1},{13,5},{2,10},{6,14},... | collective-permute-start | bytes 24584 | tf_op jit(solution)/shard_map/ppermute | solution.py:969
  24.7 1.4 %collective-permute-start.12 = (f32[16,128]{1,0:T(8,128)S(1)}, f32[16,128]{1,0:T(8,128)S(1)}, u32[]{:S(2)}, u32[]{:S(2)}) collective-permute-start(f32[16,128]{1,0:T(8,128)S(1)} %shard_map.154.refs_3_), channel_id=1, source_target_pairs={{0,12},{4,8},{8,4},{12,0},{1,13},{5,9},{9,5},{13,1},{2,14},{6,10},... | collective-permute-start | bytes 24584 | tf_op jit(solution)/shard_map/ppermute | solution.py:964
  26.1 1.3 %shard_map.155 = (f32[74,48,128]{2,1,0:T(8,128)S(1)}, f32[74,48,128]{2,1,0:T(8,128)S(1)}, f32[74,48,128]{2,1,0:T(8,128)S(1)}, f32[74,48,128]{2,1,0:T(8,128)S(1)}) custom-call(s32[64,32,128]{2,1,0:T(8,128)S(1)} %get-tuple-element.45.zone.refs_1_, f32[64,32,128]{2,1,0:T(8,128)S(1)} %get-tuple-element.46.scale.refs_0_, ...), custom_call_target="tpu_custom_call" | custom-call | flops 1000000000 | tf_op jit(solution)/shard_map/pallas_call | solution.py:1050
  27.5 0.4 collective-permute-done.11.refs_5_
  27.9 2.3 %collective-permute-done.12.refs_6_ = f32[16,128]{1,0:T(8,128)S(1)} collective-permute-done((f32[16,128]{1,0:T(8,128)S(1)}, f32[16,128]{1,0:T(8,128)S(1)}, u32[]{:S(2)}, u32[]{:S(2)}) %collective-permute-start.12) | collective-permute-done | bytes 8224 | tf_op jit(solution)/shard_map/ppermute | solution.py:964
  30.1 0.2 shard_map.156
  30.5 0.2 collective-permute-start.14
  30.7 1.2 %collective-permute-done.13.message.left = f32[392,128]{1,0:T(8,128)S(1)} collective-permute-done((f32[392,128]{1,0:T(8,128)S(1)}, f32[392,128]{1,0:T(8,128)S(1)}, u32[]{:S(2)}, u32[]{:S(2)}) %collective-permute-start.13) | collective-permute-done | bytes 200736 | tf_op jit(solution)/shard_map/ppermute | solution.py:959
  31.9 0.9 %collective-permute-start.15 = (f32[16,128]{1,0:T(8,128)S(1)}, f32[16,128]{1,0:T(8,128)S(1)}, u32[]{:S(2)}, u32[]{:S(2)}) collective-permute-start(f32[16,128]{1,0:T(8,128)S(1)} %shard_map.157.refs_0_), channel_id=1, source_target_pairs={{0,2},{1,3},{2,0},{3,1},{4,6},{5,7},{6,4},{7,5},{8,10},{9,11},{10,... | collective-permute-start | bytes 24584 | tf_op jit(solution)/shard_map/ppermute | solution.py:969
  32.8 0.9 %shard_map.159 = (f32[74,48,128]{2,1,0:T(8,128)S(1)}, f32[74,48,128]{2,1,0:T(8,128)S(1)}) custom-call(f32[74,48,128]{2,1,0:T(8,128)S(1)} %get-tuple-element.62.zone_window, f32[74,48,128]{2,1,0:T(8,128)S(1)} %get-tuple-element.63.scale_window, f32[3,3]{1,0:T(4,128)S(1)} %copy-done, f32[1,3]{1,0:T(1,128)S(1)} %bitcast.3), custom_call_target="tpu_custom_call" | custom-call | flops 1000000000 | tf_op jit(solution)/shard_map/pallas_call | solution.py:1056
  33.7 2.8 %collective-permute-done.15.refs_1_ = f32[16,128]{1,0:T(8,128)S(1)} collective-permute-done((f32[16,128]{1,0:T(8,128)S(1)}, f32[16,128]{1,0:T(8,128)S(1)}, u32[]{:S(2)}, u32[]{:S(2)}) %collective-permute-start.15) | collective-permute-done | bytes 8224 | tf_op jit(solution)/shard_map/ppermute | solution.py:969
  36.4 0.9 %shard_map.158.answers = f32[8,128]{1,0:T(8,128)S(1)} custom-call(f32[16,128]{1,0:T(8,128)S(1)} %shard_map.157.refs_0_, f32[16,128]{1,0:T(8,128)S(1)} %collective-permute-done.15.refs_1_), custom_call_target="tpu_custom_call" | custom-call | tf_op jit(solution)/shard_map/pallas_call | solution.py:1071
  37.3 5.7 %shard_map.160 = (f32[64,32,128]{2,1,0:T(8,128)S(1)}, f32[32,128]{1,0:T(8,128)S(1)}, f32[32,128]{1,0:T(8,128)S(1)}, f32[64,128]{1,0:T(8,128)S(1)}, f32[64,128]{1,0:T(8,128)S(1)}, /*index=5*/f32[64,32,128]{2,1,0:T(8,128)}) custom-call(f32[64,32,128]{2,1,0:T(8,128)S(1)} %get-tuple-element.47.local.refs_0_, f32[160,128]{1,0:T(8,128)S(1)} %collective-permute-done.4.refs_1_.low, ...), custom_call_target="tpu_custom_call" | custom-call | flops 4000000000 | tf_op jit(solution)/shard_map/pallas_call | solution.py:1077
  43.1 0.2 collective-permute-start.19
  43.3 1.9 %collective-permute-start.16 = (f32[32,128]{1,0:T(8,128)S(1)}, f32[32,128]{1,0:T(8,128)S(1)}, u32[]{:S(2)}, u32[]{:S(2)}) collective-permute-start(f32[32,128]{1,0:T(8,128)S(1)} %get-tuple-element.69), channel_id=1, source_target_pairs={{0,4},{1,5},{2,6},{3,7},{4,0},{5,1},{6,2},{7,3},{8,12},{9,13},{10,... | collective-permute-start | bytes 49160 | tf_op jit(solution)/shard_map/ppermute | solution.py:959
  45.2 1.9 %shard_map.161 = (f32[2,32,128]{2,1,0:T(8,128)S(1)}, f32[2,64,8,128]{3,2,1,0:T(8,128)S(1)}, f32[64,32,128]{2,1,0:T(8,128)}) custom-call(f32[64,32,128]{2,1,0:T(8,128)S(1)} %get-tuple-element.40.refs_0_.load, f32[64,32,128]{2,1,0:T(8,128)S(1)} %get-tuple-element.68.iterate, f32[74,48,128]{2,1,0:T(8,128)S(1)} %get-tuple-element.56.refs_7_.rest_0_.to_long, ...), custom_call_target="tpu_custom_call" | custom-call | flops 1000000000 | tf_op jit(solution)/shard_map/pallas_call | solution.py:1087
  47.1 0.2 collective-permute-done.16.low
  47.3 0.9 %shard_map.162 = f32[64,32,128]{2,1,0:T(8,128)} custom-call(f32[64,32,128]{2,1,0:T(8,128)S(1)} %get-tuple-element.68.iterate, f32[32,128]{1,0:T(8,128)S(1)} %collective-permute-done.16.low, f32[32,128]{1,0:T(8,128)S(1)} %collective-permute-done.17.high, f32[64,128]{1,0:T(8,128)S(1)} %collective-permute-done.18.left, ...), custom_call_target="tpu_custom_call", output_to_operand_aliasing={{}: (9, {})} | custom-call | tf_op jit(solution)/shard_map/pallas_call | solution.py:1099
  (44 shorter events, 0.6 us)
Async XLA Ops:
  0.6 7.4 %copy-start.1 = (f32[3]{0:T(128)S(1)}, f32[3]{0:T(128)}, u32[]{:S(2)}) copy-start(f32[3]{0:T(128)} %param.17) | copy-start | bytes 40
  0.6 7.4 %copy-start = (f32[3,3]{1,0:T(4,128)S(1)}, f32[3,3]{1,0:T(4,128)}, u32[]{:S(2)}) copy-start(f32[3,3]{1,0:T(4,128)} %diffusivity.9) | copy-start | bytes 112
  1.8 8.7 %collective-permute-start = (f32[4,32,128]{2,1,0:T(8,128)S(1)}, f32[4,32,128]{2,1,0:T(8,128)S(1)}, u32[]{:S(2)}, u32[]{:S(2)}) collective-permute-start(f32[4,32,128]{2,1,0:T(8,128)S(1)} %get-tuple-element.39.after), channel_id=1, source_target_pairs={{0,4},{1,5},{2,6},{3,7},{4,0},{5,1},{6,2},{7,3},{8,12},{9,13},{10,... | collective-permute-start | bytes 196616 | tf_op jit(solution)/shard_map/ppermute | solution.py:959
  4.9 5.6 %collective-permute-start.1 = (f32[4,32,128]{2,1,0:T(8,128)S(1)}, f32[4,32,128]{2,1,0:T(8,128)S(1)}, u32[]{:S(2)}, u32[]{:S(2)}) collective-permute-start(f32[4,32,128]{2,1,0:T(8,128)S(1)} %get-tuple-element.41), channel_id=1, source_target_pairs={{0,1},{1,0},{2,3},{3,2},{4,8},{5,9},{6,10},{7,11},{8,4},{9,5},{10,... | collective-permute-start | bytes 196616 | tf_op jit(solution)/shard_map/ppermute | solution.py:959
  4.9 6.8 %collective-permute-start.6 = (f32[10,32,128]{2,1,0:T(8,128)S(1)}, f32[10,32,128]{2,1,0:T(8,128)S(1)}, u32[]{:S(2)}, u32[]{:S(2)}) collective-permute-start(f32[10,32,128]{2,1,0:T(8,128)S(1)} %get-tuple-element.51), channel_id=1, source_target_pairs={{0,4},{1,5},{2,6},{3,7},{4,0},{5,1},{6,2},{7,3},{8,12},{9,13},{10,... | collective-permute-start | bytes 491528 | tf_op jit(solution)/shard_map/ppermute | solution.py:959
  8.0 3.6 %collective-permute-start.7 = (f32[10,32,128]{2,1,0:T(8,128)S(1)}, f32[10,32,128]{2,1,0:T(8,128)S(1)}, u32[]{:S(2)}, u32[]{:S(2)}) collective-permute-start(f32[10,32,128]{2,1,0:T(8,128)S(1)} %get-tuple-element.52), channel_id=1, source_target_pairs={{0,1},{1,0},{2,3},{3,2},{4,8},{5,9},{6,10},{7,11},{8,4},{9,5},{10,... | collective-permute-start | bytes 491528 | tf_op jit(solution)/shard_map/ppermute | solution.py:959
  10.4 6.1 %copy-start.2 = (f32[256,256]{1,0:T(8,128)S(1)}, f32[256,256]{1,0:T(8,128)}, u32[]{:S(2)}) copy-start(f32[256,256]{1,0:T(8,128)} %constant.22.clone.rest_4_.rest_9_) | copy-start | bytes 786436
  10.4 6.1 %copy-start.3 = (f32[192,216]{1,0:T(8,128)S(1)}, f32[192,216]{1,0:T(8,128)}, u32[]{:S(2)}) copy-start(f32[192,216]{1,0:T(8,128)} %constant.20.clone.rest_2_.rest_7_) | copy-start | bytes 497668
  10.4 6.1 %copy-start.4 = (f32[144,144]{1,0:T(8,128)S(1)}, f32[144,144]{1,0:T(8,128)}, u32[]{:S(2)}) copy-start(f32[144,144]{1,0:T(8,128)} %constant.19.clone.rest_1_.rest_6_) | copy-start | bytes 248836
  10.4 6.0 %copy-start.5 = (f32[256,128]{1,0:T(8,128)S(1)}, f32[256,128]{1,0:T(8,128)}, u32[]{:S(2)}) copy-start(f32[256,128]{1,0:T(8,128)} %constant.23.clone.rest_5_.rest_10_) | copy-start | bytes 393220
  10.4 6.0 %copy-start.6 = (f32[96,120]{1,0:T(8,128)S(1)}, f32[96,120]{1,0:T(8,128)}, u32[]{:S(2)}) copy-start(f32[96,120]{1,0:T(8,128)} %constant.21.clone.rest_3_.rest_8_) | copy-start | bytes 138244
  10.4 6.0 %copy-start.7 = (f32[80,80]{1,0:T(8,128)S(1)}, f32[80,80]{1,0:T(8,128)}, u32[]{:S(2)}) copy-start(f32[80,80]{1,0:T(8,128)} %constant.18.clone.rest_0_.rest_5_) | copy-start | bytes 76804
  10.4 6.0 %copy-start.8 = (f32[72,128]{1,0:T(8,128)S(1)}, f32[72,128]{1,0:T(8,128)}, u32[]{:S(2)}) copy-start(f32[72,128]{1,0:T(8,128)} %constant.24.clone.rest_6_.rest_11_) | copy-start | bytes 110596
  10.5 6.0 %copy-start.9 = (f32[40,128]{1,0:T(8,128)S(1)}, f32[40,128]{1,0:T(8,128)}, u32[]{:S(2)}) copy-start(f32[40,128]{1,0:T(8,128)} %constant.25.clone.rest_7_.rest_12_) | copy-start | bytes 61444
  10.5 6.0 %copy-start.10 = (f32[1,128]{1,0:T(1,128)S(1)}, f32[1,128]{1,0:T(1,128)}, u32[]{:S(2)}) copy-start(f32[1,128]{1,0:T(1,128)} %constant.26.clone.rest_8_.rest_13_) | copy-start | bytes 1540
  10.7 3.7 %collective-permute-start.2 = (f32[296,128]{1,0:T(8,128)S(1)}, f32[296,128]{1,0:T(8,128)S(1)}, u32[]{:S(2)}, u32[]{:S(2)}) collective-permute-start(f32[296,128]{1,0:T(8,128)S(1)} %get-tuple-element.42), channel_id=1, source_target_pairs={{0,1},{4,5},{8,9},{12,13},{1,0},{5,4},{9,8},{13,12},{2,3},{6,7},{1... | collective-permute-start | bytes 454664 | tf_op jit(solution)/shard_map/ppermute | solution.py:959
  11.3 5.2 %collective-permute-start.3 = (f32[296,128]{1,0:T(8,128)S(1)}, f32[296,128]{1,0:T(8,128)S(1)}, u32[]{:S(2)}, u32[]{:S(2)}) collective-permute-start(f32[296,128]{1,0:T(8,128)S(1)} %get-tuple-element.43), channel_id=1, source_target_pairs={{0,4},{4,0},{8,12},{12,8},{1,2},{5,6},{9,10},{13,14},{2,1},{6,5},{... | collective-permute-start | bytes 454664 | tf_op jit(solution)/shard_map/ppermute | solution.py:959
  12.1 8.7 %collective-permute-start.8 = (f32[744,128]{1,0:T(8,128)S(1)}, f32[744,128]{1,0:T(8,128)S(1)}, u32[]{:S(2)}, u32[]{:S(2)}) collective-permute-start(f32[744,128]{1,0:T(8,128)S(1)} %get-tuple-element.53), channel_id=1, source_target_pairs={{0,1},{4,5},{8,9},{12,13},{1,0},{5,4},{9,8},{13,12},{2,3},{6,7},{1... | collective-permute-start | bytes 1142792 | tf_op jit(solution)/shard_map/ppermute | solution.py:959
  13.4 7.6 %collective-permute-start.9 = (f32[744,128]{1,0:T(8,128)S(1)}, f32[744,128]{1,0:T(8,128)S(1)}, u32[]{:S(2)}, u32[]{:S(2)}) collective-permute-start(f32[744,128]{1,0:T(8,128)S(1)} %get-tuple-element.54), channel_id=1, source_target_pairs={{0,4},{4,0},{8,12},{12,8},{1,2},{5,6},{9,10},{13,14},{2,1},{6,5},{... | collective-permute-start | bytes 1142792 | tf_op jit(solution)/shard_map/ppermute | solution.py:959
  20.7 6.8 %collective-permute-start.4 = (f32[160,128]{1,0:T(8,128)S(1)}, f32[160,128]{1,0:T(8,128)S(1)}, u32[]{:S(2)}, u32[]{:S(2)}) collective-permute-start(f32[160,128]{1,0:T(8,128)S(1)} %get-tuple-element.48), channel_id=1, source_target_pairs={{0,4},{1,5},{2,6},{3,7},{4,0},{5,1},{6,2},{7,3},{8,12},{9,13},{10,... | collective-permute-start | bytes 245768 | tf_op jit(solution)/shard_map/ppermute | solution.py:959
  20.8 6.7 %collective-permute-start.5 = (f32[160,128]{1,0:T(8,128)S(1)}, f32[160,128]{1,0:T(8,128)S(1)}, u32[]{:S(2)}, u32[]{:S(2)}) collective-permute-start(f32[160,128]{1,0:T(8,128)S(1)} %get-tuple-element.49), channel_id=1, source_target_pairs={{0,1},{1,0},{2,3},{3,2},{4,8},{5,9},{6,10},{7,11},{8,4},{9,5},{10,... | collective-permute-start | bytes 245768 | tf_op jit(solution)/shard_map/ppermute | solution.py:959
  21.4 6.1 %collective-permute-start.10 = (f32[16,128]{1,0:T(8,128)S(1)}, f32[16,128]{1,0:T(8,128)S(1)}, u32[]{:S(2)}, u32[]{:S(2)}) collective-permute-start(f32[16,128]{1,0:T(8,128)S(1)} %shard_map.154.refs_3_), channel_id=1, source_target_pairs={{0,4},{1,5},{2,6},{3,7},{4,0},{5,1},{6,2},{7,3},{8,12},{9,13},{10,... | collective-permute-start | bytes 24584 | tf_op jit(solution)/shard_map/ppermute | solution.py:1048
  23.3 4.6 %collective-permute-start.11 = (f32[16,128]{1,0:T(8,128)S(1)}, f32[16,128]{1,0:T(8,128)S(1)}, u32[]{:S(2)}, u32[]{:S(2)}) collective-permute-start(f32[16,128]{1,0:T(8,128)S(1)} %shard_map.154.refs_3_), channel_id=1, source_target_pairs={{0,8},{4,12},{8,0},{12,4},{1,9},{5,13},{9,1},{13,5},{2,10},{6,14},... | collective-permute-start | bytes 24584 | tf_op jit(solution)/shard_map/ppermute | solution.py:969
  24.7 5.4 %collective-permute-start.12 = (f32[16,128]{1,0:T(8,128)S(1)}, f32[16,128]{1,0:T(8,128)S(1)}, u32[]{:S(2)}, u32[]{:S(2)}) collective-permute-start(f32[16,128]{1,0:T(8,128)S(1)} %shard_map.154.refs_3_), channel_id=1, source_target_pairs={{0,12},{4,8},{8,4},{12,0},{1,13},{5,9},{9,5},{13,1},{2,14},{6,10},... | collective-permute-start | bytes 24584 | tf_op jit(solution)/shard_map/ppermute | solution.py:964
  30.4 1.5 %collective-permute-start.13 = (f32[392,128]{1,0:T(8,128)S(1)}, f32[392,128]{1,0:T(8,128)S(1)}, u32[]{:S(2)}, u32[]{:S(2)}) collective-permute-start(f32[392,128]{1,0:T(8,128)S(1)} %get-tuple-element.57), channel_id=1, source_target_pairs={{0,1},{4,5},{8,9},{12,13},{1,0},{5,4},{9,8},{13,12},{2,3},{6,7},{1... | collective-permute-start | bytes 602120 | tf_op jit(solution)/shard_map/ppermute | solution.py:959
  30.5 6.9 %collective-permute-start.14 = (f32[392,128]{1,0:T(8,128)S(1)}, f32[392,128]{1,0:T(8,128)S(1)}, u32[]{:S(2)}, u32[]{:S(2)}) collective-permute-start(f32[392,128]{1,0:T(8,128)S(1)} %get-tuple-element.58), channel_id=1, source_target_pairs={{0,4},{4,0},{8,12},{12,8},{1,2},{5,6},{9,10},{13,14},{2,1},{6,5},{... | collective-permute-start | bytes 602120 | tf_op jit(solution)/shard_map/ppermute | solution.py:959
  31.9 4.6 %collective-permute-start.15 = (f32[16,128]{1,0:T(8,128)S(1)}, f32[16,128]{1,0:T(8,128)S(1)}, u32[]{:S(2)}, u32[]{:S(2)}) collective-permute-start(f32[16,128]{1,0:T(8,128)S(1)} %shard_map.157.refs_0_), channel_id=1, source_target_pairs={{0,2},{1,3},{2,0},{3,1},{4,6},{5,7},{6,4},{7,5},{8,10},{9,11},{10,... | collective-permute-start | bytes 24584 | tf_op jit(solution)/shard_map/ppermute | solution.py:969
  43.0 4.2 %collective-permute-start.18 = (f32[64,128]{1,0:T(8,128)S(1)}, f32[64,128]{1,0:T(8,128)S(1)}, u32[]{:S(2)}, u32[]{:S(2)}) collective-permute-start(f32[64,128]{1,0:T(8,128)S(1)} %get-tuple-element.71), channel_id=1, source_target_pairs={{0,1},{4,5},{8,9},{12,13},{1,0},{5,4},{9,8},{13,12},{2,3},{6,7},{1... | collective-permute-start | bytes 98312 | tf_op jit(solution)/shard_map/ppermute | solution.py:959
  43.1 4.2 %collective-permute-start.19 = (f32[64,128]{1,0:T(8,128)S(1)}, f32[64,128]{1,0:T(8,128)S(1)}, u32[]{:S(2)}, u32[]{:S(2)}) collective-permute-start(f32[64,128]{1,0:T(8,128)S(1)} %get-tuple-element.72), channel_id=1, source_target_pairs={{0,4},{4,0},{8,12},{12,8},{1,2},{5,6},{9,10},{13,14},{2,1},{6,5},{... | collective-permute-start | bytes 98312 | tf_op jit(solution)/shard_map/ppermute | solution.py:959
  43.3 3.9 %collective-permute-start.16 = (f32[32,128]{1,0:T(8,128)S(1)}, f32[32,128]{1,0:T(8,128)S(1)}, u32[]{:S(2)}, u32[]{:S(2)}) collective-permute-start(f32[32,128]{1,0:T(8,128)S(1)} %get-tuple-element.69), channel_id=1, source_target_pairs={{0,4},{1,5},{2,6},{3,7},{4,0},{5,1},{6,2},{7,3},{8,12},{9,13},{10,... | collective-permute-start | bytes 49160 | tf_op jit(solution)/shard_map/ppermute | solution.py:959
  45.2 2.1 %collective-permute-start.17 = (f32[32,128]{1,0:T(8,128)S(1)}, f32[32,128]{1,0:T(8,128)S(1)}, u32[]{:S(2)}, u32[]{:S(2)}) collective-permute-start(f32[32,128]{1,0:T(8,128)S(1)} %get-tuple-element.70), channel_id=1, source_target_pairs={{0,1},{1,0},{2,3},{3,2},{4,8},{5,9},{6,10},{7,11},{8,4},{9,5},{10,... | collective-permute-start | bytes 49160 | tf_op jit(solution)/shard_map/ppermute | solution.py:959

commit v23 on v22

--- a/solution.py
+++ b/solution.py
@@ -959,11 +959,6 @@
     return lax.ppermute(first, axes, ways[0]), lax.ppermute(second, axes, ways[1])
 
 
-def from_other_end(axis, table):
-    size = lax.axis_size(axis)
-    return lax.ppermute(table, axis, [(i, size - 1 - i) for i in range(size)])
-
-
 def two_away(axis, table):
     size = lax.axis_size(axis)
     return lax.ppermute(table, axis, [(i, (i + 2) % size) for i in range(size)])
@@ -1046,7 +1041,8 @@
     parts = (table,)
     if by_margins:
         partner = lax.ppermute(table, ("wide", "narrow"), swaps("wide")[0])
-        parts += (partner, two_away("wide", table), from_other_end("wide", table))
+        table = call(join_rows, table_shape, [VMEM] * 2)(table, partner)
+        parts = (table, two_away("wide", table))
     to_long, to_across, *windows = call(
         functools.partial(side_weights, box),
         (window,) * 4,

time: 48.6 us -> 48.7 us (level)
    ppermute x1 -> x0, waiting for transfers between devices: 2.25 us -> none  [from_other_end(): return lax.ppermute(table, axis, [(i, size - 1 - i) for i in range(size)])]
    ppermute x1, waiting for transfers between devices: 0.01 us -> 1.71 us  [on_device(): partner = lax.ppermute(table, ('wide', 'narrow'), swaps('wide')[0])]
    ppermute x8, starting transfers between devices: 1.55 us -> 3.23 us  [exchange(): lax.ppermute(second, axes, ways[1])]
    ppermute x1 -> x0, starting transfers between devices: 1.4 us -> none  [from_other_end(): return lax.ppermute(table, axis, [(i, size - 1 - i) for i in range(size)])]
    ppermute x1, starting transfers between devices: 1.89 us -> 1 us  [on_device(): partner = lax.ppermute(table, ('wide', 'narrow'), swaps('wide')[0])]
    ppermute x2, waiting for transfers between devices: 3.2 us -> 4.07 us  [two_away(): return lax.ppermute(table, axis, [(i, (i + 2) % size) for i in range(size)])]
    ppermute x2, starting transfers between devices: 2.33 us -> 2.85 us  [two_away(): return lax.ppermute(table, axis, [(i, (i + 2) % size) for i in range(size)])]
  transfers between devices with their start and end apart: 20 -> 19, of which waited for: 8 -> 8; matrix products, arithmetic and copies ran while one was open for 0% -> 0% of each run, Pallas kernels for 26% -> 25%
where the time goes in v23:
time: 48.7 us; the launch traced here: 48.5 us
  Pallas kernels  20.3 us (42%)
  starting transfers between devices  17.3 us (36%)
  waiting for transfers between devices  9.82 us (20%)
  between operations  1.07 us (2%)
    ppermute x8, starting transfers between devices, exchange(): lax.ppermute(first, axes, ways[0])  10.2 us
    pallas_call x1, Pallas kernels, on_device(): call(functools.partial(second_solve, box), (cells, row, row, col, col, ce...  5.63 us
    pallas_call x1, Pallas kernels, on_device(): call(functools.partial(first_solve, box), (window, cells, f32(across, dee...  4.17 us
    ppermute x2, waiting for transfers between devices, two_away(): return lax.ppermute(table, axis, [(i, (i + 2) % size) for i in range(size)])  4.07 us
    ppermute x8, starting transfers between devices, exchange(): lax.ppermute(second, axes, ways[1])  3.23 us
    ppermute x2, starting transfers between devices, two_away(): return lax.ppermute(table, axis, [(i, (i + 2) % size) for i in range(size)])  2.85 us
    ppermute x8, waiting for transfers between devices, exchange(): lax.ppermute(second, axes, ways[1])  2.42 us
    pallas_call x1, Pallas kernels, on_device(): call(functools.partial(bring_box, box), (cells, cells, whole_zone, f32(8,...  2.31 us
  transfers between devices with their start and end apart: 19, of which 8 were waited for; matrix products, arithmetic and copies ran while one was open for 0% of the time, Pallas kernels for 25%

profile of v23, /device:TPU:0, one launch (start us, length us, event | category | flops | bytes accessed | tf_op | source)
XLA Modules:
  0.0 48.5 jit_solution(4485108196825510494)
XLA Ops:
  0.6 1.1 %shard_map.149 = (f32[4,32,128]{2,1,0:T(8,128)S(1)}, f32[4,32,128]{2,1,0:T(8,128)S(1)}, f32[10,32,128]{2,1,0:T(8,128)S(1)}, f32[10,32,128]{2,1,0:T(8,128)S(1)}) custom-call(s32[64,32,128]{2,1,0:T(8,128)} %far_zone.1, f32[64,32,128]{2,1,0:T(8,128)} %far_scale.1, f32[64,32,128]{2,1,0:T(8,128)} %far_load.1), custom_call_target="tpu_custom_call" | custom-call | tf_op jit(solution)/shard_map/pallas_call | solution.py:1011
  1.8 3.1 %collective-permute-start = (f32[4,32,128]{2,1,0:T(8,128)S(1)}, f32[4,32,128]{2,1,0:T(8,128)S(1)}, u32[]{:S(2)}, u32[]{:S(2)}) collective-permute-start(f32[4,32,128]{2,1,0:T(8,128)S(1)} %get-tuple-element.39.after), channel_id=1, source_target_pairs={{0,4},{1,5},{2,6},{3,7},{4,0},{5,1},{6,2},{7,3},{8,12},{9,13},{10,... | collective-permute-start | bytes 196616 | tf_op jit(solution)/shard_map/ppermute | solution.py:959
  4.9 3.1 %collective-permute-start.6 = (f32[10,32,128]{2,1,0:T(8,128)S(1)}, f32[10,32,128]{2,1,0:T(8,128)S(1)}, u32[]{:S(2)}, u32[]{:S(2)}) collective-permute-start(f32[10,32,128]{2,1,0:T(8,128)S(1)} %get-tuple-element.51), channel_id=1, source_target_pairs={{0,4},{1,5},{2,6},{3,7},{4,0},{5,1},{6,2},{7,3},{8,12},{9,13},{10,... | collective-permute-start | bytes 491528 | tf_op jit(solution)/shard_map/ppermute | solution.py:959
  8.0 2.3 %shard_map.150 = (f32[64,32,128]{2,1,0:T(8,128)S(1)}, f32[64,32,128]{2,1,0:T(8,128)S(1)}, s32[64,32,128]{2,1,0:T(8,128)S(1)}, f32[8,128]{1,0:T(8,128)S(1)}, f32[16,128]{1,0:T(8,128)S(1)}) custom-call(f32[64,32,128]{2,1,0:T(8,128)} %far_load.1, f32[64,32,128]{2,1,0:T(8,128)} %far_scale.1, s32[64,32,128]{2,1,0:T(8,128)} %far_zone.1, ...), custom_call_target="tpu_custom_call" | custom-call | tf_op jit(solution)/shard_map/pallas_call | solution.py:1017
  10.7 0.6 %collective-permute-start.2 = (f32[296,128]{1,0:T(8,128)S(1)}, f32[296,128]{1,0:T(8,128)S(1)}, u32[]{:S(2)}, u32[]{:S(2)}) collective-permute-start(f32[296,128]{1,0:T(8,128)S(1)} %get-tuple-element.42), channel_id=1, source_target_pairs={{0,1},{4,5},{8,9},{12,13},{1,0},{5,4},{9,8},{13,12},{2,3},{6,7},{1... | collective-permute-start | bytes 454664 | tf_op jit(solution)/shard_map/ppermute | solution.py:959
  11.3 0.4 collective-permute-done.6.refs_2_.low
  11.7 0.4 shard_map.153
  12.1 1.3 %collective-permute-start.8 = (f32[744,128]{1,0:T(8,128)S(1)}, f32[744,128]{1,0:T(8,128)S(1)}, u32[]{:S(2)}, u32[]{:S(2)}) collective-permute-start(f32[744,128]{1,0:T(8,128)S(1)} %get-tuple-element.53), channel_id=1, source_target_pairs={{0,1},{4,5},{8,9},{12,13},{1,0},{5,4},{9,8},{13,12},{2,3},{6,7},{1... | collective-permute-start | bytes 1142792 | tf_op jit(solution)/shard_map/ppermute | solution.py:959
  13.4 1.0 %collective-permute-start.9 = (f32[744,128]{1,0:T(8,128)S(1)}, f32[744,128]{1,0:T(8,128)S(1)}, u32[]{:S(2)}, u32[]{:S(2)}) collective-permute-start(f32[744,128]{1,0:T(8,128)S(1)} %get-tuple-element.54), channel_id=1, source_target_pairs={{0,4},{4,0},{8,12},{12,8},{1,2},{5,6},{9,10},{13,14},{2,1},{6,5},{... | collective-permute-start | bytes 1142792 | tf_op jit(solution)/shard_map/ppermute | solution.py:959
  14.4 2.1 %collective-permute-done.3.right = f32[296,128]{1,0:T(8,128)S(1)} collective-permute-done((f32[296,128]{1,0:T(8,128)S(1)}, f32[296,128]{1,0:T(8,128)S(1)}, u32[]{:S(2)}, u32[]{:S(2)}) %collective-permute-start.3) | collective-permute-done | bytes 151584 | tf_op jit(solution)/shard_map/ppermute | solution.py:959
  16.5 4.2 %shard_map.152 = (f32[74,48,128]{2,1,0:T(8,128)S(1)}, f32[64,32,128]{2,1,0:T(8,128)S(1)}, f32[32,128]{1,0:T(8,128)S(1)}, f32[40,72,128]{2,1,0:T(8,128)S(1)}, f32...) custom-call(f32[64,32,128]{2,1,0:T(8,128)S(1)} %get-tuple-element.40.refs_0_.load, ...), custom_call_target="tpu_custom_call" | custom-call | flops 4000000000 | tf_op jit(solution)/shard_map/pallas_call | solution.py:1029
  20.7 0.3 collective-permute-done.9.right
  21.0 0.4 shard_map.154.table
  21.4 1.0 %collective-permute-start.10 = (f32[16,128]{1,0:T(8,128)S(1)}, f32[16,128]{1,0:T(8,128)S(1)}, u32[]{:S(2)}, u32[]{:S(2)}) collective-permute-start(f32[16,128]{1,0:T(8,128)S(1)} %shard_map.154.table), channel_id=1, source_target_pairs={{0,4},{1,5},{2,6},{3,7},{4,0},{5,1},{6,2},{7,3},{8,12},{9,13},{10,... | collective-permute-start | bytes 24584 | tf_op jit(solution)/shard_map/ppermute | solution.py:1043
  22.4 1.0 %collective-permute-start.4 = (f32[160,128]{1,0:T(8,128)S(1)}, f32[160,128]{1,0:T(8,128)S(1)}, u32[]{:S(2)}, u32[]{:S(2)}) collective-permute-start(f32[160,128]{1,0:T(8,128)S(1)} %get-tuple-element.48), channel_id=1, source_target_pairs={{0,4},{1,5},{2,6},{3,7},{4,0},{5,1},{6,2},{7,3},{8,12},{9,13},{10,... | collective-permute-start | bytes 245768 | tf_op jit(solution)/shard_map/ppermute | solution.py:959
  23.4 1.7 %collective-permute-done.10.message = f32[16,128]{1,0:T(8,128)S(1)} collective-permute-done((f32[16,128]{1,0:T(8,128)S(1)}, f32[16,128]{1,0:T(8,128)S(1)}, u32[]{:S(2)}, u32[]{:S(2)}) %collective-permute-start.10) | collective-permute-done | bytes 8224 | tf_op jit(solution)/shard_map/ppermute | solution.py:1043
  25.1 2.2 %collective-permute-start.11 = (f32[16,128]{1,0:T(8,128)S(1)}, f32[16,128]{1,0:T(8,128)S(1)}, u32[]{:S(2)}, u32[]{:S(2)}) collective-permute-start(f32[16,128]{1,0:T(8,128)S(1)} %shard_map.155.refs_3_), channel_id=1, source_target_pairs={{0,8},{4,12},{8,0},{12,4},{1,9},{5,13},{9,1},{13,5},{2,10},{6,14},... | collective-permute-start | bytes 24584 | tf_op jit(solution)/shard_map/ppermute | solution.py:964
  27.3 1.3 %shard_map.156 = (f32[74,48,128]{2,1,0:T(8,128)S(1)}, f32[74,48,128]{2,1,0:T(8,128)S(1)}, f32[74,48,128]{2,1,0:T(8,128)S(1)}, f32[74,48,128]{2,1,0:T(8,128)S(1)}) custom-call(s32[64,32,128]{2,1,0:T(8,128)S(1)} %get-tuple-element.45.zone.refs_1_, f32[64,32,128]{2,1,0:T(8,128)S(1)} %get-tuple-element.46.scale.refs_0_, ...), custom_call_target="tpu_custom_call" | custom-call | flops 1000000000 | tf_op jit(solution)/shard_map/pallas_call | solution.py:1046
  28.7 1.0 %collective-permute-done.11.refs_4_ = f32[16,128]{1,0:T(8,128)S(1)} collective-permute-done((f32[16,128]{1,0:T(8,128)S(1)}, f32[16,128]{1,0:T(8,128)S(1)}, u32[]{:S(2)}, u32[]{:S(2)}) %collective-permute-start.11) | collective-permute-done | bytes 8224 | tf_op jit(solution)/shard_map/ppermute | solution.py:964
  29.7 0.2 shard_map.157
  30.0 1.1 %collective-permute-start.13 = (f32[392,128]{1,0:T(8,128)S(1)}, f32[392,128]{1,0:T(8,128)S(1)}, u32[]{:S(2)}, u32[]{:S(2)}) collective-permute-start(f32[392,128]{1,0:T(8,128)S(1)} %get-tuple-element.58), channel_id=1, source_target_pairs={{0,4},{4,0},{8,12},{12,8},{1,2},{5,6},{9,10},{13,14},{2,1},{6,5},{... | collective-permute-start | bytes 602120 | tf_op jit(solution)/shard_map/ppermute | solution.py:959
  31.1 0.3 collective-permute-done.12.message.left
  31.4 0.7 %collective-permute-start.14 = (f32[16,128]{1,0:T(8,128)S(1)}, f32[16,128]{1,0:T(8,128)S(1)}, u32[]{:S(2)}, u32[]{:S(2)}) collective-permute-start(f32[16,128]{1,0:T(8,128)S(1)} %shard_map.158.refs_0_), channel_id=1, source_target_pairs={{0,2},{1,3},{2,0},{3,1},{4,6},{5,7},{6,4},{7,5},{8,10},{9,11},{10,... | collective-permute-start | bytes 24584 | tf_op jit(solution)/shard_map/ppermute | solution.py:964
  32.1 0.8 %shard_map.160 = (f32[74,48,128]{2,1,0:T(8,128)S(1)}, f32[74,48,128]{2,1,0:T(8,128)S(1)}) custom-call(f32[74,48,128]{2,1,0:T(8,128)S(1)} %get-tuple-element.62.zone_window, f32[74,48,128]{2,1,0:T(8,128)S(1)} %get-tuple-element.63.scale_window, f32[3,3]{1,0:T(4,128)S(1)} %copy-done, f32[1,3]{1,0:T(1,128)S(1)} %bitcast.3), custom_call_target="tpu_custom_call" | custom-call | flops 1000000000 | tf_op jit(solution)/shard_map/pallas_call | solution.py:1052
  33.0 3.0 %collective-permute-done.14.refs_1_ = f32[16,128]{1,0:T(8,128)S(1)} collective-permute-done((f32[16,128]{1,0:T(8,128)S(1)}, f32[16,128]{1,0:T(8,128)S(1)}, u32[]{:S(2)}, u32[]{:S(2)}) %collective-permute-start.14) | collective-permute-done | bytes 8224 | tf_op jit(solution)/shard_map/ppermute | solution.py:964
  36.0 0.9 %shard_map.159.answers = f32[8,128]{1,0:T(8,128)S(1)} custom-call(f32[16,128]{1,0:T(8,128)S(1)} %shard_map.158.refs_0_, f32[16,128]{1,0:T(8,128)S(1)} %collective-permute-done.14.refs_1_), custom_call_target="tpu_custom_call" | custom-call | tf_op jit(solution)/shard_map/pallas_call | solution.py:1067
  36.9 5.6 %shard_map.161 = (f32[64,32,128]{2,1,0:T(8,128)S(1)}, f32[32,128]{1,0:T(8,128)S(1)}, f32[32,128]{1,0:T(8,128)S(1)}, f32[64,128]{1,0:T(8,128)S(1)}, f32[64,128]{1,0:T(8,128)S(1)}, /*index=5*/f32[64,32,128]{2,1,0:T(8,128)}) custom-call(f32[64,32,128]{2,1,0:T(8,128)S(1)} %get-tuple-element.47.local.refs_0_, f32[160,128]{1,0:T(8,128)S(1)} %collective-permute-done.4.refs_1_.low, ...), custom_call_target="tpu_custom_call" | custom-call | flops 4000000000 | tf_op jit(solution)/shard_map/pallas_call | solution.py:1073
  42.6 1.1 %collective-permute-start.18 = (f32[64,128]{1,0:T(8,128)S(1)}, f32[64,128]{1,0:T(8,128)S(1)}, u32[]{:S(2)}, u32[]{:S(2)}) collective-permute-start(f32[64,128]{1,0:T(8,128)S(1)} %get-tuple-element.72), channel_id=1, source_target_pairs={{0,4},{4,0},{8,12},{12,8},{1,2},{5,6},{9,10},{13,14},{2,1},{6,5},{... | collective-permute-start | bytes 98312 | tf_op jit(solution)/shard_map/ppermute | solution.py:959
  43.7 1.0 %collective-permute-start.15 = (f32[32,128]{1,0:T(8,128)S(1)}, f32[32,128]{1,0:T(8,128)S(1)}, u32[]{:S(2)}, u32[]{:S(2)}) collective-permute-start(f32[32,128]{1,0:T(8,128)S(1)} %get-tuple-element.69), channel_id=1, source_target_pairs={{0,4},{1,5},{2,6},{3,7},{4,0},{5,1},{6,2},{7,3},{8,12},{9,13},{10,... | collective-permute-start | bytes 49160 | tf_op jit(solution)/shard_map/ppermute | solution.py:959
  44.7 1.9 %shard_map.162 = (f32[2,32,128]{2,1,0:T(8,128)S(1)}, f32[2,64,8,128]{3,2,1,0:T(8,128)S(1)}, f32[64,32,128]{2,1,0:T(8,128)}) custom-call(f32[64,32,128]{2,1,0:T(8,128)S(1)} %get-tuple-element.40.refs_0_.load, f32[64,32,128]{2,1,0:T(8,128)S(1)} %get-tuple-element.68.iterate, f32[74,48,128]{2,1,0:T(8,128)S(1)} %get-tuple-element.56.refs_5_.rest_0_.to_long, ...), custom_call_target="tpu_custom_call" | custom-call | flops 1000000000 | tf_op jit(solution)/shard_map/pallas_call | solution.py:1083
  46.5 0.9 %collective-permute-done.15.low = f32[32,128]{1,0:T(8,128)S(1)} collective-permute-done((f32[32,128]{1,0:T(8,128)S(1)}, f32[32,128]{1,0:T(8,128)S(1)}, u32[]{:S(2)}, u32[]{:S(2)}) %collective-permute-start.15) | collective-permute-done | bytes 16416 | tf_op jit(solution)/shard_map/ppermute | solution.py:959
  47.4 0.9 %shard_map.163 = f32[64,32,128]{2,1,0:T(8,128)} custom-call(f32[64,32,128]{2,1,0:T(8,128)S(1)} %get-tuple-element.68.iterate, f32[32,128]{1,0:T(8,128)S(1)} %collective-permute-done.15.low, f32[32,128]{1,0:T(8,128)S(1)} %collective-permute-done.16.high, f32[64,128]{1,0:T(8,128)S(1)} %collective-permute-done.17.left, ...), custom_call_target="tpu_custom_call", output_to_operand_aliasing={{}: (9, {})} | custom-call | tf_op jit(solution)/shard_map/pallas_call | solution.py:1095
  (43 shorter events, 0.5 us)
Async XLA Ops:
  0.6 7.4 %copy-start.1 = (f32[3]{0:T(128)S(1)}, f32[3]{0:T(128)}, u32[]{:S(2)}) copy-start(f32[3]{0:T(128)} %param.17) | copy-start | bytes 40
  0.6 7.4 %copy-start = (f32[3,3]{1,0:T(4,128)S(1)}, f32[3,3]{1,0:T(4,128)}, u32[]{:S(2)}) copy-start(f32[3,3]{1,0:T(4,128)} %diffusivity.9) | copy-start | bytes 112
  1.8 8.7 %collective-permute-start = (f32[4,32,128]{2,1,0:T(8,128)S(1)}, f32[4,32,128]{2,1,0:T(8,128)S(1)}, u32[]{:S(2)}, u32[]{:S(2)}) collective-permute-start(f32[4,32,128]{2,1,0:T(8,128)S(1)} %get-tuple-element.39.after), channel_id=1, source_target_pairs={{0,4},{1,5},{2,6},{3,7},{4,0},{5,1},{6,2},{7,3},{8,12},{9,13},{10,... | collective-permute-start | bytes 196616 | tf_op jit(solution)/shard_map/ppermute | solution.py:959
  4.9 5.6 %collective-permute-start.1 = (f32[4,32,128]{2,1,0:T(8,128)S(1)}, f32[4,32,128]{2,1,0:T(8,128)S(1)}, u32[]{:S(2)}, u32[]{:S(2)}) collective-permute-start(f32[4,32,128]{2,1,0:T(8,128)S(1)} %get-tuple-element.41), channel_id=1, source_target_pairs={{0,1},{1,0},{2,3},{3,2},{4,8},{5,9},{6,10},{7,11},{8,4},{9,5},{10,... | collective-permute-start | bytes 196616 | tf_op jit(solution)/shard_map/ppermute | solution.py:959
  4.9 6.8 %collective-permute-start.6 = (f32[10,32,128]{2,1,0:T(8,128)S(1)}, f32[10,32,128]{2,1,0:T(8,128)S(1)}, u32[]{:S(2)}, u32[]{:S(2)}) collective-permute-start(f32[10,32,128]{2,1,0:T(8,128)S(1)} %get-tuple-element.51), channel_id=1, source_target_pairs={{0,4},{1,5},{2,6},{3,7},{4,0},{5,1},{6,2},{7,3},{8,12},{9,13},{10,... | collective-permute-start | bytes 491528 | tf_op jit(solution)/shard_map/ppermute | solution.py:959
  8.0 3.6 %collective-permute-start.7 = (f32[10,32,128]{2,1,0:T(8,128)S(1)}, f32[10,32,128]{2,1,0:T(8,128)S(1)}, u32[]{:S(2)}, u32[]{:S(2)}) collective-permute-start(f32[10,32,128]{2,1,0:T(8,128)S(1)} %get-tuple-element.52), channel_id=1, source_target_pairs={{0,1},{1,0},{2,3},{3,2},{4,8},{5,9},{6,10},{7,11},{8,4},{9,5},{10,... | collective-permute-start | bytes 491528 | tf_op jit(solution)/shard_map/ppermute | solution.py:959
  10.4 6.1 %copy-start.2 = (f32[256,256]{1,0:T(8,128)S(1)}, f32[256,256]{1,0:T(8,128)}, u32[]{:S(2)}) copy-start(f32[256,256]{1,0:T(8,128)} %constant.22.clone.rest_4_.rest_9_) | copy-start | bytes 786436
  10.4 6.1 %copy-start.3 = (f32[192,216]{1,0:T(8,128)S(1)}, f32[192,216]{1,0:T(8,128)}, u32[]{:S(2)}) copy-start(f32[192,216]{1,0:T(8,128)} %constant.20.clone.rest_2_.rest_7_) | copy-start | bytes 497668
  10.4 6.1 %copy-start.4 = (f32[144,144]{1,0:T(8,128)S(1)}, f32[144,144]{1,0:T(8,128)}, u32[]{:S(2)}) copy-start(f32[144,144]{1,0:T(8,128)} %constant.19.clone.rest_1_.rest_6_) | copy-start | bytes 248836
  10.4 6.0 %copy-start.5 = (f32[256,128]{1,0:T(8,128)S(1)}, f32[256,128]{1,0:T(8,128)}, u32[]{:S(2)}) copy-start(f32[256,128]{1,0:T(8,128)} %constant.23.clone.rest_5_.rest_10_) | copy-start | bytes 393220
  10.4 6.0 %copy-start.6 = (f32[96,120]{1,0:T(8,128)S(1)}, f32[96,120]{1,0:T(8,128)}, u32[]{:S(2)}) copy-start(f32[96,120]{1,0:T(8,128)} %constant.21.clone.rest_3_.rest_8_) | copy-start | bytes 138244
  10.4 6.0 %copy-start.7 = (f32[80,80]{1,0:T(8,128)S(1)}, f32[80,80]{1,0:T(8,128)}, u32[]{:S(2)}) copy-start(f32[80,80]{1,0:T(8,128)} %constant.18.clone.rest_0_.rest_5_) | copy-start | bytes 76804
  10.4 6.0 %copy-start.8 = (f32[72,128]{1,0:T(8,128)S(1)}, f32[72,128]{1,0:T(8,128)}, u32[]{:S(2)}) copy-start(f32[72,128]{1,0:T(8,128)} %constant.24.clone.rest_6_.rest_11_) | copy-start | bytes 110596
  10.5 6.0 %copy-start.9 = (f32[40,128]{1,0:T(8,128)S(1)}, f32[40,128]{1,0:T(8,128)}, u32[]{:S(2)}) copy-start(f32[40,128]{1,0:T(8,128)} %constant.25.clone.rest_7_.rest_12_) | copy-start | bytes 61444
  10.5 6.0 %copy-start.10 = (f32[1,128]{1,0:T(1,128)S(1)}, f32[1,128]{1,0:T(1,128)}, u32[]{:S(2)}) copy-start(f32[1,128]{1,0:T(1,128)} %constant.26.clone.rest_8_.rest_13_) | copy-start | bytes 1540
  10.7 3.7 %collective-permute-start.2 = (f32[296,128]{1,0:T(8,128)S(1)}, f32[296,128]{1,0:T(8,128)S(1)}, u32[]{:S(2)}, u32[]{:S(2)}) collective-permute-start(f32[296,128]{1,0:T(8,128)S(1)} %get-tuple-element.42), channel_id=1, source_target_pairs={{0,1},{4,5},{8,9},{12,13},{1,0},{5,4},{9,8},{13,12},{2,3},{6,7},{1... | collective-permute-start | bytes 454664 | tf_op jit(solution)/shard_map/ppermute | solution.py:959
  11.3 5.2 %collective-permute-start.3 = (f32[296,128]{1,0:T(8,128)S(1)}, f32[296,128]{1,0:T(8,128)S(1)}, u32[]{:S(2)}, u32[]{:S(2)}) collective-permute-start(f32[296,128]{1,0:T(8,128)S(1)} %get-tuple-element.43), channel_id=1, source_target_pairs={{0,4},{4,0},{8,12},{12,8},{1,2},{5,6},{9,10},{13,14},{2,1},{6,5},{... | collective-permute-start | bytes 454664 | tf_op jit(solution)/shard_map/ppermute | solution.py:959
  12.1 8.6 %collective-permute-start.8 = (f32[744,128]{1,0:T(8,128)S(1)}, f32[744,128]{1,0:T(8,128)S(1)}, u32[]{:S(2)}, u32[]{:S(2)}) collective-permute-start(f32[744,128]{1,0:T(8,128)S(1)} %get-tuple-element.53), channel_id=1, source_target_pairs={{0,1},{4,5},{8,9},{12,13},{1,0},{5,4},{9,8},{13,12},{2,3},{6,7},{1... | collective-permute-start | bytes 1142792 | tf_op jit(solution)/shard_map/ppermute | solution.py:959
  13.4 7.6 %collective-permute-start.9 = (f32[744,128]{1,0:T(8,128)S(1)}, f32[744,128]{1,0:T(8,128)S(1)}, u32[]{:S(2)}, u32[]{:S(2)}) collective-permute-start(f32[744,128]{1,0:T(8,128)S(1)} %get-tuple-element.54), channel_id=1, source_target_pairs={{0,4},{4,0},{8,12},{12,8},{1,2},{5,6},{9,10},{13,14},{2,1},{6,5},{... | collective-permute-start | bytes 1142792 | tf_op jit(solution)/shard_map/ppermute | solution.py:959
  21.4 3.7 %collective-permute-start.10 = (f32[16,128]{1,0:T(8,128)S(1)}, f32[16,128]{1,0:T(8,128)S(1)}, u32[]{:S(2)}, u32[]{:S(2)}) collective-permute-start(f32[16,128]{1,0:T(8,128)S(1)} %shard_map.154.table), channel_id=1, source_target_pairs={{0,4},{1,5},{2,6},{3,7},{4,0},{5,1},{6,2},{7,3},{8,12},{9,13},{10,... | collective-permute-start | bytes 24584 | tf_op jit(solution)/shard_map/ppermute | solution.py:1043
  22.4 6.2 %collective-permute-start.4 = (f32[160,128]{1,0:T(8,128)S(1)}, f32[160,128]{1,0:T(8,128)S(1)}, u32[]{:S(2)}, u32[]{:S(2)}) collective-permute-start(f32[160,128]{1,0:T(8,128)S(1)} %get-tuple-element.48), channel_id=1, source_target_pairs={{0,4},{1,5},{2,6},{3,7},{4,0},{5,1},{6,2},{7,3},{8,12},{9,13},{10,... | collective-permute-start | bytes 245768 | tf_op jit(solution)/shard_map/ppermute | solution.py:959
  23.4 5.2 %collective-permute-start.5 = (f32[160,128]{1,0:T(8,128)S(1)}, f32[160,128]{1,0:T(8,128)S(1)}, u32[]{:S(2)}, u32[]{:S(2)}) collective-permute-start(f32[160,128]{1,0:T(8,128)S(1)} %get-tuple-element.49), channel_id=1, source_target_pairs={{0,1},{1,0},{2,3},{3,2},{4,8},{5,9},{6,10},{7,11},{8,4},{9,5},{10,... | collective-permute-start | bytes 245768 | tf_op jit(solution)/shard_map/ppermute | solution.py:959
  25.1 4.5 %collective-permute-start.11 = (f32[16,128]{1,0:T(8,128)S(1)}, f32[16,128]{1,0:T(8,128)S(1)}, u32[]{:S(2)}, u32[]{:S(2)}) collective-permute-start(f32[16,128]{1,0:T(8,128)S(1)} %shard_map.155.refs_3_), channel_id=1, source_target_pairs={{0,8},{4,12},{8,0},{12,4},{1,9},{5,13},{9,1},{13,5},{2,10},{6,14},... | collective-permute-start | bytes 24584 | tf_op jit(solution)/shard_map/ppermute | solution.py:964
  29.9 1.5 %collective-permute-start.12 = (f32[392,128]{1,0:T(8,128)S(1)}, f32[392,128]{1,0:T(8,128)S(1)}, u32[]{:S(2)}, u32[]{:S(2)}) collective-permute-start(f32[392,128]{1,0:T(8,128)S(1)} %get-tuple-element.57), channel_id=1, source_target_pairs={{0,1},{4,5},{8,9},{12,13},{1,0},{5,4},{9,8},{13,12},{2,3},{6,7},{1... | collective-permute-start | bytes 602120 | tf_op jit(solution)/shard_map/ppermute | solution.py:959
  30.0 6.9 %collective-permute-start.13 = (f32[392,128]{1,0:T(8,128)S(1)}, f32[392,128]{1,0:T(8,128)S(1)}, u32[]{:S(2)}, u32[]{:S(2)}) collective-permute-start(f32[392,128]{1,0:T(8,128)S(1)} %get-tuple-element.58), channel_id=1, source_target_pairs={{0,4},{4,0},{8,12},{12,8},{1,2},{5,6},{9,10},{13,14},{2,1},{6,5},{... | collective-permute-start | bytes 602120 | tf_op jit(solution)/shard_map/ppermute | solution.py:959
  31.4 4.6 %collective-permute-start.14 = (f32[16,128]{1,0:T(8,128)S(1)}, f32[16,128]{1,0:T(8,128)S(1)}, u32[]{:S(2)}, u32[]{:S(2)}) collective-permute-start(f32[16,128]{1,0:T(8,128)S(1)} %shard_map.158.refs_0_), channel_id=1, source_target_pairs={{0,2},{1,3},{2,0},{3,1},{4,6},{5,7},{6,4},{7,5},{8,10},{9,11},{10,... | collective-permute-start | bytes 24584 | tf_op jit(solution)/shard_map/ppermute | solution.py:964
  42.5 4.9 %collective-permute-start.17 = (f32[64,128]{1,0:T(8,128)S(1)}, f32[64,128]{1,0:T(8,128)S(1)}, u32[]{:S(2)}, u32[]{:S(2)}) collective-permute-start(f32[64,128]{1,0:T(8,128)S(1)} %get-tuple-element.71), channel_id=1, source_target_pairs={{0,1},{4,5},{8,9},{12,13},{1,0},{5,4},{9,8},{13,12},{2,3},{6,7},{1... | collective-permute-start | bytes 98312 | tf_op jit(solution)/shard_map/ppermute | solution.py:959
  42.6 4.8 %collective-permute-start.18 = (f32[64,128]{1,0:T(8,128)S(1)}, f32[64,128]{1,0:T(8,128)S(1)}, u32[]{:S(2)}, u32[]{:S(2)}) collective-permute-start(f32[64,128]{1,0:T(8,128)S(1)} %get-tuple-element.72), channel_id=1, source_target_pairs={{0,4},{4,0},{8,12},{12,8},{1,2},{5,6},{9,10},{13,14},{2,1},{6,5},{... | collective-permute-start | bytes 98312 | tf_op jit(solution)/shard_map/ppermute | solution.py:959
  43.7 3.7 %collective-permute-start.15 = (f32[32,128]{1,0:T(8,128)S(1)}, f32[32,128]{1,0:T(8,128)S(1)}, u32[]{:S(2)}, u32[]{:S(2)}) collective-permute-start(f32[32,128]{1,0:T(8,128)S(1)} %get-tuple-element.69), channel_id=1, source_target_pairs={{0,4},{1,5},{2,6},{3,7},{4,0},{5,1},{6,2},{7,3},{8,12},{9,13},{10,... | collective-permute-start | bytes 49160 | tf_op jit(solution)/shard_map/ppermute | solution.py:959
  44.7 2.7 %collective-permute-start.16 = (f32[32,128]{1,0:T(8,128)S(1)}, f32[32,128]{1,0:T(8,128)S(1)}, u32[]{:S(2)}, u32[]{:S(2)}) collective-permute-start(f32[32,128]{1,0:T(8,128)S(1)} %get-tuple-element.70), channel_id=1, source_target_pairs={{0,1},{1,0},{2,3},{3,2},{4,8},{5,9},{6,10},{7,11},{8,4},{9,5},{10,... | collective-permute-start | bytes 49160 | tf_op jit(solution)/shard_map/ppermute | solution.py:959

commit v24 on v23

--- a/solution.py
+++ b/solution.py
@@ -1038,11 +1038,17 @@
         zone, scale, local, image, *far_wide, *far_narrow, table, diffusivity
     )
     own_table = table
-    parts = (table,)
     if by_margins:
-        partner = lax.ppermute(table, ("wide", "narrow"), swaps("wide")[0])
-        table = call(join_rows, table_shape, [VMEM] * 2)(table, partner)
+        more = lax.ppermute(table, ("wide", "narrow"), swaps("narrow")[0])
+        table = call(join_rows, table_shape, [VMEM] * 2)(table, more)
+        table = call(join_rows, table_shape, [VMEM] * 2)(table, two_away("narrow", table))
+        narrow_table = table
+        more = lax.ppermute(table, ("wide", "narrow"), swaps("wide")[0])
+        table = call(join_rows, table_shape, [VMEM] * 2)(table, more)
         parts = (table, two_away("wide", table))
+    else:
+        narrow_table = table
+        parts = (tell(own_table),)
     to_long, to_across, *windows = call(
         functools.partial(side_weights, box),
         (window,) * 4,
@@ -1056,13 +1062,8 @@
         flops=10**9,
     )(*windows, diffusivity, decay)
     weights = (to_long, to_across, to_deep, mass)
-    first, second, table = pack(REACH, [local], wide, parts, [to_long])
+    first, second = pack(REACH, [local], wide, after=[to_long, narrow_table])
     narrow = exchange("narrow", first, second)
-    if by_margins:
-        table = call(join_rows, table_shape, [VMEM] * 2)(table, narrow[0])
-        parts = (table, two_away("narrow", table))
-    else:
-        parts = (tell(own_table),)
     row, col = f32(across, deep), f32(long, deep)
     answers = call(
         functools.partial(coarse_corrections, len(parts)),

time: 48.7 us -> 51.5 us (1.057)
  starting transfers between devices: 17.3 us -> 19.5 us
  waiting for transfers between devices: 9.82 us -> 10.5 us
    ppermute x8, starting transfers between devices: 3.23 us -> 7.12 us  [exchange(): lax.ppermute(second, axes, ways[1])]
    ppermute x1 -> x2, waiting for transfers between devices: 1.71 us -> 3.7 us  [the longest x1 3.7 us: on_device(): more = lax.ppermute(table, ('wide', 'narrow'), swaps('wide')[0])]
    ppermute x8, starting transfers between devices: 10.2 us -> 8.99 us  [exchange(): lax.ppermute(first, axes, ways[0])]
    ppermute x2, waiting for transfers between devices: 4.07 us -> 2.88 us  [two_away(): return lax.ppermute(table, axis, [(i, (i + 2) % size) for i in range(size)])]
    ppermute x8, waiting for transfers between devices: 1.63 us -> 0.57 us  [exchange(): lax.ppermute(first, axes, ways[0])]
    ppermute x8, waiting for transfers between devices: 2.42 us -> 3.31 us  [exchange(): lax.ppermute(second, axes, ways[1])]
    ppermute x1 -> x2, starting transfers between devices: 1 us -> 0.19 us  [the longest x1 0.12 us: on_device(): more = lax.ppermute(table, ('wide', 'narrow'), swaps('narrow')[0])]
  transfers between devices with their start and end apart: 19 -> 20, of which waited for: 8 -> 8; matrix products, arithmetic and copies ran while one was open for 0% -> 0% of each run, Pallas kernels for 25% -> 23%
where the time goes in v24:
time: 51.5 us; the launch traced here: 51.3 us
  Pallas kernels  20.3 us (39%)
  starting transfers between devices  19.5 us (38%)
  waiting for transfers between devices  10.5 us (20%)
  between operations  1.08 us (2%)
    ppermute x8, starting transfers between devices, exchange(): lax.ppermute(first, axes, ways[0])  8.99 us
    ppermute x8, starting transfers between devices, exchange(): lax.ppermute(second, axes, ways[1])  7.12 us
    pallas_call x1, Pallas kernels, on_device(): call(functools.partial(second_solve, box), (cells, row, row, col, col, ce...  5.61 us
    pallas_call x1, Pallas kernels, on_device(): call(functools.partial(first_solve, box), (window, cells, f32(across, dee...  4.17 us
    ppermute x1, waiting for transfers between devices, on_device(): more = lax.ppermute(table, ('wide', 'narrow'), swaps('wide')[0])  3.7 us
    ppermute x8, waiting for transfers between devices, exchange(): lax.ppermute(second, axes, ways[1])  3.31 us
    ppermute x2, starting transfers between devices, two_away(): return lax.ppermute(table, axis, [(i, (i + 2) % size) for i in range(size)])  3.14 us
    ppermute x2, waiting for transfers between devices, two_away(): return lax.ppermute(table, axis, [(i, (i + 2) % size) for i in range(size)])  2.88 us
  transfers between devices with their start and end apart: 20, of which 8 were waited for; matrix products, arithmetic and copies ran while one was open for 0% of the time, Pallas kernels for 23%

profile of v24, /device:TPU:0, one launch (start us, length us, event | category | flops | bytes accessed | tf_op | source)
XLA Modules:
  0.0 51.3 jit_solution(14353286368202511223)
XLA Ops:
  0.6 1.1 %shard_map.149 = (f32[4,32,128]{2,1,0:T(8,128)S(1)}, f32[4,32,128]{2,1,0:T(8,128)S(1)}, f32[10,32,128]{2,1,0:T(8,128)S(1)}, f32[10,32,128]{2,1,0:T(8,128)S(1)}) custom-call(s32[64,32,128]{2,1,0:T(8,128)} %far_zone.1, f32[64,32,128]{2,1,0:T(8,128)} %far_scale.1, f32[64,32,128]{2,1,0:T(8,128)} %far_load.1), custom_call_target="tpu_custom_call" | custom-call | tf_op jit(solution)/shard_map/pallas_call | solution.py:1011
  1.8 0.5 %collective-permute-start.1 = (f32[4,32,128]{2,1,0:T(8,128)S(1)}, f32[4,32,128]{2,1,0:T(8,128)S(1)}, u32[]{:S(2)}, u32[]{:S(2)}) collective-permute-start(f32[4,32,128]{2,1,0:T(8,128)S(1)} %get-tuple-element.40), channel_id=1, source_target_pairs={{0,1},{1,0},{2,3},{3,2},{4,8},{5,9},{6,10},{7,11},{8,4},{9,5},{10,... | collective-permute-start | bytes 196616 | tf_op jit(solution)/shard_map/ppermute | solution.py:959
  2.3 4.1 %collective-permute-start = (f32[4,32,128]{2,1,0:T(8,128)S(1)}, f32[4,32,128]{2,1,0:T(8,128)S(1)}, u32[]{:S(2)}, u32[]{:S(2)}) collective-permute-start(f32[4,32,128]{2,1,0:T(8,128)S(1)} %get-tuple-element.38.after), channel_id=1, source_target_pairs={{0,4},{1,5},{2,6},{3,7},{4,0},{5,1},{6,2},{7,3},{8,12},{9,13},{10,... | collective-permute-start | bytes 196616 | tf_op jit(solution)/shard_map/ppermute | solution.py:959
  6.5 2.3 %shard_map.150 = (f32[64,32,128]{2,1,0:T(8,128)S(1)}, f32[64,32,128]{2,1,0:T(8,128)S(1)}, s32[64,32,128]{2,1,0:T(8,128)S(1)}, f32[8,128]{1,0:T(8,128)S(1)}, f32[16,128]{1,0:T(8,128)S(1)}) custom-call(f32[64,32,128]{2,1,0:T(8,128)} %far_load.1, f32[64,32,128]{2,1,0:T(8,128)} %far_scale.1, s32[64,32,128]{2,1,0:T(8,128)} %far_zone.1, ...), custom_call_target="tpu_custom_call" | custom-call | tf_op jit(solution)/shard_map/pallas_call | solution.py:1017
  9.1 0.2 shard_map.151
  9.3 0.5 collective-permute-start.2
  9.7 2.1 %collective-permute-start.3 = (f32[296,128]{1,0:T(8,128)S(1)}, f32[296,128]{1,0:T(8,128)S(1)}, u32[]{:S(2)}, u32[]{:S(2)}) collective-permute-start(f32[296,128]{1,0:T(8,128)S(1)} %get-tuple-element.42), channel_id=1, source_target_pairs={{0,4},{4,0},{8,12},{12,8},{1,2},{5,6},{9,10},{13,14},{2,1},{6,5},{... | collective-permute-start | bytes 454664 | tf_op jit(solution)/shard_map/ppermute | solution.py:959
  11.8 0.4 collective-permute-done.6.refs_2_.low
  12.2 0.4 shard_map.153
  12.7 1.7 %collective-permute-start.9 = (f32[744,128]{1,0:T(8,128)S(1)}, f32[744,128]{1,0:T(8,128)S(1)}, u32[]{:S(2)}, u32[]{:S(2)}) collective-permute-start(f32[744,128]{1,0:T(8,128)S(1)} %get-tuple-element.52), channel_id=1, source_target_pairs={{0,4},{4,0},{8,12},{12,8},{1,2},{5,6},{9,10},{13,14},{2,1},{6,5},{... | collective-permute-start | bytes 1142792 | tf_op jit(solution)/shard_map/ppermute | solution.py:959
  14.4 0.6 %collective-permute-done.3.right = f32[296,128]{1,0:T(8,128)S(1)} collective-permute-done((f32[296,128]{1,0:T(8,128)S(1)}, f32[296,128]{1,0:T(8,128)S(1)}, u32[]{:S(2)}, u32[]{:S(2)}) %collective-permute-start.3) | collective-permute-done | bytes 151584 | tf_op jit(solution)/shard_map/ppermute | solution.py:959
  15.0 4.2 %shard_map.152 = (f32[74,48,128]{2,1,0:T(8,128)S(1)}, f32[64,32,128]{2,1,0:T(8,128)S(1)}, f32[32,128]{1,0:T(8,128)S(1)}, f32[40,72,128]{2,1,0:T(8,128)S(1)}, f32...) custom-call(f32[64,32,128]{2,1,0:T(8,128)S(1)} %get-tuple-element.39.refs_0_.load, ...), custom_call_target="tpu_custom_call" | custom-call | flops 4000000000 | tf_op jit(solution)/shard_map/pallas_call | solution.py:1029
  19.2 1.2 %collective-permute-done.9.right = f32[744,128]{1,0:T(8,128)S(1)} collective-permute-done((f32[744,128]{1,0:T(8,128)S(1)}, f32[744,128]{1,0:T(8,128)S(1)}, u32[]{:S(2)}, u32[]{:S(2)}) %collective-permute-start.9) | collective-permute-done | bytes 380960 | tf_op jit(solution)/shard_map/ppermute | solution.py:959
  20.4 0.4 shard_map.155.table
  21.0 1.6 %collective-permute-start.4 = (f32[160,128]{1,0:T(8,128)S(1)}, f32[160,128]{1,0:T(8,128)S(1)}, u32[]{:S(2)}, u32[]{:S(2)}) collective-permute-start(f32[160,128]{1,0:T(8,128)S(1)} %get-tuple-element.47), channel_id=1, source_target_pairs={{0,4},{1,5},{2,6},{3,7},{4,0},{5,1},{6,2},{7,3},{8,12},{9,13},{10,... | collective-permute-start | bytes 245768 | tf_op jit(solution)/shard_map/ppermute | solution.py:959
  22.7 0.9 %collective-permute-start.11 = (f32[16,128]{1,0:T(8,128)S(1)}, f32[16,128]{1,0:T(8,128)S(1)}, u32[]{:S(2)}, u32[]{:S(2)}) collective-permute-start(f32[16,128]{1,0:T(8,128)S(1)} %shard_map.156.table), channel_id=1, source_target_pairs={{0,2},{1,3},{2,0},{3,1},{4,6},{5,7},{6,4},{7,5},{8,10},{9,11},{10,... | collective-permute-start | bytes 24584 | tf_op jit(solution)/shard_map/ppermute | solution.py:964
  23.6 1.3 %shard_map.154 = (f32[74,48,128]{2,1,0:T(8,128)S(1)}, f32[74,48,128]{2,1,0:T(8,128)S(1)}, f32[74,48,128]{2,1,0:T(8,128)S(1)}, f32[74,48,128]{2,1,0:T(8,128)S(1)}) custom-call(s32[64,32,128]{2,1,0:T(8,128)S(1)} %get-tuple-element.44.zone.refs_1_, f32[64,32,128]{2,1,0:T(8,128)S(1)} %get-tuple-element.45.scale.refs_0_, ...), custom_call_target="tpu_custom_call" | custom-call | flops 1000000000 | tf_op jit(solution)/shard_map/pallas_call | solution.py:1052
  24.9 1.4 %collective-permute-done.11.message = f32[16,128]{1,0:T(8,128)S(1)} collective-permute-done((f32[16,128]{1,0:T(8,128)S(1)}, f32[16,128]{1,0:T(8,128)S(1)}, u32[]{:S(2)}, u32[]{:S(2)}) %collective-permute-start.11) | collective-permute-done | bytes 8224 | tf_op jit(solution)/shard_map/ppermute | solution.py:964
  26.3 0.2 shard_map.158
  26.6 2.2 %collective-permute-start.13 = (f32[376,128]{1,0:T(8,128)S(1)}, f32[376,128]{1,0:T(8,128)S(1)}, u32[]{:S(2)}, u32[]{:S(2)}) collective-permute-start(f32[376,128]{1,0:T(8,128)S(1)} %get-tuple-element.57), channel_id=1, source_target_pairs={{0,4},{4,0},{8,12},{12,8},{1,2},{5,6},{9,10},{13,14},{2,1},{6,5},{... | collective-permute-start | bytes 577544 | tf_op jit(solution)/shard_map/ppermute | solution.py:959
  29.0 3.7 %collective-permute-done.14.message = f32[16,128]{1,0:T(8,128)S(1)} collective-permute-done((f32[16,128]{1,0:T(8,128)S(1)}, f32[16,128]{1,0:T(8,128)S(1)}, u32[]{:S(2)}, u32[]{:S(2)}) %collective-permute-start.14) | collective-permute-done | bytes 8224 | tf_op jit(solution)/shard_map/ppermute | solution.py:1046
  32.7 2.2 %collective-permute-start.15 = (f32[16,128]{1,0:T(8,128)S(1)}, f32[16,128]{1,0:T(8,128)S(1)}, u32[]{:S(2)}, u32[]{:S(2)}) collective-permute-start(f32[16,128]{1,0:T(8,128)S(1)} %shard_map.159.refs_0_), channel_id=1, source_target_pairs={{0,8},{4,12},{8,0},{12,4},{1,9},{5,13},{9,1},{13,5},{2,10},{6,14},... | collective-permute-start | bytes 24584 | tf_op jit(solution)/shard_map/ppermute | solution.py:964
  34.9 0.8 %shard_map.161 = (f32[74,48,128]{2,1,0:T(8,128)S(1)}, f32[74,48,128]{2,1,0:T(8,128)S(1)}) custom-call(f32[74,48,128]{2,1,0:T(8,128)S(1)} %get-tuple-element.60.zone_window, f32[74,48,128]{2,1,0:T(8,128)S(1)} %get-tuple-element.61.scale_window, f32[3,3]{1,0:T(4,128)S(1)} %copy-done, f32[1,3]{1,0:T(1,128)S(1)} %bitcast.3), custom_call_target="tpu_custom_call" | custom-call | flops 1000000000 | tf_op jit(solution)/shard_map/pallas_call | solution.py:1058
  35.7 1.5 %collective-permute-done.15.refs_1_ = f32[16,128]{1,0:T(8,128)S(1)} collective-permute-done((f32[16,128]{1,0:T(8,128)S(1)}, f32[16,128]{1,0:T(8,128)S(1)}, u32[]{:S(2)}, u32[]{:S(2)}) %collective-permute-start.15) | collective-permute-done | bytes 8224 | tf_op jit(solution)/shard_map/ppermute | solution.py:964
  37.2 0.9 %shard_map.160.answers = f32[8,128]{1,0:T(8,128)S(1)} custom-call(f32[16,128]{1,0:T(8,128)S(1)} %shard_map.159.refs_0_, f32[16,128]{1,0:T(8,128)S(1)} %collective-permute-done.15.refs_1_), custom_call_target="tpu_custom_call" | custom-call | tf_op jit(solution)/shard_map/pallas_call | solution.py:1068
  38.1 5.6 %shard_map.162 = (f32[64,32,128]{2,1,0:T(8,128)S(1)}, f32[32,128]{1,0:T(8,128)S(1)}, f32[32,128]{1,0:T(8,128)S(1)}, f32[64,128]{1,0:T(8,128)S(1)}, f32[64,128]{1,0:T(8,128)S(1)}, /*index=5*/f32[64,32,128]{2,1,0:T(8,128)}) custom-call(f32[64,32,128]{2,1,0:T(8,128)S(1)} %get-tuple-element.46.local.refs_0_, f32[160,128]{1,0:T(8,128)S(1)} %collective-permute-done.4.refs_1_.low, ...), custom_call_target="tpu_custom_call" | custom-call | flops 4000000000 | tf_op jit(solution)/shard_map/pallas_call | solution.py:1074
  43.7 2.1 %collective-permute-start.16 = (f32[32,128]{1,0:T(8,128)S(1)}, f32[32,128]{1,0:T(8,128)S(1)}, u32[]{:S(2)}, u32[]{:S(2)}) collective-permute-start(f32[32,128]{1,0:T(8,128)S(1)} %get-tuple-element.67), channel_id=1, source_target_pairs={{0,4},{1,5},{2,6},{3,7},{4,0},{5,1},{6,2},{7,3},{8,12},{9,13},{10,... | collective-permute-start | bytes 49160 | tf_op jit(solution)/shard_map/ppermute | solution.py:959
  45.8 0.5 collective-permute-start.18
  46.3 0.5 %collective-permute-start.19 = (f32[64,128]{1,0:T(8,128)S(1)}, f32[64,128]{1,0:T(8,128)S(1)}, u32[]{:S(2)}, u32[]{:S(2)}) collective-permute-start(f32[64,128]{1,0:T(8,128)S(1)} %get-tuple-element.70), channel_id=1, source_target_pairs={{0,4},{4,0},{8,12},{12,8},{1,2},{5,6},{9,10},{13,14},{2,1},{6,5},{... | collective-permute-start | bytes 98312 | tf_op jit(solution)/shard_map/ppermute | solution.py:959
  46.9 1.9 %shard_map.163 = (f32[2,32,128]{2,1,0:T(8,128)S(1)}, f32[2,64,8,128]{3,2,1,0:T(8,128)S(1)}, f32[64,32,128]{2,1,0:T(8,128)}) custom-call(f32[64,32,128]{2,1,0:T(8,128)S(1)} %get-tuple-element.39.refs_0_.load, f32[64,32,128]{2,1,0:T(8,128)S(1)} %get-tuple-element.66.iterate, f32[74,48,128]{2,1,0:T(8,128)S(1)} %get-tuple-element.53.refs_3_.rest_0_.to_long, ...), custom_call_target="tpu_custom_call" | custom-call | flops 1000000000 | tf_op jit(solution)/shard_map/pallas_call | solution.py:1084
  48.8 1.5 %collective-permute-done.19.right = f32[64,128]{1,0:T(8,128)S(1)} collective-permute-done((f32[64,128]{1,0:T(8,128)S(1)}, f32[64,128]{1,0:T(8,128)S(1)}, u32[]{:S(2)}, u32[]{:S(2)}) %collective-permute-start.19) | collective-permute-done | bytes 32800 | tf_op jit(solution)/shard_map/ppermute | solution.py:959
  50.3 0.9 %shard_map.164 = f32[64,32,128]{2,1,0:T(8,128)} custom-call(f32[64,32,128]{2,1,0:T(8,128)S(1)} %get-tuple-element.66.iterate, f32[32,128]{1,0:T(8,128)S(1)} %collective-permute-done.16.low, f32[32,128]{1,0:T(8,128)S(1)} %collective-permute-done.17.high, f32[64,128]{1,0:T(8,128)S(1)} %collective-permute-done.18.left, ...), custom_call_target="tpu_custom_call", output_to_operand_aliasing={{}: (9, {})} | custom-call | tf_op jit(solution)/shard_map/pallas_call | solution.py:1096
  (46 shorter events, 0.7 us)
Async XLA Ops:
  0.6 5.9 %copy-start = (f32[3,3]{1,0:T(4,128)S(1)}, f32[3,3]{1,0:T(4,128)}, u32[]{:S(2)}) copy-start(f32[3,3]{1,0:T(4,128)} %diffusivity.9) | copy-start | bytes 112
  0.6 5.9 %copy-start.1 = (f32[3]{0:T(128)S(1)}, f32[3]{0:T(128)}, u32[]{:S(2)}) copy-start(f32[3]{0:T(128)} %param.17) | copy-start | bytes 40
  1.8 7.1 %collective-permute-start.1 = (f32[4,32,128]{2,1,0:T(8,128)S(1)}, f32[4,32,128]{2,1,0:T(8,128)S(1)}, u32[]{:S(2)}, u32[]{:S(2)}) collective-permute-start(f32[4,32,128]{2,1,0:T(8,128)S(1)} %get-tuple-element.40), channel_id=1, source_target_pairs={{0,1},{1,0},{2,3},{3,2},{4,8},{5,9},{6,10},{7,11},{8,4},{9,5},{10,... | collective-permute-start | bytes 196616 | tf_op jit(solution)/shard_map/ppermute | solution.py:959
  2.3 6.8 %collective-permute-start = (f32[4,32,128]{2,1,0:T(8,128)S(1)}, f32[4,32,128]{2,1,0:T(8,128)S(1)}, u32[]{:S(2)}, u32[]{:S(2)}) collective-permute-start(f32[4,32,128]{2,1,0:T(8,128)S(1)} %get-tuple-element.38.after), channel_id=1, source_target_pairs={{0,4},{1,5},{2,6},{3,7},{4,0},{5,1},{6,2},{7,3},{8,12},{9,13},{10,... | collective-permute-start | bytes 196616 | tf_op jit(solution)/shard_map/ppermute | solution.py:959
  6.5 5.8 %collective-permute-start.6 = (f32[10,32,128]{2,1,0:T(8,128)S(1)}, f32[10,32,128]{2,1,0:T(8,128)S(1)}, u32[]{:S(2)}, u32[]{:S(2)}) collective-permute-start(f32[10,32,128]{2,1,0:T(8,128)S(1)} %get-tuple-element.49), channel_id=1, source_target_pairs={{0,4},{1,5},{2,6},{3,7},{4,0},{5,1},{6,2},{7,3},{8,12},{9,13},{10,... | collective-permute-start | bytes 491528 | tf_op jit(solution)/shard_map/ppermute | solution.py:959
  6.5 5.7 %collective-permute-start.7 = (f32[10,32,128]{2,1,0:T(8,128)S(1)}, f32[10,32,128]{2,1,0:T(8,128)S(1)}, u32[]{:S(2)}, u32[]{:S(2)}) collective-permute-start(f32[10,32,128]{2,1,0:T(8,128)S(1)} %get-tuple-element.50), channel_id=1, source_target_pairs={{0,1},{1,0},{2,3},{3,2},{4,8},{5,9},{6,10},{7,11},{8,4},{9,5},{10,... | collective-permute-start | bytes 491528 | tf_op jit(solution)/shard_map/ppermute | solution.py:959
  8.8 6.1 %copy-start.2 = (f32[256,256]{1,0:T(8,128)S(1)}, f32[256,256]{1,0:T(8,128)}, u32[]{:S(2)}) copy-start(f32[256,256]{1,0:T(8,128)} %constant.22.clone.rest_4_.rest_9_) | copy-start | bytes 786436
  8.8 6.1 %copy-start.3 = (f32[192,216]{1,0:T(8,128)S(1)}, f32[192,216]{1,0:T(8,128)}, u32[]{:S(2)}) copy-start(f32[192,216]{1,0:T(8,128)} %constant.20.clone.rest_2_.rest_7_) | copy-start | bytes 497668
  8.9 6.1 %copy-start.4 = (f32[144,144]{1,0:T(8,128)S(1)}, f32[144,144]{1,0:T(8,128)}, u32[]{:S(2)}) copy-start(f32[144,144]{1,0:T(8,128)} %constant.19.clone.rest_1_.rest_6_) | copy-start | bytes 248836
  8.9 6.1 %copy-start.5 = (f32[256,128]{1,0:T(8,128)S(1)}, f32[256,128]{1,0:T(8,128)}, u32[]{:S(2)}) copy-start(f32[256,128]{1,0:T(8,128)} %constant.23.clone.rest_5_.rest_10_) | copy-start | bytes 393220
  8.9 6.1 %copy-start.6 = (f32[96,120]{1,0:T(8,128)S(1)}, f32[96,120]{1,0:T(8,128)}, u32[]{:S(2)}) copy-start(f32[96,120]{1,0:T(8,128)} %constant.21.clone.rest_3_.rest_8_) | copy-start | bytes 138244
  8.9 6.1 %copy-start.7 = (f32[80,80]{1,0:T(8,128)S(1)}, f32[80,80]{1,0:T(8,128)}, u32[]{:S(2)}) copy-start(f32[80,80]{1,0:T(8,128)} %constant.18.clone.rest_0_.rest_5_) | copy-start | bytes 76804
  8.9 6.1 %copy-start.8 = (f32[72,128]{1,0:T(8,128)S(1)}, f32[72,128]{1,0:T(8,128)}, u32[]{:S(2)}) copy-start(f32[72,128]{1,0:T(8,128)} %constant.24.clone.rest_6_.rest_11_) | copy-start | bytes 110596
  8.9 6.1 %copy-start.9 = (f32[40,128]{1,0:T(8,128)S(1)}, f32[40,128]{1,0:T(8,128)}, u32[]{:S(2)}) copy-start(f32[40,128]{1,0:T(8,128)} %constant.25.clone.rest_7_.rest_12_) | copy-start | bytes 61444
  8.9 6.1 %copy-start.10 = (f32[1,128]{1,0:T(1,128)S(1)}, f32[1,128]{1,0:T(1,128)}, u32[]{:S(2)}) copy-start(f32[1,128]{1,0:T(1,128)} %constant.26.clone.rest_8_.rest_13_) | copy-start | bytes 1540
  9.3 5.1 %collective-permute-start.2 = (f32[296,128]{1,0:T(8,128)S(1)}, f32[296,128]{1,0:T(8,128)S(1)}, u32[]{:S(2)}, u32[]{:S(2)}) collective-permute-start(f32[296,128]{1,0:T(8,128)S(1)} %get-tuple-element.41), channel_id=1, source_target_pairs={{0,1},{4,5},{8,9},{12,13},{1,0},{5,4},{9,8},{13,12},{2,3},{6,7},{1... | collective-permute-start | bytes 454664 | tf_op jit(solution)/shard_map/ppermute | solution.py:959
  9.7 5.3 %collective-permute-start.3 = (f32[296,128]{1,0:T(8,128)S(1)}, f32[296,128]{1,0:T(8,128)S(1)}, u32[]{:S(2)}, u32[]{:S(2)}) collective-permute-start(f32[296,128]{1,0:T(8,128)S(1)} %get-tuple-element.42), channel_id=1, source_target_pairs={{0,4},{4,0},{8,12},{12,8},{1,2},{5,6},{9,10},{13,14},{2,1},{6,5},{... | collective-permute-start | bytes 454664 | tf_op jit(solution)/shard_map/ppermute | solution.py:959
  12.7 6.6 %collective-permute-start.8 = (f32[744,128]{1,0:T(8,128)S(1)}, f32[744,128]{1,0:T(8,128)S(1)}, u32[]{:S(2)}, u32[]{:S(2)}) collective-permute-start(f32[744,128]{1,0:T(8,128)S(1)} %get-tuple-element.51), channel_id=1, source_target_pairs={{0,1},{4,5},{8,9},{12,13},{1,0},{5,4},{9,8},{13,12},{2,3},{6,7},{1... | collective-permute-start | bytes 1142792 | tf_op jit(solution)/shard_map/ppermute | solution.py:959
  12.7 7.7 %collective-permute-start.9 = (f32[744,128]{1,0:T(8,128)S(1)}, f32[744,128]{1,0:T(8,128)S(1)}, u32[]{:S(2)}, u32[]{:S(2)}) collective-permute-start(f32[744,128]{1,0:T(8,128)S(1)} %get-tuple-element.52), channel_id=1, source_target_pairs={{0,4},{4,0},{8,12},{12,8},{1,2},{5,6},{9,10},{13,14},{2,1},{6,5},{... | collective-permute-start | bytes 1142792 | tf_op jit(solution)/shard_map/ppermute | solution.py:959
  20.8 1.8 %collective-permute-start.10 = (f32[16,128]{1,0:T(8,128)S(1)}, f32[16,128]{1,0:T(8,128)S(1)}, u32[]{:S(2)}, u32[]{:S(2)}) collective-permute-start(f32[16,128]{1,0:T(8,128)S(1)} %shard_map.155.table), channel_id=1, source_target_pairs={{0,1},{4,5},{8,9},{12,13},{1,0},{5,4},{9,8},{13,12},{2,3},{6,7},{1... | collective-permute-start | bytes 24584 | tf_op jit(solution)/shard_map/ppermute | solution.py:1042
  21.0 5.4 %collective-permute-start.4 = (f32[160,128]{1,0:T(8,128)S(1)}, f32[160,128]{1,0:T(8,128)S(1)}, u32[]{:S(2)}, u32[]{:S(2)}) collective-permute-start(f32[160,128]{1,0:T(8,128)S(1)} %get-tuple-element.47), channel_id=1, source_target_pairs={{0,4},{1,5},{2,6},{3,7},{4,0},{5,1},{6,2},{7,3},{8,12},{9,13},{10,... | collective-permute-start | bytes 245768 | tf_op jit(solution)/shard_map/ppermute | solution.py:959
  22.6 3.8 %collective-permute-start.5 = (f32[160,128]{1,0:T(8,128)S(1)}, f32[160,128]{1,0:T(8,128)S(1)}, u32[]{:S(2)}, u32[]{:S(2)}) collective-permute-start(f32[160,128]{1,0:T(8,128)S(1)} %get-tuple-element.48), channel_id=1, source_target_pairs={{0,1},{1,0},{2,3},{3,2},{4,8},{5,9},{6,10},{7,11},{8,4},{9,5},{10,... | collective-permute-start | bytes 245768 | tf_op jit(solution)/shard_map/ppermute | solution.py:959
  22.7 3.7 %collective-permute-start.11 = (f32[16,128]{1,0:T(8,128)S(1)}, f32[16,128]{1,0:T(8,128)S(1)}, u32[]{:S(2)}, u32[]{:S(2)}) collective-permute-start(f32[16,128]{1,0:T(8,128)S(1)} %shard_map.156.table), channel_id=1, source_target_pairs={{0,2},{1,3},{2,0},{3,1},{4,6},{5,7},{6,4},{7,5},{8,10},{9,11},{10,... | collective-permute-start | bytes 24584 | tf_op jit(solution)/shard_map/ppermute | solution.py:964
  26.6 11.5 %collective-permute-start.12 = (f32[376,128]{1,0:T(8,128)S(1)}, f32[376,128]{1,0:T(8,128)S(1)}, u32[]{:S(2)}, u32[]{:S(2)}) collective-permute-start(f32[376,128]{1,0:T(8,128)S(1)} %get-tuple-element.56), channel_id=1, source_target_pairs={{0,1},{4,5},{8,9},{12,13},{1,0},{5,4},{9,8},{13,12},{2,3},{6,7},{1... | collective-permute-start | bytes 577544 | tf_op jit(solution)/shard_map/ppermute | solution.py:959
  26.6 11.5 %collective-permute-start.13 = (f32[376,128]{1,0:T(8,128)S(1)}, f32[376,128]{1,0:T(8,128)S(1)}, u32[]{:S(2)}, u32[]{:S(2)}) collective-permute-start(f32[376,128]{1,0:T(8,128)S(1)} %get-tuple-element.57), channel_id=1, source_target_pairs={{0,4},{4,0},{8,12},{12,8},{1,2},{5,6},{9,10},{13,14},{2,1},{6,5},{... | collective-permute-start | bytes 577544 | tf_op jit(solution)/shard_map/ppermute | solution.py:959
  28.9 3.8 %collective-permute-start.14 = (f32[16,128]{1,0:T(8,128)S(1)}, f32[16,128]{1,0:T(8,128)S(1)}, u32[]{:S(2)}, u32[]{:S(2)}) collective-permute-start(f32[16,128]{1,0:T(8,128)S(1)} %shard_map.157.refs_4_.table), channel_id=1, source_target_pairs={{0,4},{1,5},{2,6},{3,7},{4,0},{5,1},{6,2},{7,3},{8,12},{9,13},{10,... | collective-permute-start | bytes 24584 | tf_op jit(solution)/shard_map/ppermute | solution.py:1046
  32.7 4.5 %collective-permute-start.15 = (f32[16,128]{1,0:T(8,128)S(1)}, f32[16,128]{1,0:T(8,128)S(1)}, u32[]{:S(2)}, u32[]{:S(2)}) collective-permute-start(f32[16,128]{1,0:T(8,128)S(1)} %shard_map.159.refs_0_), channel_id=1, source_target_pairs={{0,8},{4,12},{8,0},{12,4},{1,9},{5,13},{9,1},{13,5},{2,10},{6,14},... | collective-permute-start | bytes 24584 | tf_op jit(solution)/shard_map/ppermute | solution.py:964
  43.7 5.0 %collective-permute-start.16 = (f32[32,128]{1,0:T(8,128)S(1)}, f32[32,128]{1,0:T(8,128)S(1)}, u32[]{:S(2)}, u32[]{:S(2)}) collective-permute-start(f32[32,128]{1,0:T(8,128)S(1)} %get-tuple-element.67), channel_id=1, source_target_pairs={{0,4},{1,5},{2,6},{3,7},{4,0},{5,1},{6,2},{7,3},{8,12},{9,13},{10,... | collective-permute-start | bytes 49160 | tf_op jit(solution)/shard_map/ppermute | solution.py:959
  45.8 2.9 %collective-permute-start.17 = (f32[32,128]{1,0:T(8,128)S(1)}, f32[32,128]{1,0:T(8,128)S(1)}, u32[]{:S(2)}, u32[]{:S(2)}) collective-permute-start(f32[32,128]{1,0:T(8,128)S(1)} %get-tuple-element.68), channel_id=1, source_target_pairs={{0,1},{1,0},{2,3},{3,2},{4,8},{5,9},{6,10},{7,11},{8,4},{9,5},{10,... | collective-permute-start | bytes 49160 | tf_op jit(solution)/shard_map/ppermute | solution.py:959
  45.8 2.9 %collective-permute-start.18 = (f32[64,128]{1,0:T(8,128)S(1)}, f32[64,128]{1,0:T(8,128)S(1)}, u32[]{:S(2)}, u32[]{:S(2)}) collective-permute-start(f32[64,128]{1,0:T(8,128)S(1)} %get-tuple-element.69), channel_id=1, source_target_pairs={{0,1},{4,5},{8,9},{12,13},{1,0},{5,4},{9,8},{13,12},{2,3},{6,7},{1... | collective-permute-start | bytes 98312 | tf_op jit(solution)/shard_map/ppermute | solution.py:959
  46.3 3.9 %collective-permute-start.19 = (f32[64,128]{1,0:T(8,128)S(1)}, f32[64,128]{1,0:T(8,128)S(1)}, u32[]{:S(2)}, u32[]{:S(2)}) collective-permute-start(f32[64,128]{1,0:T(8,128)S(1)} %get-tuple-element.70), channel_id=1, source_target_pairs={{0,4},{4,0},{8,12},{12,8},{1,2},{5,6},{9,10},{13,14},{2,1},{6,5},{... | collective-permute-start | bytes 98312 | tf_op jit(solution)/shard_map/ppermute | solution.py:959
